TPU v7x, 32 devices: a whole 2x2x4 slice. The times are simulated.
32 devices in a mesh: fsdp: 2 (over core), context: 4 (over z), tensor: 4 (over y, x).
Axes of the slice: x: 2, y: 2, z: 4, core: 2. Of those that a mesh axis runs over, the one named last changes fastest.
Arguments:
- hidden_in: bfloat16 [2, 1024, 1536], P('fsdp', 'context'), may hold values from -6 to 6
- segment_ids: int32 [2, 1024], P('fsdp', 'context'), may hold values from 0 to 7, never falling along the last dimension, each value on 1 to 512 neighbouring positions
- w_query: bfloat16 [2, 1536, 1536], P(None, 'fsdp', 'tensor'), may hold values from -0.15625 to 0.15625
- w_key: bfloat16 [2, 1536, 1536], P(None, 'fsdp', 'tensor'), may hold values from -0.15625 to 0.15625
- w_value: bfloat16 [2, 1536, 1536], P(None, 'fsdp', 'tensor'), may hold values from -0.15625 to 0.15625
- w_gate_out: bfloat16 [2, 1536, 1536], P(None, 'fsdp', 'tensor'), may hold values from -0.15625 to 0.15625
- w_attn_out: bfloat16 [2, 1536, 1536], P(None, 'tensor', 'fsdp'), may hold values from -2.5 to 2.5
- w_forget: bfloat16 [2, 1536, 24], P(None, 'fsdp', 'tensor'), may hold values from -0.15625 to 0.15625
- b_forget: float32 [2, 24], P(None, 'tensor'), may hold values from 2 to 12
- gain_attn: bfloat16 [2, 1536], P(None, 'fsdp'), may hold values from 0.25 to 1.75
- gain_ffn: bfloat16 [2, 1536], P(None, 'fsdp'), may hold values from 0.25 to 1.75
- w_gate: bfloat16 [2, 1536, 4096], P(None, 'fsdp', 'tensor'), may hold values from -0.15625 to 0.15625
- w_up: bfloat16 [2, 1536, 4096], P(None, 'fsdp', 'tensor'), may hold values from -0.15625 to 0.15625
- w_down: bfloat16 [2, 4096, 1536], P(None, 'tensor', 'fsdp'), may hold values from -0.1875 to 0.1875
- cotangent: bfloat16 [2, 1024, 1536], P('fsdp', 'context'), may hold values from -6 to 6
Outputs:
- output: bfloat16 [2, 1024, 1536], P('fsdp', 'context')
- grad_input: bfloat16 [2, 1024, 1536], P('fsdp', 'context')
- grad_query: float32 [2, 1536, 1536], P(None, 'fsdp', 'tensor')
- grad_key: float32 [2, 1536, 1536], P(None, 'fsdp', 'tensor')
- grad_value: float32 [2, 1536, 1536], P(None, 'fsdp', 'tensor')
- grad_gate_out: float32 [2, 1536, 1536], P(None, 'fsdp', 'tensor')
- grad_attn_out: float32 [2, 1536, 1536], P(None, 'tensor', 'fsdp')
- grad_forget: float32 [2, 1536, 24], P(None, 'fsdp', 'tensor')
- grad_forget_bias: float32 [2, 24], P(None, 'tensor')
- grad_gain_attn: float32 [2, 1536], P(None, 'fsdp')
- grad_gain_ffn: float32 [2, 1536], P(None, 'fsdp')
- grad_gate: float32 [2, 1536, 4096], P(None, 'fsdp', 'tensor')
- grad_up: float32 [2, 1536, 4096], P(None, 'fsdp', 'tensor')
- grad_down: float32 [2, 4096, 1536], P(None, 'tensor', 'fsdp')
Inputs may be any that keep to these rules, and one draw needn't show every extreme that they name: `segment_ids`: along each sequence the ids never fall; each of the 8 ids marks one document of 1 to 512 positions, and one document has exactly 512.
All inputs are finite; a program needn't handle non-finite values.
Results may differ from a plain program's by a relative error of at most 0.025.
Values may be sent and summed in bfloat16 or wider, within the bound.
No kernel may reach another device: no remote copies, remote signals or barrier semaphores. Data moves between devices by JAX's collectives and lax.ppermute only.
A program may use at most 256 MiB of HBM per device.

v0:
```python
import jax
import jax.numpy as jnp
from jax import lax
from jax.sharding import PartitionSpec as P

epsilon = 1e-06
masked_value = -1e30


def carried_in(x, axis, combine, identity, reverse):
    count, place = (lax.axis_size(axis), lax.axis_index(axis))
    everything = lax.all_gather(x, axis)
    start = jnp.broadcast_to(jnp.asarray(identity, x.dtype), x.shape)

    def step(k, before):
        at = count - 1 - k if reverse else k
        reached = at > place if reverse else at < place
        new = combine(before, everything[at])
        return jnp.where(reached, new, before)

    return lax.fori_loop(0, count, step, start)


def add_terms(earlier, later_term):
    return earlier + later_term


def norm_rows(hidden, gain):
    inverse = lax.rsqrt(jnp.mean(hidden * hidden, axis=-1, keepdims=True) + epsilon)
    return (hidden * inverse * gain, inverse)


def norm_back(grad_normed, hidden, inverse, gain):
    scaled = hidden * inverse
    weighted = grad_normed * gain
    grad_gain = jnp.sum(grad_normed * scaled, axis=0)
    grad_hidden = inverse * (
        weighted - scaled * jnp.mean(weighted * scaled, axis=-1, keepdims=True)
    )
    return (grad_hidden, grad_gain)


def block_scores(setting, block_start, block_len):
    query_rows, decay_rows, query_pos, query_seg, key_all, decay_keys, key_seg = setting
    key_block = lax.dynamic_slice_in_dim(key_all, block_start, block_len, 1)
    decay_block = lax.dynamic_slice_in_dim(decay_keys, block_start, block_len, 2)
    seg_block = lax.dynamic_slice_in_dim(key_seg, block_start, block_len, 1)
    key_pos = block_start + lax.iota(jnp.int32, block_len)
    raw_scores = (
        jnp.einsum("sqhe,skhe->shqk", query_rows, key_block, preferred_element_type=jnp.float32)
        * 0.125
    )
    scores = raw_scores + (decay_rows[:, :, :, None] - decay_block[:, :, None, :])
    live_pairs = (
        (key_pos[None, :] <= query_pos[:, None])[None]
        & (query_seg[:, :, None] == seg_block[:, None, :])
    )[:, None]
    return (jnp.where(live_pairs, scores, masked_value), live_pairs)


def over_blocks(block_len, block_count, block_step, initial):

    def one_block(block_index, carried):
        block_start = block_index * block_len
        return block_step(block_start, carried)

    return lax.fori_loop(0, block_count, one_block, initial)


def softmax_totals(setting, block_len, block_count):
    query_rows = setting[0]
    shape_rows = (query_rows.shape[0], query_rows.shape[2], query_rows.shape[1])

    def block_step(block_start, carried):
        top_now, total_now = carried
        scores, live_pairs = block_scores(setting, block_start, block_len)
        top_next = jnp.maximum(top_now, jnp.max(scores, axis=-1))
        exp_terms = jnp.where(live_pairs, jnp.exp(scores - top_next[..., None]), 0.0)
        return (top_next, total_now * jnp.exp(top_now - top_next) + jnp.sum(exp_terms, axis=-1))

    initial = (jnp.full(shape_rows, masked_value, jnp.float32), jnp.zeros(shape_rows, jnp.float32))
    top_end, total_end = over_blocks(block_len, block_count, block_step, initial)
    return top_end + jnp.log(total_end)


def attention_values(setting, value_all, log_total, block_len, block_count):
    query_rows = setting[0]

    def block_step(block_start, carried):
        scores, live_pairs = block_scores(setting, block_start, block_len)
        probability = jnp.where(live_pairs, jnp.exp(scores - log_total[..., None]), 0.0)
        value_block = lax.dynamic_slice_in_dim(value_all, block_start, block_len, 1)
        rounded = probability.astype(jnp.bfloat16)
        residue = (probability - rounded.astype(jnp.float32)).astype(jnp.bfloat16)
        main_part = jnp.einsum(
            "shqk,skhe->sqhe", rounded, value_block, preferred_element_type=jnp.float32
        )
        low_part = jnp.einsum(
            "shqk,skhe->sqhe", residue, value_block, preferred_element_type=jnp.float32
        )
        return (carried[0] + main_part, carried[1] + low_part)

    zero_rows = jnp.zeros(query_rows.shape, jnp.float32)
    attended, correction = over_blocks(block_len, block_count, block_step, (zero_rows, zero_rows))
    return (attended, attended + correction)


def attention_grads(setting, value_all, log_total, delta_rows, grad_out, block_len, block_count):
    query_rows, key_all = (setting[0], setting[4])

    def block_step(block_start, carried):
        scores, live_pairs = block_scores(setting, block_start, block_len)
        probability = jnp.where(live_pairs, jnp.exp(scores - log_total[..., None]), 0.0)
        key_block = lax.dynamic_slice_in_dim(key_all, block_start, block_len, 1)
        value_block = lax.dynamic_slice_in_dim(value_all, block_start, block_len, 1)
        grad_probs = jnp.einsum(
            "sqhe,skhe->shqk", grad_out, value_block, preferred_element_type=jnp.float32
        )
        grad_scores = (probability * (grad_probs - delta_rows[..., None])).astype(jnp.bfloat16)
        score_float = grad_scores.astype(jnp.float32)
        grad_query = (
            carried[0]
            + jnp.einsum(
                "shqk,skhe->sqhe", grad_scores, key_block, preferred_element_type=jnp.float32
            )
            * 0.125
        )
        decay_query = carried[1] + jnp.sum(score_float, axis=3)
        grad_keys, grad_values, decay_keyset = (carried[2], carried[3], carried[4])
        key_part = (
            jnp.einsum(
                "shqk,sqhe->skhe", grad_scores, query_rows, preferred_element_type=jnp.float32
            )
            * 0.125
        )
        value_part = jnp.einsum(
            "shqk,sqhe->skhe",
            probability.astype(jnp.bfloat16),
            grad_out,
            preferred_element_type=jnp.float32,
        )
        grad_keys = lax.dynamic_update_slice_in_dim(
            grad_keys,
            lax.dynamic_slice_in_dim(grad_keys, block_start, block_len, 1) + key_part,
            block_start,
            1,
        )
        grad_values = lax.dynamic_update_slice_in_dim(
            grad_values,
            lax.dynamic_slice_in_dim(grad_values, block_start, block_len, 1) + value_part,
            block_start,
            1,
        )
        decay_keyset = lax.dynamic_update_slice_in_dim(
            decay_keyset,
            lax.dynamic_slice_in_dim(decay_keyset, block_start, block_len, 2)
            - jnp.sum(score_float, axis=2),
            block_start,
            2,
        )
        return (grad_query, decay_query, grad_keys, grad_values, decay_keyset)

    seq_count, piece_len, heads_local = (
        query_rows.shape[0],
        query_rows.shape[1],
        query_rows.shape[2],
    )
    seq_len = key_all.shape[1]
    initial = (
        jnp.zeros(query_rows.shape, jnp.float32),
        jnp.zeros((seq_count, heads_local, piece_len), jnp.float32),
    )
    initial = initial + (
        jnp.zeros(key_all.shape, jnp.float32),
        jnp.zeros(key_all.shape, jnp.float32),
        jnp.zeros((seq_count, heads_local, seq_len), jnp.float32),
    )
    return over_blocks(block_len, block_count, block_step, initial)


def local(
    hidden_in,
    segment_ids,
    w_query,
    w_key,
    w_value,
    w_gate_out,
    w_attn_out,
    w_forget,
    b_forget,
    gain_attn,
    gain_ffn,
    w_gate,
    w_up,
    w_down,
    cotangent,
):
    seq_count, piece_len, model_width = hidden_in.shape
    row_count = seq_count * piece_len
    context_size = lax.axis_size("context")
    group_size = lax.axis_size("fsdp") * context_size
    piece_index = lax.axis_index("context")
    piece_start = piece_index * piece_len
    seq_len = piece_len * context_size
    heads_local = w_forget.shape[2]
    local_width = w_query.shape[2]
    head_size = local_width // heads_local
    layer_total = w_query.shape[0]
    query_pos = piece_start + lax.iota(jnp.int32, piece_len)
    query_seg = segment_ids.astype(jnp.float32)
    heads_shape = (seq_count, piece_len, heads_local, head_size)
    hidden = hidden_in.astype(jnp.float32).reshape(row_count, model_width)
    saved_state = []
    for layer_index in range(layer_total):
        gathered = (
            lax.all_gather(w_query[layer_index], "fsdp", axis=0, tiled=True),
            lax.all_gather(w_key[layer_index], "fsdp", axis=0, tiled=True),
            lax.all_gather(w_value[layer_index], "fsdp", axis=0, tiled=True),
            lax.all_gather(w_gate_out[layer_index], "fsdp", axis=0, tiled=True),
            lax.all_gather(w_attn_out[layer_index], "fsdp", axis=1, tiled=True),
            lax.all_gather(w_forget[layer_index], "fsdp", axis=0, tiled=True),
            lax.all_gather(gain_attn[layer_index], "fsdp", axis=0, tiled=True),
            lax.all_gather(gain_ffn[layer_index], "fsdp", axis=0, tiled=True),
            lax.all_gather(w_gate[layer_index], "fsdp", axis=0, tiled=True),
            lax.all_gather(w_up[layer_index], "fsdp", axis=0, tiled=True),
            lax.all_gather(w_down[layer_index], "fsdp", axis=1, tiled=True),
        )
        normed, inverse_one = norm_rows(hidden, gathered[6].astype(jnp.float32))
        normed_low = normed.astype(jnp.bfloat16)
        query_low = (
            jnp.dot(normed_low, gathered[0], preferred_element_type=jnp.float32)
            .astype(jnp.bfloat16)
            .reshape(heads_shape)
        )
        key_low = (
            jnp.dot(normed_low, gathered[1], preferred_element_type=jnp.float32)
            .astype(jnp.bfloat16)
            .reshape(seq_count, piece_len, local_width)
        )
        value_low = (
            jnp.dot(normed_low, gathered[2], preferred_element_type=jnp.float32)
            .astype(jnp.bfloat16)
            .reshape(seq_count, piece_len, local_width)
        )
        gate_pre = jnp.dot(normed_low, gathered[3], preferred_element_type=jnp.float32)
        forget_pre = (
            jnp.dot(normed_low, gathered[5], preferred_element_type=jnp.float32)
            + b_forget[layer_index]
        )
        local_sum = jnp.cumsum(
            jax.nn.log_sigmoid(forget_pre).reshape(seq_count, piece_len, heads_local), axis=1
        )
        before_sum = carried_in(
            local_sum[:, piece_len - 1, :],
            "context",
            add_terms,
            jnp.zeros((seq_count, heads_local), jnp.float32),
            False,
        )
        decay_rows = local_sum + before_sum[:, None, :]
        key_meta = (
            lax.all_gather(decay_rows, "context", axis=1, tiled=True),
            lax.all_gather(query_seg, "context", axis=1, tiled=True),
        )
        decay_keys = key_meta[0]
        key_values = (
            lax.all_gather(key_low, "context", axis=1, tiled=True),
            lax.all_gather(value_low, "context", axis=1, tiled=True),
        )
        key_all = key_values[0].reshape(seq_count, seq_len, heads_local, head_size)
        value_all = key_values[1].reshape(seq_count, seq_len, heads_local, head_size)
        setting = (
            query_low,
            jnp.transpose(decay_rows, (0, 2, 1)),
            query_pos,
            query_seg,
            key_all,
            jnp.transpose(decay_keys, (0, 2, 1)),
            key_meta[1],
        )
        log_total = softmax_totals(setting, piece_len, context_size)
        attended, full_out = attention_values(
            setting, value_all, log_total, piece_len, context_size
        )
        attended_rows = attended.reshape(row_count, local_width)
        gate_sig = jax.nn.sigmoid(gate_pre)
        gated_low = (attended_rows * gate_sig).astype(jnp.bfloat16)
        attn_total = lax.psum(
            jnp.dot(gated_low, gathered[4], preferred_element_type=jnp.float32), "tensor"
        )
        mixed_rows = hidden + attn_total
        normed_two, inverse_two = norm_rows(mixed_rows, gathered[7].astype(jnp.float32))
        normed_two_low = normed_two.astype(jnp.bfloat16)
        gate_ffn = jnp.dot(normed_two_low, gathered[8], preferred_element_type=jnp.float32)
        up_ffn = jnp.dot(normed_two_low, gathered[9], preferred_element_type=jnp.float32)
        inner_low = (jax.nn.silu(gate_ffn) * up_ffn).astype(jnp.bfloat16)
        ffn_total = lax.psum(
            jnp.dot(inner_low, gathered[10], preferred_element_type=jnp.float32), "tensor"
        )
        saved_state.append(
            (
                gathered,
                hidden,
                inverse_one,
                normed_low,
                setting,
                value_all,
                log_total,
                attended_rows,
                full_out,
                gate_sig,
                gated_low,
                forget_pre,
                mixed_rows,
                inverse_two,
                normed_two_low,
                gate_ffn,
                up_ffn,
                inner_low,
            )
        )
        hidden = mixed_rows + ffn_total
    output = hidden.astype(jnp.bfloat16).reshape(seq_count, piece_len, model_width)
    grad_hidden = cotangent.astype(jnp.float32).reshape(row_count, model_width)
    results = [None] * layer_total
    for layer_index in reversed(range(layer_total)):
        (
            gathered,
            hidden,
            inverse_one,
            normed_low,
            setting,
            value_all,
            log_total,
            attended_rows,
            full_out,
            gate_sig,
            gated_low,
            forget_pre,
            mixed_rows,
            inverse_two,
            normed_two_low,
            gate_ffn,
            up_ffn,
            inner_low,
        ) = saved_state[layer_index]
        grad_ffn_low = grad_hidden.astype(jnp.bfloat16)
        grad_down_w = jnp.einsum(
            "rf,rd->fd", inner_low, grad_ffn_low, preferred_element_type=jnp.float32
        )
        grad_inner = jnp.einsum(
            "rd,fd->rf", grad_ffn_low, gathered[10], preferred_element_type=jnp.float32
        )
        sig_gate = jax.nn.sigmoid(gate_ffn)
        grad_gate_low = (
            grad_inner * up_ffn * sig_gate * (1.0 + gate_ffn * (1.0 - sig_gate))
        ).astype(jnp.bfloat16)
        grad_up_low = (grad_inner * jax.nn.silu(gate_ffn)).astype(jnp.bfloat16)
        grad_gate_w = jnp.einsum(
            "rd,rf->df", normed_two_low, grad_gate_low, preferred_element_type=jnp.float32
        )
        grad_up_w = jnp.einsum(
            "rd,rf->df", normed_two_low, grad_up_low, preferred_element_type=jnp.float32
        )
        grad_normed_two = lax.psum(
            jnp.einsum("rf,df->rd", grad_gate_low, gathered[8], preferred_element_type=jnp.float32)
            + jnp.einsum("rf,df->rd", grad_up_low, gathered[9], preferred_element_type=jnp.float32),
            "tensor",
        )
        grad_mixed_norm, grad_gain_two = norm_back(
            grad_normed_two, mixed_rows, inverse_two, gathered[7].astype(jnp.float32)
        )
        grad_mixed = grad_hidden + grad_mixed_norm
        grad_attn_low = grad_mixed.astype(jnp.bfloat16)
        grad_attn_w = jnp.einsum(
            "rf,rd->fd", gated_low, grad_attn_low, preferred_element_type=jnp.float32
        )
        grad_gated = jnp.einsum(
            "rd,fd->rf", grad_attn_low, gathered[4], preferred_element_type=jnp.float32
        )
        grad_out_low = (grad_gated * gate_sig).astype(jnp.bfloat16)
        grad_gate_pre_low = (grad_gated * attended_rows * gate_sig * (1.0 - gate_sig)).astype(
            jnp.bfloat16
        )
        grad_out_heads = grad_out_low.reshape(heads_shape)
        delta_rows = jnp.transpose(
            jnp.sum(grad_out_heads.astype(jnp.float32) * full_out, axis=-1), (0, 2, 1)
        )
        grad_query, decay_query, grad_keys, grad_values, decay_keyset = attention_grads(
            setting, value_all, log_total, delta_rows, grad_out_heads, piece_len, context_size
        )
        returned = (
            lax.psum_scatter(
                grad_keys.reshape(seq_count, seq_len, local_width),
                "context",
                scatter_dimension=1,
                tiled=True,
            ),
            lax.psum_scatter(
                grad_values.reshape(seq_count, seq_len, local_width),
                "context",
                scatter_dimension=1,
                tiled=True,
            ),
            lax.psum_scatter(
                jnp.transpose(decay_keyset, (0, 2, 1)), "context", scatter_dimension=1, tiled=True
            ),
        )
        key_grad_rows = returned[0]
        value_grad_rows = returned[1]
        key_decay_own = returned[2]
        own_total = jnp.transpose(decay_query, (0, 2, 1)) + key_decay_own
        later_sums = carried_in(
            jnp.sum(own_total, axis=1),
            "context",
            add_terms,
            jnp.zeros((seq_count, heads_local), jnp.float32),
            True,
        )
        grad_local = jnp.concatenate(
            [own_total[:, :-1], own_total[:, -1:] + later_sums[:, None, :]], axis=1
        )
        grad_log_keep = jnp.flip(jnp.cumsum(jnp.flip(grad_local, 1), axis=1), 1)
        grad_forget_low = (
            grad_log_keep.reshape(row_count, heads_local) * jax.nn.sigmoid(-forget_pre)
        ).astype(jnp.bfloat16)
        grad_query_low = grad_query.reshape(row_count, local_width).astype(jnp.bfloat16)
        grad_key_low = key_grad_rows.reshape(row_count, local_width).astype(jnp.bfloat16)
        grad_value_low = value_grad_rows.reshape(row_count, local_width).astype(jnp.bfloat16)
        grad_query_w = jnp.einsum(
            "rd,rf->df", normed_low, grad_query_low, preferred_element_type=jnp.float32
        )
        grad_key_w = jnp.einsum(
            "rd,rf->df", normed_low, grad_key_low, preferred_element_type=jnp.float32
        )
        grad_value_w = jnp.einsum(
            "rd,rf->df", normed_low, grad_value_low, preferred_element_type=jnp.float32
        )
        grad_gate_out_w = jnp.einsum(
            "rd,rf->df", normed_low, grad_gate_pre_low, preferred_element_type=jnp.float32
        )
        grad_forget_w = jnp.einsum(
            "rd,rh->dh", normed_low, grad_forget_low, preferred_element_type=jnp.float32
        )
        bias_copies = jnp.broadcast_to(
            jnp.sum(grad_forget_low.astype(jnp.float32), axis=0)[None, :], (group_size, heads_local)
        )
        grad_normed = lax.psum(
            jnp.einsum("rf,df->rd", grad_query_low, gathered[0], preferred_element_type=jnp.float32)
            + jnp.einsum("rf,df->rd", grad_key_low, gathered[1], preferred_element_type=jnp.float32)
            + jnp.einsum(
                "rf,df->rd", grad_value_low, gathered[2], preferred_element_type=jnp.float32
            )
            + jnp.einsum(
                "rf,df->rd", grad_gate_pre_low, gathered[3], preferred_element_type=jnp.float32
            )
            + jnp.einsum(
                "rh,dh->rd", grad_forget_low, gathered[5], preferred_element_type=jnp.float32
            ),
            "tensor",
        )
        grad_hidden_norm, grad_gain_one = norm_back(
            grad_normed, hidden, inverse_one, gathered[6].astype(jnp.float32)
        )
        grad_hidden = grad_mixed + grad_hidden_norm
        shares = (
            lax.psum_scatter(grad_query_w, ("fsdp", "context"), scatter_dimension=0, tiled=True),
            lax.psum_scatter(grad_key_w, ("fsdp", "context"), scatter_dimension=0, tiled=True),
            lax.psum_scatter(grad_value_w, ("fsdp", "context"), scatter_dimension=0, tiled=True),
            lax.psum_scatter(grad_gate_out_w, ("fsdp", "context"), scatter_dimension=0, tiled=True),
            lax.psum_scatter(grad_attn_w, ("fsdp", "context"), scatter_dimension=1, tiled=True),
            lax.psum_scatter(grad_forget_w, ("fsdp", "context"), scatter_dimension=0, tiled=True),
            lax.psum_scatter(bias_copies, ("fsdp", "context"), scatter_dimension=0, tiled=True),
            lax.psum_scatter(grad_gain_one, ("fsdp", "context"), scatter_dimension=0, tiled=True),
            lax.psum_scatter(grad_gain_two, ("fsdp", "context"), scatter_dimension=0, tiled=True),
            lax.psum_scatter(grad_gate_w, ("fsdp", "context"), scatter_dimension=0, tiled=True),
            lax.psum_scatter(grad_up_w, ("fsdp", "context"), scatter_dimension=0, tiled=True),
            lax.psum_scatter(grad_down_w, ("fsdp", "context"), scatter_dimension=1, tiled=True),
        )
        regathered = (
            lax.all_gather(shares[0], "context", axis=0, tiled=True),
            lax.all_gather(shares[1], "context", axis=0, tiled=True),
            lax.all_gather(shares[2], "context", axis=0, tiled=True),
            lax.all_gather(shares[3], "context", axis=0, tiled=True),
            lax.all_gather(shares[4], "context", axis=1, tiled=True),
            lax.all_gather(shares[5], "context", axis=0, tiled=True),
            lax.all_gather(shares[6], "context", axis=0, tiled=True),
            lax.all_gather(shares[7], "context", axis=0, tiled=True),
            lax.all_gather(shares[8], "context", axis=0, tiled=True),
            lax.all_gather(shares[9], "context", axis=0, tiled=True),
            lax.all_gather(shares[10], "context", axis=0, tiled=True),
            lax.all_gather(shares[11], "context", axis=1, tiled=True),
        )
        results[layer_index] = (
            regathered[0],
            regathered[1],
            regathered[2],
            regathered[3],
            regathered[4],
            regathered[5],
            regathered[6][0],
            regathered[7],
            regathered[8],
            regathered[9],
            regathered[10],
            regathered[11],
        )
    grad_input = grad_hidden.astype(jnp.bfloat16).reshape(seq_count, piece_len, model_width)
    stacked = [
        jnp.stack([results[layer_index][member] for layer_index in range(layer_total)])
        for member in range(12)
    ]
    return (
        output,
        grad_input,
        stacked[0],
        stacked[1],
        stacked[2],
        stacked[3],
        stacked[4],
        stacked[5],
        stacked[6],
        stacked[7],
        stacked[8],
        stacked[9],
        stacked[10],
        stacked[11],
    )


def solution(mesh):
    placed = (
        P("fsdp", "context", None),
        P("fsdp", "context"),
        P(None, "fsdp", "tensor"),
        P(None, "fsdp", "tensor"),
        P(None, "fsdp", "tensor"),
        P(None, "fsdp", "tensor"),
        P(None, "tensor", "fsdp"),
        P(None, "fsdp", "tensor"),
        P(None, "tensor"),
        P(None, "fsdp"),
        P(None, "fsdp"),
        P(None, "fsdp", "tensor"),
        P(None, "fsdp", "tensor"),
        P(None, "tensor", "fsdp"),
        P("fsdp", "context", None),
    )
    return jax.shard_map(
        local,
        mesh=mesh,
        in_specs=placed,
        out_specs=(
            P("fsdp", "context", None),
            P("fsdp", "context", None),
            P(None, "fsdp", "tensor"),
            P(None, "fsdp", "tensor"),
            P(None, "fsdp", "tensor"),
            P(None, "fsdp", "tensor"),
            P(None, "tensor", "fsdp"),
            P(None, "fsdp", "tensor"),
            P(None, "tensor"),
            P(None, "fsdp"),
            P(None, "fsdp"),
            P(None, "fsdp", "tensor"),
            P(None, "fsdp", "tensor"),
            P(None, "tensor", "fsdp"),
        ),
        check_vma=False,
    )
```

profile of v0, /device:TPU:0, one launch (start us, length us, event | category | flops | bytes accessed | tf_op | source)
XLA Modules:
  0.0 3268.6 jit_solution(2482115020578662718)
XLA Ops:
  163.4 44.9 %all-reduce.23.cloned.1.call-done = f32[256,1536]{1,0:T(8,128)} async-done(((f32[256,1536]{1,0:T(8,128)}), f32[256,1536]{1,0:T(8,128)}) %all-reduce.23.cloned.1.call-update) | async-done | bytes 1572880 | tf_op jit(solution)/shard_map/psum | solution.py:288
  265.4 54.6 %all-reduce.25.cloned.1.call-done = f32[256,1536]{1,0:T(8,128)} async-done(((f32[256,1536]{1,0:T(8,128)}), f32[256,1536]{1,0:T(8,128)}) %all-reduce.25.cloned.1.call-update) | async-done | bytes 1572880 | tf_op jit(solution)/shard_map/psum | solution.py:297
  454.2 51.3 %all-reduce.27.cloned.1.call-done = f32[256,1536]{1,0:T(8,128)} async-done(((f32[256,1536]{1,0:T(8,128)}), f32[256,1536]{1,0:T(8,128)}) %all-reduce.27.cloned.1.call-update) | async-done | bytes 1572880 | tf_op jit(solution)/shard_map/psum | solution.py:288
  544.6 62.1 %all-reduce.29.cloned.1.call-done = f32[256,1536]{1,0:T(8,128)} async-done(((f32[256,1536]{1,0:T(8,128)}), f32[256,1536]{1,0:T(8,128)}) %all-reduce.29.cloned.1.call-update) | async-done | bytes 1572880 | tf_op jit(solution)/shard_map/psum | solution.py:365
  615.8 49.2 %while.174 = (s32[]{:T(128)}, f32[1,256,6,64]{1,3,2,0:T(8,128)}, f32[1,6,256]{2,1,0:T(8,128)}, f32[1,1024,6,64]{1,3,2,0:T(8,128)}, f32[1,1024,6,64]{1,3,2,0:T(8,...) while((s32[]{:T(128)}, f32[1,256,6,64]{1,3,2,0:T(8,128)}, ...), condition=%wide.region_34.35_spmd.clone, body=%wide.region_31.34_spmd.clone.sunk | while | flops 257558528 | bytes 11172274 | solution.py:67
  728.2 34.0 %reduce-scatter.31.cloned.1.call-done = f32[1,256,384]{1,2,0:T(8,128)} async-done(((f32[1,1024,384]{1,2,0:T(8,128)}), f32[1,256,384]{1,2,0:T(8,128)}) %reduce-scatter.31.cloned.1.call-update) | async-done | bytes 393232 | tf_op jit(solution)/shard_map/reduce_scatter | solution.py:399
  766.8 59.9 %all-reduce.31.cloned.1.call-done = f32[256,1536]{1,0:T(8,128)} async-done(((f32[256,1536]{1,0:T(8,128)}), f32[256,1536]{1,0:T(8,128)}) %all-reduce.31.cloned.1.call-update) | async-done | bytes 1572880 | tf_op jit(solution)/shard_map/psum | solution.py:448
  838.5 61.0 %all-reduce.33.cloned.1.call-done = f32[256,1536]{1,0:T(8,128)} async-done(((f32[256,1536]{1,0:T(8,128)}), f32[256,1536]{1,0:T(8,128)}) %all-reduce.33.cloned.1.call-update) | async-done | bytes 1572880 | tf_op jit(solution)/shard_map/psum | solution.py:365
  908.7 49.2 %while.176 = (s32[]{:T(128)}, f32[1,256,6,64]{1,3,2,0:T(8,128)}, f32[1,6,256]{2,1,0:T(8,128)}, f32[1,1024,6,64]{1,3,2,0:T(8,128)}, f32[1,1024,6,64]{1,3,2,0:T(8,...) while((s32[]{:T(128)}, f32[1,256,6,64]{1,3,2,0:T(8,128)}, ...), condition=%wide.region_51.52_spmd.clone, body=%wide.region_48.51_spmd.clone.sunk | while | flops 257558528 | bytes 11172274 | solution.py:67
  1108.8 55.3 %reduce-scatter.57.cloned.1.call-done = f32[384,192]{0,1:T(8,128)} async-done(((f32[384,1536]{0,1:T(8,128)}), f32[384,192]{0,1:T(8,128)}) %reduce-scatter.57.cloned.1.call-update) | async-done | bytes 294928 | tf_op jit(solution)/shard_map/reduce_scatter | solution.py:471
  1164.2 56.0 %reduce-scatter.43.cloned.1.call-done = f32[192,384]{1,0:T(8,128)} async-done(((f32[1536,384]{1,0:T(8,128)}), f32[192,384]{1,0:T(8,128)}) %reduce-scatter.43.cloned.1.call-update) | async-done | bytes 294928 | tf_op jit(solution)/shard_map/reduce_scatter | solution.py:467
  1220.3 56.0 %reduce-scatter.41.cloned.1.call-done = f32[192,384]{1,0:T(8,128)} async-done(((f32[1536,384]{1,0:T(8,128)}), f32[192,384]{1,0:T(8,128)}) %reduce-scatter.41.cloned.1.call-update) | async-done | bytes 294928 | tf_op jit(solution)/shard_map/reduce_scatter | solution.py:467
  1276.4 55.3 %reduce-scatter.55.cloned.1.call-done = f32[192,384]{1,0:T(8,128)} async-done(((f32[1536,384]{1,0:T(8,128)}), f32[192,384]{1,0:T(8,128)}) %reduce-scatter.55.cloned.1.call-update) | async-done | bytes 294928 | tf_op jit(solution)/shard_map/reduce_scatter | solution.py:470
  1331.7 55.4 %reduce-scatter.53.cloned.1.call-done = f32[192,384]{1,0:T(8,128)} async-done(((f32[1536,384]{1,0:T(8,128)}), f32[192,384]{1,0:T(8,128)}) %reduce-scatter.53.cloned.1.call-update) | async-done | bytes 294928 | tf_op jit(solution)/shard_map/reduce_scatter | solution.py:470
  1387.2 56.0 %reduce-scatter.47.cloned.1.call-done = f32[192,384]{1,0:T(8,128)} async-done(((f32[1536,384]{1,0:T(8,128)}), f32[192,384]{1,0:T(8,128)}) %reduce-scatter.47.cloned.1.call-update) | async-done | bytes 294928 | tf_op jit(solution)/shard_map/reduce_scatter | solution.py:468
  1443.3 55.9 %reduce-scatter.45.cloned.1.call-done = f32[192,384]{1,0:T(8,128)} async-done(((f32[1536,384]{1,0:T(8,128)}), f32[192,384]{1,0:T(8,128)}) %reduce-scatter.45.cloned.1.call-update) | async-done | bytes 294928 | tf_op jit(solution)/shard_map/reduce_scatter | solution.py:468
  1499.2 55.9 %reduce-scatter.51.cloned.1.call-done = f32[192,384]{1,0:T(8,128)} async-done(((f32[1536,384]{1,0:T(8,128)}), f32[192,384]{1,0:T(8,128)}) %reduce-scatter.51.cloned.1.call-update) | async-done | bytes 294928 | tf_op jit(solution)/shard_map/reduce_scatter | solution.py:469
  1555.2 55.4 %reduce-scatter.49.cloned.1.call-done = f32[192,384]{1,0:T(8,128)} async-done(((f32[1536,384]{1,0:T(8,128)}), f32[192,384]{1,0:T(8,128)}) %reduce-scatter.49.cloned.1.call-update) | async-done | bytes 294928 | tf_op jit(solution)/shard_map/reduce_scatter | solution.py:469
  1610.7 129.2 %reduce-scatter.71.cloned.1.call-done = f32[1024,192]{0,1:T(8,128)} async-done(((f32[1024,1536]{0,1:T(8,128)}), f32[1024,192]{0,1:T(8,128)}) %reduce-scatter.71.cloned.1.call-update) | async-done | bytes 786448 | tf_op jit(solution)/shard_map/reduce_scatter | solution.py:478
  1739.9 130.6 %reduce-scatter.69.cloned.1.call-done = f32[1024,192]{0,1:T(8,128)} async-done(((f32[1024,1536]{0,1:T(8,128)}), f32[1024,192]{0,1:T(8,128)}) %reduce-scatter.69.cloned.1.call-update) | async-done | bytes 786448 | tf_op jit(solution)/shard_map/reduce_scatter | solution.py:478
  1870.6 131.2 %reduce-scatter.63.cloned.1.call-done = f32[192,1024]{1,0:T(8,128)} async-done(((f32[1536,1024]{1,0:T(8,128)}), f32[192,1024]{1,0:T(8,128)}) %reduce-scatter.63.cloned.1.call-update) | async-done | bytes 786448 | tf_op jit(solution)/shard_map/reduce_scatter | solution.py:476
  2001.9 131.2 %reduce-scatter.61.cloned.1.call-done = f32[192,1024]{1,0:T(8,128)} async-done(((f32[1536,1024]{1,0:T(8,128)}), f32[192,1024]{1,0:T(8,128)}) %reduce-scatter.61.cloned.1.call-update) | async-done | bytes 786448 | tf_op jit(solution)/shard_map/reduce_scatter | solution.py:476
  2133.1 131.0 %reduce-scatter.67.cloned.1.call-done = f32[192,1024]{1,0:T(8,128)} async-done(((f32[1536,1024]{1,0:T(8,128)}), f32[192,1024]{1,0:T(8,128)}) %reduce-scatter.67.cloned.1.call-update) | async-done | bytes 786448 | tf_op jit(solution)/shard_map/reduce_scatter | solution.py:477
  2264.2 130.6 %reduce-scatter.65.cloned.1.call-done = f32[192,1024]{1,0:T(8,128)} async-done(((f32[1536,1024]{1,0:T(8,128)}), f32[192,1024]{1,0:T(8,128)}) %reduce-scatter.65.cloned.1.call-update) | async-done | bytes 786448 | tf_op jit(solution)/shard_map/reduce_scatter | solution.py:477
  2396.8 35.3 %reduce-scatter.75.cloned.1.call-done = f32[192,6]{1,0:T(8,128)} async-done(((f32[1536,6]{1,0:T(8,128)}), f32[192,6]{1,0:T(8,128)}) %reduce-scatter.75.cloned.1.call-update) | async-done | bytes 4624
  2482.5 74.4 %all-reduce.35.cloned.1.call-done = (f32[256,1536]{1,0:T(8,128)}, f32[256,1536]{1,0:T(8,128)}) async-done(((f32[256,1536]{1,0:T(8,128)}, f32[256,1536]{1,0:T(8,128)}), (f32[256,1536]{1,0:T(8,128)}, f32[256,1536]{1,0:T(8,128)})) %all-reduce.35.cloned.1.call-update) | async-done | bytes 3145744 | tf_op jit(solution)/shard_map/psum | solution.py:297
  2875.1 61.0 %all-gather.95.cloned.1.call-done = f32[1024,768]{0,1:T(8,128)} async-done(((f32[1024,192]{0,1:T(8,128)}), f32[1024,768]{0,1:T(8,128)}) %all-gather.95.cloned.1.call-update) | async-done | bytes 3145744 | tf_op jit(solution)/shard_map/all_gather | solution.py:492
  2936.1 63.7 %all-gather.93.cloned.1.call-done = f32[1024,768]{0,1:T(8,128)} async-done(((f32[1024,192]{0,1:T(8,128)}), f32[1024,768]{0,1:T(8,128)}) %all-gather.93.cloned.1.call-update) | async-done | bytes 3145744 | tf_op jit(solution)/shard_map/all_gather | solution.py:492
  3013.2 50.4 %all-gather.87.cloned.1.call-done = f32[768,1024]{1,0:T(8,128)} async-done(((f32[192,1024]{1,0:T(8,128)}), f32[768,1024]{1,0:T(8,128)}) %all-gather.87.cloned.1.call-update) | async-done | bytes 3145744 | tf_op jit(solution)/shard_map/all_gather | solution.py:490
  3063.6 63.8 %all-gather.85.cloned.1.call-done = f32[768,1024]{1,0:T(8,128)} async-done(((f32[192,1024]{1,0:T(8,128)}), f32[768,1024]{1,0:T(8,128)}) %all-gather.85.cloned.1.call-update) | async-done | bytes 3145744 | tf_op jit(solution)/shard_map/all_gather | solution.py:490
  3134.1 57.2 %all-gather.91.cloned.1.call-done = f32[768,1024]{1,0:T(8,128)} async-done(((f32[192,1024]{1,0:T(8,128)}), f32[768,1024]{1,0:T(8,128)}) %all-gather.91.cloned.1.call-update) | async-done | bytes 3145744 | tf_op jit(solution)/shard_map/all_gather | solution.py:491
  3191.3 63.7 %all-gather.89.cloned.1.call-done = f32[768,1024]{1,0:T(8,128)} async-done(((f32[192,1024]{1,0:T(8,128)}), f32[768,1024]{1,0:T(8,128)}) %all-gather.89.cloned.1.call-update) | async-done | bytes 3145744 | tf_op jit(solution)/shard_map/all_gather | solution.py:491
  (1085 shorter events, 1217.8 us)
Async XLA Ops:
  968.5 307.8 %reduce-scatter.41.cloned.1.call-start = ((), (), s32[]{:S(2)}) async-start(), calls=%async_computation.36 | async-start | bytes 2654208 | tf_op jit(solution)/shard_map/reduce_scatter | solution.py:467
  971.7 360.0 %reduce-scatter.55.cloned.1.call-start = ((), (), s32[]{:S(2)}) async-start(), calls=%async_computation.50 | async-start | bytes 2654208 | tf_op jit(solution)/shard_map/reduce_scatter | solution.py:470
  974.6 412.6 %reduce-scatter.53.cloned.1.call-start = ((), (), s32[]{:S(2)}) async-start(), calls=%async_computation.48 | async-start | bytes 2654208 | tf_op jit(solution)/shard_map/reduce_scatter | solution.py:470
  977.6 465.6 %reduce-scatter.47.cloned.1.call-start = ((), (), s32[]{:S(2)}) async-start(), calls=%async_computation.42 | async-start | bytes 2654208 | tf_op jit(solution)/shard_map/reduce_scatter | solution.py:468
  980.6 518.5 %reduce-scatter.45.cloned.1.call-start = ((), (), s32[]{:S(2)}) async-start(), calls=%async_computation.40 | async-start | bytes 2654208 | tf_op jit(solution)/shard_map/reduce_scatter | solution.py:468
  996.5 558.6 %reduce-scatter.51.cloned.1.call-start = ((), (), s32[]{:S(2)}) async-start(), calls=%async_computation.46 | async-start | bytes 2654208 | tf_op jit(solution)/shard_map/reduce_scatter | solution.py:469
  999.5 611.1 %reduce-scatter.49.cloned.1.call-start = ((), (), s32[]{:S(2)}) async-start(), calls=%async_computation.44 | async-start | bytes 2654208 | tf_op jit(solution)/shard_map/reduce_scatter | solution.py:469
  1033.5 706.3 %reduce-scatter.71.cloned.1.call-start = ((), (), s32[]{:S(2)}) async-start(), calls=%async_computation.66 | async-start | bytes 7077888 | tf_op jit(solution)/shard_map/reduce_scatter | solution.py:478
  1038.5 832.1 %reduce-scatter.69.cloned.1.call-start = ((), (), s32[]{:S(2)}) async-start(), calls=%async_computation.64 | async-start | bytes 7077888 | tf_op jit(solution)/shard_map/reduce_scatter | solution.py:478
  1044.7 957.1 %reduce-scatter.63.cloned.1.call-start = ((), (), s32[]{:S(2)}) async-start(), calls=%async_computation.58 | async-start | bytes 7077888 | tf_op jit(solution)/shard_map/reduce_scatter | solution.py:476
  1049.7 1083.4 %reduce-scatter.61.cloned.1.call-start = ((), (), s32[]{:S(2)}) async-start(), calls=%async_computation.56 | async-start | bytes 7077888 | tf_op jit(solution)/shard_map/reduce_scatter | solution.py:476
  1055.5 1208.6 %reduce-scatter.67.cloned.1.call-start = ((), (), s32[]{:S(2)}) async-start(), calls=%async_computation.62 | async-start | bytes 7077888 | tf_op jit(solution)/shard_map/reduce_scatter | solution.py:477
  1060.4 1334.5 %reduce-scatter.65.cloned.1.call-start = ((), (), s32[]{:S(2)}) async-start(), calls=%async_computation.60 | async-start | bytes 7077888 | tf_op jit(solution)/shard_map/reduce_scatter | solution.py:477
  1065.0 1367.1 %reduce-scatter.75.cloned.1.call-start = ((), (), s32[]{:S(2)}) async-start(), calls=%async_computation.85 | async-start | bytes 884736
  1071.4 1396.3 %reduce-scatter.73.cloned.1.call-start = ((), (), s32[]{:S(2)}) async-start(), calls=%async_computation.84 | async-start | bytes 884736
  1090.1 1466.9 %all-reduce.35.cloned.1.call-start = ((), (), s32[]{:S(2)}) async-start(), calls=%async_computation.86 | async-start | bytes 6291456 | tf_op jit(solution)/shard_map/psum | solution.py:297
  1095.8 1535.9 %all-gather.83.cloned.1.call-start = ((), (), s32[]{:S(2)}) async-start(), calls=%async_computation.55 | async-start | bytes 1474560 | tf_op jit(solution)/shard_map/all_gather | solution.py:485
  1108.8 1522.8 %all-gather.81.cloned.1.call-start = ((), (), s32[]{:S(2)}) async-start(), calls=%async_computation.53 | async-start | bytes 1474560 | tf_op jit(solution)/shard_map/all_gather | solution.py:485
  1164.1 1489.4 %all-gather.67.cloned.1.call-start = ((), (), s32[]{:S(2)}) async-start(), calls=%async_computation.39 | async-start | bytes 1474560 | tf_op jit(solution)/shard_map/all_gather | solution.py:481
  1220.2 1464.4 %all-gather.65.cloned.1.call-start = ((), (), s32[]{:S(2)}) async-start(), calls=%async_computation.37 | async-start | bytes 1474560 | tf_op jit(solution)/shard_map/all_gather | solution.py:481
  1276.3 1439.5 %all-gather.79.cloned.1.call-start = ((), (), s32[]{:S(2)}) async-start(), calls=%async_computation.51 | async-start | bytes 1474560 | tf_op jit(solution)/shard_map/all_gather | solution.py:484
  1331.7 1415.3 %all-gather.77.cloned.1.call-start = ((), (), s32[]{:S(2)}) async-start(), calls=%async_computation.49 | async-start | bytes 1474560 | tf_op jit(solution)/shard_map/all_gather | solution.py:484
  1387.2 1391.0 %all-gather.71.cloned.1.call-start = ((), (), s32[]{:S(2)}) async-start(), calls=%async_computation.43 | async-start | bytes 1474560 | tf_op jit(solution)/shard_map/all_gather | solution.py:482
  1443.3 1366.2 %all-gather.69.cloned.1.call-start = ((), (), s32[]{:S(2)}) async-start(), calls=%async_computation.41 | async-start | bytes 1474560 | tf_op jit(solution)/shard_map/all_gather | solution.py:482
  1499.2 1341.5 %all-gather.75.cloned.1.call-start = ((), (), s32[]{:S(2)}) async-start(), calls=%async_computation.47 | async-start | bytes 1474560 | tf_op jit(solution)/shard_map/all_gather | solution.py:483
  1555.1 1316.8 %all-gather.73.cloned.1.call-start = ((), (), s32[]{:S(2)}) async-start(), calls=%async_computation.45 | async-start | bytes 1474560 | tf_op jit(solution)/shard_map/all_gather | solution.py:483
  1610.6 1325.4 %all-gather.95.cloned.1.call-start = ((), (), s32[]{:S(2)}) async-start(), calls=%async_computation.67 | async-start | bytes 3932160 | tf_op jit(solution)/shard_map/all_gather | solution.py:492
  1739.9 1259.9 %all-gather.93.cloned.1.call-start = ((), (), s32[]{:S(2)}) async-start(), calls=%async_computation.65 | async-start | bytes 3932160 | tf_op jit(solution)/shard_map/all_gather | solution.py:492
  1870.6 1193.0 %all-gather.87.cloned.1.call-start = ((), (), s32[]{:S(2)}) async-start(), calls=%async_computation.59 | async-start | bytes 3932160 | tf_op jit(solution)/shard_map/all_gather | solution.py:490
  2001.8 1125.6 %all-gather.85.cloned.1.call-start = ((), (), s32[]{:S(2)}) async-start(), calls=%async_computation.57 | async-start | bytes 3932160 | tf_op jit(solution)/shard_map/all_gather | solution.py:490
  2133.1 1058.2 %all-gather.91.cloned.1.call-start = ((), (), s32[]{:S(2)}) async-start(), calls=%async_computation.63 | async-start | bytes 3932160 | tf_op jit(solution)/shard_map/all_gather | solution.py:491
  2264.2 990.7 %all-gather.89.cloned.1.call-start = ((), (), s32[]{:S(2)}) async-start(), calls=%async_computation.61 | async-start | bytes 3932160 | tf_op jit(solution)/shard_map/all_gather | solution.py:491
  (237 other events, 6992.9 us)
Sparse Core Ops, SparseCore 0:
  148.2 60.0 all-reduce.22
  257.9 62.0 all-reduce.24
  446.6 58.7 all-reduce.26
  544.6 62.0 all-reduce.28
  766.9 59.8 all-reduce.30
  838.6 60.8 all-reduce.32
  958.0 35.2 reduce-scatter.34
  996.1 34.2 reduce-scatter.36
  1056.2 52.5 reduce-scatter.58
  1110.9 53.1 reduce-scatter.56
  1167.0 53.1 reduce-scatter.42
  1223.1 53.1 reduce-scatter.40
  1278.5 53.1 reduce-scatter.54
  1334.0 53.1 reduce-scatter.52
  1390.1 53.1 reduce-scatter.46
  1446.0 53.1 reduce-scatter.44
  1501.9 53.1 reduce-scatter.50
  1557.4 53.1 reduce-scatter.48
  1612.8 127.0 reduce-scatter.70
  1742.2 128.3 reduce-scatter.68
  1873.4 128.3 reduce-scatter.62
  2004.7 128.3 reduce-scatter.60
  2135.8 128.3 reduce-scatter.66
  2266.5 128.3 reduce-scatter.64
  2397.6 34.5 reduce-scatter.74
  2470.6 86.2 all-reduce.34
  2873.4 62.6 all-gather.94
  2937.6 62.1 all-gather.92
  3001.4 62.1 all-gather.86
  3065.2 62.1 all-gather.84
  3129.1 62.1 all-gather.90
  3192.8 62.1 all-gather.88
  (31 shorter events, 621.4 us)
where the time goes:
time: 3280 us; the launch traced here: 3270 us
  waiting for transfers between devices  2530 us (77%)
  matrix products  254 us (8%)
  blocking collectives  241 us (7%)
  local copies, waits for them, and re-layouts  119 us (4%)
  other arithmetic  99.7 us (3%)
    reduce_scatter x2, waiting for transfers between devices, local(): lax.psum_scatter(grad_gate_w, ('fsdp', 'context'), scatter_dimension=0, t...  262 us
    reduce_scatter x2, waiting for transfers between devices, local(): lax.psum_scatter(grad_up_w, ('fsdp', 'context'), scatter_dimension=0, til...  262 us
    reduce_scatter x2, waiting for transfers between devices, local(): lax.psum_scatter(grad_down_w, ('fsdp', 'context'), scatter_dimension=1, t...  260 us
    psum x2, waiting for transfers between devices, local(): lax.psum(jnp.dot(inner_low, gathered[10], preferred_element_type=jnp.floa...  129 us
    all_gather x2, waiting for transfers between devices, local(): lax.all_gather(shares[11], 'context', axis=1, tiled=True)  125 us
    psum x2, waiting for transfers between devices, local(): lax.psum(jnp.einsum('rf,df->rd', grad_gate_low, gathered[8], preferred_el...  123 us
    all_gather x2, waiting for transfers between devices, local(): lax.all_gather(shares[10], 'context', axis=0, tiled=True)  121 us
    all_gather x2, waiting for transfers between devices, local(): lax.all_gather(shares[9], 'context', axis=0, tiled=True)  114 us
  transfers between devices with their start and end apart: 63, of which 49 were waited for; matrix products, arithmetic and copies ran while one was open for 8% of the time, Pallas kernels for 0%

commit v1 on v0

v1 whole, which is shorter than its diff:
```python
import functools

import jax
import jax.numpy as jnp
from jax import lax
from jax.experimental import pallas as pl
from jax.experimental.pallas import tpu as pltpu
from jax.sharding import PartitionSpec as P

epsilon = 1e-06
masked_value = -1e30
bf16 = jnp.bfloat16
f32 = jnp.float32


def query_rows(seq_len):
    return 256 if seq_len <= 2048 else 128


def swap(x, axis, k):
    n = lax.axis_size(axis)
    return lax.ppermute(x, axis, [(i, i ^ k) for i in range(n)])


def tensor_blocks(shard):
    return [shard] + [swap(shard, "tensor", k) for k in range(1, lax.axis_size("tensor"))]


def remote_blocks(shard):
    blocks = []
    for kz in range(1, lax.axis_size("context")):
        blocks += tensor_blocks(swap(shard, "context", kz))
    return blocks


def own_rows(shard):
    return jnp.concatenate(tensor_blocks(shard), axis=0)


def remote_rows(own, piece_index):
    count = lax.axis_size("context")
    rows, width = own.shape
    if count <= 4:
        block = rows // lax.axis_size("tensor")
        return jnp.concatenate(remote_blocks(own[:block]), axis=0)
    everything = lax.all_gather(own, "context")
    return jnp.concatenate(
        [lax.dynamic_index_in_dim(everything, piece_index ^ k, 0, False) for k in range(1, count)],
        axis=0,
    )


def scatter_sum(partial):
    count = lax.axis_size("tensor")
    block = partial.shape[0] // count
    total = partial[:block]
    for k in range(1, count):
        low = partial[k * block : (k + 1) * block].astype(bf16)
        total = total + swap(low, "tensor", k).astype(f32)
    return total


def sum_over(x, axis):
    total = x
    for k in range(1, lax.axis_size(axis)):
        total = total + swap(x, axis, k)
    return total


def block_place(j, place_ref, count_tensor, block):
    kz, kt = j // count_tensor, j % count_tensor
    at = ((kz ^ place_ref[0]) * count_tensor + (kt ^ place_ref[1])) * block
    return pl.multiple_of(at, block)


def shifted_sum(x, reverse):
    rows = x.shape[0]
    row = lax.broadcasted_iota(jnp.int32, x.shape, 0)
    step = 1
    while step < rows:
        if reverse:
            moved = jnp.where(row < rows - step, pltpu.roll(x, rows - step, 0), 0.0)
        else:
            moved = jnp.where(row >= step, pltpu.roll(x, step, 0), 0.0)
        x = x + moved
        step *= 2
    return x


def three_parts(x):
    high = x.astype(bf16)
    rest = x - high.astype(f32)
    middle = rest.astype(bf16)
    lowest = (rest - middle.astype(f32)).astype(bf16)
    return high.astype(f32), middle.astype(f32), lowest.astype(f32)


def head_column(table, head):
    lane = lax.broadcasted_iota(jnp.int32, table.shape, 1)
    return jnp.sum(jnp.where(lane == head, table, 0.0), axis=1, keepdims=True)


def key_windows(seq_len, rows):
    most = seq_len // 2
    found = []
    for start in range(0, seq_len, rows):
        first = max(0, start - (most // rows) * rows)
        found.append((start, first, start + rows))
    return found


def pair_setup(refs, scratch, place_ref, pair, count_tensor, block):
    q_ref, k_ref, v_ref = refs
    qa, qb, ka, kb, vv, decay = scratch
    seq_len = q_ref.shape[0]
    rows = query_rows(seq_len)

    def move(j, carry):
        at = block_place(j, place_ref, count_tensor, block)
        here = pl.ds(pl.multiple_of(j * block, block), block)
        qa[pl.ds(at, block), :] = q_ref[here, :]
        ka[pl.ds(at, block), :] = k_ref[here, :]
        vv[pl.ds(at, block), :] = v_ref[here, :]
        return carry

    lax.fori_loop(0, seq_len // block, move, 0)

    def mix(i, carry):
        here = pl.ds(pl.multiple_of(i * rows, rows), rows)
        lane = lax.broadcasted_iota(jnp.int32, (rows, 128), 1)
        table = decay[here, :]
        q = qa[here, :].astype(f32) * 0.125
        k = ka[here, :].astype(f32)
        for head, (q_out, k_out, first, mine) in enumerate(
            ((qa, ka, 64, lane < 64), (qb, kb, 0, lane >= 64))
        ):
            c = head_column(table, 2 * pair + head)
            high, middle, lowest = three_parts(c)
            spot = lane - first
            split = jnp.where(
                (spot == 0) | (spot == 3),
                high,
                jnp.where((spot == 1) | (spot == 4), middle, lowest),
            )
            low_spot = (spot >= 0) & (spot < 3)
            high_spot = (spot >= 3) & (spot < 6)
            key_side = jnp.where(low_spot, -split, jnp.where(high_spot, 1.0, 0.0))
            query_side = jnp.where(low_spot, 1.0, jnp.where(high_spot, split, 0.0))
            q_out[here, :] = jnp.where(mine, q, query_side).astype(bf16)
            k_out[here, :] = jnp.where(mine, k, key_side).astype(bf16)
        return carry

    lax.fori_loop(0, seq_len // rows, mix, 0)


def gather_decay(keep_ref, decay, place_ref, count_tensor, block):
    seq_len = keep_ref.shape[0]

    def move(j, carry):
        at = block_place(j, place_ref, count_tensor, block)
        decay[pl.ds(at, block), :] = keep_ref[pl.ds(pl.multiple_of(j * block, block), block), :]
        return carry

    lax.fori_loop(0, seq_len // block, move, 0)
    decay[...] = shifted_sum(decay[...], False)


def live_mask(start_ref, start, first, width, rows):
    key_pos = first + lax.broadcasted_iota(jnp.int32, (rows, width), 1)
    query_pos = start + lax.broadcasted_iota(jnp.int32, (rows, width), 0)
    doc_start = start_ref[pl.ds(start, rows), :]
    return (key_pos <= query_pos) & (key_pos >= doc_start)


def over_query_blocks(seq_len, rows, body):
    windows = key_windows(seq_len, rows)
    if len(windows) <= 4:
        for start, first, end in windows:
            body(start, first, end - first)
        return
    width = windows[-1][2] - windows[-1][1]

    def one(i, carry):
        start = pl.multiple_of(i * rows, rows)
        first = pl.multiple_of(jnp.maximum(start + rows - width, 0), rows)
        body(start, first, width)
        return carry

    lax.fori_loop(0, len(windows), one, 0)


nt_dims = (((1,), (1,)), ((), ()))
tn_dims = (((0,), (0,)), ((), ()))


def dot_nt(a, b):
    return lax.dot_general(a, b, nt_dims, preferred_element_type=f32)


def dot_tn(a, b):
    return lax.dot_general(a, b, tn_dims, preferred_element_type=f32)


def dot_nn(a, b):
    return jnp.dot(a, b, preferred_element_type=f32)


def probabilities(q_rows, k_rows, mask):
    s = jnp.where(mask, dot_nt(q_rows, k_rows), masked_value)
    e = jnp.exp(s - jnp.max(s, axis=1, keepdims=True))
    return e * (1.0 / jnp.sum(e, axis=1, keepdims=True))


def forward_kernel(
    count_tensor, block,
    place_ref, q_ref, k_ref, v_ref, gate_ref, keep_ref, start_ref,
    o_ref, u_ref,
    qa, qb, ka, kb, vv, decay, oo,
):
    pair = pl.program_id(0)
    seq_len, rows = q_ref.shape[0], query_rows(q_ref.shape[0])

    @pl.when(pair == 0)
    def _():
        gather_decay(keep_ref, decay, place_ref, count_tensor, block)

    pair_setup((q_ref, k_ref, v_ref), (qa, qb, ka, kb, vv, decay), place_ref, pair, count_tensor, block)
    lane = lax.broadcasted_iota(jnp.int32, (rows, 128), 1)

    def body(start, first, width):
        mask = live_mask(start_ref, start, first, width, rows)
        here, keys = pl.ds(start, rows), pl.ds(first, width)
        values = vv[keys, :]
        out = []
        for q_of, k_of in ((qa, ka), (qb, kb)):
            p = probabilities(q_of[here, :], k_of[keys, :], mask).astype(bf16)
            out.append(dot_nn(p, values))
        oo[here, :] = jnp.where(lane < 64, out[0], out[1])

    over_query_blocks(seq_len, rows, body)

    def move(j, carry):
        at = block_place(j, place_ref, count_tensor, block)
        here = pl.ds(pl.multiple_of(j * block, block), block)
        o = oo[pl.ds(at, block), :]
        o_ref[here, :] = o
        u_ref[here, :] = (o * jax.nn.sigmoid(gate_ref[here, :])).astype(bf16)
        return carry

    lax.fori_loop(0, seq_len // block, move, 0)


def backward_kernel(
    count_tensor, block,
    place_ref, q_ref, k_ref, v_ref, gate_ref, keep_ref, start_ref, o_ref, du_ref, forget_ref,
    dq_ref, dk_ref, dv_ref, dg_ref, dz_ref,
    qa, qb, ka, kb, vv, decay, dd, dqs, dka, dkb, dva, dcs,
):
    pair = pl.program_id(0)
    seq_len, rows = q_ref.shape[0], query_rows(q_ref.shape[0])
    blocks = seq_len // block

    @pl.when(pair == 0)
    def _():
        gather_decay(keep_ref, decay, place_ref, count_tensor, block)
        dcs[...] = jnp.zeros_like(dcs)

    pair_setup((q_ref, k_ref, v_ref), (qa, qb, ka, kb, vv, decay), place_ref, pair, count_tensor, block)

    def gates(j, carry):
        at = block_place(j, place_ref, count_tensor, block)
        here = pl.ds(pl.multiple_of(j * block, block), block)
        sig = jax.nn.sigmoid(gate_ref[here, :])
        du = du_ref[here, :]
        dd[pl.ds(at, block), :] = (du * sig).astype(bf16)
        dg_ref[here, :] = (du * o_ref[here, :] * sig * (1.0 - sig)).astype(bf16)
        return carry

    lax.fori_loop(0, blocks, gates, 0)
    dka[...] = jnp.zeros_like(dka)
    dkb[...] = jnp.zeros_like(dkb)
    dva[...] = jnp.zeros_like(dva)
    lane = lax.broadcasted_iota(jnp.int32, (rows, 128), 1)
    lane8 = lax.broadcasted_iota(jnp.int32, (rows, 8), 1)

    def pick(column_a, column_b):
        return jnp.where(lane8 == 2 * pair, column_a, jnp.where(lane8 == 2 * pair + 1, column_b, 0.0))

    def body(start, first, width):
        mask = live_mask(start_ref, start, first, width, rows)
        here, keys = pl.ds(start, rows), pl.ds(first, width)
        values = vv[keys, :]
        d_rows = dd[here, :]
        dq = []
        for head, (q_of, k_of, dk_of) in enumerate(((qa, ka, dka), (qb, kb, dkb))):
            mine = (lane < 64) if head == 0 else (lane >= 64)
            p = probabilities(q_of[here, :], k_of[keys, :], mask)
            d_mine = jnp.where(mine, d_rows, jnp.zeros_like(d_rows))
            dp = dot_nt(d_mine, values)
            delta = jnp.sum(p * dp, axis=1, keepdims=True)
            ds = (p * (dp - delta)).astype(bf16)
            dq.append(dot_nn(ds, k_of[keys, :]))
            dk_of[keys, :] += dot_tn(ds, q_of[here, :])
            dva[keys, :] += dot_tn(p.astype(bf16), d_mine)
        dqs[here, :] = jnp.where(lane < 64, dq[0], dq[1]) * 0.125
        dcs[here, :] += pick(dq[0][:, 67:68], dq[1][:, 3:4])

    over_query_blocks(seq_len, rows, body)

    def columns(i, carry):
        here = pl.ds(pl.multiple_of(i * rows, rows), rows)
        dcs[here, :] -= pick(dka[here, 64:65], dkb[here, 0:1])
        return carry

    lax.fori_loop(0, seq_len // rows, columns, 0)

    def move(j, carry):
        at = pl.ds(block_place(j, place_ref, count_tensor, block), block)
        here = pl.ds(pl.multiple_of(j * block, block), block)
        small = lax.broadcasted_iota(jnp.int32, (block, 128), 1)
        dq_ref[here, :] = dqs[at, :].astype(bf16)
        dk_ref[here, :] = jnp.where(small < 64, dka[at, :], dkb[at, :]).astype(bf16)
        dv_ref[here, :] = dva[at, :].astype(bf16)
        return carry

    lax.fori_loop(0, blocks, move, 0)

    @pl.when(pair == pl.num_programs(0) - 1)
    def _():
        dcs[...] = shifted_sum(dcs[...], True)

        def last(j, carry):
            at = pl.ds(block_place(j, place_ref, count_tensor, block), block)
            here = pl.ds(pl.multiple_of(j * block, block), block)
            dz_ref[here, :] = (dcs[at, :] * jax.nn.sigmoid(-forget_ref[here, :])).astype(bf16)
            return carry

        lax.fori_loop(0, blocks, last, 0)


def lanes(seq_len, at):
    return pl.BlockSpec((seq_len, 128), lambda p, place: (0, p + at))


def whole(seq_len, width):
    return pl.BlockSpec((seq_len, width), lambda p, place: (0, 0))


def attention_forward(place, qkv, gate, keep, doc_start, count_tensor, block):
    seq_len, width = gate.shape
    pairs = width // 128
    low = pltpu.VMEM((seq_len, 128), bf16)
    return pl.pallas_call(
        functools.partial(forward_kernel, count_tensor, block),
        grid_spec=pltpu.PrefetchScalarGridSpec(
            num_scalar_prefetch=1,
            grid=(pairs,),
            in_specs=[
                lanes(seq_len, 0), lanes(seq_len, pairs), lanes(seq_len, 2 * pairs), lanes(seq_len, 0),
                whole(seq_len, 8), whole(seq_len, 1),
            ],
            out_specs=[lanes(seq_len, 0), lanes(seq_len, 0)],
            scratch_shapes=[low] * 5 + [pltpu.VMEM((seq_len, 8), f32), pltpu.VMEM((seq_len, 128), f32)],
        ),
        out_shape=[
            jax.ShapeDtypeStruct((seq_len, width), f32),
            jax.ShapeDtypeStruct((seq_len, width), bf16),
        ],
        compiler_params=pltpu.CompilerParams(vmem_limit_bytes=48 << 20),
    )(place, qkv, qkv, qkv, gate, keep, doc_start)


def attention_backward(place, qkv, gate, keep, doc_start, o, du, forget, count_tensor, block):
    seq_len, width = gate.shape
    pairs = width // 128
    low, high = pltpu.VMEM((seq_len, 128), bf16), pltpu.VMEM((seq_len, 128), f32)
    small = pltpu.VMEM((seq_len, 8), f32)
    wide = jax.ShapeDtypeStruct((seq_len, width), bf16)
    return pl.pallas_call(
        functools.partial(backward_kernel, count_tensor, block),
        grid_spec=pltpu.PrefetchScalarGridSpec(
            num_scalar_prefetch=1,
            grid=(pairs,),
            in_specs=[
                lanes(seq_len, 0), lanes(seq_len, pairs), lanes(seq_len, 2 * pairs), lanes(seq_len, 0),
                whole(seq_len, 8), whole(seq_len, 1), lanes(seq_len, 0), lanes(seq_len, 0), whole(seq_len, 8),
            ],
            out_specs=[lanes(seq_len, 0)] * 4 + [whole(seq_len, 8)],
            scratch_shapes=[low] * 5 + [small] + [low] + [high] * 4 + [small],
        ),
        out_shape=[wide, wide, wide, wide, jax.ShapeDtypeStruct((seq_len, 8), bf16)],
        compiler_params=pltpu.CompilerParams(vmem_limit_bytes=56 << 20),
    )(place, qkv, qkv, qkv, gate, keep, doc_start, o, du, forget)


def inverse_rms(h):
    return lax.rsqrt(jnp.mean(h * h, axis=-1, keepdims=True) + epsilon)


def norm_back(grad_normed, hidden, inverse, gain):
    scaled = hidden * inverse
    weighted = grad_normed * gain
    grad_gain = jnp.sum(grad_normed * scaled, axis=0)
    mean = jnp.mean(weighted * scaled, axis=-1, keepdims=True)
    return inverse * (weighted - scaled * mean), grad_gain


def local(
    hidden_in, segment_ids, w_query, w_key, w_value, w_gate_out, w_attn_out, w_forget, b_forget,
    gain_attn, gain_ffn, w_gate, w_up, w_down, cotangent,
):
    seq_count, piece_len, width = hidden_in.shape
    count_z, count_t = lax.axis_size("context"), lax.axis_size("tensor")
    core, z, t = lax.axis_index("fsdp"), lax.axis_index("context"), lax.axis_index("tensor")
    layers, half, local_width = w_query.shape
    heads = w_forget.shape[2]
    block = piece_len // count_t
    seq_len = piece_len * count_z
    place = jnp.stack([z, t]).astype(jnp.int32)
    shared_rows = count_z <= 4

    def features(x):
        return jnp.where(core == 0, x, jnp.concatenate([x[..., half:], x[..., :half]], axis=-1))

    def rows_by_place(x):
        parts = x.reshape(count_t, block, x.shape[-1])
        return jnp.concatenate(
            [lax.dynamic_index_in_dim(parts, k ^ t, 0, False) for k in range(count_t)], axis=0
        )

    def full(w, axis):
        return jnp.concatenate([w, swap(w, "fsdp", 1)], axis=axis)

    segments = segment_ids.reshape(piece_len)
    if count_z <= 4:
        pieces = jnp.stack([segments] + [swap(segments, "context", k) for k in range(1, count_z)])
        seg_all = jnp.concatenate(
            [lax.dynamic_index_in_dim(pieces, k ^ z, 0, False) for k in range(count_z)]
        )
    else:
        seg_all = lax.all_gather(segments, "context", tiled=True)
    doc_start = jnp.sum((seg_all[None, :] < seg_all[:, None]).astype(jnp.int32), axis=1, keepdims=True)

    gains = jnp.concatenate([gain_attn, gain_ffn], axis=0)
    gains = full(gains, 1).astype(f32)
    w_forget_full = full(w_forget, 1)

    hidden_rows = rows_by_place(features(hidden_in.reshape(piece_len, width)).astype(f32))
    hidden = hidden_rows[:block]
    saved = []
    for layer in range(layers):
        w_qkvg = full(
            jnp.concatenate([w_query[layer], w_key[layer], w_value[layer], w_gate_out[layer]], axis=1), 0
        )
        w_out = full(w_attn_out[layer], 1)
        wg, wu, wd = full(w_gate[layer], 0), full(w_up[layer], 0), full(w_down[layer], 1)
        gain_one, gain_two = gains[layer], gains[layers + layer]
        inverse_one = inverse_rms(hidden)
        if layer == 0:
            own_a = (hidden_rows * inverse_rms(hidden_rows) * gain_one).astype(bf16)
        else:
            own_a = own_rows((hidden * inverse_one * gain_one).astype(bf16))
        a = jnp.concatenate([own_a, remote_rows(own_a, z)], axis=0)
        qkv = dot_nn(a, w_qkvg[:, : 3 * local_width]).astype(bf16)
        gate = dot_nn(a, w_qkvg[:, 3 * local_width :])
        forget = dot_nn(a, w_forget_full[layer]) + b_forget[layer]
        forget = jnp.pad(forget, ((0, 0), (0, 8 - heads)))
        keep = jax.nn.log_sigmoid(forget)
        o, u = attention_forward(place, qkv, gate, keep, doc_start, count_t, block)
        mixed = hidden + scatter_sum(dot_nn(u[:piece_len], w_out))
        inverse_two = inverse_rms(mixed)
        own_b = own_rows((mixed * inverse_two * gain_two).astype(bf16))
        gt, up = dot_nn(own_b, wg), dot_nn(own_b, wu)
        inner = (jax.nn.silu(gt) * up).astype(bf16)
        total = mixed + scatter_sum(dot_nn(inner, wd))
        saved.append(
            (w_qkvg, w_out, wg, wu, wd, gain_one, gain_two, hidden, inverse_one, a, qkv, gate, forget, keep,
             o, u, mixed, inverse_two, own_b, gt, up)
        )
        hidden = total

    def finish(x):
        return features(rows_by_place(own_rows(x.astype(bf16)))).reshape(1, piece_len, width)

    output = finish(hidden)

    cotangent_rows = rows_by_place(features(cotangent.reshape(piece_len, width)))
    grad = cotangent_rows[:block].astype(f32)
    results = [None] * layers
    gain_grads = [None] * (2 * layers)

    def exchange(mine, theirs):
        return mine + swap(theirs, "fsdp", 1).astype(f32)

    for layer in reversed(range(layers)):
        (w_qkvg, w_out, wg, wu, wd, gain_one, gain_two, hidden, inverse_one, a, qkv, gate, forget, keep,
         o, u, mixed, inverse_two, own_b, gt, up) = saved[layer]
        own_g = cotangent_rows if layer == layers - 1 else own_rows(grad.astype(bf16))

        def inner_grads(dm, gt, up):
            sig = jax.nn.sigmoid(gt)
            d_gate = (dm * up * sig * (1.0 + gt * (1.0 - sig))).astype(bf16)
            return d_gate, (dm * (gt * sig)).astype(bf16)

        d_gate, d_up = inner_grads(dot_nt(own_g, wd), gt, up)
        grad_b = scatter_sum(dot_nt(d_gate, wg) + dot_nt(d_up, wu))
        back, gain_grads[layers + layer] = norm_back(grad_b, mixed, inverse_two, gain_two)
        grad_mixed = grad + back
        own_y = own_rows(grad_mixed.astype(bf16))
        y = jnp.concatenate([own_y, remote_rows(own_y, z)], axis=0)
        du = dot_nt(y, w_out)
        dq, dk, dv, dg, dz = attention_backward(
            place, qkv, gate, keep, doc_start, o, du, forget, count_t, block
        )
        d_all = jnp.concatenate([dq, dk, dv, dg], axis=1)
        grad_a = scatter_sum(
            dot_nt(d_all[:piece_len], w_qkvg) + dot_nt(dz[:piece_len, :heads], w_forget_full[layer])
        )
        back, gain_grads[layer] = norm_back(grad_a, hidden, inverse_one, gain_one)
        grad = grad_mixed + back

        if shared_rows:
            b = jnp.concatenate([own_b, remote_rows(own_b, z)], axis=0)
            g = jnp.concatenate([own_g, remote_rows(own_g, z)], axis=0)
            gt_all, up_all = dot_nn(b, wg), dot_nn(b, wu)
            m_all = (jax.nn.silu(gt_all) * up_all).astype(bf16)
            d_gate_all, d_up_all = inner_grads(dot_nt(g, wd), gt_all, up_all)
        else:
            b, g, d_gate_all, d_up_all = own_b, own_g, d_gate, d_up
            m_all = (jax.nn.silu(gt) * up).astype(bf16)

        def by_rows(x, d):
            return exchange(dot_tn(x[:, :half], d), dot_tn(x[:, half:], d).astype(bf16))

        def by_columns(x, d):
            return exchange(dot_tn(x, d[:, :half]), dot_tn(x, d[:, half:]).astype(bf16))

        def pieces_sum(x):
            return x if shared_rows else lax.psum(x, "context")

        dzr = dz[:, :heads]
        bias = jnp.sum(dzr.astype(f32), axis=0)
        forget_theirs = dot_tn(a[:, half:], dzr)
        results[layer] = (
            by_rows(a, dq), by_rows(a, dk), by_rows(a, dv), by_rows(a, dg), by_columns(u, y),
            dot_tn(a[:, :half], dzr) + swap(forget_theirs, "fsdp", 1),
            bias + swap(bias, "fsdp", 1),
            *(pieces_sum(x) for x in (by_rows(b, d_gate_all), by_rows(b, d_up_all), by_columns(m_all, g))),
        )
    grad_input = finish(grad)
    gain_total = sum_over(sum_over(jnp.stack(gain_grads), "tensor"), "context")
    gain_total = gain_total[:, :half] + swap(gain_total[:, half:], "fsdp", 1)
    s = [jnp.stack([results[layer][k] for layer in range(layers)]) for k in range(10)]
    return (
        output, grad_input, s[0], s[1], s[2], s[3], s[4], s[5], s[6],
        gain_total[:layers], gain_total[layers:], s[7], s[8], s[9],
    )


def solution(mesh):
    rows = P("fsdp", "context", None)
    wide, tall = P(None, "fsdp", "tensor"), P(None, "tensor", "fsdp")
    heads, gain = P(None, "tensor"), P(None, "fsdp")
    return jax.shard_map(
        local,
        mesh=mesh,
        in_specs=(
            rows, P("fsdp", "context"), wide, wide, wide, wide, tall, wide, heads, gain, gain, wide, wide, tall, rows,
        ),
        out_specs=(rows, rows, wide, wide, wide, wide, tall, wide, heads, gain, gain, wide, wide, tall),
        check_vma=False,
    )
```

time: 3280 us -> 951 us (0.29)
  waiting for transfers between devices: 2530 us -> 314 us
  blocking collectives: 241 us -> 0 us
  starting transfers between devices: 2.74 us -> 236 us
  Pallas kernels: 0 us -> 103 us
  matrix products: 254 us -> 163 us
  local copies, waits for them, and re-layouts: 119 us -> 44.3 us
    reduce_scatter x22 -> x0, waiting for transfers between devices: 1410 us -> none  [the longest x2 262 us: local(): lax.psum_scatter(grad_gate_w, ('fsdp', 'context'), scatter_dimension=0, t...]
    all_gather x32 -> x0, waiting for transfers between devices: 645 us -> none  [the longest x2 125 us: local(): lax.all_gather(shares[11], 'context', axis=1, tiled=True)]
    psum x7 -> x0, waiting for transfers between devices: 408 us -> none  [the longest x2 129 us: local(): lax.psum(jnp.dot(inner_low, gathered[10], preferred_element_type=jnp.floa...]
    ppermute x0 -> x186, waiting for transfers between devices: none -> 314 us  [swap(): return lax.ppermute(x, axis, [(i, i ^ k) for i in range(n)])]
    ppermute x0 -> x186, starting transfers between devices: none -> 236 us  [swap(): return lax.ppermute(x, axis, [(i, i ^ k) for i in range(n)])]
    all_gather x19 -> x0, blocking collectives: 174 us -> none  [the longest x2 34.7 us: local(): lax.all_gather(value_low, 'context', axis=1, tiled=True)]
    pallas_call x0 -> x4, Pallas kernels: none -> 103 us  [the longest x2 64.6 us: attention_backward(): pl.pallas_call(functools.partial(backward_kernel, count_tensor, block), g...]
    dot_general x124 -> x68, matrix products: 252 us -> 163 us  [the longest x36 66 us: dot_tn(): return lax.dot_general(a, b, tn_dims, preferred_element_type=f32)]
  transfers between devices with their start and end apart: 63 -> 186, of which waited for: 49 -> 90; matrix products, arithmetic and copies ran while one was open for 8% -> 28% of each run, Pallas kernels for 0% -> 11%
where the time goes in v1:
time: 951 us; the launch traced here: 938 us
  waiting for transfers between devices  314 us (33%)
  starting transfers between devices  236 us (25%)
  matrix products  163 us (17%)
  Pallas kernels  103 us (11%)
  other arithmetic  73.3 us (8%)
  local copies, waits for them, and re-layouts  44.3 us (5%)
    ppermute x186, waiting for transfers between devices, swap(): return lax.ppermute(x, axis, [(i, i ^ k) for i in range(n)])  314 us
    ppermute x186, starting transfers between devices, swap(): return lax.ppermute(x, axis, [(i, i ^ k) for i in range(n)])  236 us
    dot_general x36, matrix products, dot_tn(): return lax.dot_general(a, b, tn_dims, preferred_element_type=f32)  66 us
    pallas_call x2, Pallas kernels, attention_backward(): pl.pallas_call(functools.partial(backward_kernel, count_tensor, block), g...  64.6 us
    dot_general x18, matrix products, dot_nn(): return jnp.dot(a, b, preferred_element_type=f32)  60.3 us
    pallas_call x2, Pallas kernels, attention_forward(): pl.pallas_call(functools.partial(forward_kernel, count_tensor, block), gr...  38.5 us
    dot_general x14, matrix products, dot_nt(): return lax.dot_general(a, b, nt_dims, preferred_element_type=f32)  37.2 us
    concatenate x2, other arithmetic, full(): return jnp.concatenate([w, swap(w, 'fsdp', 1)], axis=axis)  36.9 us
  transfers between devices with their start and end apart: 186, of which 90 were waited for; matrix products, arithmetic and copies ran while one was open for 28% of the time, Pallas kernels for 11%

profile of v1, /device:TPU:0, one launch (start us, length us, event | category | flops | bytes accessed | tf_op | source)
XLA Modules:
  0.0 938.1 jit_solution(13552687012683675392)
XLA Ops:
  78.3 5.5 collective-permute-done.175
  143.4 5.2 collective-permute-done.8
  156.2 5.6 collective-permute-done.11
  177.0 17.6 %pad_maximum_fusion.3 = bf16[1536,1536]{1,0:T(8,128)(2,1)S(1)} fusion(bf16[768,1536]{1,0:T(8,128)(2,1)S(1)} %collective-permute-done.13, bf16[768,384]{1,0:T(8,128)(2,1)S(1)} %get-tuple-element.168, bf16[768,384]{1,0:T(8,128)(2,1)S(1)} %get-tuple-element.244, bf16[768,384]{1,0:T(8,128)(2,1)S(1)} %get-tuple-element.164, bf16[768,384]{1,0:T(8,128)(2,1)S(1)} %get-tuple-element.246), kind=kLoop, calls=%fused_computation.3 | loop fusion | flops 23592960 | bytes 9437184 | tf_op jit(solution)/shard_map/concatenate | solution.py:432
  194.6 5.5 convolution_convert_fusion.1.q_ref.k_ref.v_ref
  201.9 19.3 %shard_map.254 = (f32[1024,384]{1,0:T(8,128)S(1)}, bf16[1024,384]{1,0:T(8,128)(2,1)S(1)}) custom-call(s32[2]{0:T(128)S(1)} %pad_add_fusion.2.place_ref, bf16[1024,1152]{1,0:T(8,128)(2,1)} %convolution_convert_fusion.1.q_ref.k_ref.v_ref, bf16[1024,1152]{1,0:T(8,128)(2,1)} %convolution_convert_fusion.1.q_ref.k_ref.v_ref, ...), custom_call_target="tpu_custom_call" | custom-call | tf_op jit(solution)/shard_map/pallas_call | solution.py:353
  240.3 19.2 %pad_maximum_fusion.4 = bf16[1536,1536]{1,0:T(8,128)(2,1)S(1)} fusion(bf16[768,1536]{1,0:T(8,128)(2,1)} %collective-permute-done.46, bf16[768,384]{1,0:T(8,128)(2,1)S(1)} %copy-done.21, bf16[768,384]{1,0:T(8,128)(2,1)S(1)} %copy-done.23, bf16[768,384]{1,0:T(8,128)(2,1)S(1)} %copy-done.25, bf16[768,384]{1,0:T(8,128)(2,1)S(1)} %copy-done.27), kind=kLoop, calls=%fused_computation.4 | loop fusion | flops 23592960 | bytes 9437184 | tf_op jit(solution)/shard_map/concatenate | solution.py:432
  283.1 5.2 collective-permute-done.133
  301.8 6.1 collective-permute-done.137
  309.7 7.9 collective-permute-done.138
  333.9 5.1 collective-permute-done.33
  339.1 5.6 collective-permute-done.35
  344.8 6.1 collective-permute-done.36
  357.6 6.2 collective-permute-done.39
  364.4 5.4 collective-permute-done.40
  394.7 5.6 convolution_convert_fusion.q_ref.k_ref.v_ref
  405.5 19.2 %shard_map.255 = (f32[1024,384]{1,0:T(8,128)S(1)}, bf16[1024,384]{1,0:T(8,128)(2,1)S(1)}) custom-call(s32[2]{0:T(128)S(1)} %pad_add_fusion.2.place_ref, bf16[1024,1152]{1,0:T(8,128)(2,1)} %convolution_convert_fusion.q_ref.k_ref.v_ref, bf16[1024,1152]{1,0:T(8,128)(2,1)} %convolution_convert_fusion.q_ref.k_ref.v_ref, ...), custom_call_target="tpu_custom_call" | custom-call | tf_op jit(solution)/shard_map/pallas_call | solution.py:353
  444.8 5.9 collective-permute-start.161
  474.9 6.3 collective-permute-start.165
  501.3 8.1 fusion.80
  509.4 7.4 multiply_convert_fusion
  535.1 5.1 collective-permute-done.70
  542.9 7.2 collective-permute-done.71
  574.7 32.3 %shard_map.256 = (bf16[1024,384]{1,0:T(8,128)(2,1)}, bf16[1024,384]{1,0:T(8,128)(2,1)}, bf16[1024,384]{1,0:T(8,128)(2,1)}, bf16[1024,384]{1,0:T(8,128)(2,1)}, bf16[1024,8]{1,0:T(8,128)(2,1)}) custom-call(s32[2]{0:T(128)} %copy-done.9, bf16[1024,1152]{1,0:T(8,128)(2,1)} %convolution_convert_fusion.q_ref.k_ref.v_ref, ...), custom_call_target="tpu_custom_call" | custom-call | tf_op jit(solution)/shard_map/pallas_call | solution.py:379
  701.9 5.3 collective-permute-done.153
  721.7 7.6 multiply_convert_fusion.1
  747.4 5.2 collective-permute-done.94
  759.9 6.0 collective-permute-start.101
  778.8 6.3 collective-permute-done.100
  799.5 5.5 collective-permute-done.104
  810.2 32.3 %shard_map.257 = (bf16[1024,384]{1,0:T(8,128)(2,1)}, bf16[1024,384]{1,0:T(8,128)(2,1)}, bf16[1024,384]{1,0:T(8,128)(2,1)}, bf16[1024,384]{1,0:T(8,128)(2,1)}, bf16[1024,8]{1,0:T(8,128)(2,1)}) custom-call(s32[2]{0:T(128)} %copy-done.9, bf16[1024,1152]{1,0:T(8,128)(2,1)} %convolution_convert_fusion.1.q_ref.k_ref.v_ref, ...), custom_call_target="tpu_custom_call" | custom-call | tf_op jit(solution)/shard_map/pallas_call | solution.py:379
  877.2 6.7 collective-permute-start.130
  (904 shorter events, 636.5 us)
Async XLA Ops:
  0.7 38.0 %collective-permute-start.17 = (s32[256]{0:T(256)}, s32[256]{0:T(256)}, u32[]{:S(2)}, u32[]{:S(2)}) collective-permute-start(s32[256]{0:T(256)} %bitcast.211), channel_id=1, source_target_pairs={{0,12},{4,8},{8,4},{12,0},{1,13},{5,9},{9,5},{13,1},{2,14},{6,10},... | collective-permute-start | bytes 3080 | tf_op jit(solution)/shard_map/ppermute | solution.py:22
  5.8 33.0 %collective-permute-start.16 = (s32[256]{0:T(256)}, s32[256]{0:T(256)}, u32[]{:S(2)}, u32[]{:S(2)}) collective-permute-start(s32[256]{0:T(256)} %bitcast.212), channel_id=1, source_target_pairs={{0,8},{4,12},{8,0},{12,4},{1,9},{5,13},{9,1},{13,5},{2,10},{6,14},... | collective-permute-start | bytes 3080 | tf_op jit(solution)/shard_map/ppermute | solution.py:22
  5.8 33.0 %collective-permute-start.15 = (s32[256]{0:T(256)}, s32[256]{0:T(256)}, u32[]{:S(2)}, u32[]{:S(2)}) collective-permute-start(s32[256]{0:T(256)} %bitcast.213), channel_id=1, source_target_pairs={{0,4},{4,0},{8,12},{12,8},{1,5},{5,1},{9,13},{13,9},{2,6},{6,2},{1... | collective-permute-start | bytes 3080 | tf_op jit(solution)/shard_map/ppermute | solution.py:22
  13.6 29.9 %collective-permute-start.169 = (bf16[64,1536]{1,0:T(8,128)(2,1)S(1)}, bf16[64,1536]{1,0:T(8,128)(2,1)}, u32[]{:S(2)}, u32[]{:S(2)}) collective-permute-start(bf16[64,1536]{1,0:T(8,128)(2,1)S(1)} %get-tuple-element.122), channel_id=1, source_target_pairs={{0,4},{4,0},{8,12},{12,8},{1,5},{5,1},{9,13},{13,9},{2,6},{6,2},{1... | collective-permute-start | bytes 589832 | tf_op jit(solution)/shard_map/ppermute | solution.py:22
  14.9 51.0 %collective-permute-start.173 = (bf16[64,1536]{1,0:T(8,128)(2,1)S(1)}, bf16[64,1536]{1,0:T(8,128)(2,1)}, u32[]{:S(2)}, u32[]{:S(2)}) collective-permute-start(bf16[64,1536]{1,0:T(8,128)(2,1)S(1)} %get-tuple-element.122), channel_id=1, source_target_pairs={{0,8},{4,12},{8,0},{12,4},{1,9},{5,13},{9,1},{13,5},{2,10},{6,14},... | collective-permute-start | bytes 589832 | tf_op jit(solution)/shard_map/ppermute | solution.py:22
  38.7 48.2 %collective-permute-start.177 = (bf16[64,1536]{1,0:T(8,128)(2,1)S(1)}, bf16[64,1536]{1,0:T(8,128)(2,1)}, u32[]{:S(2)}, u32[]{:S(2)}) collective-permute-start(bf16[64,1536]{1,0:T(8,128)(2,1)S(1)} %get-tuple-element.122), channel_id=1, source_target_pairs={{0,12},{4,8},{8,4},{12,0},{1,13},{5,9},{9,5},{13,1},{2,14},{6,10},... | collective-permute-start | bytes 589832 | tf_op jit(solution)/shard_map/ppermute | solution.py:22
  38.8 182.6 %collective-permute-start.18 = (bf16[384,768]{1,0:T(8,128)(2,1)}, bf16[384,768]{1,0:T(8,128)(2,1)}, u32[]{:S(2)}, u32[]{:S(2)}) collective-permute-start(bf16[384,768]{1,0:T(8,128)(2,1)} %get-tuple-element.170), channel_id=1, source_target_pairs={{0,16},{16,0},{1,17},{17,1},{2,18},{18,2},{3,19},{19,3},{4,20},{20... | collective-permute-start | bytes 1769480 | tf_op jit(solution)/shard_map/ppermute | solution.py:22
  43.1 133.8 %collective-permute-start.13 = (bf16[768,1536]{1,0:T(8,128)(2,1)S(1)}, bf16[768,1536]{1,0:T(8,128)(2,1)S(1)}, u32[]{:S(2)}, u32[]{:S(2)}) collective-permute-start(bf16[768,1536]{1,0:T(8,128)(2,1)S(1)} %copy-done.40), channel_id=1, source_target_pairs={{0,16},{16,0},{1,17},{17,1},{2,18},{18,2},{3,19},{19,3},{4,20},{20... | collective-permute-start | bytes 7077896 | tf_op jit(solution)/shard_map/ppermute | solution.py:22
  65.9 172.8 %collective-permute-start.26 = (bf16[768,1024]{1,0:T(8,128)(2,1)}, bf16[768,1024]{1,0:T(8,128)(2,1)}, u32[]{:S(2)}, u32[]{:S(2)}) collective-permute-start(bf16[768,1024]{1,0:T(8,128)(2,1)} %get-tuple-element.155), channel_id=1, source_target_pairs={{0,16},{16,0},{1,17},{17,1},{2,18},{18,2},{3,19},{19,3},{4,20},{20... | collective-permute-start | bytes 4718600 | tf_op jit(solution)/shard_map/ppermute | solution.py:22
  86.9 38.5 %collective-permute-start.5 = (bf16[64,1536]{1,0:T(8,128)(2,1)S(1)}, bf16[64,1536]{1,0:T(8,128)(2,1)S(1)}, u32[]{:S(2)}, u32[]{:S(2)}) collective-permute-start(bf16[64,1536]{1,0:T(8,128)(2,1)S(1)} %slice.437), channel_id=1, source_target_pairs={{0,8},{4,12},{8,0},{12,4},{1,9},{5,13},{9,1},{13,5},{2,10},{6,14},... | collective-permute-start | bytes 589832 | tf_op jit(solution)/shard_map/ppermute | solution.py:22
  143.4 27.1 %collective-permute-start.56 = (bf16[1024,768]{1,0:T(8,128)(2,1)S(1)}, bf16[1024,768]{1,0:T(8,128)(2,1)S(1)}, u32[]{:S(2)}, u32[]{:S(2)}) collective-permute-start(bf16[1024,768]{1,0:T(8,128)(2,1)S(1)} %copy-done.50), channel_id=1, source_target_pairs={{0,16},{16,0},{1,17},{17,1},{2,18},{18,2},{3,19},{19,3},{4,20},{20... | collective-permute-start | bytes 4718600 | tf_op jit(solution)/shard_map/ppermute | solution.py:22
  168.4 71.0 %collective-permute-start.46 = (bf16[768,1536]{1,0:T(8,128)(2,1)S(1)}, bf16[768,1536]{1,0:T(8,128)(2,1)}, u32[]{:S(2)}, u32[]{:S(2)}) collective-permute-start(bf16[768,1536]{1,0:T(8,128)(2,1)S(1)} %copy-done.39), channel_id=1, source_target_pairs={{0,16},{16,0},{1,17},{17,1},{2,18},{18,2},{3,19},{19,3},{4,20},{20... | collective-permute-start | bytes 7077896 | tf_op jit(solution)/shard_map/ppermute | solution.py:22
  232.5 32.0 %collective-permute-start.27 = (bf16[1024,768]{1,0:T(8,128)(2,1)S(1)}, bf16[1024,768]{1,0:T(8,128)(2,1)S(1)}, u32[]{:S(2)}, u32[]{:S(2)}) collective-permute-start(bf16[1024,768]{1,0:T(8,128)(2,1)S(1)} %copy-done.46), channel_id=1, source_target_pairs={{0,16},{16,0},{1,17},{17,1},{2,18},{18,2},{3,19},{19,3},{4,20},{20... | collective-permute-start | bytes 4718600 | tf_op jit(solution)/shard_map/ppermute | solution.py:22
  236.3 27.0 %collective-permute-start.25 = (bf16[768,1024]{1,0:T(8,128)(2,1)S(1)}, bf16[768,1024]{1,0:T(8,128)(2,1)S(1)}, u32[]{:S(2)}, u32[]{:S(2)}) collective-permute-start(bf16[768,1024]{1,0:T(8,128)(2,1)S(1)} %copy-done.47), channel_id=1, source_target_pairs={{0,16},{16,0},{1,17},{17,1},{2,18},{18,2},{3,19},{19,3},{4,20},{20... | collective-permute-start | bytes 4718600 | tf_op jit(solution)/shard_map/ppermute | solution.py:22
  259.6 165.1 %collective-permute-start.47 = (bf16[384,768]{1,0:T(8,128)(2,1)S(1)}, bf16[384,768]{1,0:T(8,128)(2,1)S(1)}, u32[]{:S(2)}, u32[]{:S(2)}) collective-permute-start(bf16[384,768]{1,0:T(8,128)(2,1)S(1)} %copy-done.43), channel_id=1, source_target_pairs={{0,16},{16,0},{1,17},{17,1},{2,18},{18,2},{3,19},{19,3},{4,20},{20... | collective-permute-start | bytes 1769480 | tf_op jit(solution)/shard_map/ppermute | solution.py:22
  259.7 193.9 %collective-permute-start.55 = (bf16[768,1024]{1,0:T(8,128)(2,1)S(1)}, bf16[768,1024]{1,0:T(8,128)(2,1)}, u32[]{:S(2)}, u32[]{:S(2)}) collective-permute-start(bf16[768,1024]{1,0:T(8,128)(2,1)S(1)} %copy-done.49), channel_id=1, source_target_pairs={{0,16},{16,0},{1,17},{17,1},{2,18},{18,2},{3,19},{19,3},{4,20},{20... | collective-permute-start | bytes 4718600 | tf_op jit(solution)/shard_map/ppermute | solution.py:22
  275.0 169.3 %collective-permute-start.54 = (bf16[768,1024]{1,0:T(8,128)(2,1)}, bf16[768,1024]{1,0:T(8,128)(2,1)}, u32[]{:S(2)}, u32[]{:S(2)}) collective-permute-start(bf16[768,1024]{1,0:T(8,128)(2,1)} %get-tuple-element.152), channel_id=1, source_target_pairs={{0,16},{16,0},{1,17},{17,1},{2,18},{18,2},{3,19},{19,3},{4,20},{20... | collective-permute-start | bytes 4718600 | tf_op jit(solution)/shard_map/ppermute | solution.py:22
  371.3 56.4 %collective-permute-start.143 = (bf16[64,1536]{1,0:T(8,128)(2,1)S(1)}, bf16[64,1536]{1,0:T(8,128)(2,1)S(1)}, u32[]{:S(2)}, u32[]{:S(2)}) collective-permute-start(bf16[64,1536]{1,0:T(8,128)(2,1)S(1)} %collective-permute-done.140), channel_id=1, source_target_pairs={{0,3},{1,2},{2,1},{3,0},{4,7},{5,6},{6,5},{7,4},{8,11},{9,10},{10,... | collective-permute-start | bytes 589832 | tf_op jit(solution)/shard_map/ppermute | solution.py:22
  444.8 23.4 %collective-permute-start.161 = (bf16[64,1536]{1,0:T(8,128)(2,1)S(1)}, bf16[64,1536]{1,0:T(8,128)(2,1)S(1)}, u32[]{:S(2)}, u32[]{:S(2)}) collective-permute-start(bf16[64,1536]{1,0:T(8,128)(2,1)S(1)} %get-tuple-element.124), channel_id=1, source_target_pairs={{0,8},{4,12},{8,0},{12,4},{1,9},{5,13},{9,1},{13,5},{2,10},{6,14},... | collective-permute-start | bytes 589832 | tf_op jit(solution)/shard_map/ppermute | solution.py:22
  493.3 32.9 %collective-permute-start.62 = (bf16[64,1536]{1,0:T(8,128)(2,1)S(1)}, bf16[64,1536]{1,0:T(8,128)(2,1)S(1)}, u32[]{:S(2)}, u32[]{:S(2)}) collective-permute-start(bf16[64,1536]{1,0:T(8,128)(2,1)S(1)} %get-tuple-element.215), channel_id=1, source_target_pairs={{0,3},{1,2},{2,1},{3,0},{4,7},{5,6},{6,5},{7,4},{8,11},{9,10},{10,... | collective-permute-start | bytes 589832 | tf_op jit(solution)/shard_map/ppermute | solution.py:22
  496.4 30.5 %collective-permute-start.61 = (bf16[64,1536]{1,0:T(8,128)(2,1)S(1)}, bf16[64,1536]{1,0:T(8,128)(2,1)S(1)}, u32[]{:S(2)}, u32[]{:S(2)}) collective-permute-start(bf16[64,1536]{1,0:T(8,128)(2,1)S(1)} %get-tuple-element.215), channel_id=1, source_target_pairs={{0,2},{1,3},{2,0},{3,1},{4,6},{5,7},{6,4},{7,5},{8,10},{9,11},{10,... | collective-permute-start | bytes 589832 | tf_op jit(solution)/shard_map/ppermute | solution.py:22
  496.6 30.3 %collective-permute-start.60 = (bf16[64,1536]{1,0:T(8,128)(2,1)S(1)}, bf16[64,1536]{1,0:T(8,128)(2,1)S(1)}, u32[]{:S(2)}, u32[]{:S(2)}) collective-permute-start(bf16[64,1536]{1,0:T(8,128)(2,1)S(1)} %get-tuple-element.215), channel_id=1, source_target_pairs={{0,1},{1,0},{2,3},{3,2},{4,5},{5,4},{6,7},{7,6},{8,9},{9,8},{10,11... | collective-permute-start | bytes 589832 | tf_op jit(solution)/shard_map/ppermute | solution.py:22
  497.9 32.7 %collective-permute-start.66 = (bf16[64,1536]{1,0:T(8,128)(2,1)S(1)}, bf16[64,1536]{1,0:T(8,128)(2,1)S(1)}, u32[]{:S(2)}, u32[]{:S(2)}) collective-permute-start(bf16[64,1536]{1,0:T(8,128)(2,1)S(1)} %get-tuple-element.134), channel_id=1, source_target_pairs={{0,1},{1,0},{2,3},{3,2},{4,5},{5,4},{6,7},{7,6},{8,9},{9,8},{10,11... | collective-permute-start | bytes 589832 | tf_op jit(solution)/shard_map/ppermute | solution.py:22
  499.2 33.4 %collective-permute-start.67 = (bf16[64,1536]{1,0:T(8,128)(2,1)S(1)}, bf16[64,1536]{1,0:T(8,128)(2,1)S(1)}, u32[]{:S(2)}, u32[]{:S(2)}) collective-permute-start(bf16[64,1536]{1,0:T(8,128)(2,1)S(1)} %get-tuple-element.134), channel_id=1, source_target_pairs={{0,2},{1,3},{2,0},{3,1},{4,6},{5,7},{6,4},{7,5},{8,10},{9,11},{10,... | collective-permute-start | bytes 589832 | tf_op jit(solution)/shard_map/ppermute | solution.py:22
  532.7 326.1 %collective-permute-start.181 = (bf16[768,1024]{1,0:T(8,128)(2,1)}, bf16[768,1024]{1,0:T(8,128)(2,1)}, u32[]{:S(2)}, u32[]{:S(2)}) collective-permute-start(bf16[768,1024]{1,0:T(8,128)(2,1)} %convolution_convert_fusion.6), channel_id=1, source_target_pairs={{0,16},{16,0},{1,17},{17,1},{2,18},{18,2},{3,19},{19,3},{4,20},{20... | collective-permute-start | bytes 4718600 | tf_op jit(solution)/shard_map/ppermute | solution.py:22
  532.8 330.3 %collective-permute-start.183 = (bf16[768,1024]{1,0:T(8,128)(2,1)}, bf16[768,1024]{1,0:T(8,128)(2,1)}, u32[]{:S(2)}, u32[]{:S(2)}) collective-permute-start(bf16[768,1024]{1,0:T(8,128)(2,1)} %convolution_convert_fusion.4), channel_id=1, source_target_pairs={{0,16},{16,0},{1,17},{17,1},{2,18},{18,2},{3,19},{19,3},{4,20},{20... | collective-permute-start | bytes 4718600 | tf_op jit(solution)/shard_map/ppermute | solution.py:22
  660.6 212.6 %collective-permute-start.185 = (bf16[1024,768]{1,0:T(8,128)(2,1)}, bf16[1024,768]{1,0:T(8,128)(2,1)}, u32[]{:S(2)}, u32[]{:S(2)}) collective-permute-start(bf16[1024,768]{1,0:T(8,128)(2,1)} %convolution_convert_fusion.2), channel_id=1, source_target_pairs={{0,16},{16,0},{1,17},{17,1},{2,18},{18,2},{3,19},{19,3},{4,20},{20... | collective-permute-start | bytes 4718600 | tf_op jit(solution)/shard_map/ppermute | solution.py:22
  708.9 28.5 %collective-permute-start.90 = (bf16[64,1536]{1,0:T(8,128)(2,1)S(1)}, bf16[64,1536]{1,0:T(8,128)(2,1)S(1)}, u32[]{:S(2)}, u32[]{:S(2)}) collective-permute-start(bf16[64,1536]{1,0:T(8,128)(2,1)S(1)} %get-tuple-element.129), channel_id=1, source_target_pairs={{0,1},{1,0},{2,3},{3,2},{4,5},{5,4},{6,7},{7,6},{8,9},{9,8},{10,11... | collective-permute-start | bytes 589832 | tf_op jit(solution)/shard_map/ppermute | solution.py:22
  713.8 25.3 %collective-permute-start.91 = (bf16[64,1536]{1,0:T(8,128)(2,1)S(1)}, bf16[64,1536]{1,0:T(8,128)(2,1)S(1)}, u32[]{:S(2)}, u32[]{:S(2)}) collective-permute-start(bf16[64,1536]{1,0:T(8,128)(2,1)S(1)} %get-tuple-element.129), channel_id=1, source_target_pairs={{0,2},{1,3},{2,0},{3,1},{4,6},{5,7},{6,4},{7,5},{8,10},{9,11},{10,... | collective-permute-start | bytes 589832 | tf_op jit(solution)/shard_map/ppermute | solution.py:22
  778.7 139.5 %collective-permute-start.156 = (bf16[768,1024]{1,0:T(8,128)(2,1)}, bf16[768,1024]{1,0:T(8,128)(2,1)}, u32[]{:S(2)}, u32[]{:S(2)}) collective-permute-start(bf16[768,1024]{1,0:T(8,128)(2,1)} %convolution_convert_fusion.7), channel_id=1, source_target_pairs={{0,16},{16,0},{1,17},{17,1},{2,18},{18,2},{3,19},{19,3},{4,20},{20... | collective-permute-start | bytes 4718600 | tf_op jit(solution)/shard_map/ppermute | solution.py:22
  868.6 57.5 %collective-permute-start.182 = (bf16[768,1024]{1,0:T(8,128)(2,1)S(1)}, bf16[768,1024]{1,0:T(8,128)(2,1)S(1)}, u32[]{:S(2)}, u32[]{:S(2)}) collective-permute-start(bf16[768,1024]{1,0:T(8,128)(2,1)S(1)} %copy-done.102), channel_id=1, source_target_pairs={{0,16},{16,0},{1,17},{17,1},{2,18},{18,2},{3,19},{19,3},{4,20},{20... | collective-permute-start | bytes 4718600 | tf_op jit(solution)/shard_map/ppermute | solution.py:22
  897.7 34.2 %collective-permute-start.184 = (bf16[1024,768]{1,0:T(8,128)(2,1)S(1)}, bf16[1024,768]{1,0:T(8,128)(2,1)S(1)}, u32[]{:S(2)}, u32[]{:S(2)}) collective-permute-start(bf16[1024,768]{1,0:T(8,128)(2,1)S(1)} %convolution_convert_fusion.3), channel_id=1, source_target_pairs={{0,16},{16,0},{1,17},{17,1},{2,18},{18,2},{3,19},{19,3},{4,20},{20... | collective-permute-start | bytes 4718600 | tf_op jit(solution)/shard_map/ppermute | solution.py:22
  (292 other events, 4140.7 us)

commit v2 on v1

v2 whole, which is shorter than its diff:
```python
import functools

import jax
import jax.numpy as jnp
from jax import lax
from jax.experimental import pallas as pl
from jax.experimental.pallas import tpu as pltpu
from jax.sharding import PartitionSpec as P

epsilon = 1e-06
masked_value = -1e30
bf16 = jnp.bfloat16
f32 = jnp.float32
pair_lanes = 128
hidden_block = 256
chunk_rows = 256


def query_rows(seq_len):
    return 256 if seq_len <= 2048 else 128


def swap(x, axis, k):
    n = lax.axis_size(axis)
    return lax.ppermute(x, axis, [(i, i ^ k) for i in range(n)])


def own_rows(shard):
    blocks = [shard] + [swap(shard, "tensor", k) for k in range(1, lax.axis_size("tensor"))]
    return jnp.concatenate(blocks, axis=0)


def after(x, token):
    return x + (token[:1, :1].astype(f32) * 0.0).astype(x.dtype)


def all_rows(own, token=None):
    count_z, count_t = lax.axis_size("context"), lax.axis_size("tensor")
    block = own.shape[0] // count_t
    shard = own[:block]
    if token is not None:
        shard = after(shard, token)
        own_sent = after(own, token)
    else:
        own_sent = own
    if count_z != 4:
        return (lax.all_gather(own_sent, "context", tiled=True),)
    far = [swap(shard, "context", 2), swap(shard, "context", 3)]
    near = swap(own_sent, "context", 1)
    far = jnp.concatenate(far, axis=0)
    return (own, near, far) + tuple(swap(far, "tensor", k) for k in range(1, count_t))


def row_places():
    count_z, count_t = lax.axis_size("context"), lax.axis_size("tensor")
    z, t = lax.axis_index("context"), lax.axis_index("tensor")
    own = [(z, k) for k in range(count_t)]
    if count_z != 4:
        parts = [(p, k) for p in range(count_z) for k in range(count_t)]
    else:
        parts = [(z ^ kz, k) for kz in (0, 1) for k in range(count_t)]
        parts += [(z ^ kz, k) for k in range(count_t) for kz in (2, 3)]
    return jnp.stack([(p * count_t + (t ^ k)).astype(jnp.int32) for p, k in own + parts])


def received_sum(own, sends):
    total = own
    for k, part in enumerate(sends, 1):
        total = total + swap(part, "tensor", k).astype(f32)
    return total


def sum_over(x, axis):
    total = x
    for k in range(1, lax.axis_size(axis)):
        total = total + swap(x, axis, k)
    return total


def dot_nt(a, b):
    return lax.dot_general(a, b, (((1,), (1,)), ((), ())), preferred_element_type=f32)


def dot_tn(a, b):
    return lax.dot_general(a, b, (((0,), (0,)), ((), ())), preferred_element_type=f32)


def dot_nn(a, b):
    return jnp.dot(a, b, preferred_element_type=f32)


def each(count, body):
    if count <= 4:
        for i in range(count):
            body(i)
        return

    def one(i, carry):
        body(i)
        return carry

    lax.fori_loop(0, count, one, 0)


def rows_at(i, rows):
    start = i * rows
    return pl.ds(start if isinstance(start, int) else pl.multiple_of(start, rows), rows)


def assemble(parts, whole_ref, place_ref, count_t, block):
    j = 0
    for part in parts:
        for r in range(part.shape[0] // block):
            at = j * block if place_ref is None else pl.multiple_of(place_ref[count_t + j] * block, block)
            whole_ref[pl.ds(at, block), :] = part[r * block : (r + 1) * block, :]
            j += 1


def own_of(ref, place_ref, count_t, block):
    return jnp.concatenate(
        [ref[pl.ds(pl.multiple_of(place_ref[k] * block, block), block), :] for k in range(count_t)], axis=0
    )


def hand_out(total, own_ref, send_refs):
    block = own_ref.shape[0]
    own_ref[...] = total[:block, :]
    for k, ref in enumerate(send_refs, 1):
        ref[...] = total[k * block : (k + 1) * block, :].astype(bf16)


def shifted_sum(x, reverse):
    rows = x.shape[0]
    row = lax.broadcasted_iota(jnp.int32, x.shape, 0)
    step = 1
    while step < rows:
        if reverse:
            moved = jnp.where(row < rows - step, pltpu.roll(x, rows - step, 0), 0.0)
        else:
            moved = jnp.where(row >= step, pltpu.roll(x, step, 0), 0.0)
        x = x + moved
        step *= 2
    return x


def log_sigmoid(z):
    e = jnp.exp(-jnp.abs(z))
    small = e * (1.0 - e * (1 / 2 - e * (1 / 3 - e * (1 / 4 - e * (1 / 5 - e * (1 / 6 - e * (1 / 7)))))))
    return jnp.minimum(z, 0.0) - jnp.where(e < 0.0625, small, jnp.log(1.0 + e))


def three_parts(x):
    high = x.astype(bf16).astype(f32)
    middle = (x - high).astype(bf16).astype(f32)
    lowest = (x - high - middle).astype(bf16).astype(f32)
    return high, middle, lowest


def head_column(table, head):
    lane = lax.broadcasted_iota(jnp.int32, table.shape, 1)
    return jnp.sum(jnp.where(lane == head, table, 0.0), axis=1, keepdims=True)


def mix_decay(q_ref, k_ref, decay_ref, pair, qa, qb, ka, kb):
    rows = chunk_rows

    def mix(i):
        here = rows_at(i, rows)
        lane = lax.broadcasted_iota(jnp.int32, (rows, pair_lanes), 1)
        table = decay_ref[here, :]
        q = q_ref[here, :].astype(f32) * 0.125
        k = k_ref[here, :].astype(f32)
        for head, (q_out, k_out, first, mine) in enumerate(
            ((qa, ka, 64, lane < 64), (qb, kb, 0, lane >= 64))
        ):
            high, middle, lowest = three_parts(head_column(table, 2 * pair + head))
            spot = lane - first
            split = jnp.where(
                (spot == 0) | (spot == 3), high, jnp.where((spot == 1) | (spot == 4), middle, lowest)
            )
            low_spot = (spot >= 0) & (spot < 3)
            high_spot = (spot >= 3) & (spot < 6)
            key_side = jnp.where(low_spot, -split, jnp.where(high_spot, 1.0, 0.0))
            query_side = jnp.where(low_spot, 1.0, jnp.where(high_spot, split, 0.0))
            q_out[here, :] = jnp.where(mine, q, query_side).astype(bf16)
            k_out[here, :] = jnp.where(mine, k, key_side).astype(bf16)

    each(q_ref.shape[0] // rows, mix)


def live_mask(start_ref, start, first, width, rows):
    key_pos = first + lax.broadcasted_iota(jnp.int32, (rows, width), 1)
    query_pos = start + lax.broadcasted_iota(jnp.int32, (rows, width), 0)
    doc_start = start_ref[pl.ds(start, rows), :]
    return (key_pos <= query_pos) & (key_pos >= doc_start)


def over_query_blocks(seq_len, rows, body):
    before = seq_len // 2
    if seq_len // rows <= 4:
        for start in range(0, seq_len, rows):
            first = max(0, start - before)
            body(start, first, start + rows - first)
        return
    width = before + rows

    def one(i, carry):
        start = pl.multiple_of(i * rows, rows)
        first = pl.multiple_of(jnp.maximum(start - before, 0), rows)
        body(start, first, width)
        return carry

    lax.fori_loop(0, seq_len // rows, one, 0)


def probabilities(q_rows, k_rows, mask):
    s = jnp.where(mask, dot_nt(q_rows, k_rows), masked_value)
    e = jnp.exp(s - jnp.max(s, axis=1, keepdims=True))
    return e * (1.0 / jnp.sum(e, axis=1, keepdims=True))


def lane_blocks(refs):
    return jnp.concatenate([r[0] for r in refs], axis=1)


def forward_kernel(count_parts, count_t, block, join, *refs):
    place_ref, parts, refs = refs[0], refs[1 : 1 + count_parts], list(refs[1 + count_parts :])
    mine, theirs, (wo, to, wf, bias, start_ref) = refs[:4], refs[4:8], refs[8:13]
    refs = refs[13:]
    a_ref = refs.pop(0) if join else parts[0]
    q_ref, k_ref, v_ref, gate_ref, o_ref, u_ref, z_ref, decay_ref, own_ref = refs[:9]
    sends, (qa, qb, ka, kb, acc) = refs[9:-5], refs[-5:]
    pair = pl.program_id(0)
    seq_len, half = a_ref.shape[0], a_ref.shape[1] // 2
    rows = query_rows(seq_len)

    @pl.when(pair == 0)
    def _():
        if join:
            assemble(parts, a_ref, place_ref, count_t, block)
        acc[...] = jnp.zeros_like(acc)

        def gates(i):
            here = rows_at(i, chunk_rows)
            z = (dot_nn(a_ref[here, :], wf[...]) + bias[...])[:, :8]
            z_ref[here, :] = z
            decay_ref[here, :] = log_sigmoid(z)

        each(seq_len // chunk_rows, gates)
        decay_ref[...] = shifted_sum(decay_ref[...], False)

    w_mine, w_theirs = lane_blocks(mine), lane_blocks(theirs)

    def project(i):
        here = rows_at(i, chunk_rows)
        out = dot_nn(a_ref[here, :half], w_mine) + dot_nn(a_ref[here, half:], w_theirs)
        q_ref[here, :] = out[:, :128].astype(bf16)
        k_ref[here, :] = out[:, 128:256].astype(bf16)
        v_ref[here, :] = out[:, 256:384].astype(bf16)
        gate_ref[here, :] = out[:, 384:]

    each(seq_len // chunk_rows, project)
    mix_decay(q_ref, k_ref, decay_ref, pair, qa, qb, ka, kb)
    lane = lax.broadcasted_iota(jnp.int32, (rows, pair_lanes), 1)

    def body(start, first, width):
        mask = live_mask(start_ref, start, first, width, rows)
        here, keys = pl.ds(start, rows), pl.ds(first, width)
        values = v_ref[keys, :]
        out = []
        for q_of, k_of in ((qa, ka), (qb, kb)):
            p = probabilities(q_of[here, :], k_of[keys, :], mask).astype(bf16)
            out.append(dot_nn(p, values))
        o = jnp.where(lane < 64, out[0], out[1])
        o_ref[here, :] = o
        u_ref[here, :] = (o * jax.nn.sigmoid(gate_ref[here, :])).astype(bf16)

    over_query_blocks(seq_len, rows, body)
    u_own = own_of(u_ref, place_ref, count_t, block)
    acc[:, :half] += dot_nn(u_own, wo[0])
    acc[:, half:] += dot_nn(u_own, to[0])

    @pl.when(pair == pl.num_programs(0) - 1)
    def _():
        hand_out(acc, own_ref, sends)


def backward_kernel(count_parts, count_t, block, join, *refs):
    place_ref, parts, refs = refs[0], refs[1 : 1 + count_parts], list(refs[1 + count_parts :])
    mine, theirs, (wo, to, wf) = refs[:4], refs[4:8], refs[8:11]
    q_ref, k_ref, v_ref, gate_ref, o_ref, z_ref, decay_ref, start_ref = refs[11:19]
    refs = refs[19:]
    y_ref = refs.pop(0) if join else parts[0]
    dq_ref, dk_ref, dv_ref, dg_ref, dz_ref, own_ref = refs[:6]
    sends, (qa, qb, ka, kb, dd, dka, dkb, dva, dcs, acc) = refs[6:-10], refs[-10:]
    pair = pl.program_id(0)
    seq_len, half = y_ref.shape[0], y_ref.shape[1] // 2
    rows = query_rows(seq_len)

    @pl.when(pair == 0)
    def _():
        if join:
            assemble(parts, y_ref, place_ref, count_t, block)
        acc[...] = jnp.zeros_like(acc)
        dcs[...] = jnp.zeros_like(dcs)

    def gates(i):
        here = rows_at(i, chunk_rows)
        du = dot_nt(y_ref[here, :half], wo[0]) + dot_nt(y_ref[here, half:], to[0])
        sig = jax.nn.sigmoid(gate_ref[here, :])
        dd[here, :] = (du * sig).astype(bf16)
        dg_ref[here, :] = (du * o_ref[here, :] * sig * (1.0 - sig)).astype(bf16)

    each(seq_len // chunk_rows, gates)
    mix_decay(q_ref, k_ref, decay_ref, pair, qa, qb, ka, kb)
    dka[...] = jnp.zeros_like(dka)
    dkb[...] = jnp.zeros_like(dkb)
    dva[...] = jnp.zeros_like(dva)
    lane = lax.broadcasted_iota(jnp.int32, (rows, pair_lanes), 1)

    def pick(column_a, column_b):
        at = lax.broadcasted_iota(jnp.int32, (column_a.shape[0], pair_lanes), 1)
        return jnp.where(at == 2 * pair, column_a, jnp.where(at == 2 * pair + 1, column_b, 0.0))

    def body(start, first, width):
        mask = live_mask(start_ref, start, first, width, rows)
        here, keys = pl.ds(start, rows), pl.ds(first, width)
        values = v_ref[keys, :]
        d_rows = dd[here, :]
        dq = []
        for head, (q_of, k_of, dk_of) in enumerate(((qa, ka, dka), (qb, kb, dkb))):
            own_lanes = (lane < 64) if head == 0 else (lane >= 64)
            p = probabilities(q_of[here, :], k_of[keys, :], mask)
            d_mine = jnp.where(own_lanes, d_rows, jnp.zeros_like(d_rows))
            dp = dot_nt(d_mine, values)
            delta = jnp.sum(p * dp, axis=1, keepdims=True)
            ds = (p * (dp - delta)).astype(bf16)
            dq.append(dot_nn(ds, k_of[keys, :]))
            dk_of[keys, :] += dot_tn(ds, q_of[here, :])
            dva[keys, :] += dot_tn(p.astype(bf16), d_mine)
        dq_ref[here, :] = (jnp.where(lane < 64, dq[0], dq[1]) * 0.125).astype(bf16)
        dcs[here, :] += pick(dq[0][:, 67:68], dq[1][:, 3:4])

    over_query_blocks(seq_len, rows, body)

    def finish(i):
        here = rows_at(i, chunk_rows)
        lanes_now = lax.broadcasted_iota(jnp.int32, (chunk_rows, pair_lanes), 1)
        ka_rows, kb_rows = dka[here, :], dkb[here, :]
        dk_ref[here, :] = jnp.where(lanes_now < 64, ka_rows, kb_rows).astype(bf16)
        dv_ref[here, :] = dva[here, :].astype(bf16)
        dcs[here, :] -= pick(ka_rows[:, 64:65], kb_rows[:, 0:1])

    each(seq_len // chunk_rows, finish)
    d_own = jnp.concatenate(
        [own_of(r, place_ref, count_t, block) for r in (dq_ref, dk_ref, dv_ref, dg_ref)], axis=1
    )
    acc[:, :half] += dot_nt(d_own, lane_blocks(mine))
    acc[:, half:] += dot_nt(d_own, lane_blocks(theirs))

    @pl.when(pair == pl.num_programs(0) - 1)
    def _():
        dcs[...] = shifted_sum(dcs[...], True)

        def last(i):
            here = rows_at(i, chunk_rows)
            dz_ref[here, :] = (dcs[here, :8] * jax.nn.sigmoid(-z_ref[here, :])).astype(bf16)

        each(seq_len // chunk_rows, last)
        dz_own = own_of(dz_ref, place_ref, count_t, block)
        acc[...] += dot_nt(dz_own, wf[:, :8])
        hand_out(acc, own_ref, sends)


def ffn_forward_kernel(b_ref, wg, wu, wd, tg, tu, td, gt_ref, up_ref, own_ref, *rest):
    sends, acc = rest[:-1], rest[-1]
    half = b_ref.shape[1] // 2
    low, high = b_ref[:, :half], b_ref[:, half:]
    gt = dot_nn(low, wg[0]) + dot_nn(high, tg[0])
    up = dot_nn(low, wu[0]) + dot_nn(high, tu[0])
    gt_ref[...] = gt
    up_ref[...] = up
    m = (gt * jax.nn.sigmoid(gt) * up).astype(bf16)

    @pl.when(pl.program_id(0) == 0)
    def _():
        acc[...] = jnp.zeros_like(acc)

    acc[:, :half] += dot_nn(m, wd[0])
    acc[:, half:] += dot_nn(m, td[0])

    @pl.when(pl.program_id(0) == pl.num_programs(0) - 1)
    def _():
        hand_out(acc, own_ref, sends)


def inner_grads(dm, gt, up):
    sig = jax.nn.sigmoid(gt)
    d_gate = (dm * up * sig * (1.0 + gt * (1.0 - sig))).astype(bf16)
    return d_gate, (dm * (gt * sig)).astype(bf16)


def ffn_backward_kernel(g_ref, gt_ref, up_ref, wg, wu, wd, tg, tu, td, own_ref, *rest):
    sends, acc = rest[:-1], rest[-1]
    half = g_ref.shape[1] // 2
    dm = dot_nt(g_ref[:, :half], wd[0]) + dot_nt(g_ref[:, half:], td[0])
    d_gate, d_up = inner_grads(dm, gt_ref[...], up_ref[...])

    @pl.when(pl.program_id(0) == 0)
    def _():
        acc[...] = jnp.zeros_like(acc)

    acc[:, :half] += dot_nt(d_gate, wg[0]) + dot_nt(d_up, wu[0])
    acc[:, half:] += dot_nt(d_gate, tg[0]) + dot_nt(d_up, tu[0])

    @pl.when(pl.program_id(0) == pl.num_programs(0) - 1)
    def _():
        hand_out(acc, own_ref, sends)


def ffn_inner_kernel(count_parts, block, *refs):
    b_parts, g_parts = refs[:count_parts], refs[count_parts : 2 * count_parts]
    wg, wu, wd, tg, tu, td, b_ref, g_ref, m_ref, dgate_ref, dup_ref = refs[2 * count_parts :]
    half = b_ref.shape[1] // 2

    @pl.when(pl.program_id(0) == 0)
    def _():
        assemble(b_parts, b_ref, None, 0, block)
        assemble(g_parts, g_ref, None, 0, block)

    def chunk(i):
        here = rows_at(i, chunk_rows)
        low, high = b_ref[here, :half], b_ref[here, half:]
        gt = dot_nn(low, wg[0]) + dot_nn(high, tg[0])
        up = dot_nn(low, wu[0]) + dot_nn(high, tu[0])
        dm = dot_nt(g_ref[here, :half], wd[0]) + dot_nt(g_ref[here, half:], td[0])
        m_ref[here, :] = (gt * jax.nn.sigmoid(gt) * up).astype(bf16)
        dgate_ref[here, :], dup_ref[here, :] = inner_grads(dm, gt, up)

    each(b_ref.shape[0] // chunk_rows, chunk)


def fixed(shape, single=True):
    zeros = (0,) * len(shape)
    if single:
        return pl.BlockSpec(shape, lambda *_: zeros, pipeline_mode=pl.Buffered(1))
    return pl.BlockSpec(shape, lambda *_: zeros)


def lanes(seq_len):
    return pl.BlockSpec((seq_len, pair_lanes), lambda p, *_: (0, p))


def lanes_read(seq_len):
    if seq_len <= 2048:
        return lanes(seq_len)
    return pl.BlockSpec((seq_len, pair_lanes), lambda p, *_: (0, p), pipeline_mode=pl.Buffered(1))


def columns_of(w, layer, width):
    return pl.BlockSpec((1, w.shape[1], width), lambda p, *_: (layer, 0, p))


def rows_of(w, layer, height):
    return pl.BlockSpec((1, height, w.shape[2]), lambda p, *_: (layer, p, 0))


def shape(dims, dtype):
    return jax.ShapeDtypeStruct(dims, dtype)


def share_outs(block, width, count_t):
    out = [shape((block, width), f32)] + [shape((block, width), bf16)] * (count_t - 1)
    return out, [fixed((block, width), False)] * count_t


def attention_specs(parts, layer, w4, t4, wo, to, seq_len, join):
    specs = [fixed(p.shape) for p in parts]
    specs += [columns_of(w, layer, pair_lanes) for w in (*w4, *t4)]
    specs += [rows_of(wo, layer, pair_lanes), rows_of(to, layer, pair_lanes)]
    return specs


def attention_forward(places, parts, layer, w4, t4, wo, to, wf, bias, doc_start, count_t, piece_len):
    seq_len, width = doc_start.shape[0], parts[0].shape[1]
    local_width = wo.shape[1]
    block = piece_len // count_t
    join = len(parts) > 1
    low, high = lambda: shape((seq_len, local_width), bf16), lambda: shape((seq_len, local_width), f32)
    shared, shared_specs = share_outs(block, width, count_t)
    outs = [low(), low(), low(), high(), high(), low(), shape((seq_len, 8), f32), shape((seq_len, 8), f32)]
    specs = [lanes(seq_len)] * 6 + [fixed((seq_len, 8), False)] * 2
    if join:
        outs, specs = [shape((seq_len, width), bf16)] + outs, [fixed((seq_len, width))] + specs
    got = pl.pallas_call(
        functools.partial(forward_kernel, len(parts), count_t, block, join),
        grid_spec=pltpu.PrefetchScalarGridSpec(
            num_scalar_prefetch=1,
            grid=(local_width // pair_lanes,),
            in_specs=attention_specs(parts, layer, w4, t4, wo, to, seq_len, join)
            + [fixed(wf.shape), fixed(bias.shape), fixed(doc_start.shape)],
            out_specs=specs + shared_specs,
            scratch_shapes=[pltpu.VMEM((seq_len, pair_lanes), bf16)] * 4 + [pltpu.VMEM((piece_len, width), f32)],
        ),
        out_shape=outs + shared,
        compiler_params=pltpu.CompilerParams(vmem_limit_bytes=60 << 20),
    )(places, *parts, *w4, *t4, wo, to, wf, bias, doc_start)
    got = list(got)
    a = got.pop(0) if join else parts[0]
    return a, got[:8], got[8], got[9:]


def attention_backward(places, parts, layer, w4, t4, wo, to, wf, saved, doc_start, count_t, piece_len):
    q, k, v, gate, o, u, z, decay = saved
    seq_len, width = doc_start.shape[0], parts[0].shape[1]
    local_width = wo.shape[1]
    block = piece_len // count_t
    join = len(parts) > 1
    shared, shared_specs = share_outs(block, width, count_t)
    outs = [shape((seq_len, local_width), bf16)] * 4 + [shape((seq_len, 8), bf16)]
    specs = [lanes(seq_len)] * 4 + [fixed((seq_len, 8), False)]
    if join:
        outs, specs = [shape((seq_len, width), bf16)] + outs, [fixed((seq_len, width))] + specs
    low, high = pltpu.VMEM((seq_len, pair_lanes), bf16), pltpu.VMEM((seq_len, pair_lanes), f32)
    got = pl.pallas_call(
        functools.partial(backward_kernel, len(parts), count_t, block, join),
        grid_spec=pltpu.PrefetchScalarGridSpec(
            num_scalar_prefetch=1,
            grid=(local_width // pair_lanes,),
            in_specs=attention_specs(parts, layer, w4, t4, wo, to, seq_len, join)
            + [fixed(wf.shape)]
            + [lanes_read(seq_len)] * 5
            + [fixed((seq_len, 8)), fixed((seq_len, 8)), fixed(doc_start.shape)],
            out_specs=specs + shared_specs,
            scratch_shapes=[low] * 5 + [high] * 4 + [pltpu.VMEM((piece_len, width), f32)],
        ),
        out_shape=outs + shared,
        compiler_params=pltpu.CompilerParams(vmem_limit_bytes=60 << 20),
    )(places, *parts, *w4, *t4, wo, to, wf, q, k, v, gate, o, z, decay, doc_start)
    got = list(got)
    y = got.pop(0) if join else parts[0]
    return y, got[:5], got[5], got[6:]


def ffn_weights(layer, w3, t3):
    specs = []
    for wg, wu, wd in (w3, t3):
        specs += [
            columns_of(wg, layer, hidden_block), columns_of(wu, layer, hidden_block), rows_of(wd, layer, hidden_block),
        ]
    return specs


def blocks_of(rows):
    return pl.BlockSpec((rows, hidden_block), lambda p, *_: (0, p))


def ffn_forward(b, layer, w3, t3, count_t):
    rows, width = b.shape
    inner = w3[2].shape[1]
    shared, shared_specs = share_outs(rows // count_t, width, count_t)
    got = pl.pallas_call(
        ffn_forward_kernel,
        grid=(inner // hidden_block,),
        in_specs=[fixed(b.shape)] + ffn_weights(layer, w3, t3),
        out_specs=[blocks_of(rows)] * 2 + shared_specs,
        scratch_shapes=[pltpu.VMEM((rows, width), f32)],
        out_shape=[shape((rows, inner), f32)] * 2 + shared,
        compiler_params=pltpu.CompilerParams(vmem_limit_bytes=40 << 20),
    )(b, *w3, *t3)
    return got[0], got[1], got[2], got[3:]


def ffn_backward(g, gt, up, layer, w3, t3, count_t):
    rows, width = g.shape
    shared, shared_specs = share_outs(rows // count_t, width, count_t)
    got = pl.pallas_call(
        ffn_backward_kernel,
        grid=(gt.shape[1] // hidden_block,),
        in_specs=[fixed(g.shape)] + [blocks_of(rows)] * 2 + ffn_weights(layer, w3, t3),
        out_specs=shared_specs,
        scratch_shapes=[pltpu.VMEM((rows, width), f32)],
        out_shape=shared,
        compiler_params=pltpu.CompilerParams(vmem_limit_bytes=40 << 20),
    )(g, gt, up, *w3, *t3)
    return got[0], got[1:]


def ffn_inner(b_parts, g_parts, layer, w3, t3, block):
    rows, width = sum(p.shape[0] for p in b_parts), b_parts[0].shape[1]
    inner = w3[2].shape[1]
    return pl.pallas_call(
        functools.partial(ffn_inner_kernel, len(b_parts), block),
        grid=(inner // hidden_block,),
        in_specs=[fixed(p.shape) for p in (*b_parts, *g_parts)] + ffn_weights(layer, w3, t3),
        out_specs=[fixed((rows, width))] * 2 + [blocks_of(rows)] * 3,
        out_shape=[shape((rows, width), bf16)] * 2 + [shape((rows, inner), bf16)] * 3,
        compiler_params=pltpu.CompilerParams(vmem_limit_bytes=56 << 20),
    )(*b_parts, *g_parts, *w3, *t3)


def inverse_rms(h):
    return lax.rsqrt(jnp.mean(h * h, axis=-1, keepdims=True) + epsilon)


def norm_back(grad_normed, hidden, inverse, gain):
    scaled = hidden * inverse
    weighted = grad_normed * gain
    grad_gain = jnp.sum(grad_normed * scaled, axis=0)
    mean = jnp.mean(weighted * scaled, axis=-1, keepdims=True)
    return inverse * (weighted - scaled * mean), grad_gain


def local(
    hidden_in, segment_ids, w_query, w_key, w_value, w_gate_out, w_attn_out, w_forget, b_forget,
    gain_attn, gain_ffn, w_gate, w_up, w_down, cotangent,
):
    seq_count, piece_len, width = hidden_in.shape
    count_z, count_t = lax.axis_size("context"), lax.axis_size("tensor")
    core, z, t = lax.axis_index("fsdp"), lax.axis_index("context"), lax.axis_index("tensor")
    layers, half, local_width = w_query.shape
    heads = w_forget.shape[2]
    block = piece_len // count_t
    seq_len = piece_len * count_z
    places = row_places()
    shared_rows = count_z == 4

    def features(x):
        return jnp.where(core == 0, x, jnp.concatenate([x[..., half:], x[..., :half]], axis=-1))

    def rows_by_place(x):
        parts = x.reshape(count_t, block, x.shape[-1])
        return jnp.concatenate(
            [lax.dynamic_index_in_dim(parts, k ^ t, 0, False) for k in range(count_t)], axis=0
        )

    def other(w):
        return swap(w, "fsdp", 1)

    def full(w, axis):
        return jnp.concatenate([w, other(w)], axis=axis)

    gains = full(jnp.concatenate([gain_attn, gain_ffn], axis=0), 1).astype(f32)
    hidden_rows = rows_by_place(features(hidden_in.reshape(piece_len, width)).astype(f32))
    first_a = (hidden_rows * inverse_rms(hidden_rows) * gains[0]).astype(bf16)
    a_parts = all_rows(first_a)

    w_forget_full = jnp.pad(full(w_forget, 1), ((0, 0), (0, 0), (0, pair_lanes - heads)))
    bias = jnp.pad(b_forget, ((0, 0), (0, pair_lanes - heads)))
    w4 = (w_query, w_key, w_value, w_gate_out)
    t4 = tuple(other(w) for w in w4)
    to = other(w_attn_out)
    w3 = (w_gate, w_up, w_down)
    t3 = tuple(other(w) for w in w3)

    segments = segment_ids.reshape(piece_len)
    if count_z == 4:
        pieces = jnp.stack([segments] + [swap(segments, "context", k) for k in range(1, count_z)])
        seg_all = jnp.concatenate(
            [lax.dynamic_index_in_dim(pieces, k ^ z, 0, False) for k in range(count_z)]
        )
    else:
        seg_all = lax.all_gather(segments, "context", tiled=True)
    doc_start = jnp.sum((seg_all[None, :] < seg_all[:, None]).astype(jnp.int32), axis=1, keepdims=True)

    def in_order(parts):
        if len(parts) > 1:
            return parts
        stacked = parts[0].reshape(count_z, count_t, block, width)
        return (
            jnp.concatenate(
                [lax.dynamic_index_in_dim(stacked, k ^ t, 1, True) for k in range(count_t)], axis=1
            ).reshape(seq_len, width),
        )

    hidden = hidden_rows[:block]
    saved = []
    cotangent_rows = rows_by_place(features(cotangent.reshape(piece_len, width)))
    for layer in range(layers):
        gain_one, gain_two = gains[layer], gains[layers + layer]
        inverse_one = inverse_rms(hidden)
        if layer > 0:
            a_parts = all_rows(own_rows((hidden * inverse_one * gain_one).astype(bf16)))
        a, kept, own, sends = attention_forward(
            places, in_order(a_parts), layer, w4, t4, w_attn_out, to, w_forget_full[layer],
            bias[layer : layer + 1], doc_start, count_t, piece_len,
        )
        if shared_rows:
            if layer == 0:
                g_last = all_rows(cotangent_rows, a_parts[-1])
            else:
                saved[-1]["b_parts"] = all_rows(saved[-1]["b"], a_parts[-1])
        mixed = hidden + received_sum(own, sends)
        inverse_two = inverse_rms(mixed)
        b = own_rows((mixed * inverse_two * gain_two).astype(bf16))
        gt, up, own, sends = ffn_forward(b, layer, w3, t3, count_t)
        saved.append(
            dict(hidden=hidden, inverse_one=inverse_one, a=a, kept=kept, mixed=mixed, inverse_two=inverse_two,
                 b=b, gt=gt, up=up)
        )
        hidden = mixed + received_sum(own, sends)

    def finish(x):
        return features(rows_by_place(own_rows(x.astype(bf16)))).reshape(1, piece_len, width)

    output = finish(hidden)

    grad = cotangent_rows[:block].astype(f32)
    results = [None] * layers
    gain_grads = [None] * (2 * layers)

    def exchange(mine, theirs):
        return mine + other(theirs).astype(f32)

    for layer in reversed(range(layers)):
        s = saved[layer]
        gain_one, gain_two = gains[layer], gains[layers + layer]
        g = cotangent_rows if layer == layers - 1 else own_rows(grad.astype(bf16))
        own, sends = ffn_backward(g, s["gt"], s["up"], layer, w3, t3, count_t)
        back, gain_grads[layers + layer] = norm_back(received_sum(own, sends), s["mixed"], s["inverse_two"], gain_two)
        grad_mixed = grad + back
        y_parts = all_rows(own_rows(grad_mixed.astype(bf16)))
        y, (dq, dk, dv, dg, dz), own, sends = attention_backward(
            places, in_order(y_parts), layer, w4, t4, w_attn_out, to, w_forget_full[layer], s["kept"],
            doc_start, count_t, piece_len,
        )
        if not shared_rows:
            b_parts, g_parts = (s["b"],), (g,)
        elif layer == layers - 1:
            b_parts, g_parts = all_rows(s["b"], y_parts[-1]), g_last
        else:
            b_parts, g_parts = s["b_parts"], all_rows(g, y_parts[-1])
        back, gain_grads[layer] = norm_back(received_sum(own, sends), s["hidden"], s["inverse_one"], gain_one)
        grad = grad_mixed + back

        b, g, m, d_gate, d_up = ffn_inner(b_parts, g_parts, layer, w3, t3, block)

        def by_rows(x, d):
            return exchange(dot_tn(x[:, :half], d), dot_tn(x[:, half:], d).astype(bf16))

        def by_columns(x, d):
            return exchange(dot_tn(x, d[:, :half]), dot_tn(x, d[:, half:]).astype(bf16))

        def pieces_sum(x):
            return x if shared_rows else lax.psum(x, "context")

        a, u = s["a"], s["kept"][5]
        dzr = dz[:, :heads]
        bias_grad = jnp.sum(dzr.astype(f32), axis=0)
        results[layer] = (
            by_rows(a, dq), by_rows(a, dk), by_rows(a, dv), by_rows(a, dg), by_columns(u, y),
            dot_tn(a[:, :half], dzr) + other(dot_tn(a[:, half:], dzr)),
            bias_grad + other(bias_grad),
            *(pieces_sum(x) for x in (by_rows(b, d_gate), by_rows(b, d_up), by_columns(m, g))),
        )
    grad_input = finish(grad)
    gain_total = sum_over(sum_over(jnp.stack(gain_grads), "tensor"), "context")
    gain_total = gain_total[:, :half] + other(gain_total[:, half:])
    s = [jnp.stack([results[layer][k] for layer in range(layers)]) for k in range(10)]
    return (
        output, grad_input, s[0], s[1], s[2], s[3], s[4], s[5], s[6],
        gain_total[:layers], gain_total[layers:], s[7], s[8], s[9],
    )


def solution(mesh):
    rows = P("fsdp", "context", None)
    wide, tall = P(None, "fsdp", "tensor"), P(None, "tensor", "fsdp")
    heads, gain = P(None, "tensor"), P(None, "fsdp")
    return jax.shard_map(
        local,
        mesh=mesh,
        in_specs=(
            rows, P("fsdp", "context"), wide, wide, wide, wide, tall, wide, heads, gain, gain, wide, wide, tall, rows,
        ),
        out_specs=(rows, rows, wide, wide, wide, wide, tall, wide, heads, gain, gain, wide, wide, tall),
        check_vma=False,
    )
```

time: 951 us -> 762 us (0.80)
  matrix products: 163 us -> 81.1 us
  starting transfers between devices: 236 us -> 155 us
  Pallas kernels: 103 us -> 179 us
  waiting for transfers between devices: 314 us -> 257 us
  other arithmetic: 73.3 us -> 43.1 us
    dot_general x68 -> x36, matrix products: 163 us -> 81.1 us  [dot_tn(): lax.dot_general(a, b, (((0,), (0,)), ((), ())), preferred_element_type=f32)]
    ppermute x186 -> x136, starting transfers between devices: 236 us -> 155 us  [swap(): return lax.ppermute(x, axis, [(i, i ^ k) for i in range(n)])]
    pallas_call x4 -> x10, Pallas kernels: 103 us -> 179 us  [the longest x2 64 us: attention_backward(): pl.pallas_call(functools.partial(backward_kernel, len(parts), count_t, bl...]
    ppermute x186 -> x136, waiting for transfers between devices: 314 us -> 257 us  [swap(): return lax.ppermute(x, axis, [(i, i ^ k) for i in range(n)])]
    concatenate x7 -> x10, other arithmetic: 41.1 us -> 2.59 us  [the longest x1 1.39 us: full(): return jnp.concatenate([w, other(w)], axis=axis)]
    unnamed x388 -> x349, local copies, waits for them, and re-layouts: 28.6 us -> 17.8 us
  transfers between devices with their start and end apart: 186 -> 136, of which waited for: 90 -> 63; matrix products, arithmetic and copies ran while one was open for 28% -> 18% of each run, Pallas kernels for 11% -> 23%
where the time goes in v2:
time: 762 us; the launch traced here: 757 us
  waiting for transfers between devices  257 us (34%)
  Pallas kernels  179 us (23%)
  starting transfers between devices  155 us (20%)
  matrix products  81.1 us (11%)
  other arithmetic  43.1 us (6%)
  local copies, waits for them, and re-layouts  36 us (5%)
    ppermute x136, waiting for transfers between devices, swap(): return lax.ppermute(x, axis, [(i, i ^ k) for i in range(n)])  257 us
    ppermute x136, starting transfers between devices, swap(): return lax.ppermute(x, axis, [(i, i ^ k) for i in range(n)])  155 us
    dot_general x36, matrix products, dot_tn(): lax.dot_general(a, b, (((0,), (0,)), ((), ())), preferred_element_type=f32)  81.1 us
    pallas_call x2, Pallas kernels, attention_backward(): pl.pallas_call(functools.partial(backward_kernel, len(parts), count_t, bl...  64 us
    pallas_call x2, Pallas kernels, attention_forward(): pl.pallas_call(functools.partial(forward_kernel, len(parts), count_t, blo...  53.4 us
    pallas_call x2, Pallas kernels, ffn_inner(): pl.pallas_call(functools.partial(ffn_inner_kernel, len(b_parts), block),...  32.7 us
    another operation x12, other arithmetic, local(): jnp.stack([results[layer][k] for layer in range(layers)])  19.8 us
    unnamed x349, local copies, waits for them, and re-layouts  17.8 us
  transfers between devices with their start and end apart: 136, of which 63 were waited for; matrix products, arithmetic and copies ran while one was open for 18% of the time, Pallas kernels for 23%

profile of v2, /device:TPU:0, one launch (start us, length us, event | category | flops | bytes accessed | tf_op | source)
XLA Modules:
  0.0 757.0 jit_solution(10090341627761046116)
XLA Ops:
  14.7 12.8 %collective-permute-done.2 = bf16[64,1536]{1,0:T(8,128)(2,1)S(1)} collective-permute-done((bf16[64,1536]{1,0:T(8,128)(2,1)S(1)}, bf16[64,1536]{1,0:T(8,128)(2,1)S(1)}, u32[]{:S(2)}, u32[]{:S(2)}) %collective-permute-start.2) | collective-permute-done | bytes 196640 | tf_op jit(solution)/shard_map/ppermute | solution.py:25
  49.2 8.3 %collective-permute-done.5.refs_5_ = bf16[128,1536]{1,0:T(8,128)(2,1)} collective-permute-done((bf16[128,1536]{1,0:T(8,128)(2,1)S(1)}, bf16[128,1536]{1,0:T(8,128)(2,1)}, u32[]{:S(2)}, u32[]{:S(2)}) %collective-permute-start.5) | collective-permute-done | bytes 393248 | tf_op jit(solution)/shard_map/ppermute | solution.py:25
  59.0 9.8 %collective-permute-done.6.refs_6_ = bf16[128,1536]{1,0:T(8,128)(2,1)S(1)} collective-permute-done((bf16[128,1536]{1,0:T(8,128)(2,1)S(1)}, bf16[128,1536]{1,0:T(8,128)(2,1)S(1)}, u32[]{:S(2)}, u32[]{:S(2)}) %collective-permute-start.6) | collective-permute-done | bytes 393248 | tf_op jit(solution)/shard_map/ppermute | solution.py:25
  83.2 26.7 %shard_map.254 = (bf16[1024,1536]{1,0:T(8,128)(2,1)}, bf16[1024,384]{1,0:T(8,128)(2,1)}, bf16[1024,384]{1,0:T(8,128)(2,1)}, bf16[1024,384]{1,0:T(8,128)(2,1)}, f...) custom-call(s32[20]{0:T(128)} %stack.188.refs_0_, ...), custom_call_target="tpu_custom_call" | custom-call | tf_op jit(solution)/shard_map/pallas_call | solution.py:495
  112.0 6.3 collective-permute-done.18
  128.2 4.6 collective-permute-done.21
  139.1 6.5 shard_map.255
  168.0 15.7 %collective-permute-done.32 = bf16[64,1536]{1,0:T(8,128)(2,1)S(1)} collective-permute-done((bf16[64,1536]{1,0:T(8,128)(2,1)S(1)}, bf16[64,1536]{1,0:T(8,128)(2,1)S(1)}, u32[]{:S(2)}, u32[]{:S(2)}) %collective-permute-start.32) | collective-permute-done | bytes 196640 | tf_op jit(solution)/shard_map/ppermute | solution.py:25
  203.0 26.7 %shard_map.256 = (bf16[1024,1536]{1,0:T(8,128)(2,1)}, bf16[1024,384]{1,0:T(8,128)(2,1)}, bf16[1024,384]{1,0:T(8,128)(2,1)}, bf16[1024,384]{1,0:T(8,128)(2,1)}, f...) custom-call(s32[20]{0:T(128)} %stack.188.refs_0_, ...), custom_call_target="tpu_custom_call" | custom-call | tf_op jit(solution)/shard_map/pallas_call | solution.py:495
  252.5 6.8 shard_map.257
  259.4 8.1 %shard_map.258 = (f32[64,1536]{1,0:T(8,128)S(1)}, bf16[64,1536]{1,0:T(8,128)(2,1)S(1)}, bf16[64,1536]{1,0:T(8,128)(2,1)S(1)}, bf16[64,1536]{1,0:T(8,128)(2,1)S(1)}) custom-call(bf16[256,1536]{1,0:T(8,128)(2,1)S(1)} %copy-done.4, f32[256,1024]{1,0:T(8,128)S(1)} %get-tuple-element.106.gt_ref, f32[256,1024]{1,0:T(8,128)S(1)} %get-tuple-element.107.up_ref, ...), custom_call_target="tpu_custom_call" | custom-call | tf_op jit(solution)/shard_map/pallas_call | solution.py:577
  286.7 8.6 %collective-permute-done.56 = bf16[64,1536]{1,0:T(8,128)(2,1)S(1)} collective-permute-done((bf16[64,1536]{1,0:T(8,128)(2,1)S(1)}, bf16[64,1536]{1,0:T(8,128)(2,1)S(1)}, u32[]{:S(2)}, u32[]{:S(2)}) %collective-permute-start.56) | collective-permute-done | bytes 196640 | tf_op jit(solution)/shard_map/ppermute | solution.py:25
  313.1 7.1 collective-permute-done.60.refs_6_
  323.0 9.2 %collective-permute-done.120 = bf16[64,1536]{1,0:T(8,128)(2,1)S(1)} collective-permute-done((bf16[64,1536]{1,0:T(8,128)(2,1)S(1)}, bf16[64,1536]{1,0:T(8,128)(2,1)S(1)}, u32[]{:S(2)}, u32[]{:S(2)}) %collective-permute-start.120) | collective-permute-done | bytes 196640 | tf_op jit(solution)/shard_map/ppermute | solution.py:25
  334.4 5.3 collective-permute-done.121
  342.7 31.8 %shard_map.259 = (bf16[1024,1536]{1,0:T(8,128)(2,1)}, bf16[1024,384]{1,0:T(8,128)(2,1)}, bf16[1024,384]{1,0:T(8,128)(2,1)}, bf16[1024,384]{1,0:T(8,128)(2,1)}, b...) custom-call(s32[20]{0:T(128)} %stack.188.refs_0_, ...), custom_call_target="tpu_custom_call" | custom-call | tf_op jit(solution)/shard_map/pallas_call | solution.py:525
  410.5 4.9 collective-permute-done.48
  429.0 7.5 shard_map.260
  438.4 4.8 collective-permute-done.129.refs_10_
  448.5 13.1 %collective-permute-done.123.refs_4_ = bf16[128,1536]{1,0:T(8,128)(2,1)S(1)} collective-permute-done((bf16[128,1536]{1,0:T(8,128)(2,1)S(1)}, bf16[128,1536]{1,0:T(8,128)(2,1)S(1)}, u32[]{:S(2)}, u32[]{:S(2)}) %collective-permute-start.123) | collective-permute-done | bytes 393248 | tf_op jit(solution)/shard_map/ppermute | solution.py:25
  465.9 16.4 %shard_map.263 = (bf16[1024,1536]{1,0:T(8,128)(2,1)}, bf16[1024,1536]{1,0:T(8,128)(2,1)}, bf16[1024,1024]{1,0:T(8,128)(2,1)}, bf16[1024,1024]{1,0:T(8,128)(2,1)}, bf16[1024,1024]{1,0:T(8,128)(2,1)}) custom-call(bf16[256,1536]{1,0:T(8,128)(2,1)} %copy-done.2, bf16[256,1536]{1,0:T(8,128)(2,1)} %copy-done.54, bf16[128,1536]{1,0:T(8,128)(2,1)} %copy-done.45, ...), custom_call_target="tpu_custom_call" | custom-call | tf_op jit(solution)/shard_map/pallas_call | solution.py:592
  482.3 5.2 convolution_convert_fusion.4
  509.3 9.4 %collective-permute-done.74 = bf16[64,1536]{1,0:T(8,128)(2,1)S(1)} collective-permute-done((bf16[64,1536]{1,0:T(8,128)(2,1)S(1)}, bf16[64,1536]{1,0:T(8,128)(2,1)S(1)}, u32[]{:S(2)}, u32[]{:S(2)}) %collective-permute-start.74) | collective-permute-done | bytes 196640 | tf_op jit(solution)/shard_map/ppermute | solution.py:25
  520.2 7.3 collective-permute-done.75
  536.4 8.2 %collective-permute-done.78.refs_6_ = bf16[128,1536]{1,0:T(8,128)(2,1)S(1)} collective-permute-done((bf16[128,1536]{1,0:T(8,128)(2,1)S(1)}, bf16[128,1536]{1,0:T(8,128)(2,1)S(1)}, u32[]{:S(2)}, u32[]{:S(2)}) %collective-permute-start.78) | collective-permute-done | bytes 393248 | tf_op jit(solution)/shard_map/ppermute | solution.py:25
  548.7 5.8 collective-permute-done.113
  563.6 32.2 %shard_map.261 = (bf16[1024,1536]{1,0:T(8,128)(2,1)}, bf16[1024,384]{1,0:T(8,128)(2,1)}, bf16[1024,384]{1,0:T(8,128)(2,1)}, bf16[1024,384]{1,0:T(8,128)(2,1)}, b...) custom-call(s32[20]{0:T(128)} %stack.188.refs_0_, ...), custom_call_target="tpu_custom_call" | custom-call | tf_op jit(solution)/shard_map/pallas_call | solution.py:525
  615.0 5.8 collective-permute-done.79
  652.6 10.7 %collective-permute-done.110.refs_4_ = bf16[128,1536]{1,0:T(8,128)(2,1)S(1)} collective-permute-done((bf16[128,1536]{1,0:T(8,128)(2,1)S(1)}, bf16[128,1536]{1,0:T(8,128)(2,1)S(1)}, u32[]{:S(2)}, u32[]{:S(2)}) %collective-permute-start.110) | collective-permute-done | bytes 393248 | tf_op jit(solution)/shard_map/ppermute | solution.py:25
  675.1 7.8 %collective-permute-done.115.refs_9_ = bf16[128,1536]{1,0:T(8,128)(2,1)S(1)} collective-permute-done((bf16[128,1536]{1,0:T(8,128)(2,1)S(1)}, bf16[128,1536]{1,0:T(8,128)(2,1)S(1)}, u32[]{:S(2)}, u32[]{:S(2)}) %collective-permute-start.115) | collective-permute-done | bytes 393248 | tf_op jit(solution)/shard_map/ppermute | solution.py:25
  682.8 7.4 collective-permute-done.116.refs_10_
  691.9 16.3 %shard_map.262 = (bf16[1024,1536]{1,0:T(8,128)(2,1)}, bf16[1024,1536]{1,0:T(8,128)(2,1)}, bf16[1024,1024]{1,0:T(8,128)(2,1)}, bf16[1024,1024]{1,0:T(8,128)(2,1)}, bf16[1024,1024]{1,0:T(8,128)(2,1)}) custom-call(bf16[256,1536]{1,0:T(8,128)(2,1)} %copy-done.1, bf16[256,1536]{1,0:T(8,128)(2,1)} %collective-permute-done.106.refs_1_, ...), custom_call_target="tpu_custom_call" | custom-call | tf_op jit(solution)/shard_map/pallas_call | solution.py:592
  (740 shorter events, 394.2 us)
Async XLA Ops:
  29.4 39.8 %collective-permute-start.7 = (bf16[2,768,384]{2,1,0:T(8,128)(2,1)S(1)}, bf16[2,768,384]{2,1,0:T(8,128)(2,1)S(1)}, u32[]{:S(2)}, u32[]{:S(2)}) collective-permute-start(bf16[2,768,384]{2,1,0:T(8,128)(2,1)S(1)} %copy-done.11), channel_id=1, source_target_pairs={{0,16},{16,0},{1,17},{17,1},{2,18},{18,2},{3,19},{19,3},{4,20},{20... | collective-permute-start | bytes 3538952 | tf_op jit(solution)/shard_map/ppermute | solution.py:25
  29.4 40.0 %collective-permute-start.8 = (bf16[2,768,384]{2,1,0:T(8,128)(2,1)S(1)}, bf16[2,768,384]{2,1,0:T(8,128)(2,1)S(1)}, u32[]{:S(2)}, u32[]{:S(2)}) collective-permute-start(bf16[2,768,384]{2,1,0:T(8,128)(2,1)S(1)} %copy-done.12), channel_id=1, source_target_pairs={{0,16},{16,0},{1,17},{17,1},{2,18},{18,2},{3,19},{19,3},{4,20},{20... | collective-permute-start | bytes 3538952 | tf_op jit(solution)/shard_map/ppermute | solution.py:25
  29.9 39.9 %collective-permute-start.9 = (bf16[2,768,384]{2,1,0:T(8,128)(2,1)S(1)}, bf16[2,768,384]{2,1,0:T(8,128)(2,1)S(1)}, u32[]{:S(2)}, u32[]{:S(2)}) collective-permute-start(bf16[2,768,384]{2,1,0:T(8,128)(2,1)S(1)} %copy-done.13), channel_id=1, source_target_pairs={{0,16},{16,0},{1,17},{17,1},{2,18},{18,2},{3,19},{19,3},{4,20},{20... | collective-permute-start | bytes 3538952 | tf_op jit(solution)/shard_map/ppermute | solution.py:25
  69.3 69.3 %collective-permute-start.22 = (bf16[2,768,1024]{2,1,0:T(8,128)(2,1)S(1)}, bf16[2,768,1024]{2,1,0:T(8,128)(2,1)}, u32[]{:S(2)}, u32[]{:S(2)}) collective-permute-start(bf16[2,768,1024]{2,1,0:T(8,128)(2,1)S(1)} %copy-done), channel_id=1, source_target_pairs={{0,16},{16,0},{1,17},{17,1},{2,18},{18,2},{3,19},{19,3},{4,20},{20... | collective-permute-start | bytes 9437192 | tf_op jit(solution)/shard_map/ppermute | solution.py:25
  69.4 69.2 %collective-permute-start.23 = (bf16[2,768,1024]{2,1,0:T(8,128)(2,1)}, bf16[2,768,1024]{2,1,0:T(8,128)(2,1)}, u32[]{:S(2)}, u32[]{:S(2)}) collective-permute-start(bf16[2,768,1024]{2,1,0:T(8,128)(2,1)} %refs_13_.3), channel_id=1, source_target_pairs={{0,16},{16,0},{1,17},{17,1},{2,18},{18,2},{3,19},{19,3},{4,20},{20... | collective-permute-start | bytes 9437192 | tf_op jit(solution)/shard_map/ppermute | solution.py:25
  71.7 67.4 %collective-permute-start.24 = (bf16[2,1024,768]{2,1,0:T(8,128)(2,1)}, bf16[2,1024,768]{2,1,0:T(8,128)(2,1)}, u32[]{:S(2)}, u32[]{:S(2)}) collective-permute-start(bf16[2,1024,768]{2,1,0:T(8,128)(2,1)} %refs_14_.3), channel_id=1, source_target_pairs={{0,16},{16,0},{1,17},{17,1},{2,18},{18,2},{3,19},{19,3},{4,20},{20... | collective-permute-start | bytes 9437192 | tf_op jit(solution)/shard_map/ppermute | solution.py:25
  166.8 35.3 %collective-permute-start.31 = (bf16[256,1536]{1,0:T(8,128)(2,1)S(1)}, bf16[256,1536]{1,0:T(8,128)(2,1)S(1)}, u32[]{:S(2)}, u32[]{:S(2)}) collective-permute-start(bf16[256,1536]{1,0:T(8,128)(2,1)S(1)} %pad_maximum_fusion.10.refs_1_), channel_id=1, source_target_pairs={{0,4},{4,0},{8,12},{12,8},{1,5},{5,1},{9,13},{13,9},{2,6},{6,2},{1... | collective-permute-start | bytes 2359304 | tf_op jit(solution)/shard_map/ppermute | solution.py:25
  188.6 44.7 %collective-permute-start.127 = (bf16[64,1536]{1,0:T(8,128)(2,1)}, bf16[64,1536]{1,0:T(8,128)(2,1)}, u32[]{:S(2)}, u32[]{:S(2)}) collective-permute-start(bf16[64,1536]{1,0:T(8,128)(2,1)} %get-tuple-element.234), channel_id=1, source_target_pairs={{0,12},{4,8},{8,4},{12,0},{1,13},{5,9},{9,5},{13,1},{2,14},{6,10},... | collective-permute-start | bytes 589832 | tf_op jit(solution)/shard_map/ppermute | solution.py:25
  195.8 250.3 %collective-permute-start.125 = (bf16[256,1536]{1,0:T(8,128)(2,1)}, bf16[256,1536]{1,0:T(8,128)(2,1)}, u32[]{:S(2)}, u32[]{:S(2)}) collective-permute-start(bf16[256,1536]{1,0:T(8,128)(2,1)} %get-tuple-element.255), channel_id=1, source_target_pairs={{0,4},{4,0},{8,12},{12,8},{1,5},{5,1},{9,13},{13,9},{2,6},{6,2},{1... | collective-permute-start | bytes 2359304 | tf_op jit(solution)/shard_map/ppermute | solution.py:25
  245.1 38.5 %collective-permute-start.107 = (bf16[64,1536]{1,0:T(8,128)(2,1)S(1)}, bf16[64,1536]{1,0:T(8,128)(2,1)S(1)}, u32[]{:S(2)}, u32[]{:S(2)}) collective-permute-start(bf16[64,1536]{1,0:T(8,128)(2,1)S(1)} %broadcast_add_fusion.7), channel_id=1, source_target_pairs={{0,8},{4,12},{8,0},{12,4},{1,9},{5,13},{9,1},{13,5},{2,10},{6,14},... | collective-permute-start | bytes 589832 | tf_op jit(solution)/shard_map/ppermute | solution.py:25
  276.2 29.1 %collective-permute-start.108 = (bf16[64,1536]{1,0:T(8,128)(2,1)S(1)}, bf16[64,1536]{1,0:T(8,128)(2,1)S(1)}, u32[]{:S(2)}, u32[]{:S(2)}) collective-permute-start(bf16[64,1536]{1,0:T(8,128)(2,1)S(1)} %broadcast_add_fusion.7), channel_id=1, source_target_pairs={{0,12},{4,8},{8,4},{12,0},{1,13},{5,9},{9,5},{13,1},{2,14},{6,10},... | collective-permute-start | bytes 589832 | tf_op jit(solution)/shard_map/ppermute | solution.py:25
  306.7 34.4 %collective-permute-start.58 = (bf16[128,1536]{1,0:T(8,128)(2,1)S(1)}, bf16[128,1536]{1,0:T(8,128)(2,1)S(1)}, u32[]{:S(2)}, u32[]{:S(2)}) collective-permute-start(bf16[128,1536]{1,0:T(8,128)(2,1)S(1)} %constant_dynamic-update-slice_fusion.4.refs_3_), channel_id=1, source_target_pairs={{0,1},{1,0},{2,3},{3,2},{4,5},{5,4},{6,7},{7,6},{8,9},{9,8},{10,11... | collective-permute-start | bytes 1179656 | tf_op jit(solution)/shard_map/ppermute | solution.py:25
  308.2 32.9 %collective-permute-start.59 = (bf16[128,1536]{1,0:T(8,128)(2,1)S(1)}, bf16[128,1536]{1,0:T(8,128)(2,1)S(1)}, u32[]{:S(2)}, u32[]{:S(2)}) collective-permute-start(bf16[128,1536]{1,0:T(8,128)(2,1)S(1)} %constant_dynamic-update-slice_fusion.4.refs_3_), channel_id=1, source_target_pairs={{0,2},{1,3},{2,0},{3,1},{4,6},{5,7},{6,4},{7,5},{8,10},{9,11},{10,... | collective-permute-start | bytes 1179656 | tf_op jit(solution)/shard_map/ppermute | solution.py:25
  311.2 30.0 %collective-permute-start.55 = (bf16[256,1536]{1,0:T(8,128)(2,1)S(1)}, bf16[256,1536]{1,0:T(8,128)(2,1)S(1)}, u32[]{:S(2)}, u32[]{:S(2)}) collective-permute-start(bf16[256,1536]{1,0:T(8,128)(2,1)S(1)} %pad_maximum_fusion.15.refs_1_), channel_id=1, source_target_pairs={{0,4},{4,0},{8,12},{12,8},{1,5},{5,1},{9,13},{13,9},{2,6},{6,2},{1... | collective-permute-start | bytes 2359304 | tf_op jit(solution)/shard_map/ppermute | solution.py:25
  339.7 96.9 %collective-permute-start.128 = (bf16[128,1536]{1,0:T(8,128)(2,1)}, bf16[128,1536]{1,0:T(8,128)(2,1)}, u32[]{:S(2)}, u32[]{:S(2)}) collective-permute-start(bf16[128,1536]{1,0:T(8,128)(2,1)} %constant_dynamic-update-slice_fusion.14.refs_8_), channel_id=1, source_target_pairs={{0,1},{1,0},{2,3},{3,2},{4,5},{5,4},{6,7},{7,6},{8,9},{9,8},{10,11... | collective-permute-start | bytes 1179656 | tf_op jit(solution)/shard_map/ppermute | solution.py:25
  428.9 36.2 %collective-permute-start.119 = (bf16[256,1536]{1,0:T(8,128)(2,1)S(1)}, bf16[256,1536]{1,0:T(8,128)(2,1)S(1)}, u32[]{:S(2)}, u32[]{:S(2)}) collective-permute-start(bf16[256,1536]{1,0:T(8,128)(2,1)S(1)} %copy-done.59), channel_id=1, source_target_pairs={{0,4},{4,0},{8,12},{12,8},{1,5},{5,1},{9,13},{13,9},{2,6},{6,2},{1... | collective-permute-start | bytes 2359304 | tf_op jit(solution)/shard_map/ppermute | solution.py:25
  446.2 228.8 %collective-permute-start.106 = (bf16[256,1536]{1,0:T(8,128)(2,1)}, bf16[256,1536]{1,0:T(8,128)(2,1)}, u32[]{:S(2)}, u32[]{:S(2)}) collective-permute-start(bf16[256,1536]{1,0:T(8,128)(2,1)} %broadcast_add_fusion.3), channel_id=1, source_target_pairs={{0,4},{4,0},{8,12},{12,8},{1,5},{5,1},{9,13},{13,9},{2,6},{6,2},{1... | collective-permute-start | bytes 2359304 | tf_op jit(solution)/shard_map/ppermute | solution.py:25
  448.5 47.3 %collective-permute-start.86 = (bf16[768,384]{1,0:T(8,128)(2,1)}, bf16[768,384]{1,0:T(8,128)(2,1)}, u32[]{:S(2)}, u32[]{:S(2)}) collective-permute-start(bf16[768,384]{1,0:T(8,128)(2,1)} %convolution_convert_fusion.12), channel_id=1, source_target_pairs={{0,16},{16,0},{1,17},{17,1},{2,18},{18,2},{3,19},{19,3},{4,20},{20... | collective-permute-start | bytes 1769480 | tf_op jit(solution)/shard_map/ppermute | solution.py:25
  461.6 33.2 %collective-permute-start.69 = (bf16[64,1536]{1,0:T(8,128)(2,1)S(1)}, bf16[64,1536]{1,0:T(8,128)(2,1)S(1)}, u32[]{:S(2)}, u32[]{:S(2)}) collective-permute-start(bf16[64,1536]{1,0:T(8,128)(2,1)S(1)} %get-tuple-element.128), channel_id=1, source_target_pairs={{0,3},{1,2},{2,1},{3,0},{4,7},{5,6},{6,5},{7,4},{8,11},{9,10},{10,... | collective-permute-start | bytes 589832 | tf_op jit(solution)/shard_map/ppermute | solution.py:25
  464.2 30.6 %collective-permute-start.68 = (bf16[64,1536]{1,0:T(8,128)(2,1)S(1)}, bf16[64,1536]{1,0:T(8,128)(2,1)S(1)}, u32[]{:S(2)}, u32[]{:S(2)}) collective-permute-start(bf16[64,1536]{1,0:T(8,128)(2,1)S(1)} %get-tuple-element.127), channel_id=1, source_target_pairs={{0,2},{1,3},{2,0},{3,1},{4,6},{5,7},{6,4},{7,5},{8,10},{9,11},{10,... | collective-permute-start | bytes 589832 | tf_op jit(solution)/shard_map/ppermute | solution.py:25
  465.0 30.3 %collective-permute-start.67 = (bf16[64,1536]{1,0:T(8,128)(2,1)S(1)}, bf16[64,1536]{1,0:T(8,128)(2,1)S(1)}, u32[]{:S(2)}, u32[]{:S(2)}) collective-permute-start(bf16[64,1536]{1,0:T(8,128)(2,1)S(1)} %get-tuple-element.126), channel_id=1, source_target_pairs={{0,1},{1,0},{2,3},{3,2},{4,5},{5,4},{6,7},{7,6},{8,9},{9,8},{10,11... | collective-permute-start | bytes 589832 | tf_op jit(solution)/shard_map/ppermute | solution.py:25
  495.9 32.5 %collective-permute-start.94 = (bf16[384,768]{1,0:T(8,128)(2,1)S(1)}, bf16[384,768]{1,0:T(8,128)(2,1)S(1)}, u32[]{:S(2)}, u32[]{:S(2)}) collective-permute-start(bf16[384,768]{1,0:T(8,128)(2,1)S(1)} %copy-done.164), channel_id=1, source_target_pairs={{0,16},{16,0},{1,17},{17,1},{2,18},{18,2},{3,19},{19,3},{4,20},{20... | collective-permute-start | bytes 1769480 | tf_op jit(solution)/shard_map/ppermute | solution.py:25
  500.4 31.8 %collective-permute-start.72 = (bf16[64,1536]{1,0:T(8,128)(2,1)S(1)}, bf16[64,1536]{1,0:T(8,128)(2,1)S(1)}, u32[]{:S(2)}, u32[]{:S(2)}) collective-permute-start(bf16[64,1536]{1,0:T(8,128)(2,1)S(1)} %get-tuple-element.239), channel_id=1, source_target_pairs={{0,3},{1,2},{2,1},{3,0},{4,7},{5,6},{6,5},{7,4},{8,11},{9,10},{10,... | collective-permute-start | bytes 589832 | tf_op jit(solution)/shard_map/ppermute | solution.py:25
  532.2 30.2 %collective-permute-start.76 = (bf16[128,1536]{1,0:T(8,128)(2,1)S(1)}, bf16[128,1536]{1,0:T(8,128)(2,1)S(1)}, u32[]{:S(2)}, u32[]{:S(2)}) collective-permute-start(bf16[128,1536]{1,0:T(8,128)(2,1)S(1)} %constant_dynamic-update-slice_fusion.6.refs_3_), channel_id=1, source_target_pairs={{0,1},{1,0},{2,3},{3,2},{4,5},{5,4},{6,7},{7,6},{8,9},{9,8},{10,11... | collective-permute-start | bytes 1179656 | tf_op jit(solution)/shard_map/ppermute | solution.py:25
  533.1 29.4 %collective-permute-start.77 = (bf16[128,1536]{1,0:T(8,128)(2,1)S(1)}, bf16[128,1536]{1,0:T(8,128)(2,1)S(1)}, u32[]{:S(2)}, u32[]{:S(2)}) collective-permute-start(bf16[128,1536]{1,0:T(8,128)(2,1)S(1)} %constant_dynamic-update-slice_fusion.6.refs_3_), channel_id=1, source_target_pairs={{0,2},{1,3},{2,0},{3,1},{4,6},{5,7},{6,4},{7,5},{8,10},{9,11},{10,... | collective-permute-start | bytes 1179656 | tf_op jit(solution)/shard_map/ppermute | solution.py:25
  562.4 78.9 %collective-permute-start.131 = (bf16[768,1024]{1,0:T(8,128)(2,1)}, bf16[768,1024]{1,0:T(8,128)(2,1)}, u32[]{:S(2)}, u32[]{:S(2)}) collective-permute-start(bf16[768,1024]{1,0:T(8,128)(2,1)} %convolution_convert_fusion.4), channel_id=1, source_target_pairs={{0,16},{16,0},{1,17},{17,1},{2,18},{18,2},{3,19},{19,3},{4,20},{20... | collective-permute-start | bytes 4718600 | tf_op jit(solution)/shard_map/ppermute | solution.py:25
  651.4 39.6 %collective-permute-start.112 = (bf16[256,1536]{1,0:T(8,128)(2,1)S(1)}, bf16[256,1536]{1,0:T(8,128)(2,1)S(1)}, u32[]{:S(2)}, u32[]{:S(2)}) collective-permute-start(bf16[256,1536]{1,0:T(8,128)(2,1)S(1)} %copy-done.58), channel_id=1, source_target_pairs={{0,4},{4,0},{8,12},{12,8},{1,5},{5,1},{9,13},{13,9},{2,6},{6,2},{1... | collective-permute-start | bytes 2359304 | tf_op jit(solution)/shard_map/ppermute | solution.py:25
  675.0 43.0 %collective-permute-start.85 = (bf16[768,384]{1,0:T(8,128)(2,1)}, bf16[768,384]{1,0:T(8,128)(2,1)}, u32[]{:S(2)}, u32[]{:S(2)}) collective-permute-start(bf16[768,384]{1,0:T(8,128)(2,1)} %convolution_convert_fusion.13), channel_id=1, source_target_pairs={{0,16},{16,0},{1,17},{17,1},{2,18},{18,2},{3,19},{19,3},{4,20},{20... | collective-permute-start | bytes 1769480 | tf_op jit(solution)/shard_map/ppermute | solution.py:25
  682.8 38.5 %collective-permute-start.87 = (bf16[768,384]{1,0:T(8,128)(2,1)}, bf16[768,384]{1,0:T(8,128)(2,1)}, u32[]{:S(2)}, u32[]{:S(2)}) collective-permute-start(bf16[768,384]{1,0:T(8,128)(2,1)} %convolution_convert_fusion.11), channel_id=1, source_target_pairs={{0,16},{16,0},{1,17},{17,1},{2,18},{18,2},{3,19},{19,3},{4,20},{20... | collective-permute-start | bytes 1769480 | tf_op jit(solution)/shard_map/ppermute | solution.py:25
  690.3 33.4 %collective-permute-start.89 = (bf16[768,384]{1,0:T(8,128)(2,1)}, bf16[768,384]{1,0:T(8,128)(2,1)}, u32[]{:S(2)}, u32[]{:S(2)}) collective-permute-start(bf16[768,384]{1,0:T(8,128)(2,1)} %convolution_convert_fusion.9), channel_id=1, source_target_pairs={{0,16},{16,0},{1,17},{17,1},{2,18},{18,2},{3,19},{19,3},{4,20},{20... | collective-permute-start | bytes 1769480 | tf_op jit(solution)/shard_map/ppermute | solution.py:25
  690.3 35.9 %collective-permute-start.91 = (bf16[768,384]{1,0:T(8,128)(2,1)}, bf16[768,384]{1,0:T(8,128)(2,1)}, u32[]{:S(2)}, u32[]{:S(2)}) collective-permute-start(bf16[768,384]{1,0:T(8,128)(2,1)} %convolution_convert_fusion.7), channel_id=1, source_target_pairs={{0,16},{16,0},{1,17},{17,1},{2,18},{18,2},{3,19},{19,3},{4,20},{20... | collective-permute-start | bytes 1769480 | tf_op jit(solution)/shard_map/ppermute | solution.py:25
  691.0 44.1 %collective-permute-start.93 = (bf16[384,768]{1,0:T(8,128)(2,1)}, bf16[384,768]{1,0:T(8,128)(2,1)S(1)}, u32[]{:S(2)}, u32[]{:S(2)}) collective-permute-start(bf16[384,768]{1,0:T(8,128)(2,1)} %fusion.40), channel_id=1, source_target_pairs={{0,16},{16,0},{1,17},{17,1},{2,18},{18,2},{3,19},{19,3},{4,20},{20... | collective-permute-start | bytes 1769480 | tf_op jit(solution)/shard_map/ppermute | solution.py:25
  (274 other events, 3549.2 us)

commit v3 on v2

--- a/solution.py
+++ b/solution.py
@@ -31,35 +31,29 @@
 
 
 def after(x, token):
-    return x + (token[:1, :1].astype(f32) * 0.0).astype(x.dtype)
-
-
-def all_rows(own, token=None):
+    return x if token is None else x + (token[:1, :1].astype(f32) * 0.0).astype(x.dtype)
+
+
+def all_rows(own, first=None, second=None, shard=None):
     count_z, count_t = lax.axis_size("context"), lax.axis_size("tensor")
-    block = own.shape[0] // count_t
-    shard = own[:block]
-    if token is not None:
-        shard = after(shard, token)
-        own_sent = after(own, token)
-    else:
-        own_sent = own
     if count_z != 4:
-        return (lax.all_gather(own_sent, "context", tiled=True),)
-    far = [swap(shard, "context", 2), swap(shard, "context", 3)]
-    near = swap(own_sent, "context", 1)
-    far = jnp.concatenate(far, axis=0)
-    return (own, near, far) + tuple(swap(far, "tensor", k) for k in range(1, count_t))
+        return (lax.all_gather(own, "context", tiled=True),)
+    if shard is None:
+        shard = own[: own.shape[0] // count_t]
+    shard = after(shard, first)
+    parts = [own, None]
+    for kz in (2, 3):
+        far = after(swap(shard, "context", kz), second)
+        parts += [far] + [swap(far, "tensor", k) for k in range(1, count_t)]
+    parts[1] = swap(after(own, first), "context", 1)
+    return tuple(parts)
 
 
 def row_places():
     count_z, count_t = lax.axis_size("context"), lax.axis_size("tensor")
     z, t = lax.axis_index("context"), lax.axis_index("tensor")
+    parts = [((z ^ p) if count_z == 4 else p, k) for p in range(count_z) for k in range(count_t)]
     own = [(z, k) for k in range(count_t)]
-    if count_z != 4:
-        parts = [(p, k) for p in range(count_z) for k in range(count_t)]
-    else:
-        parts = [(z ^ kz, k) for kz in (0, 1) for k in range(count_t)]
-        parts += [(z ^ kz, k) for k in range(count_t) for kz in (2, 3)]
     return jnp.stack([(p * count_t + (t ^ k)).astype(jnp.int32) for p, k in own + parts])
 
 
@@ -161,31 +155,40 @@
     return jnp.sum(jnp.where(lane == head, table, 0.0), axis=1, keepdims=True)
 
 
-def mix_decay(q_ref, k_ref, decay_ref, pair, qa, qb, ka, kb):
-    rows = chunk_rows
-
+def decay_terms(table, pair, head, lane):
+    mine, first = (lane < 64, 64) if head == 0 else (lane >= 64, 0)
+    high, middle, lowest = three_parts(head_column(table, 2 * pair + head))
+    spot = lane - first
+    split = jnp.where((spot == 0) | (spot == 3), high, jnp.where((spot == 1) | (spot == 4), middle, lowest))
+    low_spot, high_spot = (spot >= 0) & (spot < 3), (spot >= 3) & (spot < 6)
+    return mine, split, low_spot, high_spot
+
+
+def mix_keys(k_ref, decay_ref, pair, ka, kb):
     def mix(i):
-        here = rows_at(i, rows)
-        lane = lax.broadcasted_iota(jnp.int32, (rows, pair_lanes), 1)
-        table = decay_ref[here, :]
+        here = rows_at(i, chunk_rows)
+        lane = lax.broadcasted_iota(jnp.int32, (chunk_rows, pair_lanes), 1)
+        k = k_ref[here, :].astype(f32)
+        for head, out in enumerate((ka, kb)):
+            mine, split, low_spot, high_spot = decay_terms(decay_ref[here, :], pair, head, lane)
+            side = jnp.where(low_spot, -split, jnp.where(high_spot, 1.0, 0.0))
+            out[here, :] = jnp.where(mine, k, side).astype(bf16)
+
+    each(k_ref.shape[0] // chunk_rows, mix)
+
+
+def mix_queries(q_ref, decay_ref, start, pair, qa, qb):
+    def mix(i):
+        here = rows_at(i, chunk_rows)
+        lane = lax.broadcasted_iota(jnp.int32, (chunk_rows, pair_lanes), 1)
         q = q_ref[here, :].astype(f32) * 0.125
-        k = k_ref[here, :].astype(f32)
-        for head, (q_out, k_out, first, mine) in enumerate(
-            ((qa, ka, 64, lane < 64), (qb, kb, 0, lane >= 64))
-        ):
-            high, middle, lowest = three_parts(head_column(table, 2 * pair + head))
-            spot = lane - first
-            split = jnp.where(
-                (spot == 0) | (spot == 3), high, jnp.where((spot == 1) | (spot == 4), middle, lowest)
-            )
-            low_spot = (spot >= 0) & (spot < 3)
-            high_spot = (spot >= 3) & (spot < 6)
-            key_side = jnp.where(low_spot, -split, jnp.where(high_spot, 1.0, 0.0))
-            query_side = jnp.where(low_spot, 1.0, jnp.where(high_spot, split, 0.0))
-            q_out[here, :] = jnp.where(mine, q, query_side).astype(bf16)
-            k_out[here, :] = jnp.where(mine, k, key_side).astype(bf16)
-
-    each(q_ref.shape[0] // rows, mix)
+        table = decay_ref[pl.ds(pl.multiple_of(start + i * chunk_rows, chunk_rows), chunk_rows), :]
+        for head, out in enumerate((qa, qb)):
+            mine, split, low_spot, high_spot = decay_terms(table, pair, head, lane)
+            side = jnp.where(low_spot, 1.0, jnp.where(high_spot, split, 0.0))
+            out[here, :] = jnp.where(mine, q, side).astype(bf16)
+
+    each(q_ref.shape[0] // chunk_rows, mix)
 
 
 def live_mask(start_ref, start, first, width, rows):
@@ -223,16 +226,18 @@
     return jnp.concatenate([r[0] for r in refs], axis=1)
 
 
-def forward_kernel(count_parts, count_t, block, join, *refs):
+def forward_own_kernel(count_parts, count_t, block, join, *refs):
     place_ref, parts, refs = refs[0], refs[1 : 1 + count_parts], list(refs[1 + count_parts :])
-    mine, theirs, (wo, to, wf, bias, start_ref) = refs[:4], refs[4:8], refs[8:13]
+    (wq, wk, wv, wg), (tq, tk, tv, tg) = refs[:4], refs[4:8]
+    wo, to, wf, bias, start_ref = refs[8:13]
     refs = refs[13:]
     a_ref = refs.pop(0) if join else parts[0]
-    q_ref, k_ref, v_ref, gate_ref, o_ref, u_ref, z_ref, decay_ref, own_ref = refs[:9]
-    sends, (qa, qb, ka, kb, acc) = refs[9:-5], refs[-5:]
+    k_ref, v_ref, z_ref, decay_ref, own_ref = refs[:5]
+    sends, (q_own, qa, qb, ka, kb, acc) = refs[5:-6], refs[-6:]
     pair = pl.program_id(0)
     seq_len, half = a_ref.shape[0], a_ref.shape[1] // 2
-    rows = query_rows(seq_len)
+    piece_len = count_t * block
+    piece_start = pl.multiple_of(place_ref[0] // count_t * piece_len, piece_len)
 
     @pl.when(pair == 0)
     def _():
@@ -249,18 +254,62 @@
         each(seq_len // chunk_rows, gates)
         decay_ref[...] = shifted_sum(decay_ref[...], False)
 
-    w_mine, w_theirs = lane_blocks(mine), lane_blocks(theirs)
+    w_mine, w_theirs = lane_blocks((wk, wv)), lane_blocks((tk, tv))
+
+    def project(i):
+        here = rows_at(i, chunk_rows)
+        out = dot_nn(a_ref[here, :half], w_mine) + dot_nn(a_ref[here, half:], w_theirs)
+        k_ref[here, :] = out[:, :128].astype(bf16)
+        v_ref[here, :] = out[:, 128:].astype(bf16)
+
+    each(seq_len // chunk_rows, project)
+    piece = pl.ds(piece_start, piece_len)
+    out = dot_nn(a_ref[piece, :half], lane_blocks((wq, wg))) + dot_nn(a_ref[piece, half:], lane_blocks((tq, tg)))
+    q_own[...] = out[:, :128].astype(bf16)
+    gate = jax.nn.sigmoid(out[:, 128:])
+    mix_keys(k_ref, decay_ref, pair, ka, kb)
+    mix_queries(q_own, decay_ref, piece_start, pair, qa, qb)
+    before = seq_len // 2
+    for s in range(0, piece_len, query_rows(seq_len)):
+        rows = query_rows(seq_len)
+        width = before + rows
+        start = pl.multiple_of(piece_start + s, rows)
+        first = pl.multiple_of(jnp.maximum(start - before, 0), rows)
+        mask = live_mask(start_ref, start, first, width, rows)
+        keys = pl.ds(first, width)
+        out = []
+        for q_of, k_of in ((qa, ka), (qb, kb)):
+            p = probabilities(q_of[s : s + rows, :], k_of[keys, :], mask).astype(bf16)
+            out.append(dot_nn(p, v_ref[keys, :]))
+        lane = lax.broadcasted_iota(jnp.int32, (rows, pair_lanes), 1)
+        u = (jnp.where(lane < 64, out[0], out[1]) * gate[s : s + rows, :]).astype(bf16)
+        acc[s : s + rows, :half] += dot_nn(u, wo[0])
+        acc[s : s + rows, half:] += dot_nn(u, to[0])
+
+    @pl.when(pair == pl.num_programs(0) - 1)
+    def _():
+        for k, ref in enumerate((own_ref, *sends)):
+            at = pl.multiple_of(place_ref[k] % count_t * block, block)
+            ref[...] = acc[pl.ds(at, block), :].astype(ref.dtype)
+
+
+def forward_rest_kernel(*refs):
+    a_ref, wq, wg, tq, tg, k_ref, v_ref, decay_ref, start_ref = refs[:9]
+    q_ref, gate_ref, o_ref, u_ref, qa, qb, ka, kb = refs[-8:]
+    pair = pl.program_id(0)
+    seq_len, half = a_ref.shape[0], a_ref.shape[1] // 2
+    rows = query_rows(seq_len)
+    w_mine, w_theirs = lane_blocks((wq, wg)), lane_blocks((tq, tg))
 
     def project(i):
         here = rows_at(i, chunk_rows)
         out = dot_nn(a_ref[here, :half], w_mine) + dot_nn(a_ref[here, half:], w_theirs)
         q_ref[here, :] = out[:, :128].astype(bf16)
-        k_ref[here, :] = out[:, 128:256].astype(bf16)
-        v_ref[here, :] = out[:, 256:384].astype(bf16)
-        gate_ref[here, :] = out[:, 384:]
+        gate_ref[here, :] = out[:, 128:]
 
     each(seq_len // chunk_rows, project)
-    mix_decay(q_ref, k_ref, decay_ref, pair, qa, qb, ka, kb)
+    mix_keys(k_ref, decay_ref, pair, ka, kb)
+    mix_queries(q_ref, decay_ref, 0, pair, qa, qb)
     lane = lax.broadcasted_iota(jnp.int32, (rows, pair_lanes), 1)
 
     def body(start, first, width):
@@ -276,13 +325,6 @@
         u_ref[here, :] = (o * jax.nn.sigmoid(gate_ref[here, :])).astype(bf16)
 
     over_query_blocks(seq_len, rows, body)
-    u_own = own_of(u_ref, place_ref, count_t, block)
-    acc[:, :half] += dot_nn(u_own, wo[0])
-    acc[:, half:] += dot_nn(u_own, to[0])
-
-    @pl.when(pair == pl.num_programs(0) - 1)
-    def _():
-        hand_out(acc, own_ref, sends)
 
 
 def backward_kernel(count_parts, count_t, block, join, *refs):
@@ -312,7 +354,8 @@
         dg_ref[here, :] = (du * o_ref[here, :] * sig * (1.0 - sig)).astype(bf16)
 
     each(seq_len // chunk_rows, gates)
-    mix_decay(q_ref, k_ref, decay_ref, pair, qa, qb, ka, kb)
+    mix_keys(k_ref, decay_ref, pair, ka, kb)
+    mix_queries(q_ref, decay_ref, 0, pair, qa, qb)
     dka[...] = jnp.zeros_like(dka)
     dkb[...] = jnp.zeros_like(dkb)
     dva[...] = jnp.zeros_like(dva)
@@ -420,7 +463,8 @@
 
 def ffn_inner_kernel(count_parts, block, *refs):
     b_parts, g_parts = refs[:count_parts], refs[count_parts : 2 * count_parts]
-    wg, wu, wd, tg, tu, td, b_ref, g_ref, m_ref, dgate_ref, dup_ref = refs[2 * count_parts :]
+    wg, wu, wd, tg, tu, td = refs[2 * count_parts : 2 * count_parts + 6]
+    b_ref, g_ref, m_ref, dgate_ref, dup_ref = refs[-5:]
     half = b_ref.shape[1] // 2
 
     @pl.when(pl.program_id(0) == 0)
@@ -481,33 +525,63 @@
     return specs
 
 
-def attention_forward(places, parts, layer, w4, t4, wo, to, wf, bias, doc_start, count_t, piece_len):
+def cost(microseconds):
+    return pl.CostEstimate(flops=int(microseconds * 1.1e9), bytes_accessed=0, transcendentals=0)
+
+
+def token_specs(tokens):
+    return [pl.BlockSpec((16, 128), lambda *_: (0, 0)) for _ in tokens]
+
+
+def forward_own(places, parts, layer, w4, t4, wo, to, wf, bias, doc_start, count_t, piece_len):
     seq_len, width = doc_start.shape[0], parts[0].shape[1]
     local_width = wo.shape[1]
     block = piece_len // count_t
     join = len(parts) > 1
-    low, high = lambda: shape((seq_len, local_width), bf16), lambda: shape((seq_len, local_width), f32)
     shared, shared_specs = share_outs(block, width, count_t)
-    outs = [low(), low(), low(), high(), high(), low(), shape((seq_len, 8), f32), shape((seq_len, 8), f32)]
-    specs = [lanes(seq_len)] * 6 + [fixed((seq_len, 8), False)] * 2
+    outs = [shape((seq_len, local_width), bf16)] * 2 + [shape((seq_len, 8), f32)] * 2
+    specs = [lanes(seq_len)] * 2 + [fixed((seq_len, 8), False)] * 2
     if join:
         outs, specs = [shape((seq_len, width), bf16)] + outs, [fixed((seq_len, width))] + specs
+    low, piece = pltpu.VMEM((seq_len, pair_lanes), bf16), pltpu.VMEM((piece_len, pair_lanes), bf16)
     got = pl.pallas_call(
-        functools.partial(forward_kernel, len(parts), count_t, block, join),
+        functools.partial(forward_own_kernel, len(parts), count_t, block, join),
         grid_spec=pltpu.PrefetchScalarGridSpec(
             num_scalar_prefetch=1,
             grid=(local_width // pair_lanes,),
             in_specs=attention_specs(parts, layer, w4, t4, wo, to, seq_len, join)
             + [fixed(wf.shape), fixed(bias.shape), fixed(doc_start.shape)],
             out_specs=specs + shared_specs,
-            scratch_shapes=[pltpu.VMEM((seq_len, pair_lanes), bf16)] * 4 + [pltpu.VMEM((piece_len, width), f32)],
+            scratch_shapes=[piece] * 3 + [low] * 2 + [pltpu.VMEM((piece_len, width), f32)],
         ),
         out_shape=outs + shared,
+        cost_estimate=cost(14),
         compiler_params=pltpu.CompilerParams(vmem_limit_bytes=60 << 20),
     )(places, *parts, *w4, *t4, wo, to, wf, bias, doc_start)
     got = list(got)
     a = got.pop(0) if join else parts[0]
-    return a, got[:8], got[8], got[9:]
+    return a, got[:4], got[4], got[5:]
+
+
+def forward_rest(a, layer, w4, t4, k, v, decay, doc_start, *tokens):
+    seq_len = a.shape[0]
+    local_width = k.shape[1]
+    low, high = shape((seq_len, local_width), bf16), shape((seq_len, local_width), f32)
+    weights = (w4[0], w4[3], t4[0], t4[3])
+    return pl.pallas_call(
+        forward_rest_kernel,
+        grid=(local_width // pair_lanes,),
+        in_specs=[fixed(a.shape)]
+        + [columns_of(w, layer, pair_lanes) for w in weights]
+        + [lanes_read(seq_len)] * 2
+        + [fixed(decay.shape), fixed(doc_start.shape)]
+        + token_specs(tokens),
+        out_specs=[lanes(seq_len)] * 4,
+        scratch_shapes=[pltpu.VMEM((seq_len, pair_lanes), bf16)] * 4,
+        out_shape=[low, high, high, low],
+        cost_estimate=cost(20),
+        compiler_params=pltpu.CompilerParams(vmem_limit_bytes=60 << 20),
+    )(a, *weights, k, v, decay, doc_start, *tokens)
 
 
 def attention_backward(places, parts, layer, w4, t4, wo, to, wf, saved, doc_start, count_t, piece_len):
@@ -535,6 +609,7 @@
             scratch_shapes=[low] * 5 + [high] * 4 + [pltpu.VMEM((piece_len, width), f32)],
         ),
         out_shape=outs + shared,
+        cost_estimate=cost(32),
         compiler_params=pltpu.CompilerParams(vmem_limit_bytes=60 << 20),
     )(places, *parts, *w4, *t4, wo, to, wf, q, k, v, gate, o, z, decay, doc_start)
     got = list(got)
@@ -566,6 +641,7 @@
         out_specs=[blocks_of(rows)] * 2 + shared_specs,
         scratch_shapes=[pltpu.VMEM((rows, width), f32)],
         out_shape=[shape((rows, inner), f32)] * 2 + shared,
+        cost_estimate=cost(7),
         compiler_params=pltpu.CompilerParams(vmem_limit_bytes=40 << 20),
     )(b, *w3, *t3)
     return got[0], got[1], got[2], got[3:]
@@ -581,22 +657,36 @@
         out_specs=shared_specs,
         scratch_shapes=[pltpu.VMEM((rows, width), f32)],
         out_shape=shared,
+        cost_estimate=cost(8),
         compiler_params=pltpu.CompilerParams(vmem_limit_bytes=40 << 20),
     )(g, gt, up, *w3, *t3)
     return got[0], got[1:]
 
 
-def ffn_inner(b_parts, g_parts, layer, w3, t3, block):
+def ffn_inner(b_parts, g_parts, layer, w3, t3, block, *tokens):
     rows, width = sum(p.shape[0] for p in b_parts), b_parts[0].shape[1]
     inner = w3[2].shape[1]
     return pl.pallas_call(
         functools.partial(ffn_inner_kernel, len(b_parts), block),
         grid=(inner // hidden_block,),
-        in_specs=[fixed(p.shape) for p in (*b_parts, *g_parts)] + ffn_weights(layer, w3, t3),
+        in_specs=[fixed(p.shape) for p in (*b_parts, *g_parts)] + ffn_weights(layer, w3, t3) + token_specs(tokens),
         out_specs=[fixed((rows, width))] * 2 + [blocks_of(rows)] * 3,
         out_shape=[shape((rows, width), bf16)] * 2 + [shape((rows, inner), bf16)] * 3,
+        cost_estimate=cost(16),
         compiler_params=pltpu.CompilerParams(vmem_limit_bytes=56 << 20),
-    )(*b_parts, *g_parts, *w3, *t3)
+    )(*b_parts, *g_parts, *w3, *t3, *tokens)
+
+
+def unset_kernel(*refs):
+    pass
+
+
+def unset(*like):
+    return pl.pallas_call(
+        unset_kernel,
+        out_specs=[pl.BlockSpec(memory_space=pl.ANY) for _ in like],
+        out_shape=list(like),
+    )()
 
 
 def inverse_rms(h):
@@ -640,19 +730,6 @@
     def full(w, axis):
         return jnp.concatenate([w, other(w)], axis=axis)
 
-    gains = full(jnp.concatenate([gain_attn, gain_ffn], axis=0), 1).astype(f32)
-    hidden_rows = rows_by_place(features(hidden_in.reshape(piece_len, width)).astype(f32))
-    first_a = (hidden_rows * inverse_rms(hidden_rows) * gains[0]).astype(bf16)
-    a_parts = all_rows(first_a)
-
-    w_forget_full = jnp.pad(full(w_forget, 1), ((0, 0), (0, 0), (0, pair_lanes - heads)))
-    bias = jnp.pad(b_forget, ((0, 0), (0, pair_lanes - heads)))
-    w4 = (w_query, w_key, w_value, w_gate_out)
-    t4 = tuple(other(w) for w in w4)
-    to = other(w_attn_out)
-    w3 = (w_gate, w_up, w_down)
-    t3 = tuple(other(w) for w in w3)
-
     segments = segment_ids.reshape(piece_len)
     if count_z == 4:
         pieces = jnp.stack([segments] + [swap(segments, "context", k) for k in range(1, count_z)])
@@ -663,6 +740,19 @@
         seg_all = lax.all_gather(segments, "context", tiled=True)
     doc_start = jnp.sum((seg_all[None, :] < seg_all[:, None]).astype(jnp.int32), axis=1, keepdims=True)
 
+    gains = full(jnp.concatenate([gain_attn, gain_ffn], axis=0), 1).astype(f32)
+    hidden_rows = rows_by_place(features(hidden_in.reshape(piece_len, width)).astype(f32))
+    first_a = (hidden_rows * inverse_rms(hidden_rows) * gains[0]).astype(bf16)
+    a_parts = all_rows(first_a)
+
+    w_forget_full = jnp.pad(full(w_forget, 1), ((0, 0), (0, 0), (0, pair_lanes - heads)))
+    bias = jnp.pad(b_forget, ((0, 0), (0, pair_lanes - heads)))
+    w4 = (w_query, w_key, w_value, w_gate_out)
+    t4 = tuple(other(w) for w in w4)
+    to = other(w_attn_out)
+    w3 = (w_gate, w_up, w_down)
+    t3 = tuple(other(w) for w in w3)
+
     def in_order(parts):
         if len(parts) > 1:
             return parts
@@ -680,86 +770,111 @@
         gain_one, gain_two = gains[layer], gains[layers + layer]
         inverse_one = inverse_rms(hidden)
         if layer > 0:
-            a_parts = all_rows(own_rows((hidden * inverse_one * gain_one).astype(bf16)))
-        a, kept, own, sends = attention_forward(
+            shard = (hidden * inverse_one * gain_one).astype(bf16)
+            saved[-1]["rest"] = shard
+            a_parts = all_rows(own_rows(shard), shard=shard)
+        a, (k, v, forget, decay), own, sends = forward_own(
             places, in_order(a_parts), layer, w4, t4, w_attn_out, to, w_forget_full[layer],
             bias[layer : layer + 1], doc_start, count_t, piece_len,
         )
         if shared_rows:
             if layer == 0:
-                g_last = all_rows(cotangent_rows, a_parts[-1])
+                g_last = all_rows(cotangent_rows, a_parts[-1], a_parts[-1])
             else:
-                saved[-1]["b_parts"] = all_rows(saved[-1]["b"], a_parts[-1])
+                before = saved[-1]
+                before["b_parts"] = all_rows(before["b"], None, a_parts[-1], before["b_shard"])
         mixed = hidden + received_sum(own, sends)
         inverse_two = inverse_rms(mixed)
-        b = own_rows((mixed * inverse_two * gain_two).astype(bf16))
+        b_shard = (mixed * inverse_two * gain_two).astype(bf16)
+        b = own_rows(b_shard)
         gt, up, own, sends = ffn_forward(b, layer, w3, t3, count_t)
         saved.append(
-            dict(hidden=hidden, inverse_one=inverse_one, a=a, kept=kept, mixed=mixed, inverse_two=inverse_two,
-                 b=b, gt=gt, up=up)
+            dict(hidden=hidden, inverse_one=inverse_one, a=a, k=k, v=v, forget=forget, decay=decay, mixed=mixed,
+                 inverse_two=inverse_two, b=b, b_shard=b_shard, gt=gt, up=up)
         )
-        hidden = mixed + received_sum(own, sends)
+        if layer < layers - 1:
+            hidden = mixed + received_sum(own, sends)
 
     def finish(x):
         return features(rows_by_place(own_rows(x.astype(bf16)))).reshape(1, piece_len, width)
 
-    output = finish(hidden)
-
+    last_own, last_sends = own, sends
     grad = cotangent_rows[:block].astype(f32)
-    results = [None] * layers
+    wide = shape((layers, half, local_width), f32)
+    inner = shape((layers, half, w_gate.shape[2]), f32)
+    results = list(
+        unset(
+            wide, wide, wide, wide, shape((layers, local_width, half), f32),
+            inner, inner, shape((layers, w_down.shape[1], half), f32),
+        )
+    )
+    small = [[None] * layers for _ in range(2)]
     gain_grads = [None] * (2 * layers)
-
-    def exchange(mine, theirs):
-        return mine + other(theirs).astype(f32)
 
     for layer in reversed(range(layers)):
         s = saved[layer]
         gain_one, gain_two = gains[layer], gains[layers + layer]
-        g = cotangent_rows if layer == layers - 1 else own_rows(grad.astype(bf16))
+        if layer == layers - 1:
+            g = g_shard = cotangent_rows
+            if shared_rows:
+                s["b_parts"], g_parts = all_rows(s["b"], shard=s["b_shard"]), g_last
+        else:
+            g_shard = grad.astype(bf16)
+            g = own_rows(g_shard)
+            if shared_rows:
+                g_parts = all_rows(g, shard=g_shard)
         own, sends = ffn_backward(g, s["gt"], s["up"], layer, w3, t3, count_t)
         back, gain_grads[layers + layer] = norm_back(received_sum(own, sends), s["mixed"], s["inverse_two"], gain_two)
         grad_mixed = grad + back
-        y_parts = all_rows(own_rows(grad_mixed.astype(bf16)))
+        y_shard = grad_mixed.astype(bf16)
+        y_parts = all_rows(own_rows(y_shard), shard=y_shard)
+        q, gate, o, u = forward_rest(
+            s["a"], layer, w4, t4, s["k"], s["v"], s["decay"], doc_start, s.get("rest", y_shard)
+        )
+        kept = (q, s["k"], s["v"], gate, o, u, s["forget"], s["decay"])
         y, (dq, dk, dv, dg, dz), own, sends = attention_backward(
-            places, in_order(y_parts), layer, w4, t4, w_attn_out, to, w_forget_full[layer], s["kept"],
+            places, in_order(y_parts), layer, w4, t4, w_attn_out, to, w_forget_full[layer], kept,
             doc_start, count_t, piece_len,
         )
-        if not shared_rows:
-            b_parts, g_parts = (s["b"],), (g,)
-        elif layer == layers - 1:
-            b_parts, g_parts = all_rows(s["b"], y_parts[-1]), g_last
-        else:
-            b_parts, g_parts = s["b_parts"], all_rows(g, y_parts[-1])
+        if layer == layers - 1:
+            output = finish(s["mixed"] + received_sum(last_own, [after(x, y_parts[-1]) for x in last_sends]))
         back, gain_grads[layer] = norm_back(received_sum(own, sends), s["hidden"], s["inverse_one"], gain_one)
         grad = grad_mixed + back
 
-        b, g, m, d_gate, d_up = ffn_inner(b_parts, g_parts, layer, w3, t3, block)
-
-        def by_rows(x, d):
-            return exchange(dot_tn(x[:, :half], d), dot_tn(x[:, half:], d).astype(bf16))
-
-        def by_columns(x, d):
-            return exchange(dot_tn(x, d[:, :half]), dot_tn(x, d[:, half:]).astype(bf16))
-
-        def pieces_sum(x):
-            return x if shared_rows else lax.psum(x, "context")
-
-        a, u = s["a"], s["kept"][5]
+        if not shared_rows:
+            s["b_parts"], g_parts = (s["b"],), (g,)
+        token = grad.astype(bf16) if layer > 0 else y_shard
+        b, g, m, d_gate, d_up = ffn_inner(s["b_parts"], g_parts, layer, w3, t3, block, token)
+
+        def put(k, mine, theirs):
+            total = mine + other(theirs).astype(f32)
+            if k >= 5 and not shared_rows:
+                total = lax.psum(total, "context")
+            results[k] = lax.dynamic_update_slice_in_dim(results[k], total[None], layer, 0)
+
+        def by_rows(k, x, d):
+            put(k, dot_tn(x[:, :half], d), dot_tn(x[:, half:], d).astype(bf16))
+
+        def by_columns(k, x, d):
+            put(k, dot_tn(x, d[:, :half]), dot_tn(x, d[:, half:]).astype(bf16))
+
+        a = s["a"]
+        for k, d in enumerate((dq, dk, dv, dg)):
+            by_rows(k, a, d)
+        by_columns(4, u, y)
+        by_rows(5, b, d_gate)
+        by_rows(6, b, d_up)
+        by_columns(7, m, g)
         dzr = dz[:, :heads]
         bias_grad = jnp.sum(dzr.astype(f32), axis=0)
-        results[layer] = (
-            by_rows(a, dq), by_rows(a, dk), by_rows(a, dv), by_rows(a, dg), by_columns(u, y),
-            dot_tn(a[:, :half], dzr) + other(dot_tn(a[:, half:], dzr)),
-            bias_grad + other(bias_grad),
-            *(pieces_sum(x) for x in (by_rows(b, d_gate), by_rows(b, d_up), by_columns(m, g))),
-        )
+        small[0][layer] = dot_tn(a[:, :half], dzr) + other(dot_tn(a[:, half:], dzr))
+        small[1][layer] = bias_grad + other(bias_grad)
     grad_input = finish(grad)
     gain_total = sum_over(sum_over(jnp.stack(gain_grads), "tensor"), "context")
     gain_total = gain_total[:, :half] + other(gain_total[:, half:])
-    s = [jnp.stack([results[layer][k] for layer in range(layers)]) for k in range(10)]
     return (
-        output, grad_input, s[0], s[1], s[2], s[3], s[4], s[5], s[6],
-        gain_total[:layers], gain_total[layers:], s[7], s[8], s[9],
+        output, grad_input, *results[:5], jnp.stack(small[0]), jnp.stack(small[1]),
+        gain_total[:layers], gain_total[layers:], *results[5:],
     )
 
 

time: 762 us -> 702 us (0.921)
  waiting for transfers between devices: 257 us -> 190 us
  Pallas kernels: 179 us -> 204 us
  other arithmetic: 43.1 us -> 22.5 us
  starting transfers between devices: 155 us -> 174 us
  matrix products: 81.1 us -> 67.5 us
    ppermute x136 -> x160, waiting for transfers between devices: 257 us -> 190 us  [swap(): return lax.ppermute(x, axis, [(i, i ^ k) for i in range(n)])]
    pallas_call x2 -> x5, Pallas kernels: 53.4 us -> 74 us  [the longest x2 37.7 us: forward_rest(): pl.pallas_call(forward_rest_kernel, grid=(local_width // pair_lanes,), in...]
    another operation x12 -> x4, other arithmetic: 19.8 us -> 0.6 us  [the longest x3 0.58 us: local(): jnp.stack(small[1])]
    ppermute x136 -> x160, starting transfers between devices: 155 us -> 174 us  [swap(): return lax.ppermute(x, axis, [(i, i ^ k) for i in range(n)])]
    dot_general x36, matrix products: 81.1 us -> 67.5 us  [dot_tn(): lax.dot_general(a, b, (((0,), (0,)), ((), ())), preferred_element_type=f32)]
    unnamed x349 -> x417, local copies, waits for them, and re-layouts: 17.8 us -> 22.5 us
  transfers between devices with their start and end apart: 136 -> 160, of which waited for: 63 -> 67; matrix products, arithmetic and copies ran while one was open for 18% -> 14% of each run, Pallas kernels for 23% -> 28%
where the time goes in v3:
time: 702 us; the launch traced here: 698 us
  Pallas kernels  204 us (29%)
  waiting for transfers between devices  190 us (27%)
  starting transfers between devices  174 us (25%)
  matrix products  67.5 us (10%)
  local copies, waits for them, and re-layouts  34.4 us (5%)
  other arithmetic  22.5 us (3%)
    ppermute x160, waiting for transfers between devices, swap(): return lax.ppermute(x, axis, [(i, i ^ k) for i in range(n)])  190 us
    ppermute x160, starting transfers between devices, swap(): return lax.ppermute(x, axis, [(i, i ^ k) for i in range(n)])  174 us
    dot_general x36, matrix products, dot_tn(): lax.dot_general(a, b, (((0,), (0,)), ((), ())), preferred_element_type=f32)  67.5 us
    pallas_call x2, Pallas kernels, attention_backward(): pl.pallas_call(functools.partial(backward_kernel, len(parts), count_t, bl...  66.5 us
    pallas_call x2, Pallas kernels, forward_rest(): pl.pallas_call(forward_rest_kernel, grid=(local_width // pair_lanes,), in...  37.7 us
    pallas_call x2, Pallas kernels, forward_own(): pl.pallas_call(functools.partial(forward_own_kernel, len(parts), count_t,...  36.3 us
    pallas_call x2, Pallas kernels, ffn_inner(): pl.pallas_call(functools.partial(ffn_inner_kernel, len(b_parts), block),...  33.2 us
    unnamed x417, local copies, waits for them, and re-layouts  22.5 us
  transfers between devices with their start and end apart: 160, of which 67 were waited for; matrix products, arithmetic and copies ran while one was open for 14% of the time, Pallas kernels for 28%

profile of v3, /device:TPU:0, one launch (start us, length us, event | category | flops | bytes accessed | tf_op | source)
XLA Modules:
  0.0 697.9 jit_solution(4446481210908494766)
XLA Ops:
  14.7 19.4 %collective-permute-done.2.refs_3_ = bf16[64,1536]{1,0:T(8,128)(2,1)S(1)} collective-permute-done((bf16[64,1536]{1,0:T(8,128)(2,1)S(1)}, bf16[64,1536]{1,0:T(8,128)(2,1)S(1)}, u32[]{:S(2)}, u32[]{:S(2)}) %collective-permute-start.2) | collective-permute-done | bytes 196640 | tf_op jit(solution)/shard_map/ppermute | solution.py:25
  56.1 4.3 collective-permute-done.5.refs_6_
  74.5 18.1 %shard_map.254 = (bf16[1024,1536]{1,0:T(8,128)(2,1)}, bf16[1024,384]{1,0:T(8,128)(2,1)}, bf16[1024,384]{1,0:T(8,128)(2,1)}, f32[1024,8]{1,0:T(8,128)}, f32[1024,...) custom-call(s32[20]{0:T(128)} %stack.116.refs_0_, ...), custom_call_target="tpu_custom_call" | custom-call | flops 15399999488 | tf_op jit(solution)/shard_map/pallas_call | solution.py:547
  94.6 6.5 collective-permute-done.21
  111.9 4.7 collective-permute-done.24
  123.5 6.9 shard_map.255
  144.9 4.1 collective-permute-done.33
  152.8 11.7 %collective-permute-done.35.refs_3_ = bf16[64,1536]{1,0:T(8,128)(2,1)S(1)} collective-permute-done((bf16[64,1536]{1,0:T(8,128)(2,1)S(1)}, bf16[64,1536]{1,0:T(8,128)(2,1)S(1)}, u32[]{:S(2)}, u32[]{:S(2)}) %collective-permute-start.35) | collective-permute-done | bytes 196640 | tf_op jit(solution)/shard_map/ppermute | solution.py:25
  184.6 18.2 %shard_map.256 = (bf16[1024,1536]{1,0:T(8,128)(2,1)}, bf16[1024,384]{1,0:T(8,128)(2,1)}, bf16[1024,384]{1,0:T(8,128)(2,1)}, f32[1024,8]{1,0:T(8,128)}, f32[1024,...) custom-call(s32[20]{0:T(128)} %stack.116.refs_0_, ...), custom_call_target="tpu_custom_call" | custom-call | flops 15399999488 | tf_op jit(solution)/shard_map/pallas_call | solution.py:547
  206.4 18.9 %shard_map.262 = (bf16[1024,384]{1,0:T(8,128)(2,1)}, f32[1024,384]{1,0:T(8,128)}, f32[1024,384]{1,0:T(8,128)}, bf16[1024,384]{1,0:T(8,128)(2,1)}) custom-call(bf16[1024,1536]{1,0:T(8,128)(2,1)} %get-tuple-element.138.refs_0_, bf16[2,768,384]{2,1,0:T(8,128)(2,1)} %refs_11_.7, bf16[2,768,384]{2,1,0:T(8,128)(2,1)} %refs_14_.7, ...), custom_call_target="tpu_custom_call" | custom-call | flops 22000001024 | tf_op jit(solution)/shard_map/pallas_call | solution.py:571
  236.4 6.9 shard_map.257
  243.3 8.0 %shard_map.258 = (f32[64,1536]{1,0:T(8,128)S(1)}, bf16[64,1536]{1,0:T(8,128)(2,1)S(1)}, bf16[64,1536]{1,0:T(8,128)(2,1)S(1)}, bf16[64,1536]{1,0:T(8,128)(2,1)S(1)}) custom-call(bf16[256,1536]{1,0:T(8,128)(2,1)S(1)} %get-tuple-element.272.g_ref.refs_10_, f32[256,1024]{1,0:T(8,128)S(1)} %get-tuple-element.112.gt_ref, ...), custom_call_target="tpu_custom_call" | custom-call | flops 8800000000 | tf_op jit(solution)/shard_map/pallas_call | solution.py:653
  258.0 5.5 collective-permute-done.50
  270.3 18.8 %shard_map.259 = (bf16[1024,384]{1,0:T(8,128)(2,1)}, f32[1024,384]{1,0:T(8,128)}, f32[1024,384]{1,0:T(8,128)}, bf16[1024,384]{1,0:T(8,128)(2,1)}) custom-call(bf16[1024,1536]{1,0:T(8,128)(2,1)} %get-tuple-element.120.refs_0_, bf16[2,768,384]{2,1,0:T(8,128)(2,1)} %refs_11_.7, bf16[2,768,384]{2,1,0:T(8,128)(2,1)} %refs_14_.7, ...), custom_call_target="tpu_custom_call" | custom-call | flops 22000001024 | tf_op jit(solution)/shard_map/pallas_call | solution.py:571
  316.0 33.4 %shard_map.260 = (bf16[1024,1536]{1,0:T(8,128)(2,1)}, bf16[1024,384]{1,0:T(8,128)(2,1)}, bf16[1024,384]{1,0:T(8,128)(2,1)}, bf16[1024,384]{1,0:T(8,128)(2,1)}, b...) custom-call(s32[20]{0:T(128)} %stack.116.refs_0_, ...), custom_call_target="tpu_custom_call" | custom-call | flops 35200000000 | tf_op jit(solution)/shard_map/pallas_call | solution.py:599
  368.9 6.0 collective-permute-done.119.refs_2_
  380.0 5.9 collective-permute-done.134.refs_18_
  390.0 7.3 %collective-permute-done.121.refs_4_ = bf16[64,1536]{1,0:T(8,128)(2,1)S(1)} collective-permute-done((bf16[64,1536]{1,0:T(8,128)(2,1)S(1)}, bf16[64,1536]{1,0:T(8,128)(2,1)S(1)}, u32[]{:S(2)}, u32[]{:S(2)}) %collective-permute-start.121) | collective-permute-done | bytes 196640 | tf_op jit(solution)/shard_map/ppermute | solution.py:25
  417.2 16.6 %shard_map.265 = (bf16[1024,1536]{1,0:T(8,128)(2,1)}, bf16[1024,1536]{1,0:T(8,128)(2,1)}, bf16[1024,1024]{1,0:T(8,128)(2,1)}, bf16[1024,1024]{1,0:T(8,128)(2,1)}, bf16[1024,1024]{1,0:T(8,128)(2,1)}) custom-call(bf16[256,1536]{1,0:T(8,128)(2,1)} %copy-done.2, bf16[256,1536]{1,0:T(8,128)(2,1)} %copy-done.65, bf16[64,1536]{1,0:T(8,128)(2,1)} %copy-done.87, ...), custom_call_target="tpu_custom_call" | custom-call | flops 17600000000 | tf_op jit(solution)/shard_map/pallas_call | solution.py:669
  433.9 5.2 convolution_convert_fusion.5
  453.3 8.3 %shard_map.261 = (f32[64,1536]{1,0:T(8,128)S(1)}, bf16[64,1536]{1,0:T(8,128)(2,1)S(1)}, bf16[64,1536]{1,0:T(8,128)(2,1)S(1)}, bf16[64,1536]{1,0:T(8,128)(2,1)S(1)}) custom-call(bf16[256,1536]{1,0:T(8,128)(2,1)S(1)} %pad_maximum_fusion.8.g_ref.refs_10_, f32[256,1024]{1,0:T(8,128)S(1)} %copy-done.5, f32[256,1024]{1,0:T(8,128)S(1)} %copy-done.7, ...), custom_call_target="tpu_custom_call" | custom-call | flops 8800000000 | tf_op jit(solution)/shard_map/pallas_call | solution.py:653
  481.2 4.0 collective-permute-done.141.refs_5_
  489.3 3.9 collective-permute-start.147
  495.0 10.0 %collective-permute-done.147.refs_12_ = bf16[64,1536]{1,0:T(8,128)(2,1)S(1)} collective-permute-done((bf16[64,1536]{1,0:T(8,128)(2,1)S(1)}, bf16[64,1536]{1,0:T(8,128)(2,1)S(1)}, u32[]{:S(2)}, u32[]{:S(2)}) %collective-permute-start.147) | collective-permute-done | bytes 196640 | tf_op jit(solution)/shard_map/ppermute | solution.py:25
  527.4 6.4 collective-permute-start.83
  533.8 3.9 collective-permute-start.87
  543.4 4.2 collective-permute-done.87.refs_7_
  550.1 16.5 %shard_map.266 = (bf16[1024,1536]{1,0:T(8,128)(2,1)}, bf16[1024,1536]{1,0:T(8,128)(2,1)}, bf16[1024,1024]{1,0:T(8,128)(2,1)}, bf16[1024,1024]{1,0:T(8,128)(2,1)}, bf16[1024,1024]{1,0:T(8,128)(2,1)}) custom-call(bf16[256,1536]{1,0:T(8,128)(2,1)} %copy-done.1, bf16[256,1536]{1,0:T(8,128)(2,1)} %copy-done.62, bf16[64,1536]{1,0:T(8,128)(2,1)} %broadcast_add_fusion.2.refs_2_, ...), custom_call_target="tpu_custom_call" | custom-call | flops 17600000000 | tf_op jit(solution)/shard_map/pallas_call | solution.py:669
  566.7 5.3 convolution_convert_fusion.4
  584.2 33.1 %shard_map.263 = (bf16[1024,1536]{1,0:T(8,128)(2,1)}, bf16[1024,384]{1,0:T(8,128)(2,1)}, bf16[1024,384]{1,0:T(8,128)(2,1)}, bf16[1024,384]{1,0:T(8,128)(2,1)}, b...) custom-call(s32[20]{0:T(128)} %stack.116.refs_0_, ...), custom_call_target="tpu_custom_call" | custom-call | flops 35200000000 | tf_op jit(solution)/shard_map/pallas_call | solution.py:599
  648.8 4.3 collective-permute-start.114
  659.3 4.5 collective-permute-done.96
  (846 shorter events, 361.7 us)
Async XLA Ops:
  9.4 58.6 %collective-permute-start.1 = (bf16[256,1536]{1,0:T(8,128)(2,1)S(1)}, bf16[256,1536]{1,0:T(8,128)(2,1)S(1)}, u32[]{:S(2)}, u32[]{:S(2)}) collective-permute-start(bf16[256,1536]{1,0:T(8,128)(2,1)S(1)} %multiply_convert_fusion.refs_1_), channel_id=1, source_target_pairs={{0,4},{4,0},{8,12},{12,8},{1,5},{5,1},{9,13},{13,9},{2,6},{6,2},{1... | collective-permute-start | bytes 2359304 | tf_op jit(solution)/shard_map/ppermute | solution.py:25
  14.7 37.9 %collective-permute-start.6 = (bf16[64,1536]{1,0:T(8,128)(2,1)S(1)}, bf16[64,1536]{1,0:T(8,128)(2,1)S(1)}, u32[]{:S(2)}, u32[]{:S(2)}) collective-permute-start(bf16[64,1536]{1,0:T(8,128)(2,1)S(1)} %slice.203), channel_id=1, source_target_pairs={{0,12},{4,8},{8,4},{12,0},{1,13},{5,9},{9,5},{13,1},{2,14},{6,10},... | collective-permute-start | bytes 589832 | tf_op jit(solution)/shard_map/ppermute | solution.py:25
  73.8 49.7 %collective-permute-start.25 = (bf16[2,768,1024]{2,1,0:T(8,128)(2,1)}, bf16[2,768,1024]{2,1,0:T(8,128)(2,1)}, u32[]{:S(2)}, u32[]{:S(2)}) collective-permute-start(bf16[2,768,1024]{2,1,0:T(8,128)(2,1)} %refs_20_.3), channel_id=1, source_target_pairs={{0,16},{16,0},{1,17},{17,1},{2,18},{18,2},{3,19},{19,3},{4,20},{20... | collective-permute-start | bytes 9437192 | tf_op jit(solution)/shard_map/ppermute | solution.py:25
  73.9 49.7 %collective-permute-start.26 = (bf16[2,768,1024]{2,1,0:T(8,128)(2,1)}, bf16[2,768,1024]{2,1,0:T(8,128)(2,1)}, u32[]{:S(2)}, u32[]{:S(2)}) collective-permute-start(bf16[2,768,1024]{2,1,0:T(8,128)(2,1)} %refs_21_.3), channel_id=1, source_target_pairs={{0,16},{16,0},{1,17},{17,1},{2,18},{18,2},{3,19},{19,3},{4,20},{20... | collective-permute-start | bytes 9437192 | tf_op jit(solution)/shard_map/ppermute | solution.py:25
  74.3 49.2 %collective-permute-start.27 = (bf16[2,1024,768]{2,1,0:T(8,128)(2,1)}, bf16[2,1024,768]{2,1,0:T(8,128)(2,1)}, u32[]{:S(2)}, u32[]{:S(2)}) collective-permute-start(bf16[2,1024,768]{2,1,0:T(8,128)(2,1)} %refs_22_.3), channel_id=1, source_target_pairs={{0,16},{16,0},{1,17},{17,1},{2,18},{18,2},{3,19},{19,3},{4,20},{20... | collective-permute-start | bytes 9437192 | tf_op jit(solution)/shard_map/ppermute | solution.py:25
  134.0 32.1 %collective-permute-start.128 = (bf16[64,1536]{1,0:T(8,128)(2,1)S(1)}, bf16[64,1536]{1,0:T(8,128)(2,1)S(1)}, u32[]{:S(2)}, u32[]{:S(2)}) collective-permute-start(bf16[64,1536]{1,0:T(8,128)(2,1)S(1)} %get-tuple-element.250), channel_id=1, source_target_pairs={{0,8},{4,12},{8,0},{12,4},{1,9},{5,13},{9,1},{13,5},{2,10},{6,14},... | collective-permute-start | bytes 589832 | tf_op jit(solution)/shard_map/ppermute | solution.py:25
  135.7 31.6 %collective-permute-start.132 = (bf16[64,1536]{1,0:T(8,128)(2,1)S(1)}, bf16[64,1536]{1,0:T(8,128)(2,1)S(1)}, u32[]{:S(2)}, u32[]{:S(2)}) collective-permute-start(bf16[64,1536]{1,0:T(8,128)(2,1)S(1)} %get-tuple-element.250), channel_id=1, source_target_pairs={{0,12},{4,8},{8,4},{12,0},{1,13},{5,9},{9,5},{13,1},{2,14},{6,10},... | collective-permute-start | bytes 589832 | tf_op jit(solution)/shard_map/ppermute | solution.py:25
  152.7 30.9 %collective-permute-start.34 = (bf16[256,1536]{1,0:T(8,128)(2,1)S(1)}, bf16[256,1536]{1,0:T(8,128)(2,1)S(1)}, u32[]{:S(2)}, u32[]{:S(2)}) collective-permute-start(bf16[256,1536]{1,0:T(8,128)(2,1)S(1)} %pad_maximum_fusion.2.refs_1_), channel_id=1, source_target_pairs={{0,4},{4,0},{8,12},{12,8},{1,5},{5,1},{9,13},{13,9},{2,6},{6,2},{1... | collective-permute-start | bytes 2359304 | tf_op jit(solution)/shard_map/ppermute | solution.py:25
  179.2 51.9 %collective-permute-start.138 = (bf16[64,1536]{1,0:T(8,128)(2,1)}, bf16[64,1536]{1,0:T(8,128)(2,1)S(1)}, u32[]{:S(2)}, u32[]{:S(2)}) collective-permute-start(bf16[64,1536]{1,0:T(8,128)(2,1)} %multiply_convert_fusion.3), channel_id=1, source_target_pairs={{0,8},{4,12},{8,0},{12,4},{1,9},{5,13},{9,1},{13,5},{2,10},{6,14},... | collective-permute-start | bytes 589832 | tf_op jit(solution)/shard_map/ppermute | solution.py:25
  180.6 74.2 %collective-permute-start.142 = (bf16[64,1536]{1,0:T(8,128)(2,1)}, bf16[64,1536]{1,0:T(8,128)(2,1)}, u32[]{:S(2)}, u32[]{:S(2)}) collective-permute-start(bf16[64,1536]{1,0:T(8,128)(2,1)} %multiply_convert_fusion.3), channel_id=1, source_target_pairs={{0,12},{4,8},{8,4},{12,0},{1,13},{5,9},{9,5},{13,1},{2,14},{6,10},... | collective-permute-start | bytes 589832 | tf_op jit(solution)/shard_map/ppermute | solution.py:25
  306.7 79.8 %collective-permute-start.127 = (bf16[256,1536]{1,0:T(8,128)(2,1)}, bf16[256,1536]{1,0:T(8,128)(2,1)}, u32[]{:S(2)}, u32[]{:S(2)}) collective-permute-start(bf16[256,1536]{1,0:T(8,128)(2,1)} %get-tuple-element.271), channel_id=1, source_target_pairs={{0,4},{4,0},{8,12},{12,8},{1,5},{5,1},{9,13},{13,9},{2,6},{6,2},{1... | collective-permute-start | bytes 2359304 | tf_op jit(solution)/shard_map/ppermute | solution.py:25
  307.9 53.2 %collective-permute-start.129 = (bf16[64,1536]{1,0:T(8,128)(2,1)}, bf16[64,1536]{1,0:T(8,128)(2,1)S(1)}, u32[]{:S(2)}, u32[]{:S(2)}) collective-permute-start(bf16[64,1536]{1,0:T(8,128)(2,1)} %broadcast_add_fusion.4.refs_12_), channel_id=1, source_target_pairs={{0,1},{1,0},{2,3},{3,2},{4,5},{5,4},{6,7},{7,6},{8,9},{9,8},{10,11... | collective-permute-start | bytes 589832 | tf_op jit(solution)/shard_map/ppermute | solution.py:25
  311.6 51.0 %collective-permute-start.130 = (bf16[64,1536]{1,0:T(8,128)(2,1)}, bf16[64,1536]{1,0:T(8,128)(2,1)}, u32[]{:S(2)}, u32[]{:S(2)}) collective-permute-start(bf16[64,1536]{1,0:T(8,128)(2,1)} %broadcast_add_fusion.4.refs_12_), channel_id=1, source_target_pairs={{0,2},{1,3},{2,0},{3,1},{4,6},{5,7},{6,4},{7,5},{8,10},{9,11},{10,... | collective-permute-start | bytes 589832 | tf_op jit(solution)/shard_map/ppermute | solution.py:25
  312.4 52.5 %collective-permute-start.131 = (bf16[64,1536]{1,0:T(8,128)(2,1)}, bf16[64,1536]{1,0:T(8,128)(2,1)}, u32[]{:S(2)}, u32[]{:S(2)}) collective-permute-start(bf16[64,1536]{1,0:T(8,128)(2,1)} %broadcast_add_fusion.4.refs_12_), channel_id=1, source_target_pairs={{0,3},{1,2},{2,1},{3,0},{4,7},{5,6},{6,5},{7,4},{8,11},{9,10},{10,... | collective-permute-start | bytes 589832 | tf_op jit(solution)/shard_map/ppermute | solution.py:25
  314.6 51.1 %collective-permute-start.133 = (bf16[64,1536]{1,0:T(8,128)(2,1)}, bf16[64,1536]{1,0:T(8,128)(2,1)}, u32[]{:S(2)}, u32[]{:S(2)}) collective-permute-start(bf16[64,1536]{1,0:T(8,128)(2,1)} %broadcast_add_fusion.3.refs_16_), channel_id=1, source_target_pairs={{0,1},{1,0},{2,3},{3,2},{4,5},{5,4},{6,7},{7,6},{8,9},{9,8},{10,11... | collective-permute-start | bytes 589832 | tf_op jit(solution)/shard_map/ppermute | solution.py:25
  385.9 29.1 %collective-permute-start.118 = (bf16[256,1536]{1,0:T(8,128)(2,1)S(1)}, bf16[256,1536]{1,0:T(8,128)(2,1)S(1)}, u32[]{:S(2)}, u32[]{:S(2)}) collective-permute-start(bf16[256,1536]{1,0:T(8,128)(2,1)S(1)} %pad_maximum_fusion.3.b_ref.refs_0_), channel_id=1, source_target_pairs={{0,4},{4,0},{8,12},{12,8},{1,5},{5,1},{9,13},{13,9},{2,6},{6,2},{1... | collective-permute-start | bytes 2359304 | tf_op jit(solution)/shard_map/ppermute | solution.py:25
  405.5 70.9 %collective-permute-start.137 = (bf16[256,1536]{1,0:T(8,128)(2,1)S(1)}, bf16[256,1536]{1,0:T(8,128)(2,1)S(1)}, u32[]{:S(2)}, u32[]{:S(2)}) collective-permute-start(bf16[256,1536]{1,0:T(8,128)(2,1)S(1)} %pad_maximum_fusion.1.b_ref.refs_0_), channel_id=1, source_target_pairs={{0,4},{4,0},{8,12},{12,8},{1,5},{5,1},{9,13},{13,9},{2,6},{6,2},{1... | collective-permute-start | bytes 2359304 | tf_op jit(solution)/shard_map/ppermute | solution.py:25
  409.7 68.2 %collective-permute-start.139 = (bf16[64,1536]{1,0:T(8,128)(2,1)S(1)}, bf16[64,1536]{1,0:T(8,128)(2,1)S(1)}, u32[]{:S(2)}, u32[]{:S(2)}) collective-permute-start(bf16[64,1536]{1,0:T(8,128)(2,1)S(1)} %copy-done.35), channel_id=1, source_target_pairs={{0,1},{1,0},{2,3},{3,2},{4,5},{5,4},{6,7},{7,6},{8,9},{9,8},{10,11... | collective-permute-start | bytes 589832 | tf_op jit(solution)/shard_map/ppermute | solution.py:25
  412.8 31.2 %collective-permute-start.59 = (bf16[64,1536]{1,0:T(8,128)(2,1)S(1)}, bf16[64,1536]{1,0:T(8,128)(2,1)S(1)}, u32[]{:S(2)}, u32[]{:S(2)}) collective-permute-start(bf16[64,1536]{1,0:T(8,128)(2,1)S(1)} %get-tuple-element.294), channel_id=1, source_target_pairs={{0,3},{1,2},{2,1},{3,0},{4,7},{5,6},{6,5},{7,4},{8,11},{9,10},{10,... | collective-permute-start | bytes 589832 | tf_op jit(solution)/shard_map/ppermute | solution.py:25
  413.2 31.5 %collective-permute-start.58 = (bf16[64,1536]{1,0:T(8,128)(2,1)S(1)}, bf16[64,1536]{1,0:T(8,128)(2,1)S(1)}, u32[]{:S(2)}, u32[]{:S(2)}) collective-permute-start(bf16[64,1536]{1,0:T(8,128)(2,1)S(1)} %get-tuple-element.294), channel_id=1, source_target_pairs={{0,2},{1,3},{2,0},{3,1},{4,6},{5,7},{6,4},{7,5},{8,10},{9,11},{10,... | collective-permute-start | bytes 589832 | tf_op jit(solution)/shard_map/ppermute | solution.py:25
  415.0 31.3 %collective-permute-start.57 = (bf16[64,1536]{1,0:T(8,128)(2,1)S(1)}, bf16[64,1536]{1,0:T(8,128)(2,1)S(1)}, u32[]{:S(2)}, u32[]{:S(2)}) collective-permute-start(bf16[64,1536]{1,0:T(8,128)(2,1)S(1)} %get-tuple-element.294), channel_id=1, source_target_pairs={{0,1},{1,0},{2,3},{3,2},{4,5},{5,4},{6,7},{7,6},{8,9},{9,8},{10,11... | collective-permute-start | bytes 589832 | tf_op jit(solution)/shard_map/ppermute | solution.py:25
  494.3 54.7 %collective-permute-start.146 = (bf16[256,1536]{1,0:T(8,128)(2,1)S(1)}, bf16[256,1536]{1,0:T(8,128)(2,1)S(1)}, u32[]{:S(2)}, u32[]{:S(2)}) collective-permute-start(bf16[256,1536]{1,0:T(8,128)(2,1)S(1)} %pad_maximum_fusion.8.g_ref.refs_10_), channel_id=1, source_target_pairs={{0,4},{4,0},{8,12},{12,8},{1,5},{5,1},{9,13},{13,9},{2,6},{6,2},{1... | collective-permute-start | bytes 2359304 | tf_op jit(solution)/shard_map/ppermute | solution.py:25
  537.7 45.5 %collective-permute-start.82 = (bf16[256,1536]{1,0:T(8,128)(2,1)S(1)}, bf16[256,1536]{1,0:T(8,128)(2,1)S(1)}, u32[]{:S(2)}, u32[]{:S(2)}) collective-permute-start(bf16[256,1536]{1,0:T(8,128)(2,1)S(1)} %pad_maximum_fusion.9.refs_1_), channel_id=1, source_target_pairs={{0,4},{4,0},{8,12},{12,8},{1,5},{5,1},{9,13},{13,9},{2,6},{6,2},{1... | collective-permute-start | bytes 2359304 | tf_op jit(solution)/shard_map/ppermute | solution.py:25
  541.5 33.5 %collective-permute-start.84 = (bf16[64,1536]{1,0:T(8,128)(2,1)S(1)}, bf16[64,1536]{1,0:T(8,128)(2,1)S(1)}, u32[]{:S(2)}, u32[]{:S(2)}) collective-permute-start(bf16[64,1536]{1,0:T(8,128)(2,1)S(1)} %collective-permute-done.83.refs_3_), channel_id=1, source_target_pairs={{0,1},{1,0},{2,3},{3,2},{4,5},{5,4},{6,7},{7,6},{8,9},{9,8},{10,11... | collective-permute-start | bytes 589832 | tf_op jit(solution)/shard_map/ppermute | solution.py:25
  542.6 33.4 %collective-permute-start.85 = (bf16[64,1536]{1,0:T(8,128)(2,1)S(1)}, bf16[64,1536]{1,0:T(8,128)(2,1)S(1)}, u32[]{:S(2)}, u32[]{:S(2)}) collective-permute-start(bf16[64,1536]{1,0:T(8,128)(2,1)S(1)} %collective-permute-done.83.refs_3_), channel_id=1, source_target_pairs={{0,2},{1,3},{2,0},{3,1},{4,6},{5,7},{6,4},{7,5},{8,10},{9,11},{10,... | collective-permute-start | bytes 589832 | tf_op jit(solution)/shard_map/ppermute | solution.py:25
  547.6 33.0 %collective-permute-start.86 = (bf16[64,1536]{1,0:T(8,128)(2,1)S(1)}, bf16[64,1536]{1,0:T(8,128)(2,1)S(1)}, u32[]{:S(2)}, u32[]{:S(2)}) collective-permute-start(bf16[64,1536]{1,0:T(8,128)(2,1)S(1)} %collective-permute-done.83.refs_3_), channel_id=1, source_target_pairs={{0,3},{1,2},{2,1},{3,0},{4,7},{5,6},{6,5},{7,4},{8,11},{9,10},{10,... | collective-permute-start | bytes 589832 | tf_op jit(solution)/shard_map/ppermute | solution.py:25
  549.1 31.6 %collective-permute-start.88 = (bf16[64,1536]{1,0:T(8,128)(2,1)S(1)}, bf16[64,1536]{1,0:T(8,128)(2,1)S(1)}, u32[]{:S(2)}, u32[]{:S(2)}) collective-permute-start(bf16[64,1536]{1,0:T(8,128)(2,1)S(1)} %collective-permute-done.87.refs_7_), channel_id=1, source_target_pairs={{0,1},{1,0},{2,3},{3,2},{4,5},{5,4},{6,7},{7,6},{8,9},{9,8},{10,11... | collective-permute-start | bytes 589832 | tf_op jit(solution)/shard_map/ppermute | solution.py:25
  580.6 49.4 %collective-permute-start.136 = (bf16[768,1024]{1,0:T(8,128)(2,1)}, bf16[768,1024]{1,0:T(8,128)(2,1)}, u32[]{:S(2)}, u32[]{:S(2)}) collective-permute-start(bf16[768,1024]{1,0:T(8,128)(2,1)} %convolution_convert_fusion.5), channel_id=1, source_target_pairs={{0,16},{16,0},{1,17},{17,1},{2,18},{18,2},{3,19},{19,3},{4,20},{20... | collective-permute-start | bytes 4718600 | tf_op jit(solution)/shard_map/ppermute | solution.py:25
  580.7 54.2 %collective-permute-start.156 = (bf16[768,1024]{1,0:T(8,128)(2,1)}, bf16[768,1024]{1,0:T(8,128)(2,1)}, u32[]{:S(2)}, u32[]{:S(2)}) collective-permute-start(bf16[768,1024]{1,0:T(8,128)(2,1)} %convolution_convert_fusion.3), channel_id=1, source_target_pairs={{0,16},{16,0},{1,17},{17,1},{2,18},{18,2},{3,19},{19,3},{4,20},{20... | collective-permute-start | bytes 4718600 | tf_op jit(solution)/shard_map/ppermute | solution.py:25
  582.7 61.4 %collective-permute-start.158 = (bf16[1024,768]{1,0:T(8,128)(2,1)S(1)}, bf16[1024,768]{1,0:T(8,128)(2,1)}, u32[]{:S(2)}, u32[]{:S(2)}) collective-permute-start(bf16[1024,768]{1,0:T(8,128)(2,1)S(1)} %convolution_convert_fusion.1), channel_id=1, source_target_pairs={{0,16},{16,0},{1,17},{17,1},{2,18},{18,2},{3,19},{19,3},{4,20},{20... | collective-permute-start | bytes 4718600 | tf_op jit(solution)/shard_map/ppermute | solution.py:25
  582.8 98.9 %collective-permute-start.155 = (bf16[768,1024]{1,0:T(8,128)(2,1)}, bf16[768,1024]{1,0:T(8,128)(2,1)}, u32[]{:S(2)}, u32[]{:S(2)}) collective-permute-start(bf16[768,1024]{1,0:T(8,128)(2,1)} %convolution_convert_fusion.4), channel_id=1, source_target_pairs={{0,16},{16,0},{1,17},{17,1},{2,18},{18,2},{3,19},{19,3},{4,20},{20... | collective-permute-start | bytes 4718600 | tf_op jit(solution)/shard_map/ppermute | solution.py:25
  639.4 47.0 %collective-permute-start.157 = (bf16[768,1024]{1,0:T(8,128)(2,1)S(1)}, bf16[768,1024]{1,0:T(8,128)(2,1)S(1)}, u32[]{:S(2)}, u32[]{:S(2)}) collective-permute-start(bf16[768,1024]{1,0:T(8,128)(2,1)S(1)} %copy-done.60), channel_id=1, source_target_pairs={{0,16},{16,0},{1,17},{17,1},{2,18},{18,2},{3,19},{19,3},{4,20},{20... | collective-permute-start | bytes 4718600 | tf_op jit(solution)/shard_map/ppermute | solution.py:25
  (336 other events, 4482.8 us)

commit v4 on v3

v4 whole, which is shorter than its diff:
```python
import functools

import jax
import jax.numpy as jnp
from jax import lax
from jax.experimental import pallas as pl
from jax.experimental.pallas import tpu as pltpu
from jax.sharding import PartitionSpec as P

epsilon = 1e-06
masked_value = -1e30
bf16 = jnp.bfloat16
f32 = jnp.float32
pair_lanes = 128
hidden_block = 256
chunk_rows = 256


def query_rows(seq_len):
    return 256 if seq_len <= 2048 else 128


def swap(x, axis, k):
    n = lax.axis_size(axis)
    return lax.ppermute(x, axis, [(i, i ^ k) for i in range(n)])


def after(x, token):
    return x if token is None else x + (token[:1, :1].astype(f32) * 0.0).astype(x.dtype)


def gathered(block, axis):
    count = lax.axis_size(axis)
    copies = jnp.broadcast_to(block[None], (count,) + block.shape)
    return lax.all_to_all(copies, axis, 0, 0, tiled=True).reshape((-1,) + block.shape[1:])


def all_rows(shard, own=None, token=None):
    shard = after(shard, token)
    if own is None:
        own = sent = gathered(shard, "tensor")
    else:
        sent = after(own, token)
    if lax.axis_size("context") != 4:
        return (lax.all_gather(sent, "context", tiled=True),)
    far = [swap(shard, "context", k) for k in (2, 3)]
    if token is None:
        far = [gathered(x, "tensor") for x in far]
    else:
        block, width = shard.shape
        both = gathered(jnp.concatenate(far, axis=0), "tensor").reshape(-1, 2, block, width)
        far = [both]
    return (own, swap(sent, "context", 1), *far)


def received_sum(sends):
    count = lax.axis_size("tensor")
    got = lax.all_to_all(sends.reshape(count, -1, sends.shape[1]), "tensor", 0, 0, tiled=True)
    return jnp.sum(got.astype(f32), axis=0)


def sum_over(x, axis):
    total = x
    for k in range(1, lax.axis_size(axis)):
        total = total + swap(x, axis, k)
    return total


def dot_nt(a, b):
    return lax.dot_general(a, b, (((1,), (1,)), ((), ())), preferred_element_type=f32)


def dot_tn(a, b):
    return lax.dot_general(a, b, (((0,), (0,)), ((), ())), preferred_element_type=f32)


def dot_nn(a, b):
    return jnp.dot(a, b, preferred_element_type=f32)


def each(count, body):
    if count <= 4:
        for i in range(count):
            body(i)
        return

    def one(i, carry):
        body(i)
        return carry

    lax.fori_loop(0, count, one, 0)


def rows_at(i, rows):
    start = i * rows
    return pl.ds(start if isinstance(start, int) else pl.multiple_of(start, rows), rows)


def assemble(parts, whole_ref, z):
    first, piece_len = 0, parts[0].shape[0]
    for part in parts:
        if len(part.shape) == 2:
            at = pl.multiple_of((z ^ first) * piece_len, piece_len)
            whole_ref[pl.ds(at, piece_len), :] = part[...]
            first += 1
            continue
        blocks, pieces, block = part.shape[:3]
        for p in range(pieces):
            for b in range(blocks):
                at = pl.multiple_of((z ^ (first + p)) * piece_len + b * block, block)
                whole_ref[pl.ds(at, block), :] = part[b, p]
        first += pieces


def triangle(rows, reverse):
    row = lax.broadcasted_iota(jnp.int32, (rows, rows), 0)
    column = lax.broadcasted_iota(jnp.int32, (rows, rows), 1)
    return jnp.where((column >= row) if reverse else (column <= row), 1.0, 0.0).astype(bf16)


def running_sum(ref, reverse):
    rows = chunk_rows
    ones = triangle(rows, reverse)
    count = ref.shape[0] // rows
    edge = 0 if reverse else rows - 1

    def chunk(i, carry):
        here = pl.ds(pl.multiple_of((count - 1 - i if reverse else i) * rows, rows), rows)
        high, middle, lowest = three_parts(ref[here, :])
        total = dot_nn(ones, high) + dot_nn(ones, middle) + dot_nn(ones, lowest) + carry
        ref[here, :] = total
        return total[edge : edge + 1, :]

    lax.fori_loop(0, count, chunk, jnp.zeros((1, ref.shape[1]), f32), unroll=count <= 4)


def log_sigmoid(z):
    e = jnp.exp(-jnp.abs(z))
    small = e * (1.0 - e * (1 / 2 - e * (1 / 3 - e * (1 / 4 - e * (1 / 5 - e * (1 / 6 - e * (1 / 7)))))))
    return jnp.minimum(z, 0.0) - jnp.where(e < 0.0625, small, jnp.log(1.0 + e))


def three_parts(x):
    high = x.astype(bf16)
    middle = (x - high.astype(f32)).astype(bf16)
    return high, middle, (x - high.astype(f32) - middle.astype(f32)).astype(bf16)


def decay_side(terms, pair, key_side):
    row = lax.broadcasted_iota(jnp.int32, (pair_lanes, pair_lanes), 0)
    lane = lax.broadcasted_iota(jnp.int32, (pair_lanes, pair_lanes), 1)
    spot = lane & 63
    term = spot if key_side else spot - 3
    head = jnp.where(lane >= 64, 2 * pair, 2 * pair + 1)
    chosen = (term >= 0) & (term < 3) & (row == 8 * term + head)
    pick = jnp.where(chosen, -1.0 if key_side else 1.0, 0.0).astype(bf16)
    lanes_now = lax.broadcasted_iota(jnp.int32, (1, pair_lanes), 1) & 63
    other = lanes_now - 3 if key_side else lanes_now
    ones = jnp.where((other >= 0) & (other < 3), 1.0, 0.0)
    return (dot_nn(terms, pick) + ones).astype(bf16)


def mix_keys(k_ref, terms_ref, pair, ka, kb):
    def mix(i):
        here = rows_at(i, chunk_rows)
        lane = lax.broadcasted_iota(jnp.int32, (chunk_rows, pair_lanes), 1)
        k, side = k_ref[here, :], decay_side(terms_ref[here, :], pair, True)
        ka[here, :] = jnp.where(lane < 64, k, side)
        kb[here, :] = jnp.where(lane < 64, side, k)

    each(k_ref.shape[0] // chunk_rows, mix)


def mix_queries(q_ref, terms_ref, start, pair, qa, qb):
    def mix(i):
        here = rows_at(i, chunk_rows)
        lane = lax.broadcasted_iota(jnp.int32, (chunk_rows, pair_lanes), 1)
        q = (q_ref[here, :].astype(f32) * 0.125).astype(bf16)
        terms = terms_ref[pl.ds(pl.multiple_of(start + i * chunk_rows, chunk_rows), chunk_rows), :]
        side = decay_side(terms, pair, False)
        qa[here, :] = jnp.where(lane < 64, q, side)
        qb[here, :] = jnp.where(lane < 64, side, q)

    each(q_ref.shape[0] // chunk_rows, mix)


def live_mask(start_ref, start, first, width, rows):
    key_pos = first + lax.broadcasted_iota(jnp.int32, (rows, width), 1)
    query_pos = start + lax.broadcasted_iota(jnp.int32, (rows, width), 0)
    doc_start = start_ref[pl.ds(start, rows), :]
    return (key_pos <= query_pos) & (key_pos >= doc_start)


def over_query_blocks(seq_len, rows, body):
    before = seq_len // 2
    if seq_len // rows <= 4:
        for start in range(0, seq_len, rows):
            first = max(0, start - before)
            body(start, first, start + rows - first)
        return
    width = before + rows

    def one(i, carry):
        start = pl.multiple_of(i * rows, rows)
        first = pl.multiple_of(jnp.maximum(start - before, 0), rows)
        body(start, first, width)
        return carry

    lax.fori_loop(0, seq_len // rows, one, 0)


def probabilities(q_rows, k_rows, mask):
    s = jnp.where(mask, dot_nt(q_rows, k_rows), masked_value)
    e = jnp.exp(s - jnp.max(s, axis=1, keepdims=True))
    return e * (1.0 / jnp.sum(e, axis=1, keepdims=True))


def lane_blocks(refs):
    return jnp.concatenate([r[0] for r in refs], axis=1)


def forward_own_kernel(count_parts, piece_len, join, *refs):
    place_ref, parts, refs = refs[0], refs[1 : 1 + count_parts], list(refs[1 + count_parts :])
    (wq, wk, wv, wg), (tq, tk, tv, tg) = refs[:4], refs[4:8]
    wo, to, wf, bias, start_ref = refs[8:13]
    refs = refs[13:]
    a_ref = refs.pop(0) if join else parts[0]
    k_ref, v_ref, z_ref, terms_ref, send_ref, q_own, qa, qb, ka, kb, decay, acc = refs
    pair = pl.program_id(0)
    seq_len, half = a_ref.shape[0], a_ref.shape[1] // 2
    piece_start = pl.multiple_of(place_ref[0] * piece_len, piece_len)

    @pl.when(pair == 0)
    def _():
        if join:
            assemble(parts, a_ref, place_ref[0])
        acc[...] = jnp.zeros_like(acc)

        def gates(i):
            here = rows_at(i, chunk_rows)
            z = dot_nn(a_ref[here, :], wf[...]) + bias[...]
            z_ref[here, :] = z
            decay[here, :] = log_sigmoid(z)

        each(seq_len // chunk_rows, gates)
        running_sum(decay, False)

        def split(i):
            here = rows_at(i, chunk_rows)
            lane = lax.broadcasted_iota(jnp.int32, (chunk_rows, pair_lanes), 1)
            high, middle, lowest = (x.astype(f32) for x in three_parts(decay[here, :]))
            later = jnp.where(lane < 16, pltpu.roll(middle, 8, 1), pltpu.roll(lowest, 16, 1))
            terms = jnp.where(lane < 8, high, later)
            terms_ref[here, :] = jnp.where(lane < 24, terms, 0.0).astype(bf16)

        each(seq_len // chunk_rows, split)

    w_mine, w_theirs = lane_blocks((wk, wv)), lane_blocks((tk, tv))

    def project(i):
        here = rows_at(i, chunk_rows)
        out = dot_nn(a_ref[here, :half], w_mine) + dot_nn(a_ref[here, half:], w_theirs)
        k_ref[here, :] = out[:, :128].astype(bf16)
        v_ref[here, :] = out[:, 128:].astype(bf16)

    each(seq_len // chunk_rows, project)
    piece = pl.ds(piece_start, piece_len)
    out = dot_nn(a_ref[piece, :half], lane_blocks((wq, wg))) + dot_nn(a_ref[piece, half:], lane_blocks((tq, tg)))
    q_own[...] = out[:, :128].astype(bf16)
    gate = jax.nn.sigmoid(out[:, 128:])
    mix_keys(k_ref, terms_ref, pair, ka, kb)
    mix_queries(q_own, terms_ref, piece_start, pair, qa, qb)
    before = seq_len // 2
    for s in range(0, piece_len, query_rows(seq_len)):
        rows = query_rows(seq_len)
        width = before + rows
        start = pl.multiple_of(piece_start + s, rows)
        first = pl.multiple_of(jnp.maximum(start - before, 0), rows)
        mask = live_mask(start_ref, start, first, width, rows)
        keys = pl.ds(first, width)
        out = []
        for q_of, k_of in ((qa, ka), (qb, kb)):
            p = probabilities(q_of[s : s + rows, :], k_of[keys, :], mask).astype(bf16)
            out.append(dot_nn(p, v_ref[keys, :]))
        lane = lax.broadcasted_iota(jnp.int32, (rows, pair_lanes), 1)
        u = (jnp.where(lane < 64, out[0], out[1]) * gate[s : s + rows, :]).astype(bf16)
        acc[s : s + rows, :half] += dot_nn(u, wo[0])
        acc[s : s + rows, half:] += dot_nn(u, to[0])

    @pl.when(pair == pl.num_programs(0) - 1)
    def _():
        send_ref[...] = acc[...].astype(bf16)


def forward_rest_kernel(*refs):
    a_ref, wq, wg, tq, tg, k_ref, v_ref, terms_ref, start_ref = refs[:9]
    q_ref, gate_ref, o_ref, u_ref, qa, qb, ka, kb = refs[-8:]
    pair = pl.program_id(0)
    seq_len, half = a_ref.shape[0], a_ref.shape[1] // 2
    rows = query_rows(seq_len)
    w_mine, w_theirs = lane_blocks((wq, wg)), lane_blocks((tq, tg))

    def project(i):
        here = rows_at(i, chunk_rows)
        out = dot_nn(a_ref[here, :half], w_mine) + dot_nn(a_ref[here, half:], w_theirs)
        q_ref[here, :] = out[:, :128].astype(bf16)
        gate_ref[here, :] = out[:, 128:]

    each(seq_len // chunk_rows, project)
    mix_keys(k_ref, terms_ref, pair, ka, kb)
    mix_queries(q_ref, terms_ref, 0, pair, qa, qb)
    lane = lax.broadcasted_iota(jnp.int32, (rows, pair_lanes), 1)

    def body(start, first, width):
        mask = live_mask(start_ref, start, first, width, rows)
        here, keys = pl.ds(start, rows), pl.ds(first, width)
        values = v_ref[keys, :]
        out = []
        for q_of, k_of in ((qa, ka), (qb, kb)):
            p = probabilities(q_of[here, :], k_of[keys, :], mask).astype(bf16)
            out.append(dot_nn(p, values))
        o = jnp.where(lane < 64, out[0], out[1])
        o_ref[here, :] = o
        u_ref[here, :] = (o * jax.nn.sigmoid(gate_ref[here, :])).astype(bf16)

    over_query_blocks(seq_len, rows, body)


def backward_kernel(count_parts, piece_len, join, *refs):
    place_ref, parts, refs = refs[0], refs[1 : 1 + count_parts], list(refs[1 + count_parts :])
    mine, theirs, (wo, to, wf) = refs[:4], refs[4:8], refs[8:11]
    q_ref, k_ref, v_ref, gate_ref, o_ref, z_ref, terms_ref, start_ref = refs[11:19]
    refs = refs[19:]
    y_ref = refs.pop(0) if join else parts[0]
    dq_ref, dk_ref, dv_ref, dg_ref, dz_ref, send_ref = refs[:6]
    qa, qb, ka, kb, dd, dka, dkb, dva, dcs, acc = refs[6:]
    pair = pl.program_id(0)
    seq_len, half = y_ref.shape[0], y_ref.shape[1] // 2
    rows = query_rows(seq_len)
    piece = pl.ds(pl.multiple_of(place_ref[0] * piece_len, piece_len), piece_len)

    @pl.when(pair == 0)
    def _():
        if join:
            assemble(parts, y_ref, place_ref[0])
        acc[...] = jnp.zeros_like(acc)
        dcs[...] = jnp.zeros_like(dcs)

    def gates(i):
        here = rows_at(i, chunk_rows)
        du = dot_nt(y_ref[here, :half], wo[0]) + dot_nt(y_ref[here, half:], to[0])
        sig = jax.nn.sigmoid(gate_ref[here, :])
        dd[here, :] = (du * sig).astype(bf16)
        dg_ref[here, :] = (du * o_ref[here, :] * sig * (1.0 - sig)).astype(bf16)

    each(seq_len // chunk_rows, gates)
    mix_keys(k_ref, terms_ref, pair, ka, kb)
    mix_queries(q_ref, terms_ref, 0, pair, qa, qb)
    dka[...] = jnp.zeros_like(dka)
    dkb[...] = jnp.zeros_like(dkb)
    dva[...] = jnp.zeros_like(dva)
    lane = lax.broadcasted_iota(jnp.int32, (rows, pair_lanes), 1)

    def pick(column_a, column_b):
        at = lax.broadcasted_iota(jnp.int32, (column_a.shape[0], pair_lanes), 1)
        return jnp.where(at == 2 * pair, column_a, jnp.where(at == 2 * pair + 1, column_b, 0.0))

    def body(start, first, width):
        mask = live_mask(start_ref, start, first, width, rows)
        here, keys = pl.ds(start, rows), pl.ds(first, width)
        values = v_ref[keys, :]
        d_rows = dd[here, :]
        dq = []
        for head, (q_of, k_of, dk_of) in enumerate(((qa, ka, dka), (qb, kb, dkb))):
            own_lanes = (lane < 64) if head == 0 else (lane >= 64)
            p = probabilities(q_of[here, :], k_of[keys, :], mask)
            d_mine = jnp.where(own_lanes, d_rows, jnp.zeros_like(d_rows))
            dp = dot_nt(d_mine, values)
            delta = jnp.sum(p * dp, axis=1, keepdims=True)
            ds = (p * (dp - delta)).astype(bf16)
            dq.append(dot_nn(ds, k_of[keys, :]))
            dk_of[keys, :] += dot_tn(ds, q_of[here, :])
            dva[keys, :] += dot_tn(p.astype(bf16), d_mine)
        dq_ref[here, :] = (jnp.where(lane < 64, dq[0], dq[1]) * 0.125).astype(bf16)
        dcs[here, :] += pick(dq[0][:, 67:68], dq[1][:, 3:4])

    over_query_blocks(seq_len, rows, body)

    def finish(i):
        here = rows_at(i, chunk_rows)
        lanes_now = lax.broadcasted_iota(jnp.int32, (chunk_rows, pair_lanes), 1)
        ka_rows, kb_rows = dka[here, :], dkb[here, :]
        dk_ref[here, :] = jnp.where(lanes_now < 64, ka_rows, kb_rows).astype(bf16)
        dv_ref[here, :] = dva[here, :].astype(bf16)
        dcs[here, :] -= pick(ka_rows[:, 64:65], kb_rows[:, 0:1])

    each(seq_len // chunk_rows, finish)
    d_own = jnp.concatenate([r[piece, :] for r in (dq_ref, dk_ref, dv_ref, dg_ref)], axis=1)
    acc[:, :half] += dot_nt(d_own, lane_blocks(mine))
    acc[:, half:] += dot_nt(d_own, lane_blocks(theirs))

    @pl.when(pair == pl.num_programs(0) - 1)
    def _():
        running_sum(dcs, True)

        def last(i):
            here = rows_at(i, chunk_rows)
            dz_ref[here, :] = (dcs[here, :] * jax.nn.sigmoid(-z_ref[here, :])).astype(bf16)

        each(seq_len // chunk_rows, last)
        send_ref[...] = (acc[...] + dot_nt(dz_ref[piece, :], wf[...])).astype(bf16)


def ffn_forward_kernel(b_ref, wg, wu, wd, tg, tu, td, gt_ref, up_ref, send_ref, acc):
    half = b_ref.shape[1] // 2
    low, high = b_ref[:, :half], b_ref[:, half:]
    gt = dot_nn(low, wg[0]) + dot_nn(high, tg[0])
    up = dot_nn(low, wu[0]) + dot_nn(high, tu[0])
    gt_ref[...] = gt
    up_ref[...] = up
    m = (gt * jax.nn.sigmoid(gt) * up).astype(bf16)

    @pl.when(pl.program_id(0) == 0)
    def _():
        acc[...] = jnp.zeros_like(acc)

    acc[:, :half] += dot_nn(m, wd[0])
    acc[:, half:] += dot_nn(m, td[0])

    @pl.when(pl.program_id(0) == pl.num_programs(0) - 1)
    def _():
        send_ref[...] = acc[...].astype(bf16)


def inner_grads(dm, gt, up):
    sig = jax.nn.sigmoid(gt)
    d_gate = (dm * up * sig * (1.0 + gt * (1.0 - sig))).astype(bf16)
    return d_gate, (dm * (gt * sig)).astype(bf16)


def ffn_backward_kernel(g_ref, gt_ref, up_ref, wg, wu, wd, tg, tu, td, send_ref, acc):
    half = g_ref.shape[1] // 2
    dm = dot_nt(g_ref[:, :half], wd[0]) + dot_nt(g_ref[:, half:], td[0])
    d_gate, d_up = inner_grads(dm, gt_ref[...], up_ref[...])

    @pl.when(pl.program_id(0) == 0)
    def _():
        acc[...] = jnp.zeros_like(acc)

    acc[:, :half] += dot_nt(d_gate, wg[0]) + dot_nt(d_up, wu[0])
    acc[:, half:] += dot_nt(d_gate, tg[0]) + dot_nt(d_up, tu[0])

    @pl.when(pl.program_id(0) == pl.num_programs(0) - 1)
    def _():
        send_ref[...] = acc[...].astype(bf16)


def ffn_inner_kernel(count_parts, *refs):
    place_ref, refs = refs[0], refs[1:]
    b_parts, g_parts = refs[:count_parts], refs[count_parts : 2 * count_parts]
    wg, wu, wd, tg, tu, td = refs[2 * count_parts : 2 * count_parts + 6]
    b_ref, g_ref, m_ref, dgate_ref, dup_ref = refs[-5:]
    half = b_ref.shape[1] // 2

    @pl.when(pl.program_id(0) == 0)
    def _():
        assemble(b_parts, b_ref, place_ref[0])
        assemble(g_parts, g_ref, place_ref[0])

    def chunk(i):
        here = rows_at(i, chunk_rows)
        low, high = b_ref[here, :half], b_ref[here, half:]
        gt = dot_nn(low, wg[0]) + dot_nn(high, tg[0])
        up = dot_nn(low, wu[0]) + dot_nn(high, tu[0])
        dm = dot_nt(g_ref[here, :half], wd[0]) + dot_nt(g_ref[here, half:], td[0])
        m_ref[here, :] = (gt * jax.nn.sigmoid(gt) * up).astype(bf16)
        dgate_ref[here, :], dup_ref[here, :] = inner_grads(dm, gt, up)

    each(b_ref.shape[0] // chunk_rows, chunk)


def fixed(shape, single=True):
    zeros = (0,) * len(shape)
    if single:
        return pl.BlockSpec(shape, lambda *_: zeros, pipeline_mode=pl.Buffered(1))
    return pl.BlockSpec(shape, lambda *_: zeros)


def lanes(seq_len):
    return pl.BlockSpec((seq_len, pair_lanes), lambda p, *_: (0, p))


def lanes_read(seq_len):
    if seq_len <= 2048:
        return lanes(seq_len)
    return pl.BlockSpec((seq_len, pair_lanes), lambda p, *_: (0, p), pipeline_mode=pl.Buffered(1))


def columns_of(w, layer, width):
    return pl.BlockSpec((1, w.shape[1], width), lambda p, *_: (layer, 0, p))


def rows_of(w, layer, height):
    return pl.BlockSpec((1, height, w.shape[2]), lambda p, *_: (layer, p, 0))


def shape(dims, dtype):
    return jax.ShapeDtypeStruct(dims, dtype)


def attention_specs(parts, layer, w4, t4, wo, to, seq_len, join):
    specs = [fixed(p.shape) for p in parts]
    specs += [columns_of(w, layer, pair_lanes) for w in (*w4, *t4)]
    specs += [rows_of(wo, layer, pair_lanes), rows_of(to, layer, pair_lanes)]
    return specs


def cost(microseconds):
    return pl.CostEstimate(flops=int(microseconds * 1.1e9), bytes_accessed=0, transcendentals=0)


def token_specs(tokens):
    return [pl.BlockSpec((16, 128), lambda *_: (0, 0)) for _ in tokens]


def forward_own(place, parts, layer, w4, t4, wo, to, wf, bias, doc_start, piece_len):
    seq_len, width = doc_start.shape[0], parts[0].shape[1]
    local_width = wo.shape[1]
    join = len(parts) > 1
    terms = (seq_len, pair_lanes)
    outs = [shape((seq_len, local_width), bf16)] * 2 + [shape(terms, f32), shape(terms, bf16)]
    outs += [shape((piece_len, width), bf16)]
    specs = [lanes(seq_len)] * 2 + [fixed(terms, False)] * 2 + [fixed((piece_len, width), False)]
    if join:
        outs, specs = [shape((seq_len, width), bf16)] + outs, [fixed((seq_len, width))] + specs
    low, piece = pltpu.VMEM((seq_len, pair_lanes), bf16), pltpu.VMEM((piece_len, pair_lanes), bf16)
    got = pl.pallas_call(
        functools.partial(forward_own_kernel, len(parts), piece_len, join),
        grid_spec=pltpu.PrefetchScalarGridSpec(
            num_scalar_prefetch=1,
            grid=(local_width // pair_lanes,),
            in_specs=attention_specs(parts, layer, w4, t4, wo, to, seq_len, join)
            + [fixed(wf.shape), fixed(bias.shape), fixed(doc_start.shape)],
            out_specs=specs,
            scratch_shapes=[piece] * 3 + [low] * 2 + [pltpu.VMEM(terms, f32), pltpu.VMEM((piece_len, width), f32)],
        ),
        out_shape=outs,
        cost_estimate=cost(14),
        compiler_params=pltpu.CompilerParams(vmem_limit_bytes=60 << 20),
    )(place, *parts, *w4, *t4, wo, to, wf, bias, doc_start)
    got = list(got)
    a = got.pop(0) if join else parts[0]
    return a, got[:4], got[4]


def forward_rest(a, layer, w4, t4, k, v, terms, doc_start, *tokens):
    seq_len = a.shape[0]
    local_width = k.shape[1]
    low, high = shape((seq_len, local_width), bf16), shape((seq_len, local_width), f32)
    weights = (w4[0], w4[3], t4[0], t4[3])
    return pl.pallas_call(
        forward_rest_kernel,
        grid=(local_width // pair_lanes,),
        in_specs=[fixed(a.shape)]
        + [columns_of(w, layer, pair_lanes) for w in weights]
        + [lanes_read(seq_len)] * 2
        + [fixed(terms.shape), fixed(doc_start.shape)]
        + token_specs(tokens),
        out_specs=[lanes(seq_len)] * 4,
        scratch_shapes=[pltpu.VMEM((seq_len, pair_lanes), bf16)] * 4,
        out_shape=[low, high, high, low],
        cost_estimate=cost(20),
        compiler_params=pltpu.CompilerParams(vmem_limit_bytes=60 << 20),
    )(a, *weights, k, v, terms, doc_start, *tokens)


def attention_backward(place, parts, layer, w4, t4, wo, to, wf, saved, doc_start, piece_len):
    q, k, v, gate, o, z, terms = saved
    seq_len, width = doc_start.shape[0], parts[0].shape[1]
    local_width = wo.shape[1]
    join = len(parts) > 1
    outs = [shape((seq_len, local_width), bf16)] * 4 + [shape((seq_len, pair_lanes), bf16)]
    outs += [shape((piece_len, width), bf16)]
    specs = [lanes(seq_len)] * 4 + [fixed((seq_len, pair_lanes), False), fixed((piece_len, width), False)]
    if join:
        outs, specs = [shape((seq_len, width), bf16)] + outs, [fixed((seq_len, width))] + specs
    low, high = pltpu.VMEM((seq_len, pair_lanes), bf16), pltpu.VMEM((seq_len, pair_lanes), f32)
    got = pl.pallas_call(
        functools.partial(backward_kernel, len(parts), piece_len, join),
        grid_spec=pltpu.PrefetchScalarGridSpec(
            num_scalar_prefetch=1,
            grid=(local_width // pair_lanes,),
            in_specs=attention_specs(parts, layer, w4, t4, wo, to, seq_len, join)
            + [fixed(wf.shape)]
            + [lanes_read(seq_len)] * 5
            + [fixed(z.shape), fixed(terms.shape), fixed(doc_start.shape)],
            out_specs=specs,
            scratch_shapes=[low] * 5 + [high] * 4 + [pltpu.VMEM((piece_len, width), f32)],
        ),
        out_shape=outs,
        cost_estimate=cost(32),
        compiler_params=pltpu.CompilerParams(vmem_limit_bytes=60 << 20),
    )(place, *parts, *w4, *t4, wo, to, wf, q, k, v, gate, o, z, terms, doc_start)
    got = list(got)
    y = got.pop(0) if join else parts[0]
    return y, got[:5], got[5]


def ffn_weights(layer, w3, t3):
    specs = []
    for wg, wu, wd in (w3, t3):
        specs += [
            columns_of(wg, layer, hidden_block), columns_of(wu, layer, hidden_block), rows_of(wd, layer, hidden_block),
        ]
    return specs


def blocks_of(rows):
    return pl.BlockSpec((rows, hidden_block), lambda p, *_: (0, p))


def ffn_forward(b, layer, w3, t3):
    rows, width = b.shape
    inner = w3[2].shape[1]
    return pl.pallas_call(
        ffn_forward_kernel,
        grid=(inner // hidden_block,),
        in_specs=[fixed(b.shape)] + ffn_weights(layer, w3, t3),
        out_specs=[blocks_of(rows)] * 2 + [fixed((rows, width), False)],
        scratch_shapes=[pltpu.VMEM((rows, width), f32)],
        out_shape=[shape((rows, inner), f32)] * 2 + [shape((rows, width), bf16)],
        cost_estimate=cost(7),
        compiler_params=pltpu.CompilerParams(vmem_limit_bytes=40 << 20),
    )(b, *w3, *t3)


def ffn_backward(g, gt, up, layer, w3, t3):
    rows, width = g.shape
    return pl.pallas_call(
        ffn_backward_kernel,
        grid=(gt.shape[1] // hidden_block,),
        in_specs=[fixed(g.shape)] + [blocks_of(rows)] * 2 + ffn_weights(layer, w3, t3),
        out_specs=fixed((rows, width), False),
        scratch_shapes=[pltpu.VMEM((rows, width), f32)],
        out_shape=shape((rows, width), bf16),
        cost_estimate=cost(8),
        compiler_params=pltpu.CompilerParams(vmem_limit_bytes=40 << 20),
    )(g, gt, up, *w3, *t3)


def ffn_inner(place, b_parts, g_parts, layer, w3, t3, *tokens):
    width = b_parts[0].shape[1]
    rows = sum(p.size for p in b_parts) // width
    inner = w3[2].shape[1]
    return pl.pallas_call(
        functools.partial(ffn_inner_kernel, len(b_parts)),
        grid_spec=pltpu.PrefetchScalarGridSpec(
            num_scalar_prefetch=1,
            grid=(inner // hidden_block,),
            in_specs=[fixed(p.shape) for p in (*b_parts, *g_parts)]
            + ffn_weights(layer, w3, t3)
            + token_specs(tokens),
            out_specs=[fixed((rows, width))] * 2 + [blocks_of(rows)] * 3,
        ),
        out_shape=[shape((rows, width), bf16)] * 2 + [shape((rows, inner), bf16)] * 3,
        cost_estimate=cost(16),
        compiler_params=pltpu.CompilerParams(vmem_limit_bytes=56 << 20),
    )(place, *b_parts, *g_parts, *w3, *t3, *tokens)


def unset_kernel(*refs):
    pass


def unset(*like):
    return pl.pallas_call(
        unset_kernel,
        out_specs=[pl.BlockSpec(memory_space=pl.ANY) for _ in like],
        out_shape=list(like),
    )()


def inverse_rms(h):
    return lax.rsqrt(jnp.mean(h * h, axis=-1, keepdims=True) + epsilon)


def norm_back(grad_normed, hidden, inverse, gain):
    scaled = hidden * inverse
    weighted = grad_normed * gain
    grad_gain = jnp.sum(grad_normed * scaled, axis=0)
    mean = jnp.mean(weighted * scaled, axis=-1, keepdims=True)
    return inverse * (weighted - scaled * mean), grad_gain


def local(
    hidden_in, segment_ids, w_query, w_key, w_value, w_gate_out, w_attn_out, w_forget, b_forget,
    gain_attn, gain_ffn, w_gate, w_up, w_down, cotangent,
):
    seq_count, piece_len, width = hidden_in.shape
    count_z, count_t = lax.axis_size("context"), lax.axis_size("tensor")
    core, z, t = lax.axis_index("fsdp"), lax.axis_index("context"), lax.axis_index("tensor")
    layers, half, local_width = w_query.shape
    heads = w_forget.shape[2]
    block = piece_len // count_t
    seq_len = piece_len * count_z
    shared_rows = count_z == 4
    place = z.reshape(1).astype(jnp.int32)
    own_place = place if shared_rows else jnp.zeros((1,), jnp.int32)

    def features(x):
        return jnp.where(core == 0, x, jnp.concatenate([x[..., half:], x[..., :half]], axis=-1))

    def own_block(x):
        return lax.dynamic_slice_in_dim(x, t * block, block, 0)

    def other(w):
        return swap(w, "fsdp", 1)

    def full(w, axis):
        return jnp.concatenate([w, other(w)], axis=axis)

    seg_all = gathered(segment_ids.reshape(1, piece_len), "context").reshape(seq_len)
    doc_start = jnp.sum((seg_all[None, :] < seg_all[:, None]).astype(jnp.int32), axis=1, keepdims=True)

    gains = full(jnp.concatenate([gain_attn, gain_ffn], axis=0), 1).astype(f32)
    hidden_rows = features(hidden_in.reshape(piece_len, width)).astype(f32)
    first_a = (hidden_rows * inverse_rms(hidden_rows) * gains[0]).astype(bf16)
    first_a = after(first_a, seg_all.reshape(1, seq_len))
    a_parts = all_rows(own_block(first_a), first_a)

    w_forget_full = jnp.pad(full(w_forget, 1), ((0, 0), (0, 0), (0, pair_lanes - heads)))
    bias = jnp.pad(b_forget, ((0, 0), (0, pair_lanes - heads)))
    w4 = (w_query, w_key, w_value, w_gate_out)
    t4 = tuple(other(w) for w in w4)
    to = other(w_attn_out)
    w3 = (w_gate, w_up, w_down)
    t3 = tuple(other(w) for w in w3)

    hidden = own_block(hidden_rows)
    saved = []
    cotangent_rows = features(cotangent.reshape(piece_len, width))
    for layer in range(layers):
        gain_one, gain_two = gains[layer], gains[layers + layer]
        inverse_one = inverse_rms(hidden)
        if layer > 0:
            a_parts = all_rows((hidden * inverse_one * gain_one).astype(bf16))
        a, (k, v, forget, terms), sends = forward_own(
            place, a_parts, layer, w4, t4, w_attn_out, to, w_forget_full[layer],
            bias[layer : layer + 1], doc_start, piece_len,
        )
        if shared_rows:
            if layer == 0:
                g_last = all_rows(own_block(cotangent_rows), cotangent_rows, a_parts[-1])
            else:
                before = saved[-1]
                before["b_parts"] = all_rows(before["b_shard"], before["b"], a_parts[-1])
        mixed = hidden + received_sum(sends)
        inverse_two = inverse_rms(mixed)
        b_shard = (mixed * inverse_two * gain_two).astype(bf16)
        b = gathered(b_shard, "tensor")
        gt, up, sends = ffn_forward(b, layer, w3, t3)
        saved.append(
            dict(hidden=hidden, inverse_one=inverse_one, a=a, k=k, v=v, forget=forget, terms=terms, mixed=mixed,
                 inverse_two=inverse_two, b=b, b_shard=b_shard, gt=gt, up=up)
        )
        if layer < layers - 1:
            hidden = mixed + received_sum(sends)

    def finish(x):
        return features(gathered(x.astype(bf16), "tensor")).reshape(1, piece_len, width)

    last_sends = sends
    grad = own_block(cotangent_rows).astype(f32)
    wide = shape((layers, half, local_width), f32)
    inner = shape((layers, half, w_gate.shape[2]), f32)
    results = list(
        unset(
            wide, wide, wide, wide, shape((layers, local_width, half), f32),
            inner, inner, shape((layers, w_down.shape[1], half), f32),
        )
    )
    small = [[None] * layers for _ in range(2)]
    gain_grads = [None] * (2 * layers)

    for layer in reversed(range(layers)):
        s = saved[layer]
        gain_one, gain_two = gains[layer], gains[layers + layer]
        g_shard = grad.astype(bf16)
        g = cotangent_rows if layer == layers - 1 else gathered(g_shard, "tensor")
        sends = ffn_backward(g, s["gt"], s["up"], layer, w3, t3)
        back, gain_grads[layers + layer] = norm_back(received_sum(sends), s["mixed"], s["inverse_two"], gain_two)
        grad_mixed = grad + back
        y_shard = grad_mixed.astype(bf16)
        if layer == layers - 1:
            rest_token = y_shard
        y_parts = all_rows(y_shard)
        q, gate, o, u = forward_rest(s["a"], layer, w4, t4, s["k"], s["v"], s["terms"], doc_start, rest_token)
        y, (dq, dk, dv, dg, dz), sends = attention_backward(
            place, y_parts, layer, w4, t4, w_attn_out, to, w_forget_full[layer],
            (q, s["k"], s["v"], gate, o, s["forget"], s["terms"]), doc_start, piece_len,
        )
        if not shared_rows:
            b_parts, g_parts = (s["b"],), (g,)
        elif layer == layers - 1:
            b_parts, g_parts = all_rows(s["b_shard"], s["b"], y_parts[-1]), g_last
        else:
            b_parts, g_parts = s["b_parts"], all_rows(g_shard, g, y_parts[-1])
        if layer == layers - 1:
            output = finish(s["mixed"] + received_sum(after(last_sends, y_parts[-1])))
        back, gain_grads[layer] = norm_back(received_sum(sends), s["hidden"], s["inverse_one"], gain_one)
        grad = grad_mixed + back
        s.update(u=u, y=y, d=(dq, dk, dv, dg), dz=dz, b_parts=b_parts, g_parts=g_parts, y_shard=y_shard)

    def weight_grads(layer, token):
        s = saved[layer]
        b, g, m, d_gate, d_up = ffn_inner(own_place, s["b_parts"], s["g_parts"], layer, w3, t3, token)

        def put(k, mine, theirs):
            total = mine + other(theirs).astype(f32)
            if k >= 5 and not shared_rows:
                total = lax.psum(total, "context")
            results[k] = lax.dynamic_update_slice_in_dim(results[k], total[None], layer, 0)

        def by_rows(k, x, d):
            put(k, dot_tn(x[:, :half], d), dot_tn(x[:, half:], d).astype(bf16))

        def by_columns(k, x, d):
            put(k, dot_tn(x, d[:, :half]), dot_tn(x, d[:, half:]).astype(bf16))

        a = s["a"]
        for k, d in enumerate(s["d"]):
            by_rows(k, a, d)
        by_columns(4, s["u"], s["y"])
        by_rows(5, b, d_gate)
        by_rows(6, b, d_up)
        by_columns(7, m, g)
        dzr = s["dz"][:, :heads]
        bias_grad = jnp.sum(dzr.astype(f32), axis=0)
        small[0][layer] = dot_tn(a[:, :half], dzr) + other(dot_tn(a[:, half:], dzr))
        small[1][layer] = bias_grad + other(bias_grad)

    for layer in reversed(range(layers)):
        weight_grads(layer, saved[max(layer - 1, 0)]["y_shard"])
    grad_input = finish(grad)
    gain_total = sum_over(sum_over(jnp.stack(gain_grads), "tensor"), "context")
    gain_total = gain_total[:, :half] + other(gain_total[:, half:])
    return (
        output, grad_input, *results[:5], jnp.stack(small[0]), jnp.stack(small[1]),
        gain_total[:layers], gain_total[layers:], *results[5:],
    )


def solution(mesh):
    rows = P("fsdp", "context", None)
    wide, tall = P(None, "fsdp", "tensor"), P(None, "tensor", "fsdp")
    heads, gain = P(None, "tensor"), P(None, "fsdp")
    return jax.shard_map(
        local,
        mesh=mesh,
        in_specs=(
            rows, P("fsdp", "context"), wide, wide, wide, wide, tall, wide, heads, gain, gain, wide, wide, tall, rows,
        ),
        out_specs=(rows, rows, wide, wide, wide, wide, tall, wide, heads, gain, gain, wide, wide, tall),
        check_vma=False,
    )
```

time: 702 us -> 751 us (1.070)
  matrix products: 67.5 us -> 110 us
  blocking collectives: 0 us -> 34 us
  waiting for transfers between devices: 190 us -> 165 us
  starting transfers between devices: 174 us -> 150 us
  local copies, waits for them, and re-layouts: 34.4 us -> 49.5 us
    ppermute x160 -> x61, starting transfers between devices: 174 us -> 41.3 us  [swap(): return lax.ppermute(x, axis, [(i, i ^ k) for i in range(n)])]
    ppermute x160 -> x61, waiting for transfers between devices: 190 us -> 79.8 us  [swap(): return lax.ppermute(x, axis, [(i, i ^ k) for i in range(n)])]
    all_to_all x0 -> x26, starting transfers between devices: none -> 109 us  [the longest x20 84.5 us: gathered(): lax.all_to_all(copies, axis, 0, 0, tiled=True)]
    all_to_all x0 -> x26, waiting for transfers between devices: none -> 85 us  [the longest x20 70.9 us: gathered(): lax.all_to_all(copies, axis, 0, 0, tiled=True)]
    dot_general x36, matrix products: 67.5 us -> 110 us  [dot_tn(): lax.dot_general(a, b, (((0,), (0,)), ((), ())), preferred_element_type=f32)]
    all_to_all x0 -> x3, blocking collectives: none -> 34 us  [the longest x2 23.1 us: received_sum(): lax.all_to_all(sends.reshape(count, -1, sends.shape[1]), 'tensor', 0, 0,...]
    broadcast_in_dim x0 -> x21, local copies, waits for them, and re-layouts: none -> 24.9 us  [gathered(): copies = jnp.broadcast_to(block[None], (count,) + block.shape)]
    unnamed x417 -> x227, local copies, waits for them, and re-layouts: 22.5 us -> 11.1 us
  transfers between devices with their start and end apart: 160 -> 87, of which waited for: 67 -> 27; matrix products, arithmetic and copies ran while one was open for 14% -> 23% of each run, Pallas kernels for 28% -> 24%
where the time goes in v4:
time: 751 us; the launch traced here: 741 us
  Pallas kernels  198 us (26%)
  waiting for transfers between devices  165 us (22%)
  starting transfers between devices  150 us (20%)
  matrix products  110 us (15%)
  local copies, waits for them, and re-layouts  49.5 us (7%)
  blocking collectives  34 us (5%)
  other arithmetic  28 us (4%)
    dot_general x36, matrix products, dot_tn(): lax.dot_general(a, b, (((0,), (0,)), ((), ())), preferred_element_type=f32)  110 us
    all_to_all x20, starting transfers between devices, gathered(): lax.all_to_all(copies, axis, 0, 0, tiled=True)  84.5 us
    ppermute x61, waiting for transfers between devices, swap(): return lax.ppermute(x, axis, [(i, i ^ k) for i in range(n)])  79.8 us
    all_to_all x20, waiting for transfers between devices, gathered(): lax.all_to_all(copies, axis, 0, 0, tiled=True)  70.9 us
    pallas_call x2, Pallas kernels, attention_backward(): pl.pallas_call(functools.partial(backward_kernel, len(parts), piece_len,...  61.9 us
    ppermute x61, starting transfers between devices, swap(): return lax.ppermute(x, axis, [(i, i ^ k) for i in range(n)])  41.3 us
    pallas_call x2, Pallas kernels, forward_rest(): pl.pallas_call(forward_rest_kernel, grid=(local_width // pair_lanes,), in...  36.9 us
    pallas_call x2, Pallas kernels, ffn_inner(): pl.pallas_call(functools.partial(ffn_inner_kernel, len(b_parts)), grid_sp...  36.1 us
  transfers between devices with their start and end apart: 87, of which 27 were waited for; matrix products, arithmetic and copies ran while one was open for 23% of the time, Pallas kernels for 24%

profile of v4, /device:TPU:0, one launch (start us, length us, event | category | flops | bytes accessed | tf_op | source)
XLA Modules:
  0.0 740.8 jit_solution(7714524276899680297)
XLA Ops:
  3.2 5.9 all-to-all-start
  19.8 21.1 %collective-permute-done.3 = bf16[64,1536]{1,0:T(8,128)(2,1)S(1)} collective-permute-done((bf16[64,1536]{1,0:T(8,128)(2,1)S(1)}, bf16[64,1536]{1,0:T(8,128)(2,1)S(1)}, u32[]{:S(2)}, u32[]{:S(2)}) %collective-permute-start.3) | collective-permute-done | bytes 196640 | tf_op jit(solution)/shard_map/ppermute | solution.py:25
  66.9 16.8 %shard_map.254 = (bf16[1024,1536]{1,0:T(8,128)(2,1)}, bf16[1024,384]{1,0:T(8,128)(2,1)}, bf16[1024,384]{1,0:T(8,128)(2,1)}, f32[1024,128]{1,0:T(8,128)}, bf16[10...) custom-call(s32[1]{0:T(128)} %bitcast.1.refs_0_, bf16[256,1536]{1,0:T(8,128)(2,1)} %copy-done.25, ...), custom_call_target="tpu_custom_call" | custom-call | flops 15399999488 | tf_op jit(solution)/shard_map/pallas_call | solution.py:537
  83.7 12.0 %all_to_all.145 = bf16[4,64,1536]{2,1,0:T(8,128)(2,1)S(1)} all-to-all(bf16[4,64,1536]{2,1,0:T(8,128)(2,1)} %bitcast.177), channel_id=1, replica_groups=mesh['fsdp'=2,'context'=4,'tensor'=4] {'tensor'}, dimensions={0} | all-to-all | bytes 1572864 | tf_op jit(solution)/shard_map/all_to_all | solution.py:58
  97.3 10.9 %all_to_all.146 = bf16[4,64,1536]{2,1,0:T(8,128)(2,1)S(1)} all-to-all(bf16[4,64,1536]{2,1,0:T(8,128)(2,1)S(1)} %broadcast_in_dim.83), channel_id=1, replica_groups=mesh['fsdp'=2,'context'=4,'tensor'=4] {'tensor'}, dimensions={0} | all-to-all | bytes 1572864 | tf_op jit(solution)/shard_map/all_to_all | solution.py:35
  108.2 6.9 shard_map.255
  115.2 11.1 %all_to_all.147 = bf16[4,64,1536]{2,1,0:T(8,128)(2,1)S(1)} all-to-all(bf16[4,64,1536]{2,1,0:T(8,128)(2,1)S(1)} %bitcast.164), channel_id=1, replica_groups=mesh['fsdp'=2,'context'=4,'tensor'=4] {'tensor'}, dimensions={0} | all-to-all | bytes 1572864 | tf_op jit(solution)/shard_map/all_to_all | solution.py:58
  131.9 8.6 %collective-permute-done.14 = bf16[64,1536]{1,0:T(8,128)(2,1)S(1)} collective-permute-done((bf16[64,1536]{1,0:T(8,128)(2,1)S(1)}, bf16[64,1536]{1,0:T(8,128)(2,1)S(1)}, u32[]{:S(2)}, u32[]{:S(2)}) %collective-permute-start.14) | collective-permute-done | bytes 196640 | tf_op jit(solution)/shard_map/ppermute | solution.py:25
  146.9 7.4 %collective-permute-done.15 = bf16[64,1536]{1,0:T(8,128)(2,1)S(1)} collective-permute-done((bf16[64,1536]{1,0:T(8,128)(2,1)S(1)}, bf16[64,1536]{1,0:T(8,128)(2,1)S(1)}, u32[]{:S(2)}, u32[]{:S(2)}) %collective-permute-start.15) | collective-permute-done | bytes 196640 | tf_op jit(solution)/shard_map/ppermute | solution.py:25
  170.5 16.8 %shard_map.256 = (bf16[1024,1536]{1,0:T(8,128)(2,1)}, bf16[1024,384]{1,0:T(8,128)(2,1)}, bf16[1024,384]{1,0:T(8,128)(2,1)}, f32[1024,128]{1,0:T(8,128)}, bf16[10...) custom-call(s32[1]{0:T(128)} %bitcast.1.refs_0_, bf16[256,1536]{1,0:T(8,128)(2,1)} %bitcast.13.refs_1_, ...), custom_call_target="tpu_custom_call" | custom-call | flops 15399999488 | tf_op jit(solution)/shard_map/pallas_call | solution.py:537
  218.3 6.9 shard_map.257
  225.2 7.5 %shard_map.258 = bf16[256,1536]{1,0:T(8,128)(2,1)S(1)} custom-call(bf16[256,1536]{1,0:T(8,128)(2,1)S(1)} %get-tuple-element.199.g_ref.refs_4_, f32[256,1024]{1,0:T(8,128)S(1)} %get-tuple-element.76.gt_ref, f32[256,1024]{1,0:T(8,128)S(1)} %get-tuple-element.77.up_ref, bf16[2,768,1024]{2,1,0:T(8,128)(2,1)} %refs_7_.11, bf16[2,768,1024]{2,1,0:T(8,128)(2,1)} %refs_8_.11, ...), custom_call_target="tpu_custom_call" | custom-call | flops 8800000000 | tf_op jit(solution)/shard_map/pallas_call | solution.py:639
  240.6 6.0 all-to-all-done.11
  258.8 18.4 %shard_map.259 = (bf16[1024,384]{1,0:T(8,128)(2,1)}, f32[1024,384]{1,0:T(8,128)}, f32[1024,384]{1,0:T(8,128)}, bf16[1024,384]{1,0:T(8,128)(2,1)}) custom-call(bf16[1024,1536]{1,0:T(8,128)(2,1)} %get-tuple-element.78.refs_0_, bf16[2,768,384]{2,1,0:T(8,128)(2,1)} %refs_5_.7, bf16[2,768,384]{2,1,0:T(8,128)(2,1)} %refs_8_.9, ...), custom_call_target="tpu_custom_call" | custom-call | flops 22000001024 | tf_op jit(solution)/shard_map/pallas_call | solution.py:561
  283.2 18.6 %shard_map.262 = (bf16[1024,384]{1,0:T(8,128)(2,1)}, f32[1024,384]{1,0:T(8,128)}, f32[1024,384]{1,0:T(8,128)}, bf16[1024,384]{1,0:T(8,128)(2,1)}) custom-call(bf16[1024,1536]{1,0:T(8,128)(2,1)} %get-tuple-element.89.refs_0_, bf16[2,768,384]{2,1,0:T(8,128)(2,1)} %refs_5_.7, bf16[2,768,384]{2,1,0:T(8,128)(2,1)} %refs_8_.9, ...), custom_call_target="tpu_custom_call" | custom-call | flops 22000001024 | tf_op jit(solution)/shard_map/pallas_call | solution.py:561
  316.4 10.0 %collective-permute-done.45 = bf16[64,1536]{1,0:T(8,128)(2,1)S(1)} collective-permute-done((bf16[64,1536]{1,0:T(8,128)(2,1)S(1)}, bf16[64,1536]{1,0:T(8,128)(2,1)S(1)}, u32[]{:S(2)}, u32[]{:S(2)}) %collective-permute-start.45) | collective-permute-done | bytes 196640 | tf_op jit(solution)/shard_map/ppermute | solution.py:25
  331.6 31.0 %shard_map.260 = (bf16[1024,1536]{1,0:T(8,128)(2,1)}, bf16[1024,384]{1,0:T(8,128)(2,1)}, bf16[1024,384]{1,0:T(8,128)(2,1)}, bf16[1024,384]{1,0:T(8,128)(2,1)}, b...) custom-call(s32[1]{0:T(128)} %bitcast.1.refs_0_, ...), custom_call_target="tpu_custom_call" | custom-call | flops 35200000000 | tf_op jit(solution)/shard_map/pallas_call | solution.py:588
  386.1 6.5 all-to-all-done.17
  404.3 13.3 %all-to-all-done.26 = bf16[4,128,1536]{2,1,0:T(8,128)(2,1)} async-done(((bf16[4,128,1536]{2,1,0:T(8,128)(2,1)}), bf16[4,128,1536]{2,1,0:T(8,128)(2,1)}, u32[]{:S(2)}, u32[]{:S(2)}) %all-to-all-start.26) | async-done | bytes 1572896 | tf_op jit(solution)/shard_map/all_to_all | solution.py:35
  438.6 8.4 %shard_map.261 = bf16[256,1536]{1,0:T(8,128)(2,1)} custom-call(bf16[256,1536]{1,0:T(8,128)(2,1)S(1)} %bitcast.159, f32[256,1024]{1,0:T(8,128)S(1)} %copy-done.6, f32[256,1024]{1,0:T(8,128)S(1)} %copy-done.8, bf16[2,768,1024]{2,1,0:T(8,128)(2,1)} %refs_7_.11, bf16[2,768,1024]{2,1,0:T(8,128)(2,1)} %refs_8_.11, bf16[2,1024,768]{2,1,0:T(8,128)(2,1)} %refs_9_.3, ...), custom_call_target="tpu_custom_call" | custom-call | flops 8800000000 | tf_op jit(solution)/shard_map/pallas_call | solution.py:639
  476.3 11.0 %all-to-all-done.25 = bf16[4,128,1536]{2,1,0:T(8,128)(2,1)} async-done(((bf16[4,128,1536]{2,1,0:T(8,128)(2,1)}), bf16[4,128,1536]{2,1,0:T(8,128)(2,1)}, u32[]{:S(2)}, u32[]{:S(2)}) %all-to-all-start.25) | async-done | bytes 1572896 | tf_op jit(solution)/shard_map/all_to_all | solution.py:35
  491.7 17.9 %shard_map.265 = (bf16[1024,1536]{1,0:T(8,128)(2,1)}, bf16[1024,1536]{1,0:T(8,128)(2,1)}, bf16[1024,1024]{1,0:T(8,128)(2,1)}, bf16[1024,1024]{1,0:T(8,128)(2,1)}, bf16[1024,1024]{1,0:T(8,128)(2,1)}) custom-call(s32[1]{0:T(128)} %bitcast.1.refs_0_, bf16[256,1536]{1,0:T(8,128)(2,1)} %bitcast.162, bf16[256,1536]{1,0:T(8,128)(2,1)} %collective-permute-done.43.refs_2_, ...), custom_call_target="tpu_custom_call" | custom-call | flops 17600000000 | tf_op jit(solution)/shard_map/pallas_call | solution.py:655
  509.7 5.1 convolution_convert_fusion.5
  520.0 5.2 convolution_convert_fusion.3
  544.7 10.6 %collective-permute-done.55 = bf16[64,1536]{1,0:T(8,128)(2,1)S(1)} collective-permute-done((bf16[64,1536]{1,0:T(8,128)(2,1)S(1)}, bf16[64,1536]{1,0:T(8,128)(2,1)S(1)}, u32[]{:S(2)}, u32[]{:S(2)}) %collective-permute-start.55) | collective-permute-done | bytes 196640 | tf_op jit(solution)/shard_map/ppermute | solution.py:25
  555.3 5.8 collective-permute-done.54
  561.1 30.9 %shard_map.263 = (bf16[1024,1536]{1,0:T(8,128)(2,1)}, bf16[1024,384]{1,0:T(8,128)(2,1)}, bf16[1024,384]{1,0:T(8,128)(2,1)}, bf16[1024,384]{1,0:T(8,128)(2,1)}, b...) custom-call(s32[1]{0:T(128)} %bitcast.1.refs_0_, bf16[256,1536]{1,0:T(8,128)(2,1)} %bitcast.173, ...), custom_call_target="tpu_custom_call" | custom-call | flops 35200000000 | tf_op jit(solution)/shard_map/pallas_call | solution.py:588
  650.7 7.1 collective-permute-done.38
  675.0 15.2 %all-to-all-done.28 = bf16[4,128,1536]{2,1,0:T(8,128)(2,1)S(1)} async-done(((bf16[4,128,1536]{2,1,0:T(8,128)(2,1)}), bf16[4,128,1536]{2,1,0:T(8,128)(2,1)S(1)}, u32[]{:S(2)}, u32[]{:S(2)}) %all-to-all-start.28) | async-done | bytes 1572896 | tf_op jit(solution)/shard_map/all_to_all | solution.py:35
  694.8 18.1 %shard_map.266 = (bf16[1024,1536]{1,0:T(8,128)(2,1)}, bf16[1024,1536]{1,0:T(8,128)(2,1)}, bf16[1024,1024]{1,0:T(8,128)(2,1)}, bf16[1024,1024]{1,0:T(8,128)(2,1)}, bf16[1024,1024]{1,0:T(8,128)(2,1)}) custom-call(s32[1]{0:T(128)} %bitcast.1.refs_0_, bf16[256,1536]{1,0:T(8,128)(2,1)} %bitcast.158, bf16[256,1536]{1,0:T(8,128)(2,1)} %collective-permute-done.50.refs_2_, ...), custom_call_target="tpu_custom_call" | custom-call | flops 17600000000 | tf_op jit(solution)/shard_map/pallas_call | solution.py:655
  712.9 5.2 convolution_convert_fusion.4
  726.9 6.3 bitcast_dynamic-update-slice_fusion.4
  (528 shorter events, 352.2 us)
Async XLA Ops:
  16.1 31.3 %collective-permute-start.1 = (bf16[256,1536]{1,0:T(8,128)(2,1)S(1)}, bf16[256,1536]{1,0:T(8,128)(2,1)}, u32[]{:S(2)}, u32[]{:S(2)}) collective-permute-start(bf16[256,1536]{1,0:T(8,128)(2,1)S(1)} %fusion.84.refs_1_), channel_id=1, source_target_pairs={{0,4},{4,0},{8,12},{12,8},{1,5},{5,1},{9,13},{13,9},{2,6},{6,2},{1... | collective-permute-start | bytes 2359304 | tf_op jit(solution)/shard_map/ppermute | solution.py:25
  18.3 28.8 %collective-permute-start.2 = (bf16[64,1536]{1,0:T(8,128)(2,1)S(1)}, bf16[64,1536]{1,0:T(8,128)(2,1)S(1)}, u32[]{:S(2)}, u32[]{:S(2)}) collective-permute-start(bf16[64,1536]{1,0:T(8,128)(2,1)S(1)} %constant_dynamic-slice_fusion), channel_id=1, source_target_pairs={{0,8},{4,12},{8,0},{12,4},{1,9},{5,13},{9,1},{13,5},{2,10},{6,14},... | collective-permute-start | bytes 589832 | tf_op jit(solution)/shard_map/ppermute | solution.py:25
  62.0 46.2 %collective-permute-start.10 = (bf16[2,768,1024]{2,1,0:T(8,128)(2,1)}, bf16[2,768,1024]{2,1,0:T(8,128)(2,1)}, u32[]{:S(2)}, u32[]{:S(2)}) collective-permute-start(bf16[2,768,1024]{2,1,0:T(8,128)(2,1)} %refs_7_.11), channel_id=1, source_target_pairs={{0,16},{16,0},{1,17},{17,1},{2,18},{18,2},{3,19},{19,3},{4,20},{20... | collective-permute-start | bytes 9437192 | tf_op jit(solution)/shard_map/ppermute | solution.py:25
  62.0 46.2 %collective-permute-start.11 = (bf16[2,768,1024]{2,1,0:T(8,128)(2,1)}, bf16[2,768,1024]{2,1,0:T(8,128)(2,1)}, u32[]{:S(2)}, u32[]{:S(2)}) collective-permute-start(bf16[2,768,1024]{2,1,0:T(8,128)(2,1)} %refs_8_.11), channel_id=1, source_target_pairs={{0,16},{16,0},{1,17},{17,1},{2,18},{18,2},{3,19},{19,3},{4,20},{20... | collective-permute-start | bytes 9437192 | tf_op jit(solution)/shard_map/ppermute | solution.py:25
  62.5 45.7 %collective-permute-start.12 = (bf16[2,1024,768]{2,1,0:T(8,128)(2,1)}, bf16[2,1024,768]{2,1,0:T(8,128)(2,1)}, u32[]{:S(2)}, u32[]{:S(2)}) collective-permute-start(bf16[2,1024,768]{2,1,0:T(8,128)(2,1)} %refs_9_.3), channel_id=1, source_target_pairs={{0,16},{16,0},{1,17},{17,1},{2,18},{18,2},{3,19},{19,3},{4,20},{20... | collective-permute-start | bytes 9437192 | tf_op jit(solution)/shard_map/ppermute | solution.py:25
  191.0 300.7 %collective-permute-start.46 = (bf16[256,1536]{1,0:T(8,128)(2,1)}, bf16[256,1536]{1,0:T(8,128)(2,1)}, u32[]{:S(2)}, u32[]{:S(2)}) collective-permute-start(bf16[256,1536]{1,0:T(8,128)(2,1)} %get-tuple-element.198), channel_id=1, source_target_pairs={{0,4},{4,0},{8,12},{12,8},{1,5},{5,1},{9,13},{13,9},{2,6},{6,2},{1... | collective-permute-start | bytes 2359304 | tf_op jit(solution)/shard_map/ppermute | solution.py:25
  238.8 456.0 %collective-permute-start.50 = (bf16[256,1536]{1,0:T(8,128)(2,1)}, bf16[256,1536]{1,0:T(8,128)(2,1)}, u32[]{:S(2)}, u32[]{:S(2)}) collective-permute-start(bf16[256,1536]{1,0:T(8,128)(2,1)} %broadcast_add_fusion.1), channel_id=1, source_target_pairs={{0,4},{4,0},{8,12},{12,8},{1,5},{5,1},{9,13},{13,9},{2,6},{6,2},{1... | collective-permute-start | bytes 2359304 | tf_op jit(solution)/shard_map/ppermute | solution.py:25
  251.4 53.5 %collective-permute-start.18 = (bf16[64,1536]{1,0:T(8,128)(2,1)}, bf16[64,1536]{1,0:T(8,128)(2,1)}, u32[]{:S(2)}, u32[]{:S(2)}) collective-permute-start(bf16[64,1536]{1,0:T(8,128)(2,1)} %fusion.92.refs_9_), channel_id=1, source_target_pairs={{0,8},{4,12},{8,0},{12,4},{1,9},{5,13},{9,1},{13,5},{2,10},{6,14},... | collective-permute-start | bytes 589832 | tf_op jit(solution)/shard_map/ppermute | solution.py:25
  251.4 25.7 %collective-permute-start.16 = (bf16[64,1536]{1,0:T(8,128)(2,1)}, bf16[64,1536]{1,0:T(8,128)(2,1)}, u32[]{:S(2)}, u32[]{:S(2)}) collective-permute-start(bf16[64,1536]{1,0:T(8,128)(2,1)} %fusion.92.refs_9_), channel_id=1, source_target_pairs={{0,12},{4,8},{8,4},{12,0},{1,13},{5,9},{9,5},{13,1},{2,14},{6,10},... | collective-permute-start | bytes 589832 | tf_op jit(solution)/shard_map/ppermute | solution.py:25
  279.0 25.9 %all-to-all-start.12 = ((bf16[4,64,1536]{2,1,0:T(8,128)(2,1)}), bf16[4,64,1536]{2,1,0:T(8,128)(2,1)}, u32[]{:S(2)}, u32[]{:S(2)}) async-start(bf16[4,64,1536]{2,1,0:T(8,128)(2,1)} %broadcast_in_dim.88), calls=%async_computation.12 | async-start | bytes 1572864 | tf_op jit(solution)/shard_map/all_to_all | solution.py:35
  302.4 29.1 %collective-permute-start.17 = (bf16[256,1536]{1,0:T(8,128)(2,1)}, bf16[256,1536]{1,0:T(8,128)(2,1)}, u32[]{:S(2)}, u32[]{:S(2)}) collective-permute-start(bf16[256,1536]{1,0:T(8,128)(2,1)} %bitcast.28.refs_1_), channel_id=1, source_target_pairs={{0,4},{4,0},{8,12},{12,8},{1,5},{5,1},{9,13},{13,9},{2,6},{6,2},{1... | collective-permute-start | bytes 2359304 | tf_op jit(solution)/shard_map/ppermute | solution.py:25
  326.5 165.2 %collective-permute-start.43 = (bf16[256,1536]{1,0:T(8,128)(2,1)}, bf16[256,1536]{1,0:T(8,128)(2,1)}, u32[]{:S(2)}, u32[]{:S(2)}) collective-permute-start(bf16[256,1536]{1,0:T(8,128)(2,1)} %broadcast_add_fusion.3), channel_id=1, source_target_pairs={{0,4},{4,0},{8,12},{12,8},{1,5},{5,1},{9,13},{13,9},{2,6},{6,2},{1... | collective-permute-start | bytes 2359304 | tf_op jit(solution)/shard_map/ppermute | solution.py:25
  327.3 49.6 %all-to-all-start.13 = ((bf16[4,64,1536]{2,1,0:T(8,128)(2,1)}), bf16[4,64,1536]{2,1,0:T(8,128)(2,1)S(1)}, u32[]{:S(2)}, u32[]{:S(2)}) async-start(bf16[4,64,1536]{2,1,0:T(8,128)(2,1)} %bitcast.23), calls=%async_computation.13 | async-start | bytes 1572864 | tf_op jit(solution)/shard_map/all_to_all | solution.py:58
  369.1 31.4 %collective-permute-start.22 = (bf16[768,384]{1,0:T(8,128)(2,1)}, bf16[768,384]{1,0:T(8,128)(2,1)}, u32[]{:S(2)}, u32[]{:S(2)}) collective-permute-start(bf16[768,384]{1,0:T(8,128)(2,1)} %convolution_convert_fusion.13), channel_id=1, source_target_pairs={{0,16},{16,0},{1,17},{17,1},{2,18},{18,2},{3,19},{19,3},{4,20},{20... | collective-permute-start | bytes 1769480 | tf_op jit(solution)/shard_map/ppermute | solution.py:25
  400.6 25.5 %collective-permute-start.26 = (bf16[768,384]{1,0:T(8,128)(2,1)S(1)}, bf16[768,384]{1,0:T(8,128)(2,1)S(1)}, u32[]{:S(2)}, u32[]{:S(2)}) collective-permute-start(bf16[768,384]{1,0:T(8,128)(2,1)S(1)} %copy-done.59), channel_id=1, source_target_pairs={{0,16},{16,0},{1,17},{17,1},{2,18},{18,2},{3,19},{19,3},{4,20},{20... | collective-permute-start | bytes 1769480 | tf_op jit(solution)/shard_map/ppermute | solution.py:25
  404.3 52.1 %collective-permute-start.28 = (bf16[768,384]{1,0:T(8,128)(2,1)}, bf16[768,384]{1,0:T(8,128)(2,1)}, u32[]{:S(2)}, u32[]{:S(2)}) collective-permute-start(bf16[768,384]{1,0:T(8,128)(2,1)} %convolution_convert_fusion.7), channel_id=1, source_target_pairs={{0,16},{16,0},{1,17},{17,1},{2,18},{18,2},{3,19},{19,3},{4,20},{20... | collective-permute-start | bytes 1769480 | tf_op jit(solution)/shard_map/ppermute | solution.py:25
  426.0 26.6 %collective-permute-start.30 = (bf16[384,768]{1,0:T(8,128)(2,1)}, bf16[384,768]{1,0:T(8,128)(2,1)}, u32[]{:S(2)}, u32[]{:S(2)}) collective-permute-start(bf16[384,768]{1,0:T(8,128)(2,1)} %fusion.54), channel_id=1, source_target_pairs={{0,16},{16,0},{1,17},{17,1},{2,18},{18,2},{3,19},{19,3},{4,20},{20... | collective-permute-start | bytes 1769480 | tf_op jit(solution)/shard_map/ppermute | solution.py:25
  471.3 59.7 %collective-permute-start.20 = (bf16[64,1536]{1,0:T(8,128)(2,1)S(1)}, bf16[64,1536]{1,0:T(8,128)(2,1)S(1)}, u32[]{:S(2)}, u32[]{:S(2)}) collective-permute-start(bf16[64,1536]{1,0:T(8,128)(2,1)S(1)} %get-tuple-element.200.refs_13_), channel_id=1, source_target_pairs={{0,8},{4,12},{8,0},{12,4},{1,9},{5,13},{9,1},{13,5},{2,10},{6,14},... | collective-permute-start | bytes 589832 | tf_op jit(solution)/shard_map/ppermute | solution.py:25
  474.2 40.5 %collective-permute-start.21 = (bf16[64,1536]{1,0:T(8,128)(2,1)S(1)}, bf16[64,1536]{1,0:T(8,128)(2,1)S(1)}, u32[]{:S(2)}, u32[]{:S(2)}) collective-permute-start(bf16[64,1536]{1,0:T(8,128)(2,1)S(1)} %get-tuple-element.200.refs_13_), channel_id=1, source_target_pairs={{0,12},{4,8},{8,4},{12,0},{1,13},{5,9},{9,5},{13,1},{2,14},{6,10},... | collective-permute-start | bytes 589832 | tf_op jit(solution)/shard_map/ppermute | solution.py:25
  488.2 26.6 %all-to-all-start.20 = ((bf16[4,64,1536]{2,1,0:T(8,128)(2,1)}), bf16[4,64,1536]{2,1,0:T(8,128)(2,1)S(1)}, u32[]{:S(2)}, u32[]{:S(2)}) async-start(bf16[4,64,1536]{2,1,0:T(8,128)(2,1)} %broadcast_in_dim.93), calls=%async_computation.20 | async-start | bytes 1572864 | tf_op jit(solution)/shard_map/all_to_all | solution.py:35
  514.7 99.0 %collective-permute-start.49 = (bf16[768,1024]{1,0:T(8,128)(2,1)}, bf16[768,1024]{1,0:T(8,128)(2,1)}, u32[]{:S(2)}, u32[]{:S(2)}) collective-permute-start(bf16[768,1024]{1,0:T(8,128)(2,1)} %convolution_convert_fusion.5), channel_id=1, source_target_pairs={{0,16},{16,0},{1,17},{17,1},{2,18},{18,2},{3,19},{19,3},{4,20},{20... | collective-permute-start | bytes 4718600 | tf_op jit(solution)/shard_map/ppermute | solution.py:25
  528.3 32.8 %collective-permute-start.19 = (bf16[256,1536]{1,0:T(8,128)(2,1)S(1)}, bf16[256,1536]{1,0:T(8,128)(2,1)}, u32[]{:S(2)}, u32[]{:S(2)}) collective-permute-start(bf16[256,1536]{1,0:T(8,128)(2,1)S(1)} %bitcast.172), channel_id=1, source_target_pairs={{0,4},{4,0},{8,12},{12,8},{1,5},{5,1},{9,13},{13,9},{2,6},{6,2},{1... | collective-permute-start | bytes 2359304 | tf_op jit(solution)/shard_map/ppermute | solution.py:25
  533.1 28.0 %all-to-all-start.21 = ((bf16[4,64,1536]{2,1,0:T(8,128)(2,1)}), bf16[4,64,1536]{2,1,0:T(8,128)(2,1)}, u32[]{:S(2)}, u32[]{:S(2)}) async-start(bf16[4,64,1536]{2,1,0:T(8,128)(2,1)} %broadcast_in_dim.94), calls=%async_computation.21 | async-start | bytes 1572864 | tf_op jit(solution)/shard_map/all_to_all | solution.py:35
  555.3 62.1 %collective-permute-start.57 = (bf16[768,1024]{1,0:T(8,128)(2,1)}, bf16[768,1024]{1,0:T(8,128)(2,1)}, u32[]{:S(2)}, u32[]{:S(2)}) collective-permute-start(bf16[768,1024]{1,0:T(8,128)(2,1)} %convolution_convert_fusion.3), channel_id=1, source_target_pairs={{0,16},{16,0},{1,17},{17,1},{2,18},{18,2},{3,19},{19,3},{4,20},{20... | collective-permute-start | bytes 4718600 | tf_op jit(solution)/shard_map/ppermute | solution.py:25
  561.1 61.3 %collective-permute-start.59 = (bf16[1024,768]{1,0:T(8,128)(2,1)}, bf16[1024,768]{1,0:T(8,128)(2,1)}, u32[]{:S(2)}, u32[]{:S(2)}) collective-permute-start(bf16[1024,768]{1,0:T(8,128)(2,1)} %convolution_convert_fusion.1), channel_id=1, source_target_pairs={{0,16},{16,0},{1,17},{17,1},{2,18},{18,2},{3,19},{19,3},{4,20},{20... | collective-permute-start | bytes 4718600 | tf_op jit(solution)/shard_map/ppermute | solution.py:25
  597.9 32.2 %all-to-all-start.23 = ((bf16[4,64,1536]{2,1,0:T(8,128)(2,1)}), bf16[4,64,1536]{2,1,0:T(8,128)(2,1)S(1)}, u32[]{:S(2)}, u32[]{:S(2)}) async-start(bf16[4,64,1536]{2,1,0:T(8,128)(2,1)} %bitcast.36), calls=%async_computation.23 | async-start | bytes 1572864 | tf_op jit(solution)/shard_map/all_to_all | solution.py:58
  613.7 29.5 %collective-permute-start.25 = (bf16[768,384]{1,0:T(8,128)(2,1)}, bf16[768,384]{1,0:T(8,128)(2,1)}, u32[]{:S(2)}, u32[]{:S(2)}) collective-permute-start(bf16[768,384]{1,0:T(8,128)(2,1)} %convolution_convert_fusion.10), channel_id=1, source_target_pairs={{0,16},{16,0},{1,17},{17,1},{2,18},{18,2},{3,19},{19,3},{4,20},{20... | collective-permute-start | bytes 1769480 | tf_op jit(solution)/shard_map/ppermute | solution.py:25
  617.4 28.5 %collective-permute-start.27 = (bf16[768,384]{1,0:T(8,128)(2,1)}, bf16[768,384]{1,0:T(8,128)(2,1)}, u32[]{:S(2)}, u32[]{:S(2)}) collective-permute-start(bf16[768,384]{1,0:T(8,128)(2,1)} %convolution_convert_fusion.8), channel_id=1, source_target_pairs={{0,16},{16,0},{1,17},{17,1},{2,18},{18,2},{3,19},{19,3},{4,20},{20... | collective-permute-start | bytes 1769480 | tf_op jit(solution)/shard_map/ppermute | solution.py:25
  622.4 37.4 %collective-permute-start.29 = (bf16[768,384]{1,0:T(8,128)(2,1)}, bf16[768,384]{1,0:T(8,128)(2,1)}, u32[]{:S(2)}, u32[]{:S(2)}) collective-permute-start(bf16[768,384]{1,0:T(8,128)(2,1)} %convolution_convert_fusion.6), channel_id=1, source_target_pairs={{0,16},{16,0},{1,17},{17,1},{2,18},{18,2},{3,19},{19,3},{4,20},{20... | collective-permute-start | bytes 1769480 | tf_op jit(solution)/shard_map/ppermute | solution.py:25
  631.4 34.5 %all-to-all-start.27 = ((bf16[4,128,1536]{2,1,0:T(8,128)(2,1)}), bf16[4,128,1536]{2,1,0:T(8,128)(2,1)}, u32[]{:S(2)}, u32[]{:S(2)}) async-start(bf16[4,128,1536]{2,1,0:T(8,128)(2,1)} %broadcast_in_dim.220), calls=%async_computation.27 | async-start | bytes 3145728 | tf_op jit(solution)/shard_map/all_to_all | solution.py:35
  665.9 28.9 %collective-permute-start.53 = (bf16[256,1536]{1,0:T(8,128)(2,1)}, bf16[256,1536]{1,0:T(8,128)(2,1)}, u32[]{:S(2)}, u32[]{:S(2)}) collective-permute-start(bf16[256,1536]{1,0:T(8,128)(2,1)} %broadcast_add_fusion), channel_id=1, source_target_pairs={{0,4},{4,0},{8,12},{12,8},{1,5},{5,1},{9,13},{13,9},{2,6},{6,2},{1... | collective-permute-start | bytes 2359304 | tf_op jit(solution)/shard_map/ppermute | solution.py:25
  691.2 33.4 %all-to-all-start.24 = ((bf16[4,64,1536]{2,1,0:T(8,128)(2,1)}), bf16[4,64,1536]{2,1,0:T(8,128)(2,1)S(1)}, u32[]{:S(2)}, u32[]{:S(2)}) async-start(bf16[4,64,1536]{2,1,0:T(8,128)(2,1)} %broadcast_in_dim.96), calls=%async_computation.24 | async-start | bytes 1572864 | tf_op jit(solution)/shard_map/all_to_all | solution.py:35
  (168 other events, 2160.8 us)

commit v5 on v4

--- a/solution.py
+++ b/solution.py
@@ -25,8 +25,12 @@
     return lax.ppermute(x, axis, [(i, i ^ k) for i in range(n)])
 
 
-def after(x, token):
-    return x if token is None else x + (token[:1, :1].astype(f32) * 0.0).astype(x.dtype)
+def after(x, *tokens):
+    for token in tokens:
+        if token is not None:
+            first = lax.slice(token, (0,) * token.ndim, (1,) * token.ndim).reshape(1, 1)
+            x = x + (first.astype(f32) * 0.0).astype(x.dtype)
+    return x
 
 
 def gathered(block, axis):
@@ -35,22 +39,30 @@
     return lax.all_to_all(copies, axis, 0, 0, tiled=True).reshape((-1,) + block.shape[1:])
 
 
-def all_rows(shard, own=None, token=None):
-    shard = after(shard, token)
+def over_context(shard, own):
+    if lax.axis_size("context") != 4:
+        return (lax.all_gather(own, "context", tiled=True),)
+    return swap(own, "context", 1), swap(shard, "context", 2), swap(shard, "context", 3)
+
+
+def all_rows(shard, own=None, token=None, together=False):
     if own is None:
-        own = sent = gathered(shard, "tensor")
-    else:
-        sent = after(own, token)
+        own = gathered(shard, "tensor")
     if lax.axis_size("context") != 4:
-        return (lax.all_gather(sent, "context", tiled=True),)
-    far = [swap(shard, "context", k) for k in (2, 3)]
-    if token is None:
-        far = [gathered(x, "tensor") for x in far]
-    else:
-        block, width = shard.shape
-        both = gathered(jnp.concatenate(far, axis=0), "tensor").reshape(-1, 2, block, width)
-        far = [both]
-    return (own, swap(sent, "context", 1), *far)
+        return over_context(shard, own)
+    near, second, third = over_context(shard, own)
+    if together:
+        return all_rows_later(own, (near, second, third), token)
+    second, third = after(second, token), after(third, second)
+    blocks = [second] + [swap(second, "tensor", k) for k in range(1, lax.axis_size("tensor"))]
+    return (own, near, *blocks, gathered(third, "tensor"))
+
+
+def all_rows_later(own, sent, token):
+    near, second, third = sent
+    block, width = second.shape
+    both = gathered(after(jnp.concatenate([second, third], axis=0), token), "tensor")
+    return own, near, both.reshape(-1, 2, block, width)
 
 
 def received_sum(sends):
@@ -96,20 +108,28 @@
     return pl.ds(start if isinstance(start, int) else pl.multiple_of(start, rows), rows)
 
 
-def assemble(parts, whole_ref, z):
-    first, piece_len = 0, parts[0].shape[0]
+def assemble(parts, whole_ref, place_ref):
+    z, t = place_ref[0], place_ref[1]
+    piece, blocks_seen, piece_len = 0, 0, parts[0].shape[0]
     for part in parts:
-        if len(part.shape) == 2:
-            at = pl.multiple_of((z ^ first) * piece_len, piece_len)
-            whole_ref[pl.ds(at, piece_len), :] = part[...]
-            first += 1
+        if len(part.shape) == 4:
+            blocks, pieces, block = part.shape[:3]
+            for p in range(pieces):
+                for b in range(blocks):
+                    at = pl.multiple_of((z ^ (piece + p)) * piece_len + b * block, block)
+                    whole_ref[pl.ds(at, block), :] = part[b, p]
+            piece += pieces
             continue
-        blocks, pieces, block = part.shape[:3]
-        for p in range(pieces):
-            for b in range(blocks):
-                at = pl.multiple_of((z ^ (first + p)) * piece_len + b * block, block)
-                whole_ref[pl.ds(at, block), :] = part[b, p]
-        first += pieces
+        rows = part.shape[0]
+        if rows == piece_len:
+            at = pl.multiple_of((z ^ piece) * piece_len, piece_len)
+            piece += 1
+        else:
+            at = pl.multiple_of((z ^ piece) * piece_len + (t ^ blocks_seen) * rows, rows)
+            blocks_seen += 1
+            if blocks_seen * rows == piece_len:
+                piece, blocks_seen = piece + 1, 0
+        whole_ref[pl.ds(at, rows), :] = part[...]
 
 
 def triangle(rows, reverse):
@@ -225,7 +245,7 @@
     wo, to, wf, bias, start_ref = refs[8:13]
     refs = refs[13:]
     a_ref = refs.pop(0) if join else parts[0]
-    k_ref, v_ref, z_ref, terms_ref, send_ref, q_own, qa, qb, ka, kb, decay, acc = refs
+    q_ref, k_ref, v_ref, gate_ref, z_ref, terms_ref, send_ref, qa, qb, ka, kb, decay, acc = refs
     pair = pl.program_id(0)
     seq_len, half = a_ref.shape[0], a_ref.shape[1] // 2
     piece_start = pl.multiple_of(place_ref[0] * piece_len, piece_len)
@@ -233,7 +253,7 @@
     @pl.when(pair == 0)
     def _():
         if join:
-            assemble(parts, a_ref, place_ref[0])
+            assemble(parts, a_ref, place_ref)
         acc[...] = jnp.zeros_like(acc)
 
         def gates(i):
@@ -255,21 +275,21 @@
 
         each(seq_len // chunk_rows, split)
 
-    w_mine, w_theirs = lane_blocks((wk, wv)), lane_blocks((tk, tv))
+    w_mine, w_theirs = lane_blocks((wq, wk, wv, wg)), lane_blocks((tq, tk, tv, tg))
 
     def project(i):
         here = rows_at(i, chunk_rows)
         out = dot_nn(a_ref[here, :half], w_mine) + dot_nn(a_ref[here, half:], w_theirs)
-        k_ref[here, :] = out[:, :128].astype(bf16)
-        v_ref[here, :] = out[:, 128:].astype(bf16)
+        q_ref[here, :] = out[:, :128].astype(bf16)
+        k_ref[here, :] = out[:, 128:256].astype(bf16)
+        v_ref[here, :] = out[:, 256:384].astype(bf16)
+        gate_ref[here, :] = out[:, 384:]
 
     each(seq_len // chunk_rows, project)
     piece = pl.ds(piece_start, piece_len)
-    out = dot_nn(a_ref[piece, :half], lane_blocks((wq, wg))) + dot_nn(a_ref[piece, half:], lane_blocks((tq, tg)))
-    q_own[...] = out[:, :128].astype(bf16)
-    gate = jax.nn.sigmoid(out[:, 128:])
+    gate = jax.nn.sigmoid(gate_ref[piece, :])
     mix_keys(k_ref, terms_ref, pair, ka, kb)
-    mix_queries(q_own, terms_ref, piece_start, pair, qa, qb)
+    mix_queries(q_ref.at[piece, :], terms_ref, piece_start, pair, qa, qb)
     before = seq_len // 2
     for s in range(0, piece_len, query_rows(seq_len)):
         rows = query_rows(seq_len)
@@ -292,48 +312,14 @@
         send_ref[...] = acc[...].astype(bf16)
 
 
-def forward_rest_kernel(*refs):
-    a_ref, wq, wg, tq, tg, k_ref, v_ref, terms_ref, start_ref = refs[:9]
-    q_ref, gate_ref, o_ref, u_ref, qa, qb, ka, kb = refs[-8:]
-    pair = pl.program_id(0)
-    seq_len, half = a_ref.shape[0], a_ref.shape[1] // 2
-    rows = query_rows(seq_len)
-    w_mine, w_theirs = lane_blocks((wq, wg)), lane_blocks((tq, tg))
-
-    def project(i):
-        here = rows_at(i, chunk_rows)
-        out = dot_nn(a_ref[here, :half], w_mine) + dot_nn(a_ref[here, half:], w_theirs)
-        q_ref[here, :] = out[:, :128].astype(bf16)
-        gate_ref[here, :] = out[:, 128:]
-
-    each(seq_len // chunk_rows, project)
-    mix_keys(k_ref, terms_ref, pair, ka, kb)
-    mix_queries(q_ref, terms_ref, 0, pair, qa, qb)
-    lane = lax.broadcasted_iota(jnp.int32, (rows, pair_lanes), 1)
-
-    def body(start, first, width):
-        mask = live_mask(start_ref, start, first, width, rows)
-        here, keys = pl.ds(start, rows), pl.ds(first, width)
-        values = v_ref[keys, :]
-        out = []
-        for q_of, k_of in ((qa, ka), (qb, kb)):
-            p = probabilities(q_of[here, :], k_of[keys, :], mask).astype(bf16)
-            out.append(dot_nn(p, values))
-        o = jnp.where(lane < 64, out[0], out[1])
-        o_ref[here, :] = o
-        u_ref[here, :] = (o * jax.nn.sigmoid(gate_ref[here, :])).astype(bf16)
-
-    over_query_blocks(seq_len, rows, body)
-
-
 def backward_kernel(count_parts, piece_len, join, *refs):
     place_ref, parts, refs = refs[0], refs[1 : 1 + count_parts], list(refs[1 + count_parts :])
     mine, theirs, (wo, to, wf) = refs[:4], refs[4:8], refs[8:11]
-    q_ref, k_ref, v_ref, gate_ref, o_ref, z_ref, terms_ref, start_ref = refs[11:19]
-    refs = refs[19:]
+    q_ref, k_ref, v_ref, gate_ref, z_ref, terms_ref, start_ref = refs[11:18]
+    refs = refs[18:]
     y_ref = refs.pop(0) if join else parts[0]
-    dq_ref, dk_ref, dv_ref, dg_ref, dz_ref, send_ref = refs[:6]
-    qa, qb, ka, kb, dd, dka, dkb, dva, dcs, acc = refs[6:]
+    dq_ref, dk_ref, dv_ref, dg_ref, u_ref, dz_ref, send_ref = refs[:7]
+    qa, qb, ka, kb, dd, dus, dka, dkb, dva, dcs, acc = refs[7:]
     pair = pl.program_id(0)
     seq_len, half = y_ref.shape[0], y_ref.shape[1] // 2
     rows = query_rows(seq_len)
@@ -342,7 +328,7 @@
     @pl.when(pair == 0)
     def _():
         if join:
-            assemble(parts, y_ref, place_ref[0])
+            assemble(parts, y_ref, place_ref)
         acc[...] = jnp.zeros_like(acc)
         dcs[...] = jnp.zeros_like(dcs)
 
@@ -351,7 +337,7 @@
         du = dot_nt(y_ref[here, :half], wo[0]) + dot_nt(y_ref[here, half:], to[0])
         sig = jax.nn.sigmoid(gate_ref[here, :])
         dd[here, :] = (du * sig).astype(bf16)
-        dg_ref[here, :] = (du * o_ref[here, :] * sig * (1.0 - sig)).astype(bf16)
+        dus[here, :] = du * sig * (1.0 - sig)
 
     each(seq_len // chunk_rows, gates)
     mix_keys(k_ref, terms_ref, pair, ka, kb)
@@ -370,7 +356,7 @@
         here, keys = pl.ds(start, rows), pl.ds(first, width)
         values = v_ref[keys, :]
         d_rows = dd[here, :]
-        dq = []
+        dq, o = [], []
         for head, (q_of, k_of, dk_of) in enumerate(((qa, ka, dka), (qb, kb, dkb))):
             own_lanes = (lane < 64) if head == 0 else (lane >= 64)
             p = probabilities(q_of[here, :], k_of[keys, :], mask)
@@ -380,7 +366,12 @@
             ds = (p * (dp - delta)).astype(bf16)
             dq.append(dot_nn(ds, k_of[keys, :]))
             dk_of[keys, :] += dot_tn(ds, q_of[here, :])
-            dva[keys, :] += dot_tn(p.astype(bf16), d_mine)
+            low = p.astype(bf16)
+            dva[keys, :] += dot_tn(low, d_mine)
+            o.append(dot_nn(low, values))
+        o = jnp.where(lane < 64, o[0], o[1])
+        dg_ref[here, :] = (dus[here, :] * o).astype(bf16)
+        u_ref[here, :] = (o * jax.nn.sigmoid(gate_ref[here, :])).astype(bf16)
         dq_ref[here, :] = (jnp.where(lane < 64, dq[0], dq[1]) * 0.125).astype(bf16)
         dcs[here, :] += pick(dq[0][:, 67:68], dq[1][:, 3:4])
 
@@ -438,7 +429,8 @@
     return d_gate, (dm * (gt * sig)).astype(bf16)
 
 
-def ffn_backward_kernel(g_ref, gt_ref, up_ref, wg, wu, wd, tg, tu, td, send_ref, acc):
+def ffn_backward_kernel(g_ref, gt_ref, up_ref, wg, wu, wd, tg, tu, td, *refs):
+    send_ref, acc = refs[-2:]
     half = g_ref.shape[1] // 2
     dm = dot_nt(g_ref[:, :half], wd[0]) + dot_nt(g_ref[:, half:], td[0])
     d_gate, d_up = inner_grads(dm, gt_ref[...], up_ref[...])
@@ -455,17 +447,18 @@
         send_ref[...] = acc[...].astype(bf16)
 
 
-def ffn_inner_kernel(count_parts, *refs):
+def ffn_theirs_kernel(count_parts, *refs):
     place_ref, refs = refs[0], refs[1:]
     b_parts, g_parts = refs[:count_parts], refs[count_parts : 2 * count_parts]
     wg, wu, wd, tg, tu, td = refs[2 * count_parts : 2 * count_parts + 6]
-    b_ref, g_ref, m_ref, dgate_ref, dup_ref = refs[-5:]
+    b_ref, g_ref, m_ref, dgate_ref, dup_ref, gate_out, up_out, down_out, turned = refs[-9:]
     half = b_ref.shape[1] // 2
 
     @pl.when(pl.program_id(0) == 0)
     def _():
-        assemble(b_parts, b_ref, place_ref[0])
-        assemble(g_parts, g_ref, place_ref[0])
+        assemble(b_parts, b_ref, place_ref)
+        assemble(g_parts, g_ref, place_ref)
+        turned[...] = b_ref[:, half:].T
 
     def chunk(i):
         here = rows_at(i, chunk_rows)
@@ -477,6 +470,59 @@
         dgate_ref[here, :], dup_ref[here, :] = inner_grads(dm, gt, up)
 
     each(b_ref.shape[0] // chunk_rows, chunk)
+    gate_out[...] = dot_nn(turned[...], dgate_ref[...]).astype(bf16)
+    up_out[...] = dot_nn(turned[...], dup_ref[...]).astype(bf16)
+    down_out[...] = dot_tn(m_ref[...], g_ref[:, half:]).astype(bf16)
+
+
+def ffn_mine_kernel(b_ref, g_ref, m_ref, dgate_ref, dup_ref, gate_in, up_in, down_in, *refs):
+    gate_out, up_out, down_out, turned = refs[-4:]
+
+    @pl.when(pl.program_id(0) == 0)
+    def _():
+        turned[...] = b_ref[...].T
+
+    gate_out[0] = dot_nn(turned[...], dgate_ref[...]) + gate_in[...].astype(f32)
+    up_out[0] = dot_nn(turned[...], dup_ref[...]) + up_in[...].astype(f32)
+    down_out[0] = dot_tn(m_ref[...], g_ref[...]) + down_in[...].astype(f32)
+
+
+def attention_grads_kernel(steps, mine, *refs):
+    a_ref, dq, dk, dv, dg, dz, u_ref, y_ref = refs[:8]
+    received = refs[8:14] if mine else [None] * 6
+    acc, acc_out = refs[-2:]
+    outs = refs[-8:-2]
+    turned = a_ref[...].T
+    width = dq.shape[1]
+    parts = [dot_nn(turned, d[...]) for d in (dq, dk, dv, dg, dz)]
+    out = dot_tn(u_ref[...], y_ref[...])
+
+    def give(values):
+        for ref, value, more in zip(outs, values, received):
+            total = value if more is None else value + more[...].astype(f32)
+            if len(ref.shape) == 3:
+                ref[0] = total.astype(ref.dtype)
+            else:
+                ref[...] = total.astype(ref.dtype)
+
+    if steps == 1:
+        give([*parts, out])
+        return
+    step = pl.program_id(0)
+
+    @pl.when(step == 0)
+    def _():
+        acc[...] = jnp.zeros_like(acc)
+        acc_out[...] = jnp.zeros_like(acc_out)
+
+    for k, part in enumerate(parts):
+        acc[:, k * width : k * width + part.shape[1]] += part
+    acc_out[...] += out
+
+    @pl.when(step == steps - 1)
+    def _():
+        found = [acc[:, k * width : k * width + p.shape[1]] for k, p in enumerate(parts)]
+        give([*found, acc_out[...]])
 
 
 def fixed(shape, single=True):
@@ -528,9 +574,9 @@
     local_width = wo.shape[1]
     join = len(parts) > 1
     terms = (seq_len, pair_lanes)
-    outs = [shape((seq_len, local_width), bf16)] * 2 + [shape(terms, f32), shape(terms, bf16)]
-    outs += [shape((piece_len, width), bf16)]
-    specs = [lanes(seq_len)] * 2 + [fixed(terms, False)] * 2 + [fixed((piece_len, width), False)]
+    outs = [shape((seq_len, local_width), bf16)] * 3 + [shape((seq_len, local_width), f32)]
+    outs += [shape(terms, f32), shape(terms, bf16), shape((piece_len, width), bf16)]
+    specs = [lanes(seq_len)] * 4 + [fixed(terms, False)] * 2 + [fixed((piece_len, width), False)]
     if join:
         outs, specs = [shape((seq_len, width), bf16)] + outs, [fixed((seq_len, width))] + specs
     low, piece = pltpu.VMEM((seq_len, pair_lanes), bf16), pltpu.VMEM((piece_len, pair_lanes), bf16)
@@ -542,46 +588,25 @@
             in_specs=attention_specs(parts, layer, w4, t4, wo, to, seq_len, join)
             + [fixed(wf.shape), fixed(bias.shape), fixed(doc_start.shape)],
             out_specs=specs,
-            scratch_shapes=[piece] * 3 + [low] * 2 + [pltpu.VMEM(terms, f32), pltpu.VMEM((piece_len, width), f32)],
+            scratch_shapes=[piece] * 2 + [low] * 2 + [pltpu.VMEM(terms, f32), pltpu.VMEM((piece_len, width), f32)],
         ),
         out_shape=outs,
-        cost_estimate=cost(14),
+        cost_estimate=cost(19),
         compiler_params=pltpu.CompilerParams(vmem_limit_bytes=60 << 20),
     )(place, *parts, *w4, *t4, wo, to, wf, bias, doc_start)
     got = list(got)
     a = got.pop(0) if join else parts[0]
-    return a, got[:4], got[4]
-
-
-def forward_rest(a, layer, w4, t4, k, v, terms, doc_start, *tokens):
-    seq_len = a.shape[0]
-    local_width = k.shape[1]
-    low, high = shape((seq_len, local_width), bf16), shape((seq_len, local_width), f32)
-    weights = (w4[0], w4[3], t4[0], t4[3])
-    return pl.pallas_call(
-        forward_rest_kernel,
-        grid=(local_width // pair_lanes,),
-        in_specs=[fixed(a.shape)]
-        + [columns_of(w, layer, pair_lanes) for w in weights]
-        + [lanes_read(seq_len)] * 2
-        + [fixed(terms.shape), fixed(doc_start.shape)]
-        + token_specs(tokens),
-        out_specs=[lanes(seq_len)] * 4,
-        scratch_shapes=[pltpu.VMEM((seq_len, pair_lanes), bf16)] * 4,
-        out_shape=[low, high, high, low],
-        cost_estimate=cost(20),
-        compiler_params=pltpu.CompilerParams(vmem_limit_bytes=60 << 20),
-    )(a, *weights, k, v, terms, doc_start, *tokens)
+    return a, got[:6], got[6]
 
 
 def attention_backward(place, parts, layer, w4, t4, wo, to, wf, saved, doc_start, piece_len):
-    q, k, v, gate, o, z, terms = saved
+    q, k, v, gate, z, terms = saved
     seq_len, width = doc_start.shape[0], parts[0].shape[1]
     local_width = wo.shape[1]
     join = len(parts) > 1
-    outs = [shape((seq_len, local_width), bf16)] * 4 + [shape((seq_len, pair_lanes), bf16)]
+    outs = [shape((seq_len, local_width), bf16)] * 5 + [shape((seq_len, pair_lanes), bf16)]
     outs += [shape((piece_len, width), bf16)]
-    specs = [lanes(seq_len)] * 4 + [fixed((seq_len, pair_lanes), False), fixed((piece_len, width), False)]
+    specs = [lanes(seq_len)] * 5 + [fixed((seq_len, pair_lanes), False), fixed((piece_len, width), False)]
     if join:
         outs, specs = [shape((seq_len, width), bf16)] + outs, [fixed((seq_len, width))] + specs
     low, high = pltpu.VMEM((seq_len, pair_lanes), bf16), pltpu.VMEM((seq_len, pair_lanes), f32)
@@ -592,18 +617,18 @@
             grid=(local_width // pair_lanes,),
             in_specs=attention_specs(parts, layer, w4, t4, wo, to, seq_len, join)
             + [fixed(wf.shape)]
-            + [lanes_read(seq_len)] * 5
+            + [lanes_read(seq_len)] * 4
             + [fixed(z.shape), fixed(terms.shape), fixed(doc_start.shape)],
             out_specs=specs,
-            scratch_shapes=[low] * 5 + [high] * 4 + [pltpu.VMEM((piece_len, width), f32)],
+            scratch_shapes=[low] * 5 + [high] * 5 + [pltpu.VMEM((piece_len, width), f32)],
         ),
         out_shape=outs,
-        cost_estimate=cost(32),
+        cost_estimate=cost(33),
         compiler_params=pltpu.CompilerParams(vmem_limit_bytes=60 << 20),
-    )(place, *parts, *w4, *t4, wo, to, wf, q, k, v, gate, o, z, terms, doc_start)
+    )(place, *parts, *w4, *t4, wo, to, wf, q, k, v, gate, z, terms, doc_start)
     got = list(got)
     y = got.pop(0) if join else parts[0]
-    return y, got[:5], got[5]
+    return y, got[:6], got[6]
 
 
 def ffn_weights(layer, w3, t3):
@@ -634,38 +659,110 @@
     )(b, *w3, *t3)
 
 
-def ffn_backward(g, gt, up, layer, w3, t3):
+def ffn_backward(g, gt, up, layer, w3, t3, *tokens):
     rows, width = g.shape
     return pl.pallas_call(
         ffn_backward_kernel,
         grid=(gt.shape[1] // hidden_block,),
-        in_specs=[fixed(g.shape)] + [blocks_of(rows)] * 2 + ffn_weights(layer, w3, t3),
+        in_specs=[fixed(g.shape)] + [blocks_of(rows)] * 2 + ffn_weights(layer, w3, t3) + token_specs(tokens),
         out_specs=fixed((rows, width), False),
         scratch_shapes=[pltpu.VMEM((rows, width), f32)],
         out_shape=shape((rows, width), bf16),
         cost_estimate=cost(8),
         compiler_params=pltpu.CompilerParams(vmem_limit_bytes=40 << 20),
-    )(g, gt, up, *w3, *t3)
-
-
-def ffn_inner(place, b_parts, g_parts, layer, w3, t3, *tokens):
+    )(g, gt, up, *w3, *t3, *tokens)
+
+
+def ffn_theirs(place, b_parts, g_parts, layer, w3, t3, *tokens):
     width = b_parts[0].shape[1]
+    half = width // 2
     rows = sum(p.size for p in b_parts) // width
     inner = w3[2].shape[1]
+    wide = pl.BlockSpec((half, hidden_block), lambda p, *_: (0, p))
     return pl.pallas_call(
-        functools.partial(ffn_inner_kernel, len(b_parts)),
+        functools.partial(ffn_theirs_kernel, len(b_parts)),
         grid_spec=pltpu.PrefetchScalarGridSpec(
             num_scalar_prefetch=1,
             grid=(inner // hidden_block,),
             in_specs=[fixed(p.shape) for p in (*b_parts, *g_parts)]
             + ffn_weights(layer, w3, t3)
             + token_specs(tokens),
-            out_specs=[fixed((rows, width))] * 2 + [blocks_of(rows)] * 3,
+            out_specs=[fixed((rows, width))] * 2
+            + [blocks_of(rows)] * 3
+            + [wide, wide, pl.BlockSpec((hidden_block, half), lambda p, *_: (p, 0))],
+            scratch_shapes=[pltpu.VMEM((half, rows), bf16)],
         ),
-        out_shape=[shape((rows, width), bf16)] * 2 + [shape((rows, inner), bf16)] * 3,
-        cost_estimate=cost(16),
-        compiler_params=pltpu.CompilerParams(vmem_limit_bytes=56 << 20),
+        out_shape=[shape((rows, width), bf16)] * 2
+        + [shape((rows, inner), bf16)] * 3
+        + [shape((half, inner), bf16)] * 2
+        + [shape((inner, half), bf16)],
+        cost_estimate=cost(24),
+        compiler_params=pltpu.CompilerParams(vmem_limit_bytes=60 << 20),
     )(place, *b_parts, *g_parts, *w3, *t3, *tokens)
+
+
+def anywhere():
+    return pl.BlockSpec(memory_space=pl.ANY)
+
+
+def ffn_mine(layer, b, g, values, received, totals, *tokens):
+    rows, width = b.shape
+    half, inner = width // 2, values[0].shape[1]
+    wide = pl.BlockSpec((half, hidden_block), lambda p: (0, p))
+    tall = pl.BlockSpec((hidden_block, half), lambda p: (p, 0))
+    wide_out = pl.BlockSpec((1, half, hidden_block), lambda p: (layer, 0, p))
+    tall_out = pl.BlockSpec((1, hidden_block, half), lambda p: (layer, p, 0))
+    return pl.pallas_call(
+        ffn_mine_kernel,
+        grid=(inner // hidden_block,),
+        in_specs=[fixed((rows, half))] * 2
+        + [blocks_of(rows)] * 3
+        + [wide, wide, tall]
+        + [anywhere()] * 3
+        + token_specs(tokens),
+        out_specs=[wide_out, wide_out, tall_out],
+        out_shape=[shape(x.shape, x.dtype) for x in totals],
+        scratch_shapes=[pltpu.VMEM((half, rows), bf16)],
+        input_output_aliases={8: 0, 9: 1, 10: 2},
+        cost_estimate=cost(9),
+        compiler_params=pltpu.CompilerParams(vmem_limit_bytes=40 << 20),
+    )(b, g, *values, *received, *totals, *tokens)
+
+
+def attention_grads(layer, a, ds, dz, u, y, received=None, totals=None, tokens=()):
+    rows, width = a.shape
+    half, local_width = width // 2, u.shape[1]
+    part = min(rows, 1024)
+    steps = rows // part
+    mine = received is not None
+    side = 0 if mine else 1
+    features = pl.BlockSpec((part, half), lambda p: (p, side))
+    across = [pl.BlockSpec((part, x.shape[1]), lambda p: (p, 0)) for x in (*ds, dz, u)]
+    specs = [features, *across, features]
+    operands = [a, *ds, dz, u, y]
+    flat = [(half, local_width)] * 4 + [(half, pair_lanes), (local_width, half)]
+    if mine:
+        specs += [fixed(x) for x in flat] + [anywhere()] * 5
+        operands += [*received, *totals]
+        outs = [shape(x.shape, f32) for x in totals[:4]] + [shape(flat[4], f32), shape(totals[4].shape, f32)]
+        layered = pl.BlockSpec((1, half, local_width), lambda p: (layer, 0, 0))
+        out_specs = [layered] * 4 + [fixed(flat[4], False)]
+        out_specs += [pl.BlockSpec((1, local_width, half), lambda p: (layer, 0, 0))]
+        aliases = {14: 0, 15: 1, 16: 2, 17: 3, 18: 5}
+    else:
+        outs, out_specs, aliases = [shape(x, bf16) for x in flat], [fixed(x, False) for x in flat], {}
+    sizes = [(half, 4 * local_width + pair_lanes), (local_width, half)] if steps > 1 else [(8, 128)] * 2
+    return pl.pallas_call(
+        functools.partial(attention_grads_kernel, steps, mine),
+        grid=(steps,),
+        in_specs=specs + token_specs(tokens),
+        out_specs=out_specs,
+        out_shape=outs,
+        scratch_shapes=[pltpu.VMEM(x, f32) for x in sizes],
+        input_output_aliases=aliases,
+        cost_estimate=cost(7),
+        compiler_params=pltpu.CompilerParams(vmem_limit_bytes=60 << 20),
+    )(*operands, *tokens)
 
 
 def unset_kernel(*refs):
@@ -704,8 +801,8 @@
     block = piece_len // count_t
     seq_len = piece_len * count_z
     shared_rows = count_z == 4
-    place = z.reshape(1).astype(jnp.int32)
-    own_place = place if shared_rows else jnp.zeros((1,), jnp.int32)
+    place = jnp.stack([z, t]).astype(jnp.int32)
+    own_place = place if shared_rows else jnp.zeros((2,), jnp.int32)
 
     def features(x):
         return jnp.where(core == 0, x, jnp.concatenate([x[..., half:], x[..., :half]], axis=-1))
@@ -725,8 +822,7 @@
     gains = full(jnp.concatenate([gain_attn, gain_ffn], axis=0), 1).astype(f32)
     hidden_rows = features(hidden_in.reshape(piece_len, width)).astype(f32)
     first_a = (hidden_rows * inverse_rms(hidden_rows) * gains[0]).astype(bf16)
-    first_a = after(first_a, seg_all.reshape(1, seq_len))
-    a_parts = all_rows(own_block(first_a), first_a)
+    a_parts = all_rows(own_block(first_a), first_a, seg_all)
 
     w_forget_full = jnp.pad(full(w_forget, 1), ((0, 0), (0, 0), (0, pair_lanes - heads)))
     bias = jnp.pad(b_forget, ((0, 0), (0, pair_lanes - heads)))
@@ -739,38 +835,46 @@
     hidden = own_block(hidden_rows)
     saved = []
     cotangent_rows = features(cotangent.reshape(piece_len, width))
+    last = layers - 1
+    grad = own_block(cotangent_rows).astype(f32)
+    far = {}
     for layer in range(layers):
         gain_one, gain_two = gains[layer], gains[layers + layer]
         inverse_one = inverse_rms(hidden)
         if layer > 0:
-            a_parts = all_rows((hidden * inverse_one * gain_one).astype(bf16))
-        a, (k, v, forget, terms), sends = forward_own(
+            a_shard = (hidden * inverse_one * gain_one).astype(bf16)
+            a_parts = all_rows(after(a_shard, *far.get("b", ())))
+        a, (q, k, v, gate, forget, terms), sends = forward_own(
             place, a_parts, layer, w4, t4, w_attn_out, to, w_forget_full[layer],
             bias[layer : layer + 1], doc_start, piece_len,
         )
-        if shared_rows:
-            if layer == 0:
-                g_last = all_rows(own_block(cotangent_rows), cotangent_rows, a_parts[-1])
-            else:
-                before = saved[-1]
-                before["b_parts"] = all_rows(before["b_shard"], before["b"], a_parts[-1])
+        if shared_rows and layer == 0:
+            token = a_parts[-1]
+            far["g"] = over_context(after(own_block(cotangent_rows), token), after(cotangent_rows, token))
+        if shared_rows and layer == last:
+            g_last = all_rows_later(cotangent_rows, far["g"], a_parts[-1])
+            sends = after(sends, *g_last[1:])
         mixed = hidden + received_sum(sends)
         inverse_two = inverse_rms(mixed)
         b_shard = (mixed * inverse_two * gain_two).astype(bf16)
         b = gathered(b_shard, "tensor")
+        if shared_rows:
+            if layer > 0:
+                before = saved[-1]
+                before["b_parts"] = all_rows_later(before["b"], far["b"], b)
+            far["b"] = over_context(b_shard, b)
         gt, up, sends = ffn_forward(b, layer, w3, t3)
         saved.append(
-            dict(hidden=hidden, inverse_one=inverse_one, a=a, k=k, v=v, forget=forget, terms=terms, mixed=mixed,
-                 inverse_two=inverse_two, b=b, b_shard=b_shard, gt=gt, up=up)
+            dict(hidden=hidden, inverse_one=inverse_one, a=a, kept=(q, k, v, gate, forget, terms), mixed=mixed,
+                 inverse_two=inverse_two, b=b, gt=gt, up=up)
         )
-        if layer < layers - 1:
-            hidden = mixed + received_sum(sends)
+        if layer < last:
+            hidden = mixed + received_sum(after(sends, *far.get("b", ())[1:]))
 
     def finish(x):
         return features(gathered(x.astype(bf16), "tensor")).reshape(1, piece_len, width)
 
     last_sends = sends
-    grad = own_block(cotangent_rows).astype(f32)
     wide = shape((layers, half, local_width), f32)
     inner = shape((layers, half, w_gate.shape[2]), f32)
     results = list(
@@ -785,62 +889,73 @@
     for layer in reversed(range(layers)):
         s = saved[layer]
         gain_one, gain_two = gains[layer], gains[layers + layer]
-        g_shard = grad.astype(bf16)
-        g = cotangent_rows if layer == layers - 1 else gathered(g_shard, "tensor")
-        sends = ffn_backward(g, s["gt"], s["up"], layer, w3, t3)
+        if layer == last:
+            g = cotangent_rows
+        else:
+            g_shard = grad.astype(bf16)
+            g = gathered(g_shard, "tensor")
+            if shared_rows:
+                far["g"] = over_context(g_shard, g)
+        if not shared_rows:
+            sends = ffn_backward(g, s["gt"], s["up"], layer, w3, t3)
+        elif layer == last:
+            sends = ffn_backward(g, s["gt"], s["up"], layer, w3, t3, *far["b"][1:])
+            sends = after(sends, *[x["b_parts"][-1] for x in saved[:-1]])
+        else:
+            sends = ffn_backward(g, s["gt"], s["up"], layer, w3, t3)
+            sends = after(sends, *far["g"][1:])
         back, gain_grads[layers + layer] = norm_back(received_sum(sends), s["mixed"], s["inverse_two"], gain_two)
         grad_mixed = grad + back
         y_shard = grad_mixed.astype(bf16)
-        if layer == layers - 1:
-            rest_token = y_shard
-        y_parts = all_rows(y_shard)
-        q, gate, o, u = forward_rest(s["a"], layer, w4, t4, s["k"], s["v"], s["terms"], doc_start, rest_token)
-        y, (dq, dk, dv, dg, dz), sends = attention_backward(
-            place, y_parts, layer, w4, t4, w_attn_out, to, w_forget_full[layer],
-            (q, s["k"], s["v"], gate, o, s["forget"], s["terms"]), doc_start, piece_len,
+        sent_before = far["b" if layer == last else "g"] if shared_rows else ()
+        y_parts = all_rows(after(y_shard, *sent_before), together=layer < last)
+        y, (dq, dk, dv, dg, u, dz), sends = attention_backward(
+            place, y_parts, layer, w4, t4, w_attn_out, to, w_forget_full[layer], s["kept"], doc_start, piece_len,
         )
+        token = y_parts[-1]
         if not shared_rows:
-            b_parts, g_parts = (s["b"],), (g,)
-        elif layer == layers - 1:
-            b_parts, g_parts = all_rows(s["b_shard"], s["b"], y_parts[-1]), g_last
+            s["b_parts"], g_parts = (s["b"],), (g,)
+        elif layer == last:
+            s["b_parts"], g_parts = all_rows_later(s["b"], far["b"], token), g_last
+            sends = after(sends, s["b_parts"][-1])
         else:
-            b_parts, g_parts = s["b_parts"], all_rows(g_shard, g, y_parts[-1])
-        if layer == layers - 1:
-            output = finish(s["mixed"] + received_sum(after(last_sends, y_parts[-1])))
+            g_parts = all_rows_later(g, far["g"], token)
+            sends = after(sends, g_parts[-1])
         back, gain_grads[layer] = norm_back(received_sum(sends), s["hidden"], s["inverse_one"], gain_one)
         grad = grad_mixed + back
-        s.update(u=u, y=y, d=(dq, dk, dv, dg), dz=dz, b_parts=b_parts, g_parts=g_parts, y_shard=y_shard)
-
-    def weight_grads(layer, token):
+        s.update(u=u, y=y, d=(dq, dk, dv, dg), dz=dz, g_parts=g_parts, y_shard=y_shard)
+
+    def ffn_theirs_of(layer, *tokens):
         s = saved[layer]
-        b, g, m, d_gate, d_up = ffn_inner(own_place, s["b_parts"], s["g_parts"], layer, w3, t3, token)
-
-        def put(k, mine, theirs):
-            total = mine + other(theirs).astype(f32)
-            if k >= 5 and not shared_rows:
-                total = lax.psum(total, "context")
-            results[k] = lax.dynamic_update_slice_in_dim(results[k], total[None], layer, 0)
-
-        def by_rows(k, x, d):
-            put(k, dot_tn(x[:, :half], d), dot_tn(x[:, half:], d).astype(bf16))
-
-        def by_columns(k, x, d):
-            put(k, dot_tn(x, d[:, :half]), dot_tn(x, d[:, half:]).astype(bf16))
-
-        a = s["a"]
-        for k, d in enumerate(s["d"]):
-            by_rows(k, a, d)
-        by_columns(4, s["u"], s["y"])
-        by_rows(5, b, d_gate)
-        by_rows(6, b, d_up)
-        by_columns(7, m, g)
-        dzr = s["dz"][:, :heads]
-        bias_grad = jnp.sum(dzr.astype(f32), axis=0)
-        small[0][layer] = dot_tn(a[:, :half], dzr) + other(dot_tn(a[:, half:], dzr))
+        b, g, *values = ffn_theirs(own_place, s["b_parts"], s["g_parts"], layer, w3, t3, *tokens)
+        s.update(ffn=(b, g, values[:3]), ffn_received=[other(x) for x in values[3:]])
+
+    def ffn_mine_of(layer, *tokens):
+        s = saved[layer]
+        results[5:] = ffn_mine(layer, *s["ffn"], s["ffn_received"], results[5:], *tokens)
+
+    def attention_grads_of(layer, tokens=(), mine_tokens=()):
+        s = saved[layer]
+        parts = (s["a"], s["d"], s["dz"], s["u"], s["y"])
+        theirs = attention_grads(layer, *parts, tokens=tokens)
+        found = attention_grads(layer, *parts, [other(x) for x in theirs], results[:5], mine_tokens)
+        results[:5] = [*found[:4], found[5]]
+        bias_grad = jnp.sum(s["dz"].astype(f32), axis=0)[:heads]
+        small[0][layer] = found[4][:, :heads]
         small[1][layer] = bias_grad + other(bias_grad)
 
-    for layer in reversed(range(layers)):
-        weight_grads(layer, saved[max(layer - 1, 0)]["y_shard"])
+    for layer in reversed(range(1, layers)):
+        attention_grads_of(layer)
+        ffn_theirs_of(layer, saved[layer - 1]["y_shard"])
+    ffn_theirs_of(0)
+    token = saved[0]["ffn"][0]
+    for layer in reversed(range(1, layers)):
+        ffn_mine_of(layer, token)
+    attention_grads_of(0, (token,), saved[0]["ffn_received"])
+    ffn_mine_of(0)
+    if not shared_rows:
+        results[5:] = [lax.psum(x, "context") for x in results[5:]]
+    output = finish(saved[last]["mixed"] + received_sum(after(last_sends, grad)))
     grad_input = finish(grad)
     gain_total = sum_over(sum_over(jnp.stack(gain_grads), "tensor"), "context")
     gain_total = gain_total[:, :half] + other(gain_total[:, half:])

time: 751 us -> 699 us (0.931)
  matrix products: 110 us -> 0 us
  Pallas kernels: 198 us -> 237 us
  waiting for transfers between devices: 165 us -> 144 us
  local copies, waits for them, and re-layouts: 49.5 us -> 67.4 us
  between operations: 6.14 us -> 18.1 us
    dot_general x36 -> x0, matrix products: 110 us -> none  [dot_tn(): lax.dot_general(a, b, (((0,), (0,)), ((), ())), preferred_element_type=f32)]
    pallas_call x4 -> x8, Pallas kernels: 73 us -> 103 us  [the longest x2 48.1 us: ffn_theirs(): pl.pallas_call(functools.partial(ffn_theirs_kernel, len(b_parts)), grid_s...]
    all_to_all x20 -> x17, waiting for transfers between devices: 70.9 us -> 45 us  [gathered(): lax.all_to_all(copies, axis, 0, 0, tiled=True)]
    ppermute x61 -> x70, starting transfers between devices: 41.3 us -> 60.6 us  [swap(): return lax.ppermute(x, axis, [(i, i ^ k) for i in range(n)])]
    all_to_all x2 -> x3, blocking collectives: 23.1 us -> 40.9 us  [received_sum(): lax.all_to_all(sends.reshape(count, -1, sends.shape[1]), 'tensor', 0, 0,...]
    all_to_all x20 -> x17, starting transfers between devices: 84.5 us -> 67.4 us  [gathered(): lax.all_to_all(copies, axis, 0, 0, tiled=True)]
    slice x5 -> x24, local copies, waits for them, and re-layouts: 5.19 us -> 19.1 us  [after(): first = lax.slice(token, (0,) * token.ndim, (1,) * token.ndim).reshape(1, 1)]
    ppermute x61 -> x70, waiting for transfers between devices: 79.8 us -> 91.7 us  [swap(): return lax.ppermute(x, axis, [(i, i ^ k) for i in range(n)])]
  transfers between devices with their start and end apart: 87 -> 92, of which waited for: 27 -> 29; matrix products, arithmetic and copies ran while one was open for 23% -> 9% of each run, Pallas kernels for 24% -> 35%
where the time goes in v5:
time: 699 us; the launch traced here: 686 us
  Pallas kernels  237 us (34%)
  starting transfers between devices  149 us (21%)
  waiting for transfers between devices  144 us (21%)
  local copies, waits for them, and re-layouts  67.4 us (10%)
  blocking collectives  40.9 us (6%)
  other arithmetic  29.5 us (4%)
  between operations  18.1 us (3%)
    ppermute x70, waiting for transfers between devices, swap(): return lax.ppermute(x, axis, [(i, i ^ k) for i in range(n)])  91.7 us
    all_to_all x17, starting transfers between devices, gathered(): lax.all_to_all(copies, axis, 0, 0, tiled=True)  67.4 us
    pallas_call x2, Pallas kernels, attention_backward(): pl.pallas_call(functools.partial(backward_kernel, len(parts), piece_len,...  67.2 us
    ppermute x70, starting transfers between devices, swap(): return lax.ppermute(x, axis, [(i, i ^ k) for i in range(n)])  60.6 us
    pallas_call x2, Pallas kernels, ffn_theirs(): pl.pallas_call(functools.partial(ffn_theirs_kernel, len(b_parts)), grid_s...  48.1 us
    all_to_all x17, waiting for transfers between devices, gathered(): lax.all_to_all(copies, axis, 0, 0, tiled=True)  45 us
    all_to_all x3, blocking collectives, received_sum(): lax.all_to_all(sends.reshape(count, -1, sends.shape[1]), 'tensor', 0, 0,...  40.9 us
    pallas_call x2, Pallas kernels, forward_own(): pl.pallas_call(functools.partial(forward_own_kernel, len(parts), piece_le...  38.3 us
  transfers between devices with their start and end apart: 92, of which 29 were waited for; matrix products, arithmetic and copies ran while one was open for 9% of the time, Pallas kernels for 35%

profile of v5, /device:TPU:0, one launch (start us, length us, event | category | flops | bytes accessed | tf_op | source)
XLA Modules:
  0.0 685.9 jit_solution(16920387127162729171)
XLA Ops:
  18.1 14.7 %all-to-all-done = s32[4,1,256]{2,1,0:T(1,128)S(1)} async-done(((s32[4,1,256]{2,1,0:T(1,128)}), s32[4,1,256]{2,1,0:T(1,128)S(1)}, u32[]{:S(2)}, u32[]{:S(2)}) %all-to-all-start) | async-done | bytes 4128 | tf_op jit(solution)/shard_map/all_to_all | solution.py:39
  57.1 7.7 %all-to-all-done.1 = bf16[4,64,1536]{2,1,0:T(8,128)(2,1)} async-done(((bf16[4,64,1536]{2,1,0:T(8,128)(2,1)}), bf16[4,64,1536]{2,1,0:T(8,128)(2,1)}, u32[]{:S(2)}, u32[]{:S(2)}) %all-to-all-start.1) | async-done | bytes 786464 | tf_op jit(solution)/shard_map/all_to_all | solution.py:39
  64.8 19.2 %shard_map.254 = (bf16[1024,1536]{1,0:T(8,128)(2,1)}, bf16[1024,384]{1,0:T(8,128)(2,1)}, bf16[1024,384]{1,0:T(8,128)(2,1)}, bf16[1024,384]{1,0:T(8,128)(2,1)}, f...) custom-call(s32[2]{0:T(128)} %pad_add_fusion.refs_0_, ...), custom_call_target="tpu_custom_call" | custom-call | flops 20899999744 | tf_op jit(solution)/shard_map/pallas_call | solution.py:583
  84.0 14.9 %all_to_all.125 = bf16[4,64,1536]{2,1,0:T(8,128)(2,1)S(1)} all-to-all(bf16[4,64,1536]{2,1,0:T(8,128)(2,1)} %bitcast.116), channel_id=1, replica_groups=mesh['fsdp'=2,'context'=4,'tensor'=4] {'tensor'}, dimensions={0} | all-to-all | bytes 1572864 | tf_op jit(solution)/shard_map/all_to_all | solution.py:70
  106.9 6.6 collective-permute-done.17
  114.7 7.9 %collective-permute-done.16 = bf16[64,1536]{1,0:T(8,128)(2,1)S(1)} collective-permute-done((bf16[64,1536]{1,0:T(8,128)(2,1)S(1)}, bf16[64,1536]{1,0:T(8,128)(2,1)S(1)}, u32[]{:S(2)}, u32[]{:S(2)}) %collective-permute-start.16) | collective-permute-done | bytes 196640 | tf_op jit(solution)/shard_map/ppermute | solution.py:25
  123.9 6.8 shard_map.255
  157.8 5.4 collective-permute-done.20.refs_3_
  174.7 8.8 %collective-permute-done.25.refs_5_ = bf16[256,1536]{1,0:T(8,128)(2,1)} collective-permute-done((bf16[256,1536]{1,0:T(8,128)(2,1)S(1)}, bf16[256,1536]{1,0:T(8,128)(2,1)}, u32[]{:S(2)}, u32[]{:S(2)}) %collective-permute-start.25) | collective-permute-done | bytes 786464 | tf_op jit(solution)/shard_map/ppermute | solution.py:25
  189.2 9.1 %collective-permute-done.27 = bf16[64,1536]{1,0:T(8,128)(2,1)S(1)} collective-permute-done((bf16[64,1536]{1,0:T(8,128)(2,1)S(1)}, bf16[64,1536]{1,0:T(8,128)(2,1)S(1)}, u32[]{:S(2)}, u32[]{:S(2)}) %collective-permute-start.27) | collective-permute-done | bytes 196640 | tf_op jit(solution)/shard_map/ppermute | solution.py:25
  205.2 19.2 %shard_map.256 = (bf16[1024,1536]{1,0:T(8,128)(2,1)}, bf16[1024,384]{1,0:T(8,128)(2,1)}, bf16[1024,384]{1,0:T(8,128)(2,1)}, bf16[1024,384]{1,0:T(8,128)(2,1)}, f...) custom-call(s32[2]{0:T(128)} %pad_add_fusion.refs_0_, ...), custom_call_target="tpu_custom_call" | custom-call | flops 20899999744 | tf_op jit(solution)/shard_map/pallas_call | solution.py:583
  226.8 13.5 %all_to_all.126 = bf16[4,64,1536]{2,1,0:T(8,128)(2,1)S(1)} all-to-all(bf16[4,64,1536]{2,1,0:T(8,128)(2,1)S(1)} %bitcast.105), channel_id=1, replica_groups=mesh['fsdp'=2,'context'=4,'tensor'=4] {'tensor'}, dimensions={0} | all-to-all | bytes 1572864 | tf_op jit(solution)/shard_map/all_to_all | solution.py:70
  261.6 6.6 shard_map.257
  269.1 7.5 %shard_map.258 = bf16[256,1536]{1,0:T(8,128)(2,1)S(1)} custom-call(bf16[256,1536]{1,0:T(8,128)(2,1)S(1)} %get-tuple-element.248.g_ref.refs_4_, f32[256,1024]{1,0:T(8,128)S(1)} %get-tuple-element.110.gt_ref, f32[256,1024]{1,0:T(8,128)S(1)} %get-tuple-element.111.up_ref, bf16[2,768,1024]{2,1,0:T(8,128)(2,1)} %refs_7_.5, bf16[2,768,1024]{2,1,0:T(8,128)(2,1)} %refs_8_.9, ...), custom_call_target="tpu_custom_call" | custom-call | flops 8800000000 | tf_op jit(solution)/shard_map/pallas_call | solution.py:664
  303.0 8.0 %collective-permute-done.32.refs_3_ = bf16[64,1536]{1,0:T(8,128)(2,1)} collective-permute-done((bf16[64,1536]{1,0:T(8,128)(2,1)S(1)}, bf16[64,1536]{1,0:T(8,128)(2,1)}, u32[]{:S(2)}, u32[]{:S(2)}) %collective-permute-start.32) | collective-permute-done | bytes 196640 | tf_op jit(solution)/shard_map/ppermute | solution.py:25
  322.6 7.9 %all-to-all-done.13 = bf16[4,64,1536]{2,1,0:T(8,128)(2,1)} async-done(((bf16[4,64,1536]{2,1,0:T(8,128)(2,1)}), bf16[4,64,1536]{2,1,0:T(8,128)(2,1)}, u32[]{:S(2)}, u32[]{:S(2)}) %all-to-all-start.13) | async-done | bytes 786464 | tf_op jit(solution)/shard_map/all_to_all | solution.py:39
  339.2 33.5 %shard_map.259 = (bf16[1024,1536]{1,0:T(8,128)(2,1)}, bf16[1024,384]{1,0:T(8,128)(2,1)}, bf16[1024,384]{1,0:T(8,128)(2,1)}, bf16[1024,384]{1,0:T(8,128)(2,1)}, b...) custom-call(s32[2]{0:T(128)} %pad_add_fusion.refs_0_, ...), custom_call_target="tpu_custom_call" | custom-call | flops 36300001280 | tf_op jit(solution)/shard_map/pallas_call | solution.py:613
  375.7 12.5 %all_to_all.127 = bf16[4,64,1536]{2,1,0:T(8,128)(2,1)S(1)} all-to-all(bf16[4,64,1536]{2,1,0:T(8,128)(2,1)S(1)} %bitcast.101), channel_id=1, replica_groups=mesh['fsdp'=2,'context'=4,'tensor'=4] {'tensor'}, dimensions={0} | all-to-all | bytes 1572864 | tf_op jit(solution)/shard_map/all_to_all | solution.py:70
  396.5 5.2 collective-permute-done.38
  403.0 6.7 collective-permute-done.37
  411.1 7.6 %shard_map.260 = bf16[256,1536]{1,0:T(8,128)(2,1)S(1)} custom-call(bf16[256,1536]{1,0:T(8,128)(2,1)S(1)} %bitcast.95, f32[256,1024]{1,0:T(8,128)S(1)} %copy-done.17, f32[256,1024]{1,0:T(8,128)S(1)} %copy-done.19, bf16[2,768,1024]{2,1,0:T(8,128)(2,1)} %refs_7_.5, bf16[2,768,1024]{2,1,0:T(8,128)(2,1)} %refs_8_.9, bf16[2,1024,768]{2,1,0:T(8,128)(2,1)} %refs_9_.9, ...), custom_call_target="tpu_custom_call" | custom-call | flops 8800000000 | tf_op jit(solution)/shard_map/pallas_call | solution.py:664
  423.6 8.5 %shard_map.264 = (bf16[768,384]{1,0:T(8,128)(2,1)}, bf16[768,384]{1,0:T(8,128)(2,1)}, bf16[768,384]{1,0:T(8,128)(2,1)}, bf16[768,384]{1,0:T(8,128)(2,1)}, bf16[7...) custom-call(bf16[1024,1536]{1,0:T(8,128)(2,1)} %get-tuple-element.143.refs_0_, ...), custom_call_target="tpu_custom_call" | custom-call | flops 7699999744 | tf_op jit(solution)/shard_map/pallas_call | solution.py:755
  445.7 9.5 %shard_map.266 = (f32[2,768,384]{2,1,0:T(8,128)}, f32[2,768,384]{2,1,0:T(8,128)}, f32[2,768,384]{2,1,0:T(8,128)}, f32[2,768,384]{2,1,0:T(8,128)}, f32[768,128]{1,0:T(8,128)}, /*index=5*/f32[2,384,768]{2,1,0:T(8,128)}) custom-call(bf16[1024,1536]{1,0:T(8,128)(2,1)} %get-tuple-element.14, ...), custom_call_target="tpu_custom_call", output_to_operand_aliasing={{0}: (14, {}), {1}: (15, {}), {2}: (16, {}), {3}: (17, {}),... | custom-call | flops 7699999744 | tf_op jit(solution)/shard_map/pallas_call | solution.py:755
  464.8 11.4 %collective-permute-done.41 = bf16[64,1536]{1,0:T(8,128)(2,1)S(1)} collective-permute-done((bf16[64,1536]{1,0:T(8,128)(2,1)S(1)}, bf16[64,1536]{1,0:T(8,128)(2,1)S(1)}, u32[]{:S(2)}, u32[]{:S(2)}) %collective-permute-start.41) | collective-permute-done | bytes 196640 | tf_op jit(solution)/shard_map/ppermute | solution.py:25
  481.8 24.1 %shard_map.268 = (bf16[1024,1536]{1,0:T(8,128)(2,1)}, bf16[1024,1536]{1,0:T(8,128)(2,1)}, bf16[1024,1024]{1,0:T(8,128)(2,1)}, bf16[1024,1024]{1,0:T(8,128)(2,1)}...) custom-call(s32[2]{0:T(128)} %pad_add_fusion.refs_0_, ...), custom_call_target="tpu_custom_call" | custom-call | flops 26400000000 | tf_op jit(solution)/shard_map/pallas_call | solution.py:682
  513.4 33.6 %shard_map.261 = (bf16[1024,1536]{1,0:T(8,128)(2,1)}, bf16[1024,384]{1,0:T(8,128)(2,1)}, bf16[1024,384]{1,0:T(8,128)(2,1)}, bf16[1024,384]{1,0:T(8,128)(2,1)}, b...) custom-call(s32[2]{0:T(128)} %pad_add_fusion.refs_0_, ...), custom_call_target="tpu_custom_call" | custom-call | flops 36300001280 | tf_op jit(solution)/shard_map/pallas_call | solution.py:613
  557.8 24.0 %shard_map.262 = (bf16[1024,1536]{1,0:T(8,128)(2,1)}, bf16[1024,1536]{1,0:T(8,128)(2,1)}, bf16[1024,1024]{1,0:T(8,128)(2,1)}, bf16[1024,1024]{1,0:T(8,128)(2,1)}...) custom-call(s32[2]{0:T(128)} %pad_add_fusion.refs_0_, ...), custom_call_target="tpu_custom_call" | custom-call | flops 26400000000 | tf_op jit(solution)/shard_map/pallas_call | solution.py:682
  581.8 8.5 %shard_map.263 = (bf16[768,384]{1,0:T(8,128)(2,1)}, bf16[768,384]{1,0:T(8,128)(2,1)}, bf16[768,384]{1,0:T(8,128)(2,1)}, bf16[768,384]{1,0:T(8,128)(2,1)}, bf16[7...) custom-call(bf16[1024,1536]{1,0:T(8,128)(2,1)} %get-tuple-element.128.refs_0_, ...), custom_call_target="tpu_custom_call" | custom-call | flops 7699999744 | tf_op jit(solution)/shard_map/pallas_call | solution.py:755
  617.4 9.6 %shard_map.269 = (f32[2,768,1024]{2,1,0:T(8,128)}, f32[2,768,1024]{2,1,0:T(8,128)}, f32[2,1024,768]{2,1,0:T(8,128)}) custom-call(bf16[1024,1536]{1,0:T(8,128)(2,1)S(1)} %copy-done.1, bf16[1024,1536]{1,0:T(8,128)(2,1)} %get-tuple-element.182.g_ref, bf16[1024,1024]{1,0:T(8,128)(2,1)S(1)} %copy-done.3, ...), custom_call_target="tpu_custom_call", output_to_operand_aliasing={{0}: (8, {}), {1}: (9, {}), {2}: (10, {})} | custom-call | flops 9900000256 | tf_op jit(solution)/shard_map/pallas_call | solution.py:715
  637.3 9.1 %all-to-all-done.24 = bf16[4,64,1536]{2,1,0:T(8,128)(2,1)S(1)} async-done(((bf16[4,64,1536]{2,1,0:T(8,128)(2,1)}), bf16[4,64,1536]{2,1,0:T(8,128)(2,1)S(1)}, u32[]{:S(2)}, u32[]{:S(2)}) %all-to-all-start.24) | async-done | bytes 786464 | tf_op jit(solution)/shard_map/all_to_all | solution.py:39
  653.9 9.6 %shard_map.267 = (f32[2,768,384]{2,1,0:T(8,128)}, f32[2,768,384]{2,1,0:T(8,128)}, f32[2,768,384]{2,1,0:T(8,128)}, f32[2,768,384]{2,1,0:T(8,128)}, f32[768,128]{1,0:T(8,128)}, /*index=5*/f32[2,384,768]{2,1,0:T(8,128)}) custom-call(bf16[1024,1536]{1,0:T(8,128)(2,1)} %get-tuple-element.12, ...), custom_call_target="tpu_custom_call", output_to_operand_aliasing={{0}: (14, {}), {1}: (15, {}), {2}: (16, {}), {3}: (17, {}),... | custom-call | flops 7699999744 | tf_op jit(solution)/shard_map/pallas_call | solution.py:755
  672.9 9.4 %shard_map.270 = (f32[2,768,1024]{2,1,0:T(8,128)}, f32[2,768,1024]{2,1,0:T(8,128)}, f32[2,1024,768]{2,1,0:T(8,128)}) custom-call(bf16[1024,1536]{1,0:T(8,128)(2,1)S(1)} %copy-done, bf16[1024,1536]{1,0:T(8,128)(2,1)} %get-tuple-element.177.g_ref, bf16[1024,1024]{1,0:T(8,128)(2,1)S(1)} %copy-done.13, ...), custom_call_target="tpu_custom_call", output_to_operand_aliasing={{0}: (8, {}), {1}: (9, {}), {2}: (10, {})} | custom-call | flops 9900000256 | tf_op jit(solution)/shard_map/pallas_call | solution.py:715
  (446 shorter events, 281.3 us)
Async XLA Ops:
  5.2 28.8 %collective-permute-start.2 = (bf16[64,1536]{1,0:T(8,128)(2,1)S(1)}, bf16[64,1536]{1,0:T(8,128)(2,1)S(1)}, u32[]{:S(2)}, u32[]{:S(2)}) collective-permute-start(bf16[64,1536]{1,0:T(8,128)(2,1)S(1)} %constant_dynamic-slice_fusion), channel_id=1, source_target_pairs={{0,8},{4,12},{8,0},{12,4},{1,9},{5,13},{9,1},{13,5},{2,10},{6,14},... | collective-permute-start | bytes 589832 | tf_op jit(solution)/shard_map/ppermute | solution.py:25
  8.9 37.2 %collective-permute-start.1 = (bf16[256,1536]{1,0:T(8,128)(2,1)S(1)}, bf16[256,1536]{1,0:T(8,128)(2,1)}, u32[]{:S(2)}, u32[]{:S(2)}) collective-permute-start(bf16[256,1536]{1,0:T(8,128)(2,1)S(1)} %multiply_convert_fusion.refs_1_), channel_id=1, source_target_pairs={{0,4},{4,0},{8,12},{12,8},{1,5},{5,1},{9,13},{13,9},{2,6},{6,2},{1... | collective-permute-start | bytes 2359304 | tf_op jit(solution)/shard_map/ppermute | solution.py:25
  11.1 21.8 %all-to-all-start = ((s32[4,1,256]{2,1,0:T(1,128)}), s32[4,1,256]{2,1,0:T(1,128)S(1)}, u32[]{:S(2)}, u32[]{:S(2)}) async-start(s32[4,1,256]{2,1,0:T(1,128)} %broadcast_in_dim.39), calls=%async_computation | async-start | bytes 8192 | tf_op jit(solution)/shard_map/all_to_all | solution.py:39
  14.4 22.8 %collective-permute-start.12 = (bf16[2,768,6]{1,0,2:T(2,128)(2,1)S(1)}, bf16[2,768,6]{1,0,2:T(2,128)(2,1)S(1)}, u32[]{:S(2)}, u32[]{:S(2)}) collective-permute-start(bf16[2,768,6]{1,0,2:T(2,128)(2,1)S(1)} %copy-done.52), channel_id=1, source_target_pairs={{0,16},{16,0},{1,17},{17,1},{2,18},{18,2},{3,19},{19,3},{4,20},{20... | collective-permute-start | bytes 55304 | tf_op jit(solution)/shard_map/ppermute | solution.py:25
  14.4 23.7 %collective-permute-start.6 = (bf16[64,1536]{1,0:T(8,128)(2,1)S(1)}, bf16[64,1536]{1,0:T(8,128)(2,1)S(1)}, u32[]{:S(2)}, u32[]{:S(2)}) collective-permute-start(bf16[64,1536]{1,0:T(8,128)(2,1)S(1)} %constant_dynamic-slice_fusion), channel_id=1, source_target_pairs={{0,12},{4,8},{8,4},{12,0},{1,13},{5,9},{9,5},{13,1},{2,14},{6,10},... | collective-permute-start | bytes 589832 | tf_op jit(solution)/shard_map/ppermute | solution.py:25
  56.2 67.7 %collective-permute-start.13 = (bf16[2,768,1024]{2,1,0:T(8,128)(2,1)}, bf16[2,768,1024]{2,1,0:T(8,128)(2,1)}, u32[]{:S(2)}, u32[]{:S(2)}) collective-permute-start(bf16[2,768,1024]{2,1,0:T(8,128)(2,1)} %refs_7_.5), channel_id=1, source_target_pairs={{0,16},{16,0},{1,17},{17,1},{2,18},{18,2},{3,19},{19,3},{4,20},{20... | collective-permute-start | bytes 9437192 | tf_op jit(solution)/shard_map/ppermute | solution.py:25
  56.6 67.3 %collective-permute-start.14 = (bf16[2,768,1024]{2,1,0:T(8,128)(2,1)}, bf16[2,768,1024]{2,1,0:T(8,128)(2,1)}, u32[]{:S(2)}, u32[]{:S(2)}) collective-permute-start(bf16[2,768,1024]{2,1,0:T(8,128)(2,1)} %refs_8_.9), channel_id=1, source_target_pairs={{0,16},{16,0},{1,17},{17,1},{2,18},{18,2},{3,19},{19,3},{4,20},{20... | collective-permute-start | bytes 9437192 | tf_op jit(solution)/shard_map/ppermute | solution.py:25
  56.7 67.2 %collective-permute-start.15 = (bf16[2,1024,768]{2,1,0:T(8,128)(2,1)}, bf16[2,1024,768]{2,1,0:T(8,128)(2,1)}, u32[]{:S(2)}, u32[]{:S(2)}) collective-permute-start(bf16[2,1024,768]{2,1,0:T(8,128)(2,1)} %refs_9_.9), channel_id=1, source_target_pairs={{0,16},{16,0},{1,17},{17,1},{2,18},{18,2},{3,19},{19,3},{4,20},{20... | collective-permute-start | bytes 9437192 | tf_op jit(solution)/shard_map/ppermute | solution.py:25
  100.8 23.0 %all-to-all-start.3 = ((bf16[4,64,1536]{2,1,0:T(8,128)(2,1)}), bf16[4,64,1536]{2,1,0:T(8,128)(2,1)S(1)}, u32[]{:S(2)}, u32[]{:S(2)}) async-start(bf16[4,64,1536]{2,1,0:T(8,128)(2,1)} %broadcast_in_dim.42), calls=%async_computation.3 | async-start | bytes 1572864 | tf_op jit(solution)/shard_map/all_to_all | solution.py:39
  157.7 25.7 %collective-permute-start.25 = (bf16[256,1536]{1,0:T(8,128)(2,1)S(1)}, bf16[256,1536]{1,0:T(8,128)(2,1)}, u32[]{:S(2)}, u32[]{:S(2)}) collective-permute-start(bf16[256,1536]{1,0:T(8,128)(2,1)S(1)} %get-tuple-element.247), channel_id=1, source_target_pairs={{0,4},{4,0},{8,12},{12,8},{1,5},{5,1},{9,13},{13,9},{2,6},{6,2},{1... | collective-permute-start | bytes 2359304 | tf_op jit(solution)/shard_map/ppermute | solution.py:25
  167.3 20.6 %all-to-all-start.6 = ((bf16[4,64,1536]{2,1,0:T(8,128)(2,1)}), bf16[4,64,1536]{2,1,0:T(8,128)(2,1)S(1)}, u32[]{:S(2)}, u32[]{:S(2)}) async-start(bf16[4,64,1536]{2,1,0:T(8,128)(2,1)} %broadcast_in_dim.44), calls=%async_computation.6 | async-start | bytes 1572864 | tf_op jit(solution)/shard_map/all_to_all | solution.py:39
  171.0 34.2 %collective-permute-start.19 = (bf16[256,1536]{1,0:T(8,128)(2,1)}, bf16[256,1536]{1,0:T(8,128)(2,1)}, u32[]{:S(2)}, u32[]{:S(2)}) collective-permute-start(bf16[256,1536]{1,0:T(8,128)(2,1)} %bitcast.16.refs_1_), channel_id=1, source_target_pairs={{0,4},{4,0},{8,12},{12,8},{1,5},{5,1},{9,13},{13,9},{2,6},{6,2},{1... | collective-permute-start | bytes 2359304 | tf_op jit(solution)/shard_map/ppermute | solution.py:25
  172.8 25.4 %collective-permute-start.27 = (bf16[64,1536]{1,0:T(8,128)(2,1)S(1)}, bf16[64,1536]{1,0:T(8,128)(2,1)S(1)}, u32[]{:S(2)}, u32[]{:S(2)}) collective-permute-start(bf16[64,1536]{1,0:T(8,128)(2,1)S(1)} %dynamic-slice_add_fusion.1), channel_id=1, source_target_pairs={{0,12},{4,8},{8,4},{12,0},{1,13},{5,9},{9,5},{13,1},{2,14},{6,10},... | collective-permute-start | bytes 589832 | tf_op jit(solution)/shard_map/ppermute | solution.py:25
  174.2 25.6 %collective-permute-start.26 = (bf16[64,1536]{1,0:T(8,128)(2,1)S(1)}, bf16[64,1536]{1,0:T(8,128)(2,1)S(1)}, u32[]{:S(2)}, u32[]{:S(2)}) collective-permute-start(bf16[64,1536]{1,0:T(8,128)(2,1)S(1)} %dynamic-slice_add_fusion.1), channel_id=1, source_target_pairs={{0,8},{4,12},{8,0},{12,4},{1,9},{5,13},{9,1},{13,5},{2,10},{6,14},... | collective-permute-start | bytes 589832 | tf_op jit(solution)/shard_map/ppermute | solution.py:25
  201.1 23.3 %all-to-all-start.7 = ((bf16[4,128,1536]{2,1,0:T(8,128)(2,1)}), bf16[4,128,1536]{2,1,0:T(8,128)(2,1)S(1)}, u32[]{:S(2)}, u32[]{:S(2)}) async-start(bf16[4,128,1536]{2,1,0:T(8,128)(2,1)} %broadcast_in_dim.45), calls=%async_computation.7 | async-start | bytes 3145728 | tf_op jit(solution)/shard_map/all_to_all | solution.py:39
  245.1 23.9 %collective-permute-start.29 = (bf16[64,1536]{1,0:T(8,128)(2,1)S(1)}, bf16[64,1536]{1,0:T(8,128)(2,1)S(1)}, u32[]{:S(2)}, u32[]{:S(2)}) collective-permute-start(bf16[64,1536]{1,0:T(8,128)(2,1)S(1)} %multiply_convert_fusion.1), channel_id=1, source_target_pairs={{0,12},{4,8},{8,4},{12,0},{1,13},{5,9},{9,5},{13,1},{2,14},{6,10},... | collective-permute-start | bytes 589832 | tf_op jit(solution)/shard_map/ppermute | solution.py:25
  246.5 22.6 %collective-permute-start.28 = (bf16[64,1536]{1,0:T(8,128)(2,1)S(1)}, bf16[64,1536]{1,0:T(8,128)(2,1)S(1)}, u32[]{:S(2)}, u32[]{:S(2)}) collective-permute-start(bf16[64,1536]{1,0:T(8,128)(2,1)S(1)} %multiply_convert_fusion.1), channel_id=1, source_target_pairs={{0,8},{4,12},{8,0},{12,4},{1,9},{5,13},{9,1},{13,5},{2,10},{6,14},... | collective-permute-start | bytes 589832 | tf_op jit(solution)/shard_map/ppermute | solution.py:25
  253.3 32.5 %collective-permute-start.30 = (bf16[256,1536]{1,0:T(8,128)(2,1)S(1)}, bf16[256,1536]{1,0:T(8,128)(2,1)}, u32[]{:S(2)}, u32[]{:S(2)}) collective-permute-start(bf16[256,1536]{1,0:T(8,128)(2,1)S(1)} %bitcast.90), channel_id=1, source_target_pairs={{0,4},{4,0},{8,12},{12,8},{1,5},{5,1},{9,13},{13,9},{2,6},{6,2},{1... | collective-permute-start | bytes 2359304 | tf_op jit(solution)/shard_map/ppermute | solution.py:25
  333.6 39.1 %all-to-all-start.14 = ((bf16[4,128,1536]{2,1,0:T(8,128)(2,1)}), bf16[4,128,1536]{2,1,0:T(8,128)(2,1)}, u32[]{:S(2)}, u32[]{:S(2)}) async-start(bf16[4,128,1536]{2,1,0:T(8,128)(2,1)} %broadcast_in_dim.50), calls=%async_computation.14 | async-start | bytes 3145728 | tf_op jit(solution)/shard_map/all_to_all | solution.py:39
  411.0 25.7 %collective-permute-start.39 = (bf16[256,1536]{1,0:T(8,128)(2,1)S(1)}, bf16[256,1536]{1,0:T(8,128)(2,1)}, u32[]{:S(2)}, u32[]{:S(2)}) collective-permute-start(bf16[256,1536]{1,0:T(8,128)(2,1)S(1)} %bitcast.94), channel_id=1, source_target_pairs={{0,4},{4,0},{8,12},{12,8},{1,5},{5,1},{9,13},{13,9},{2,6},{6,2},{1... | collective-permute-start | bytes 2359304 | tf_op jit(solution)/shard_map/ppermute | solution.py:25
  440.6 35.6 %all-to-all-start.18 = ((bf16[4,64,1536]{2,1,0:T(8,128)(2,1)}), bf16[4,64,1536]{2,1,0:T(8,128)(2,1)}, u32[]{:S(2)}, u32[]{:S(2)}) async-start(bf16[4,64,1536]{2,1,0:T(8,128)(2,1)} %broadcast_in_dim.52), calls=%async_computation.18 | async-start | bytes 1572864 | tf_op jit(solution)/shard_map/all_to_all | solution.py:39
  477.6 28.9 %all-to-all-start.19 = ((bf16[4,128,1536]{2,1,0:T(8,128)(2,1)}), bf16[4,128,1536]{2,1,0:T(8,128)(2,1)S(1)}, u32[]{:S(2)}, u32[]{:S(2)}) async-start(bf16[4,128,1536]{2,1,0:T(8,128)(2,1)} %broadcast_in_dim.53), calls=%async_computation.19 | async-start | bytes 3145728 | tf_op jit(solution)/shard_map/all_to_all | solution.py:39
  481.8 31.7 %collective-permute-start.40 = (bf16[256,1536]{1,0:T(8,128)(2,1)}, bf16[256,1536]{1,0:T(8,128)(2,1)}, u32[]{:S(2)}, u32[]{:S(2)}) collective-permute-start(bf16[256,1536]{1,0:T(8,128)(2,1)} %bitcast.47.refs_1_), channel_id=1, source_target_pairs={{0,4},{4,0},{8,12},{12,8},{1,5},{5,1},{9,13},{13,9},{2,6},{6,2},{1... | collective-permute-start | bytes 2359304 | tf_op jit(solution)/shard_map/ppermute | solution.py:25
  505.9 106.0 %collective-permute-start.67 = (bf16[768,1024]{1,0:T(8,128)(2,1)}, bf16[768,1024]{1,0:T(8,128)(2,1)}, u32[]{:S(2)}, u32[]{:S(2)}) collective-permute-start(bf16[768,1024]{1,0:T(8,128)(2,1)} %get-tuple-element.186), channel_id=1, source_target_pairs={{0,16},{16,0},{1,17},{17,1},{2,18},{18,2},{3,19},{19,3},{4,20},{20... | collective-permute-start | bytes 4718600 | tf_op jit(solution)/shard_map/ppermute | solution.py:25
  506.0 106.1 %collective-permute-start.68 = (bf16[768,1024]{1,0:T(8,128)(2,1)}, bf16[768,1024]{1,0:T(8,128)(2,1)}, u32[]{:S(2)}, u32[]{:S(2)}) collective-permute-start(bf16[768,1024]{1,0:T(8,128)(2,1)} %get-tuple-element.187), channel_id=1, source_target_pairs={{0,16},{16,0},{1,17},{17,1},{2,18},{18,2},{3,19},{19,3},{4,20},{20... | collective-permute-start | bytes 4718600 | tf_op jit(solution)/shard_map/ppermute | solution.py:25
  509.0 40.9 %all-to-all-start.20 = ((bf16[4,128,1536]{2,1,0:T(8,128)(2,1)}), bf16[4,128,1536]{2,1,0:T(8,128)(2,1)S(1)}, u32[]{:S(2)}, u32[]{:S(2)}) async-start(bf16[4,128,1536]{2,1,0:T(8,128)(2,1)} %broadcast_in_dim.54), calls=%async_computation.20 | async-start | bytes 3145728 | tf_op jit(solution)/shard_map/all_to_all | solution.py:39
  553.2 37.1 %all-to-all-start.21 = ((bf16[4,64,1536]{2,1,0:T(8,128)(2,1)}), bf16[4,64,1536]{2,1,0:T(8,128)(2,1)S(1)}, u32[]{:S(2)}, u32[]{:S(2)}) async-start(bf16[4,64,1536]{2,1,0:T(8,128)(2,1)} %bitcast.52), calls=%async_computation.21 | async-start | bytes 1572864 | tf_op jit(solution)/shard_map/all_to_all | solution.py:70
  606.2 23.1 %all-to-all-start.22 = ((bf16[4,64,1536]{2,1,0:T(8,128)(2,1)}), bf16[4,64,1536]{2,1,0:T(8,128)(2,1)}, u32[]{:S(2)}, u32[]{:S(2)}) async-start(bf16[4,64,1536]{2,1,0:T(8,128)(2,1)} %bitcast.99), calls=%async_computation.22 | async-start | bytes 1572864 | tf_op jit(solution)/shard_map/all_to_all | solution.py:70
  611.9 40.8 %collective-permute-start.55 = (bf16[768,1024]{1,0:T(8,128)(2,1)}, bf16[768,1024]{1,0:T(8,128)(2,1)}, u32[]{:S(2)}, u32[]{:S(2)}) collective-permute-start(bf16[768,1024]{1,0:T(8,128)(2,1)} %get-tuple-element.167), channel_id=1, source_target_pairs={{0,16},{16,0},{1,17},{17,1},{2,18},{18,2},{3,19},{19,3},{4,20},{20... | collective-permute-start | bytes 4718600 | tf_op jit(solution)/shard_map/ppermute | solution.py:25
  612.1 40.6 %collective-permute-start.56 = (bf16[768,1024]{1,0:T(8,128)(2,1)}, bf16[768,1024]{1,0:T(8,128)(2,1)}, u32[]{:S(2)}, u32[]{:S(2)}) collective-permute-start(bf16[768,1024]{1,0:T(8,128)(2,1)} %get-tuple-element.168), channel_id=1, source_target_pairs={{0,16},{16,0},{1,17},{17,1},{2,18},{18,2},{3,19},{19,3},{4,20},{20... | collective-permute-start | bytes 4718600 | tf_op jit(solution)/shard_map/ppermute | solution.py:25
  626.9 25.8 %collective-permute-start.57 = (bf16[1024,768]{1,0:T(8,128)(2,1)}, bf16[1024,768]{1,0:T(8,128)(2,1)S(1)}, u32[]{:S(2)}, u32[]{:S(2)}) collective-permute-start(bf16[1024,768]{1,0:T(8,128)(2,1)} %get-tuple-element.169), channel_id=1, source_target_pairs={{0,16},{16,0},{1,17},{17,1},{2,18},{18,2},{3,19},{19,3},{4,20},{20... | collective-permute-start | bytes 4718600 | tf_op jit(solution)/shard_map/ppermute | solution.py:25
  647.4 35.0 %all-to-all-start.23 = ((bf16[4,64,1536]{2,1,0:T(8,128)(2,1)}), bf16[4,64,1536]{2,1,0:T(8,128)(2,1)}, u32[]{:S(2)}, u32[]{:S(2)}) async-start(bf16[4,64,1536]{2,1,0:T(8,128)(2,1)} %broadcast_in_dim.55), calls=%async_computation.23 | async-start | bytes 1572864 | tf_op jit(solution)/shard_map/all_to_all | solution.py:39
  (132 other events, 1729.6 us)

commit v6 on v5

--- a/solution.py
+++ b/solution.py
@@ -25,12 +25,21 @@
     return lax.ppermute(x, axis, [(i, i ^ k) for i in range(n)])
 
 
+def pass_kernel(*refs):
+    pass
+
+
 def after(x, *tokens):
-    for token in tokens:
-        if token is not None:
-            first = lax.slice(token, (0,) * token.ndim, (1,) * token.ndim).reshape(1, 1)
-            x = x + (first.astype(f32) * 0.0).astype(x.dtype)
-    return x
+    if not tokens:
+        return x
+    anywhere = pl.BlockSpec(memory_space=pl.ANY)
+    return pl.pallas_call(
+        pass_kernel,
+        in_specs=[anywhere] * (1 + len(tokens)),
+        out_specs=anywhere,
+        out_shape=jax.ShapeDtypeStruct(x.shape, x.dtype),
+        input_output_aliases={0: 0},
+    )(x, *tokens)
 
 
 def gathered(block, axis):
@@ -39,43 +48,39 @@
     return lax.all_to_all(copies, axis, 0, 0, tiled=True).reshape((-1,) + block.shape[1:])
 
 
-def over_context(shard, own):
-    if lax.axis_size("context") != 4:
-        return (lax.all_gather(own, "context", tiled=True),)
-    return swap(own, "context", 1), swap(shard, "context", 2), swap(shard, "context", 3)
+def near_rows(own):
+    return swap(own, "context", 1)
+
+
+def far_blocks(shard):
+    return swap(shard, "context", 2), swap(shard, "context", 3)
+
+
+def far_rows(blocks, *tokens):
+    block, width = blocks[0].shape
+    return gathered(after(jnp.concatenate(blocks, axis=0), *tokens), "tensor").reshape(-1, 2, block, width)
 
 
 def all_rows(shard, own=None, token=None, together=False):
     if own is None:
         own = gathered(shard, "tensor")
     if lax.axis_size("context") != 4:
-        return over_context(shard, own)
-    near, second, third = over_context(shard, own)
+        return (lax.all_gather(own, "context", tiled=True),), ()
+    second, third = far_blocks(shard)
+    near = near_rows(own)
     if together:
-        return all_rows_later(own, (near, second, third), token)
-    second, third = after(second, token), after(third, second)
+        return (own, near, far_rows((second, third))), (second, third)
+    if token is not None:
+        second = after(second, token)
+    third = after(third, second)
     blocks = [second] + [swap(second, "tensor", k) for k in range(1, lax.axis_size("tensor"))]
-    return (own, near, *blocks, gathered(third, "tensor"))
-
-
-def all_rows_later(own, sent, token):
-    near, second, third = sent
-    block, width = second.shape
-    both = gathered(after(jnp.concatenate([second, third], axis=0), token), "tensor")
-    return own, near, both.reshape(-1, 2, block, width)
+    return (own, near, *blocks, gathered(third, "tensor")), (second, third)
 
 
 def received_sum(sends):
     count = lax.axis_size("tensor")
     got = lax.all_to_all(sends.reshape(count, -1, sends.shape[1]), "tensor", 0, 0, tiled=True)
     return jnp.sum(got.astype(f32), axis=0)
-
-
-def sum_over(x, axis):
-    total = x
-    for k in range(1, lax.axis_size(axis)):
-        total = total + swap(x, axis, k)
-    return total
 
 
 def dot_nt(a, b):
@@ -765,13 +770,9 @@
     )(*operands, *tokens)
 
 
-def unset_kernel(*refs):
-    pass
-
-
 def unset(*like):
     return pl.pallas_call(
-        unset_kernel,
+        pass_kernel,
         out_specs=[pl.BlockSpec(memory_space=pl.ANY) for _ in like],
         out_shape=list(like),
     )()
@@ -822,7 +823,7 @@
     gains = full(jnp.concatenate([gain_attn, gain_ffn], axis=0), 1).astype(f32)
     hidden_rows = features(hidden_in.reshape(piece_len, width)).astype(f32)
     first_a = (hidden_rows * inverse_rms(hidden_rows) * gains[0]).astype(bf16)
-    a_parts = all_rows(own_block(first_a), first_a, seg_all)
+    a_parts, _ = all_rows(own_block(first_a), first_a, seg_all)
 
     w_forget_full = jnp.pad(full(w_forget, 1), ((0, 0), (0, 0), (0, pair_lanes - heads)))
     bias = jnp.pad(b_forget, ((0, 0), (0, pair_lanes - heads)))
@@ -837,39 +838,40 @@
     cotangent_rows = features(cotangent.reshape(piece_len, width))
     last = layers - 1
     grad = own_block(cotangent_rows).astype(f32)
-    far = {}
     for layer in range(layers):
         gain_one, gain_two = gains[layer], gains[layers + layer]
         inverse_one = inverse_rms(hidden)
         if layer > 0:
-            a_shard = (hidden * inverse_one * gain_one).astype(bf16)
-            a_parts = all_rows(after(a_shard, *far.get("b", ())))
+            a_parts, _ = all_rows((hidden * inverse_one * gain_one).astype(bf16))
         a, (q, k, v, gate, forget, terms), sends = forward_own(
             place, a_parts, layer, w4, t4, w_attn_out, to, w_forget_full[layer],
             bias[layer : layer + 1], doc_start, piece_len,
         )
+        token = a_parts[-1]
         if shared_rows and layer == 0:
-            token = a_parts[-1]
-            far["g"] = over_context(after(own_block(cotangent_rows), token), after(cotangent_rows, token))
+            g_far = far_blocks(after(own_block(cotangent_rows), token))
+            sends = after(sends, *g_far)
         if shared_rows and layer == last:
-            g_last = all_rows_later(cotangent_rows, far["g"], a_parts[-1])
-            sends = after(sends, *g_last[1:])
+            g_last = far_rows(g_far, token)
+            tokens = [g_last]
+            for s in saved:
+                s["b_far"] = far_blocks(after(s["b_shard"], token))
+                tokens += s["b_far"]
+            sends = after(sends, *tokens)
         mixed = hidden + received_sum(sends)
         inverse_two = inverse_rms(mixed)
         b_shard = (mixed * inverse_two * gain_two).astype(bf16)
         b = gathered(b_shard, "tensor")
-        if shared_rows:
-            if layer > 0:
-                before = saved[-1]
-                before["b_parts"] = all_rows_later(before["b"], far["b"], b)
-            far["b"] = over_context(b_shard, b)
+        if shared_rows and layer == last:
+            for s in saved:
+                s["b_rows"] = far_rows(s["b_far"], b)
         gt, up, sends = ffn_forward(b, layer, w3, t3)
         saved.append(
             dict(hidden=hidden, inverse_one=inverse_one, a=a, kept=(q, k, v, gate, forget, terms), mixed=mixed,
-                 inverse_two=inverse_two, b=b, gt=gt, up=up)
+                 inverse_two=inverse_two, b=b, b_shard=b_shard, gt=gt, up=up)
         )
         if layer < last:
-            hidden = mixed + received_sum(after(sends, *far.get("b", ())[1:]))
+            hidden = mixed + received_sum(sends)
 
     def finish(x):
         return features(gathered(x.astype(bf16), "tensor")).reshape(1, piece_len, width)
@@ -889,41 +891,49 @@
     for layer in reversed(range(layers)):
         s = saved[layer]
         gain_one, gain_two = gains[layer], gains[layers + layer]
+        before_y, tokens = (), ()
         if layer == last:
             g = cotangent_rows
+            if shared_rows:
+                tokens = s["b_far"] = far_blocks(s["b_shard"])
         else:
             g_shard = grad.astype(bf16)
             g = gathered(g_shard, "tensor")
             if shared_rows:
-                far["g"] = over_context(g_shard, g)
-        if not shared_rows:
-            sends = ffn_backward(g, s["gt"], s["up"], layer, w3, t3)
-        elif layer == last:
-            sends = ffn_backward(g, s["gt"], s["up"], layer, w3, t3, *far["b"][1:])
-            sends = after(sends, *[x["b_parts"][-1] for x in saved[:-1]])
-        else:
-            sends = ffn_backward(g, s["gt"], s["up"], layer, w3, t3)
-            sends = after(sends, *far["g"][1:])
+                before_y = g_far = far_blocks(g_shard)
+        sends = ffn_backward(g, s["gt"], s["up"], layer, w3, t3, *tokens)
+        if shared_rows and layer == last:
+            sends = after(sends, *[x["b_rows"] for x in saved[:-1]])
         back, gain_grads[layers + layer] = norm_back(received_sum(sends), s["mixed"], s["inverse_two"], gain_two)
         grad_mixed = grad + back
-        y_shard = grad_mixed.astype(bf16)
-        sent_before = far["b" if layer == last else "g"] if shared_rows else ()
-        y_parts = all_rows(after(y_shard, *sent_before), together=layer < last)
+        y_parts, y_far = all_rows(after(grad_mixed.astype(bf16), *before_y), together=layer < last)
         y, (dq, dk, dv, dg, u, dz), sends = attention_backward(
             place, y_parts, layer, w4, t4, w_attn_out, to, w_forget_full[layer], s["kept"], doc_start, piece_len,
         )
         token = y_parts[-1]
+        if layer == last:
+            block_sum = own_block(last_sends).astype(f32) + s["mixed"]
+            with_rows = lax.dynamic_update_slice_in_dim(last_sends, block_sum.astype(bf16), t * block, 0)
+            output = lax.psum(after(with_rows, token), "tensor")
         if not shared_rows:
-            s["b_parts"], g_parts = (s["b"],), (g,)
+            s["b_parts"], s["g_parts"] = (s["b"],), (g,)
         elif layer == last:
-            s["b_parts"], g_parts = all_rows_later(s["b"], far["b"], token), g_last
-            sends = after(sends, s["b_parts"][-1])
+            s["b_rows"] = far_rows(s["b_far"], token)
+            g_near = near_rows(after(g, token))
+            s["g_parts"] = (g, g_near, g_last)
+            tokens = [s["b_rows"], g_near]
+            for x in saved:
+                x["b_near"] = near_rows(after(x["b"], token))
+                tokens.append(x["b_near"])
+            sends = after(sends, *tokens)
         else:
-            g_parts = all_rows_later(g, far["g"], token)
-            sends = after(sends, g_parts[-1])
+            s["g_parts"] = (g, near_rows(after(g, token)), far_rows(g_far, token))
+            sends = after(sends, *s["g_parts"][1:])
+        if shared_rows:
+            s["b_parts"] = (s["b"], s["b_near"], s["b_rows"])
         back, gain_grads[layer] = norm_back(received_sum(sends), s["hidden"], s["inverse_one"], gain_one)
         grad = grad_mixed + back
-        s.update(u=u, y=y, d=(dq, dk, dv, dg), dz=dz, g_parts=g_parts, y_shard=y_shard)
+        s.update(u=u, y=y, d=(dq, dk, dv, dg), dz=dz, y_far=y_far)
 
     def ffn_theirs_of(layer, *tokens):
         s = saved[layer]
@@ -944,21 +954,20 @@
         small[0][layer] = found[4][:, :heads]
         small[1][layer] = bias_grad + other(bias_grad)
 
+    for layer in reversed(range(layers)):
+        ffn_theirs_of(layer, *(saved[layer - 1]["y_far"] if layer > 0 else ()))
+    tokens = (saved[0]["ffn"][0], grad)
     for layer in reversed(range(1, layers)):
-        attention_grads_of(layer)
-        ffn_theirs_of(layer, saved[layer - 1]["y_shard"])
-    ffn_theirs_of(0)
-    token = saved[0]["ffn"][0]
-    for layer in reversed(range(1, layers)):
-        ffn_mine_of(layer, token)
-    attention_grads_of(0, (token,), saved[0]["ffn_received"])
+        attention_grads_of(layer, (), tokens)
+        ffn_mine_of(layer, *tokens)
+    attention_grads_of(0, tokens, saved[0]["ffn_received"])
     ffn_mine_of(0)
     if not shared_rows:
         results[5:] = [lax.psum(x, "context") for x in results[5:]]
-    output = finish(saved[last]["mixed"] + received_sum(after(last_sends, grad)))
+    output = features(output).reshape(1, piece_len, width)
     grad_input = finish(grad)
-    gain_total = sum_over(sum_over(jnp.stack(gain_grads), "tensor"), "context")
-    gain_total = gain_total[:, :half] + other(gain_total[:, half:])
+    gain_total = lax.psum(features(jnp.stack(gain_grads)), ("fsdp", "context", "tensor"))
+    gain_total = lax.dynamic_slice_in_dim(gain_total, core * half, half, 1)
     return (
         output, grad_input, *results[:5], jnp.stack(small[0]), jnp.stack(small[1]),
         gain_total[:layers], gain_total[layers:], *results[5:],

time: 699 us -> 728 us (1.041)
  blocking collectives: 40.9 us -> 106 us
  waiting for transfers between devices: 144 us -> 118 us
  starting transfers between devices: 149 us -> 128 us
  local copies, waits for them, and re-layouts: 67.4 us -> 86.7 us
    ppermute x70 -> x63, waiting for transfers between devices: 91.7 us -> 51.5 us  [swap(): return lax.ppermute(x, axis, [(i, i ^ k) for i in range(n)])]
    psum x0 -> x1, blocking collectives: none -> 40 us  [local(): lax.psum(features(jnp.stack(gain_grads)), ('fsdp', 'context', 'tensor'))]
    unnamed x144 -> x214, local copies, waits for them, and re-layouts: 17.8 us -> 42.1 us
    slice x25 -> x0, local copies, waits for them, and re-layouts: 19.1 us -> none  [the longest x24 19.1 us: after(): first = lax.slice(token, (0,) * token.ndim, (1,) * token.ndim).reshape(1, 1)]
    psum x0 -> x1, waiting for transfers between devices: none -> 14.1 us  [local(): output = lax.psum(after(with_rows, token), 'tensor')]
    all_to_all x0 -> x1, blocking collectives: none -> 13.4 us  [gathered(): lax.all_to_all(copies, axis, 0, 0, tiled=True)]
    add x23 -> x0, other arithmetic: 13.1 us -> none  [the longest x20 11.7 us: after(): x = x + (first.astype(f32) * 0.0).astype(x.dtype)]
    all_to_all x3 -> x4, blocking collectives: 40.9 us -> 52.9 us  [received_sum(): lax.all_to_all(sends.reshape(count, -1, sends.shape[1]), 'tensor', 0, 0,...]
  transfers between devices with their start and end apart: 92 -> 82, of which waited for: 29 -> 20; matrix products, arithmetic and copies ran while one was open for 9% -> 9% of each run, Pallas kernels for 35% -> 29%
where the time goes in v6:
time: 728 us; the launch traced here: 716 us
  Pallas kernels  236 us (32%)
  starting transfers between devices  128 us (18%)
  waiting for transfers between devices  118 us (16%)
  blocking collectives  106 us (15%)
  local copies, waits for them, and re-layouts  86.7 us (12%)
  other arithmetic  25.9 us (4%)
  between operations  15.8 us (2%)
    pallas_call x2, Pallas kernels, attention_backward(): pl.pallas_call(functools.partial(backward_kernel, len(parts), piece_len,...  67 us
    all_to_all x15, starting transfers between devices, gathered(): lax.all_to_all(copies, axis, 0, 0, tiled=True)  60.7 us
    ppermute x63, starting transfers between devices, swap(): return lax.ppermute(x, axis, [(i, i ^ k) for i in range(n)])  54.4 us
    all_to_all x4, blocking collectives, received_sum(): lax.all_to_all(sends.reshape(count, -1, sends.shape[1]), 'tensor', 0, 0,...  52.9 us
    ppermute x63, waiting for transfers between devices, swap(): return lax.ppermute(x, axis, [(i, i ^ k) for i in range(n)])  51.5 us
    pallas_call x2, Pallas kernels, ffn_theirs(): pl.pallas_call(functools.partial(ffn_theirs_kernel, len(b_parts)), grid_s...  48.2 us
    all_to_all x15, waiting for transfers between devices, gathered(): lax.all_to_all(copies, axis, 0, 0, tiled=True)  45.2 us
    unnamed x214, local copies, waits for them, and re-layouts  42.1 us
  transfers between devices with their start and end apart: 82, of which 20 were waited for; matrix products, arithmetic and copies ran while one was open for 9% of the time, Pallas kernels for 29%

profile of v6, /device:TPU:0, one launch (start us, length us, event | category | flops | bytes accessed | tf_op | source)
XLA Modules:
  0.0 716.3 jit_solution(16656729114056663302)
XLA Ops:
  24.7 12.0 %all-to-all-done = s32[4,1,256]{2,1,0:T(1,128)} async-done(((s32[4,1,256]{2,1,0:T(1,128)}), s32[4,1,256]{2,1,0:T(1,128)}, u32[]{:S(2)}, u32[]{:S(2)}) %all-to-all-start) | async-done | bytes 4128 | tf_op jit(solution)/shard_map/all_to_all | solution.py:48
  63.2 5.1 all-to-all-done.1
  74.8 19.2 %shard_map.256 = (bf16[1024,1536]{1,0:T(8,128)(2,1)}, bf16[1024,384]{1,0:T(8,128)(2,1)}, bf16[1024,384]{1,0:T(8,128)(2,1)}, bf16[1024,384]{1,0:T(8,128)(2,1)}, f...) custom-call(s32[2]{0:T(128)} %pad_add_fusion.refs_0_, ...), custom_call_target="tpu_custom_call" | custom-call | flops 20899999744 | tf_op jit(solution)/shard_map/pallas_call | solution.py:588
  94.8 15.7 %all_to_all.115 = bf16[4,64,1536]{2,1,0:T(8,128)(2,1)S(1)} all-to-all(bf16[4,64,1536]{2,1,0:T(8,128)(2,1)} %bitcast.82), channel_id=1, replica_groups=mesh['fsdp'=2,'context'=4,'tensor'=4] {'tensor'}, dimensions={0} | all-to-all | bytes 1572864 | tf_op jit(solution)/shard_map/all_to_all | solution.py:82
  111.5 13.4 %all_to_all.116 = bf16[4,64,1536]{2,1,0:T(8,128)(2,1)S(1)} all-to-all(bf16[4,64,1536]{2,1,0:T(8,128)(2,1)S(1)} %broadcast_in_dim.40), channel_id=1, replica_groups=mesh['fsdp'=2,'context'=4,'tensor'=4] {'tensor'}, dimensions={0} | all-to-all | bytes 1572864 | tf_op jit(solution)/shard_map/all_to_all | solution.py:48
  127.1 6.1 shard_map.259
  133.2 11.8 %all_to_all.117 = bf16[4,64,1536]{2,1,0:T(8,128)(2,1)S(1)} all-to-all(bf16[4,64,1536]{2,1,0:T(8,128)(2,1)S(1)} %bitcast.66), channel_id=1, replica_groups=mesh['fsdp'=2,'context'=4,'tensor'=4] {'tensor'}, dimensions={0} | all-to-all | bytes 1572864 | tf_op jit(solution)/shard_map/all_to_all | solution.py:82
  153.8 5.2 all-to-all-done.5
  175.3 7.8 %all-to-all-done.6 = bf16[4,64,1536]{2,1,0:T(8,128)(2,1)S(1)} async-done(((bf16[4,64,1536]{2,1,0:T(8,128)(2,1)}), bf16[4,64,1536]{2,1,0:T(8,128)(2,1)S(1)}, u32[]{:S(2)}, u32[]{:S(2)}) %all-to-all-start.6) | async-done | bytes 786464 | tf_op jit(solution)/shard_map/all_to_all | solution.py:48
  195.9 19.2 %shard_map.261 = (bf16[1024,1536]{1,0:T(8,128)(2,1)}, bf16[1024,384]{1,0:T(8,128)(2,1)}, bf16[1024,384]{1,0:T(8,128)(2,1)}, bf16[1024,384]{1,0:T(8,128)(2,1)}, f...) custom-call(s32[2]{0:T(128)} %pad_add_fusion.refs_0_, ...), custom_call_target="tpu_custom_call" | custom-call | flops 20899999744 | tf_op jit(solution)/shard_map/pallas_call | solution.py:588
  217.0 12.6 %all_to_all.118 = bf16[4,64,1536]{2,1,0:T(8,128)(2,1)S(1)} all-to-all(bf16[4,64,1536]{2,1,0:T(8,128)(2,1)} %bitcast.78), channel_id=1, replica_groups=mesh['fsdp'=2,'context'=4,'tensor'=4] {'tensor'}, dimensions={0} | all-to-all | bytes 1572864 | tf_op jit(solution)/shard_map/all_to_all | solution.py:82
  258.1 6.1 shard_map.265
  264.2 7.1 shard_map.266.refs_0_
  272.2 12.8 %all_to_all.119 = bf16[4,64,1536]{2,1,0:T(8,128)(2,1)S(1)} all-to-all(bf16[4,64,1536]{2,1,0:T(8,128)(2,1)} %bitcast.65), channel_id=1, replica_groups=mesh['fsdp'=2,'context'=4,'tensor'=4] {'tensor'}, dimensions={0} | all-to-all | bytes 1572864 | tf_op jit(solution)/shard_map/all_to_all | solution.py:82
  293.4 6.9 all-to-all-done.13
  331.3 33.5 %shard_map.271 = (bf16[1024,1536]{1,0:T(8,128)(2,1)}, bf16[1024,384]{1,0:T(8,128)(2,1)}, bf16[1024,384]{1,0:T(8,128)(2,1)}, bf16[1024,384]{1,0:T(8,128)(2,1)}, b...) custom-call(s32[2]{0:T(128)} %pad_add_fusion.refs_0_, ...), custom_call_target="tpu_custom_call" | custom-call | flops 36300001280 | tf_op jit(solution)/shard_map/pallas_call | solution.py:618
  364.9 8.3 %collective-permute-done.36.refs_4_.refs_2_ = bf16[256,1536]{1,0:T(8,128)(2,1)} collective-permute-done((bf16[256,1536]{1,0:T(8,128)(2,1)}, bf16[256,1536]{1,0:T(8,128)(2,1)}, u32[]{:S(2)}, u32[]{:S(2)}) %collective-permute-start.36) | collective-permute-done | bytes 786464 | tf_op jit(solution)/shard_map/ppermute | solution.py:25
  378.8 6.8 all-to-all-done.15
  393.4 8.7 %shard_map.285 = (bf16[768,384]{1,0:T(8,128)(2,1)}, bf16[768,384]{1,0:T(8,128)(2,1)}, bf16[768,384]{1,0:T(8,128)(2,1)}, bf16[768,384]{1,0:T(8,128)(2,1)}, bf16[7...) custom-call(bf16[1024,1536]{1,0:T(8,128)(2,1)} %get-tuple-element.143.refs_0_, ...), custom_call_target="tpu_custom_call" | custom-call | flops 7699999744 | tf_op jit(solution)/shard_map/pallas_call | solution.py:760
  408.6 8.0 %shard_map.277 = bf16[256,1536]{1,0:T(8,128)(2,1)} custom-call(bf16[256,1536]{1,0:T(8,128)(2,1)S(1)} %bitcast.62, f32[256,1024]{1,0:T(8,128)S(1)} %copy-done.26, f32[256,1024]{1,0:T(8,128)S(1)} %copy-done.28, bf16[2,768,1024]{2,1,0:T(8,128)(2,1)S(1)} %copy-done.15, bf16[2,768,1024]{2,1,0:T(8,128)(2,1)S(1)} %copy-done.18, ...), custom_call_target="tpu_custom_call" | custom-call | flops 8800000000 | tf_op jit(solution)/shard_map/pallas_call | solution.py:669
  422.6 14.1 %all-reduce.4.cloned.1.call-done = bf16[256,1536]{1,0:T(8,128)(2,1)} async-done(((bf16[256,1536]{1,0:T(8,128)(2,1)}), bf16[256,1536]{1,0:T(8,128)(2,1)}) %all-reduce.4.cloned.1.call-update) | async-done | bytes 786448 | tf_op jit(solution)/shard_map/psum | solution.py:917
  442.2 11.9 %collective-permute-done.37.refs_1_ = bf16[64,1536]{1,0:T(8,128)(2,1)} collective-permute-done((bf16[64,1536]{1,0:T(8,128)(2,1)}, bf16[64,1536]{1,0:T(8,128)(2,1)}, u32[]{:S(2)}, u32[]{:S(2)}) %collective-permute-start.37) | collective-permute-done | bytes 196640 | tf_op jit(solution)/shard_map/ppermute | solution.py:25
  470.9 11.7 %collective-permute-done.40.refs_13_ = bf16[64,1536]{1,0:T(8,128)(2,1)S(1)} collective-permute-done((bf16[64,1536]{1,0:T(8,128)(2,1)S(1)}, bf16[64,1536]{1,0:T(8,128)(2,1)S(1)}, u32[]{:S(2)}, u32[]{:S(2)}) %collective-permute-start.40) | collective-permute-done | bytes 196640 | tf_op jit(solution)/shard_map/ppermute | solution.py:25
  487.9 24.1 %shard_map.289 = (bf16[1024,1536]{1,0:T(8,128)(2,1)}, bf16[1024,1536]{1,0:T(8,128)(2,1)}, bf16[1024,1024]{1,0:T(8,128)(2,1)}, bf16[1024,1024]{1,0:T(8,128)(2,1)}...) custom-call(s32[2]{0:T(128)} %pad_add_fusion.refs_0_, ...), custom_call_target="tpu_custom_call" | custom-call | flops 26400000000 | tf_op jit(solution)/shard_map/pallas_call | solution.py:687
  521.8 33.5 %shard_map.279 = (bf16[1024,1536]{1,0:T(8,128)(2,1)}, bf16[1024,384]{1,0:T(8,128)(2,1)}, bf16[1024,384]{1,0:T(8,128)(2,1)}, bf16[1024,384]{1,0:T(8,128)(2,1)}, b...) custom-call(s32[2]{0:T(128)} %pad_add_fusion.refs_0_, ...), custom_call_target="tpu_custom_call" | custom-call | flops 36300001280 | tf_op jit(solution)/shard_map/pallas_call | solution.py:618
  564.4 24.1 %shard_map.283 = (bf16[1024,1536]{1,0:T(8,128)(2,1)}, bf16[1024,1536]{1,0:T(8,128)(2,1)}, bf16[1024,1024]{1,0:T(8,128)(2,1)}, bf16[1024,1024]{1,0:T(8,128)(2,1)}...) custom-call(s32[2]{0:T(128)} %pad_add_fusion.refs_0_, ...), custom_call_target="tpu_custom_call" | custom-call | flops 26400000000 | tf_op jit(solution)/shard_map/pallas_call | solution.py:687
  595.0 8.4 %shard_map.284 = (bf16[768,384]{1,0:T(8,128)(2,1)}, bf16[768,384]{1,0:T(8,128)(2,1)}, bf16[768,384]{1,0:T(8,128)(2,1)}, bf16[768,384]{1,0:T(8,128)(2,1)}, bf16[7...) custom-call(bf16[1024,1536]{1,0:T(8,128)(2,1)} %get-tuple-element.128.refs_0_, ...), custom_call_target="tpu_custom_call" | custom-call | flops 7699999744 | tf_op jit(solution)/shard_map/pallas_call | solution.py:760
  606.1 9.6 %shard_map.287 = (f32[2,768,384]{2,1,0:T(8,128)}, f32[2,768,384]{2,1,0:T(8,128)}, f32[2,768,384]{2,1,0:T(8,128)}, f32[2,768,384]{2,1,0:T(8,128)}, f32[768,128]{1,0:T(8,128)}, /*index=5*/f32[2,384,768]{2,1,0:T(8,128)}) custom-call(bf16[1024,1536]{1,0:T(8,128)(2,1)} %get-tuple-element.14, ...), custom_call_target="tpu_custom_call", output_to_operand_aliasing={{0}: (14, {}), {1}: (15, {}), {2}: (16, {}), {3}: (17, {}),... | custom-call | flops 7699999744 | tf_op jit(solution)/shard_map/pallas_call | solution.py:760
  620.0 40.0 %psum.15 = f32[4,1536]{1,0:T(4,128)} all-reduce(f32[4,1536]{1,0:T(4,128)} %maximum_select_fusion.4), channel_id=1, replica_groups=mesh['fsdp'=2,'context'=4,'tensor'=4] {'fsdp','context','tensor'}, use_global_device_ids=true, to_apply=%region_24.25 | all-reduce | flops 6144 | bytes 49152 | tf_op jit(solution)/shard_map/psum | solution.py:969
  667.3 9.6 %shard_map.290 = (f32[2,768,1024]{2,1,0:T(8,128)}, f32[2,768,1024]{2,1,0:T(8,128)}, f32[2,1024,768]{2,1,0:T(8,128)}) custom-call(bf16[1024,1536]{1,0:T(8,128)(2,1)S(1)} %copy-done.6, bf16[1024,1536]{1,0:T(8,128)(2,1)} %get-tuple-element.182.g_ref, bf16[1024,1024]{1,0:T(8,128)(2,1)S(1)} %copy-done.10, ...), custom_call_target="tpu_custom_call", output_to_operand_aliasing={{0}: (8, {}), {1}: (9, {}), {2}: (10, {})} | custom-call | flops 9900000256 | tf_op jit(solution)/shard_map/pallas_call | solution.py:720
  681.9 9.6 %shard_map.288 = (f32[2,768,384]{2,1,0:T(8,128)}, f32[2,768,384]{2,1,0:T(8,128)}, f32[2,768,384]{2,1,0:T(8,128)}, f32[2,768,384]{2,1,0:T(8,128)}, f32[768,128]{1,0:T(8,128)}, /*index=5*/f32[2,384,768]{2,1,0:T(8,128)}) custom-call(bf16[1024,1536]{1,0:T(8,128)(2,1)} %get-tuple-element.12, ...), custom_call_target="tpu_custom_call", output_to_operand_aliasing={{0}: (14, {}), {1}: (15, {}), {2}: (16, {}), {3}: (17, {}),... | custom-call | flops 7699999744 | tf_op jit(solution)/shard_map/pallas_call | solution.py:760
  699.5 9.5 %shard_map.291 = (f32[2,768,1024]{2,1,0:T(8,128)}, f32[2,768,1024]{2,1,0:T(8,128)}, f32[2,1024,768]{2,1,0:T(8,128)}) custom-call(bf16[1024,1536]{1,0:T(8,128)(2,1)S(1)} %copy-done, bf16[1024,1536]{1,0:T(8,128)(2,1)} %get-tuple-element.177.g_ref, bf16[1024,1024]{1,0:T(8,128)(2,1)S(1)} %copy-done.22, ...), custom_call_target="tpu_custom_call", output_to_operand_aliasing={{0}: (8, {}), {1}: (9, {}), {2}: (10, {})} | custom-call | flops 9900000256 | tf_op jit(solution)/shard_map/pallas_call | solution.py:720
  (482 shorter events, 268.1 us)
Async XLA Ops:
  11.4 38.8 %collective-permute-start.1 = (bf16[256,1536]{1,0:T(8,128)(2,1)S(1)}, bf16[256,1536]{1,0:T(8,128)(2,1)}, u32[]{:S(2)}, u32[]{:S(2)}) collective-permute-start(bf16[256,1536]{1,0:T(8,128)(2,1)S(1)} %multiply_convert_fusion.refs_1_), channel_id=1, source_target_pairs={{0,4},{4,0},{8,12},{12,8},{1,5},{5,1},{9,13},{13,9},{2,6},{6,2},{1... | collective-permute-start | bytes 2359304 | tf_op jit(solution)/shard_map/ppermute | solution.py:25
  42.9 26.4 %collective-permute-start.7 = (bf16[2,768,384]{2,1,0:T(8,128)(2,1)}, bf16[2,768,384]{2,1,0:T(8,128)(2,1)}, u32[]{:S(2)}, u32[]{:S(2)}) collective-permute-start(bf16[2,768,384]{2,1,0:T(8,128)(2,1)} %refs_4_.1), channel_id=1, source_target_pairs={{0,16},{16,0},{1,17},{17,1},{2,18},{18,2},{3,19},{19,3},{4,20},{20... | collective-permute-start | bytes 3538952 | tf_op jit(solution)/shard_map/ppermute | solution.py:25
  69.3 55.6 %collective-permute-start.15 = (bf16[2,768,1024]{2,1,0:T(8,128)(2,1)}, bf16[2,768,1024]{2,1,0:T(8,128)(2,1)}, u32[]{:S(2)}, u32[]{:S(2)}) collective-permute-start(bf16[2,768,1024]{2,1,0:T(8,128)(2,1)} %refs_7_.5), channel_id=1, source_target_pairs={{0,16},{16,0},{1,17},{17,1},{2,18},{18,2},{3,19},{19,3},{4,20},{20... | collective-permute-start | bytes 9437192 | tf_op jit(solution)/shard_map/ppermute | solution.py:25
  69.3 55.6 %collective-permute-start.16 = (bf16[2,768,1024]{2,1,0:T(8,128)(2,1)}, bf16[2,768,1024]{2,1,0:T(8,128)(2,1)}, u32[]{:S(2)}, u32[]{:S(2)}) collective-permute-start(bf16[2,768,1024]{2,1,0:T(8,128)(2,1)} %refs_8_.9), channel_id=1, source_target_pairs={{0,16},{16,0},{1,17},{17,1},{2,18},{18,2},{3,19},{19,3},{4,20},{20... | collective-permute-start | bytes 9437192 | tf_op jit(solution)/shard_map/ppermute | solution.py:25
  69.8 55.1 %collective-permute-start.17 = (bf16[2,1024,768]{2,1,0:T(8,128)(2,1)}, bf16[2,1024,768]{2,1,0:T(8,128)(2,1)}, u32[]{:S(2)}, u32[]{:S(2)}) collective-permute-start(bf16[2,1024,768]{2,1,0:T(8,128)(2,1)} %refs_9_.9), channel_id=1, source_target_pairs={{0,16},{16,0},{1,17},{17,1},{2,18},{18,2},{3,19},{19,3},{4,20},{20... | collective-permute-start | bytes 9437192 | tf_op jit(solution)/shard_map/ppermute | solution.py:25
  159.0 36.9 %collective-permute-start.18 = (bf16[256,1536]{1,0:T(8,128)(2,1)}, bf16[256,1536]{1,0:T(8,128)(2,1)}, u32[]{:S(2)}, u32[]{:S(2)}) collective-permute-start(bf16[256,1536]{1,0:T(8,128)(2,1)} %bitcast.12.refs_1_), channel_id=1, source_target_pairs={{0,4},{4,0},{8,12},{12,8},{1,5},{5,1},{9,13},{13,9},{2,6},{6,2},{1... | collective-permute-start | bytes 2359304 | tf_op jit(solution)/shard_map/ppermute | solution.py:25
  186.2 29.6 %all-to-all-start.7 = ((bf16[4,128,1536]{2,1,0:T(8,128)(2,1)}), bf16[4,128,1536]{2,1,0:T(8,128)(2,1)S(1)}, u32[]{:S(2)}, u32[]{:S(2)}) async-start(bf16[4,128,1536]{2,1,0:T(8,128)(2,1)} %broadcast_in_dim.43), calls=%async_computation.7 | async-start | bytes 3145728 | tf_op jit(solution)/shard_map/all_to_all | solution.py:48
  238.5 25.7 %collective-permute-start.26 = (bf16[64,1536]{1,0:T(8,128)(2,1)}, bf16[64,1536]{1,0:T(8,128)(2,1)S(1)}, u32[]{:S(2)}, u32[]{:S(2)}) collective-permute-start(bf16[64,1536]{1,0:T(8,128)(2,1)} %multiply_convert_fusion.1), channel_id=1, source_target_pairs={{0,8},{4,12},{8,0},{12,4},{1,9},{5,13},{9,1},{13,5},{2,10},{6,14},... | collective-permute-start | bytes 589832 | tf_op jit(solution)/shard_map/ppermute | solution.py:25
  238.5 25.7 %collective-permute-start.27 = (bf16[64,1536]{1,0:T(8,128)(2,1)}, bf16[64,1536]{1,0:T(8,128)(2,1)S(1)}, u32[]{:S(2)}, u32[]{:S(2)}) collective-permute-start(bf16[64,1536]{1,0:T(8,128)(2,1)} %multiply_convert_fusion.1), channel_id=1, source_target_pairs={{0,12},{4,8},{8,4},{12,0},{1,13},{5,9},{9,5},{13,1},{2,14},{6,10},... | collective-permute-start | bytes 589832 | tf_op jit(solution)/shard_map/ppermute | solution.py:25
  300.3 31.0 %collective-permute-start.30 = (bf16[256,1536]{1,0:T(8,128)(2,1)}, bf16[256,1536]{1,0:T(8,128)(2,1)}, u32[]{:S(2)}, u32[]{:S(2)}) collective-permute-start(bf16[256,1536]{1,0:T(8,128)(2,1)} %bitcast.22.refs_1_), channel_id=1, source_target_pairs={{0,4},{4,0},{8,12},{12,8},{1,5},{5,1},{9,13},{13,9},{2,6},{6,2},{1... | collective-permute-start | bytes 2359304 | tf_op jit(solution)/shard_map/ppermute | solution.py:25
  323.4 49.8 %all-to-all-start.14 = ((bf16[4,128,1536]{2,1,0:T(8,128)(2,1)}), bf16[4,128,1536]{2,1,0:T(8,128)(2,1)}, u32[]{:S(2)}, u32[]{:S(2)}) async-start(bf16[4,128,1536]{2,1,0:T(8,128)(2,1)} %broadcast_in_dim.48), calls=%async_computation.14 | async-start | bytes 3145728 | tf_op jit(solution)/shard_map/all_to_all | solution.py:48
  328.0 36.9 %collective-permute-start.34 = (bf16[256,1536]{1,0:T(8,128)(2,1)}, bf16[256,1536]{1,0:T(8,128)(2,1)}, u32[]{:S(2)}, u32[]{:S(2)}) collective-permute-start(bf16[256,1536]{1,0:T(8,128)(2,1)} %shard_map.273), channel_id=1, source_target_pairs={{0,4},{4,0},{8,12},{12,8},{1,5},{5,1},{9,13},{13,9},{2,6},{6,2},{1... | collective-permute-start | bytes 2359304 | tf_op jit(solution)/shard_map/ppermute | solution.py:25
  329.2 35.6 %collective-permute-start.35 = (bf16[256,1536]{1,0:T(8,128)(2,1)S(1)}, bf16[256,1536]{1,0:T(8,128)(2,1)S(1)}, u32[]{:S(2)}, u32[]{:S(2)}) collective-permute-start(bf16[256,1536]{1,0:T(8,128)(2,1)S(1)} %copy-done.48), channel_id=1, source_target_pairs={{0,4},{4,0},{8,12},{12,8},{1,5},{5,1},{9,13},{13,9},{2,6},{6,2},{1... | collective-permute-start | bytes 2359304 | tf_op jit(solution)/shard_map/ppermute | solution.py:25
  331.2 41.9 %collective-permute-start.36 = (bf16[256,1536]{1,0:T(8,128)(2,1)}, bf16[256,1536]{1,0:T(8,128)(2,1)}, u32[]{:S(2)}, u32[]{:S(2)}) collective-permute-start(bf16[256,1536]{1,0:T(8,128)(2,1)} %shard_map.275), channel_id=1, source_target_pairs={{0,4},{4,0},{8,12},{12,8},{1,5},{5,1},{9,13},{13,9},{2,6},{6,2},{1... | collective-permute-start | bytes 2359304 | tf_op jit(solution)/shard_map/ppermute | solution.py:25
  377.2 59.5 %all-reduce.4.cloned.1.call-start = ((), (), s32[]{:S(2)}) async-start(), calls=%async_computation.23 | async-start | bytes 1572864 | tf_op jit(solution)/shard_map/psum | solution.py:917
  402.1 201.4 %collective-permute-start.49 = (bf16[768,384]{1,0:T(8,128)(2,1)}, bf16[768,384]{1,0:T(8,128)(2,1)}, u32[]{:S(2)}, u32[]{:S(2)}) collective-permute-start(bf16[768,384]{1,0:T(8,128)(2,1)} %get-tuple-element.151), channel_id=1, source_target_pairs={{0,16},{16,0},{1,17},{17,1},{2,18},{18,2},{3,19},{19,3},{4,20},{20... | collective-permute-start | bytes 1769480 | tf_op jit(solution)/shard_map/ppermute | solution.py:25
  402.1 201.9 %collective-permute-start.50 = (bf16[768,384]{1,0:T(8,128)(2,1)}, bf16[768,384]{1,0:T(8,128)(2,1)}, u32[]{:S(2)}, u32[]{:S(2)}) collective-permute-start(bf16[768,384]{1,0:T(8,128)(2,1)} %get-tuple-element.152), channel_id=1, source_target_pairs={{0,16},{16,0},{1,17},{17,1},{2,18},{18,2},{3,19},{19,3},{4,20},{20... | collective-permute-start | bytes 1769480 | tf_op jit(solution)/shard_map/ppermute | solution.py:25
  402.6 201.5 %collective-permute-start.51 = (bf16[768,384]{1,0:T(8,128)(2,1)}, bf16[768,384]{1,0:T(8,128)(2,1)}, u32[]{:S(2)}, u32[]{:S(2)}) collective-permute-start(bf16[768,384]{1,0:T(8,128)(2,1)} %get-tuple-element.153), channel_id=1, source_target_pairs={{0,16},{16,0},{1,17},{17,1},{2,18},{18,2},{3,19},{19,3},{4,20},{20... | collective-permute-start | bytes 1769480 | tf_op jit(solution)/shard_map/ppermute | solution.py:25
  456.1 26.6 %all-to-all-start.18 = ((bf16[4,64,1536]{2,1,0:T(8,128)(2,1)}), bf16[4,64,1536]{2,1,0:T(8,128)(2,1)}, u32[]{:S(2)}, u32[]{:S(2)}) async-start(bf16[4,64,1536]{2,1,0:T(8,128)(2,1)} %broadcast_in_dim.50), calls=%async_computation.18 | async-start | bytes 1572864 | tf_op jit(solution)/shard_map/all_to_all | solution.py:48
  484.0 27.9 %all-to-all-start.19 = ((bf16[4,128,1536]{2,1,0:T(8,128)(2,1)}), bf16[4,128,1536]{2,1,0:T(8,128)(2,1)S(1)}, u32[]{:S(2)}, u32[]{:S(2)}) async-start(bf16[4,128,1536]{2,1,0:T(8,128)(2,1)} %broadcast_in_dim.51), calls=%async_computation.19 | async-start | bytes 3145728 | tf_op jit(solution)/shard_map/all_to_all | solution.py:48
  487.9 34.0 %collective-permute-start.39 = (bf16[256,1536]{1,0:T(8,128)(2,1)}, bf16[256,1536]{1,0:T(8,128)(2,1)}, u32[]{:S(2)}, u32[]{:S(2)}) collective-permute-start(bf16[256,1536]{1,0:T(8,128)(2,1)} %bitcast.27.refs_1_), channel_id=1, source_target_pairs={{0,4},{4,0},{8,12},{12,8},{1,5},{5,1},{9,13},{13,9},{2,6},{6,2},{1... | collective-permute-start | bytes 2359304 | tf_op jit(solution)/shard_map/ppermute | solution.py:25
  513.1 45.3 %collective-permute-start.42 = (bf16[256,1536]{1,0:T(8,128)(2,1)}, bf16[256,1536]{1,0:T(8,128)(2,1)S(1)}, u32[]{:S(2)}, u32[]{:S(2)}) collective-permute-start(bf16[256,1536]{1,0:T(8,128)(2,1)} %shard_map.280), channel_id=1, source_target_pairs={{0,4},{4,0},{8,12},{12,8},{1,5},{5,1},{9,13},{13,9},{2,6},{6,2},{1... | collective-permute-start | bytes 2359304 | tf_op jit(solution)/shard_map/ppermute | solution.py:25
  517.4 41.3 %all-to-all-start.20 = ((bf16[4,128,1536]{2,1,0:T(8,128)(2,1)}), bf16[4,128,1536]{2,1,0:T(8,128)(2,1)S(1)}, u32[]{:S(2)}, u32[]{:S(2)}) async-start(bf16[4,128,1536]{2,1,0:T(8,128)(2,1)} %broadcast_in_dim.52), calls=%async_computation.20 | async-start | bytes 3145728 | tf_op jit(solution)/shard_map/all_to_all | solution.py:48
  557.7 47.5 %collective-permute-start.52 = (bf16[768,384]{1,0:T(8,128)(2,1)}, bf16[768,384]{1,0:T(8,128)(2,1)}, u32[]{:S(2)}, u32[]{:S(2)}) collective-permute-start(bf16[768,384]{1,0:T(8,128)(2,1)} %get-tuple-element.154), channel_id=1, source_target_pairs={{0,16},{16,0},{1,17},{17,1},{2,18},{18,2},{3,19},{19,3},{4,20},{20... | collective-permute-start | bytes 1769480 | tf_op jit(solution)/shard_map/ppermute | solution.py:25
  558.4 36.4 %collective-permute-start.53 = (bf16[768,128]{1,0:T(8,128)(2,1)}, bf16[768,128]{1,0:T(8,128)(2,1)}, u32[]{:S(2)}, u32[]{:S(2)}) collective-permute-start(bf16[768,128]{1,0:T(8,128)(2,1)} %get-tuple-element.155), channel_id=1, source_target_pairs={{0,16},{16,0},{1,17},{17,1},{2,18},{18,2},{3,19},{19,3},{4,20},{20... | collective-permute-start | bytes 589832 | tf_op jit(solution)/shard_map/ppermute | solution.py:25
  559.9 28.5 %all-to-all-start.21 = ((bf16[4,64,1536]{2,1,0:T(8,128)(2,1)}), bf16[4,64,1536]{2,1,0:T(8,128)(2,1)S(1)}, u32[]{:S(2)}, u32[]{:S(2)}) async-start(bf16[4,64,1536]{2,1,0:T(8,128)(2,1)} %bitcast.83), calls=%async_computation.21 | async-start | bytes 1572864 | tf_op jit(solution)/shard_map/all_to_all | solution.py:82
  590.7 86.8 %all-to-all-start.22 = ((bf16[4,64,1536]{2,1,0:T(8,128)(2,1)}), bf16[4,64,1536]{2,1,0:T(8,128)(2,1)}, u32[]{:S(2)}, u32[]{:S(2)}) async-start(bf16[4,64,1536]{2,1,0:T(8,128)(2,1)} %broadcast_in_dim.53), calls=%async_computation.22 | async-start | bytes 1572864 | tf_op jit(solution)/shard_map/all_to_all | solution.py:48
  603.5 58.0 %collective-permute-start.60 = (bf16[768,1024]{1,0:T(8,128)(2,1)}, bf16[768,1024]{1,0:T(8,128)(2,1)}, u32[]{:S(2)}, u32[]{:S(2)}) collective-permute-start(bf16[768,1024]{1,0:T(8,128)(2,1)} %get-tuple-element.186), channel_id=1, source_target_pairs={{0,16},{16,0},{1,17},{17,1},{2,18},{18,2},{3,19},{19,3},{4,20},{20... | collective-permute-start | bytes 4718600 | tf_op jit(solution)/shard_map/ppermute | solution.py:25
  604.0 57.4 %collective-permute-start.61 = (bf16[768,1024]{1,0:T(8,128)(2,1)}, bf16[768,1024]{1,0:T(8,128)(2,1)}, u32[]{:S(2)}, u32[]{:S(2)}) collective-permute-start(bf16[768,1024]{1,0:T(8,128)(2,1)} %get-tuple-element.187), channel_id=1, source_target_pairs={{0,16},{16,0},{1,17},{17,1},{2,18},{18,2},{3,19},{19,3},{4,20},{20... | collective-permute-start | bytes 4718600 | tf_op jit(solution)/shard_map/ppermute | solution.py:25
  604.1 57.8 %collective-permute-start.62 = (bf16[1024,768]{1,0:T(8,128)(2,1)}, bf16[1024,768]{1,0:T(8,128)(2,1)}, u32[]{:S(2)}, u32[]{:S(2)}) collective-permute-start(bf16[1024,768]{1,0:T(8,128)(2,1)} %get-tuple-element.188), channel_id=1, source_target_pairs={{0,16},{16,0},{1,17},{17,1},{2,18},{18,2},{3,19},{19,3},{4,20},{20... | collective-permute-start | bytes 4718600 | tf_op jit(solution)/shard_map/ppermute | solution.py:25
  605.2 57.3 %collective-permute-start.43 = (bf16[768,384]{1,0:T(8,128)(2,1)}, bf16[768,384]{1,0:T(8,128)(2,1)}, u32[]{:S(2)}, u32[]{:S(2)}) collective-permute-start(bf16[768,384]{1,0:T(8,128)(2,1)} %get-tuple-element.137), channel_id=1, source_target_pairs={{0,16},{16,0},{1,17},{17,1},{2,18},{18,2},{3,19},{19,3},{4,20},{20... | collective-permute-start | bytes 1769480 | tf_op jit(solution)/shard_map/ppermute | solution.py:25
  605.3 56.7 %collective-permute-start.47 = (bf16[768,128]{1,0:T(8,128)(2,1)}, bf16[768,128]{1,0:T(8,128)(2,1)}, u32[]{:S(2)}, u32[]{:S(2)}) collective-permute-start(bf16[768,128]{1,0:T(8,128)(2,1)} %get-tuple-element.141), channel_id=1, source_target_pairs={{0,16},{16,0},{1,17},{17,1},{2,18},{18,2},{3,19},{19,3},{4,20},{20... | collective-permute-start | bytes 589832 | tf_op jit(solution)/shard_map/ppermute | solution.py:25
  (155 other events, 2393.2 us)
Sparse Core Ops, SparseCore 0:
  381.7 55.0 all-reduce.3

commit v7 on v6

--- a/solution.py
+++ b/solution.py
@@ -48,17 +48,16 @@
     return lax.all_to_all(copies, axis, 0, 0, tiled=True).reshape((-1,) + block.shape[1:])
 
 
+def sequence_rows(shard):
+    return lax.all_gather(shard, ("context", "tensor"), tiled=True)
+
+
 def near_rows(own):
     return swap(own, "context", 1)
 
 
 def far_blocks(shard):
     return swap(shard, "context", 2), swap(shard, "context", 3)
-
-
-def far_rows(blocks, *tokens):
-    block, width = blocks[0].shape
-    return gathered(after(jnp.concatenate(blocks, axis=0), *tokens), "tensor").reshape(-1, 2, block, width)
 
 
 def all_rows(shard, own=None, token=None, together=False):
@@ -69,7 +68,9 @@
     second, third = far_blocks(shard)
     near = near_rows(own)
     if together:
-        return (own, near, far_rows((second, third))), (second, third)
+        block, width = shard.shape
+        far = gathered(jnp.concatenate([second, third], axis=0), "tensor")
+        return (own, near, far.reshape(-1, 2, block, width)), (second, third)
     if token is not None:
         second = after(second, token)
     third = after(third, second)
@@ -452,17 +453,12 @@
         send_ref[...] = acc[...].astype(bf16)
 
 
-def ffn_theirs_kernel(count_parts, *refs):
-    place_ref, refs = refs[0], refs[1:]
-    b_parts, g_parts = refs[:count_parts], refs[count_parts : 2 * count_parts]
-    wg, wu, wd, tg, tu, td = refs[2 * count_parts : 2 * count_parts + 6]
-    b_ref, g_ref, m_ref, dgate_ref, dup_ref, gate_out, up_out, down_out, turned = refs[-9:]
+def ffn_theirs_kernel(b_ref, g_ref, wg, wu, wd, tg, tu, td, *refs):
+    m_ref, dgate_ref, dup_ref, gate_out, up_out, down_out, turned = refs[-7:]
     half = b_ref.shape[1] // 2
 
     @pl.when(pl.program_id(0) == 0)
     def _():
-        assemble(b_parts, b_ref, place_ref)
-        assemble(g_parts, g_ref, place_ref)
         turned[...] = b_ref[:, half:].T
 
     def chunk(i):
@@ -660,7 +656,7 @@
         scratch_shapes=[pltpu.VMEM((rows, width), f32)],
         out_shape=[shape((rows, inner), f32)] * 2 + [shape((rows, width), bf16)],
         cost_estimate=cost(7),
-        compiler_params=pltpu.CompilerParams(vmem_limit_bytes=40 << 20),
+        compiler_params=pltpu.CompilerParams(vmem_limit_bytes=60 << 20),
     )(b, *w3, *t3)
 
 
@@ -674,36 +670,27 @@
         scratch_shapes=[pltpu.VMEM((rows, width), f32)],
         out_shape=shape((rows, width), bf16),
         cost_estimate=cost(8),
-        compiler_params=pltpu.CompilerParams(vmem_limit_bytes=40 << 20),
+        compiler_params=pltpu.CompilerParams(vmem_limit_bytes=60 << 20),
     )(g, gt, up, *w3, *t3, *tokens)
 
 
-def ffn_theirs(place, b_parts, g_parts, layer, w3, t3, *tokens):
-    width = b_parts[0].shape[1]
+def ffn_theirs(b, g, layer, w3, t3, *tokens):
+    rows, width = b.shape
     half = width // 2
-    rows = sum(p.size for p in b_parts) // width
     inner = w3[2].shape[1]
-    wide = pl.BlockSpec((half, hidden_block), lambda p, *_: (0, p))
+    wide = pl.BlockSpec((half, hidden_block), lambda p: (0, p))
     return pl.pallas_call(
-        functools.partial(ffn_theirs_kernel, len(b_parts)),
-        grid_spec=pltpu.PrefetchScalarGridSpec(
-            num_scalar_prefetch=1,
-            grid=(inner // hidden_block,),
-            in_specs=[fixed(p.shape) for p in (*b_parts, *g_parts)]
-            + ffn_weights(layer, w3, t3)
-            + token_specs(tokens),
-            out_specs=[fixed((rows, width))] * 2
-            + [blocks_of(rows)] * 3
-            + [wide, wide, pl.BlockSpec((hidden_block, half), lambda p, *_: (p, 0))],
-            scratch_shapes=[pltpu.VMEM((half, rows), bf16)],
-        ),
-        out_shape=[shape((rows, width), bf16)] * 2
-        + [shape((rows, inner), bf16)] * 3
+        ffn_theirs_kernel,
+        grid=(inner // hidden_block,),
+        in_specs=[fixed(b.shape), fixed(g.shape)] + ffn_weights(layer, w3, t3) + token_specs(tokens),
+        out_specs=[blocks_of(rows)] * 3 + [wide, wide, pl.BlockSpec((hidden_block, half), lambda p: (p, 0))],
+        scratch_shapes=[pltpu.VMEM((half, rows), bf16)],
+        out_shape=[shape((rows, inner), bf16)] * 3
         + [shape((half, inner), bf16)] * 2
         + [shape((inner, half), bf16)],
         cost_estimate=cost(24),
         compiler_params=pltpu.CompilerParams(vmem_limit_bytes=60 << 20),
-    )(place, *b_parts, *g_parts, *w3, *t3, *tokens)
+    )(b, g, *w3, *t3, *tokens)
 
 
 def anywhere():
@@ -730,7 +717,7 @@
         scratch_shapes=[pltpu.VMEM((half, rows), bf16)],
         input_output_aliases={8: 0, 9: 1, 10: 2},
         cost_estimate=cost(9),
-        compiler_params=pltpu.CompilerParams(vmem_limit_bytes=40 << 20),
+        compiler_params=pltpu.CompilerParams(vmem_limit_bytes=60 << 20),
     )(b, g, *values, *received, *totals, *tokens)
 
 
@@ -803,7 +790,6 @@
     seq_len = piece_len * count_z
     shared_rows = count_z == 4
     place = jnp.stack([z, t]).astype(jnp.int32)
-    own_place = place if shared_rows else jnp.zeros((2,), jnp.int32)
 
     def features(x):
         return jnp.where(core == 0, x, jnp.concatenate([x[..., half:], x[..., :half]], axis=-1))
@@ -843,28 +829,23 @@
         inverse_one = inverse_rms(hidden)
         if layer > 0:
             a_parts, _ = all_rows((hidden * inverse_one * gain_one).astype(bf16))
+        forget_weights = w_forget_full[layer]
+        if shared_rows and layer == 1:
+            forget_weights = after(forget_weights, g_last)
         a, (q, k, v, gate, forget, terms), sends = forward_own(
-            place, a_parts, layer, w4, t4, w_attn_out, to, w_forget_full[layer],
+            place, a_parts, layer, w4, t4, w_attn_out, to, forget_weights,
             bias[layer : layer + 1], doc_start, piece_len,
         )
-        token = a_parts[-1]
-        if shared_rows and layer == 0:
-            g_far = far_blocks(after(own_block(cotangent_rows), token))
-            sends = after(sends, *g_far)
-        if shared_rows and layer == last:
-            g_last = far_rows(g_far, token)
-            tokens = [g_last]
-            for s in saved:
-                s["b_far"] = far_blocks(after(s["b_shard"], token))
-                tokens += s["b_far"]
-            sends = after(sends, *tokens)
+        if shared_rows:
+            token = a_parts[-1]
+            if layer == 0:
+                g_last = sequence_rows(after(own_block(cotangent_rows), token))
+            else:
+                saved[-1]["b_rows"] = sequence_rows(after(saved[-1]["b_shard"], token))
         mixed = hidden + received_sum(sends)
         inverse_two = inverse_rms(mixed)
         b_shard = (mixed * inverse_two * gain_two).astype(bf16)
         b = gathered(b_shard, "tensor")
-        if shared_rows and layer == last:
-            for s in saved:
-                s["b_rows"] = far_rows(s["b_far"], b)
         gt, up, sends = ffn_forward(b, layer, w3, t3)
         saved.append(
             dict(hidden=hidden, inverse_one=inverse_one, a=a, kept=(q, k, v, gate, forget, terms), mixed=mixed,
@@ -888,27 +869,33 @@
     small = [[None] * layers for _ in range(2)]
     gain_grads = [None] * (2 * layers)
 
+    def ffn_theirs_of(layer, *tokens):
+        s = saved[layer]
+        values = ffn_theirs(s["b_rows"], s["g_rows"], layer, w3, t3, *tokens)
+        s.update(values=values[:3], ffn_received=[other(x) for x in values[3:]])
+
     for layer in reversed(range(layers)):
         s = saved[layer]
         gain_one, gain_two = gains[layer], gains[layers + layer]
-        before_y, tokens = (), ()
         if layer == last:
             g = cotangent_rows
-            if shared_rows:
-                tokens = s["b_far"] = far_blocks(s["b_shard"])
         else:
             g_shard = grad.astype(bf16)
             g = gathered(g_shard, "tensor")
             if shared_rows:
-                before_y = g_far = far_blocks(g_shard)
-        sends = ffn_backward(g, s["gt"], s["up"], layer, w3, t3, *tokens)
-        if shared_rows and layer == last:
-            sends = after(sends, *[x["b_rows"] for x in saved[:-1]])
+                s["g_rows"] = sequence_rows(g_shard)
+        sends = ffn_backward(g, s["gt"], s["up"], layer, w3, t3)
         back, gain_grads[layers + layer] = norm_back(received_sum(sends), s["mixed"], s["inverse_two"], gain_two)
         grad_mixed = grad + back
-        y_parts, y_far = all_rows(after(grad_mixed.astype(bf16), *before_y), together=layer < last)
+        y_parts, y_far = all_rows(grad_mixed.astype(bf16), together=layer < last)
+        kept = s["kept"]
+        if layer == last and shared_rows:
+            kept = (*kept[:-1], after(kept[-1], *[x["b_rows"] for x in saved[:-1]]))
+        if layer < last:
+            ffn_theirs_of(layer + 1, *y_far)
+            kept = (*kept[:-1], after(kept[-1], saved[layer + 1]["values"][0]))
         y, (dq, dk, dv, dg, u, dz), sends = attention_backward(
-            place, y_parts, layer, w4, t4, w_attn_out, to, w_forget_full[layer], s["kept"], doc_start, piece_len,
+            place, y_parts, layer, w4, t4, w_attn_out, to, w_forget_full[layer], kept, doc_start, piece_len,
         )
         token = y_parts[-1]
         if layer == last:
@@ -916,33 +903,17 @@
             with_rows = lax.dynamic_update_slice_in_dim(last_sends, block_sum.astype(bf16), t * block, 0)
             output = lax.psum(after(with_rows, token), "tensor")
         if not shared_rows:
-            s["b_parts"], s["g_parts"] = (s["b"],), (g,)
+            s.update(b_rows=s["b"], g_rows=g)
         elif layer == last:
-            s["b_rows"] = far_rows(s["b_far"], token)
-            g_near = near_rows(after(g, token))
-            s["g_parts"] = (g, g_near, g_last)
-            tokens = [s["b_rows"], g_near]
-            for x in saved:
-                x["b_near"] = near_rows(after(x["b"], token))
-                tokens.append(x["b_near"])
-            sends = after(sends, *tokens)
-        else:
-            s["g_parts"] = (g, near_rows(after(g, token)), far_rows(g_far, token))
-            sends = after(sends, *s["g_parts"][1:])
-        if shared_rows:
-            s["b_parts"] = (s["b"], s["b_near"], s["b_rows"])
+            s.update(b_rows=sequence_rows(after(s["b_shard"], token)), g_rows=g_last)
         back, gain_grads[layer] = norm_back(received_sum(sends), s["hidden"], s["inverse_one"], gain_one)
         grad = grad_mixed + back
         s.update(u=u, y=y, d=(dq, dk, dv, dg), dz=dz, y_far=y_far)
 
-    def ffn_theirs_of(layer, *tokens):
-        s = saved[layer]
-        b, g, *values = ffn_theirs(own_place, s["b_parts"], s["g_parts"], layer, w3, t3, *tokens)
-        s.update(ffn=(b, g, values[:3]), ffn_received=[other(x) for x in values[3:]])
-
     def ffn_mine_of(layer, *tokens):
         s = saved[layer]
-        results[5:] = ffn_mine(layer, *s["ffn"], s["ffn_received"], results[5:], *tokens)
+        received = s["ffn_received"]
+        results[5:] = ffn_mine(layer, s["b_rows"], s["g_rows"], s["values"], received, results[5:], *tokens)
 
     def attention_grads_of(layer, tokens=(), mine_tokens=()):
         s = saved[layer]
@@ -954,9 +925,8 @@
         small[0][layer] = found[4][:, :heads]
         small[1][layer] = bias_grad + other(bias_grad)
 
-    for layer in reversed(range(layers)):
-        ffn_theirs_of(layer, *(saved[layer - 1]["y_far"] if layer > 0 else ()))
-    tokens = (saved[0]["ffn"][0], grad)
+    ffn_theirs_of(0)
+    tokens = (saved[0]["values"][0], grad)
     for layer in reversed(range(1, layers)):
         attention_grads_of(layer, (), tokens)
         ffn_mine_of(layer, *tokens)
@@ -964,10 +934,13 @@
     ffn_mine_of(0)
     if not shared_rows:
         results[5:] = [lax.psum(x, "context") for x in results[5:]]
-    output = features(output).reshape(1, piece_len, width)
+    output = features(after(output, saved[0]["values"][0])).reshape(1, piece_len, width)
     grad_input = finish(grad)
-    gain_total = lax.psum(features(jnp.stack(gain_grads)), ("fsdp", "context", "tensor"))
-    gain_total = lax.dynamic_slice_in_dim(gain_total, core * half, half, 1)
+    gain_total = jnp.stack(gain_grads).reshape(1, -1)
+    for axis in (("context", "tensor"),) if shared_rows else ("context", "tensor"):
+        gain_total = jnp.sum(gathered(gain_total, axis), axis=0, keepdims=True)
+    gain_total = gain_total.reshape(2 * layers, width)
+    gain_total = gain_total[:, :half] + other(gain_total[:, half:])
     return (
         output, grad_input, *results[:5], jnp.stack(small[0]), jnp.stack(small[1]),
         gain_total[:layers], gain_total[layers:], *results[5:],

time: 728 us -> 675 us (0.927)
  local copies, waits for them, and re-layouts: 86.7 us -> 36.8 us
  starting transfers between devices: 128 us -> 92.1 us
  waiting for transfers between devices: 118 us -> 152 us
  other arithmetic: 25.9 us -> 17.7 us
  Pallas kernels: 236 us -> 244 us
    psum x1 -> x0, blocking collectives: 40 us -> none  [local(): lax.psum(features(jnp.stack(gain_grads)), ('fsdp', 'context', 'tensor'))]
    all_to_all x1 -> x3, blocking collectives: 13.4 us -> 50.2 us  [gathered(): lax.all_to_all(copies, axis, 0, 0, tiled=True)]
    unnamed x214 -> x117, local copies, waits for them, and re-layouts: 42.1 us -> 11.4 us
    all_to_all x15 -> x10, starting transfers between devices: 60.7 us -> 39 us  [gathered(): lax.all_to_all(copies, axis, 0, 0, tiled=True)]
    ppermute x63 -> x52, waiting for transfers between devices: 51.5 us -> 72 us  [swap(): return lax.ppermute(x, axis, [(i, i ^ k) for i in range(n)])]
    all_to_all x3, waiting for transfers between devices: 6.8 us -> 23.8 us  [received_sum(): lax.all_to_all(sends.reshape(count, -1, sends.shape[1]), 'tensor', 0, 0,...]
    psum x1, waiting for transfers between devices: 14.1 us -> 0.02 us  [local(): output = lax.psum(after(with_rows, token), 'tensor')]
    broadcast_in_dim x16 -> x14, local copies, waits for them, and re-layouts: 25.2 us -> 12.6 us  [gathered(): copies = jnp.broadcast_to(block[None], (count,) + block.shape)]
  transfers between devices with their start and end apart: 82 -> 70, of which waited for: 20 -> 27; matrix products, arithmetic and copies ran while one was open for 9% -> 6% of each run, Pallas kernels for 29% -> 31%
where the time goes in v7:
time: 675 us; the launch traced here: 665 us
  Pallas kernels  244 us (36%)
  waiting for transfers between devices  152 us (23%)
  blocking collectives  108 us (16%)
  starting transfers between devices  92.1 us (14%)
  local copies, waits for them, and re-layouts  36.8 us (5%)
  other arithmetic  17.7 us (3%)
  between operations  14.9 us (2%)
    ppermute x52, waiting for transfers between devices, swap(): return lax.ppermute(x, axis, [(i, i ^ k) for i in range(n)])  72 us
    pallas_call x2, Pallas kernels, attention_backward(): pl.pallas_call(functools.partial(backward_kernel, len(parts), piece_len,...  67.4 us
    all_to_all x4, blocking collectives, received_sum(): lax.all_to_all(sends.reshape(count, -1, sends.shape[1]), 'tensor', 0, 0,...  57.6 us
    all_to_all x10, waiting for transfers between devices, gathered(): lax.all_to_all(copies, axis, 0, 0, tiled=True)  55.5 us
    all_to_all x3, blocking collectives, gathered(): lax.all_to_all(copies, axis, 0, 0, tiled=True)  50.2 us
    pallas_call x2, Pallas kernels, ffn_theirs(): pl.pallas_call(ffn_theirs_kernel, grid=(inner // hidden_block,), in_specs...  42.1 us
    ppermute x52, starting transfers between devices, swap(): return lax.ppermute(x, axis, [(i, i ^ k) for i in range(n)])  41.9 us
    all_to_all x10, starting transfers between devices, gathered(): lax.all_to_all(copies, axis, 0, 0, tiled=True)  39 us
  transfers between devices with their start and end apart: 70, of which 27 were waited for; matrix products, arithmetic and copies ran while one was open for 6% of the time, Pallas kernels for 31%

profile of v7, /device:TPU:0, one launch (start us, length us, event | category | flops | bytes accessed | tf_op | source)
XLA Modules:
  0.0 665.0 jit_solution(6480876543313260426)
XLA Ops:
  26.1 12.9 %all-to-all-done = s32[4,1,256]{2,1,0:T(1,128)} async-done(((s32[4,1,256]{2,1,0:T(1,128)}), s32[4,1,256]{2,1,0:T(1,128)}, u32[]{:S(2)}, u32[]{:S(2)}) %all-to-all-start) | async-done | bytes 4128 | tf_op jit(solution)/shard_map/all_to_all | solution.py:48
  71.3 19.2 %shard_map.256 = (bf16[1024,1536]{1,0:T(8,128)(2,1)}, bf16[1024,384]{1,0:T(8,128)(2,1)}, bf16[1024,384]{1,0:T(8,128)(2,1)}, bf16[1024,384]{1,0:T(8,128)(2,1)}, f...) custom-call(s32[2]{0:T(128)} %pad_add_fusion.refs_0_, ...), custom_call_target="tpu_custom_call" | custom-call | flops 20899999744 | tf_op jit(solution)/shard_map/pallas_call | solution.py:584
  95.7 9.2 %all-to-all-done.2 = bf16[4,64,1536]{2,1,0:T(8,128)(2,1)S(1)} async-done(((bf16[4,64,1536]{2,1,0:T(8,128)(2,1)}), bf16[4,64,1536]{2,1,0:T(8,128)(2,1)S(1)}, u32[]{:S(2)}, u32[]{:S(2)}) %all-to-all-start.2) | async-done | bytes 786464 | tf_op jit(solution)/shard_map/all_to_all | solution.py:83
  105.9 15.2 %all_to_all.100 = bf16[4,64,1536]{2,1,0:T(8,128)(2,1)} all-to-all(bf16[4,64,1536]{2,1,0:T(8,128)(2,1)S(1)} %broadcast_in_dim.36), channel_id=1, replica_groups=mesh['fsdp'=2,'context'=4,'tensor'=4] {'tensor'}, dimensions={0} | all-to-all | bytes 1572864 | tf_op jit(solution)/shard_map/all_to_all | solution.py:48
  121.2 8.6 %shard_map.257 = (f32[256,1024]{1,0:T(8,128)}, f32[256,1024]{1,0:T(8,128)}, bf16[256,1536]{1,0:T(8,128)(2,1)}) custom-call(bf16[256,1536]{1,0:T(8,128)(2,1)} %bitcast.71, bf16[2,768,1024]{2,1,0:T(8,128)(2,1)} %wg.11, bf16[2,768,1024]{2,1,0:T(8,128)(2,1)} %wu.11, bf16[2,1024,768]{2,1,0:T(8,128)(2,1)} %wd.11, ...), custom_call_target="tpu_custom_call" | custom-call | flops 7699999744 | tf_op jit(solution)/shard_map/pallas_call | solution.py:651
  129.8 14.2 %all_to_all.101 = bf16[4,64,1536]{2,1,0:T(8,128)(2,1)S(1)} all-to-all(bf16[4,64,1536]{2,1,0:T(8,128)(2,1)} %bitcast.72), channel_id=1, replica_groups=mesh['fsdp'=2,'context'=4,'tensor'=4] {'tensor'}, dimensions={0} | all-to-all | bytes 1572864 | tf_op jit(solution)/shard_map/all_to_all | solution.py:83
  152.4 15.8 %all-to-all-done.5 = bf16[4,64,1536]{2,1,0:T(8,128)(2,1)S(1)} async-done(((bf16[4,64,1536]{2,1,0:T(8,128)(2,1)}), bf16[4,64,1536]{2,1,0:T(8,128)(2,1)S(1)}, u32[]{:S(2)}, u32[]{:S(2)}) %all-to-all-start.5) | async-done | bytes 786464 | tf_op jit(solution)/shard_map/all_to_all | solution.py:48
  169.7 13.5 %collective-permute-done.17.refs_1_.refs_3_ = bf16[64,1536]{1,0:T(8,128)(2,1)S(1)} collective-permute-done((bf16[64,1536]{1,0:T(8,128)(2,1)S(1)}, bf16[64,1536]{1,0:T(8,128)(2,1)S(1)}, u32[]{:S(2)}, u32[]{:S(2)}) %collective-permute-start.17) | collective-permute-done | bytes 196640 | tf_op jit(solution)/shard_map/ppermute | solution.py:25
  194.1 13.0 %collective-permute-done.20.refs_6_ = bf16[64,1536]{1,0:T(8,128)(2,1)S(1)} collective-permute-done((bf16[64,1536]{1,0:T(8,128)(2,1)S(1)}, bf16[64,1536]{1,0:T(8,128)(2,1)S(1)}, u32[]{:S(2)}, u32[]{:S(2)}) %collective-permute-start.20) | collective-permute-done | bytes 196640 | tf_op jit(solution)/shard_map/ppermute | solution.py:25
  209.9 19.2 %shard_map.261 = (bf16[1024,1536]{1,0:T(8,128)(2,1)}, bf16[1024,384]{1,0:T(8,128)(2,1)}, bf16[1024,384]{1,0:T(8,128)(2,1)}, bf16[1024,384]{1,0:T(8,128)(2,1)}, f...) custom-call(s32[2]{0:T(128)} %pad_add_fusion.refs_0_, ...), custom_call_target="tpu_custom_call" | custom-call | flops 20899999744 | tf_op jit(solution)/shard_map/pallas_call | solution.py:584
  233.3 9.5 %all-to-all-done.7 = bf16[4,64,1536]{2,1,0:T(8,128)(2,1)S(1)} async-done(((bf16[4,64,1536]{2,1,0:T(8,128)(2,1)}), bf16[4,64,1536]{2,1,0:T(8,128)(2,1)S(1)}, u32[]{:S(2)}, u32[]{:S(2)}) %all-to-all-start.7) | async-done | bytes 786464 | tf_op jit(solution)/shard_map/all_to_all | solution.py:83
  243.3 14.2 %all_to_all.102 = bf16[4,64,1536]{2,1,0:T(8,128)(2,1)} all-to-all(bf16[4,64,1536]{2,1,0:T(8,128)(2,1)S(1)} %broadcast_in_dim.39), channel_id=1, replica_groups=mesh['fsdp'=2,'context'=4,'tensor'=4] {'tensor'}, dimensions={0} | all-to-all | bytes 1572864 | tf_op jit(solution)/shard_map/all_to_all | solution.py:48
  257.5 8.6 %shard_map.262 = (f32[256,1024]{1,0:T(8,128)}, f32[256,1024]{1,0:T(8,128)}, bf16[256,1536]{1,0:T(8,128)(2,1)}) custom-call(bf16[256,1536]{1,0:T(8,128)(2,1)} %bitcast.73, bf16[2,768,1024]{2,1,0:T(8,128)(2,1)} %wg.11, bf16[2,768,1024]{2,1,0:T(8,128)(2,1)} %wu.11, bf16[2,1024,768]{2,1,0:T(8,128)(2,1)} %wd.11, ...), custom_call_target="tpu_custom_call" | custom-call | flops 7699999744 | tf_op jit(solution)/shard_map/pallas_call | solution.py:651
  266.1 9.3 %shard_map.263 = bf16[256,1536]{1,0:T(8,128)(2,1)} custom-call(bf16[256,1536]{1,0:T(8,128)(2,1)} %maximum_select_fusion.1.g_ref, f32[256,1024]{1,0:T(8,128)} %get-tuple-element.106.gt_ref, f32[256,1024]{1,0:T(8,128)} %get-tuple-element.107.up_ref, bf16[2,768,1024]{2,1,0:T(8,128)(2,1)} %wg.11, bf16[2,768,1024]{2,1,0:T(8,128)(2,1)} %wu.11, ...), custom_call_target="tpu_custom_call" | custom-call | flops 8800000000 | tf_op jit(solution)/shard_map/pallas_call | solution.py:665
  275.4 18.3 %all_to_all.103 = bf16[4,64,1536]{2,1,0:T(8,128)(2,1)S(1)} all-to-all(bf16[4,64,1536]{2,1,0:T(8,128)(2,1)} %bitcast.76), channel_id=1, replica_groups=mesh['fsdp'=2,'context'=4,'tensor'=4] {'tensor'}, dimensions={0} | all-to-all | bytes 1572864 | tf_op jit(solution)/shard_map/all_to_all | solution.py:83
  308.0 10.2 %collective-permute-done.23.refs_1_.refs_3_ = bf16[64,1536]{1,0:T(8,128)(2,1)S(1)} collective-permute-done((bf16[64,1536]{1,0:T(8,128)(2,1)S(1)}, bf16[64,1536]{1,0:T(8,128)(2,1)S(1)}, u32[]{:S(2)}, u32[]{:S(2)}) %collective-permute-start.23) | collective-permute-done | bytes 196640 | tf_op jit(solution)/shard_map/ppermute | solution.py:25
  337.5 33.5 %shard_map.268 = (bf16[1024,1536]{1,0:T(8,128)(2,1)}, bf16[1024,384]{1,0:T(8,128)(2,1)}, bf16[1024,384]{1,0:T(8,128)(2,1)}, bf16[1024,384]{1,0:T(8,128)(2,1)}, b...) custom-call(s32[2]{0:T(128)} %pad_add_fusion.refs_0_, ...), custom_call_target="tpu_custom_call" | custom-call | flops 36300001280 | tf_op jit(solution)/shard_map/pallas_call | solution.py:614
  371.0 12.0 %all_to_all.104 = bf16[4,64,1536]{2,1,0:T(8,128)(2,1)S(1)} all-to-all(bf16[4,64,1536]{2,1,0:T(8,128)(2,1)} %bitcast.70), channel_id=1, replica_groups=mesh['fsdp'=2,'context'=4,'tensor'=4] {'tensor'}, dimensions={0} | all-to-all | bytes 1572864 | tf_op jit(solution)/shard_map/all_to_all | solution.py:83
  385.0 20.9 %all_to_all.105 = bf16[4,64,1536]{2,1,0:T(8,128)(2,1)} all-to-all(bf16[4,64,1536]{2,1,0:T(8,128)(2,1)S(1)} %broadcast_in_dim.42), channel_id=1, replica_groups=mesh['fsdp'=2,'context'=4,'tensor'=4] {'tensor'}, dimensions={0} | all-to-all | bytes 1572864 | tf_op jit(solution)/shard_map/all_to_all | solution.py:48
  405.9 9.3 %shard_map.271 = bf16[256,1536]{1,0:T(8,128)(2,1)} custom-call(bf16[256,1536]{1,0:T(8,128)(2,1)} %bitcast.74, f32[256,1024]{1,0:T(8,128)} %get-tuple-element.116.gt_ref, f32[256,1024]{1,0:T(8,128)} %get-tuple-element.117.up_ref, bf16[2,768,1024]{2,1,0:T(8,128)(2,1)} %wg.11, bf16[2,768,1024]{2,1,0:T(8,128)(2,1)} %wu.11, bf16[2,1024,768]{2,1,0:T(8,128)(2,1)} %wd.11, ...), custom_call_target="tpu_custom_call" | custom-call | flops 8800000000 | tf_op jit(solution)/shard_map/pallas_call | solution.py:665
  415.2 13.1 %all_to_all.106 = bf16[4,64,1536]{2,1,0:T(8,128)(2,1)S(1)} all-to-all(bf16[4,64,1536]{2,1,0:T(8,128)(2,1)} %bitcast.75), channel_id=1, replica_groups=mesh['fsdp'=2,'context'=4,'tensor'=4] {'tensor'}, dimensions={0} | all-to-all | bytes 1572864 | tf_op jit(solution)/shard_map/all_to_all | solution.py:83
  442.1 10.5 %collective-permute-done.29.refs_0_ = bf16[64,1536]{1,0:T(8,128)(2,1)S(1)} collective-permute-done((bf16[64,1536]{1,0:T(8,128)(2,1)S(1)}, bf16[64,1536]{1,0:T(8,128)(2,1)S(1)}, u32[]{:S(2)}, u32[]{:S(2)}) %collective-permute-start.29) | collective-permute-done | bytes 196640 | tf_op jit(solution)/shard_map/ppermute | solution.py:25
  458.5 21.1 %shard_map.273 = (bf16[1024,1024]{1,0:T(8,128)(2,1)}, bf16[1024,1024]{1,0:T(8,128)(2,1)}, bf16[1024,1024]{1,0:T(8,128)(2,1)}, bf16[768,1024]{1,0:T(8,128)(2,1)},...) custom-call(bf16[1024,1536]{1,0:T(8,128)(2,1)} %all-gather.11.cloned.1.call-done.b_ref, ...), custom_call_target="tpu_custom_call" | custom-call | flops 26400000000 | tf_op jit(solution)/shard_map/pallas_call | solution.py:682
  487.0 33.9 %shard_map.275 = (bf16[1024,1536]{1,0:T(8,128)(2,1)}, bf16[1024,384]{1,0:T(8,128)(2,1)}, bf16[1024,384]{1,0:T(8,128)(2,1)}, bf16[1024,384]{1,0:T(8,128)(2,1)}, b...) custom-call(s32[2]{0:T(128)} %pad_add_fusion.refs_0_, ...), custom_call_target="tpu_custom_call" | custom-call | flops 36300001280 | tf_op jit(solution)/shard_map/pallas_call | solution.py:614
  538.5 8.5 %shard_map.277 = (bf16[768,384]{1,0:T(8,128)(2,1)}, bf16[768,384]{1,0:T(8,128)(2,1)}, bf16[768,384]{1,0:T(8,128)(2,1)}, bf16[768,384]{1,0:T(8,128)(2,1)}, bf16[7...) custom-call(bf16[1024,1536]{1,0:T(8,128)(2,1)} %get-tuple-element.140.refs_0_, ...), custom_call_target="tpu_custom_call" | custom-call | flops 7699999744 | tf_op jit(solution)/shard_map/pallas_call | solution.py:747
  557.1 10.3 %all-to-all-done.19 = f32[16,1,6144]{2,1,0:T(1,128)S(1)} async-done(((f32[16,1,6144]{2,1,0:T(1,128)}), f32[16,1,6144]{2,1,0:T(1,128)S(1)}, u32[]{:S(2)}, u32[]{:S(2)}) %all-to-all-start.19) | async-done | bytes 393248 | tf_op jit(solution)/shard_map/all_to_all | solution.py:48
  571.3 21.0 %shard_map.269 = (bf16[1024,1024]{1,0:T(8,128)(2,1)}, bf16[1024,1024]{1,0:T(8,128)(2,1)}, bf16[1024,1024]{1,0:T(8,128)(2,1)}, bf16[768,1024]{1,0:T(8,128)(2,1)},...) custom-call(bf16[1024,1536]{1,0:T(8,128)(2,1)} %all-gather.7.cloned.1.call-done.refs_1_.b_ref, ...), custom_call_target="tpu_custom_call" | custom-call | flops 26400000000 | tf_op jit(solution)/shard_map/pallas_call | solution.py:682
  592.4 8.5 %shard_map.276 = (bf16[768,384]{1,0:T(8,128)(2,1)}, bf16[768,384]{1,0:T(8,128)(2,1)}, bf16[768,384]{1,0:T(8,128)(2,1)}, bf16[768,384]{1,0:T(8,128)(2,1)}, bf16[7...) custom-call(bf16[1024,1536]{1,0:T(8,128)(2,1)} %get-tuple-element.126.refs_0_, ...), custom_call_target="tpu_custom_call" | custom-call | flops 7699999744 | tf_op jit(solution)/shard_map/pallas_call | solution.py:747
  602.6 12.0 %shard_map.281 = (f32[2,768,1024]{2,1,0:T(8,128)}, f32[2,768,1024]{2,1,0:T(8,128)}, f32[2,1024,768]{2,1,0:T(8,128)}) custom-call(bf16[1024,1536]{1,0:T(8,128)(2,1)} %all-gather.11.cloned.1.call-done.b_ref, bf16[1024,1536]{1,0:T(8,128)(2,1)} %all-gather.5.cloned.1.call-done.refs_1_.g_ref, ...), custom_call_target="tpu_custom_call", output_to_operand_aliasing={{0}: (8, {}), {1}: (9, {}), {2}: (10, {})} | custom-call | flops 9900000256 | tf_op jit(solution)/shard_map/pallas_call | solution.py:707
  621.0 9.5 %shard_map.279 = (f32[2,768,384]{2,1,0:T(8,128)}, f32[2,768,384]{2,1,0:T(8,128)}, f32[2,768,384]{2,1,0:T(8,128)}, f32[2,768,384]{2,1,0:T(8,128)}, f32[768,128]{1,0:T(8,128)}, /*index=5*/f32[2,384,768]{2,1,0:T(8,128)}) custom-call(bf16[1024,1536]{1,0:T(8,128)(2,1)} %get-tuple-element.14, ...), custom_call_target="tpu_custom_call", output_to_operand_aliasing={{0}: (14, {}), {1}: (15, {}), {2}: (16, {}), {3}: (17, {}),... | custom-call | flops 7699999744 | tf_op jit(solution)/shard_map/pallas_call | solution.py:747
  635.1 9.5 %shard_map.280 = (f32[2,768,384]{2,1,0:T(8,128)}, f32[2,768,384]{2,1,0:T(8,128)}, f32[2,768,384]{2,1,0:T(8,128)}, f32[2,768,384]{2,1,0:T(8,128)}, f32[768,128]{1,0:T(8,128)}, /*index=5*/f32[2,384,768]{2,1,0:T(8,128)}) custom-call(bf16[1024,1536]{1,0:T(8,128)(2,1)} %get-tuple-element.12, ...), custom_call_target="tpu_custom_call", output_to_operand_aliasing={{0}: (14, {}), {1}: (15, {}), {2}: (16, {}), {3}: (17, {}),... | custom-call | flops 7699999744 | tf_op jit(solution)/shard_map/pallas_call | solution.py:747
  646.5 11.8 %shard_map.282 = (f32[2,768,1024]{2,1,0:T(8,128)}, f32[2,768,1024]{2,1,0:T(8,128)}, f32[2,1024,768]{2,1,0:T(8,128)}) custom-call(bf16[1024,1536]{1,0:T(8,128)(2,1)} %all-gather.7.cloned.1.call-done.refs_1_.b_ref, bf16[1024,1536]{1,0:T(8,128)(2,1)} %all-gather.9.cloned.1.call-done.g_ref, ...), custom_call_target="tpu_custom_call", output_to_operand_aliasing={{0}: (8, {}), {1}: (9, {}), {2}: (10, {})} | custom-call | flops 9900000256 | tf_op jit(solution)/shard_map/pallas_call | solution.py:707
  (353 shorter events, 193.8 us)
Async XLA Ops:
  11.4 40.1 %collective-permute-start.1 = (bf16[256,1536]{1,0:T(8,128)(2,1)S(1)}, bf16[256,1536]{1,0:T(8,128)(2,1)}, u32[]{:S(2)}, u32[]{:S(2)}) collective-permute-start(bf16[256,1536]{1,0:T(8,128)(2,1)S(1)} %multiply_convert_fusion.refs_1_), channel_id=1, source_target_pairs={{0,4},{4,0},{8,12},{12,8},{1,5},{5,1},{9,13},{13,9},{2,6},{6,2},{1... | collective-permute-start | bytes 2359304 | tf_op jit(solution)/shard_map/ppermute | solution.py:25
  14.7 24.3 %collective-permute-start.2 = (bf16[64,1536]{1,0:T(8,128)(2,1)}, bf16[64,1536]{1,0:T(8,128)(2,1)S(1)}, u32[]{:S(2)}, u32[]{:S(2)}) collective-permute-start(bf16[64,1536]{1,0:T(8,128)(2,1)} %constant_dynamic-slice_fusion.1), channel_id=1, source_target_pairs={{0,8},{4,12},{8,0},{12,4},{1,9},{5,13},{9,1},{13,5},{2,10},{6,14},... | collective-permute-start | bytes 589832 | tf_op jit(solution)/shard_map/ppermute | solution.py:25
  17.9 21.1 %all-to-all-start = ((s32[4,1,256]{2,1,0:T(1,128)}), s32[4,1,256]{2,1,0:T(1,128)}, u32[]{:S(2)}, u32[]{:S(2)}) async-start(s32[4,1,256]{2,1,0:T(1,128)} %broadcast_in_dim.33), calls=%async_computation | async-start | bytes 8192 | tf_op jit(solution)/shard_map/all_to_all | solution.py:48
  21.7 20.9 %collective-permute-start.12 = (bf16[2,768,6]{1,0,2:T(2,128)(2,1)}, bf16[2,768,6]{1,0,2:T(2,128)(2,1)}, u32[]{:S(2)}, u32[]{:S(2)}) collective-permute-start(bf16[2,768,6]{1,0,2:T(2,128)(2,1)} %param.22), channel_id=1, source_target_pairs={{0,16},{16,0},{1,17},{17,1},{2,18},{18,2},{3,19},{19,3},{4,20},{20... | collective-permute-start | bytes 55304 | tf_op jit(solution)/shard_map/ppermute | solution.py:25
  22.4 20.8 %collective-permute-start.6 = (bf16[64,1536]{1,0:T(8,128)(2,1)}, bf16[64,1536]{1,0:T(8,128)(2,1)S(1)}, u32[]{:S(2)}, u32[]{:S(2)}) collective-permute-start(bf16[64,1536]{1,0:T(8,128)(2,1)} %constant_dynamic-slice_fusion.1), channel_id=1, source_target_pairs={{0,12},{4,8},{8,4},{12,0},{1,13},{5,9},{9,5},{13,1},{2,14},{6,10},... | collective-permute-start | bytes 589832 | tf_op jit(solution)/shard_map/ppermute | solution.py:25
  43.3 20.0 %collective-permute-start.7 = (bf16[2,768,384]{2,1,0:T(8,128)(2,1)}, bf16[2,768,384]{2,1,0:T(8,128)(2,1)}, u32[]{:S(2)}, u32[]{:S(2)}) collective-permute-start(bf16[2,768,384]{2,1,0:T(8,128)(2,1)} %refs_4_.1), channel_id=1, source_target_pairs={{0,16},{16,0},{1,17},{17,1},{2,18},{18,2},{3,19},{19,3},{4,20},{20... | collective-permute-start | bytes 3538952 | tf_op jit(solution)/shard_map/ppermute | solution.py:25
  51.1 19.4 %collective-permute-start.10 = (bf16[2,768,384]{2,1,0:T(8,128)(2,1)}, bf16[2,768,384]{2,1,0:T(8,128)(2,1)}, u32[]{:S(2)}, u32[]{:S(2)}) collective-permute-start(bf16[2,768,384]{2,1,0:T(8,128)(2,1)} %refs_7_.1), channel_id=1, source_target_pairs={{0,16},{16,0},{1,17},{17,1},{2,18},{18,2},{3,19},{19,3},{4,20},{20... | collective-permute-start | bytes 3538952 | tf_op jit(solution)/shard_map/ppermute | solution.py:25
  63.3 57.8 %collective-permute-start.13 = (bf16[2,768,1024]{2,1,0:T(8,128)(2,1)}, bf16[2,768,1024]{2,1,0:T(8,128)(2,1)}, u32[]{:S(2)}, u32[]{:S(2)}) collective-permute-start(bf16[2,768,1024]{2,1,0:T(8,128)(2,1)} %wg.11), channel_id=1, source_target_pairs={{0,16},{16,0},{1,17},{17,1},{2,18},{18,2},{3,19},{19,3},{4,20},{20... | collective-permute-start | bytes 9437192 | tf_op jit(solution)/shard_map/ppermute | solution.py:25
  63.7 57.4 %collective-permute-start.14 = (bf16[2,768,1024]{2,1,0:T(8,128)(2,1)}, bf16[2,768,1024]{2,1,0:T(8,128)(2,1)}, u32[]{:S(2)}, u32[]{:S(2)}) collective-permute-start(bf16[2,768,1024]{2,1,0:T(8,128)(2,1)} %wu.11), channel_id=1, source_target_pairs={{0,16},{16,0},{1,17},{17,1},{2,18},{18,2},{3,19},{19,3},{4,20},{20... | collective-permute-start | bytes 9437192 | tf_op jit(solution)/shard_map/ppermute | solution.py:25
  63.8 57.3 %collective-permute-start.15 = (bf16[2,1024,768]{2,1,0:T(8,128)(2,1)}, bf16[2,1024,768]{2,1,0:T(8,128)(2,1)}, u32[]{:S(2)}, u32[]{:S(2)}) collective-permute-start(bf16[2,1024,768]{2,1,0:T(8,128)(2,1)} %wd.11), channel_id=1, source_target_pairs={{0,16},{16,0},{1,17},{17,1},{2,18},{18,2},{3,19},{19,3},{4,20},{20... | collective-permute-start | bytes 9437192 | tf_op jit(solution)/shard_map/ppermute | solution.py:25
  94.0 100.1 %all-gather.5.cloned.1.call-start = ((), (), s32[]{:S(2)}) async-start(), calls=%async_computation.20 | async-start | bytes 3342336 | tf_op jit(solution)/shard_map/all_gather | solution.py:52
  145.7 22.5 %all-to-all-start.5 = ((bf16[4,64,1536]{2,1,0:T(8,128)(2,1)}), bf16[4,64,1536]{2,1,0:T(8,128)(2,1)S(1)}, u32[]{:S(2)}, u32[]{:S(2)}) async-start(bf16[4,64,1536]{2,1,0:T(8,128)(2,1)} %broadcast_in_dim.37), calls=%async_computation.5 | async-start | bytes 1572864 | tf_op jit(solution)/shard_map/all_to_all | solution.py:48
  149.2 20.5 %collective-permute-start.21 = (bf16[64,1536]{1,0:T(8,128)(2,1)S(1)}, bf16[64,1536]{1,0:T(8,128)(2,1)S(1)}, u32[]{:S(2)}, u32[]{:S(2)}) collective-permute-start(bf16[64,1536]{1,0:T(8,128)(2,1)S(1)} %multiply_convert_fusion.2), channel_id=1, source_target_pairs={{0,12},{4,8},{8,4},{12,0},{1,13},{5,9},{9,5},{13,1},{2,14},{6,10},... | collective-permute-start | bytes 589832 | tf_op jit(solution)/shard_map/ppermute | solution.py:25
  152.4 30.8 %collective-permute-start.17 = (bf16[64,1536]{1,0:T(8,128)(2,1)S(1)}, bf16[64,1536]{1,0:T(8,128)(2,1)S(1)}, u32[]{:S(2)}, u32[]{:S(2)}) collective-permute-start(bf16[64,1536]{1,0:T(8,128)(2,1)S(1)} %multiply_convert_fusion.2), channel_id=1, source_target_pairs={{0,8},{4,12},{8,0},{12,4},{1,9},{5,13},{9,1},{13,5},{2,10},{6,14},... | collective-permute-start | bytes 589832 | tf_op jit(solution)/shard_map/ppermute | solution.py:25
  168.2 40.8 %collective-permute-start.16 = (bf16[256,1536]{1,0:T(8,128)(2,1)S(1)}, bf16[256,1536]{1,0:T(8,128)(2,1)}, u32[]{:S(2)}, u32[]{:S(2)}) collective-permute-start(bf16[256,1536]{1,0:T(8,128)(2,1)S(1)} %bitcast.65), channel_id=1, source_target_pairs={{0,4},{4,0},{8,12},{12,8},{1,5},{5,1},{9,13},{13,9},{2,6},{6,2},{1... | collective-permute-start | bytes 2359304 | tf_op jit(solution)/shard_map/ppermute | solution.py:25
  185.8 23.2 %all-to-all-start.6 = ((bf16[4,64,1536]{2,1,0:T(8,128)(2,1)}), bf16[4,64,1536]{2,1,0:T(8,128)(2,1)S(1)}, u32[]{:S(2)}, u32[]{:S(2)}) async-start(bf16[4,64,1536]{2,1,0:T(8,128)(2,1)} %broadcast_in_dim.38), calls=%async_computation.6 | async-start | bytes 1572864 | tf_op jit(solution)/shard_map/all_to_all | solution.py:48
  232.6 101.5 %all-gather.7.cloned.1.call-start = ((), (), s32[]{:S(2)}) async-start(), calls=%async_computation.22 | async-start | bytes 3342336 | tf_op jit(solution)/shard_map/all_gather | solution.py:52
  308.0 29.5 %collective-permute-start.24 = (bf16[256,1536]{1,0:T(8,128)(2,1)}, bf16[256,1536]{1,0:T(8,128)(2,1)}, u32[]{:S(2)}, u32[]{:S(2)}) collective-permute-start(bf16[256,1536]{1,0:T(8,128)(2,1)} %bitcast.19.refs_1_), channel_id=1, source_target_pairs={{0,4},{4,0},{8,12},{12,8},{1,5},{5,1},{9,13},{13,9},{2,6},{6,2},{1... | collective-permute-start | bytes 2359304 | tf_op jit(solution)/shard_map/ppermute | solution.py:25
  325.1 133.5 %all-gather.11.cloned.1.call-start = ((), (), s32[]{:S(2)}) async-start(), calls=%async_computation.24 | async-start | bytes 3342336 | tf_op jit(solution)/shard_map/all_gather | solution.py:52
  429.8 22.8 %all-to-all-start.15 = ((bf16[4,64,1536]{2,1,0:T(8,128)(2,1)}), bf16[4,64,1536]{2,1,0:T(8,128)(2,1)S(1)}, u32[]{:S(2)}, u32[]{:S(2)}) async-start(bf16[4,64,1536]{2,1,0:T(8,128)(2,1)} %broadcast_in_dim.43), calls=%async_computation.15 | async-start | bytes 1572864 | tf_op jit(solution)/shard_map/all_to_all | solution.py:48
  433.3 138.0 %all-gather.9.cloned.1.call-start = ((), (), s32[]{:S(2)}) async-start(), calls=%async_computation.23 | async-start | bytes 3342336 | tf_op jit(solution)/shard_map/all_gather | solution.py:52
  454.0 31.7 %all-to-all-start.16 = ((bf16[4,128,1536]{2,1,0:T(8,128)(2,1)}), bf16[4,128,1536]{2,1,0:T(8,128)(2,1)S(1)}, u32[]{:S(2)}, u32[]{:S(2)}) async-start(bf16[4,128,1536]{2,1,0:T(8,128)(2,1)} %broadcast_in_dim.44), calls=%async_computation.16 | async-start | bytes 3145728 | tf_op jit(solution)/shard_map/all_to_all | solution.py:48
  457.9 27.9 %collective-permute-start.28 = (bf16[256,1536]{1,0:T(8,128)(2,1)S(1)}, bf16[256,1536]{1,0:T(8,128)(2,1)}, u32[]{:S(2)}, u32[]{:S(2)}) collective-permute-start(bf16[256,1536]{1,0:T(8,128)(2,1)S(1)} %bitcast.63), channel_id=1, source_target_pairs={{0,4},{4,0},{8,12},{12,8},{1,5},{5,1},{9,13},{13,9},{2,6},{6,2},{1... | collective-permute-start | bytes 2359304 | tf_op jit(solution)/shard_map/ppermute | solution.py:25
  524.4 90.3 %all-reduce.4.cloned.1.call-start = ((), (), s32[]{:S(2)}) async-start(), calls=%async_computation.21 | async-start | bytes 1572864 | tf_op jit(solution)/shard_map/psum | solution.py:904
  527.2 27.9 %collective-permute-start.47 = (f32[6]{0:T(128)S(1)}, f32[6]{0:T(128)S(1)}, u32[]{:S(2)}, u32[]{:S(2)}) collective-permute-start(f32[6]{0:T(128)S(1)} %bitcast.79), channel_id=1, source_target_pairs={{0,16},{16,0},{1,17},{17,1},{2,18},{18,2},{3,19},{19,3},{4,20},{20... | collective-permute-start | bytes 80 | tf_op jit(solution)/shard_map/ppermute | solution.py:25
  547.0 53.8 %collective-permute-start.41 = (bf16[768,128]{1,0:T(8,128)(2,1)}, bf16[768,128]{1,0:T(8,128)(2,1)}, u32[]{:S(2)}, u32[]{:S(2)}) collective-permute-start(bf16[768,128]{1,0:T(8,128)(2,1)} %get-tuple-element.152), channel_id=1, source_target_pairs={{0,16},{16,0},{1,17},{17,1},{2,18},{18,2},{3,19},{19,3},{4,20},{20... | collective-permute-start | bytes 589832 | tf_op jit(solution)/shard_map/ppermute | solution.py:25
  547.1 54.0 %collective-permute-start.37 = (bf16[768,384]{1,0:T(8,128)(2,1)}, bf16[768,384]{1,0:T(8,128)(2,1)}, u32[]{:S(2)}, u32[]{:S(2)}) collective-permute-start(bf16[768,384]{1,0:T(8,128)(2,1)} %get-tuple-element.148), channel_id=1, source_target_pairs={{0,16},{16,0},{1,17},{17,1},{2,18},{18,2},{3,19},{19,3},{4,20},{20... | collective-permute-start | bytes 1769480 | tf_op jit(solution)/shard_map/ppermute | solution.py:25
  555.3 46.1 %collective-permute-start.49 = (bf16[768,1024]{1,0:T(8,128)(2,1)}, bf16[768,1024]{1,0:T(8,128)(2,1)S(1)}, u32[]{:S(2)}, u32[]{:S(2)}) collective-permute-start(bf16[768,1024]{1,0:T(8,128)(2,1)} %get-tuple-element.178), channel_id=1, source_target_pairs={{0,16},{16,0},{1,17},{17,1},{2,18},{18,2},{3,19},{19,3},{4,20},{20... | collective-permute-start | bytes 4718600 | tf_op jit(solution)/shard_map/ppermute | solution.py:25
  555.8 45.8 %collective-permute-start.50 = (bf16[768,1024]{1,0:T(8,128)(2,1)}, bf16[768,1024]{1,0:T(8,128)(2,1)}, u32[]{:S(2)}, u32[]{:S(2)}) collective-permute-start(bf16[768,1024]{1,0:T(8,128)(2,1)} %get-tuple-element.179), channel_id=1, source_target_pairs={{0,16},{16,0},{1,17},{17,1},{2,18},{18,2},{3,19},{19,3},{4,20},{20... | collective-permute-start | bytes 4718600 | tf_op jit(solution)/shard_map/ppermute | solution.py:25
  570.3 31.8 %collective-permute-start.51 = (bf16[1024,768]{1,0:T(8,128)(2,1)}, bf16[1024,768]{1,0:T(8,128)(2,1)}, u32[]{:S(2)}, u32[]{:S(2)}) collective-permute-start(bf16[1024,768]{1,0:T(8,128)(2,1)} %get-tuple-element.180), channel_id=1, source_target_pairs={{0,16},{16,0},{1,17},{17,1},{2,18},{18,2},{3,19},{19,3},{4,20},{20... | collective-permute-start | bytes 4718600 | tf_op jit(solution)/shard_map/ppermute | solution.py:25
  614.7 19.2 %collective-permute-start.43 = (bf16[768,1024]{1,0:T(8,128)(2,1)}, bf16[768,1024]{1,0:T(8,128)(2,1)S(1)}, u32[]{:S(2)}, u32[]{:S(2)}) collective-permute-start(bf16[768,1024]{1,0:T(8,128)(2,1)} %get-tuple-element.164), channel_id=1, source_target_pairs={{0,16},{16,0},{1,17},{17,1},{2,18},{18,2},{3,19},{19,3},{4,20},{20... | collective-permute-start | bytes 4718600 | tf_op jit(solution)/shard_map/ppermute | solution.py:25
  614.9 19.0 %collective-permute-start.44 = (bf16[768,1024]{1,0:T(8,128)(2,1)}, bf16[768,1024]{1,0:T(8,128)(2,1)}, u32[]{:S(2)}, u32[]{:S(2)}) collective-permute-start(bf16[768,1024]{1,0:T(8,128)(2,1)} %get-tuple-element.165), channel_id=1, source_target_pairs={{0,16},{16,0},{1,17},{17,1},{2,18},{18,2},{3,19},{19,3},{4,20},{20... | collective-permute-start | bytes 4718600 | tf_op jit(solution)/shard_map/ppermute | solution.py:25
  (96 other events, 1120.8 us)
Sparse Core Ops, SparseCore 0:
  98.2 87.2 all-gather.4
  236.2 83.3 all-gather.6
  334.1 83.0 all-gather.10
  440.3 73.0 all-gather.8
  528.5 55.2 all-reduce.3

commit v8 on v7

--- a/solution.py
+++ b/solution.py
@@ -836,12 +836,8 @@
             place, a_parts, layer, w4, t4, w_attn_out, to, forget_weights,
             bias[layer : layer + 1], doc_start, piece_len,
         )
-        if shared_rows:
-            token = a_parts[-1]
-            if layer == 0:
-                g_last = sequence_rows(after(own_block(cotangent_rows), token))
-            else:
-                saved[-1]["b_rows"] = sequence_rows(after(saved[-1]["b_shard"], token))
+        if shared_rows and layer == 0:
+            g_last = sequence_rows(after(own_block(cotangent_rows), a_parts[-1]))
         mixed = hidden + received_sum(sends)
         inverse_two = inverse_rms(mixed)
         b_shard = (mixed * inverse_two * gain_two).astype(bf16)
@@ -874,26 +870,54 @@
         values = ffn_theirs(s["b_rows"], s["g_rows"], layer, w3, t3, *tokens)
         s.update(values=values[:3], ffn_received=[other(x) for x in values[3:]])
 
+    def ffn_mine_of(layer, *tokens):
+        s = saved[layer]
+        received = s["ffn_received"]
+        results[5:] = ffn_mine(layer, s["b_rows"], s["g_rows"], s["values"], received, results[5:], *tokens)
+
+    def attention_theirs_of(layer, *tokens):
+        s = saved[layer]
+        s["theirs"] = attention_grads(layer, *s["grads"], tokens=tokens)
+        s["received"] = [other(x) for x in s["theirs"]]
+        bias_grad = jnp.sum(s["grads"][2].astype(f32), axis=0)[:heads]
+        small[1][layer] = bias_grad + other(bias_grad)
+
+    def attention_mine_of(layer, *tokens):
+        s = saved[layer]
+        found = attention_grads(layer, *s["grads"], s["received"], results[:5], tokens)
+        results[:5] = [*found[:4], found[5]]
+        small[0][layer] = found[4][:, :heads]
+
     for layer in reversed(range(layers)):
         s = saved[layer]
         gain_one, gain_two = gains[layer], gains[layers + layer]
+        tokens = ()
         if layer == last:
             g = cotangent_rows
+            if shared_rows:
+                s.update(b_rows=sequence_rows(s["b_shard"]), g_rows=g_last)
         else:
             g_shard = grad.astype(bf16)
             g = gathered(g_shard, "tensor")
+            tokens = (saved[layer + 1]["theirs"][0],)
             if shared_rows:
-                s["g_rows"] = sequence_rows(g_shard)
-        sends = ffn_backward(g, s["gt"], s["up"], layer, w3, t3)
+                s.update(b_rows=sequence_rows(after(s["b_shard"], token)), g_rows=sequence_rows(g_shard))
+        if not shared_rows:
+            s.update(b_rows=s["b"], g_rows=g)
+        sends = ffn_backward(g, s["gt"], s["up"], layer, w3, t3, *tokens)
         back, gain_grads[layers + layer] = norm_back(received_sum(sends), s["mixed"], s["inverse_two"], gain_two)
         grad_mixed = grad + back
-        y_parts, y_far = all_rows(grad_mixed.astype(bf16), together=layer < last)
-        kept = s["kept"]
-        if layer == last and shared_rows:
-            kept = (*kept[:-1], after(kept[-1], *[x["b_rows"] for x in saved[:-1]]))
-        if layer < last:
-            ffn_theirs_of(layer + 1, *y_far)
-            kept = (*kept[:-1], after(kept[-1], saved[layer + 1]["values"][0]))
+        y_parts, y_far = all_rows(grad_mixed.astype(bf16), together=True)
+        if layer == last:
+            ffn_theirs_of(layer, *y_far)
+            tokens = (s["values"][0],)
+        else:
+            if layer + 1 < last:
+                ffn_theirs_of(layer + 1)
+            attention_mine_of(layer + 1)
+            ffn_mine_of(layer + 1)
+            tokens = (results[0], results[5])
+        kept = (*s["kept"][:-1], after(s["kept"][-1], *tokens))
         y, (dq, dk, dv, dg, u, dz), sends = attention_backward(
             place, y_parts, layer, w4, t4, w_attn_out, to, w_forget_full[layer], kept, doc_start, piece_len,
         )
@@ -902,35 +926,16 @@
             block_sum = own_block(last_sends).astype(f32) + s["mixed"]
             with_rows = lax.dynamic_update_slice_in_dim(last_sends, block_sum.astype(bf16), t * block, 0)
             output = lax.psum(after(with_rows, token), "tensor")
-        if not shared_rows:
-            s.update(b_rows=s["b"], g_rows=g)
-        elif layer == last:
-            s.update(b_rows=sequence_rows(after(s["b_shard"], token)), g_rows=g_last)
+        s["grads"] = (s["a"], (dq, dk, dv, dg), dz, u, y)
+        if layer > 0:
+            attention_theirs_of(layer)
         back, gain_grads[layer] = norm_back(received_sum(sends), s["hidden"], s["inverse_one"], gain_one)
         grad = grad_mixed + back
-        s.update(u=u, y=y, d=(dq, dk, dv, dg), dz=dz, y_far=y_far)
-
-    def ffn_mine_of(layer, *tokens):
-        s = saved[layer]
-        received = s["ffn_received"]
-        results[5:] = ffn_mine(layer, s["b_rows"], s["g_rows"], s["values"], received, results[5:], *tokens)
-
-    def attention_grads_of(layer, tokens=(), mine_tokens=()):
-        s = saved[layer]
-        parts = (s["a"], s["d"], s["dz"], s["u"], s["y"])
-        theirs = attention_grads(layer, *parts, tokens=tokens)
-        found = attention_grads(layer, *parts, [other(x) for x in theirs], results[:5], mine_tokens)
-        results[:5] = [*found[:4], found[5]]
-        bias_grad = jnp.sum(s["dz"].astype(f32), axis=0)[:heads]
-        small[0][layer] = found[4][:, :heads]
-        small[1][layer] = bias_grad + other(bias_grad)
-
-    ffn_theirs_of(0)
-    tokens = (saved[0]["values"][0], grad)
-    for layer in reversed(range(1, layers)):
-        attention_grads_of(layer, (), tokens)
-        ffn_mine_of(layer, *tokens)
-    attention_grads_of(0, tokens, saved[0]["ffn_received"])
+
+    if layers > 1:
+        ffn_theirs_of(0)
+    attention_theirs_of(0, saved[0]["values"][0], grad)
+    attention_mine_of(0, *saved[0]["ffn_received"])
     ffn_mine_of(0)
     if not shared_rows:
         results[5:] = [lax.psum(x, "context") for x in results[5:]]

time: 675 us -> 686 us (1.016)
  starting transfers between devices: 92.1 us -> 125 us
  blocking collectives: 108 us -> 89.5 us
  waiting for transfers between devices: 152 us -> 139 us
    ppermute x52 -> x49, starting transfers between devices: 41.9 us -> 69.8 us  [swap(): return lax.ppermute(x, axis, [(i, i ^ k) for i in range(n)])]
    all_to_all x3 -> x2, blocking collectives: 50.2 us -> 26.9 us  [gathered(): lax.all_to_all(copies, axis, 0, 0, tiled=True)]
    all_to_all x10 -> x11, waiting for transfers between devices: 55.5 us -> 41.1 us  [gathered(): lax.all_to_all(copies, axis, 0, 0, tiled=True)]
    all_to_all x10 -> x11, starting transfers between devices: 39 us -> 43 us  [gathered(): lax.all_to_all(copies, axis, 0, 0, tiled=True)]
    ppermute x52 -> x49, waiting for transfers between devices: 72 us -> 74.7 us  [swap(): return lax.ppermute(x, axis, [(i, i ^ k) for i in range(n)])]
  transfers between devices with their start and end apart: 70 -> 68, of which waited for: 27 -> 20; matrix products, arithmetic and copies ran while one was open for 6% -> 7% of each run, Pallas kernels for 31% -> 30%
where the time goes in v8:
time: 686 us; the launch traced here: 676 us
  Pallas kernels  244 us (36%)
  waiting for transfers between devices  139 us (20%)
  starting transfers between devices  125 us (18%)
  blocking collectives  89.5 us (13%)
  local copies, waits for them, and re-layouts  39.6 us (6%)
  other arithmetic  24.2 us (4%)
  between operations  14.9 us (2%)
    ppermute x49, waiting for transfers between devices, swap(): return lax.ppermute(x, axis, [(i, i ^ k) for i in range(n)])  74.7 us
    ppermute x49, starting transfers between devices, swap(): return lax.ppermute(x, axis, [(i, i ^ k) for i in range(n)])  69.8 us
    pallas_call x2, Pallas kernels, attention_backward(): pl.pallas_call(functools.partial(backward_kernel, len(parts), piece_len,...  67.8 us
    all_to_all x4, blocking collectives, received_sum(): lax.all_to_all(sends.reshape(count, -1, sends.shape[1]), 'tensor', 0, 0,...  62.7 us
    all_to_all x11, starting transfers between devices, gathered(): lax.all_to_all(copies, axis, 0, 0, tiled=True)  43 us
    pallas_call x2, Pallas kernels, ffn_theirs(): pl.pallas_call(ffn_theirs_kernel, grid=(inner // hidden_block,), in_specs...  42.1 us
    all_to_all x11, waiting for transfers between devices, gathered(): lax.all_to_all(copies, axis, 0, 0, tiled=True)  41.1 us
    pallas_call x2, Pallas kernels, forward_own(): pl.pallas_call(functools.partial(forward_own_kernel, len(parts), piece_le...  38.3 us
  transfers between devices with their start and end apart: 68, of which 20 were waited for; matrix products, arithmetic and copies ran while one was open for 7% of the time, Pallas kernels for 30%

profile of v8, /device:TPU:0, one launch (start us, length us, event | category | flops | bytes accessed | tf_op | source)
XLA Modules:
  0.0 675.6 jit_solution(13063441752576834239)
XLA Ops:
  26.7 13.1 %all-to-all-done = s32[4,1,256]{2,1,0:T(1,128)} async-done(((s32[4,1,256]{2,1,0:T(1,128)}), s32[4,1,256]{2,1,0:T(1,128)}, u32[]{:S(2)}, u32[]{:S(2)}) %all-to-all-start) | async-done | bytes 4128 | tf_op jit(solution)/shard_map/all_to_all | solution.py:48
  72.3 19.2 %shard_map.256 = (bf16[1024,1536]{1,0:T(8,128)(2,1)}, bf16[1024,384]{1,0:T(8,128)(2,1)}, bf16[1024,384]{1,0:T(8,128)(2,1)}, bf16[1024,384]{1,0:T(8,128)(2,1)}, f...) custom-call(s32[2]{0:T(128)} %pad_add_fusion.refs_0_, ...), custom_call_target="tpu_custom_call" | custom-call | flops 20899999744 | tf_op jit(solution)/shard_map/pallas_call | solution.py:584
  96.7 9.2 %all-to-all-done.2 = bf16[4,64,1536]{2,1,0:T(8,128)(2,1)S(1)} async-done(((bf16[4,64,1536]{2,1,0:T(8,128)(2,1)}), bf16[4,64,1536]{2,1,0:T(8,128)(2,1)S(1)}, u32[]{:S(2)}, u32[]{:S(2)}) %all-to-all-start.2) | async-done | bytes 786464 | tf_op jit(solution)/shard_map/all_to_all | solution.py:83
  106.9 15.2 %all_to_all.100 = bf16[4,64,1536]{2,1,0:T(8,128)(2,1)} all-to-all(bf16[4,64,1536]{2,1,0:T(8,128)(2,1)S(1)} %broadcast_in_dim.36), channel_id=1, replica_groups=mesh['fsdp'=2,'context'=4,'tensor'=4] {'tensor'}, dimensions={0} | all-to-all | bytes 1572864 | tf_op jit(solution)/shard_map/all_to_all | solution.py:48
  122.1 8.6 %shard_map.257 = (f32[256,1024]{1,0:T(8,128)}, f32[256,1024]{1,0:T(8,128)}, bf16[256,1536]{1,0:T(8,128)(2,1)}) custom-call(bf16[256,1536]{1,0:T(8,128)(2,1)} %bitcast.74, bf16[2,768,1024]{2,1,0:T(8,128)(2,1)} %wg.11, bf16[2,768,1024]{2,1,0:T(8,128)(2,1)} %wu.11, bf16[2,1024,768]{2,1,0:T(8,128)(2,1)} %wd.11, ...), custom_call_target="tpu_custom_call" | custom-call | flops 7699999744 | tf_op jit(solution)/shard_map/pallas_call | solution.py:651
  130.7 14.1 %all_to_all.101 = bf16[4,64,1536]{2,1,0:T(8,128)(2,1)S(1)} all-to-all(bf16[4,64,1536]{2,1,0:T(8,128)(2,1)} %bitcast.75), channel_id=1, replica_groups=mesh['fsdp'=2,'context'=4,'tensor'=4] {'tensor'}, dimensions={0} | all-to-all | bytes 1572864 | tf_op jit(solution)/shard_map/all_to_all | solution.py:83
  153.8 15.4 %all-to-all-done.5 = bf16[4,64,1536]{2,1,0:T(8,128)(2,1)S(1)} async-done(((bf16[4,64,1536]{2,1,0:T(8,128)(2,1)}), bf16[4,64,1536]{2,1,0:T(8,128)(2,1)S(1)}, u32[]{:S(2)}, u32[]{:S(2)}) %all-to-all-start.5) | async-done | bytes 786464 | tf_op jit(solution)/shard_map/all_to_all | solution.py:48
  187.5 11.0 %collective-permute-done.18.refs_4_ = bf16[64,1536]{1,0:T(8,128)(2,1)S(1)} collective-permute-done((bf16[64,1536]{1,0:T(8,128)(2,1)S(1)}, bf16[64,1536]{1,0:T(8,128)(2,1)S(1)}, u32[]{:S(2)}, u32[]{:S(2)}) %collective-permute-start.18) | collective-permute-done | bytes 196640 | tf_op jit(solution)/shard_map/ppermute | solution.py:25
  202.4 19.2 %shard_map.261 = (bf16[1024,1536]{1,0:T(8,128)(2,1)}, bf16[1024,384]{1,0:T(8,128)(2,1)}, bf16[1024,384]{1,0:T(8,128)(2,1)}, bf16[1024,384]{1,0:T(8,128)(2,1)}, f...) custom-call(s32[2]{0:T(128)} %pad_add_fusion.refs_0_, ...), custom_call_target="tpu_custom_call" | custom-call | flops 20899999744 | tf_op jit(solution)/shard_map/pallas_call | solution.py:584
  221.6 12.1 %all_to_all.102 = bf16[4,64,1536]{2,1,0:T(8,128)(2,1)S(1)} all-to-all(bf16[4,64,1536]{2,1,0:T(8,128)(2,1)} %bitcast.72), channel_id=1, replica_groups=mesh['fsdp'=2,'context'=4,'tensor'=4] {'tensor'}, dimensions={0} | all-to-all | bytes 1572864 | tf_op jit(solution)/shard_map/all_to_all | solution.py:83
  235.7 11.7 %all_to_all.103 = bf16[4,64,1536]{2,1,0:T(8,128)(2,1)} all-to-all(bf16[4,64,1536]{2,1,0:T(8,128)(2,1)S(1)} %broadcast_in_dim.39), channel_id=1, replica_groups=mesh['fsdp'=2,'context'=4,'tensor'=4] {'tensor'}, dimensions={0} | all-to-all | bytes 1572864 | tf_op jit(solution)/shard_map/all_to_all | solution.py:48
  247.4 8.4 %shard_map.262 = (f32[256,1024]{1,0:T(8,128)}, f32[256,1024]{1,0:T(8,128)}, bf16[256,1536]{1,0:T(8,128)(2,1)}) custom-call(bf16[256,1536]{1,0:T(8,128)(2,1)} %bitcast.76, bf16[2,768,1024]{2,1,0:T(8,128)(2,1)} %wg.11, bf16[2,768,1024]{2,1,0:T(8,128)(2,1)} %wu.11, bf16[2,1024,768]{2,1,0:T(8,128)(2,1)} %wd.11, ...), custom_call_target="tpu_custom_call" | custom-call | flops 7699999744 | tf_op jit(solution)/shard_map/pallas_call | solution.py:651
  255.8 9.3 %shard_map.263 = bf16[256,1536]{1,0:T(8,128)(2,1)} custom-call(bf16[256,1536]{1,0:T(8,128)(2,1)} %maximum_select_fusion.1.g_ref, f32[256,1024]{1,0:T(8,128)} %get-tuple-element.106.gt_ref, f32[256,1024]{1,0:T(8,128)} %get-tuple-element.107.up_ref, bf16[2,768,1024]{2,1,0:T(8,128)(2,1)} %wg.11, bf16[2,768,1024]{2,1,0:T(8,128)(2,1)} %wu.11, ...), custom_call_target="tpu_custom_call" | custom-call | flops 8800000000 | tf_op jit(solution)/shard_map/pallas_call | solution.py:665
  265.1 16.2 %all_to_all.104 = bf16[4,64,1536]{2,1,0:T(8,128)(2,1)S(1)} all-to-all(bf16[4,64,1536]{2,1,0:T(8,128)(2,1)} %bitcast.77), channel_id=1, replica_groups=mesh['fsdp'=2,'context'=4,'tensor'=4] {'tensor'}, dimensions={0} | all-to-all | bytes 1572864 | tf_op jit(solution)/shard_map/all_to_all | solution.py:83
  287.7 9.5 %collective-permute-start.22 = (bf16[64,1536]{1,0:T(8,128)(2,1)S(1)}, bf16[64,1536]{1,0:T(8,128)(2,1)S(1)}, u32[]{:S(2)}, u32[]{:S(2)}) collective-permute-start(bf16[64,1536]{1,0:T(8,128)(2,1)S(1)} %fusion.5), channel_id=1, source_target_pairs={{0,8},{4,12},{8,0},{12,4},{1,9},{5,13},{9,1},{13,5},{2,10},{6,14},... | collective-permute-start | bytes 589832 | tf_op jit(solution)/shard_map/ppermute | solution.py:25
  300.0 20.0 %collective-permute-done.22.refs_0_ = bf16[64,1536]{1,0:T(8,128)(2,1)S(1)} collective-permute-done((bf16[64,1536]{1,0:T(8,128)(2,1)S(1)}, bf16[64,1536]{1,0:T(8,128)(2,1)S(1)}, u32[]{:S(2)}, u32[]{:S(2)}) %collective-permute-start.22) | collective-permute-done | bytes 196640 | tf_op jit(solution)/shard_map/ppermute | solution.py:25
  338.8 21.1 %shard_map.266 = (bf16[1024,1024]{1,0:T(8,128)(2,1)}, bf16[1024,1024]{1,0:T(8,128)(2,1)}, bf16[1024,1024]{1,0:T(8,128)(2,1)}, bf16[768,1024]{1,0:T(8,128)(2,1)},...) custom-call(bf16[1024,1536]{1,0:T(8,128)(2,1)} %all-gather.9.cloned.1.call-done.b_ref, ...), custom_call_target="tpu_custom_call" | custom-call | flops 26400000000 | tf_op jit(solution)/shard_map/pallas_call | solution.py:682
  360.0 34.0 %shard_map.268 = (bf16[1024,1536]{1,0:T(8,128)(2,1)}, bf16[1024,384]{1,0:T(8,128)(2,1)}, bf16[1024,384]{1,0:T(8,128)(2,1)}, bf16[1024,384]{1,0:T(8,128)(2,1)}, b...) custom-call(s32[2]{0:T(128)} %pad_add_fusion.refs_0_, ...), custom_call_target="tpu_custom_call" | custom-call | flops 36300001280 | tf_op jit(solution)/shard_map/pallas_call | solution.py:614
  394.0 20.4 %all_to_all.105 = bf16[4,64,1536]{2,1,0:T(8,128)(2,1)S(1)} all-to-all(bf16[4,64,1536]{2,1,0:T(8,128)(2,1)} %bitcast.73), channel_id=1, replica_groups=mesh['fsdp'=2,'context'=4,'tensor'=4] {'tensor'}, dimensions={0} | all-to-all | bytes 1572864 | tf_op jit(solution)/shard_map/all_to_all | solution.py:83
  422.7 8.5 %shard_map.271 = (bf16[768,384]{1,0:T(8,128)(2,1)}, bf16[768,384]{1,0:T(8,128)(2,1)}, bf16[768,384]{1,0:T(8,128)(2,1)}, bf16[768,384]{1,0:T(8,128)(2,1)}, bf16[7...) custom-call(bf16[1024,1536]{1,0:T(8,128)(2,1)} %get-tuple-element.119.refs_0_, ...), custom_call_target="tpu_custom_call" | custom-call | flops 7699999744 | tf_op jit(solution)/shard_map/pallas_call | solution.py:747
  432.0 9.2 %shard_map.272 = bf16[256,1536]{1,0:T(8,128)(2,1)} custom-call(bf16[256,1536]{1,0:T(8,128)(2,1)} %bitcast.71, f32[256,1024]{1,0:T(8,128)} %get-tuple-element.117.gt_ref, f32[256,1024]{1,0:T(8,128)} %get-tuple-element.118.up_ref, bf16[2,768,1024]{2,1,0:T(8,128)(2,1)} %wg.11, bf16[2,768,1024]{2,1,0:T(8,128)(2,1)} %wu.11, bf16[2,1024,768]{2,1,0:T(8,128)(2,1)} %wd.11, ...), custom_call_target="tpu_custom_call" | custom-call | flops 8800000000 | tf_op jit(solution)/shard_map/pallas_call | solution.py:665
  446.5 7.0 %all-to-all-done.14 = bf16[4,64,1536]{2,1,0:T(8,128)(2,1)S(1)} async-done(((bf16[4,64,1536]{2,1,0:T(8,128)(2,1)}), bf16[4,64,1536]{2,1,0:T(8,128)(2,1)S(1)}, u32[]{:S(2)}, u32[]{:S(2)}) %all-to-all-start.14) | async-done | bytes 786464 | tf_op jit(solution)/shard_map/all_to_all | solution.py:83
  455.5 13.7 %collective-permute-start.26 = (bf16[64,1536]{1,0:T(8,128)(2,1)S(1)}, bf16[64,1536]{1,0:T(8,128)(2,1)S(1)}, u32[]{:S(2)}, u32[]{:S(2)}) collective-permute-start(bf16[64,1536]{1,0:T(8,128)(2,1)S(1)} %get-tuple-element.232), channel_id=1, source_target_pairs={{0,8},{4,12},{8,0},{12,4},{1,9},{5,13},{9,1},{13,5},{2,10},{6,14},... | collective-permute-start | bytes 589832 | tf_op jit(solution)/shard_map/ppermute | solution.py:25
  475.4 15.5 %collective-permute-done.26 = bf16[64,1536]{1,0:T(8,128)(2,1)S(1)} collective-permute-done((bf16[64,1536]{1,0:T(8,128)(2,1)S(1)}, bf16[64,1536]{1,0:T(8,128)(2,1)S(1)}, u32[]{:S(2)}, u32[]{:S(2)}) %collective-permute-start.26) | collective-permute-done | bytes 196640 | tf_op jit(solution)/shard_map/ppermute | solution.py:25
  500.2 9.6 %shard_map.274 = (f32[2,768,384]{2,1,0:T(8,128)}, f32[2,768,384]{2,1,0:T(8,128)}, f32[2,768,384]{2,1,0:T(8,128)}, f32[2,768,384]{2,1,0:T(8,128)}, f32[768,128]{1,0:T(8,128)}, /*index=5*/f32[2,384,768]{2,1,0:T(8,128)}) custom-call(bf16[1024,1536]{1,0:T(8,128)(2,1)} %get-tuple-element.11, ...), custom_call_target="tpu_custom_call", output_to_operand_aliasing={{0}: (14, {}), {1}: (15, {}), {2}: (16, {}), {3}: (17, {}),... | custom-call | flops 7699999744 | tf_op jit(solution)/shard_map/pallas_call | solution.py:747
  509.8 8.0 %collective-permute-start.25 = (bf16[256,1536]{1,0:T(8,128)(2,1)S(1)}, bf16[256,1536]{1,0:T(8,128)(2,1)S(1)}, u32[]{:S(2)}, u32[]{:S(2)}) collective-permute-start(bf16[256,1536]{1,0:T(8,128)(2,1)S(1)} %bitcast.61), channel_id=1, source_target_pairs={{0,4},{4,0},{8,12},{12,8},{1,5},{5,1},{9,13},{13,9},{2,6},{6,2},{1... | collective-permute-start | bytes 2359304 | tf_op jit(solution)/shard_map/ppermute | solution.py:25
  517.8 12.0 %shard_map.275 = (f32[2,768,1024]{2,1,0:T(8,128)}, f32[2,768,1024]{2,1,0:T(8,128)}, f32[2,1024,768]{2,1,0:T(8,128)}) custom-call(bf16[1024,1536]{1,0:T(8,128)(2,1)} %all-gather.9.cloned.1.call-done.b_ref, bf16[1024,1536]{1,0:T(8,128)(2,1)} %all-gather.5.cloned.1.call-done.refs_1_.g_ref, ...), custom_call_target="tpu_custom_call", output_to_operand_aliasing={{0}: (8, {}), {1}: (9, {}), {2}: (10, {})} | custom-call | flops 9900000256 | tf_op jit(solution)/shard_map/pallas_call | solution.py:707
  536.5 33.9 %shard_map.277 = (bf16[1024,1536]{1,0:T(8,128)(2,1)}, bf16[1024,384]{1,0:T(8,128)(2,1)}, bf16[1024,384]{1,0:T(8,128)(2,1)}, bf16[1024,384]{1,0:T(8,128)(2,1)}, b...) custom-call(s32[2]{0:T(128)} %pad_add_fusion.refs_0_, ...), custom_call_target="tpu_custom_call" | custom-call | flops 36300001280 | tf_op jit(solution)/shard_map/pallas_call | solution.py:614
  593.7 21.0 %shard_map.269 = (bf16[1024,1024]{1,0:T(8,128)(2,1)}, bf16[1024,1024]{1,0:T(8,128)(2,1)}, bf16[1024,1024]{1,0:T(8,128)(2,1)}, bf16[768,1024]{1,0:T(8,128)(2,1)},...) custom-call(bf16[1024,1536]{1,0:T(8,128)(2,1)} %all-gather.7.cloned.1.call-done.b_ref, ...), custom_call_target="tpu_custom_call" | custom-call | flops 26400000000 | tf_op jit(solution)/shard_map/pallas_call | solution.py:682
  619.9 8.4 %shard_map.278 = (bf16[768,384]{1,0:T(8,128)(2,1)}, bf16[768,384]{1,0:T(8,128)(2,1)}, bf16[768,384]{1,0:T(8,128)(2,1)}, bf16[768,384]{1,0:T(8,128)(2,1)}, bf16[7...) custom-call(bf16[1024,1536]{1,0:T(8,128)(2,1)} %get-tuple-element.155.refs_0_, ...), custom_call_target="tpu_custom_call" | custom-call | flops 7699999744 | tf_op jit(solution)/shard_map/pallas_call | solution.py:747
  645.6 9.5 %shard_map.279 = (f32[2,768,384]{2,1,0:T(8,128)}, f32[2,768,384]{2,1,0:T(8,128)}, f32[2,768,384]{2,1,0:T(8,128)}, f32[2,768,384]{2,1,0:T(8,128)}, f32[768,128]{1,0:T(8,128)}, /*index=5*/f32[2,384,768]{2,1,0:T(8,128)}) custom-call(bf16[1024,1536]{1,0:T(8,128)(2,1)} %get-tuple-element.15, ...), custom_call_target="tpu_custom_call", output_to_operand_aliasing={{0}: (14, {}), {1}: (15, {}), {2}: (16, {}), {3}: (17, {}),... | custom-call | flops 7699999744 | tf_op jit(solution)/shard_map/pallas_call | solution.py:747
  657.0 11.8 %shard_map.280 = (f32[2,768,1024]{2,1,0:T(8,128)}, f32[2,768,1024]{2,1,0:T(8,128)}, f32[2,1024,768]{2,1,0:T(8,128)}) custom-call(bf16[1024,1536]{1,0:T(8,128)(2,1)} %all-gather.7.cloned.1.call-done.b_ref, bf16[1024,1536]{1,0:T(8,128)(2,1)} %all-gather.11.cloned.1.call-done.g_ref, ...), custom_call_target="tpu_custom_call", output_to_operand_aliasing={{0}: (8, {}), {1}: (9, {}), {2}: (10, {})} | custom-call | flops 9900000256 | tf_op jit(solution)/shard_map/pallas_call | solution.py:707
  (365 shorter events, 205.1 us)
Async XLA Ops:
  12.0 40.5 %collective-permute-start.1 = (bf16[256,1536]{1,0:T(8,128)(2,1)S(1)}, bf16[256,1536]{1,0:T(8,128)(2,1)}, u32[]{:S(2)}, u32[]{:S(2)}) collective-permute-start(bf16[256,1536]{1,0:T(8,128)(2,1)S(1)} %multiply_convert_fusion.refs_1_), channel_id=1, source_target_pairs={{0,4},{4,0},{8,12},{12,8},{1,5},{5,1},{9,13},{13,9},{2,6},{6,2},{1... | collective-permute-start | bytes 2359304 | tf_op jit(solution)/shard_map/ppermute | solution.py:25
  15.3 24.4 %collective-permute-start.2 = (bf16[64,1536]{1,0:T(8,128)(2,1)}, bf16[64,1536]{1,0:T(8,128)(2,1)S(1)}, u32[]{:S(2)}, u32[]{:S(2)}) collective-permute-start(bf16[64,1536]{1,0:T(8,128)(2,1)} %constant_dynamic-slice_fusion.1), channel_id=1, source_target_pairs={{0,8},{4,12},{8,0},{12,4},{1,9},{5,13},{9,1},{13,5},{2,10},{6,14},... | collective-permute-start | bytes 589832 | tf_op jit(solution)/shard_map/ppermute | solution.py:25
  18.5 21.2 %all-to-all-start = ((s32[4,1,256]{2,1,0:T(1,128)}), s32[4,1,256]{2,1,0:T(1,128)}, u32[]{:S(2)}, u32[]{:S(2)}) async-start(s32[4,1,256]{2,1,0:T(1,128)} %broadcast_in_dim.33), calls=%async_computation | async-start | bytes 8192 | tf_op jit(solution)/shard_map/all_to_all | solution.py:48
  64.4 57.7 %collective-permute-start.13 = (bf16[2,768,1024]{2,1,0:T(8,128)(2,1)}, bf16[2,768,1024]{2,1,0:T(8,128)(2,1)}, u32[]{:S(2)}, u32[]{:S(2)}) collective-permute-start(bf16[2,768,1024]{2,1,0:T(8,128)(2,1)} %wg.11), channel_id=1, source_target_pairs={{0,16},{16,0},{1,17},{17,1},{2,18},{18,2},{3,19},{19,3},{4,20},{20... | collective-permute-start | bytes 9437192 | tf_op jit(solution)/shard_map/ppermute | solution.py:25
  64.8 57.3 %collective-permute-start.14 = (bf16[2,768,1024]{2,1,0:T(8,128)(2,1)}, bf16[2,768,1024]{2,1,0:T(8,128)(2,1)}, u32[]{:S(2)}, u32[]{:S(2)}) collective-permute-start(bf16[2,768,1024]{2,1,0:T(8,128)(2,1)} %wu.11), channel_id=1, source_target_pairs={{0,16},{16,0},{1,17},{17,1},{2,18},{18,2},{3,19},{19,3},{4,20},{20... | collective-permute-start | bytes 9437192 | tf_op jit(solution)/shard_map/ppermute | solution.py:25
  64.9 57.2 %collective-permute-start.15 = (bf16[2,1024,768]{2,1,0:T(8,128)(2,1)}, bf16[2,1024,768]{2,1,0:T(8,128)(2,1)}, u32[]{:S(2)}, u32[]{:S(2)}) collective-permute-start(bf16[2,1024,768]{2,1,0:T(8,128)(2,1)} %wd.11), channel_id=1, source_target_pairs={{0,16},{16,0},{1,17},{17,1},{2,18},{18,2},{3,19},{19,3},{4,20},{20... | collective-permute-start | bytes 9437192 | tf_op jit(solution)/shard_map/ppermute | solution.py:25
  95.0 92.5 %all-gather.5.cloned.1.call-start = ((), (), s32[]{:S(2)}) async-start(), calls=%async_computation.20 | async-start | bytes 3342336 | tf_op jit(solution)/shard_map/all_gather | solution.py:52
  146.6 22.6 %all-to-all-start.5 = ((bf16[4,64,1536]{2,1,0:T(8,128)(2,1)}), bf16[4,64,1536]{2,1,0:T(8,128)(2,1)S(1)}, u32[]{:S(2)}, u32[]{:S(2)}) async-start(bf16[4,64,1536]{2,1,0:T(8,128)(2,1)} %broadcast_in_dim.37), calls=%async_computation.5 | async-start | bytes 1572864 | tf_op jit(solution)/shard_map/all_to_all | solution.py:48
  150.1 25.5 %collective-permute-start.17 = (bf16[64,1536]{1,0:T(8,128)(2,1)S(1)}, bf16[64,1536]{1,0:T(8,128)(2,1)S(1)}, u32[]{:S(2)}, u32[]{:S(2)}) collective-permute-start(bf16[64,1536]{1,0:T(8,128)(2,1)S(1)} %multiply_convert_fusion.2), channel_id=1, source_target_pairs={{0,8},{4,12},{8,0},{12,4},{1,9},{5,13},{9,1},{13,5},{2,10},{6,14},... | collective-permute-start | bytes 589832 | tf_op jit(solution)/shard_map/ppermute | solution.py:25
  152.3 23.2 %collective-permute-start.21 = (bf16[64,1536]{1,0:T(8,128)(2,1)S(1)}, bf16[64,1536]{1,0:T(8,128)(2,1)S(1)}, u32[]{:S(2)}, u32[]{:S(2)}) collective-permute-start(bf16[64,1536]{1,0:T(8,128)(2,1)S(1)} %multiply_convert_fusion.2), channel_id=1, source_target_pairs={{0,12},{4,8},{8,4},{12,0},{1,13},{5,9},{9,5},{13,1},{2,14},{6,10},... | collective-permute-start | bytes 589832 | tf_op jit(solution)/shard_map/ppermute | solution.py:25
  169.2 32.3 %collective-permute-start.16 = (bf16[256,1536]{1,0:T(8,128)(2,1)S(1)}, bf16[256,1536]{1,0:T(8,128)(2,1)}, u32[]{:S(2)}, u32[]{:S(2)}) collective-permute-start(bf16[256,1536]{1,0:T(8,128)(2,1)S(1)} %bitcast.65), channel_id=1, source_target_pairs={{0,4},{4,0},{8,12},{12,8},{1,5},{5,1},{9,13},{13,9},{2,6},{6,2},{1... | collective-permute-start | bytes 2359304 | tf_op jit(solution)/shard_map/ppermute | solution.py:25
  178.8 22.7 %all-to-all-start.6 = ((bf16[4,64,1536]{2,1,0:T(8,128)(2,1)}), bf16[4,64,1536]{2,1,0:T(8,128)(2,1)S(1)}, u32[]{:S(2)}, u32[]{:S(2)}) async-start(bf16[4,64,1536]{2,1,0:T(8,128)(2,1)} %broadcast_in_dim.38), calls=%async_computation.6 | async-start | bytes 1572864 | tf_op jit(solution)/shard_map/all_to_all | solution.py:48
  182.9 155.9 %all-gather.9.cloned.1.call-start = ((), (), s32[]{:S(2)}) async-start(), calls=%async_computation.23 | async-start | bytes 3342336 | tf_op jit(solution)/shard_map/all_gather | solution.py:52
  284.2 35.8 %all-to-all-start.11 = ((bf16[4,64,1536]{2,1,0:T(8,128)(2,1)}), bf16[4,64,1536]{2,1,0:T(8,128)(2,1)S(1)}, u32[]{:S(2)}, u32[]{:S(2)}) async-start(bf16[4,64,1536]{2,1,0:T(8,128)(2,1)} %broadcast_in_dim.41), calls=%async_computation.11 | async-start | bytes 1572864 | tf_op jit(solution)/shard_map/all_to_all | solution.py:48
  287.7 32.2 %collective-permute-start.22 = (bf16[64,1536]{1,0:T(8,128)(2,1)S(1)}, bf16[64,1536]{1,0:T(8,128)(2,1)S(1)}, u32[]{:S(2)}, u32[]{:S(2)}) collective-permute-start(bf16[64,1536]{1,0:T(8,128)(2,1)S(1)} %fusion.5), channel_id=1, source_target_pairs={{0,8},{4,12},{8,0},{12,4},{1,9},{5,13},{9,1},{13,5},{2,10},{6,14},... | collective-permute-start | bytes 589832 | tf_op jit(solution)/shard_map/ppermute | solution.py:25
  297.2 22.7 %collective-permute-start.23 = (bf16[64,1536]{1,0:T(8,128)(2,1)S(1)}, bf16[64,1536]{1,0:T(8,128)(2,1)S(1)}, u32[]{:S(2)}, u32[]{:S(2)}) collective-permute-start(bf16[64,1536]{1,0:T(8,128)(2,1)S(1)} %fusion.5), channel_id=1, source_target_pairs={{0,12},{4,8},{8,4},{12,0},{1,13},{5,9},{9,5},{13,1},{2,14},{6,10},... | collective-permute-start | bytes 589832 | tf_op jit(solution)/shard_map/ppermute | solution.py:25
  325.3 268.4 %all-gather.7.cloned.1.call-start = ((), (), s32[]{:S(2)}) async-start(), calls=%async_computation.22 | async-start | bytes 3342336 | tf_op jit(solution)/shard_map/all_gather | solution.py:52
  325.3 34.6 %collective-permute-start.24 = (bf16[256,1536]{1,0:T(8,128)(2,1)}, bf16[256,1536]{1,0:T(8,128)(2,1)}, u32[]{:S(2)}, u32[]{:S(2)}) collective-permute-start(bf16[256,1536]{1,0:T(8,128)(2,1)} %bitcast.63), channel_id=1, source_target_pairs={{0,4},{4,0},{8,12},{12,8},{1,5},{5,1},{9,13},{13,9},{2,6},{6,2},{1... | collective-permute-start | bytes 2359304 | tf_op jit(solution)/shard_map/ppermute | solution.py:25
  338.8 254.9 %all-gather.11.cloned.1.call-start = ((), (), s32[]{:S(2)}) async-start(), calls=%async_computation.24 | async-start | bytes 3342336 | tf_op jit(solution)/shard_map/all_gather | solution.py:52
  445.5 72.4 %collective-permute-start.34 = (bf16[768,1024]{1,0:T(8,128)(2,1)}, bf16[768,1024]{1,0:T(8,128)(2,1)}, u32[]{:S(2)}, u32[]{:S(2)}) collective-permute-start(bf16[768,1024]{1,0:T(8,128)(2,1)} %get-tuple-element.147), channel_id=1, source_target_pairs={{0,16},{16,0},{1,17},{17,1},{2,18},{18,2},{3,19},{19,3},{4,20},{20... | collective-permute-start | bytes 4718600 | tf_op jit(solution)/shard_map/ppermute | solution.py:25
  446.0 23.2 %collective-permute-start.30 = (bf16[768,384]{1,0:T(8,128)(2,1)}, bf16[768,384]{1,0:T(8,128)(2,1)}, u32[]{:S(2)}, u32[]{:S(2)}) collective-permute-start(bf16[768,384]{1,0:T(8,128)(2,1)} %get-tuple-element.135), channel_id=1, source_target_pairs={{0,16},{16,0},{1,17},{17,1},{2,18},{18,2},{3,19},{19,3},{4,20},{20... | collective-permute-start | bytes 1769480 | tf_op jit(solution)/shard_map/ppermute | solution.py:25
  454.6 63.3 %collective-permute-start.35 = (bf16[768,1024]{1,0:T(8,128)(2,1)}, bf16[768,1024]{1,0:T(8,128)(2,1)}, u32[]{:S(2)}, u32[]{:S(2)}) collective-permute-start(bf16[768,1024]{1,0:T(8,128)(2,1)} %get-tuple-element.148), channel_id=1, source_target_pairs={{0,16},{16,0},{1,17},{17,1},{2,18},{18,2},{3,19},{19,3},{4,20},{20... | collective-permute-start | bytes 4718600 | tf_op jit(solution)/shard_map/ppermute | solution.py:25
  454.7 63.2 %collective-permute-start.36 = (bf16[1024,768]{1,0:T(8,128)(2,1)}, bf16[1024,768]{1,0:T(8,128)(2,1)}, u32[]{:S(2)}, u32[]{:S(2)}) collective-permute-start(bf16[1024,768]{1,0:T(8,128)(2,1)} %get-tuple-element.149), channel_id=1, source_target_pairs={{0,16},{16,0},{1,17},{17,1},{2,18},{18,2},{3,19},{19,3},{4,20},{20... | collective-permute-start | bytes 4718600 | tf_op jit(solution)/shard_map/ppermute | solution.py:25
  455.5 35.4 %collective-permute-start.26 = (bf16[64,1536]{1,0:T(8,128)(2,1)S(1)}, bf16[64,1536]{1,0:T(8,128)(2,1)S(1)}, u32[]{:S(2)}, u32[]{:S(2)}) collective-permute-start(bf16[64,1536]{1,0:T(8,128)(2,1)S(1)} %get-tuple-element.232), channel_id=1, source_target_pairs={{0,8},{4,12},{8,0},{12,4},{1,9},{5,13},{9,1},{13,5},{2,10},{6,14},... | collective-permute-start | bytes 589832 | tf_op jit(solution)/shard_map/ppermute | solution.py:25
  469.2 21.9 %collective-permute-start.27 = (bf16[64,1536]{1,0:T(8,128)(2,1)S(1)}, bf16[64,1536]{1,0:T(8,128)(2,1)S(1)}, u32[]{:S(2)}, u32[]{:S(2)}) collective-permute-start(bf16[64,1536]{1,0:T(8,128)(2,1)S(1)} %get-tuple-element.232), channel_id=1, source_target_pairs={{0,12},{4,8},{8,4},{12,0},{1,13},{5,9},{9,5},{13,1},{2,14},{6,10},... | collective-permute-start | bytes 589832 | tf_op jit(solution)/shard_map/ppermute | solution.py:25
  471.8 23.4 %all-to-all-start.15 = ((bf16[4,64,1536]{2,1,0:T(8,128)(2,1)}), bf16[4,64,1536]{2,1,0:T(8,128)(2,1)S(1)}, u32[]{:S(2)}, u32[]{:S(2)}) async-start(bf16[4,64,1536]{2,1,0:T(8,128)(2,1)} %broadcast_in_dim.43), calls=%async_computation.15 | async-start | bytes 1572864 | tf_op jit(solution)/shard_map/all_to_all | solution.py:48
  475.3 159.6 %all-reduce.4.cloned.1.call-start = ((), (), s32[]{:S(2)}) async-start(), calls=%async_computation.21 | async-start | bytes 1572864 | tf_op jit(solution)/shard_map/psum | solution.py:928
  494.7 79.8 %collective-permute-start.47 = (f32[6]{0:T(128)}, f32[6]{0:T(128)}, u32[]{:S(2)}, u32[]{:S(2)}) collective-permute-start(f32[6]{0:T(128)} %bitcast.49), channel_id=1, source_target_pairs={{0,16},{16,0},{1,17},{17,1},{2,18},{18,2},{3,19},{19,3},{4,20},{20... | collective-permute-start | bytes 80 | tf_op jit(solution)/shard_map/ppermute | solution.py:25
  496.6 33.2 %all-to-all-start.16 = ((bf16[4,128,1536]{2,1,0:T(8,128)(2,1)}), bf16[4,128,1536]{2,1,0:T(8,128)(2,1)S(1)}, u32[]{:S(2)}, u32[]{:S(2)}) async-start(bf16[4,128,1536]{2,1,0:T(8,128)(2,1)} %broadcast_in_dim.44), calls=%async_computation.16 | async-start | bytes 3145728 | tf_op jit(solution)/shard_map/all_to_all | solution.py:48
  509.8 25.8 %collective-permute-start.25 = (bf16[256,1536]{1,0:T(8,128)(2,1)S(1)}, bf16[256,1536]{1,0:T(8,128)(2,1)S(1)}, u32[]{:S(2)}, u32[]{:S(2)}) collective-permute-start(bf16[256,1536]{1,0:T(8,128)(2,1)S(1)} %bitcast.61), channel_id=1, source_target_pairs={{0,4},{4,0},{8,12},{12,8},{1,5},{5,1},{9,13},{13,9},{2,6},{6,2},{1... | collective-permute-start | bytes 2359304 | tf_op jit(solution)/shard_map/ppermute | solution.py:25
  578.3 50.0 %collective-permute-start.46 = (f32[6]{0:T(128)}, f32[6]{0:T(128)}, u32[]{:S(2)}, u32[]{:S(2)}) collective-permute-start(f32[6]{0:T(128)} %bitcast.50), channel_id=1, source_target_pairs={{0,16},{16,0},{1,17},{17,1},{2,18},{18,2},{3,19},{19,3},{4,20},{20... | collective-permute-start | bytes 80 | tf_op jit(solution)/shard_map/ppermute | solution.py:25
  586.3 28.5 %all-to-all-start.19 = ((f32[16,1,6144]{2,1,0:T(1,128)}), f32[16,1,6144]{2,1,0:T(1,128)S(1)}, u32[]{:S(2)}, u32[]{:S(2)}) async-start(f32[16,1,6144]{2,1,0:T(1,128)} %broadcast_in_dim.47), calls=%async_computation.19 | async-start | bytes 786432 | tf_op jit(solution)/shard_map/all_to_all | solution.py:48
  (103 other events, 1104.6 us)
Sparse Core Ops, SparseCore 0:
  99.2 84.7 all-gather.4
  234.9 90.5 all-gather.8
  338.9 83.8 all-gather.6
  425.4 81.4 all-gather.10
  510.4 57.2 all-reduce.3

commit v9 on v8

--- a/solution.py
+++ b/solution.py
@@ -838,6 +838,8 @@
         )
         if shared_rows and layer == 0:
             g_last = sequence_rows(after(own_block(cotangent_rows), a_parts[-1]))
+        if shared_rows and layer > 0:
+            saved[-1]["b_rows"] = sequence_rows(after(saved[-1]["b_shard"], a_parts[-1]))
         mixed = hidden + received_sum(sends)
         inverse_two = inverse_rms(mixed)
         b_shard = (mixed * inverse_two * gain_two).astype(bf16)
@@ -894,29 +896,28 @@
         tokens = ()
         if layer == last:
             g = cotangent_rows
-            if shared_rows:
-                s.update(b_rows=sequence_rows(s["b_shard"]), g_rows=g_last)
         else:
             g_shard = grad.astype(bf16)
             g = gathered(g_shard, "tensor")
             tokens = (saved[layer + 1]["theirs"][0],)
             if shared_rows:
-                s.update(b_rows=sequence_rows(after(s["b_shard"], token)), g_rows=sequence_rows(g_shard))
+                s["g_rows"] = sequence_rows(g_shard)
         if not shared_rows:
             s.update(b_rows=s["b"], g_rows=g)
         sends = ffn_backward(g, s["gt"], s["up"], layer, w3, t3, *tokens)
+        if layer < last:
+            sends = after(sends, *saved[layer + 1]["received"])
         back, gain_grads[layers + layer] = norm_back(received_sum(sends), s["mixed"], s["inverse_two"], gain_two)
         grad_mixed = grad + back
         y_parts, y_far = all_rows(grad_mixed.astype(bf16), together=True)
-        if layer == last:
-            ffn_theirs_of(layer, *y_far)
-            tokens = (s["values"][0],)
-        else:
-            if layer + 1 < last:
-                ffn_theirs_of(layer + 1)
+        tokens = ()
+        if layer < last:
+            above = saved[layer + 1]
             attention_mine_of(layer + 1)
-            ffn_mine_of(layer + 1)
-            tokens = (results[0], results[5])
+            ffn_theirs_of(layer + 1, *y_far)
+            tokens = (results[0], above["values"][0])
+        elif shared_rows:
+            tokens = [x["b_rows"] for x in saved[:-1]]
         kept = (*s["kept"][:-1], after(s["kept"][-1], *tokens))
         y, (dq, dk, dv, dg, u, dz), sends = attention_backward(
             place, y_parts, layer, w4, t4, w_attn_out, to, w_forget_full[layer], kept, doc_start, piece_len,
@@ -926,14 +927,19 @@
             block_sum = own_block(last_sends).astype(f32) + s["mixed"]
             with_rows = lax.dynamic_update_slice_in_dim(last_sends, block_sum.astype(bf16), t * block, 0)
             output = lax.psum(after(with_rows, token), "tensor")
+        if layer < last:
+            sends = after(sends, *above["ffn_received"])
+        if shared_rows and layer == last:
+            s.update(b_rows=sequence_rows(after(s["b_shard"], token)), g_rows=g_last)
         s["grads"] = (s["a"], (dq, dk, dv, dg), dz, u, y)
         if layer > 0:
             attention_theirs_of(layer)
         back, gain_grads[layer] = norm_back(received_sum(sends), s["hidden"], s["inverse_one"], gain_one)
         grad = grad_mixed + back
 
-    if layers > 1:
-        ffn_theirs_of(0)
+    for layer in reversed(range(1, layers)):
+        ffn_mine_of(layer)
+    ffn_theirs_of(0)
     attention_theirs_of(0, saved[0]["values"][0], grad)
     attention_mine_of(0, *saved[0]["ffn_received"])
     ffn_mine_of(0)

time: 686 us -> 695 us (1.013)
  waiting for transfers between devices: 139 us -> 171 us
  starting transfers between devices: 125 us -> 106 us
    all_to_all x2 -> x3, blocking collectives: 26.9 us -> 49.3 us  [gathered(): lax.all_to_all(copies, axis, 0, 0, tiled=True)]
    all_to_all x4 -> x3, blocking collectives: 62.7 us -> 41.9 us  [received_sum(): lax.all_to_all(sends.reshape(count, -1, sends.shape[1]), 'tensor', 0, 0,...]
    ppermute x49, starting transfers between devices: 69.8 us -> 50.3 us  [swap(): return lax.ppermute(x, axis, [(i, i ^ k) for i in range(n)])]
    ppermute x49, waiting for transfers between devices: 74.7 us -> 92.4 us  [swap(): return lax.ppermute(x, axis, [(i, i ^ k) for i in range(n)])]
    all_to_all x11 -> x10, waiting for transfers between devices: 41.1 us -> 55.2 us  [gathered(): lax.all_to_all(copies, axis, 0, 0, tiled=True)]
    all_to_all x3 -> x4, starting transfers between devices: 11.7 us -> 14.8 us  [received_sum(): lax.all_to_all(sends.reshape(count, -1, sends.shape[1]), 'tensor', 0, 0,...]
    all_to_all x11 -> x10, starting transfers between devices: 43 us -> 40.2 us  [gathered(): lax.all_to_all(copies, axis, 0, 0, tiled=True)]
    all_to_all x3 -> x4, waiting for transfers between devices: 22.8 us -> 22.5 us  [received_sum(): lax.all_to_all(sends.reshape(count, -1, sends.shape[1]), 'tensor', 0, 0,...]
  transfers between devices with their start and end apart: 68 -> 68, of which waited for: 20 -> 22; matrix products, arithmetic and copies ran while one was open for 7% -> 6% of each run, Pallas kernels for 30% -> 33%
where the time goes in v9:
time: 695 us; the launch traced here: 685 us
  Pallas kernels  244 us (35%)
  waiting for transfers between devices  171 us (25%)
  starting transfers between devices  106 us (15%)
  blocking collectives  91.2 us (13%)
  local copies, waits for them, and re-layouts  38.6 us (6%)
  other arithmetic  19.1 us (3%)
  between operations  15.3 us (2%)
    ppermute x49, waiting for transfers between devices, swap(): return lax.ppermute(x, axis, [(i, i ^ k) for i in range(n)])  92.4 us
    pallas_call x2, Pallas kernels, attention_backward(): pl.pallas_call(functools.partial(backward_kernel, len(parts), piece_len,...  67.1 us
    all_to_all x10, waiting for transfers between devices, gathered(): lax.all_to_all(copies, axis, 0, 0, tiled=True)  55.2 us
    ppermute x49, starting transfers between devices, swap(): return lax.ppermute(x, axis, [(i, i ^ k) for i in range(n)])  50.3 us
    all_to_all x3, blocking collectives, gathered(): lax.all_to_all(copies, axis, 0, 0, tiled=True)  49.3 us
    pallas_call x2, Pallas kernels, ffn_theirs(): pl.pallas_call(ffn_theirs_kernel, grid=(inner // hidden_block,), in_specs...  42.6 us
    all_to_all x3, blocking collectives, received_sum(): lax.all_to_all(sends.reshape(count, -1, sends.shape[1]), 'tensor', 0, 0,...  41.9 us
    all_to_all x10, starting transfers between devices, gathered(): lax.all_to_all(copies, axis, 0, 0, tiled=True)  40.2 us
  transfers between devices with their start and end apart: 68, of which 22 were waited for; matrix products, arithmetic and copies ran while one was open for 6% of the time, Pallas kernels for 33%

profile of v9, /device:TPU:0, one launch (start us, length us, event | category | flops | bytes accessed | tf_op | source)
XLA Modules:
  0.0 684.9 jit_solution(17617058306470783039)
XLA Ops:
  26.7 12.9 %all-to-all-done = s32[4,1,256]{2,1,0:T(1,128)} async-done(((s32[4,1,256]{2,1,0:T(1,128)}), s32[4,1,256]{2,1,0:T(1,128)}, u32[]{:S(2)}, u32[]{:S(2)}) %all-to-all-start) | async-done | bytes 4128 | tf_op jit(solution)/shard_map/all_to_all | solution.py:48
  72.3 19.2 %shard_map.256 = (bf16[1024,1536]{1,0:T(8,128)(2,1)}, bf16[1024,384]{1,0:T(8,128)(2,1)}, bf16[1024,384]{1,0:T(8,128)(2,1)}, bf16[1024,384]{1,0:T(8,128)(2,1)}, f...) custom-call(s32[2]{0:T(128)} %pad_add_fusion.refs_0_, ...), custom_call_target="tpu_custom_call" | custom-call | flops 20899999744 | tf_op jit(solution)/shard_map/pallas_call | solution.py:584
  96.7 9.2 %all-to-all-done.2 = bf16[4,64,1536]{2,1,0:T(8,128)(2,1)S(1)} async-done(((bf16[4,64,1536]{2,1,0:T(8,128)(2,1)}), bf16[4,64,1536]{2,1,0:T(8,128)(2,1)S(1)}, u32[]{:S(2)}, u32[]{:S(2)}) %all-to-all-start.2) | async-done | bytes 786464 | tf_op jit(solution)/shard_map/all_to_all | solution.py:83
  106.9 15.2 %all_to_all.100 = bf16[4,64,1536]{2,1,0:T(8,128)(2,1)} all-to-all(bf16[4,64,1536]{2,1,0:T(8,128)(2,1)S(1)} %broadcast_in_dim.36), channel_id=1, replica_groups=mesh['fsdp'=2,'context'=4,'tensor'=4] {'tensor'}, dimensions={0} | all-to-all | bytes 1572864 | tf_op jit(solution)/shard_map/all_to_all | solution.py:48
  122.1 8.6 %shard_map.257 = (f32[256,1024]{1,0:T(8,128)}, f32[256,1024]{1,0:T(8,128)}, bf16[256,1536]{1,0:T(8,128)(2,1)}) custom-call(bf16[256,1536]{1,0:T(8,128)(2,1)} %bitcast.75, bf16[2,768,1024]{2,1,0:T(8,128)(2,1)} %wg.11, bf16[2,768,1024]{2,1,0:T(8,128)(2,1)} %wu.11, bf16[2,1024,768]{2,1,0:T(8,128)(2,1)} %wd.11, ...), custom_call_target="tpu_custom_call" | custom-call | flops 7699999744 | tf_op jit(solution)/shard_map/pallas_call | solution.py:651
  130.7 14.2 %all_to_all.101 = bf16[4,64,1536]{2,1,0:T(8,128)(2,1)S(1)} all-to-all(bf16[4,64,1536]{2,1,0:T(8,128)(2,1)} %bitcast.76), channel_id=1, replica_groups=mesh['fsdp'=2,'context'=4,'tensor'=4] {'tensor'}, dimensions={0} | all-to-all | bytes 1572864 | tf_op jit(solution)/shard_map/all_to_all | solution.py:83
  153.7 15.4 %all-to-all-done.5 = bf16[4,64,1536]{2,1,0:T(8,128)(2,1)S(1)} async-done(((bf16[4,64,1536]{2,1,0:T(8,128)(2,1)}), bf16[4,64,1536]{2,1,0:T(8,128)(2,1)S(1)}, u32[]{:S(2)}, u32[]{:S(2)}) %all-to-all-start.5) | async-done | bytes 786464 | tf_op jit(solution)/shard_map/all_to_all | solution.py:48
  187.5 11.1 %collective-permute-done.18.refs_4_ = bf16[64,1536]{1,0:T(8,128)(2,1)S(1)} collective-permute-done((bf16[64,1536]{1,0:T(8,128)(2,1)S(1)}, bf16[64,1536]{1,0:T(8,128)(2,1)S(1)}, u32[]{:S(2)}, u32[]{:S(2)}) %collective-permute-start.18) | collective-permute-done | bytes 196640 | tf_op jit(solution)/shard_map/ppermute | solution.py:25
  202.5 19.2 %shard_map.261 = (bf16[1024,1536]{1,0:T(8,128)(2,1)}, bf16[1024,384]{1,0:T(8,128)(2,1)}, bf16[1024,384]{1,0:T(8,128)(2,1)}, bf16[1024,384]{1,0:T(8,128)(2,1)}, f...) custom-call(s32[2]{0:T(128)} %pad_add_fusion.refs_0_, ...), custom_call_target="tpu_custom_call" | custom-call | flops 20899999744 | tf_op jit(solution)/shard_map/pallas_call | solution.py:584
  233.7 11.7 %all_to_all.102 = bf16[4,64,1536]{2,1,0:T(8,128)(2,1)} all-to-all(bf16[4,64,1536]{2,1,0:T(8,128)(2,1)S(1)} %broadcast_in_dim.39), channel_id=1, replica_groups=mesh['fsdp'=2,'context'=4,'tensor'=4] {'tensor'}, dimensions={0} | all-to-all | bytes 1572864 | tf_op jit(solution)/shard_map/all_to_all | solution.py:48
  245.4 8.5 %shard_map.262 = (f32[256,1024]{1,0:T(8,128)}, f32[256,1024]{1,0:T(8,128)}, bf16[256,1536]{1,0:T(8,128)(2,1)}) custom-call(bf16[256,1536]{1,0:T(8,128)(2,1)} %bitcast.77, bf16[2,768,1024]{2,1,0:T(8,128)(2,1)} %wg.11, bf16[2,768,1024]{2,1,0:T(8,128)(2,1)} %wu.11, bf16[2,1024,768]{2,1,0:T(8,128)(2,1)} %wd.11, ...), custom_call_target="tpu_custom_call" | custom-call | flops 7699999744 | tf_op jit(solution)/shard_map/pallas_call | solution.py:651
  253.9 9.3 %shard_map.263 = bf16[256,1536]{1,0:T(8,128)(2,1)} custom-call(bf16[256,1536]{1,0:T(8,128)(2,1)} %maximum_select_fusion.1.g_ref, f32[256,1024]{1,0:T(8,128)} %get-tuple-element.106.gt_ref, f32[256,1024]{1,0:T(8,128)} %get-tuple-element.107.up_ref, bf16[2,768,1024]{2,1,0:T(8,128)(2,1)} %wg.11, bf16[2,768,1024]{2,1,0:T(8,128)(2,1)} %wu.11, ...), custom_call_target="tpu_custom_call" | custom-call | flops 8800000000 | tf_op jit(solution)/shard_map/pallas_call | solution.py:665
  263.2 15.7 %all_to_all.103 = bf16[4,64,1536]{2,1,0:T(8,128)(2,1)S(1)} all-to-all(bf16[4,64,1536]{2,1,0:T(8,128)(2,1)} %bitcast.78), channel_id=1, replica_groups=mesh['fsdp'=2,'context'=4,'tensor'=4] {'tensor'}, dimensions={0} | all-to-all | bytes 1572864 | tf_op jit(solution)/shard_map/all_to_all | solution.py:83
  281.8 17.2 %collective-permute-start.22 = (bf16[64,1536]{1,0:T(8,128)(2,1)S(1)}, bf16[64,1536]{1,0:T(8,128)(2,1)S(1)}, u32[]{:S(2)}, u32[]{:S(2)}) collective-permute-start(bf16[64,1536]{1,0:T(8,128)(2,1)S(1)} %fusion.5), channel_id=1, source_target_pairs={{0,8},{4,12},{8,0},{12,4},{1,9},{5,13},{9,1},{13,5},{2,10},{6,14},... | collective-permute-start | bytes 589832 | tf_op jit(solution)/shard_map/ppermute | solution.py:25
  299.0 18.0 %collective-permute-done.22 = bf16[64,1536]{1,0:T(8,128)(2,1)S(1)} collective-permute-done((bf16[64,1536]{1,0:T(8,128)(2,1)S(1)}, bf16[64,1536]{1,0:T(8,128)(2,1)S(1)}, u32[]{:S(2)}, u32[]{:S(2)}) %collective-permute-start.22) | collective-permute-done | bytes 196640 | tf_op jit(solution)/shard_map/ppermute | solution.py:25
  317.2 22.4 %all_to_all.104 = bf16[4,128,1536]{2,1,0:T(8,128)(2,1)} all-to-all(bf16[4,128,1536]{2,1,0:T(8,128)(2,1)S(1)} %broadcast_in_dim.40), channel_id=1, replica_groups=mesh['fsdp'=2,'context'=4,'tensor'=4] {'tensor'}, dimensions={0} | all-to-all | bytes 3145728 | tf_op jit(solution)/shard_map/all_to_all | solution.py:48
  345.0 7.8 %all-to-all-done.11 = bf16[4,64,1536]{2,1,0:T(8,128)(2,1)S(1)} async-done(((bf16[4,64,1536]{2,1,0:T(8,128)(2,1)}), bf16[4,64,1536]{2,1,0:T(8,128)(2,1)S(1)}, u32[]{:S(2)}, u32[]{:S(2)}) %all-to-all-start.11) | async-done | bytes 786464 | tf_op jit(solution)/shard_map/all_to_all | solution.py:48
  353.7 19.9 %collective-permute-done.24.refs_2_ = bf16[256,1536]{1,0:T(8,128)(2,1)} collective-permute-done((bf16[256,1536]{1,0:T(8,128)(2,1)S(1)}, bf16[256,1536]{1,0:T(8,128)(2,1)}, u32[]{:S(2)}, u32[]{:S(2)}) %collective-permute-start.24) | collective-permute-done | bytes 786464 | tf_op jit(solution)/shard_map/ppermute | solution.py:25
  373.7 33.5 %shard_map.267 = (bf16[1024,1536]{1,0:T(8,128)(2,1)}, bf16[1024,384]{1,0:T(8,128)(2,1)}, bf16[1024,384]{1,0:T(8,128)(2,1)}, bf16[1024,384]{1,0:T(8,128)(2,1)}, b...) custom-call(s32[2]{0:T(128)} %pad_add_fusion.refs_0_, ...), custom_call_target="tpu_custom_call" | custom-call | flops 36300001280 | tf_op jit(solution)/shard_map/pallas_call | solution.py:614
  407.2 12.0 %all_to_all.105 = bf16[4,64,1536]{2,1,0:T(8,128)(2,1)S(1)} all-to-all(bf16[4,64,1536]{2,1,0:T(8,128)(2,1)} %bitcast.74), channel_id=1, replica_groups=mesh['fsdp'=2,'context'=4,'tensor'=4] {'tensor'}, dimensions={0} | all-to-all | bytes 1572864 | tf_op jit(solution)/shard_map/all_to_all | solution.py:83
  426.9 8.6 %shard_map.270 = (bf16[768,384]{1,0:T(8,128)(2,1)}, bf16[768,384]{1,0:T(8,128)(2,1)}, bf16[768,384]{1,0:T(8,128)(2,1)}, bf16[768,384]{1,0:T(8,128)(2,1)}, bf16[7...) custom-call(bf16[1024,1536]{1,0:T(8,128)(2,1)} %get-tuple-element.118.refs_0_, ...), custom_call_target="tpu_custom_call" | custom-call | flops 7699999744 | tf_op jit(solution)/shard_map/pallas_call | solution.py:747
  438.6 9.2 %shard_map.271.refs_0_ = bf16[256,1536]{1,0:T(8,128)(2,1)} custom-call(bf16[256,1536]{1,0:T(8,128)(2,1)} %bitcast.69, f32[256,1024]{1,0:T(8,128)} %get-tuple-element.116.gt_ref, f32[256,1024]{1,0:T(8,128)} %get-tuple-element.117.up_ref, bf16[2,768,1024]{2,1,0:T(8,128)(2,1)} %wg.11, bf16[2,768,1024]{2,1,0:T(8,128)(2,1)} %wu.11, bf16[2,1024,768]{2,1,0:T(8,128)(2,1)} %wd.11, ...), custom_call_target="tpu_custom_call" | custom-call | flops 8800000000 | tf_op jit(solution)/shard_map/pallas_call | solution.py:665
  469.2 9.6 %shard_map.274 = (f32[2,768,384]{2,1,0:T(8,128)}, f32[2,768,384]{2,1,0:T(8,128)}, f32[2,768,384]{2,1,0:T(8,128)}, f32[2,768,384]{2,1,0:T(8,128)}, f32[768,128]{1,0:T(8,128)}, /*index=5*/f32[2,384,768]{2,1,0:T(8,128)}) custom-call(bf16[1024,1536]{1,0:T(8,128)(2,1)} %get-tuple-element.11, ...), custom_call_target="tpu_custom_call", output_to_operand_aliasing={{0}: (14, {}), {1}: (15, {}), {2}: (16, {}), {3}: (17, {}),... | custom-call | flops 7699999744 | tf_op jit(solution)/shard_map/pallas_call | solution.py:747
  490.0 17.0 %collective-permute-done.32.refs_0_ = bf16[64,1536]{1,0:T(8,128)(2,1)S(1)} collective-permute-done((bf16[64,1536]{1,0:T(8,128)(2,1)S(1)}, bf16[64,1536]{1,0:T(8,128)(2,1)S(1)}, u32[]{:S(2)}, u32[]{:S(2)}) %collective-permute-start.32) | collective-permute-done | bytes 196640 | tf_op jit(solution)/shard_map/ppermute | solution.py:25
  512.3 21.4 %shard_map.276 = (bf16[1024,1024]{1,0:T(8,128)(2,1)}, bf16[1024,1024]{1,0:T(8,128)(2,1)}, bf16[1024,1024]{1,0:T(8,128)(2,1)}, bf16[768,1024]{1,0:T(8,128)(2,1)},...) custom-call(bf16[1024,1536]{1,0:T(8,128)(2,1)} %all-gather.11.cloned.1.call-done.b_ref, ...), custom_call_target="tpu_custom_call" | custom-call | flops 26400000000 | tf_op jit(solution)/shard_map/pallas_call | solution.py:682
  536.7 33.7 %shard_map.278 = (bf16[1024,1536]{1,0:T(8,128)(2,1)}, bf16[1024,384]{1,0:T(8,128)(2,1)}, bf16[1024,384]{1,0:T(8,128)(2,1)}, bf16[1024,384]{1,0:T(8,128)(2,1)}, b...) custom-call(s32[2]{0:T(128)} %pad_add_fusion.refs_0_, ...), custom_call_target="tpu_custom_call" | custom-call | flops 36300001280 | tf_op jit(solution)/shard_map/pallas_call | solution.py:614
  573.2 21.2 %shard_map.268 = (bf16[1024,1024]{1,0:T(8,128)(2,1)}, bf16[1024,1024]{1,0:T(8,128)(2,1)}, bf16[1024,1024]{1,0:T(8,128)(2,1)}, bf16[768,1024]{1,0:T(8,128)(2,1)},...) custom-call(bf16[1024,1536]{1,0:T(8,128)(2,1)} %all-gather.7.cloned.1.call-done.refs_1_.b_ref, ...), custom_call_target="tpu_custom_call" | custom-call | flops 26400000000 | tf_op jit(solution)/shard_map/pallas_call | solution.py:682
  601.2 12.0 %shard_map.282 = (f32[2,768,1024]{2,1,0:T(8,128)}, f32[2,768,1024]{2,1,0:T(8,128)}, f32[2,1024,768]{2,1,0:T(8,128)}) custom-call(bf16[1024,1536]{1,0:T(8,128)(2,1)} %all-gather.11.cloned.1.call-done.b_ref, bf16[1024,1536]{1,0:T(8,128)(2,1)} %all-gather.5.cloned.1.call-done.refs_1_.g_ref, ...), custom_call_target="tpu_custom_call", output_to_operand_aliasing={{0}: (8, {}), {1}: (9, {}), {2}: (10, {})} | custom-call | flops 9900000256 | tf_op jit(solution)/shard_map/pallas_call | solution.py:707
  619.8 8.4 %shard_map.280 = (bf16[768,384]{1,0:T(8,128)(2,1)}, bf16[768,384]{1,0:T(8,128)(2,1)}, bf16[768,384]{1,0:T(8,128)(2,1)}, bf16[768,384]{1,0:T(8,128)(2,1)}, bf16[7...) custom-call(bf16[1024,1536]{1,0:T(8,128)(2,1)} %get-tuple-element.149.refs_0_, ...), custom_call_target="tpu_custom_call" | custom-call | flops 7699999744 | tf_op jit(solution)/shard_map/pallas_call | solution.py:747
  631.8 11.8 %shard_map.283 = (f32[2,768,1024]{2,1,0:T(8,128)}, f32[2,768,1024]{2,1,0:T(8,128)}, f32[2,1024,768]{2,1,0:T(8,128)}) custom-call(bf16[1024,1536]{1,0:T(8,128)(2,1)} %all-gather.7.cloned.1.call-done.refs_1_.b_ref, bf16[1024,1536]{1,0:T(8,128)(2,1)} %all-gather.9.cloned.1.call-done.g_ref, ...), custom_call_target="tpu_custom_call", output_to_operand_aliasing={{0}: (8, {}), {1}: (9, {}), {2}: (10, {})} | custom-call | flops 9900000256 | tf_op jit(solution)/shard_map/pallas_call | solution.py:707
  645.1 9.5 %shard_map.281 = (f32[2,768,384]{2,1,0:T(8,128)}, f32[2,768,384]{2,1,0:T(8,128)}, f32[2,768,384]{2,1,0:T(8,128)}, f32[2,768,384]{2,1,0:T(8,128)}, f32[768,128]{1,0:T(8,128)}, /*index=5*/f32[2,384,768]{2,1,0:T(8,128)}) custom-call(bf16[1024,1536]{1,0:T(8,128)(2,1)} %get-tuple-element.14, ...), custom_call_target="tpu_custom_call", output_to_operand_aliasing={{0}: (14, {}), {1}: (15, {}), {2}: (16, {}), {3}: (17, {}),... | custom-call | flops 7699999744 | tf_op jit(solution)/shard_map/pallas_call | solution.py:747
  664.0 11.7 %all-to-all-done.19 = f32[16,1,6144]{2,1,0:T(1,128)S(1)} async-done(((f32[16,1,6144]{2,1,0:T(1,128)}), f32[16,1,6144]{2,1,0:T(1,128)S(1)}, u32[]{:S(2)}, u32[]{:S(2)}) %all-to-all-start.19) | async-done | bytes 393248 | tf_op jit(solution)/shard_map/all_to_all | solution.py:48
  (360 shorter events, 194.6 us)
Async XLA Ops:
  12.0 40.4 %collective-permute-start.1 = (bf16[256,1536]{1,0:T(8,128)(2,1)S(1)}, bf16[256,1536]{1,0:T(8,128)(2,1)}, u32[]{:S(2)}, u32[]{:S(2)}) collective-permute-start(bf16[256,1536]{1,0:T(8,128)(2,1)S(1)} %multiply_convert_fusion.refs_1_), channel_id=1, source_target_pairs={{0,4},{4,0},{8,12},{12,8},{1,5},{5,1},{9,13},{13,9},{2,6},{6,2},{1... | collective-permute-start | bytes 2359304 | tf_op jit(solution)/shard_map/ppermute | solution.py:25
  15.3 24.3 %collective-permute-start.2 = (bf16[64,1536]{1,0:T(8,128)(2,1)}, bf16[64,1536]{1,0:T(8,128)(2,1)S(1)}, u32[]{:S(2)}, u32[]{:S(2)}) collective-permute-start(bf16[64,1536]{1,0:T(8,128)(2,1)} %constant_dynamic-slice_fusion.1), channel_id=1, source_target_pairs={{0,8},{4,12},{8,0},{12,4},{1,9},{5,13},{9,1},{13,5},{2,10},{6,14},... | collective-permute-start | bytes 589832 | tf_op jit(solution)/shard_map/ppermute | solution.py:25
  18.5 21.1 %all-to-all-start = ((s32[4,1,256]{2,1,0:T(1,128)}), s32[4,1,256]{2,1,0:T(1,128)}, u32[]{:S(2)}, u32[]{:S(2)}) async-start(s32[4,1,256]{2,1,0:T(1,128)} %broadcast_in_dim.33), calls=%async_computation | async-start | bytes 8192 | tf_op jit(solution)/shard_map/all_to_all | solution.py:48
  22.3 20.9 %collective-permute-start.12 = (bf16[2,768,6]{1,0,2:T(2,128)(2,1)}, bf16[2,768,6]{1,0,2:T(2,128)(2,1)}, u32[]{:S(2)}, u32[]{:S(2)}) collective-permute-start(bf16[2,768,6]{1,0,2:T(2,128)(2,1)} %param.22), channel_id=1, source_target_pairs={{0,16},{16,0},{1,17},{17,1},{2,18},{18,2},{3,19},{19,3},{4,20},{20... | collective-permute-start | bytes 55304 | tf_op jit(solution)/shard_map/ppermute | solution.py:25
  23.0 20.8 %collective-permute-start.6 = (bf16[64,1536]{1,0:T(8,128)(2,1)}, bf16[64,1536]{1,0:T(8,128)(2,1)S(1)}, u32[]{:S(2)}, u32[]{:S(2)}) collective-permute-start(bf16[64,1536]{1,0:T(8,128)(2,1)} %constant_dynamic-slice_fusion.1), channel_id=1, source_target_pairs={{0,12},{4,8},{8,4},{12,0},{1,13},{5,9},{9,5},{13,1},{2,14},{6,10},... | collective-permute-start | bytes 589832 | tf_op jit(solution)/shard_map/ppermute | solution.py:25
  43.9 20.5 %collective-permute-start.7 = (bf16[2,768,384]{2,1,0:T(8,128)(2,1)}, bf16[2,768,384]{2,1,0:T(8,128)(2,1)}, u32[]{:S(2)}, u32[]{:S(2)}) collective-permute-start(bf16[2,768,384]{2,1,0:T(8,128)(2,1)} %refs_4_.3), channel_id=1, source_target_pairs={{0,16},{16,0},{1,17},{17,1},{2,18},{18,2},{3,19},{19,3},{4,20},{20... | collective-permute-start | bytes 3538952 | tf_op jit(solution)/shard_map/ppermute | solution.py:25
  64.3 57.8 %collective-permute-start.13 = (bf16[2,768,1024]{2,1,0:T(8,128)(2,1)}, bf16[2,768,1024]{2,1,0:T(8,128)(2,1)}, u32[]{:S(2)}, u32[]{:S(2)}) collective-permute-start(bf16[2,768,1024]{2,1,0:T(8,128)(2,1)} %wg.11), channel_id=1, source_target_pairs={{0,16},{16,0},{1,17},{17,1},{2,18},{18,2},{3,19},{19,3},{4,20},{20... | collective-permute-start | bytes 9437192 | tf_op jit(solution)/shard_map/ppermute | solution.py:25
  64.8 57.3 %collective-permute-start.14 = (bf16[2,768,1024]{2,1,0:T(8,128)(2,1)}, bf16[2,768,1024]{2,1,0:T(8,128)(2,1)}, u32[]{:S(2)}, u32[]{:S(2)}) collective-permute-start(bf16[2,768,1024]{2,1,0:T(8,128)(2,1)} %wu.11), channel_id=1, source_target_pairs={{0,16},{16,0},{1,17},{17,1},{2,18},{18,2},{3,19},{19,3},{4,20},{20... | collective-permute-start | bytes 9437192 | tf_op jit(solution)/shard_map/ppermute | solution.py:25
  64.9 57.2 %collective-permute-start.15 = (bf16[2,1024,768]{2,1,0:T(8,128)(2,1)}, bf16[2,1024,768]{2,1,0:T(8,128)(2,1)}, u32[]{:S(2)}, u32[]{:S(2)}) collective-permute-start(bf16[2,1024,768]{2,1,0:T(8,128)(2,1)} %wd.11), channel_id=1, source_target_pairs={{0,16},{16,0},{1,17},{17,1},{2,18},{18,2},{3,19},{19,3},{4,20},{20... | collective-permute-start | bytes 9437192 | tf_op jit(solution)/shard_map/ppermute | solution.py:25
  95.0 92.5 %all-gather.5.cloned.1.call-start = ((), (), s32[]{:S(2)}) async-start(), calls=%async_computation.20 | async-start | bytes 3342336 | tf_op jit(solution)/shard_map/all_gather | solution.py:52
  146.6 22.5 %all-to-all-start.5 = ((bf16[4,64,1536]{2,1,0:T(8,128)(2,1)}), bf16[4,64,1536]{2,1,0:T(8,128)(2,1)S(1)}, u32[]{:S(2)}, u32[]{:S(2)}) async-start(bf16[4,64,1536]{2,1,0:T(8,128)(2,1)} %broadcast_in_dim.37), calls=%async_computation.5 | async-start | bytes 1572864 | tf_op jit(solution)/shard_map/all_to_all | solution.py:48
  150.1 25.4 %collective-permute-start.17 = (bf16[64,1536]{1,0:T(8,128)(2,1)S(1)}, bf16[64,1536]{1,0:T(8,128)(2,1)S(1)}, u32[]{:S(2)}, u32[]{:S(2)}) collective-permute-start(bf16[64,1536]{1,0:T(8,128)(2,1)S(1)} %multiply_convert_fusion.2), channel_id=1, source_target_pairs={{0,8},{4,12},{8,0},{12,4},{1,9},{5,13},{9,1},{13,5},{2,10},{6,14},... | collective-permute-start | bytes 589832 | tf_op jit(solution)/shard_map/ppermute | solution.py:25
  152.3 23.3 %collective-permute-start.21 = (bf16[64,1536]{1,0:T(8,128)(2,1)S(1)}, bf16[64,1536]{1,0:T(8,128)(2,1)S(1)}, u32[]{:S(2)}, u32[]{:S(2)}) collective-permute-start(bf16[64,1536]{1,0:T(8,128)(2,1)S(1)} %multiply_convert_fusion.2), channel_id=1, source_target_pairs={{0,12},{4,8},{8,4},{12,0},{1,13},{5,9},{9,5},{13,1},{2,14},{6,10},... | collective-permute-start | bytes 589832 | tf_op jit(solution)/shard_map/ppermute | solution.py:25
  169.1 32.5 %collective-permute-start.16 = (bf16[256,1536]{1,0:T(8,128)(2,1)S(1)}, bf16[256,1536]{1,0:T(8,128)(2,1)}, u32[]{:S(2)}, u32[]{:S(2)}) collective-permute-start(bf16[256,1536]{1,0:T(8,128)(2,1)S(1)} %bitcast.67), channel_id=1, source_target_pairs={{0,4},{4,0},{8,12},{12,8},{1,5},{5,1},{9,13},{13,9},{2,6},{6,2},{1... | collective-permute-start | bytes 2359304 | tf_op jit(solution)/shard_map/ppermute | solution.py:25
  178.8 22.7 %all-to-all-start.6 = ((bf16[4,64,1536]{2,1,0:T(8,128)(2,1)}), bf16[4,64,1536]{2,1,0:T(8,128)(2,1)S(1)}, u32[]{:S(2)}, u32[]{:S(2)}) async-start(bf16[4,64,1536]{2,1,0:T(8,128)(2,1)} %broadcast_in_dim.38), calls=%async_computation.6 | async-start | bytes 1572864 | tf_op jit(solution)/shard_map/all_to_all | solution.py:48
  225.2 127.6 %all-gather.7.cloned.1.call-start = ((), (), s32[]{:S(2)}) async-start(), calls=%async_computation.22 | async-start | bytes 3342336 | tf_op jit(solution)/shard_map/all_gather | solution.py:52
  281.8 35.2 %collective-permute-start.22 = (bf16[64,1536]{1,0:T(8,128)(2,1)S(1)}, bf16[64,1536]{1,0:T(8,128)(2,1)S(1)}, u32[]{:S(2)}, u32[]{:S(2)}) collective-permute-start(bf16[64,1536]{1,0:T(8,128)(2,1)S(1)} %fusion.5), channel_id=1, source_target_pairs={{0,8},{4,12},{8,0},{12,4},{1,9},{5,13},{9,1},{13,5},{2,10},{6,14},... | collective-permute-start | bytes 589832 | tf_op jit(solution)/shard_map/ppermute | solution.py:25
  344.0 168.2 %all-gather.11.cloned.1.call-start = ((), (), s32[]{:S(2)}) async-start(), calls=%async_computation.24 | async-start | bytes 3342336 | tf_op jit(solution)/shard_map/all_gather | solution.py:52
  344.8 228.5 %all-gather.9.cloned.1.call-start = ((), (), s32[]{:S(2)}) async-start(), calls=%async_computation.23 | async-start | bytes 3342336 | tf_op jit(solution)/shard_map/all_gather | solution.py:52
  352.9 20.8 %collective-permute-start.24 = (bf16[256,1536]{1,0:T(8,128)(2,1)S(1)}, bf16[256,1536]{1,0:T(8,128)(2,1)}, u32[]{:S(2)}, u32[]{:S(2)}) collective-permute-start(bf16[256,1536]{1,0:T(8,128)(2,1)S(1)} %bitcast.70), channel_id=1, source_target_pairs={{0,4},{4,0},{8,12},{12,8},{1,5},{5,1},{9,13},{13,9},{2,6},{6,2},{1... | collective-permute-start | bytes 2359304 | tf_op jit(solution)/shard_map/ppermute | solution.py:25
  453.1 141.9 %all-reduce.4.cloned.1.call-start = ((), (), s32[]{:S(2)}) async-start(), calls=%async_computation.21 | async-start | bytes 1572864 | tf_op jit(solution)/shard_map/psum | solution.py:929
  465.6 41.4 %all-to-all-start.15 = ((bf16[4,64,1536]{2,1,0:T(8,128)(2,1)}), bf16[4,64,1536]{2,1,0:T(8,128)(2,1)S(1)}, u32[]{:S(2)}, u32[]{:S(2)}) async-start(bf16[4,64,1536]{2,1,0:T(8,128)(2,1)} %broadcast_in_dim.43), calls=%async_computation.15 | async-start | bytes 1572864 | tf_op jit(solution)/shard_map/all_to_all | solution.py:48
  481.9 25.1 %collective-permute-start.32 = (bf16[64,1536]{1,0:T(8,128)(2,1)S(1)}, bf16[64,1536]{1,0:T(8,128)(2,1)S(1)}, u32[]{:S(2)}, u32[]{:S(2)}) collective-permute-start(bf16[64,1536]{1,0:T(8,128)(2,1)S(1)} %get-tuple-element.232), channel_id=1, source_target_pairs={{0,8},{4,12},{8,0},{12,4},{1,9},{5,13},{9,1},{13,5},{2,10},{6,14},... | collective-permute-start | bytes 589832 | tf_op jit(solution)/shard_map/ppermute | solution.py:25
  508.4 27.2 %all-to-all-start.16 = ((bf16[4,128,1536]{2,1,0:T(8,128)(2,1)}), bf16[4,128,1536]{2,1,0:T(8,128)(2,1)S(1)}, u32[]{:S(2)}, u32[]{:S(2)}) async-start(bf16[4,128,1536]{2,1,0:T(8,128)(2,1)} %broadcast_in_dim.44), calls=%async_computation.16 | async-start | bytes 3145728 | tf_op jit(solution)/shard_map/all_to_all | solution.py:48
  512.2 22.2 %collective-permute-start.31 = (bf16[256,1536]{1,0:T(8,128)(2,1)S(1)}, bf16[256,1536]{1,0:T(8,128)(2,1)}, u32[]{:S(2)}, u32[]{:S(2)}) collective-permute-start(bf16[256,1536]{1,0:T(8,128)(2,1)S(1)} %bitcast.65), channel_id=1, source_target_pairs={{0,4},{4,0},{8,12},{12,8},{1,5},{5,1},{9,13},{13,9},{2,6},{6,2},{1... | collective-permute-start | bytes 2359304 | tf_op jit(solution)/shard_map/ppermute | solution.py:25
  533.7 63.8 %collective-permute-start.34 = (bf16[768,1024]{1,0:T(8,128)(2,1)}, bf16[768,1024]{1,0:T(8,128)(2,1)}, u32[]{:S(2)}, u32[]{:S(2)}) collective-permute-start(bf16[768,1024]{1,0:T(8,128)(2,1)} %get-tuple-element.146), channel_id=1, source_target_pairs={{0,16},{16,0},{1,17},{17,1},{2,18},{18,2},{3,19},{19,3},{4,20},{20... | collective-permute-start | bytes 4718600 | tf_op jit(solution)/shard_map/ppermute | solution.py:25
  533.7 63.9 %collective-permute-start.35 = (bf16[768,1024]{1,0:T(8,128)(2,1)}, bf16[768,1024]{1,0:T(8,128)(2,1)}, u32[]{:S(2)}, u32[]{:S(2)}) collective-permute-start(bf16[768,1024]{1,0:T(8,128)(2,1)} %get-tuple-element.147), channel_id=1, source_target_pairs={{0,16},{16,0},{1,17},{17,1},{2,18},{18,2},{3,19},{19,3},{4,20},{20... | collective-permute-start | bytes 4718600 | tf_op jit(solution)/shard_map/ppermute | solution.py:25
  534.2 63.5 %collective-permute-start.36 = (bf16[1024,768]{1,0:T(8,128)(2,1)}, bf16[1024,768]{1,0:T(8,128)(2,1)}, u32[]{:S(2)}, u32[]{:S(2)}) collective-permute-start(bf16[1024,768]{1,0:T(8,128)(2,1)} %get-tuple-element.148), channel_id=1, source_target_pairs={{0,16},{16,0},{1,17},{17,1},{2,18},{18,2},{3,19},{19,3},{4,20},{20... | collective-permute-start | bytes 4718600 | tf_op jit(solution)/shard_map/ppermute | solution.py:25
  594.5 36.4 %collective-permute-start.43 = (bf16[768,1024]{1,0:T(8,128)(2,1)}, bf16[768,1024]{1,0:T(8,128)(2,1)}, u32[]{:S(2)}, u32[]{:S(2)}) collective-permute-start(bf16[768,1024]{1,0:T(8,128)(2,1)} %get-tuple-element.167), channel_id=1, source_target_pairs={{0,16},{16,0},{1,17},{17,1},{2,18},{18,2},{3,19},{19,3},{4,20},{20... | collective-permute-start | bytes 4718600 | tf_op jit(solution)/shard_map/ppermute | solution.py:25
  594.7 36.5 %collective-permute-start.44 = (bf16[768,1024]{1,0:T(8,128)(2,1)}, bf16[768,1024]{1,0:T(8,128)(2,1)}, u32[]{:S(2)}, u32[]{:S(2)}) collective-permute-start(bf16[768,1024]{1,0:T(8,128)(2,1)} %get-tuple-element.168), channel_id=1, source_target_pairs={{0,16},{16,0},{1,17},{17,1},{2,18},{18,2},{3,19},{19,3},{4,20},{20... | collective-permute-start | bytes 4718600 | tf_op jit(solution)/shard_map/ppermute | solution.py:25
  597.5 33.9 %collective-permute-start.45 = (bf16[1024,768]{1,0:T(8,128)(2,1)}, bf16[1024,768]{1,0:T(8,128)(2,1)}, u32[]{:S(2)}, u32[]{:S(2)}) collective-permute-start(bf16[1024,768]{1,0:T(8,128)(2,1)} %get-tuple-element.169), channel_id=1, source_target_pairs={{0,16},{16,0},{1,17},{17,1},{2,18},{18,2},{3,19},{19,3},{4,20},{20... | collective-permute-start | bytes 4718600 | tf_op jit(solution)/shard_map/ppermute | solution.py:25
  615.4 40.3 %all-to-all-start.18 = ((bf16[4,64,1536]{2,1,0:T(8,128)(2,1)}), bf16[4,64,1536]{2,1,0:T(8,128)(2,1)S(1)}, u32[]{:S(2)}, u32[]{:S(2)}) async-start(bf16[4,64,1536]{2,1,0:T(8,128)(2,1)} %broadcast_in_dim.45), calls=%async_computation.18 | async-start | bytes 1572864 | tf_op jit(solution)/shard_map/all_to_all | solution.py:48
  (99 other events, 1086.3 us)
Sparse Core Ops, SparseCore 0:
  99.2 84.7 all-gather.4
  228.9 85.9 all-gather.6
  347.7 69.2 all-gather.10
  421.3 82.8 all-gather.8
  507.7 59.0 all-reduce.3

commit v10 on v9

--- a/solution.py
+++ b/solution.py
@@ -567,7 +567,7 @@
 
 
 def token_specs(tokens):
-    return [pl.BlockSpec((16, 128), lambda *_: (0, 0)) for _ in tokens]
+    return [pl.BlockSpec(memory_space=pl.ANY) for _ in tokens]
 
 
 def forward_own(place, parts, layer, w4, t4, wo, to, wf, bias, doc_start, piece_len):
@@ -909,13 +909,16 @@
             sends = after(sends, *saved[layer + 1]["received"])
         back, gain_grads[layers + layer] = norm_back(received_sum(sends), s["mixed"], s["inverse_two"], gain_two)
         grad_mixed = grad + back
-        y_parts, y_far = all_rows(grad_mixed.astype(bf16), together=True)
+        y_shard = grad_mixed.astype(bf16)
+        if layer < last:
+            attention_mine_of(layer + 1)
+            y_shard = after(y_shard, results[0])
+        y_parts, y_far = all_rows(y_shard, together=layer < last)
         tokens = ()
         if layer < last:
             above = saved[layer + 1]
-            attention_mine_of(layer + 1)
             ffn_theirs_of(layer + 1, *y_far)
-            tokens = (results[0], above["values"][0])
+            tokens = (above["values"][0], s["g_rows"])
         elif shared_rows:
             tokens = [x["b_rows"] for x in saved[:-1]]
         kept = (*s["kept"][:-1], after(s["kept"][-1], *tokens))
@@ -927,8 +930,6 @@
             block_sum = own_block(last_sends).astype(f32) + s["mixed"]
             with_rows = lax.dynamic_update_slice_in_dim(last_sends, block_sum.astype(bf16), t * block, 0)
             output = lax.psum(after(with_rows, token), "tensor")
-        if layer < last:
-            sends = after(sends, *above["ffn_received"])
         if shared_rows and layer == last:
             s.update(b_rows=sequence_rows(after(s["b_shard"], token)), g_rows=g_last)
         s["grads"] = (s["a"], (dq, dk, dv, dg), dz, u, y)
@@ -940,18 +941,19 @@
     for layer in reversed(range(1, layers)):
         ffn_mine_of(layer)
     ffn_theirs_of(0)
-    attention_theirs_of(0, saved[0]["values"][0], grad)
-    attention_mine_of(0, *saved[0]["ffn_received"])
+    grad = after(grad, saved[0]["values"][0])
+    attention_theirs_of(0, grad)
+    gain_total = jnp.stack(gain_grads).reshape(1, -1)
+    for axis in (("context", "tensor"),) if shared_rows else ("context", "tensor"):
+        gain_total = jnp.sum(gathered(gain_total, axis), axis=0, keepdims=True)
+    gain_total = gain_total.reshape(2 * layers, width)
+    gain_total = gain_total[:, :half] + other(gain_total[:, half:])
+    attention_mine_of(0, gain_total, *saved[0]["ffn_received"])
     ffn_mine_of(0)
     if not shared_rows:
         results[5:] = [lax.psum(x, "context") for x in results[5:]]
     output = features(after(output, saved[0]["values"][0])).reshape(1, piece_len, width)
     grad_input = finish(grad)
-    gain_total = jnp.stack(gain_grads).reshape(1, -1)
-    for axis in (("context", "tensor"),) if shared_rows else ("context", "tensor"):
-        gain_total = jnp.sum(gathered(gain_total, axis), axis=0, keepdims=True)
-    gain_total = gain_total.reshape(2 * layers, width)
-    gain_total = gain_total[:, :half] + other(gain_total[:, half:])
     return (
         output, grad_input, *results[:5], jnp.stack(small[0]), jnp.stack(small[1]),
         gain_total[:layers], gain_total[layers:], *results[5:],

time: 695 us -> 678 us (0.976)
  waiting for transfers between devices: 171 us -> 147 us
  starting transfers between devices: 106 us -> 124 us
  blocking collectives: 91.2 us -> 79.2 us
    ppermute x49 -> x52, waiting for transfers between devices: 92.4 us -> 68.8 us  [swap(): return lax.ppermute(x, axis, [(i, i ^ k) for i in range(n)])]
    all_to_all x3 -> x2, blocking collectives: 49.3 us -> 26.8 us  [gathered(): lax.all_to_all(copies, axis, 0, 0, tiled=True)]
    ppermute x49 -> x52, starting transfers between devices: 50.3 us -> 63.5 us  [swap(): return lax.ppermute(x, axis, [(i, i ^ k) for i in range(n)])]
    all_to_all x3, blocking collectives: 41.9 us -> 52.3 us  [received_sum(): lax.all_to_all(sends.reshape(count, -1, sends.shape[1]), 'tensor', 0, 0,...]
    all_to_all x10 -> x11, waiting for transfers between devices: 55.2 us -> 59.1 us  [gathered(): lax.all_to_all(copies, axis, 0, 0, tiled=True)]
    all_to_all x10 -> x11, starting transfers between devices: 40.2 us -> 44 us  [gathered(): lax.all_to_all(copies, axis, 0, 0, tiled=True)]
    unnamed x127 -> x153, local copies, waits for them, and re-layouts: 12.5 us -> 15.7 us
  transfers between devices with their start and end apart: 68 -> 72, of which waited for: 22 -> 23; matrix products, arithmetic and copies ran while one was open for 6% -> 6% of each run, Pallas kernels for 33% -> 30%
where the time goes in v10:
time: 678 us; the launch traced here: 668 us
  Pallas kernels  243 us (36%)
  waiting for transfers between devices  147 us (22%)
  starting transfers between devices  124 us (18%)
  blocking collectives  79.2 us (12%)
  local copies, waits for them, and re-layouts  40.6 us (6%)
  other arithmetic  19.7 us (3%)
  between operations  15.3 us (2%)
    ppermute x52, waiting for transfers between devices, swap(): return lax.ppermute(x, axis, [(i, i ^ k) for i in range(n)])  68.8 us
    pallas_call x2, Pallas kernels, attention_backward(): pl.pallas_call(functools.partial(backward_kernel, len(parts), piece_len,...  67.1 us
    ppermute x52, starting transfers between devices, swap(): return lax.ppermute(x, axis, [(i, i ^ k) for i in range(n)])  63.5 us
    all_to_all x11, waiting for transfers between devices, gathered(): lax.all_to_all(copies, axis, 0, 0, tiled=True)  59.1 us
    all_to_all x3, blocking collectives, received_sum(): lax.all_to_all(sends.reshape(count, -1, sends.shape[1]), 'tensor', 0, 0,...  52.3 us
    all_to_all x11, starting transfers between devices, gathered(): lax.all_to_all(copies, axis, 0, 0, tiled=True)  44 us
    pallas_call x2, Pallas kernels, ffn_theirs(): pl.pallas_call(ffn_theirs_kernel, grid=(inner // hidden_block,), in_specs...  42.1 us
    pallas_call x2, Pallas kernels, forward_own(): pl.pallas_call(functools.partial(forward_own_kernel, len(parts), piece_le...  38.3 us
  transfers between devices with their start and end apart: 72, of which 23 were waited for; matrix products, arithmetic and copies ran while one was open for 6% of the time, Pallas kernels for 30%

profile of v10, /device:TPU:0, one launch (start us, length us, event | category | flops | bytes accessed | tf_op | source)
XLA Modules:
  0.0 668.3 jit_solution(2164864210478346154)
XLA Ops:
  26.6 13.1 %all-to-all-done = s32[4,1,256]{2,1,0:T(1,128)} async-done(((s32[4,1,256]{2,1,0:T(1,128)}), s32[4,1,256]{2,1,0:T(1,128)}, u32[]{:S(2)}, u32[]{:S(2)}) %all-to-all-start) | async-done | bytes 4128 | tf_op jit(solution)/shard_map/all_to_all | solution.py:48
  72.3 19.2 %shard_map.256 = (bf16[1024,1536]{1,0:T(8,128)(2,1)}, bf16[1024,384]{1,0:T(8,128)(2,1)}, bf16[1024,384]{1,0:T(8,128)(2,1)}, bf16[1024,384]{1,0:T(8,128)(2,1)}, f...) custom-call(s32[2]{0:T(128)} %pad_add_fusion.refs_0_, ...), custom_call_target="tpu_custom_call" | custom-call | flops 20899999744 | tf_op jit(solution)/shard_map/pallas_call | solution.py:584
  96.7 9.2 %all-to-all-done.2 = bf16[4,64,1536]{2,1,0:T(8,128)(2,1)S(1)} async-done(((bf16[4,64,1536]{2,1,0:T(8,128)(2,1)}), bf16[4,64,1536]{2,1,0:T(8,128)(2,1)S(1)}, u32[]{:S(2)}, u32[]{:S(2)}) %all-to-all-start.2) | async-done | bytes 786464 | tf_op jit(solution)/shard_map/all_to_all | solution.py:83
  106.9 15.2 %all_to_all.100 = bf16[4,64,1536]{2,1,0:T(8,128)(2,1)} all-to-all(bf16[4,64,1536]{2,1,0:T(8,128)(2,1)S(1)} %broadcast_in_dim.36), channel_id=1, replica_groups=mesh['fsdp'=2,'context'=4,'tensor'=4] {'tensor'}, dimensions={0} | all-to-all | bytes 1572864 | tf_op jit(solution)/shard_map/all_to_all | solution.py:48
  122.1 8.6 %shard_map.257 = (f32[256,1024]{1,0:T(8,128)}, f32[256,1024]{1,0:T(8,128)}, bf16[256,1536]{1,0:T(8,128)(2,1)}) custom-call(bf16[256,1536]{1,0:T(8,128)(2,1)} %bitcast.73, bf16[2,768,1024]{2,1,0:T(8,128)(2,1)} %wg.11, bf16[2,768,1024]{2,1,0:T(8,128)(2,1)} %wu.11, bf16[2,1024,768]{2,1,0:T(8,128)(2,1)} %wd.11, ...), custom_call_target="tpu_custom_call" | custom-call | flops 7699999744 | tf_op jit(solution)/shard_map/pallas_call | solution.py:651
  130.7 14.2 %all_to_all.101 = bf16[4,64,1536]{2,1,0:T(8,128)(2,1)S(1)} all-to-all(bf16[4,64,1536]{2,1,0:T(8,128)(2,1)} %bitcast.74), channel_id=1, replica_groups=mesh['fsdp'=2,'context'=4,'tensor'=4] {'tensor'}, dimensions={0} | all-to-all | bytes 1572864 | tf_op jit(solution)/shard_map/all_to_all | solution.py:83
  153.7 15.4 %all-to-all-done.5 = bf16[4,64,1536]{2,1,0:T(8,128)(2,1)S(1)} async-done(((bf16[4,64,1536]{2,1,0:T(8,128)(2,1)}), bf16[4,64,1536]{2,1,0:T(8,128)(2,1)S(1)}, u32[]{:S(2)}, u32[]{:S(2)}) %all-to-all-start.5) | async-done | bytes 786464 | tf_op jit(solution)/shard_map/all_to_all | solution.py:48
  187.5 11.1 %collective-permute-done.18.refs_4_ = bf16[64,1536]{1,0:T(8,128)(2,1)S(1)} collective-permute-done((bf16[64,1536]{1,0:T(8,128)(2,1)S(1)}, bf16[64,1536]{1,0:T(8,128)(2,1)S(1)}, u32[]{:S(2)}, u32[]{:S(2)}) %collective-permute-start.18) | collective-permute-done | bytes 196640 | tf_op jit(solution)/shard_map/ppermute | solution.py:25
  202.5 19.2 %shard_map.261 = (bf16[1024,1536]{1,0:T(8,128)(2,1)}, bf16[1024,384]{1,0:T(8,128)(2,1)}, bf16[1024,384]{1,0:T(8,128)(2,1)}, bf16[1024,384]{1,0:T(8,128)(2,1)}, f...) custom-call(s32[2]{0:T(128)} %pad_add_fusion.refs_0_, ...), custom_call_target="tpu_custom_call" | custom-call | flops 20899999744 | tf_op jit(solution)/shard_map/pallas_call | solution.py:584
  225.9 7.3 %all-to-all-done.7 = bf16[4,64,1536]{2,1,0:T(8,128)(2,1)S(1)} async-done(((bf16[4,64,1536]{2,1,0:T(8,128)(2,1)}), bf16[4,64,1536]{2,1,0:T(8,128)(2,1)S(1)}, u32[]{:S(2)}, u32[]{:S(2)}) %all-to-all-start.7) | async-done | bytes 786464 | tf_op jit(solution)/shard_map/all_to_all | solution.py:83
  233.7 11.6 %all_to_all.102 = bf16[4,64,1536]{2,1,0:T(8,128)(2,1)} all-to-all(bf16[4,64,1536]{2,1,0:T(8,128)(2,1)S(1)} %broadcast_in_dim.39), channel_id=1, replica_groups=mesh['fsdp'=2,'context'=4,'tensor'=4] {'tensor'}, dimensions={0} | all-to-all | bytes 1572864 | tf_op jit(solution)/shard_map/all_to_all | solution.py:48
  245.3 8.5 %shard_map.262 = (f32[256,1024]{1,0:T(8,128)}, f32[256,1024]{1,0:T(8,128)}, bf16[256,1536]{1,0:T(8,128)(2,1)}) custom-call(bf16[256,1536]{1,0:T(8,128)(2,1)} %bitcast.75, bf16[2,768,1024]{2,1,0:T(8,128)(2,1)} %wg.11, bf16[2,768,1024]{2,1,0:T(8,128)(2,1)} %wu.11, bf16[2,1024,768]{2,1,0:T(8,128)(2,1)} %wd.11, ...), custom_call_target="tpu_custom_call" | custom-call | flops 7699999744 | tf_op jit(solution)/shard_map/pallas_call | solution.py:651
  253.8 9.3 %shard_map.263 = bf16[256,1536]{1,0:T(8,128)(2,1)} custom-call(bf16[256,1536]{1,0:T(8,128)(2,1)} %maximum_select_fusion.1.g_ref, f32[256,1024]{1,0:T(8,128)} %get-tuple-element.106.gt_ref, f32[256,1024]{1,0:T(8,128)} %get-tuple-element.107.up_ref, bf16[2,768,1024]{2,1,0:T(8,128)(2,1)} %wg.11, bf16[2,768,1024]{2,1,0:T(8,128)(2,1)} %wu.11, ...), custom_call_target="tpu_custom_call" | custom-call | flops 8800000000 | tf_op jit(solution)/shard_map/pallas_call | solution.py:665
  263.1 15.7 %all_to_all.103 = bf16[4,64,1536]{2,1,0:T(8,128)(2,1)S(1)} all-to-all(bf16[4,64,1536]{2,1,0:T(8,128)(2,1)} %bitcast.76), channel_id=1, replica_groups=mesh['fsdp'=2,'context'=4,'tensor'=4] {'tensor'}, dimensions={0} | all-to-all | bytes 1572864 | tf_op jit(solution)/shard_map/all_to_all | solution.py:83
  287.2 17.3 %collective-permute-start.23 = (bf16[64,1536]{1,0:T(8,128)(2,1)S(1)}, bf16[64,1536]{1,0:T(8,128)(2,1)S(1)}, u32[]{:S(2)}, u32[]{:S(2)}) collective-permute-start(bf16[64,1536]{1,0:T(8,128)(2,1)S(1)} %fusion.5), channel_id=1, source_target_pairs={{0,8},{4,12},{8,0},{12,4},{1,9},{5,13},{9,1},{13,5},{2,10},{6,14},... | collective-permute-start | bytes 589832 | tf_op jit(solution)/shard_map/ppermute | solution.py:25
  311.0 10.1 %collective-permute-done.23.refs_1_.refs_3_ = bf16[64,1536]{1,0:T(8,128)(2,1)S(1)} collective-permute-done((bf16[64,1536]{1,0:T(8,128)(2,1)S(1)}, bf16[64,1536]{1,0:T(8,128)(2,1)S(1)}, u32[]{:S(2)}, u32[]{:S(2)}) %collective-permute-start.23) | collective-permute-done | bytes 196640 | tf_op jit(solution)/shard_map/ppermute | solution.py:25
  331.3 8.4 %all-to-all-done.10 = bf16[4,64,1536]{2,1,0:T(8,128)(2,1)S(1)} async-done(((bf16[4,64,1536]{2,1,0:T(8,128)(2,1)}), bf16[4,64,1536]{2,1,0:T(8,128)(2,1)S(1)}, u32[]{:S(2)}, u32[]{:S(2)}) %all-to-all-start.10) | async-done | bytes 786464 | tf_op jit(solution)/shard_map/all_to_all | solution.py:48
  347.0 33.5 %shard_map.268 = (bf16[1024,1536]{1,0:T(8,128)(2,1)}, bf16[1024,384]{1,0:T(8,128)(2,1)}, bf16[1024,384]{1,0:T(8,128)(2,1)}, bf16[1024,384]{1,0:T(8,128)(2,1)}, b...) custom-call(s32[2]{0:T(128)} %pad_add_fusion.refs_0_, ...), custom_call_target="tpu_custom_call" | custom-call | flops 36300001280 | tf_op jit(solution)/shard_map/pallas_call | solution.py:614
  380.6 22.5 %all_to_all.104 = bf16[4,64,1536]{2,1,0:T(8,128)(2,1)S(1)} all-to-all(bf16[4,64,1536]{2,1,0:T(8,128)(2,1)} %bitcast.72), channel_id=1, replica_groups=mesh['fsdp'=2,'context'=4,'tensor'=4] {'tensor'}, dimensions={0} | all-to-all | bytes 1572864 | tf_op jit(solution)/shard_map/all_to_all | solution.py:83
  409.1 8.5 %shard_map.271 = (bf16[768,384]{1,0:T(8,128)(2,1)}, bf16[768,384]{1,0:T(8,128)(2,1)}, bf16[768,384]{1,0:T(8,128)(2,1)}, bf16[768,384]{1,0:T(8,128)(2,1)}, bf16[7...) custom-call(bf16[1024,1536]{1,0:T(8,128)(2,1)} %get-tuple-element.118.refs_0_, ...), custom_call_target="tpu_custom_call" | custom-call | flops 7699999744 | tf_op jit(solution)/shard_map/pallas_call | solution.py:747
  420.3 9.4 %shard_map.272.refs_0_ = bf16[256,1536]{1,0:T(8,128)(2,1)} custom-call(bf16[256,1536]{1,0:T(8,128)(2,1)} %bitcast.68, f32[256,1024]{1,0:T(8,128)} %get-tuple-element.116.gt_ref, f32[256,1024]{1,0:T(8,128)} %get-tuple-element.117.up_ref, bf16[2,768,1024]{2,1,0:T(8,128)(2,1)} %wg.11, bf16[2,768,1024]{2,1,0:T(8,128)(2,1)} %wu.11, bf16[2,1024,768]{2,1,0:T(8,128)(2,1)} %wd.11, ...), custom_call_target="tpu_custom_call" | custom-call | flops 8800000000 | tf_op jit(solution)/shard_map/pallas_call | solution.py:665
  434.8 9.5 %shard_map.275 = (f32[2,768,384]{2,1,0:T(8,128)}, f32[2,768,384]{2,1,0:T(8,128)}, f32[2,768,384]{2,1,0:T(8,128)}, f32[2,768,384]{2,1,0:T(8,128)}, f32[768,128]{1,0:T(8,128)}, /*index=5*/f32[2,384,768]{2,1,0:T(8,128)}) custom-call(bf16[1024,1536]{1,0:T(8,128)(2,1)} %get-tuple-element.11, ...), custom_call_target="tpu_custom_call", output_to_operand_aliasing={{0}: (14, {}), {1}: (15, {}), {2}: (16, {}), {3}: (17, {}),... | custom-call | flops 7699999744 | tf_op jit(solution)/shard_map/pallas_call | solution.py:747
  447.5 18.8 %collective-permute-done.35.refs_0_ = bf16[64,1536]{1,0:T(8,128)(2,1)S(1)} collective-permute-done((bf16[64,1536]{1,0:T(8,128)(2,1)}, bf16[64,1536]{1,0:T(8,128)(2,1)S(1)}, u32[]{:S(2)}, u32[]{:S(2)}) %collective-permute-start.35) | collective-permute-done | bytes 196640 | tf_op jit(solution)/shard_map/ppermute | solution.py:25
  467.1 21.0 %shard_map.278 = (bf16[1024,1024]{1,0:T(8,128)(2,1)}, bf16[1024,1024]{1,0:T(8,128)(2,1)}, bf16[1024,1024]{1,0:T(8,128)(2,1)}, bf16[768,1024]{1,0:T(8,128)(2,1)},...) custom-call(bf16[1024,1536]{1,0:T(8,128)(2,1)} %all-gather.11.cloned.1.call-done.b_ref, ...), custom_call_target="tpu_custom_call" | custom-call | flops 26400000000 | tf_op jit(solution)/shard_map/pallas_call | solution.py:682
  497.0 8.3 %all-to-all-done.15 = bf16[4,64,1536]{2,1,0:T(8,128)(2,1)S(1)} async-done(((bf16[4,64,1536]{2,1,0:T(8,128)(2,1)}), bf16[4,64,1536]{2,1,0:T(8,128)(2,1)S(1)}, u32[]{:S(2)}, u32[]{:S(2)}) %all-to-all-start.15) | async-done | bytes 786464 | tf_op jit(solution)/shard_map/all_to_all | solution.py:48
  518.5 11.9 %shard_map.284 = (f32[2,768,1024]{2,1,0:T(8,128)}, f32[2,768,1024]{2,1,0:T(8,128)}, f32[2,1024,768]{2,1,0:T(8,128)}) custom-call(bf16[1024,1536]{1,0:T(8,128)(2,1)} %all-gather.11.cloned.1.call-done.b_ref, bf16[1024,1536]{1,0:T(8,128)(2,1)} %all-gather.5.cloned.1.call-done.refs_1_.g_ref, ...), custom_call_target="tpu_custom_call", output_to_operand_aliasing={{0}: (8, {}), {1}: (9, {}), {2}: (10, {})} | custom-call | flops 9900000256 | tf_op jit(solution)/shard_map/pallas_call | solution.py:707
  535.1 33.5 %shard_map.280 = (bf16[1024,1536]{1,0:T(8,128)(2,1)}, bf16[1024,384]{1,0:T(8,128)(2,1)}, bf16[1024,384]{1,0:T(8,128)(2,1)}, bf16[1024,384]{1,0:T(8,128)(2,1)}, b...) custom-call(s32[2]{0:T(128)} %pad_add_fusion.refs_0_, ...), custom_call_target="tpu_custom_call" | custom-call | flops 36300001280 | tf_op jit(solution)/shard_map/pallas_call | solution.py:614
  572.7 21.0 %shard_map.269 = (bf16[1024,1024]{1,0:T(8,128)(2,1)}, bf16[1024,1024]{1,0:T(8,128)(2,1)}, bf16[1024,1024]{1,0:T(8,128)(2,1)}, bf16[768,1024]{1,0:T(8,128)(2,1)},...) custom-call(bf16[1024,1536]{1,0:T(8,128)(2,1)} %all-gather.7.cloned.1.call-done.refs_1_.b_ref, ...), custom_call_target="tpu_custom_call" | custom-call | flops 26400000000 | tf_op jit(solution)/shard_map/pallas_call | solution.py:682
  604.8 8.6 %shard_map.282 = (bf16[768,384]{1,0:T(8,128)(2,1)}, bf16[768,384]{1,0:T(8,128)(2,1)}, bf16[768,384]{1,0:T(8,128)(2,1)}, bf16[768,384]{1,0:T(8,128)(2,1)}, bf16[7...) custom-call(bf16[1024,1536]{1,0:T(8,128)(2,1)} %get-tuple-element.146.refs_0_, ...), custom_call_target="tpu_custom_call" | custom-call | flops 7699999744 | tf_op jit(solution)/shard_map/pallas_call | solution.py:747
  625.9 6.7 %all-to-all-done.18 = bf16[4,64,1536]{2,1,0:T(8,128)(2,1)S(1)} async-done(((bf16[4,64,1536]{2,1,0:T(8,128)(2,1)}), bf16[4,64,1536]{2,1,0:T(8,128)(2,1)S(1)}, u32[]{:S(2)}, u32[]{:S(2)}) %all-to-all-start.18) | async-done | bytes 786464 | tf_op jit(solution)/shard_map/all_to_all | solution.py:48
  638.2 9.5 %shard_map.283 = (f32[2,768,384]{2,1,0:T(8,128)}, f32[2,768,384]{2,1,0:T(8,128)}, f32[2,768,384]{2,1,0:T(8,128)}, f32[2,768,384]{2,1,0:T(8,128)}, f32[768,128]{1,0:T(8,128)}, /*index=5*/f32[2,384,768]{2,1,0:T(8,128)}) custom-call(bf16[1024,1536]{1,0:T(8,128)(2,1)} %get-tuple-element.14, ...), custom_call_target="tpu_custom_call", output_to_operand_aliasing={{0}: (14, {}), {1}: (15, {}), {2}: (16, {}), {3}: (17, {}),... | custom-call | flops 7699999744 | tf_op jit(solution)/shard_map/pallas_call | solution.py:747
  649.5 11.8 %shard_map.285 = (f32[2,768,1024]{2,1,0:T(8,128)}, f32[2,768,1024]{2,1,0:T(8,128)}, f32[2,1024,768]{2,1,0:T(8,128)}) custom-call(bf16[1024,1536]{1,0:T(8,128)(2,1)} %all-gather.7.cloned.1.call-done.refs_1_.b_ref, bf16[1024,1536]{1,0:T(8,128)(2,1)} %all-gather.9.cloned.1.call-done.g_ref.refs_2_, ...), custom_call_target="tpu_custom_call", output_to_operand_aliasing={{0}: (8, {}), {1}: (9, {}), {2}: (10, {})} | custom-call | flops 9900000256 | tf_op jit(solution)/shard_map/pallas_call | solution.py:707
  (395 shorter events, 205.3 us)
Async XLA Ops:
  12.0 40.5 %collective-permute-start.1 = (bf16[256,1536]{1,0:T(8,128)(2,1)S(1)}, bf16[256,1536]{1,0:T(8,128)(2,1)}, u32[]{:S(2)}, u32[]{:S(2)}) collective-permute-start(bf16[256,1536]{1,0:T(8,128)(2,1)S(1)} %multiply_convert_fusion.refs_1_), channel_id=1, source_target_pairs={{0,4},{4,0},{8,12},{12,8},{1,5},{5,1},{9,13},{13,9},{2,6},{6,2},{1... | collective-permute-start | bytes 2359304 | tf_op jit(solution)/shard_map/ppermute | solution.py:25
  15.3 24.4 %collective-permute-start.2 = (bf16[64,1536]{1,0:T(8,128)(2,1)}, bf16[64,1536]{1,0:T(8,128)(2,1)S(1)}, u32[]{:S(2)}, u32[]{:S(2)}) collective-permute-start(bf16[64,1536]{1,0:T(8,128)(2,1)} %constant_dynamic-slice_fusion.1), channel_id=1, source_target_pairs={{0,8},{4,12},{8,0},{12,4},{1,9},{5,13},{9,1},{13,5},{2,10},{6,14},... | collective-permute-start | bytes 589832 | tf_op jit(solution)/shard_map/ppermute | solution.py:25
  18.5 21.2 %all-to-all-start = ((s32[4,1,256]{2,1,0:T(1,128)}), s32[4,1,256]{2,1,0:T(1,128)}, u32[]{:S(2)}, u32[]{:S(2)}) async-start(s32[4,1,256]{2,1,0:T(1,128)} %broadcast_in_dim.33), calls=%async_computation | async-start | bytes 8192 | tf_op jit(solution)/shard_map/all_to_all | solution.py:48
  22.3 21.1 %collective-permute-start.12 = (bf16[2,768,6]{1,0,2:T(2,128)(2,1)}, bf16[2,768,6]{1,0,2:T(2,128)(2,1)}, u32[]{:S(2)}, u32[]{:S(2)}) collective-permute-start(bf16[2,768,6]{1,0,2:T(2,128)(2,1)} %param.22), channel_id=1, source_target_pairs={{0,16},{16,0},{1,17},{17,1},{2,18},{18,2},{3,19},{19,3},{4,20},{20... | collective-permute-start | bytes 55304 | tf_op jit(solution)/shard_map/ppermute | solution.py:25
  22.9 21.1 %collective-permute-start.6 = (bf16[64,1536]{1,0:T(8,128)(2,1)}, bf16[64,1536]{1,0:T(8,128)(2,1)S(1)}, u32[]{:S(2)}, u32[]{:S(2)}) collective-permute-start(bf16[64,1536]{1,0:T(8,128)(2,1)} %constant_dynamic-slice_fusion.1), channel_id=1, source_target_pairs={{0,12},{4,8},{8,4},{12,0},{1,13},{5,9},{9,5},{13,1},{2,14},{6,10},... | collective-permute-start | bytes 589832 | tf_op jit(solution)/shard_map/ppermute | solution.py:25
  44.0 20.4 %collective-permute-start.10 = (bf16[2,768,384]{2,1,0:T(8,128)(2,1)}, bf16[2,768,384]{2,1,0:T(8,128)(2,1)}, u32[]{:S(2)}, u32[]{:S(2)}) collective-permute-start(bf16[2,768,384]{2,1,0:T(8,128)(2,1)} %refs_7_.1), channel_id=1, source_target_pairs={{0,16},{16,0},{1,17},{17,1},{2,18},{18,2},{3,19},{19,3},{4,20},{20... | collective-permute-start | bytes 3538952 | tf_op jit(solution)/shard_map/ppermute | solution.py:25
  64.4 57.7 %collective-permute-start.13 = (bf16[2,768,1024]{2,1,0:T(8,128)(2,1)}, bf16[2,768,1024]{2,1,0:T(8,128)(2,1)}, u32[]{:S(2)}, u32[]{:S(2)}) collective-permute-start(bf16[2,768,1024]{2,1,0:T(8,128)(2,1)} %wg.11), channel_id=1, source_target_pairs={{0,16},{16,0},{1,17},{17,1},{2,18},{18,2},{3,19},{19,3},{4,20},{20... | collective-permute-start | bytes 9437192 | tf_op jit(solution)/shard_map/ppermute | solution.py:25
  64.8 57.3 %collective-permute-start.14 = (bf16[2,768,1024]{2,1,0:T(8,128)(2,1)}, bf16[2,768,1024]{2,1,0:T(8,128)(2,1)}, u32[]{:S(2)}, u32[]{:S(2)}) collective-permute-start(bf16[2,768,1024]{2,1,0:T(8,128)(2,1)} %wu.11), channel_id=1, source_target_pairs={{0,16},{16,0},{1,17},{17,1},{2,18},{18,2},{3,19},{19,3},{4,20},{20... | collective-permute-start | bytes 9437192 | tf_op jit(solution)/shard_map/ppermute | solution.py:25
  64.9 57.2 %collective-permute-start.15 = (bf16[2,1024,768]{2,1,0:T(8,128)(2,1)}, bf16[2,1024,768]{2,1,0:T(8,128)(2,1)}, u32[]{:S(2)}, u32[]{:S(2)}) collective-permute-start(bf16[2,1024,768]{2,1,0:T(8,128)(2,1)} %wd.11), channel_id=1, source_target_pairs={{0,16},{16,0},{1,17},{17,1},{2,18},{18,2},{3,19},{19,3},{4,20},{20... | collective-permute-start | bytes 9437192 | tf_op jit(solution)/shard_map/ppermute | solution.py:25
  95.0 92.4 %all-gather.5.cloned.1.call-start = ((), (), s32[]{:S(2)}) async-start(), calls=%async_computation.20 | async-start | bytes 3342336 | tf_op jit(solution)/shard_map/all_gather | solution.py:52
  146.6 22.5 %all-to-all-start.5 = ((bf16[4,64,1536]{2,1,0:T(8,128)(2,1)}), bf16[4,64,1536]{2,1,0:T(8,128)(2,1)S(1)}, u32[]{:S(2)}, u32[]{:S(2)}) async-start(bf16[4,64,1536]{2,1,0:T(8,128)(2,1)} %broadcast_in_dim.37), calls=%async_computation.5 | async-start | bytes 1572864 | tf_op jit(solution)/shard_map/all_to_all | solution.py:48
  150.1 25.4 %collective-permute-start.17 = (bf16[64,1536]{1,0:T(8,128)(2,1)S(1)}, bf16[64,1536]{1,0:T(8,128)(2,1)S(1)}, u32[]{:S(2)}, u32[]{:S(2)}) collective-permute-start(bf16[64,1536]{1,0:T(8,128)(2,1)S(1)} %multiply_convert_fusion.2), channel_id=1, source_target_pairs={{0,8},{4,12},{8,0},{12,4},{1,9},{5,13},{9,1},{13,5},{2,10},{6,14},... | collective-permute-start | bytes 589832 | tf_op jit(solution)/shard_map/ppermute | solution.py:25
  152.3 23.3 %collective-permute-start.21 = (bf16[64,1536]{1,0:T(8,128)(2,1)S(1)}, bf16[64,1536]{1,0:T(8,128)(2,1)S(1)}, u32[]{:S(2)}, u32[]{:S(2)}) collective-permute-start(bf16[64,1536]{1,0:T(8,128)(2,1)S(1)} %multiply_convert_fusion.2), channel_id=1, source_target_pairs={{0,12},{4,8},{8,4},{12,0},{1,13},{5,9},{9,5},{13,1},{2,14},{6,10},... | collective-permute-start | bytes 589832 | tf_op jit(solution)/shard_map/ppermute | solution.py:25
  169.1 32.4 %collective-permute-start.16 = (bf16[256,1536]{1,0:T(8,128)(2,1)S(1)}, bf16[256,1536]{1,0:T(8,128)(2,1)}, u32[]{:S(2)}, u32[]{:S(2)}) collective-permute-start(bf16[256,1536]{1,0:T(8,128)(2,1)S(1)} %bitcast.66), channel_id=1, source_target_pairs={{0,4},{4,0},{8,12},{12,8},{1,5},{5,1},{9,13},{13,9},{2,6},{6,2},{1... | collective-permute-start | bytes 2359304 | tf_op jit(solution)/shard_map/ppermute | solution.py:25
  178.8 22.7 %all-to-all-start.6 = ((bf16[4,64,1536]{2,1,0:T(8,128)(2,1)}), bf16[4,64,1536]{2,1,0:T(8,128)(2,1)S(1)}, u32[]{:S(2)}, u32[]{:S(2)}) async-start(bf16[4,64,1536]{2,1,0:T(8,128)(2,1)} %broadcast_in_dim.38), calls=%async_computation.6 | async-start | bytes 1572864 | tf_op jit(solution)/shard_map/all_to_all | solution.py:48
  225.2 115.4 %all-gather.7.cloned.1.call-start = ((), (), s32[]{:S(2)}) async-start(), calls=%async_computation.22 | async-start | bytes 3342336 | tf_op jit(solution)/shard_map/all_gather | solution.py:52
  281.1 23.4 %all-to-all-start.11 = ((bf16[4,64,1536]{2,1,0:T(8,128)(2,1)}), bf16[4,64,1536]{2,1,0:T(8,128)(2,1)}, u32[]{:S(2)}, u32[]{:S(2)}) async-start(bf16[4,64,1536]{2,1,0:T(8,128)(2,1)} %broadcast_in_dim.41), calls=%async_computation.11 | async-start | bytes 1572864 | tf_op jit(solution)/shard_map/all_to_all | solution.py:48
  285.3 25.7 %collective-permute-start.22 = (bf16[64,1536]{1,0:T(8,128)(2,1)S(1)}, bf16[64,1536]{1,0:T(8,128)(2,1)S(1)}, u32[]{:S(2)}, u32[]{:S(2)}) collective-permute-start(bf16[64,1536]{1,0:T(8,128)(2,1)S(1)} %fusion.5), channel_id=1, source_target_pairs={{0,12},{4,8},{8,4},{12,0},{1,13},{5,9},{9,5},{13,1},{2,14},{6,10},... | collective-permute-start | bytes 589832 | tf_op jit(solution)/shard_map/ppermute | solution.py:25
  287.2 33.9 %collective-permute-start.23 = (bf16[64,1536]{1,0:T(8,128)(2,1)S(1)}, bf16[64,1536]{1,0:T(8,128)(2,1)S(1)}, u32[]{:S(2)}, u32[]{:S(2)}) collective-permute-start(bf16[64,1536]{1,0:T(8,128)(2,1)S(1)} %fusion.5), channel_id=1, source_target_pairs={{0,8},{4,12},{8,0},{12,4},{1,9},{5,13},{9,1},{13,5},{2,10},{6,14},... | collective-permute-start | bytes 589832 | tf_op jit(solution)/shard_map/ppermute | solution.py:25
  304.5 42.5 %collective-permute-start.24 = (bf16[256,1536]{1,0:T(8,128)(2,1)}, bf16[256,1536]{1,0:T(8,128)(2,1)}, u32[]{:S(2)}, u32[]{:S(2)}) collective-permute-start(bf16[256,1536]{1,0:T(8,128)(2,1)} %bitcast.19.refs_1_), channel_id=1, source_target_pairs={{0,4},{4,0},{8,12},{12,8},{1,5},{5,1},{9,13},{13,9},{2,6},{6,2},{1... | collective-permute-start | bytes 2359304 | tf_op jit(solution)/shard_map/ppermute | solution.py:25
  327.4 138.9 %all-gather.11.cloned.1.call-start = ((), (), s32[]{:S(2)}) async-start(), calls=%async_computation.24 | async-start | bytes 3342336 | tf_op jit(solution)/shard_map/all_gather | solution.py:52
  408.7 121.7 %all-gather.9.cloned.1.call-start = ((), (), s32[]{:S(2)}) async-start(), calls=%async_computation.23 | async-start | bytes 3342336 | tf_op jit(solution)/shard_map/all_gather | solution.py:52
  488.1 30.4 %collective-permute-start.49 = (bf16[768,1024]{1,0:T(8,128)(2,1)}, bf16[768,1024]{1,0:T(8,128)(2,1)}, u32[]{:S(2)}, u32[]{:S(2)}) collective-permute-start(bf16[768,1024]{1,0:T(8,128)(2,1)} %get-tuple-element.178), channel_id=1, source_target_pairs={{0,16},{16,0},{1,17},{17,1},{2,18},{18,2},{3,19},{19,3},{4,20},{20... | collective-permute-start | bytes 4718600 | tf_op jit(solution)/shard_map/ppermute | solution.py:25
  488.2 30.3 %collective-permute-start.50 = (bf16[768,1024]{1,0:T(8,128)(2,1)}, bf16[768,1024]{1,0:T(8,128)(2,1)}, u32[]{:S(2)}, u32[]{:S(2)}) collective-permute-start(bf16[768,1024]{1,0:T(8,128)(2,1)} %get-tuple-element.179), channel_id=1, source_target_pairs={{0,16},{16,0},{1,17},{17,1},{2,18},{18,2},{3,19},{19,3},{4,20},{20... | collective-permute-start | bytes 4718600 | tf_op jit(solution)/shard_map/ppermute | solution.py:25
  488.7 29.8 %collective-permute-start.51 = (bf16[1024,768]{1,0:T(8,128)(2,1)}, bf16[1024,768]{1,0:T(8,128)(2,1)}, u32[]{:S(2)}, u32[]{:S(2)}) collective-permute-start(bf16[1024,768]{1,0:T(8,128)(2,1)} %get-tuple-element.180), channel_id=1, source_target_pairs={{0,16},{16,0},{1,17},{17,1},{2,18},{18,2},{3,19},{19,3},{4,20},{20... | collective-permute-start | bytes 4718600 | tf_op jit(solution)/shard_map/ppermute | solution.py:25
  493.7 100.9 %all-reduce.4.cloned.1.call-start = ((), (), s32[]{:S(2)}) async-start(), calls=%async_computation.21 | async-start | bytes 1572864 | tf_op jit(solution)/shard_map/psum | solution.py:932
  506.8 23.6 %all-to-all-start.16 = ((bf16[4,128,1536]{2,1,0:T(8,128)(2,1)}), bf16[4,128,1536]{2,1,0:T(8,128)(2,1)S(1)}, u32[]{:S(2)}, u32[]{:S(2)}) async-start(bf16[4,128,1536]{2,1,0:T(8,128)(2,1)} %broadcast_in_dim.44), calls=%async_computation.16 | async-start | bytes 3145728 | tf_op jit(solution)/shard_map/all_to_all | solution.py:48
  512.6 22.5 %collective-permute-start.34 = (bf16[256,1536]{1,0:T(8,128)(2,1)S(1)}, bf16[256,1536]{1,0:T(8,128)(2,1)}, u32[]{:S(2)}, u32[]{:S(2)}) collective-permute-start(bf16[256,1536]{1,0:T(8,128)(2,1)S(1)} %bitcast.64), channel_id=1, source_target_pairs={{0,4},{4,0},{8,12},{12,8},{1,5},{5,1},{9,13},{13,9},{2,6},{6,2},{1... | collective-permute-start | bytes 2359304 | tf_op jit(solution)/shard_map/ppermute | solution.py:25
  568.6 26.1 %all-to-all-start.17 = ((bf16[4,64,1536]{2,1,0:T(8,128)(2,1)}), bf16[4,64,1536]{2,1,0:T(8,128)(2,1)S(1)}, u32[]{:S(2)}, u32[]{:S(2)}) async-start(bf16[4,64,1536]{2,1,0:T(8,128)(2,1)} %bitcast.69), calls=%async_computation.17 | async-start | bytes 1572864 | tf_op jit(solution)/shard_map/all_to_all | solution.py:83
  593.8 43.0 %collective-permute-start.44 = (bf16[768,1024]{1,0:T(8,128)(2,1)}, bf16[768,1024]{1,0:T(8,128)(2,1)}, u32[]{:S(2)}, u32[]{:S(2)}) collective-permute-start(bf16[768,1024]{1,0:T(8,128)(2,1)} %get-tuple-element.164), channel_id=1, source_target_pairs={{0,16},{16,0},{1,17},{17,1},{2,18},{18,2},{3,19},{19,3},{4,20},{20... | collective-permute-start | bytes 4718600 | tf_op jit(solution)/shard_map/ppermute | solution.py:25
  593.9 42.9 %collective-permute-start.45 = (bf16[768,1024]{1,0:T(8,128)(2,1)}, bf16[768,1024]{1,0:T(8,128)(2,1)}, u32[]{:S(2)}, u32[]{:S(2)}) collective-permute-start(bf16[768,1024]{1,0:T(8,128)(2,1)} %get-tuple-element.165), channel_id=1, source_target_pairs={{0,16},{16,0},{1,17},{17,1},{2,18},{18,2},{3,19},{19,3},{4,20},{20... | collective-permute-start | bytes 4718600 | tf_op jit(solution)/shard_map/ppermute | solution.py:25
  614.8 21.9 %collective-permute-start.46 = (bf16[1024,768]{1,0:T(8,128)(2,1)}, bf16[1024,768]{1,0:T(8,128)(2,1)S(1)}, u32[]{:S(2)}, u32[]{:S(2)}) collective-permute-start(bf16[1024,768]{1,0:T(8,128)(2,1)} %get-tuple-element.166), channel_id=1, source_target_pairs={{0,16},{16,0},{1,17},{17,1},{2,18},{18,2},{3,19},{19,3},{4,20},{20... | collective-permute-start | bytes 4718600 | tf_op jit(solution)/shard_map/ppermute | solution.py:25
  (116 other events, 1211.0 us)
Sparse Core Ops, SparseCore 0:
  99.2 84.7 all-gather.4
  228.8 89.6 all-gather.6
  340.7 75.0 all-gather.10
  418.8 79.1 all-gather.8
  501.5 58.6 all-reduce.3

commit v11 on v10

--- a/solution.py
+++ b/solution.py
@@ -69,13 +69,14 @@
     near = near_rows(own)
     if together:
         block, width = shard.shape
-        far = gathered(jnp.concatenate([second, third], axis=0), "tensor")
+        far = gathered(after(jnp.concatenate([second, third], axis=0), own), "tensor")
         return (own, near, far.reshape(-1, 2, block, width)), (second, third)
     if token is not None:
         second = after(second, token)
-    third = after(third, second)
-    blocks = [second] + [swap(second, "tensor", k) for k in range(1, lax.axis_size("tensor"))]
-    return (own, near, *blocks, gathered(third, "tensor")), (second, third)
+    parts = [own, near]
+    for far in (second, third):
+        parts += [far] + [swap(far, "tensor", k) for k in range(1, lax.axis_size("tensor"))]
+    return tuple(parts), (second, third)
 
 
 def received_sum(sends):
@@ -830,16 +831,16 @@
         if layer > 0:
             a_parts, _ = all_rows((hidden * inverse_one * gain_one).astype(bf16))
         forget_weights = w_forget_full[layer]
-        if shared_rows and layer == 1:
-            forget_weights = after(forget_weights, g_last)
+        if shared_rows and layer > 0:
+            b_sent = after(saved[-1]["b_shard"], a_parts[-1])
+            saved[-1]["b_rows"] = sequence_rows(b_sent)
+            forget_weights = after(forget_weights, *([g_last] if layer == 1 else []), b_sent)
         a, (q, k, v, gate, forget, terms), sends = forward_own(
             place, a_parts, layer, w4, t4, w_attn_out, to, forget_weights,
             bias[layer : layer + 1], doc_start, piece_len,
         )
         if shared_rows and layer == 0:
             g_last = sequence_rows(after(own_block(cotangent_rows), a_parts[-1]))
-        if shared_rows and layer > 0:
-            saved[-1]["b_rows"] = sequence_rows(after(saved[-1]["b_shard"], a_parts[-1]))
         mixed = hidden + received_sum(sends)
         inverse_two = inverse_rms(mixed)
         b_shard = (mixed * inverse_two * gain_two).astype(bf16)
@@ -913,14 +914,14 @@
         if layer < last:
             attention_mine_of(layer + 1)
             y_shard = after(y_shard, results[0])
+        elif shared_rows:
+            y_shard = after(y_shard, *[x["b_rows"] for x in saved[:-1]])
         y_parts, y_far = all_rows(y_shard, together=layer < last)
         tokens = ()
         if layer < last:
             above = saved[layer + 1]
-            ffn_theirs_of(layer + 1, *y_far)
-            tokens = (above["values"][0], s["g_rows"])
-        elif shared_rows:
-            tokens = [x["b_rows"] for x in saved[:-1]]
+            ffn_theirs_of(layer + 1, *y_far, y_parts[0])
+            tokens = (above["values"][0], *([s["g_rows"]] if shared_rows else []))
         kept = (*s["kept"][:-1], after(s["kept"][-1], *tokens))
         y, (dq, dk, dv, dg, u, dz), sends = attention_backward(
             place, y_parts, layer, w4, t4, w_attn_out, to, w_forget_full[layer], kept, doc_start, piece_len,
@@ -938,10 +939,9 @@
         back, gain_grads[layer] = norm_back(received_sum(sends), s["hidden"], s["inverse_one"], gain_one)
         grad = grad_mixed + back
 
+    ffn_theirs_of(0)
     for layer in reversed(range(1, layers)):
-        ffn_mine_of(layer)
-    ffn_theirs_of(0)
-    grad = after(grad, saved[0]["values"][0])
+        ffn_mine_of(layer, grad)
     attention_theirs_of(0, grad)
     gain_total = jnp.stack(gain_grads).reshape(1, -1)
     for axis in (("context", "tensor"),) if shared_rows else ("context", "tensor"):

time: 678 us -> 673 us (level)
  blocking collectives: 79.2 us -> 108 us
  waiting for transfers between devices: 147 us -> 121 us
  starting transfers between devices: 124 us -> 117 us
    all_to_all x11 -> x7, waiting for transfers between devices: 59.1 us -> 21 us  [gathered(): lax.all_to_all(copies, axis, 0, 0, tiled=True)]
    all_to_all x2 -> x3, blocking collectives: 26.8 us -> 52.7 us  [gathered(): lax.all_to_all(copies, axis, 0, 0, tiled=True)]
    ppermute x52 -> x61, waiting for transfers between devices: 68.8 us -> 85.3 us  [swap(): return lax.ppermute(x, axis, [(i, i ^ k) for i in range(n)])]
    all_to_all x11 -> x7, starting transfers between devices: 44 us -> 28.4 us  [gathered(): lax.all_to_all(copies, axis, 0, 0, tiled=True)]
    ppermute x52 -> x61, starting transfers between devices: 63.5 us -> 77.2 us  [swap(): return lax.ppermute(x, axis, [(i, i ^ k) for i in range(n)])]
    all_to_all x4 -> x3, starting transfers between devices: 15.2 us -> 11.5 us  [received_sum(): lax.all_to_all(sends.reshape(count, -1, sends.shape[1]), 'tensor', 0, 0,...]
    all_to_all x4 -> x3, waiting for transfers between devices: 18.3 us -> 14.8 us  [received_sum(): lax.all_to_all(sends.reshape(count, -1, sends.shape[1]), 'tensor', 0, 0,...]
    unnamed x153 -> x159, local copies, waits for them, and re-layouts: 15.7 us -> 12.3 us
  transfers between devices with their start and end apart: 72 -> 76, of which waited for: 23 -> 25; matrix products, arithmetic and copies ran while one was open for 6% -> 6% of each run, Pallas kernels for 30% -> 33%
where the time goes in v11:
time: 673 us; the launch traced here: 664 us
  Pallas kernels  243 us (36%)
  waiting for transfers between devices  121 us (18%)
  starting transfers between devices  117 us (17%)
  blocking collectives  108 us (16%)
  local copies, waits for them, and re-layouts  36.5 us (5%)
  other arithmetic  22.6 us (3%)
  between operations  15.2 us (2%)
    ppermute x61, waiting for transfers between devices, swap(): return lax.ppermute(x, axis, [(i, i ^ k) for i in range(n)])  85.3 us
    ppermute x61, starting transfers between devices, swap(): return lax.ppermute(x, axis, [(i, i ^ k) for i in range(n)])  77.2 us
    pallas_call x2, Pallas kernels, attention_backward(): pl.pallas_call(functools.partial(backward_kernel, len(parts), piece_len,...  67.2 us
    all_to_all x4, blocking collectives, received_sum(): lax.all_to_all(sends.reshape(count, -1, sends.shape[1]), 'tensor', 0, 0,...  55.1 us
    all_to_all x3, blocking collectives, gathered(): lax.all_to_all(copies, axis, 0, 0, tiled=True)  52.7 us
    pallas_call x2, Pallas kernels, ffn_theirs(): pl.pallas_call(ffn_theirs_kernel, grid=(inner // hidden_block,), in_specs...  42.2 us
    pallas_call x2, Pallas kernels, forward_own(): pl.pallas_call(functools.partial(forward_own_kernel, len(parts), piece_le...  38.6 us
    pallas_call x4, Pallas kernels, attention_grads(): pl.pallas_call(functools.partial(attention_grads_kernel, steps, mine), gr...  36 us
  transfers between devices with their start and end apart: 76, of which 25 were waited for; matrix products, arithmetic and copies ran while one was open for 6% of the time, Pallas kernels for 33%

profile of v11, /device:TPU:0, one launch (start us, length us, event | category | flops | bytes accessed | tf_op | source)
XLA Modules:
  0.0 664.1 jit_solution(14195432863853579577)
XLA Ops:
  25.6 13.5 %all-to-all-done = s32[4,1,256]{2,1,0:T(1,128)} async-done(((s32[4,1,256]{2,1,0:T(1,128)}), s32[4,1,256]{2,1,0:T(1,128)}, u32[]{:S(2)}, u32[]{:S(2)}) %all-to-all-start) | async-done | bytes 4128 | tf_op jit(solution)/shard_map/all_to_all | solution.py:48
  66.7 19.2 %shard_map.255 = (bf16[1024,1536]{1,0:T(8,128)(2,1)}, bf16[1024,384]{1,0:T(8,128)(2,1)}, bf16[1024,384]{1,0:T(8,128)(2,1)}, bf16[1024,384]{1,0:T(8,128)(2,1)}, f...) custom-call(s32[2]{0:T(128)} %pad_add_fusion.refs_0_, ...), custom_call_target="tpu_custom_call" | custom-call | flops 20899999744 | tf_op jit(solution)/shard_map/pallas_call | solution.py:585
  90.3 10.8 %all-to-all-done.1 = bf16[4,64,1536]{2,1,0:T(8,128)(2,1)S(1)} async-done(((bf16[4,64,1536]{2,1,0:T(8,128)(2,1)}), bf16[4,64,1536]{2,1,0:T(8,128)(2,1)S(1)}, u32[]{:S(2)}, u32[]{:S(2)}) %all-to-all-start.1) | async-done | bytes 786464 | tf_op jit(solution)/shard_map/all_to_all | solution.py:84
  102.2 16.0 %all_to_all.85 = bf16[4,64,1536]{2,1,0:T(8,128)(2,1)} all-to-all(bf16[4,64,1536]{2,1,0:T(8,128)(2,1)S(1)} %broadcast_in_dim.29), channel_id=1, replica_groups=mesh['fsdp'=2,'context'=4,'tensor'=4] {'tensor'}, dimensions={0} | all-to-all | bytes 1572864 | tf_op jit(solution)/shard_map/all_to_all | solution.py:48
  118.1 8.5 %shard_map.256 = (f32[256,1024]{1,0:T(8,128)}, f32[256,1024]{1,0:T(8,128)}, bf16[256,1536]{1,0:T(8,128)(2,1)}) custom-call(bf16[256,1536]{1,0:T(8,128)(2,1)} %bitcast.67, bf16[2,768,1024]{2,1,0:T(8,128)(2,1)} %wg.11, bf16[2,768,1024]{2,1,0:T(8,128)(2,1)} %wu.11, bf16[2,1024,768]{2,1,0:T(8,128)(2,1)} %wd.11, ...), custom_call_target="tpu_custom_call" | custom-call | flops 7699999744 | tf_op jit(solution)/shard_map/pallas_call | solution.py:652
  126.6 14.2 %all_to_all.86 = bf16[4,64,1536]{2,1,0:T(8,128)(2,1)S(1)} all-to-all(bf16[4,64,1536]{2,1,0:T(8,128)(2,1)} %bitcast.68), channel_id=1, replica_groups=mesh['fsdp'=2,'context'=4,'tensor'=4] {'tensor'}, dimensions={0} | all-to-all | bytes 1572864 | tf_op jit(solution)/shard_map/all_to_all | solution.py:84
  141.7 21.5 %all_to_all.87 = bf16[4,64,1536]{2,1,0:T(8,128)(2,1)S(1)} all-to-all(bf16[4,64,1536]{2,1,0:T(8,128)(2,1)S(1)} %broadcast_in_dim.30), channel_id=1, replica_groups=mesh['fsdp'=2,'context'=4,'tensor'=4] {'tensor'}, dimensions={0} | all-to-all | bytes 1572864 | tf_op jit(solution)/shard_map/all_to_all | solution.py:48
  168.0 27.6 %collective-permute-done.24.refs_7_ = bf16[64,1536]{1,0:T(8,128)(2,1)S(1)} collective-permute-done((bf16[64,1536]{1,0:T(8,128)(2,1)S(1)}, bf16[64,1536]{1,0:T(8,128)(2,1)S(1)}, u32[]{:S(2)}, u32[]{:S(2)}) %collective-permute-start.24) | collective-permute-done | bytes 196640 | tf_op jit(solution)/shard_map/ppermute | solution.py:25
  213.4 19.4 %shard_map.260 = (bf16[1024,1536]{1,0:T(8,128)(2,1)}, bf16[1024,384]{1,0:T(8,128)(2,1)}, bf16[1024,384]{1,0:T(8,128)(2,1)}, bf16[1024,384]{1,0:T(8,128)(2,1)}, f...) custom-call(s32[2]{0:T(128)} %pad_add_fusion.refs_0_, ...), custom_call_target="tpu_custom_call" | custom-call | flops 20899999744 | tf_op jit(solution)/shard_map/pallas_call | solution.py:585
  232.8 16.2 %all_to_all.88 = bf16[4,64,1536]{2,1,0:T(8,128)(2,1)S(1)} all-to-all(bf16[4,64,1536]{2,1,0:T(8,128)(2,1)} %bitcast.66), channel_id=1, replica_groups=mesh['fsdp'=2,'context'=4,'tensor'=4] {'tensor'}, dimensions={0} | all-to-all | bytes 1572864 | tf_op jit(solution)/shard_map/all_to_all | solution.py:84
  249.5 15.2 %all_to_all.89 = bf16[4,64,1536]{2,1,0:T(8,128)(2,1)} all-to-all(bf16[4,64,1536]{2,1,0:T(8,128)(2,1)S(1)} %broadcast_in_dim.31), channel_id=1, replica_groups=mesh['fsdp'=2,'context'=4,'tensor'=4] {'tensor'}, dimensions={0} | all-to-all | bytes 1572864 | tf_op jit(solution)/shard_map/all_to_all | solution.py:48
  264.7 8.4 %shard_map.261 = (f32[256,1024]{1,0:T(8,128)}, f32[256,1024]{1,0:T(8,128)}, bf16[256,1536]{1,0:T(8,128)(2,1)}) custom-call(bf16[256,1536]{1,0:T(8,128)(2,1)} %bitcast.69, bf16[2,768,1024]{2,1,0:T(8,128)(2,1)} %wg.11, bf16[2,768,1024]{2,1,0:T(8,128)(2,1)} %wu.11, bf16[2,1024,768]{2,1,0:T(8,128)(2,1)} %wd.11, ...), custom_call_target="tpu_custom_call" | custom-call | flops 7699999744 | tf_op jit(solution)/shard_map/pallas_call | solution.py:652
  273.2 9.3 %shard_map.262 = bf16[256,1536]{1,0:T(8,128)(2,1)} custom-call(bf16[256,1536]{1,0:T(8,128)(2,1)} %copy-done.8, f32[256,1024]{1,0:T(8,128)} %get-tuple-element.106.gt_ref, f32[256,1024]{1,0:T(8,128)} %get-tuple-element.107.up_ref, bf16[2,768,1024]{2,1,0:T(8,128)(2,1)} %wg.11, bf16[2,768,1024]{2,1,0:T(8,128)(2,1)} %wu.11, bf16[2,1024,768]{2,1,0:T(8,128)(2,1)} %wd.11, ...), custom_call_target="tpu_custom_call" | custom-call | flops 8800000000 | tf_op jit(solution)/shard_map/pallas_call | solution.py:666
  282.5 12.1 %all_to_all.90 = bf16[4,64,1536]{2,1,0:T(8,128)(2,1)S(1)} all-to-all(bf16[4,64,1536]{2,1,0:T(8,128)(2,1)} %bitcast.70), channel_id=1, replica_groups=mesh['fsdp'=2,'context'=4,'tensor'=4] {'tensor'}, dimensions={0} | all-to-all | bytes 1572864 | tf_op jit(solution)/shard_map/all_to_all | solution.py:84
  302.3 9.0 %collective-permute-start.28 = (bf16[64,1536]{1,0:T(8,128)(2,1)S(1)}, bf16[64,1536]{1,0:T(8,128)(2,1)S(1)}, u32[]{:S(2)}, u32[]{:S(2)}) collective-permute-start(bf16[64,1536]{1,0:T(8,128)(2,1)S(1)} %copy-done.10), channel_id=1, source_target_pairs={{0,12},{4,8},{8,4},{12,0},{1,13},{5,9},{9,5},{13,1},{2,14},{6,10},... | collective-permute-start | bytes 589832 | tf_op jit(solution)/shard_map/ppermute | solution.py:25
  327.6 13.0 %collective-permute-done.31.refs_3_ = bf16[64,1536]{1,0:T(8,128)(2,1)S(1)} collective-permute-done((bf16[64,1536]{1,0:T(8,128)(2,1)S(1)}, bf16[64,1536]{1,0:T(8,128)(2,1)S(1)}, u32[]{:S(2)}, u32[]{:S(2)}) %collective-permute-start.31) | collective-permute-done | bytes 196640 | tf_op jit(solution)/shard_map/ppermute | solution.py:25
  354.2 33.6 %shard_map.265 = (bf16[1024,1536]{1,0:T(8,128)(2,1)}, bf16[1024,384]{1,0:T(8,128)(2,1)}, bf16[1024,384]{1,0:T(8,128)(2,1)}, bf16[1024,384]{1,0:T(8,128)(2,1)}, b...) custom-call(s32[2]{0:T(128)} %pad_add_fusion.refs_0_, ...), custom_call_target="tpu_custom_call" | custom-call | flops 36300001280 | tf_op jit(solution)/shard_map/pallas_call | solution.py:615
  387.8 12.5 %all_to_all.91 = bf16[4,64,1536]{2,1,0:T(8,128)(2,1)S(1)} all-to-all(bf16[4,64,1536]{2,1,0:T(8,128)(2,1)} %bitcast.65), channel_id=1, replica_groups=mesh['fsdp'=2,'context'=4,'tensor'=4] {'tensor'}, dimensions={0} | all-to-all | bytes 1572864 | tf_op jit(solution)/shard_map/all_to_all | solution.py:84
  402.8 8.5 %shard_map.268 = (bf16[768,384]{1,0:T(8,128)(2,1)}, bf16[768,384]{1,0:T(8,128)(2,1)}, bf16[768,384]{1,0:T(8,128)(2,1)}, bf16[768,384]{1,0:T(8,128)(2,1)}, bf16[7...) custom-call(bf16[1024,1536]{1,0:T(8,128)(2,1)} %get-tuple-element.118.refs_0_, ...), custom_call_target="tpu_custom_call" | custom-call | flops 7699999744 | tf_op jit(solution)/shard_map/pallas_call | solution.py:748
  419.9 7.5 %all-to-all-done.10 = bf16[4,64,1536]{2,1,0:T(8,128)(2,1)S(1)} async-done(((bf16[4,64,1536]{2,1,0:T(8,128)(2,1)}), bf16[4,64,1536]{2,1,0:T(8,128)(2,1)S(1)}, u32[]{:S(2)}, u32[]{:S(2)}) %all-to-all-start.10) | async-done | bytes 786464 | tf_op jit(solution)/shard_map/all_to_all | solution.py:48
  428.4 9.3 %shard_map.269.refs_0_ = bf16[256,1536]{1,0:T(8,128)(2,1)} custom-call(bf16[256,1536]{1,0:T(8,128)(2,1)} %bitcast.62, f32[256,1024]{1,0:T(8,128)} %get-tuple-element.116.gt_ref, f32[256,1024]{1,0:T(8,128)} %get-tuple-element.117.up_ref, bf16[2,768,1024]{2,1,0:T(8,128)(2,1)} %wg.11, bf16[2,768,1024]{2,1,0:T(8,128)(2,1)} %wu.11, bf16[2,1024,768]{2,1,0:T(8,128)(2,1)} %wd.11, ...), custom_call_target="tpu_custom_call" | custom-call | flops 8800000000 | tf_op jit(solution)/shard_map/pallas_call | solution.py:666
  442.3 9.5 %shard_map.272 = (f32[2,768,384]{2,1,0:T(8,128)}, f32[2,768,384]{2,1,0:T(8,128)}, f32[2,768,384]{2,1,0:T(8,128)}, f32[2,768,384]{2,1,0:T(8,128)}, f32[768,128]{1,0:T(8,128)}, /*index=5*/f32[2,384,768]{2,1,0:T(8,128)}) custom-call(bf16[1024,1536]{1,0:T(8,128)(2,1)} %get-tuple-element.11, ...), custom_call_target="tpu_custom_call", output_to_operand_aliasing={{0}: (14, {}), {1}: (15, {}), {2}: (16, {}), {3}: (17, {}),... | custom-call | flops 7699999744 | tf_op jit(solution)/shard_map/pallas_call | solution.py:748
  463.5 7.6 %collective-permute-start.44 = (bf16[64,1536]{1,0:T(8,128)(2,1)S(1)}, bf16[64,1536]{1,0:T(8,128)(2,1)S(1)}, u32[]{:S(2)}, u32[]{:S(2)}) collective-permute-start(bf16[64,1536]{1,0:T(8,128)(2,1)S(1)} %copy-done.12), channel_id=1, source_target_pairs={{0,8},{4,12},{8,0},{12,4},{1,9},{5,13},{9,1},{13,5},{2,10},{6,14},... | collective-permute-start | bytes 589832 | tf_op jit(solution)/shard_map/ppermute | solution.py:25
  471.1 6.4 collective-permute-start.45
  478.9 11.1 %collective-permute-done.44.refs_0_ = bf16[64,1536]{1,0:T(8,128)(2,1)S(1)} collective-permute-done((bf16[64,1536]{1,0:T(8,128)(2,1)S(1)}, bf16[64,1536]{1,0:T(8,128)(2,1)S(1)}, u32[]{:S(2)}, u32[]{:S(2)}) %collective-permute-start.44) | collective-permute-done | bytes 196640 | tf_op jit(solution)/shard_map/ppermute | solution.py:25
  500.4 21.2 %shard_map.276 = (bf16[1024,1024]{1,0:T(8,128)(2,1)}, bf16[1024,1024]{1,0:T(8,128)(2,1)}, bf16[1024,1024]{1,0:T(8,128)(2,1)}, bf16[768,1024]{1,0:T(8,128)(2,1)},...) custom-call(bf16[1024,1536]{1,0:T(8,128)(2,1)} %all-gather.11.cloned.1.call-done.b_ref, ...), custom_call_target="tpu_custom_call" | custom-call | flops 26400000000 | tf_op jit(solution)/shard_map/pallas_call | solution.py:683
  523.4 33.5 %shard_map.278 = (bf16[1024,1536]{1,0:T(8,128)(2,1)}, bf16[1024,384]{1,0:T(8,128)(2,1)}, bf16[1024,384]{1,0:T(8,128)(2,1)}, bf16[1024,384]{1,0:T(8,128)(2,1)}, b...) custom-call(s32[2]{0:T(128)} %pad_add_fusion.refs_0_, ...), custom_call_target="tpu_custom_call" | custom-call | flops 36300001280 | tf_op jit(solution)/shard_map/pallas_call | solution.py:615
  562.3 21.0 %shard_map.266 = (bf16[1024,1024]{1,0:T(8,128)(2,1)}, bf16[1024,1024]{1,0:T(8,128)(2,1)}, bf16[1024,1024]{1,0:T(8,128)(2,1)}, bf16[768,1024]{1,0:T(8,128)(2,1)},...) custom-call(bf16[1024,1536]{1,0:T(8,128)(2,1)} %all-gather.7.cloned.1.call-done.refs_1_.b_ref, ...), custom_call_target="tpu_custom_call" | custom-call | flops 26400000000 | tf_op jit(solution)/shard_map/pallas_call | solution.py:683
  596.1 8.6 %shard_map.279 = (bf16[768,384]{1,0:T(8,128)(2,1)}, bf16[768,384]{1,0:T(8,128)(2,1)}, bf16[768,384]{1,0:T(8,128)(2,1)}, bf16[768,384]{1,0:T(8,128)(2,1)}, bf16[7...) custom-call(bf16[1024,1536]{1,0:T(8,128)(2,1)} %get-tuple-element.146.refs_0_, ...), custom_call_target="tpu_custom_call" | custom-call | flops 7699999744 | tf_op jit(solution)/shard_map/pallas_call | solution.py:748
  614.8 11.9 %shard_map.281 = (f32[2,768,1024]{2,1,0:T(8,128)}, f32[2,768,1024]{2,1,0:T(8,128)}, f32[2,1024,768]{2,1,0:T(8,128)}) custom-call(bf16[1024,1536]{1,0:T(8,128)(2,1)} %all-gather.11.cloned.1.call-done.b_ref, bf16[1024,1536]{1,0:T(8,128)(2,1)} %all-gather.5.cloned.1.call-done.refs_1_.g_ref, ...), custom_call_target="tpu_custom_call", output_to_operand_aliasing={{0}: (8, {}), {1}: (9, {}), {2}: (10, {})} | custom-call | flops 9900000256 | tf_op jit(solution)/shard_map/pallas_call | solution.py:708
  634.0 9.5 %shard_map.280 = (f32[2,768,384]{2,1,0:T(8,128)}, f32[2,768,384]{2,1,0:T(8,128)}, f32[2,768,384]{2,1,0:T(8,128)}, f32[2,768,384]{2,1,0:T(8,128)}, f32[768,128]{1,0:T(8,128)}, /*index=5*/f32[2,384,768]{2,1,0:T(8,128)}) custom-call(bf16[1024,1536]{1,0:T(8,128)(2,1)} %get-tuple-element.14, ...), custom_call_target="tpu_custom_call", output_to_operand_aliasing={{0}: (14, {}), {1}: (15, {}), {2}: (16, {}), {3}: (17, {}),... | custom-call | flops 7699999744 | tf_op jit(solution)/shard_map/pallas_call | solution.py:748
  645.3 11.8 %shard_map.282 = (f32[2,768,1024]{2,1,0:T(8,128)}, f32[2,768,1024]{2,1,0:T(8,128)}, f32[2,1024,768]{2,1,0:T(8,128)}) custom-call(bf16[1024,1536]{1,0:T(8,128)(2,1)} %all-gather.7.cloned.1.call-done.refs_1_.b_ref, bf16[1024,1536]{1,0:T(8,128)(2,1)} %all-gather.9.cloned.1.call-done.g_ref.refs_2_, ...), custom_call_target="tpu_custom_call", output_to_operand_aliasing={{0}: (8, {}), {1}: (9, {}), {2}: (10, {})} | custom-call | flops 9900000256 | tf_op jit(solution)/shard_map/pallas_call | solution.py:708
  (404 shorter events, 191.3 us)
Async XLA Ops:
  11.4 49.5 %collective-permute-start.1 = (bf16[256,1536]{1,0:T(8,128)(2,1)S(1)}, bf16[256,1536]{1,0:T(8,128)(2,1)}, u32[]{:S(2)}, u32[]{:S(2)}) collective-permute-start(bf16[256,1536]{1,0:T(8,128)(2,1)S(1)} %multiply_convert_fusion.refs_1_), channel_id=1, source_target_pairs={{0,4},{4,0},{8,12},{12,8},{1,5},{5,1},{9,13},{13,9},{2,6},{6,2},{1... | collective-permute-start | bytes 2359304 | tf_op jit(solution)/shard_map/ppermute | solution.py:25
  14.1 25.0 %collective-permute-start.2 = (bf16[64,1536]{1,0:T(8,128)(2,1)S(1)}, bf16[64,1536]{1,0:T(8,128)(2,1)S(1)}, u32[]{:S(2)}, u32[]{:S(2)}) collective-permute-start(bf16[64,1536]{1,0:T(8,128)(2,1)S(1)} %constant_dynamic-slice_fusion.1), channel_id=1, source_target_pairs={{0,8},{4,12},{8,0},{12,4},{1,9},{5,13},{9,1},{13,5},{2,10},{6,14},... | collective-permute-start | bytes 589832 | tf_op jit(solution)/shard_map/ppermute | solution.py:25
  18.0 21.0 %all-to-all-start = ((s32[4,1,256]{2,1,0:T(1,128)}), s32[4,1,256]{2,1,0:T(1,128)}, u32[]{:S(2)}, u32[]{:S(2)}) async-start(s32[4,1,256]{2,1,0:T(1,128)} %broadcast_in_dim.27), calls=%async_computation | async-start | bytes 8192 | tf_op jit(solution)/shard_map/all_to_all | solution.py:48
  21.8 22.8 %collective-permute-start.6 = (bf16[64,1536]{1,0:T(8,128)(2,1)S(1)}, bf16[64,1536]{1,0:T(8,128)(2,1)}, u32[]{:S(2)}, u32[]{:S(2)}) collective-permute-start(bf16[64,1536]{1,0:T(8,128)(2,1)S(1)} %constant_dynamic-slice_fusion.1), channel_id=1, source_target_pairs={{0,12},{4,8},{8,4},{12,0},{1,13},{5,9},{9,5},{13,1},{2,14},{6,10},... | collective-permute-start | bytes 589832 | tf_op jit(solution)/shard_map/ppermute | solution.py:25
  66.1 52.0 %collective-permute-start.16 = (bf16[2,768,1024]{2,1,0:T(8,128)(2,1)}, bf16[2,768,1024]{2,1,0:T(8,128)(2,1)}, u32[]{:S(2)}, u32[]{:S(2)}) collective-permute-start(bf16[2,768,1024]{2,1,0:T(8,128)(2,1)} %wg.11), channel_id=1, source_target_pairs={{0,16},{16,0},{1,17},{17,1},{2,18},{18,2},{3,19},{19,3},{4,20},{20... | collective-permute-start | bytes 9437192 | tf_op jit(solution)/shard_map/ppermute | solution.py:25
  66.2 51.9 %collective-permute-start.17 = (bf16[2,768,1024]{2,1,0:T(8,128)(2,1)}, bf16[2,768,1024]{2,1,0:T(8,128)(2,1)}, u32[]{:S(2)}, u32[]{:S(2)}) collective-permute-start(bf16[2,768,1024]{2,1,0:T(8,128)(2,1)} %wu.11), channel_id=1, source_target_pairs={{0,16},{16,0},{1,17},{17,1},{2,18},{18,2},{3,19},{19,3},{4,20},{20... | collective-permute-start | bytes 9437192 | tf_op jit(solution)/shard_map/ppermute | solution.py:25
  66.7 51.5 %collective-permute-start.18 = (bf16[2,1024,768]{2,1,0:T(8,128)(2,1)}, bf16[2,1024,768]{2,1,0:T(8,128)(2,1)}, u32[]{:S(2)}, u32[]{:S(2)}) collective-permute-start(bf16[2,1024,768]{2,1,0:T(8,128)(2,1)} %wd.11), channel_id=1, source_target_pairs={{0,16},{16,0},{1,17},{17,1},{2,18},{18,2},{3,19},{19,3},{4,20},{20... | collective-permute-start | bytes 9437192 | tf_op jit(solution)/shard_map/ppermute | solution.py:25
  89.5 119.9 %all-gather.5.cloned.1.call-start = ((), (), s32[]{:S(2)}) async-start(), calls=%async_computation.17 | async-start | bytes 3342336 | tf_op jit(solution)/shard_map/all_gather | solution.py:52
  90.2 206.6 %all-gather.7.cloned.1.call-start = ((), (), s32[]{:S(2)}) async-start(), calls=%async_computation.18 | async-start | bytes 3342336 | tf_op jit(solution)/shard_map/all_gather | solution.py:52
  163.2 49.3 %collective-permute-start.19 = (bf16[256,1536]{1,0:T(8,128)(2,1)S(1)}, bf16[256,1536]{1,0:T(8,128)(2,1)S(1)}, u32[]{:S(2)}, u32[]{:S(2)}) collective-permute-start(bf16[256,1536]{1,0:T(8,128)(2,1)S(1)} %bitcast.60), channel_id=1, source_target_pairs={{0,4},{4,0},{8,12},{12,8},{1,5},{5,1},{9,13},{13,9},{2,6},{6,2},{1... | collective-permute-start | bytes 2359304 | tf_op jit(solution)/shard_map/ppermute | solution.py:25
  165.5 30.0 %collective-permute-start.24 = (bf16[64,1536]{1,0:T(8,128)(2,1)S(1)}, bf16[64,1536]{1,0:T(8,128)(2,1)S(1)}, u32[]{:S(2)}, u32[]{:S(2)}) collective-permute-start(bf16[64,1536]{1,0:T(8,128)(2,1)S(1)} %multiply_convert_fusion.2), channel_id=1, source_target_pairs={{0,12},{4,8},{8,4},{12,0},{1,13},{5,9},{9,5},{13,1},{2,14},{6,10},... | collective-permute-start | bytes 589832 | tf_op jit(solution)/shard_map/ppermute | solution.py:25
  168.0 28.9 %collective-permute-start.20 = (bf16[64,1536]{1,0:T(8,128)(2,1)S(1)}, bf16[64,1536]{1,0:T(8,128)(2,1)S(1)}, u32[]{:S(2)}, u32[]{:S(2)}) collective-permute-start(bf16[64,1536]{1,0:T(8,128)(2,1)S(1)} %multiply_convert_fusion.2), channel_id=1, source_target_pairs={{0,8},{4,12},{8,0},{12,4},{1,9},{5,13},{9,1},{13,5},{2,10},{6,14},... | collective-permute-start | bytes 589832 | tf_op jit(solution)/shard_map/ppermute | solution.py:25
  298.8 24.5 %all-to-all-start.8 = ((bf16[4,64,1536]{2,1,0:T(8,128)(2,1)}), bf16[4,64,1536]{2,1,0:T(8,128)(2,1)S(1)}, u32[]{:S(2)}, u32[]{:S(2)}) async-start(bf16[4,64,1536]{2,1,0:T(8,128)(2,1)} %broadcast_in_dim.32), calls=%async_computation.8 | async-start | bytes 1572864 | tf_op jit(solution)/shard_map/all_to_all | solution.py:48
  302.3 198.1 %all-gather.11.cloned.1.call-start = ((), (), s32[]{:S(2)}) async-start(), calls=%async_computation.21 | async-start | bytes 3342336 | tf_op jit(solution)/shard_map/all_gather | solution.py:52
  323.0 199.2 %all-gather.9.cloned.1.call-start = ((), (), s32[]{:S(2)}) async-start(), calls=%async_computation.20 | async-start | bytes 3342336 | tf_op jit(solution)/shard_map/all_gather | solution.py:52
  323.3 29.9 %collective-permute-start.30 = (bf16[256,1536]{1,0:T(8,128)(2,1)S(1)}, bf16[256,1536]{1,0:T(8,128)(2,1)S(1)}, u32[]{:S(2)}, u32[]{:S(2)}) collective-permute-start(bf16[256,1536]{1,0:T(8,128)(2,1)S(1)} %bitcast.58), channel_id=1, source_target_pairs={{0,4},{4,0},{8,12},{12,8},{1,5},{5,1},{9,13},{13,9},{2,6},{6,2},{1... | collective-permute-start | bytes 2359304 | tf_op jit(solution)/shard_map/ppermute | solution.py:25
  415.8 167.6 %all-reduce.4.cloned.1.call-start = ((), (), s32[]{:S(2)}) async-start(), calls=%async_computation.19 | async-start | bytes 1572864 | tf_op jit(solution)/shard_map/psum | solution.py:933
  437.7 24.7 %collective-permute-start.57 = (f32[6]{0:T(128)S(1)}, f32[6]{0:T(128)S(1)}, u32[]{:S(2)}, u32[]{:S(2)}) collective-permute-start(f32[6]{0:T(128)S(1)} %bitcast.73), channel_id=1, source_target_pairs={{0,16},{16,0},{1,17},{17,1},{2,18},{18,2},{3,19},{19,3},{4,20},{20... | collective-permute-start | bytes 80 | tf_op jit(solution)/shard_map/ppermute | solution.py:25
  458.9 31.9 %all-to-all-start.12 = ((bf16[4,64,1536]{2,1,0:T(8,128)(2,1)}), bf16[4,64,1536]{2,1,0:T(8,128)(2,1)S(1)}, u32[]{:S(2)}, u32[]{:S(2)}) async-start(bf16[4,64,1536]{2,1,0:T(8,128)(2,1)} %broadcast_in_dim.34), calls=%async_computation.12 | async-start | bytes 1572864 | tf_op jit(solution)/shard_map/all_to_all | solution.py:48
  463.5 26.5 %collective-permute-start.44 = (bf16[64,1536]{1,0:T(8,128)(2,1)S(1)}, bf16[64,1536]{1,0:T(8,128)(2,1)S(1)}, u32[]{:S(2)}, u32[]{:S(2)}) collective-permute-start(bf16[64,1536]{1,0:T(8,128)(2,1)S(1)} %copy-done.12), channel_id=1, source_target_pairs={{0,8},{4,12},{8,0},{12,4},{1,9},{5,13},{9,1},{13,5},{2,10},{6,14},... | collective-permute-start | bytes 589832 | tf_op jit(solution)/shard_map/ppermute | solution.py:25
  490.8 31.4 %collective-permute-start.43 = (bf16[256,1536]{1,0:T(8,128)(2,1)S(1)}, bf16[256,1536]{1,0:T(8,128)(2,1)}, u32[]{:S(2)}, u32[]{:S(2)}) collective-permute-start(bf16[256,1536]{1,0:T(8,128)(2,1)S(1)} %bitcast.52), channel_id=1, source_target_pairs={{0,4},{4,0},{8,12},{12,8},{1,5},{5,1},{9,13},{13,9},{2,6},{6,2},{1... | collective-permute-start | bytes 2359304 | tf_op jit(solution)/shard_map/ppermute | solution.py:25
  496.6 25.6 %all-to-all-start.13 = ((bf16[4,128,1536]{2,1,0:T(8,128)(2,1)}), bf16[4,128,1536]{2,1,0:T(8,128)(2,1)S(1)}, u32[]{:S(2)}, u32[]{:S(2)}) async-start(bf16[4,128,1536]{2,1,0:T(8,128)(2,1)} %broadcast_in_dim.35), calls=%async_computation.13 | async-start | bytes 3145728 | tf_op jit(solution)/shard_map/all_to_all | solution.py:48
  521.6 86.0 %collective-permute-start.58 = (bf16[768,1024]{1,0:T(8,128)(2,1)}, bf16[768,1024]{1,0:T(8,128)(2,1)}, u32[]{:S(2)}, u32[]{:S(2)}) collective-permute-start(bf16[768,1024]{1,0:T(8,128)(2,1)} %get-tuple-element.178), channel_id=1, source_target_pairs={{0,16},{16,0},{1,17},{17,1},{2,18},{18,2},{3,19},{19,3},{4,20},{20... | collective-permute-start | bytes 4718600 | tf_op jit(solution)/shard_map/ppermute | solution.py:25
  521.7 86.1 %collective-permute-start.59 = (bf16[768,1024]{1,0:T(8,128)(2,1)}, bf16[768,1024]{1,0:T(8,128)(2,1)}, u32[]{:S(2)}, u32[]{:S(2)}) collective-permute-start(bf16[768,1024]{1,0:T(8,128)(2,1)} %get-tuple-element.179), channel_id=1, source_target_pairs={{0,16},{16,0},{1,17},{17,1},{2,18},{18,2},{3,19},{19,3},{4,20},{20... | collective-permute-start | bytes 4718600 | tf_op jit(solution)/shard_map/ppermute | solution.py:25
  522.1 85.9 %collective-permute-start.60 = (bf16[1024,768]{1,0:T(8,128)(2,1)}, bf16[1024,768]{1,0:T(8,128)(2,1)}, u32[]{:S(2)}, u32[]{:S(2)}) collective-permute-start(bf16[1024,768]{1,0:T(8,128)(2,1)} %get-tuple-element.180), channel_id=1, source_target_pairs={{0,16},{16,0},{1,17},{17,1},{2,18},{18,2},{3,19},{19,3},{4,20},{20... | collective-permute-start | bytes 4718600 | tf_op jit(solution)/shard_map/ppermute | solution.py:25
  557.0 28.5 %all-to-all-start.14 = ((bf16[4,64,1536]{2,1,0:T(8,128)(2,1)}), bf16[4,64,1536]{2,1,0:T(8,128)(2,1)S(1)}, u32[]{:S(2)}, u32[]{:S(2)}) async-start(bf16[4,64,1536]{2,1,0:T(8,128)(2,1)} %bitcast.63), calls=%async_computation.14 | async-start | bytes 1572864 | tf_op jit(solution)/shard_map/all_to_all | solution.py:84
  562.2 43.8 %collective-permute-start.56 = (f32[6]{0:T(128)}, f32[6]{0:T(128)}, u32[]{:S(2)}, u32[]{:S(2)}) collective-permute-start(f32[6]{0:T(128)} %bitcast.47), channel_id=1, source_target_pairs={{0,16},{16,0},{1,17},{17,1},{2,18},{18,2},{3,19},{19,3},{4,20},{20... | collective-permute-start | bytes 80 | tf_op jit(solution)/shard_map/ppermute | solution.py:25
  588.2 21.4 %all-to-all-start.16 = ((f32[16,1,6144]{2,1,0:T(1,128)}), f32[16,1,6144]{2,1,0:T(1,128)S(1)}, u32[]{:S(2)}, u32[]{:S(2)}) async-start(f32[16,1,6144]{2,1,0:T(1,128)} %broadcast_in_dim.38), calls=%async_computation.16 | async-start | bytes 786432 | tf_op jit(solution)/shard_map/all_to_all | solution.py:48
  607.5 25.0 %collective-permute-start.53 = (bf16[768,1024]{1,0:T(8,128)(2,1)}, bf16[768,1024]{1,0:T(8,128)(2,1)S(1)}, u32[]{:S(2)}, u32[]{:S(2)}) collective-permute-start(bf16[768,1024]{1,0:T(8,128)(2,1)} %get-tuple-element.164), channel_id=1, source_target_pairs={{0,16},{16,0},{1,17},{17,1},{2,18},{18,2},{3,19},{19,3},{4,20},{20... | collective-permute-start | bytes 4718600 | tf_op jit(solution)/shard_map/ppermute | solution.py:25
  607.8 25.0 %collective-permute-start.54 = (bf16[768,1024]{1,0:T(8,128)(2,1)}, bf16[768,1024]{1,0:T(8,128)(2,1)}, u32[]{:S(2)}, u32[]{:S(2)}) collective-permute-start(bf16[768,1024]{1,0:T(8,128)(2,1)} %get-tuple-element.165), channel_id=1, source_target_pairs={{0,16},{16,0},{1,17},{17,1},{2,18},{18,2},{3,19},{19,3},{4,20},{20... | collective-permute-start | bytes 4718600 | tf_op jit(solution)/shard_map/ppermute | solution.py:25
  608.1 25.3 %collective-permute-start.55 = (bf16[1024,768]{1,0:T(8,128)(2,1)}, bf16[1024,768]{1,0:T(8,128)(2,1)}, u32[]{:S(2)}, u32[]{:S(2)}) collective-permute-start(bf16[1024,768]{1,0:T(8,128)(2,1)} %get-tuple-element.166), channel_id=1, source_target_pairs={{0,16},{16,0},{1,17},{17,1},{2,18},{18,2},{3,19},{19,3},{4,20},{20... | collective-permute-start | bytes 4718600 | tf_op jit(solution)/shard_map/ppermute | solution.py:25
  608.3 20.1 %collective-permute-start.47 = (bf16[768,384]{1,0:T(8,128)(2,1)}, bf16[768,384]{1,0:T(8,128)(2,1)S(1)}, u32[]{:S(2)}, u32[]{:S(2)}) collective-permute-start(bf16[768,384]{1,0:T(8,128)(2,1)} %get-tuple-element.155), channel_id=1, source_target_pairs={{0,16},{16,0},{1,17},{17,1},{2,18},{18,2},{3,19},{19,3},{4,20},{20... | collective-permute-start | bytes 1769480 | tf_op jit(solution)/shard_map/ppermute | solution.py:25
  (123 other events, 1304.9 us)
Sparse Core Ops, SparseCore 0:
  93.6 87.8 all-gather.4
  209.4 74.1 all-gather.6
  323.1 73.1 all-gather.10
  402.4 80.8 all-gather.8
  486.8 60.7 all-reduce.3

commit v12 on v11

--- a/solution.py
+++ b/solution.py
@@ -810,7 +810,7 @@
     gains = full(jnp.concatenate([gain_attn, gain_ffn], axis=0), 1).astype(f32)
     hidden_rows = features(hidden_in.reshape(piece_len, width)).astype(f32)
     first_a = (hidden_rows * inverse_rms(hidden_rows) * gains[0]).astype(bf16)
-    a_parts, _ = all_rows(own_block(first_a), first_a, seg_all)
+    a_parts, a_far = all_rows(own_block(first_a), first_a, seg_all)
 
     w_forget_full = jnp.pad(full(w_forget, 1), ((0, 0), (0, 0), (0, pair_lanes - heads)))
     bias = jnp.pad(b_forget, ((0, 0), (0, pair_lanes - heads)))
@@ -829,18 +829,21 @@
         gain_one, gain_two = gains[layer], gains[layers + layer]
         inverse_one = inverse_rms(hidden)
         if layer > 0:
-            a_parts, _ = all_rows((hidden * inverse_one * gain_one).astype(bf16))
+            a_shard = (hidden * inverse_one * gain_one).astype(bf16)
+            if shared_rows and layer == 1:
+                a_shard = after(a_shard, g_last)
+            a_parts, _ = all_rows(a_shard)
         forget_weights = w_forget_full[layer]
         if shared_rows and layer > 0:
             b_sent = after(saved[-1]["b_shard"], a_parts[-1])
             saved[-1]["b_rows"] = sequence_rows(b_sent)
-            forget_weights = after(forget_weights, *([g_last] if layer == 1 else []), b_sent)
+            forget_weights = after(forget_weights, b_sent)
         a, (q, k, v, gate, forget, terms), sends = forward_own(
             place, a_parts, layer, w4, t4, w_attn_out, to, forget_weights,
             bias[layer : layer + 1], doc_start, piece_len,
         )
         if shared_rows and layer == 0:
-            g_last = sequence_rows(after(own_block(cotangent_rows), a_parts[-1]))
+            g_last = lax.all_gather(after(cotangent_rows, *a_far), "context", tiled=True)
         mixed = hidden + received_sum(sends)
         inverse_two = inverse_rms(mixed)
         b_shard = (mixed * inverse_two * gain_two).astype(bf16)
@@ -901,8 +904,6 @@
             g_shard = grad.astype(bf16)
             g = gathered(g_shard, "tensor")
             tokens = (saved[layer + 1]["theirs"][0],)
-            if shared_rows:
-                s["g_rows"] = sequence_rows(g_shard)
         if not shared_rows:
             s.update(b_rows=s["b"], g_rows=g)
         sends = ffn_backward(g, s["gt"], s["up"], layer, w3, t3, *tokens)
@@ -921,34 +922,35 @@
         if layer < last:
             above = saved[layer + 1]
             ffn_theirs_of(layer + 1, *y_far, y_parts[0])
-            tokens = (above["values"][0], *([s["g_rows"]] if shared_rows else []))
+            tokens = (above["values"][0],)
         kept = (*s["kept"][:-1], after(s["kept"][-1], *tokens))
         y, (dq, dk, dv, dg, u, dz), sends = attention_backward(
             place, y_parts, layer, w4, t4, w_attn_out, to, w_forget_full[layer], kept, doc_start, piece_len,
         )
         token = y_parts[-1]
-        if layer == last:
-            block_sum = own_block(last_sends).astype(f32) + s["mixed"]
-            with_rows = lax.dynamic_update_slice_in_dim(last_sends, block_sum.astype(bf16), t * block, 0)
-            output = lax.psum(after(with_rows, token), "tensor")
         if shared_rows and layer == last:
-            s.update(b_rows=sequence_rows(after(s["b_shard"], token)), g_rows=g_last)
+            s.update(b_rows=sequence_rows(after(s["b_shard"], *y_parts)), g_rows=g_last)
+        elif shared_rows:
+            s["g_rows"] = sequence_rows(after(g_shard, above["values"][0]))
         s["grads"] = (s["a"], (dq, dk, dv, dg), dz, u, y)
         if layer > 0:
             attention_theirs_of(layer)
         back, gain_grads[layer] = norm_back(received_sum(sends), s["hidden"], s["inverse_one"], gain_one)
         grad = grad_mixed + back
 
+    block_sum = own_block(last_sends).astype(f32) + saved[last]["mixed"]
+    with_rows = lax.dynamic_update_slice_in_dim(last_sends, block_sum.astype(bf16), t * block, 0)
+    output = lax.psum(after(with_rows, sends), "tensor")
     ffn_theirs_of(0)
     for layer in reversed(range(1, layers)):
-        ffn_mine_of(layer, grad)
-    attention_theirs_of(0, grad)
+        ffn_mine_of(layer, sends)
+    attention_theirs_of(0, sends)
     gain_total = jnp.stack(gain_grads).reshape(1, -1)
     for axis in (("context", "tensor"),) if shared_rows else ("context", "tensor"):
         gain_total = jnp.sum(gathered(gain_total, axis), axis=0, keepdims=True)
     gain_total = gain_total.reshape(2 * layers, width)
     gain_total = gain_total[:, :half] + other(gain_total[:, half:])
-    attention_mine_of(0, gain_total, *saved[0]["ffn_received"])
+    attention_mine_of(0, gain_total)
     ffn_mine_of(0)
     if not shared_rows:
         results[5:] = [lax.psum(x, "context") for x in results[5:]]

time: 673 us -> 651 us (0.967)
  starting transfers between devices: 117 us -> 87.3 us
  blocking collectives: 108 us -> 125 us
    ppermute x61, starting transfers between devices: 77.2 us -> 54.9 us  [swap(): return lax.ppermute(x, axis, [(i, i ^ k) for i in range(n)])]
    all_to_all x4 -> x5, blocking collectives: 55.1 us -> 68.1 us  [received_sum(): lax.all_to_all(sends.reshape(count, -1, sends.shape[1]), 'tensor', 0, 0,...]
    all_to_all x7 -> x6, waiting for transfers between devices: 21 us -> 32.4 us  [gathered(): lax.all_to_all(copies, axis, 0, 0, tiled=True)]
    ppermute x61, waiting for transfers between devices: 85.3 us -> 77.3 us  [swap(): return lax.ppermute(x, axis, [(i, i ^ k) for i in range(n)])]
    all_to_all x3 -> x2, waiting for transfers between devices: 14.8 us -> 8.62 us  [received_sum(): lax.all_to_all(sends.reshape(count, -1, sends.shape[1]), 'tensor', 0, 0,...]
    all_to_all x7 -> x6, starting transfers between devices: 28.4 us -> 24.2 us  [gathered(): lax.all_to_all(copies, axis, 0, 0, tiled=True)]
    all_to_all x3 -> x4, blocking collectives: 52.7 us -> 56.9 us  [gathered(): lax.all_to_all(copies, axis, 0, 0, tiled=True)]
  transfers between devices with their start and end apart: 76 -> 74, of which waited for: 25 -> 26; matrix products, arithmetic and copies ran while one was open for 6% -> 6% of each run, Pallas kernels for 33% -> 36%
where the time goes in v12:
time: 651 us; the launch traced here: 641 us
  Pallas kernels  243 us (37%)
  blocking collectives  125 us (19%)
  waiting for transfers between devices  118 us (18%)
  starting transfers between devices  87.3 us (13%)
  local copies, waits for them, and re-layouts  34 us (5%)
  other arithmetic  18 us (3%)
  between operations  15.2 us (2%)
    ppermute x61, waiting for transfers between devices, swap(): return lax.ppermute(x, axis, [(i, i ^ k) for i in range(n)])  77.3 us
    all_to_all x5, blocking collectives, received_sum(): lax.all_to_all(sends.reshape(count, -1, sends.shape[1]), 'tensor', 0, 0,...  68.1 us
    pallas_call x2, Pallas kernels, attention_backward(): pl.pallas_call(functools.partial(backward_kernel, len(parts), piece_len,...  67.3 us
    all_to_all x4, blocking collectives, gathered(): lax.all_to_all(copies, axis, 0, 0, tiled=True)  56.9 us
    ppermute x61, starting transfers between devices, swap(): return lax.ppermute(x, axis, [(i, i ^ k) for i in range(n)])  54.9 us
    pallas_call x2, Pallas kernels, ffn_theirs(): pl.pallas_call(ffn_theirs_kernel, grid=(inner // hidden_block,), in_specs...  42.4 us
    pallas_call x2, Pallas kernels, forward_own(): pl.pallas_call(functools.partial(forward_own_kernel, len(parts), piece_le...  38.4 us
    pallas_call x4, Pallas kernels, attention_grads(): pl.pallas_call(functools.partial(attention_grads_kernel, steps, mine), gr...  36 us
  transfers between devices with their start and end apart: 74, of which 26 were waited for; matrix products, arithmetic and copies ran while one was open for 6% of the time, Pallas kernels for 36%

profile of v12, /device:TPU:0, one launch (start us, length us, event | category | flops | bytes accessed | tf_op | source)
XLA Modules:
  0.0 641.1 jit_solution(7531176301833646201)
XLA Ops:
  25.6 13.6 %all-to-all-done = s32[4,1,256]{2,1,0:T(1,128)} async-done(((s32[4,1,256]{2,1,0:T(1,128)}), s32[4,1,256]{2,1,0:T(1,128)}, u32[]{:S(2)}, u32[]{:S(2)}) %all-to-all-start) | async-done | bytes 4128 | tf_op jit(solution)/shard_map/all_to_all | solution.py:48
  68.3 19.2 %shard_map.255 = (bf16[1024,1536]{1,0:T(8,128)(2,1)}, bf16[1024,384]{1,0:T(8,128)(2,1)}, bf16[1024,384]{1,0:T(8,128)(2,1)}, bf16[1024,384]{1,0:T(8,128)(2,1)}, f...) custom-call(s32[2]{0:T(128)} %pad_add_fusion.refs_0_, ...), custom_call_target="tpu_custom_call" | custom-call | flops 20899999744 | tf_op jit(solution)/shard_map/pallas_call | solution.py:585
  87.5 15.7 %all_to_all.85 = bf16[4,64,1536]{2,1,0:T(8,128)(2,1)S(1)} all-to-all(bf16[4,64,1536]{2,1,0:T(8,128)(2,1)} %bitcast.67), channel_id=1, replica_groups=mesh['fsdp'=2,'context'=4,'tensor'=4] {'tensor'}, dimensions={0} | all-to-all | bytes 1572864 | tf_op jit(solution)/shard_map/all_to_all | solution.py:84
  104.2 14.3 %all_to_all.86 = bf16[4,64,1536]{2,1,0:T(8,128)(2,1)} all-to-all(bf16[4,64,1536]{2,1,0:T(8,128)(2,1)S(1)} %broadcast_in_dim.29), channel_id=1, replica_groups=mesh['fsdp'=2,'context'=4,'tensor'=4] {'tensor'}, dimensions={0} | all-to-all | bytes 1572864 | tf_op jit(solution)/shard_map/all_to_all | solution.py:48
  118.6 8.4 %shard_map.256 = (f32[256,1024]{1,0:T(8,128)}, f32[256,1024]{1,0:T(8,128)}, bf16[256,1536]{1,0:T(8,128)(2,1)}) custom-call(bf16[256,1536]{1,0:T(8,128)(2,1)} %bitcast.68, bf16[2,768,1024]{2,1,0:T(8,128)(2,1)} %wg.11, bf16[2,768,1024]{2,1,0:T(8,128)(2,1)} %wu.11, bf16[2,1024,768]{2,1,0:T(8,128)(2,1)} %wd.11, ...), custom_call_target="tpu_custom_call" | custom-call | flops 7699999744 | tf_op jit(solution)/shard_map/pallas_call | solution.py:652
  127.0 13.4 %all_to_all.87 = bf16[4,64,1536]{2,1,0:T(8,128)(2,1)S(1)} all-to-all(bf16[4,64,1536]{2,1,0:T(8,128)(2,1)} %bitcast.69), channel_id=1, replica_groups=mesh['fsdp'=2,'context'=4,'tensor'=4] {'tensor'}, dimensions={0} | all-to-all | bytes 1572864 | tf_op jit(solution)/shard_map/all_to_all | solution.py:84
  142.9 11.2 %all_to_all.88 = bf16[4,64,1536]{2,1,0:T(8,128)(2,1)S(1)} all-to-all(bf16[4,64,1536]{2,1,0:T(8,128)(2,1)S(1)} %broadcast_in_dim.30), channel_id=1, replica_groups=mesh['fsdp'=2,'context'=4,'tensor'=4] {'tensor'}, dimensions={0} | all-to-all | bytes 1572864 | tf_op jit(solution)/shard_map/all_to_all | solution.py:48
  160.1 13.2 %collective-permute-done.20.refs_3_ = bf16[64,1536]{1,0:T(8,128)(2,1)S(1)} collective-permute-done((bf16[64,1536]{1,0:T(8,128)(2,1)S(1)}, bf16[64,1536]{1,0:T(8,128)(2,1)S(1)}, u32[]{:S(2)}, u32[]{:S(2)}) %collective-permute-start.20) | collective-permute-done | bytes 196640 | tf_op jit(solution)/shard_map/ppermute | solution.py:25
  174.4 6.9 %collective-permute-done.24.refs_7_ = bf16[64,1536]{1,0:T(8,128)(2,1)S(1)} collective-permute-done((bf16[64,1536]{1,0:T(8,128)(2,1)S(1)}, bf16[64,1536]{1,0:T(8,128)(2,1)S(1)}, u32[]{:S(2)}, u32[]{:S(2)}) %collective-permute-start.24) | collective-permute-done | bytes 196640 | tf_op jit(solution)/shard_map/ppermute | solution.py:25
  197.5 19.2 %shard_map.261 = (bf16[1024,1536]{1,0:T(8,128)(2,1)}, bf16[1024,384]{1,0:T(8,128)(2,1)}, bf16[1024,384]{1,0:T(8,128)(2,1)}, bf16[1024,384]{1,0:T(8,128)(2,1)}, f...) custom-call(s32[2]{0:T(128)} %pad_add_fusion.refs_0_, ...), custom_call_target="tpu_custom_call" | custom-call | flops 20899999744 | tf_op jit(solution)/shard_map/pallas_call | solution.py:585
  216.7 14.6 %all_to_all.89 = bf16[4,64,1536]{2,1,0:T(8,128)(2,1)S(1)} all-to-all(bf16[4,64,1536]{2,1,0:T(8,128)(2,1)} %bitcast.66), channel_id=1, replica_groups=mesh['fsdp'=2,'context'=4,'tensor'=4] {'tensor'}, dimensions={0} | all-to-all | bytes 1572864 | tf_op jit(solution)/shard_map/all_to_all | solution.py:84
  231.7 20.2 %all_to_all.90 = bf16[4,64,1536]{2,1,0:T(8,128)(2,1)} all-to-all(bf16[4,64,1536]{2,1,0:T(8,128)(2,1)S(1)} %broadcast_in_dim.31), channel_id=1, replica_groups=mesh['fsdp'=2,'context'=4,'tensor'=4] {'tensor'}, dimensions={0} | all-to-all | bytes 1572864 | tf_op jit(solution)/shard_map/all_to_all | solution.py:48
  252.0 8.4 %shard_map.262 = (f32[256,1024]{1,0:T(8,128)}, f32[256,1024]{1,0:T(8,128)}, bf16[256,1536]{1,0:T(8,128)(2,1)}) custom-call(bf16[256,1536]{1,0:T(8,128)(2,1)} %bitcast.70, bf16[2,768,1024]{2,1,0:T(8,128)(2,1)} %wg.11, bf16[2,768,1024]{2,1,0:T(8,128)(2,1)} %wu.11, bf16[2,1024,768]{2,1,0:T(8,128)(2,1)} %wd.11, ...), custom_call_target="tpu_custom_call" | custom-call | flops 7699999744 | tf_op jit(solution)/shard_map/pallas_call | solution.py:652
  260.4 9.3 %shard_map.263 = bf16[256,1536]{1,0:T(8,128)(2,1)} custom-call(bf16[256,1536]{1,0:T(8,128)(2,1)} %copy-done.3, f32[256,1024]{1,0:T(8,128)} %get-tuple-element.106.gt_ref, f32[256,1024]{1,0:T(8,128)} %get-tuple-element.107.up_ref, bf16[2,768,1024]{2,1,0:T(8,128)(2,1)} %wg.11, bf16[2,768,1024]{2,1,0:T(8,128)(2,1)} %wu.11, bf16[2,1024,768]{2,1,0:T(8,128)(2,1)} %wd.11, ...), custom_call_target="tpu_custom_call" | custom-call | flops 8800000000 | tf_op jit(solution)/shard_map/pallas_call | solution.py:666
  269.7 12.4 %all_to_all.91 = bf16[4,64,1536]{2,1,0:T(8,128)(2,1)S(1)} all-to-all(bf16[4,64,1536]{2,1,0:T(8,128)(2,1)} %bitcast.71), channel_id=1, replica_groups=mesh['fsdp'=2,'context'=4,'tensor'=4] {'tensor'}, dimensions={0} | all-to-all | bytes 1572864 | tf_op jit(solution)/shard_map/all_to_all | solution.py:84
  285.3 11.1 %all_to_all.92 = bf16[4,64,1536]{2,1,0:T(8,128)(2,1)S(1)} all-to-all(bf16[4,64,1536]{2,1,0:T(8,128)(2,1)S(1)} %broadcast_in_dim.32), channel_id=1, replica_groups=mesh['fsdp'=2,'context'=4,'tensor'=4] {'tensor'}, dimensions={0} | all-to-all | bytes 1572864 | tf_op jit(solution)/shard_map/all_to_all | solution.py:48
  300.9 8.5 %collective-permute-done.29.refs_3_ = bf16[64,1536]{1,0:T(8,128)(2,1)S(1)} collective-permute-done((bf16[64,1536]{1,0:T(8,128)(2,1)S(1)}, bf16[64,1536]{1,0:T(8,128)(2,1)S(1)}, u32[]{:S(2)}, u32[]{:S(2)}) %collective-permute-start.29) | collective-permute-done | bytes 196640 | tf_op jit(solution)/shard_map/ppermute | solution.py:25
  325.4 33.6 %shard_map.265 = (bf16[1024,1536]{1,0:T(8,128)(2,1)}, bf16[1024,384]{1,0:T(8,128)(2,1)}, bf16[1024,384]{1,0:T(8,128)(2,1)}, bf16[1024,384]{1,0:T(8,128)(2,1)}, b...) custom-call(s32[2]{0:T(128)} %pad_add_fusion.refs_0_, ...), custom_call_target="tpu_custom_call" | custom-call | flops 36300001280 | tf_op jit(solution)/shard_map/pallas_call | solution.py:615
  359.1 12.0 %all_to_all.93 = bf16[4,64,1536]{2,1,0:T(8,128)(2,1)S(1)} all-to-all(bf16[4,64,1536]{2,1,0:T(8,128)(2,1)} %bitcast.65), channel_id=1, replica_groups=mesh['fsdp'=2,'context'=4,'tensor'=4] {'tensor'}, dimensions={0} | all-to-all | bytes 1572864 | tf_op jit(solution)/shard_map/all_to_all | solution.py:84
  377.1 8.5 %shard_map.266 = (bf16[768,384]{1,0:T(8,128)(2,1)}, bf16[768,384]{1,0:T(8,128)(2,1)}, bf16[768,384]{1,0:T(8,128)(2,1)}, bf16[768,384]{1,0:T(8,128)(2,1)}, bf16[7...) custom-call(bf16[1024,1536]{1,0:T(8,128)(2,1)} %get-tuple-element.117.refs_0_, ...), custom_call_target="tpu_custom_call" | custom-call | flops 7699999744 | tf_op jit(solution)/shard_map/pallas_call | solution.py:748
  393.0 9.3 %shard_map.267.refs_0_ = bf16[256,1536]{1,0:T(8,128)(2,1)} custom-call(bf16[256,1536]{1,0:T(8,128)(2,1)} %bitcast.64, f32[256,1024]{1,0:T(8,128)} %get-tuple-element.115.gt_ref, f32[256,1024]{1,0:T(8,128)} %get-tuple-element.116.up_ref, bf16[2,768,1024]{2,1,0:T(8,128)(2,1)} %wg.11, bf16[2,768,1024]{2,1,0:T(8,128)(2,1)} %wu.11, bf16[2,1024,768]{2,1,0:T(8,128)(2,1)} %wd.11, ...), custom_call_target="tpu_custom_call" | custom-call | flops 8800000000 | tf_op jit(solution)/shard_map/pallas_call | solution.py:666
  406.9 9.5 %shard_map.270 = (f32[2,768,384]{2,1,0:T(8,128)}, f32[2,768,384]{2,1,0:T(8,128)}, f32[2,768,384]{2,1,0:T(8,128)}, f32[2,768,384]{2,1,0:T(8,128)}, f32[768,128]{1,0:T(8,128)}, /*index=5*/f32[2,384,768]{2,1,0:T(8,128)}) custom-call(bf16[1024,1536]{1,0:T(8,128)(2,1)} %get-tuple-element.11, ...), custom_call_target="tpu_custom_call", output_to_operand_aliasing={{0}: (14, {}), {1}: (15, {}), {2}: (16, {}), {3}: (17, {}),... | custom-call | flops 7699999744 | tf_op jit(solution)/shard_map/pallas_call | solution.py:748
  434.8 10.6 %collective-permute-done.44.refs_0_ = bf16[64,1536]{1,0:T(8,128)(2,1)S(1)} collective-permute-done((bf16[64,1536]{1,0:T(8,128)(2,1)S(1)}, bf16[64,1536]{1,0:T(8,128)(2,1)S(1)}, u32[]{:S(2)}, u32[]{:S(2)}) %collective-permute-start.44) | collective-permute-done | bytes 196640 | tf_op jit(solution)/shard_map/ppermute | solution.py:25
  453.3 21.0 %shard_map.274 = (bf16[1024,1024]{1,0:T(8,128)(2,1)}, bf16[1024,1024]{1,0:T(8,128)(2,1)}, bf16[1024,1024]{1,0:T(8,128)(2,1)}, bf16[768,1024]{1,0:T(8,128)(2,1)},...) custom-call(bf16[1024,1536]{1,0:T(8,128)(2,1)} %all-gather.9.cloned.1.call-done.b_ref, ...), custom_call_target="tpu_custom_call" | custom-call | flops 26400000000 | tf_op jit(solution)/shard_map/pallas_call | solution.py:683
  475.5 33.7 %shard_map.276 = (bf16[1024,1536]{1,0:T(8,128)(2,1)}, bf16[1024,384]{1,0:T(8,128)(2,1)}, bf16[1024,384]{1,0:T(8,128)(2,1)}, bf16[1024,384]{1,0:T(8,128)(2,1)}, b...) custom-call(s32[2]{0:T(128)} %pad_add_fusion.refs_0_, ...), custom_call_target="tpu_custom_call" | custom-call | flops 36300001280 | tf_op jit(solution)/shard_map/pallas_call | solution.py:615
  516.6 8.6 %all-to-all-done.14 = bf16[4,64,1536]{2,1,0:T(8,128)(2,1)S(1)} async-done(((bf16[4,64,1536]{2,1,0:T(8,128)(2,1)}), bf16[4,64,1536]{2,1,0:T(8,128)(2,1)S(1)}, u32[]{:S(2)}, u32[]{:S(2)}) %all-to-all-start.14) | async-done | bytes 786464 | tf_op jit(solution)/shard_map/all_to_all | solution.py:84
  532.1 14.1 %all-to-all-done.16 = f32[16,1,6144]{2,1,0:T(1,128)S(1)} async-done(((f32[16,1,6144]{2,1,0:T(1,128)}), f32[16,1,6144]{2,1,0:T(1,128)S(1)}, u32[]{:S(2)}, u32[]{:S(2)}) %all-to-all-start.16) | async-done | bytes 393248 | tf_op jit(solution)/shard_map/all_to_all | solution.py:48
  552.4 8.5 %shard_map.281 = (bf16[768,384]{1,0:T(8,128)(2,1)}, bf16[768,384]{1,0:T(8,128)(2,1)}, bf16[768,384]{1,0:T(8,128)(2,1)}, bf16[768,384]{1,0:T(8,128)(2,1)}, bf16[7...) custom-call(bf16[1024,1536]{1,0:T(8,128)(2,1)} %get-tuple-element.146.refs_0_, ...), custom_call_target="tpu_custom_call" | custom-call | flops 7699999744 | tf_op jit(solution)/shard_map/pallas_call | solution.py:748
  571.4 9.6 %shard_map.282 = (f32[2,768,384]{2,1,0:T(8,128)}, f32[2,768,384]{2,1,0:T(8,128)}, f32[2,768,384]{2,1,0:T(8,128)}, f32[2,768,384]{2,1,0:T(8,128)}, f32[768,128]{1,0:T(8,128)}, /*index=5*/f32[2,384,768]{2,1,0:T(8,128)}) custom-call(bf16[1024,1536]{1,0:T(8,128)(2,1)} %get-tuple-element.14, ...), custom_call_target="tpu_custom_call", output_to_operand_aliasing={{0}: (14, {}), {1}: (15, {}), {2}: (16, {}), {3}: (17, {}),... | custom-call | flops 7699999744 | tf_op jit(solution)/shard_map/pallas_call | solution.py:748
  584.2 21.4 %shard_map.279 = (bf16[1024,1024]{1,0:T(8,128)(2,1)}, bf16[1024,1024]{1,0:T(8,128)(2,1)}, bf16[1024,1024]{1,0:T(8,128)(2,1)}, bf16[768,1024]{1,0:T(8,128)(2,1)},...) custom-call(bf16[1024,1536]{1,0:T(8,128)(2,1)} %all-gather.7.cloned.1.call-done.refs_1_.b_ref, ...), custom_call_target="tpu_custom_call" | custom-call | flops 26400000000 | tf_op jit(solution)/shard_map/pallas_call | solution.py:683
  607.9 11.9 %shard_map.283 = (f32[2,768,1024]{2,1,0:T(8,128)}, f32[2,768,1024]{2,1,0:T(8,128)}, f32[2,1024,768]{2,1,0:T(8,128)}) custom-call(bf16[1024,1536]{1,0:T(8,128)(2,1)} %all-gather.9.cloned.1.call-done.b_ref, bf16[1024,1536]{1,0:T(8,128)(2,1)} %all-gather.5.cloned.1.call-done.refs_1_.g_ref, ...), custom_call_target="tpu_custom_call", output_to_operand_aliasing={{0}: (8, {}), {1}: (9, {}), {2}: (10, {})} | custom-call | flops 9900000256 | tf_op jit(solution)/shard_map/pallas_call | solution.py:708
  622.3 11.8 %shard_map.284 = (f32[2,768,1024]{2,1,0:T(8,128)}, f32[2,768,1024]{2,1,0:T(8,128)}, f32[2,1024,768]{2,1,0:T(8,128)}) custom-call(bf16[1024,1536]{1,0:T(8,128)(2,1)} %all-gather.7.cloned.1.call-done.refs_1_.b_ref, bf16[1024,1536]{1,0:T(8,128)(2,1)} %all-gather.11.cloned.1.call-done.g_ref, ...), custom_call_target="tpu_custom_call", output_to_operand_aliasing={{0}: (8, {}), {1}: (9, {}), {2}: (10, {})} | custom-call | flops 9900000256 | tf_op jit(solution)/shard_map/pallas_call | solution.py:708
  (394 shorter events, 182.1 us)
Async XLA Ops:
  11.4 49.4 %collective-permute-start.1 = (bf16[256,1536]{1,0:T(8,128)(2,1)S(1)}, bf16[256,1536]{1,0:T(8,128)(2,1)}, u32[]{:S(2)}, u32[]{:S(2)}) collective-permute-start(bf16[256,1536]{1,0:T(8,128)(2,1)S(1)} %multiply_convert_fusion.refs_1_), channel_id=1, source_target_pairs={{0,4},{4,0},{8,12},{12,8},{1,5},{5,1},{9,13},{13,9},{2,6},{6,2},{1... | collective-permute-start | bytes 2359304 | tf_op jit(solution)/shard_map/ppermute | solution.py:25
  14.1 25.1 %collective-permute-start.2 = (bf16[64,1536]{1,0:T(8,128)(2,1)S(1)}, bf16[64,1536]{1,0:T(8,128)(2,1)S(1)}, u32[]{:S(2)}, u32[]{:S(2)}) collective-permute-start(bf16[64,1536]{1,0:T(8,128)(2,1)S(1)} %constant_dynamic-slice_fusion), channel_id=1, source_target_pairs={{0,8},{4,12},{8,0},{12,4},{1,9},{5,13},{9,1},{13,5},{2,10},{6,14},... | collective-permute-start | bytes 589832 | tf_op jit(solution)/shard_map/ppermute | solution.py:25
  18.0 21.2 %all-to-all-start = ((s32[4,1,256]{2,1,0:T(1,128)}), s32[4,1,256]{2,1,0:T(1,128)}, u32[]{:S(2)}, u32[]{:S(2)}) async-start(s32[4,1,256]{2,1,0:T(1,128)} %broadcast_in_dim.27), calls=%async_computation | async-start | bytes 8192 | tf_op jit(solution)/shard_map/all_to_all | solution.py:48
  21.8 120.0 %all-gather.5.cloned.1.call-start = ((), (), s32[]{:S(2)}) async-start(), calls=%async_computation.17 | async-start | bytes 3932160 | tf_op jit(solution)/shard_map/all_gather | solution.py:846
  21.9 22.9 %collective-permute-start.6 = (bf16[64,1536]{1,0:T(8,128)(2,1)S(1)}, bf16[64,1536]{1,0:T(8,128)(2,1)}, u32[]{:S(2)}, u32[]{:S(2)}) collective-permute-start(bf16[64,1536]{1,0:T(8,128)(2,1)S(1)} %constant_dynamic-slice_fusion), channel_id=1, source_target_pairs={{0,12},{4,8},{8,4},{12,0},{1,13},{5,9},{9,5},{13,1},{2,14},{6,10},... | collective-permute-start | bytes 589832 | tf_op jit(solution)/shard_map/ppermute | solution.py:25
  67.6 216.7 %all-gather.7.cloned.1.call-start = ((), (), s32[]{:S(2)}) async-start(), calls=%async_computation.18 | async-start | bytes 3342336 | tf_op jit(solution)/shard_map/all_gather | solution.py:52
  67.7 50.9 %collective-permute-start.16 = (bf16[2,768,1024]{2,1,0:T(8,128)(2,1)}, bf16[2,768,1024]{2,1,0:T(8,128)(2,1)}, u32[]{:S(2)}, u32[]{:S(2)}) collective-permute-start(bf16[2,768,1024]{2,1,0:T(8,128)(2,1)} %wg.11), channel_id=1, source_target_pairs={{0,16},{16,0},{1,17},{17,1},{2,18},{18,2},{3,19},{19,3},{4,20},{20... | collective-permute-start | bytes 9437192 | tf_op jit(solution)/shard_map/ppermute | solution.py:25
  67.7 50.8 %collective-permute-start.17 = (bf16[2,768,1024]{2,1,0:T(8,128)(2,1)}, bf16[2,768,1024]{2,1,0:T(8,128)(2,1)}, u32[]{:S(2)}, u32[]{:S(2)}) collective-permute-start(bf16[2,768,1024]{2,1,0:T(8,128)(2,1)} %wu.11), channel_id=1, source_target_pairs={{0,16},{16,0},{1,17},{17,1},{2,18},{18,2},{3,19},{19,3},{4,20},{20... | collective-permute-start | bytes 9437192 | tf_op jit(solution)/shard_map/ppermute | solution.py:25
  68.2 50.3 %collective-permute-start.18 = (bf16[2,1024,768]{2,1,0:T(8,128)(2,1)}, bf16[2,1024,768]{2,1,0:T(8,128)(2,1)}, u32[]{:S(2)}, u32[]{:S(2)}) collective-permute-start(bf16[2,1024,768]{2,1,0:T(8,128)(2,1)} %wd.11), channel_id=1, source_target_pairs={{0,16},{16,0},{1,17},{17,1},{2,18},{18,2},{3,19},{19,3},{4,20},{20... | collective-permute-start | bytes 9437192 | tf_op jit(solution)/shard_map/ppermute | solution.py:25
  154.1 42.5 %collective-permute-start.19 = (bf16[256,1536]{1,0:T(8,128)(2,1)S(1)}, bf16[256,1536]{1,0:T(8,128)(2,1)S(1)}, u32[]{:S(2)}, u32[]{:S(2)}) collective-permute-start(bf16[256,1536]{1,0:T(8,128)(2,1)S(1)} %bitcast.62), channel_id=1, source_target_pairs={{0,4},{4,0},{8,12},{12,8},{1,5},{5,1},{9,13},{13,9},{2,6},{6,2},{1... | collective-permute-start | bytes 2359304 | tf_op jit(solution)/shard_map/ppermute | solution.py:25
  154.1 19.2 %collective-permute-start.20 = (bf16[64,1536]{1,0:T(8,128)(2,1)S(1)}, bf16[64,1536]{1,0:T(8,128)(2,1)S(1)}, u32[]{:S(2)}, u32[]{:S(2)}) collective-permute-start(bf16[64,1536]{1,0:T(8,128)(2,1)S(1)} %copy-done.13), channel_id=1, source_target_pairs={{0,8},{4,12},{8,0},{12,4},{1,9},{5,13},{9,1},{13,5},{2,10},{6,14},... | collective-permute-start | bytes 589832 | tf_op jit(solution)/shard_map/ppermute | solution.py:25
  160.1 21.2 %collective-permute-start.24 = (bf16[64,1536]{1,0:T(8,128)(2,1)S(1)}, bf16[64,1536]{1,0:T(8,128)(2,1)S(1)}, u32[]{:S(2)}, u32[]{:S(2)}) collective-permute-start(bf16[64,1536]{1,0:T(8,128)(2,1)S(1)} %copy-done.13), channel_id=1, source_target_pairs={{0,12},{4,8},{8,4},{12,0},{1,13},{5,9},{9,5},{13,1},{2,14},{6,10},... | collective-permute-start | bytes 589832 | tf_op jit(solution)/shard_map/ppermute | solution.py:25
  190.3 262.9 %all-gather.9.cloned.1.call-start = ((), (), s32[]{:S(2)}) async-start(), calls=%async_computation.19 | async-start | bytes 3342336 | tf_op jit(solution)/shard_map/all_gather | solution.py:52
  296.5 28.9 %collective-permute-start.28 = (bf16[256,1536]{1,0:T(8,128)(2,1)S(1)}, bf16[256,1536]{1,0:T(8,128)(2,1)}, u32[]{:S(2)}, u32[]{:S(2)}) collective-permute-start(bf16[256,1536]{1,0:T(8,128)(2,1)S(1)} %bitcast.52), channel_id=1, source_target_pairs={{0,4},{4,0},{8,12},{12,8},{1,5},{5,1},{9,13},{13,9},{2,6},{6,2},{1... | collective-permute-start | bytes 2359304 | tf_op jit(solution)/shard_map/ppermute | solution.py:25
  373.2 18.9 %all-to-all-start.10 = ((bf16[4,64,1536]{2,1,0:T(8,128)(2,1)}), bf16[4,64,1536]{2,1,0:T(8,128)(2,1)S(1)}, u32[]{:S(2)}, u32[]{:S(2)}) async-start(bf16[4,64,1536]{2,1,0:T(8,128)(2,1)} %broadcast_in_dim.33), calls=%async_computation.10 | async-start | bytes 1572864 | tf_op jit(solution)/shard_map/all_to_all | solution.py:48
  385.6 16.7 %collective-permute-start.37 = (bf16[768,384]{1,0:T(8,128)(2,1)}, bf16[768,384]{1,0:T(8,128)(2,1)S(1)}, u32[]{:S(2)}, u32[]{:S(2)}) collective-permute-start(bf16[768,384]{1,0:T(8,128)(2,1)} %get-tuple-element.125.refs_0_), channel_id=1, source_target_pairs={{0,16},{16,0},{1,17},{17,1},{2,18},{18,2},{3,19},{19,3},{4,20},{20... | collective-permute-start | bytes 1769480 | tf_op jit(solution)/shard_map/ppermute | solution.py:25
  386.1 16.2 %collective-permute-start.38 = (bf16[768,384]{1,0:T(8,128)(2,1)}, bf16[768,384]{1,0:T(8,128)(2,1)S(1)}, u32[]{:S(2)}, u32[]{:S(2)}) collective-permute-start(bf16[768,384]{1,0:T(8,128)(2,1)} %get-tuple-element.126), channel_id=1, source_target_pairs={{0,16},{16,0},{1,17},{17,1},{2,18},{18,2},{3,19},{19,3},{4,20},{20... | collective-permute-start | bytes 1769480 | tf_op jit(solution)/shard_map/ppermute | solution.py:25
  386.2 16.2 %collective-permute-start.39 = (bf16[768,384]{1,0:T(8,128)(2,1)}, bf16[768,384]{1,0:T(8,128)(2,1)}, u32[]{:S(2)}, u32[]{:S(2)}) collective-permute-start(bf16[768,384]{1,0:T(8,128)(2,1)} %get-tuple-element.127), channel_id=1, source_target_pairs={{0,16},{16,0},{1,17},{17,1},{2,18},{18,2},{3,19},{19,3},{4,20},{20... | collective-permute-start | bytes 1769480 | tf_op jit(solution)/shard_map/ppermute | solution.py:25
  420.0 26.3 %all-to-all-start.12 = ((bf16[4,64,1536]{2,1,0:T(8,128)(2,1)}), bf16[4,64,1536]{2,1,0:T(8,128)(2,1)S(1)}, u32[]{:S(2)}, u32[]{:S(2)}) async-start(bf16[4,64,1536]{2,1,0:T(8,128)(2,1)} %broadcast_in_dim.34), calls=%async_computation.12 | async-start | bytes 1572864 | tf_op jit(solution)/shard_map/all_to_all | solution.py:48
  429.0 16.5 %collective-permute-start.44 = (bf16[64,1536]{1,0:T(8,128)(2,1)S(1)}, bf16[64,1536]{1,0:T(8,128)(2,1)S(1)}, u32[]{:S(2)}, u32[]{:S(2)}) collective-permute-start(bf16[64,1536]{1,0:T(8,128)(2,1)S(1)} %copy-done.14), channel_id=1, source_target_pairs={{0,8},{4,12},{8,0},{12,4},{1,9},{5,13},{9,1},{13,5},{2,10},{6,14},... | collective-permute-start | bytes 589832 | tf_op jit(solution)/shard_map/ppermute | solution.py:25
  446.3 28.0 %collective-permute-start.43 = (bf16[256,1536]{1,0:T(8,128)(2,1)S(1)}, bf16[256,1536]{1,0:T(8,128)(2,1)}, u32[]{:S(2)}, u32[]{:S(2)}) collective-permute-start(bf16[256,1536]{1,0:T(8,128)(2,1)S(1)} %bitcast.56), channel_id=1, source_target_pairs={{0,4},{4,0},{8,12},{12,8},{1,5},{5,1},{9,13},{13,9},{2,6},{6,2},{1... | collective-permute-start | bytes 2359304 | tf_op jit(solution)/shard_map/ppermute | solution.py:25
  449.5 24.9 %all-to-all-start.13 = ((bf16[4,128,1536]{2,1,0:T(8,128)(2,1)}), bf16[4,128,1536]{2,1,0:T(8,128)(2,1)S(1)}, u32[]{:S(2)}, u32[]{:S(2)}) async-start(bf16[4,128,1536]{2,1,0:T(8,128)(2,1)} %broadcast_in_dim.35), calls=%async_computation.13 | async-start | bytes 3145728 | tf_op jit(solution)/shard_map/all_to_all | solution.py:48
  453.3 131.0 %all-gather.11.cloned.1.call-start = ((), (), s32[]{:S(2)}) async-start(), calls=%async_computation.21 | async-start | bytes 3342336 | tf_op jit(solution)/shard_map/all_gather | solution.py:52
  526.6 19.6 %all-to-all-start.16 = ((f32[16,1,6144]{2,1,0:T(1,128)}), f32[16,1,6144]{2,1,0:T(1,128)S(1)}, u32[]{:S(2)}, u32[]{:S(2)}) async-start(f32[16,1,6144]{2,1,0:T(1,128)} %broadcast_in_dim.38), calls=%async_computation.16 | async-start | bytes 786432 | tf_op jit(solution)/shard_map/all_to_all | solution.py:48
  547.1 18.8 %all-to-all-start.15 = ((bf16[4,64,1536]{2,1,0:T(8,128)(2,1)}), bf16[4,64,1536]{2,1,0:T(8,128)(2,1)S(1)}, u32[]{:S(2)}, u32[]{:S(2)}) async-start(bf16[4,64,1536]{2,1,0:T(8,128)(2,1)} %broadcast_in_dim.36), calls=%async_computation.15 | async-start | bytes 1572864 | tf_op jit(solution)/shard_map/all_to_all | solution.py:48
  552.2 67.7 %all-reduce.4.cloned.1.call-start = ((), (), s32[]{:S(2)}) async-start(), calls=%async_computation.20 | async-start | bytes 1572864 | tf_op jit(solution)/shard_map/psum | solution.py:943
  569.7 36.5 %collective-permute-start.58 = (bf16[768,1024]{1,0:T(8,128)(2,1)}, bf16[768,1024]{1,0:T(8,128)(2,1)S(1)}, u32[]{:S(2)}, u32[]{:S(2)}) collective-permute-start(bf16[768,1024]{1,0:T(8,128)(2,1)} %get-tuple-element.178), channel_id=1, source_target_pairs={{0,16},{16,0},{1,17},{17,1},{2,18},{18,2},{3,19},{19,3},{4,20},{20... | collective-permute-start | bytes 4718600 | tf_op jit(solution)/shard_map/ppermute | solution.py:25
  570.9 35.4 %collective-permute-start.59 = (bf16[768,1024]{1,0:T(8,128)(2,1)}, bf16[768,1024]{1,0:T(8,128)(2,1)S(1)}, u32[]{:S(2)}, u32[]{:S(2)}) collective-permute-start(bf16[768,1024]{1,0:T(8,128)(2,1)} %get-tuple-element.179), channel_id=1, source_target_pairs={{0,16},{16,0},{1,17},{17,1},{2,18},{18,2},{3,19},{19,3},{4,20},{20... | collective-permute-start | bytes 4718600 | tf_op jit(solution)/shard_map/ppermute | solution.py:25
  571.1 35.3 %collective-permute-start.60 = (bf16[1024,768]{1,0:T(8,128)(2,1)}, bf16[1024,768]{1,0:T(8,128)(2,1)}, u32[]{:S(2)}, u32[]{:S(2)}) collective-permute-start(bf16[1024,768]{1,0:T(8,128)(2,1)} %get-tuple-element.180), channel_id=1, source_target_pairs={{0,16},{16,0},{1,17},{17,1},{2,18},{18,2},{3,19},{19,3},{4,20},{20... | collective-permute-start | bytes 4718600 | tf_op jit(solution)/shard_map/ppermute | solution.py:25
  605.6 16.7 %collective-permute-start.55 = (bf16[768,1024]{1,0:T(8,128)(2,1)}, bf16[768,1024]{1,0:T(8,128)(2,1)}, u32[]{:S(2)}, u32[]{:S(2)}) collective-permute-start(bf16[768,1024]{1,0:T(8,128)(2,1)} %get-tuple-element.173), channel_id=1, source_target_pairs={{0,16},{16,0},{1,17},{17,1},{2,18},{18,2},{3,19},{19,3},{4,20},{20... | collective-permute-start | bytes 4718600 | tf_op jit(solution)/shard_map/ppermute | solution.py:25
  605.8 16.5 %collective-permute-start.56 = (bf16[768,1024]{1,0:T(8,128)(2,1)}, bf16[768,1024]{1,0:T(8,128)(2,1)}, u32[]{:S(2)}, u32[]{:S(2)}) collective-permute-start(bf16[768,1024]{1,0:T(8,128)(2,1)} %get-tuple-element.174), channel_id=1, source_target_pairs={{0,16},{16,0},{1,17},{17,1},{2,18},{18,2},{3,19},{19,3},{4,20},{20... | collective-permute-start | bytes 4718600 | tf_op jit(solution)/shard_map/ppermute | solution.py:25
  606.2 16.1 %collective-permute-start.57 = (bf16[1024,768]{1,0:T(8,128)(2,1)}, bf16[1024,768]{1,0:T(8,128)(2,1)}, u32[]{:S(2)}, u32[]{:S(2)}) collective-permute-start(bf16[1024,768]{1,0:T(8,128)(2,1)} %get-tuple-element.175), channel_id=1, source_target_pairs={{0,16},{16,0},{1,17},{17,1},{2,18},{18,2},{3,19},{19,3},{4,20},{20... | collective-permute-start | bytes 4718600 | tf_op jit(solution)/shard_map/ppermute | solution.py:25
  (116 other events, 1171.2 us)
Sparse Core Ops, SparseCore 0:
  67.7 64.7 all-gather.4
  190.5 72.2 all-gather.6
  325.6 74.8 all-gather.8
  474.4 75.0 all-gather.10
  562.6 49.8 all-reduce.3

commit v13 on v12

--- a/solution.py
+++ b/solution.py
@@ -941,21 +941,21 @@
     block_sum = own_block(last_sends).astype(f32) + saved[last]["mixed"]
     with_rows = lax.dynamic_update_slice_in_dim(last_sends, block_sum.astype(bf16), t * block, 0)
     output = lax.psum(after(with_rows, sends), "tensor")
-    ffn_theirs_of(0)
     for layer in reversed(range(1, layers)):
         ffn_mine_of(layer, sends)
     attention_theirs_of(0, sends)
-    gain_total = jnp.stack(gain_grads).reshape(1, -1)
+    gain_total = after(jnp.stack(gain_grads).reshape(1, -1), *([results[5]] if layers > 1 else []))
     for axis in (("context", "tensor"),) if shared_rows else ("context", "tensor"):
         gain_total = jnp.sum(gathered(gain_total, axis), axis=0, keepdims=True)
     gain_total = gain_total.reshape(2 * layers, width)
     gain_total = gain_total[:, :half] + other(gain_total[:, half:])
-    attention_mine_of(0, gain_total)
+    grad_input = finish(after(grad, saved[0]["theirs"][0]))
+    ffn_theirs_of(0)
+    attention_mine_of(0, gain_total, saved[0]["values"][0])
     ffn_mine_of(0)
     if not shared_rows:
         results[5:] = [lax.psum(x, "context") for x in results[5:]]
     output = features(after(output, saved[0]["values"][0])).reshape(1, piece_len, width)
-    grad_input = finish(grad)
     return (
         output, grad_input, *results[:5], jnp.stack(small[0]), jnp.stack(small[1]),
         gain_total[:layers], gain_total[layers:], *results[5:],

time: 651 us -> 646 us (level)
  waiting for transfers between devices: 118 us -> 137 us
  blocking collectives: 125 us -> 111 us
  starting transfers between devices: 87.3 us -> 76.6 us
    ppermute x61, waiting for transfers between devices: 77.3 us -> 100 us  [swap(): return lax.ppermute(x, axis, [(i, i ^ k) for i in range(n)])]
    all_to_all x6, waiting for transfers between devices: 32.4 us -> 12.2 us  [gathered(): lax.all_to_all(copies, axis, 0, 0, tiled=True)]
    ppermute x61, starting transfers between devices: 54.9 us -> 41.4 us  [swap(): return lax.ppermute(x, axis, [(i, i ^ k) for i in range(n)])]
    all_to_all x5 -> x4, blocking collectives: 68.1 us -> 58.5 us  [received_sum(): lax.all_to_all(sends.reshape(count, -1, sends.shape[1]), 'tensor', 0, 0,...]
    all_to_all x2 -> x3, waiting for transfers between devices: 8.62 us -> 16.3 us  [received_sum(): lax.all_to_all(sends.reshape(count, -1, sends.shape[1]), 'tensor', 0, 0,...]
    psum x1, waiting for transfers between devices: 0.01 us -> 7.35 us  [local(): output = lax.psum(after(with_rows, sends), 'tensor')]
  transfers between devices with their start and end apart: 74 -> 75, of which waited for: 26 -> 27; matrix products, arithmetic and copies ran while one was open for 6% -> 6% of each run, Pallas kernels for 36% -> 31%
where the time goes in v13:
time: 646 us; the launch traced here: 636 us
  Pallas kernels  244 us (38%)
  waiting for transfers between devices  137 us (21%)
  blocking collectives  111 us (17%)
  starting transfers between devices  76.6 us (12%)
  local copies, waits for them, and re-layouts  32 us (5%)
  other arithmetic  20.3 us (3%)
  between operations  15.4 us (2%)
    ppermute x61, waiting for transfers between devices, swap(): return lax.ppermute(x, axis, [(i, i ^ k) for i in range(n)])  100 us
    pallas_call x2, Pallas kernels, attention_backward(): pl.pallas_call(functools.partial(backward_kernel, len(parts), piece_len,...  67.2 us
    all_to_all x4, blocking collectives, received_sum(): lax.all_to_all(sends.reshape(count, -1, sends.shape[1]), 'tensor', 0, 0,...  58.5 us
    all_to_all x4, blocking collectives, gathered(): lax.all_to_all(copies, axis, 0, 0, tiled=True)  52.7 us
    pallas_call x2, Pallas kernels, ffn_theirs(): pl.pallas_call(ffn_theirs_kernel, grid=(inner // hidden_block,), in_specs...  42.4 us
    ppermute x61, starting transfers between devices, swap(): return lax.ppermute(x, axis, [(i, i ^ k) for i in range(n)])  41.4 us
    pallas_call x2, Pallas kernels, forward_own(): pl.pallas_call(functools.partial(forward_own_kernel, len(parts), piece_le...  39 us
    pallas_call x4, Pallas kernels, attention_grads(): pl.pallas_call(functools.partial(attention_grads_kernel, steps, mine), gr...  36.1 us
  transfers between devices with their start and end apart: 75, of which 27 were waited for; matrix products, arithmetic and copies ran while one was open for 6% of the time, Pallas kernels for 31%

profile of v13, /device:TPU:0, one launch (start us, length us, event | category | flops | bytes accessed | tf_op | source)
XLA Modules:
  0.0 636.2 jit_solution(13693533567689789958)
XLA Ops:
  16.8 22.4 %collective-permute-done.6.refs_7_.refs_2_ = bf16[64,1536]{1,0:T(8,128)(2,1)} collective-permute-done((bf16[64,1536]{1,0:T(8,128)(2,1)S(1)}, bf16[64,1536]{1,0:T(8,128)(2,1)}, u32[]{:S(2)}, u32[]{:S(2)}) %collective-permute-start.6) | collective-permute-done | bytes 196640 | tf_op jit(solution)/shard_map/ppermute | solution.py:25
  57.7 11.7 %collective-permute-done.7.refs_8_ = bf16[64,1536]{1,0:T(8,128)(2,1)S(1)} collective-permute-done((bf16[64,1536]{1,0:T(8,128)(2,1)}, bf16[64,1536]{1,0:T(8,128)(2,1)S(1)}, u32[]{:S(2)}, u32[]{:S(2)}) %collective-permute-start.7) | collective-permute-done | bytes 196640 | tf_op jit(solution)/shard_map/ppermute | solution.py:25
  79.3 19.7 %shard_map.255 = (bf16[1024,1536]{1,0:T(8,128)(2,1)}, bf16[1024,384]{1,0:T(8,128)(2,1)}, bf16[1024,384]{1,0:T(8,128)(2,1)}, bf16[1024,384]{1,0:T(8,128)(2,1)}, f...) custom-call(s32[2]{0:T(128)} %pad_add_fusion.refs_0_, ...), custom_call_target="tpu_custom_call" | custom-call | flops 20899999744 | tf_op jit(solution)/shard_map/pallas_call | solution.py:585
  99.0 15.4 %all_to_all.85 = bf16[4,64,1536]{2,1,0:T(8,128)(2,1)S(1)} all-to-all(bf16[4,64,1536]{2,1,0:T(8,128)(2,1)} %bitcast.72), channel_id=1, replica_groups=mesh['fsdp'=2,'context'=4,'tensor'=4] {'tensor'}, dimensions={0} | all-to-all | bytes 1572864 | tf_op jit(solution)/shard_map/all_to_all | solution.py:84
  115.4 14.0 %all_to_all.86 = bf16[4,64,1536]{2,1,0:T(8,128)(2,1)} all-to-all(bf16[4,64,1536]{2,1,0:T(8,128)(2,1)S(1)} %broadcast_in_dim.29), channel_id=1, replica_groups=mesh['fsdp'=2,'context'=4,'tensor'=4] {'tensor'}, dimensions={0} | all-to-all | bytes 1572864 | tf_op jit(solution)/shard_map/all_to_all | solution.py:48
  129.4 8.4 %shard_map.256 = (f32[256,1024]{1,0:T(8,128)}, f32[256,1024]{1,0:T(8,128)}, bf16[256,1536]{1,0:T(8,128)(2,1)}) custom-call(bf16[256,1536]{1,0:T(8,128)(2,1)} %bitcast.73, bf16[2,768,1024]{2,1,0:T(8,128)(2,1)} %wg.11, bf16[2,768,1024]{2,1,0:T(8,128)(2,1)} %wu.11, bf16[2,1024,768]{2,1,0:T(8,128)(2,1)} %wd.11, ...), custom_call_target="tpu_custom_call" | custom-call | flops 7699999744 | tf_op jit(solution)/shard_map/pallas_call | solution.py:652
  137.8 13.0 %all_to_all.87 = bf16[4,64,1536]{2,1,0:T(8,128)(2,1)S(1)} all-to-all(bf16[4,64,1536]{2,1,0:T(8,128)(2,1)} %bitcast.74), channel_id=1, replica_groups=mesh['fsdp'=2,'context'=4,'tensor'=4] {'tensor'}, dimensions={0} | all-to-all | bytes 1572864 | tf_op jit(solution)/shard_map/all_to_all | solution.py:84
  153.4 11.1 %all_to_all.88 = bf16[4,64,1536]{2,1,0:T(8,128)(2,1)S(1)} all-to-all(bf16[4,64,1536]{2,1,0:T(8,128)(2,1)S(1)} %broadcast_in_dim.30), channel_id=1, replica_groups=mesh['fsdp'=2,'context'=4,'tensor'=4] {'tensor'}, dimensions={0} | all-to-all | bytes 1572864 | tf_op jit(solution)/shard_map/all_to_all | solution.py:48
  168.0 16.7 %collective-permute-done.24.refs_7_ = bf16[64,1536]{1,0:T(8,128)(2,1)S(1)} collective-permute-done((bf16[64,1536]{1,0:T(8,128)(2,1)S(1)}, bf16[64,1536]{1,0:T(8,128)(2,1)S(1)}, u32[]{:S(2)}, u32[]{:S(2)}) %collective-permute-start.24) | collective-permute-done | bytes 196640 | tf_op jit(solution)/shard_map/ppermute | solution.py:25
  200.2 19.3 %shard_map.261 = (bf16[1024,1536]{1,0:T(8,128)(2,1)}, bf16[1024,384]{1,0:T(8,128)(2,1)}, bf16[1024,384]{1,0:T(8,128)(2,1)}, bf16[1024,384]{1,0:T(8,128)(2,1)}, f...) custom-call(s32[2]{0:T(128)} %pad_add_fusion.refs_0_, ...), custom_call_target="tpu_custom_call" | custom-call | flops 20899999744 | tf_op jit(solution)/shard_map/pallas_call | solution.py:585
  219.5 17.9 %all_to_all.89 = bf16[4,64,1536]{2,1,0:T(8,128)(2,1)S(1)} all-to-all(bf16[4,64,1536]{2,1,0:T(8,128)(2,1)} %bitcast.71), channel_id=1, replica_groups=mesh['fsdp'=2,'context'=4,'tensor'=4] {'tensor'}, dimensions={0} | all-to-all | bytes 1572864 | tf_op jit(solution)/shard_map/all_to_all | solution.py:84
  237.9 16.5 %all_to_all.90 = bf16[4,64,1536]{2,1,0:T(8,128)(2,1)} all-to-all(bf16[4,64,1536]{2,1,0:T(8,128)(2,1)S(1)} %broadcast_in_dim.31), channel_id=1, replica_groups=mesh['fsdp'=2,'context'=4,'tensor'=4] {'tensor'}, dimensions={0} | all-to-all | bytes 1572864 | tf_op jit(solution)/shard_map/all_to_all | solution.py:48
  254.4 8.4 %shard_map.262 = (f32[256,1024]{1,0:T(8,128)}, f32[256,1024]{1,0:T(8,128)}, bf16[256,1536]{1,0:T(8,128)(2,1)}) custom-call(bf16[256,1536]{1,0:T(8,128)(2,1)} %bitcast.75, bf16[2,768,1024]{2,1,0:T(8,128)(2,1)} %wg.11, bf16[2,768,1024]{2,1,0:T(8,128)(2,1)} %wu.11, bf16[2,1024,768]{2,1,0:T(8,128)(2,1)} %wd.11, ...), custom_call_target="tpu_custom_call" | custom-call | flops 7699999744 | tf_op jit(solution)/shard_map/pallas_call | solution.py:652
  262.8 9.3 %shard_map.263 = bf16[256,1536]{1,0:T(8,128)(2,1)} custom-call(bf16[256,1536]{1,0:T(8,128)(2,1)} %copy-done.3, f32[256,1024]{1,0:T(8,128)} %get-tuple-element.106.gt_ref, f32[256,1024]{1,0:T(8,128)} %get-tuple-element.107.up_ref, bf16[2,768,1024]{2,1,0:T(8,128)(2,1)} %wg.11, bf16[2,768,1024]{2,1,0:T(8,128)(2,1)} %wu.11, bf16[2,1024,768]{2,1,0:T(8,128)(2,1)} %wd.11, ...), custom_call_target="tpu_custom_call" | custom-call | flops 8800000000 | tf_op jit(solution)/shard_map/pallas_call | solution.py:666
  272.1 12.1 %all_to_all.91 = bf16[4,64,1536]{2,1,0:T(8,128)(2,1)S(1)} all-to-all(bf16[4,64,1536]{2,1,0:T(8,128)(2,1)} %bitcast.76), channel_id=1, replica_groups=mesh['fsdp'=2,'context'=4,'tensor'=4] {'tensor'}, dimensions={0} | all-to-all | bytes 1572864 | tf_op jit(solution)/shard_map/all_to_all | solution.py:84
  287.0 11.1 %all_to_all.92 = bf16[4,64,1536]{2,1,0:T(8,128)(2,1)S(1)} all-to-all(bf16[4,64,1536]{2,1,0:T(8,128)(2,1)S(1)} %broadcast_in_dim.32), channel_id=1, replica_groups=mesh['fsdp'=2,'context'=4,'tensor'=4] {'tensor'}, dimensions={0} | all-to-all | bytes 1572864 | tf_op jit(solution)/shard_map/all_to_all | solution.py:48
  302.7 12.1 %collective-permute-done.33.refs_7_ = bf16[64,1536]{1,0:T(8,128)(2,1)S(1)} collective-permute-done((bf16[64,1536]{1,0:T(8,128)(2,1)S(1)}, bf16[64,1536]{1,0:T(8,128)(2,1)S(1)}, u32[]{:S(2)}, u32[]{:S(2)}) %collective-permute-start.33) | collective-permute-done | bytes 196640 | tf_op jit(solution)/shard_map/ppermute | solution.py:25
  330.1 33.6 %shard_map.265 = (bf16[1024,1536]{1,0:T(8,128)(2,1)}, bf16[1024,384]{1,0:T(8,128)(2,1)}, bf16[1024,384]{1,0:T(8,128)(2,1)}, bf16[1024,384]{1,0:T(8,128)(2,1)}, b...) custom-call(s32[2]{0:T(128)} %pad_add_fusion.refs_0_, ...), custom_call_target="tpu_custom_call" | custom-call | flops 36300001280 | tf_op jit(solution)/shard_map/pallas_call | solution.py:615
  368.0 7.2 %all-to-all-done.9 = bf16[4,64,1536]{2,1,0:T(8,128)(2,1)S(1)} async-done(((bf16[4,64,1536]{2,1,0:T(8,128)(2,1)}), bf16[4,64,1536]{2,1,0:T(8,128)(2,1)S(1)}, u32[]{:S(2)}, u32[]{:S(2)}) %all-to-all-start.9) | async-done | bytes 786464 | tf_op jit(solution)/shard_map/all_to_all | solution.py:84
  381.3 8.5 %shard_map.266 = (bf16[768,384]{1,0:T(8,128)(2,1)}, bf16[768,384]{1,0:T(8,128)(2,1)}, bf16[768,384]{1,0:T(8,128)(2,1)}, bf16[768,384]{1,0:T(8,128)(2,1)}, bf16[7...) custom-call(bf16[1024,1536]{1,0:T(8,128)(2,1)} %get-tuple-element.117.refs_0_, ...), custom_call_target="tpu_custom_call" | custom-call | flops 7699999744 | tf_op jit(solution)/shard_map/pallas_call | solution.py:748
  392.7 9.3 %shard_map.267.refs_0_ = bf16[256,1536]{1,0:T(8,128)(2,1)} custom-call(bf16[256,1536]{1,0:T(8,128)(2,1)} %bitcast.69, f32[256,1024]{1,0:T(8,128)} %get-tuple-element.115.gt_ref, f32[256,1024]{1,0:T(8,128)} %get-tuple-element.116.up_ref, bf16[2,768,1024]{2,1,0:T(8,128)(2,1)} %wg.11, bf16[2,768,1024]{2,1,0:T(8,128)(2,1)} %wu.11, bf16[2,1024,768]{2,1,0:T(8,128)(2,1)} %wd.11, ...), custom_call_target="tpu_custom_call" | custom-call | flops 8800000000 | tf_op jit(solution)/shard_map/pallas_call | solution.py:666
  407.2 9.5 %shard_map.270 = (f32[2,768,384]{2,1,0:T(8,128)}, f32[2,768,384]{2,1,0:T(8,128)}, f32[2,768,384]{2,1,0:T(8,128)}, f32[2,768,384]{2,1,0:T(8,128)}, f32[768,128]{1,0:T(8,128)}, /*index=5*/f32[2,384,768]{2,1,0:T(8,128)}) custom-call(bf16[1024,1536]{1,0:T(8,128)(2,1)} %get-tuple-element.11, ...), custom_call_target="tpu_custom_call", output_to_operand_aliasing={{0}: (14, {}), {1}: (15, {}), {2}: (16, {}), {3}: (17, {}),... | custom-call | flops 7699999744 | tf_op jit(solution)/shard_map/pallas_call | solution.py:748
  431.5 8.1 %collective-permute-done.45.refs_1_ = bf16[64,1536]{1,0:T(8,128)(2,1)S(1)} collective-permute-done((bf16[64,1536]{1,0:T(8,128)(2,1)S(1)}, bf16[64,1536]{1,0:T(8,128)(2,1)S(1)}, u32[]{:S(2)}, u32[]{:S(2)}) %collective-permute-start.45) | collective-permute-done | bytes 196640 | tf_op jit(solution)/shard_map/ppermute | solution.py:25
  439.6 12.5 %collective-permute-done.44.refs_0_ = bf16[64,1536]{1,0:T(8,128)(2,1)S(1)} collective-permute-done((bf16[64,1536]{1,0:T(8,128)(2,1)S(1)}, bf16[64,1536]{1,0:T(8,128)(2,1)S(1)}, u32[]{:S(2)}, u32[]{:S(2)}) %collective-permute-start.44) | collective-permute-done | bytes 196640 | tf_op jit(solution)/shard_map/ppermute | solution.py:25
  460.2 21.0 %shard_map.274 = (bf16[1024,1024]{1,0:T(8,128)(2,1)}, bf16[1024,1024]{1,0:T(8,128)(2,1)}, bf16[1024,1024]{1,0:T(8,128)(2,1)}, bf16[768,1024]{1,0:T(8,128)(2,1)},...) custom-call(bf16[1024,1536]{1,0:T(8,128)(2,1)} %all-gather.9.cloned.1.call-done.b_ref, ...), custom_call_target="tpu_custom_call" | custom-call | flops 26400000000 | tf_op jit(solution)/shard_map/pallas_call | solution.py:683
  482.5 33.6 %shard_map.276 = (bf16[1024,1536]{1,0:T(8,128)(2,1)}, bf16[1024,384]{1,0:T(8,128)(2,1)}, bf16[1024,384]{1,0:T(8,128)(2,1)}, bf16[1024,384]{1,0:T(8,128)(2,1)}, b...) custom-call(s32[2]{0:T(128)} %pad_add_fusion.refs_0_, ...), custom_call_target="tpu_custom_call" | custom-call | flops 36300001280 | tf_op jit(solution)/shard_map/pallas_call | solution.py:615
  521.1 8.6 %shard_map.281 = (bf16[768,384]{1,0:T(8,128)(2,1)}, bf16[768,384]{1,0:T(8,128)(2,1)}, bf16[768,384]{1,0:T(8,128)(2,1)}, bf16[768,384]{1,0:T(8,128)(2,1)}, bf16[7...) custom-call(bf16[1024,1536]{1,0:T(8,128)(2,1)} %get-tuple-element.146.refs_0_, ...), custom_call_target="tpu_custom_call" | custom-call | flops 7699999744 | tf_op jit(solution)/shard_map/pallas_call | solution.py:748
  542.9 12.0 %shard_map.283 = (f32[2,768,1024]{2,1,0:T(8,128)}, f32[2,768,1024]{2,1,0:T(8,128)}, f32[2,1024,768]{2,1,0:T(8,128)}) custom-call(bf16[1024,1536]{1,0:T(8,128)(2,1)} %all-gather.9.cloned.1.call-done.b_ref, bf16[1024,1536]{1,0:T(8,128)(2,1)} %all-gather.5.cloned.1.call-done.refs_1_.g_ref, ...), custom_call_target="tpu_custom_call", output_to_operand_aliasing={{0}: (8, {}), {1}: (9, {}), {2}: (10, {})} | custom-call | flops 9900000256 | tf_op jit(solution)/shard_map/pallas_call | solution.py:708
  573.2 21.4 %shard_map.279 = (bf16[1024,1024]{1,0:T(8,128)(2,1)}, bf16[1024,1024]{1,0:T(8,128)(2,1)}, bf16[1024,1024]{1,0:T(8,128)(2,1)}, bf16[768,1024]{1,0:T(8,128)(2,1)},...) custom-call(bf16[1024,1536]{1,0:T(8,128)(2,1)} %all-gather.7.cloned.1.call-done.refs_1_.b_ref, ...), custom_call_target="tpu_custom_call" | custom-call | flops 26400000000 | tf_op jit(solution)/shard_map/pallas_call | solution.py:683
  596.4 9.5 %shard_map.285 = (f32[2,768,384]{2,1,0:T(8,128)}, f32[2,768,384]{2,1,0:T(8,128)}, f32[2,768,384]{2,1,0:T(8,128)}, f32[2,768,384]{2,1,0:T(8,128)}, f32[768,128]{1,0:T(8,128)}, /*index=5*/f32[2,384,768]{2,1,0:T(8,128)}) custom-call(bf16[1024,1536]{1,0:T(8,128)(2,1)} %get-tuple-element.14, ...), custom_call_target="tpu_custom_call", output_to_operand_aliasing={{0}: (14, {}), {1}: (15, {}), {2}: (16, {}), {3}: (17, {}),... | custom-call | flops 7699999744 | tf_op jit(solution)/shard_map/pallas_call | solution.py:748
  607.1 7.4 %all-reduce.4.cloned.1.call-done.refs_0_ = bf16[256,1536]{1,0:T(8,128)(2,1)} async-done(((bf16[256,1536]{1,0:T(8,128)(2,1)}), bf16[256,1536]{1,0:T(8,128)(2,1)}) %all-reduce.4.cloned.1.call-update) | async-done | bytes 786448 | tf_op jit(solution)/shard_map/psum | solution.py:943
  617.4 11.8 %shard_map.286 = (f32[2,768,1024]{2,1,0:T(8,128)}, f32[2,768,1024]{2,1,0:T(8,128)}, f32[2,1024,768]{2,1,0:T(8,128)}) custom-call(bf16[1024,1536]{1,0:T(8,128)(2,1)} %all-gather.7.cloned.1.call-done.refs_1_.b_ref, bf16[1024,1536]{1,0:T(8,128)(2,1)} %all-gather.11.cloned.1.call-done.g_ref, ...), custom_call_target="tpu_custom_call", output_to_operand_aliasing={{0}: (8, {}), {1}: (9, {}), {2}: (10, {})} | custom-call | flops 9900000256 | tf_op jit(solution)/shard_map/pallas_call | solution.py:708
  (406 shorter events, 167.6 us)
Async XLA Ops:
  11.4 59.1 %collective-permute-start.1 = (bf16[256,1536]{1,0:T(8,128)(2,1)S(1)}, bf16[256,1536]{1,0:T(8,128)(2,1)}, u32[]{:S(2)}, u32[]{:S(2)}) collective-permute-start(bf16[256,1536]{1,0:T(8,128)(2,1)S(1)} %multiply_convert_fusion.refs_1_), channel_id=1, source_target_pairs={{0,4},{4,0},{8,12},{12,8},{1,5},{5,1},{9,13},{13,9},{2,6},{6,2},{1... | collective-permute-start | bytes 2359304 | tf_op jit(solution)/shard_map/ppermute | solution.py:25
  14.1 25.1 %collective-permute-start.6 = (bf16[64,1536]{1,0:T(8,128)(2,1)S(1)}, bf16[64,1536]{1,0:T(8,128)(2,1)}, u32[]{:S(2)}, u32[]{:S(2)}) collective-permute-start(bf16[64,1536]{1,0:T(8,128)(2,1)S(1)} %constant_dynamic-slice_fusion), channel_id=1, source_target_pairs={{0,12},{4,8},{8,4},{12,0},{1,13},{5,9},{9,5},{13,1},{2,14},{6,10},... | collective-permute-start | bytes 589832 | tf_op jit(solution)/shard_map/ppermute | solution.py:25
  16.6 36.3 %collective-permute-start.2 = (bf16[64,1536]{1,0:T(8,128)(2,1)S(1)}, bf16[64,1536]{1,0:T(8,128)(2,1)S(1)}, u32[]{:S(2)}, u32[]{:S(2)}) collective-permute-start(bf16[64,1536]{1,0:T(8,128)(2,1)S(1)} %constant_dynamic-slice_fusion), channel_id=1, source_target_pairs={{0,8},{4,12},{8,0},{12,4},{1,9},{5,13},{9,1},{13,5},{2,10},{6,14},... | collective-permute-start | bytes 589832 | tf_op jit(solution)/shard_map/ppermute | solution.py:25
  47.3 105.1 %all-gather.5.cloned.1.call-start = ((), (), s32[]{:S(2)}) async-start(), calls=%async_computation.17 | async-start | bytes 3932160 | tf_op jit(solution)/shard_map/all_gather | solution.py:846
  77.5 208.4 %all-gather.7.cloned.1.call-start = ((), (), s32[]{:S(2)}) async-start(), calls=%async_computation.18 | async-start | bytes 3342336 | tf_op jit(solution)/shard_map/all_gather | solution.py:52
  77.6 51.8 %collective-permute-start.16 = (bf16[2,768,1024]{2,1,0:T(8,128)(2,1)}, bf16[2,768,1024]{2,1,0:T(8,128)(2,1)}, u32[]{:S(2)}, u32[]{:S(2)}) collective-permute-start(bf16[2,768,1024]{2,1,0:T(8,128)(2,1)} %wg.11), channel_id=1, source_target_pairs={{0,16},{16,0},{1,17},{17,1},{2,18},{18,2},{3,19},{19,3},{4,20},{20... | collective-permute-start | bytes 9437192 | tf_op jit(solution)/shard_map/ppermute | solution.py:25
  78.1 51.3 %collective-permute-start.17 = (bf16[2,768,1024]{2,1,0:T(8,128)(2,1)}, bf16[2,768,1024]{2,1,0:T(8,128)(2,1)}, u32[]{:S(2)}, u32[]{:S(2)}) collective-permute-start(bf16[2,768,1024]{2,1,0:T(8,128)(2,1)} %wu.11), channel_id=1, source_target_pairs={{0,16},{16,0},{1,17},{17,1},{2,18},{18,2},{3,19},{19,3},{4,20},{20... | collective-permute-start | bytes 9437192 | tf_op jit(solution)/shard_map/ppermute | solution.py:25
  78.2 51.2 %collective-permute-start.18 = (bf16[2,1024,768]{2,1,0:T(8,128)(2,1)}, bf16[2,1024,768]{2,1,0:T(8,128)(2,1)}, u32[]{:S(2)}, u32[]{:S(2)}) collective-permute-start(bf16[2,1024,768]{2,1,0:T(8,128)(2,1)} %wd.11), channel_id=1, source_target_pairs={{0,16},{16,0},{1,17},{17,1},{2,18},{18,2},{3,19},{19,3},{4,20},{20... | collective-permute-start | bytes 9437192 | tf_op jit(solution)/shard_map/ppermute | solution.py:25
  164.5 34.7 %collective-permute-start.19 = (bf16[256,1536]{1,0:T(8,128)(2,1)S(1)}, bf16[256,1536]{1,0:T(8,128)(2,1)S(1)}, u32[]{:S(2)}, u32[]{:S(2)}) collective-permute-start(bf16[256,1536]{1,0:T(8,128)(2,1)S(1)} %bitcast.67), channel_id=1, source_target_pairs={{0,4},{4,0},{8,12},{12,8},{1,5},{5,1},{9,13},{13,9},{2,6},{6,2},{1... | collective-permute-start | bytes 2359304 | tf_op jit(solution)/shard_map/ppermute | solution.py:25
  164.8 19.9 %collective-permute-start.24 = (bf16[64,1536]{1,0:T(8,128)(2,1)S(1)}, bf16[64,1536]{1,0:T(8,128)(2,1)S(1)}, u32[]{:S(2)}, u32[]{:S(2)}) collective-permute-start(bf16[64,1536]{1,0:T(8,128)(2,1)S(1)} %copy-done.13), channel_id=1, source_target_pairs={{0,12},{4,8},{8,4},{12,0},{1,13},{5,9},{9,5},{13,1},{2,14},{6,10},... | collective-permute-start | bytes 589832 | tf_op jit(solution)/shard_map/ppermute | solution.py:25
  165.9 22.4 %collective-permute-start.20 = (bf16[64,1536]{1,0:T(8,128)(2,1)S(1)}, bf16[64,1536]{1,0:T(8,128)(2,1)S(1)}, u32[]{:S(2)}, u32[]{:S(2)}) collective-permute-start(bf16[64,1536]{1,0:T(8,128)(2,1)S(1)} %copy-done.13), channel_id=1, source_target_pairs={{0,8},{4,12},{8,0},{12,4},{1,9},{5,13},{9,1},{13,5},{2,10},{6,14},... | collective-permute-start | bytes 589832 | tf_op jit(solution)/shard_map/ppermute | solution.py:25
  298.2 30.9 %collective-permute-start.28 = (bf16[256,1536]{1,0:T(8,128)(2,1)S(1)}, bf16[256,1536]{1,0:T(8,128)(2,1)S(1)}, u32[]{:S(2)}, u32[]{:S(2)}) collective-permute-start(bf16[256,1536]{1,0:T(8,128)(2,1)S(1)} %bitcast.57), channel_id=1, source_target_pairs={{0,4},{4,0},{8,12},{12,8},{1,5},{5,1},{9,13},{13,9},{2,6},{6,2},{1... | collective-permute-start | bytes 2359304 | tf_op jit(solution)/shard_map/ppermute | solution.py:25
  367.3 92.9 %all-gather.9.cloned.1.call-start = ((), (), s32[]{:S(2)}) async-start(), calls=%async_computation.19 | async-start | bytes 3342336 | tf_op jit(solution)/shard_map/all_gather | solution.py:52
  403.0 17.0 %all-to-all-start.11 = ((bf16[4,64,1536]{2,1,0:T(8,128)(2,1)}), bf16[4,64,1536]{2,1,0:T(8,128)(2,1)S(1)}, u32[]{:S(2)}, u32[]{:S(2)}) async-start(bf16[4,64,1536]{2,1,0:T(8,128)(2,1)} %bitcast.60), calls=%async_computation.11 | async-start | bytes 1572864 | tf_op jit(solution)/shard_map/all_to_all | solution.py:84
  423.2 29.7 %all-to-all-start.12 = ((bf16[4,64,1536]{2,1,0:T(8,128)(2,1)}), bf16[4,64,1536]{2,1,0:T(8,128)(2,1)S(1)}, u32[]{:S(2)}, u32[]{:S(2)}) async-start(bf16[4,64,1536]{2,1,0:T(8,128)(2,1)} %broadcast_in_dim.34), calls=%async_computation.12 | async-start | bytes 1572864 | tf_op jit(solution)/shard_map/all_to_all | solution.py:48
  428.7 23.4 %collective-permute-start.44 = (bf16[64,1536]{1,0:T(8,128)(2,1)S(1)}, bf16[64,1536]{1,0:T(8,128)(2,1)S(1)}, u32[]{:S(2)}, u32[]{:S(2)}) collective-permute-start(bf16[64,1536]{1,0:T(8,128)(2,1)S(1)} %copy-done.14), channel_id=1, source_target_pairs={{0,8},{4,12},{8,0},{12,4},{1,9},{5,13},{9,1},{13,5},{2,10},{6,14},... | collective-permute-start | bytes 589832 | tf_op jit(solution)/shard_map/ppermute | solution.py:25
  452.9 28.4 %collective-permute-start.43 = (bf16[256,1536]{1,0:T(8,128)(2,1)S(1)}, bf16[256,1536]{1,0:T(8,128)(2,1)}, u32[]{:S(2)}, u32[]{:S(2)}) collective-permute-start(bf16[256,1536]{1,0:T(8,128)(2,1)S(1)} %bitcast.61), channel_id=1, source_target_pairs={{0,4},{4,0},{8,12},{12,8},{1,5},{5,1},{9,13},{13,9},{2,6},{6,2},{1... | collective-permute-start | bytes 2359304 | tf_op jit(solution)/shard_map/ppermute | solution.py:25
  456.0 25.3 %all-to-all-start.13 = ((bf16[4,128,1536]{2,1,0:T(8,128)(2,1)}), bf16[4,128,1536]{2,1,0:T(8,128)(2,1)S(1)}, u32[]{:S(2)}, u32[]{:S(2)}) async-start(bf16[4,128,1536]{2,1,0:T(8,128)(2,1)} %broadcast_in_dim.35), calls=%async_computation.13 | async-start | bytes 3145728 | tf_op jit(solution)/shard_map/all_to_all | solution.py:48
  460.0 113.2 %all-gather.11.cloned.1.call-start = ((), (), s32[]{:S(2)}) async-start(), calls=%async_computation.21 | async-start | bytes 3342336 | tf_op jit(solution)/shard_map/all_gather | solution.py:52
  516.0 19.4 %all-to-all-start.14 = ((bf16[4,64,1536]{2,1,0:T(8,128)(2,1)}), bf16[4,64,1536]{2,1,0:T(8,128)(2,1)S(1)}, u32[]{:S(2)}, u32[]{:S(2)}) async-start(bf16[4,64,1536]{2,1,0:T(8,128)(2,1)} %bitcast.55), calls=%async_computation.14 | async-start | bytes 1572864 | tf_op jit(solution)/shard_map/all_to_all | solution.py:84
  520.5 22.4 %collective-permute-start.52 = (bf16[768,1024]{1,0:T(8,128)(2,1)}, bf16[768,1024]{1,0:T(8,128)(2,1)}, u32[]{:S(2)}, u32[]{:S(2)}) collective-permute-start(bf16[768,1024]{1,0:T(8,128)(2,1)} %get-tuple-element.166), channel_id=1, source_target_pairs={{0,16},{16,0},{1,17},{17,1},{2,18},{18,2},{3,19},{19,3},{4,20},{20... | collective-permute-start | bytes 4718600 | tf_op jit(solution)/shard_map/ppermute | solution.py:25
  520.5 22.3 %collective-permute-start.53 = (bf16[768,1024]{1,0:T(8,128)(2,1)}, bf16[768,1024]{1,0:T(8,128)(2,1)}, u32[]{:S(2)}, u32[]{:S(2)}) collective-permute-start(bf16[768,1024]{1,0:T(8,128)(2,1)} %get-tuple-element.167), channel_id=1, source_target_pairs={{0,16},{16,0},{1,17},{17,1},{2,18},{18,2},{3,19},{19,3},{4,20},{20... | collective-permute-start | bytes 4718600 | tf_op jit(solution)/shard_map/ppermute | solution.py:25
  521.0 21.8 %collective-permute-start.54 = (bf16[1024,768]{1,0:T(8,128)(2,1)}, bf16[1024,768]{1,0:T(8,128)(2,1)}, u32[]{:S(2)}, u32[]{:S(2)}) collective-permute-start(bf16[1024,768]{1,0:T(8,128)(2,1)} %get-tuple-element.168), channel_id=1, source_target_pairs={{0,16},{16,0},{1,17},{17,1},{2,18},{18,2},{3,19},{19,3},{4,20},{20... | collective-permute-start | bytes 4718600 | tf_op jit(solution)/shard_map/ppermute | solution.py:25
  560.8 53.7 %all-reduce.4.cloned.1.call-start = ((), (), s32[]{:S(2)}) async-start(), calls=%async_computation.20 | async-start | bytes 1572864 | tf_op jit(solution)/shard_map/psum | solution.py:943
  561.1 34.5 %collective-permute-start.46 = (bf16[768,384]{1,0:T(8,128)(2,1)S(1)}, bf16[768,384]{1,0:T(8,128)(2,1)}, u32[]{:S(2)}, u32[]{:S(2)}) collective-permute-start(bf16[768,384]{1,0:T(8,128)(2,1)S(1)} %copy-done.24), channel_id=1, source_target_pairs={{0,16},{16,0},{1,17},{17,1},{2,18},{18,2},{3,19},{19,3},{4,20},{20... | collective-permute-start | bytes 1769480 | tf_op jit(solution)/shard_map/ppermute | solution.py:25
  562.6 32.0 %collective-permute-start.47 = (bf16[768,384]{1,0:T(8,128)(2,1)}, bf16[768,384]{1,0:T(8,128)(2,1)}, u32[]{:S(2)}, u32[]{:S(2)}) collective-permute-start(bf16[768,384]{1,0:T(8,128)(2,1)} %get-tuple-element.155), channel_id=1, source_target_pairs={{0,16},{16,0},{1,17},{17,1},{2,18},{18,2},{3,19},{19,3},{4,20},{20... | collective-permute-start | bytes 1769480 | tf_op jit(solution)/shard_map/ppermute | solution.py:25
  562.7 32.4 %collective-permute-start.48 = (bf16[768,384]{1,0:T(8,128)(2,1)}, bf16[768,384]{1,0:T(8,128)(2,1)}, u32[]{:S(2)}, u32[]{:S(2)}) collective-permute-start(bf16[768,384]{1,0:T(8,128)(2,1)} %get-tuple-element.156), channel_id=1, source_target_pairs={{0,16},{16,0},{1,17},{17,1},{2,18},{18,2},{3,19},{19,3},{4,20},{20... | collective-permute-start | bytes 1769480 | tf_op jit(solution)/shard_map/ppermute | solution.py:25
  572.0 23.2 %collective-permute-start.49 = (bf16[768,384]{1,0:T(8,128)(2,1)}, bf16[768,384]{1,0:T(8,128)(2,1)S(1)}, u32[]{:S(2)}, u32[]{:S(2)}) collective-permute-start(bf16[768,384]{1,0:T(8,128)(2,1)} %get-tuple-element.157), channel_id=1, source_target_pairs={{0,16},{16,0},{1,17},{17,1},{2,18},{18,2},{3,19},{19,3},{4,20},{20... | collective-permute-start | bytes 1769480 | tf_op jit(solution)/shard_map/ppermute | solution.py:25
  573.0 22.6 %collective-permute-start.51 = (bf16[384,768]{1,0:T(8,128)(2,1)S(1)}, bf16[384,768]{1,0:T(8,128)(2,1)S(1)}, u32[]{:S(2)}, u32[]{:S(2)}) collective-permute-start(bf16[384,768]{1,0:T(8,128)(2,1)S(1)} %copy-done.65), channel_id=1, source_target_pairs={{0,16},{16,0},{1,17},{17,1},{2,18},{18,2},{3,19},{19,3},{4,20},{20... | collective-permute-start | bytes 1769480 | tf_op jit(solution)/shard_map/ppermute | solution.py:25
  594.6 22.8 %collective-permute-start.58 = (bf16[768,1024]{1,0:T(8,128)(2,1)}, bf16[768,1024]{1,0:T(8,128)(2,1)}, u32[]{:S(2)}, u32[]{:S(2)}) collective-permute-start(bf16[768,1024]{1,0:T(8,128)(2,1)} %get-tuple-element.182), channel_id=1, source_target_pairs={{0,16},{16,0},{1,17},{17,1},{2,18},{18,2},{3,19},{19,3},{4,20},{20... | collective-permute-start | bytes 4718600 | tf_op jit(solution)/shard_map/ppermute | solution.py:25
  595.1 22.3 %collective-permute-start.59 = (bf16[768,1024]{1,0:T(8,128)(2,1)}, bf16[768,1024]{1,0:T(8,128)(2,1)}, u32[]{:S(2)}, u32[]{:S(2)}) collective-permute-start(bf16[768,1024]{1,0:T(8,128)(2,1)} %get-tuple-element.183), channel_id=1, source_target_pairs={{0,16},{16,0},{1,17},{17,1},{2,18},{18,2},{3,19},{19,3},{4,20},{20... | collective-permute-start | bytes 4718600 | tf_op jit(solution)/shard_map/ppermute | solution.py:25
  595.2 22.2 %collective-permute-start.60 = (bf16[1024,768]{1,0:T(8,128)(2,1)}, bf16[1024,768]{1,0:T(8,128)(2,1)}, u32[]{:S(2)}, u32[]{:S(2)}) collective-permute-start(bf16[1024,768]{1,0:T(8,128)(2,1)} %get-tuple-element.184), channel_id=1, source_target_pairs={{0,16},{16,0},{1,17},{17,1},{2,18},{18,2},{3,19},{19,3},{4,20},{20... | collective-permute-start | bytes 4718600 | tf_op jit(solution)/shard_map/ppermute | solution.py:25
  (121 other events, 1289.4 us)
Sparse Core Ops, SparseCore 0:
  77.6 60.1 all-gather.4
  195.5 71.6 all-gather.6
  370.9 81.9 all-gather.8
  481.4 69.4 all-gather.10
  564.4 50.0 all-reduce.3

commit v14 on v13

--- a/solution.py
+++ b/solution.py
@@ -56,23 +56,23 @@
     return swap(own, "context", 1)
 
 
-def far_blocks(shard):
+def far_blocks(shard, *tokens):
+    shard = after(shard, *tokens)
     return swap(shard, "context", 2), swap(shard, "context", 3)
 
 
-def all_rows(shard, own=None, token=None, together=False):
+def all_rows(shard, own=None, first=(), second_stage=(), together=False):
     if own is None:
         own = gathered(shard, "tensor")
     if lax.axis_size("context") != 4:
         return (lax.all_gather(own, "context", tiled=True),), ()
-    second, third = far_blocks(shard)
+    second, third = far_blocks(shard, *first)
     near = near_rows(own)
     if together:
         block, width = shard.shape
         far = gathered(after(jnp.concatenate([second, third], axis=0), own), "tensor")
         return (own, near, far.reshape(-1, 2, block, width)), (second, third)
-    if token is not None:
-        second = after(second, token)
+    second = after(second, *second_stage)
     parts = [own, near]
     for far in (second, third):
         parts += [far] + [swap(far, "tensor", k) for k in range(1, lax.axis_size("tensor"))]
@@ -810,10 +810,13 @@
     gains = full(jnp.concatenate([gain_attn, gain_ffn], axis=0), 1).astype(f32)
     hidden_rows = features(hidden_in.reshape(piece_len, width)).astype(f32)
     first_a = (hidden_rows * inverse_rms(hidden_rows) * gains[0]).astype(bf16)
-    a_parts, a_far = all_rows(own_block(first_a), first_a, seg_all)
-
     w_forget_full = jnp.pad(full(w_forget, 1), ((0, 0), (0, 0), (0, pair_lanes - heads)))
+    w_forget_full = [w_forget_full[layer] for layer in range(layers)]
     bias = jnp.pad(b_forget, ((0, 0), (0, pair_lanes - heads)))
+    bias = [bias[layer : layer + 1] for layer in range(layers)]
+    a_parts, a_far = all_rows(
+        own_block(first_a), first_a, (seg_all,), (doc_start, w_forget_full[0], bias[0], place)
+    )
     w4 = (w_query, w_key, w_value, w_gate_out)
     t4 = tuple(other(w) for w in w4)
     to = other(w_attn_out)
@@ -840,7 +843,7 @@
             forget_weights = after(forget_weights, b_sent)
         a, (q, k, v, gate, forget, terms), sends = forward_own(
             place, a_parts, layer, w4, t4, w_attn_out, to, forget_weights,
-            bias[layer : layer + 1], doc_start, piece_len,
+            bias[layer], doc_start, piece_len,
         )
         if shared_rows and layer == 0:
             g_last = lax.all_gather(after(cotangent_rows, *a_far), "context", tiled=True)

time: 646 us -> 641 us (level)
  waiting for transfers between devices: 137 us -> 126 us
  transfers between devices with their start and end apart: 75 -> 75, of which waited for: 27 -> 30; matrix products, arithmetic and copies ran while one was open for 6% -> 7% of each run, Pallas kernels for 31% -> 31%
where the time goes in v14:
time: 641 us; the launch traced here: 631 us
  Pallas kernels  244 us (38%)
  waiting for transfers between devices  126 us (20%)
  blocking collectives  111 us (17%)
  starting transfers between devices  81.1 us (13%)
  local copies, waits for them, and re-layouts  34.2 us (5%)
  other arithmetic  19.7 us (3%)
  between operations  15.4 us (2%)
    ppermute x61, waiting for transfers between devices, swap(): return lax.ppermute(x, axis, [(i, i ^ k) for i in range(n)])  95.2 us
    pallas_call x2, Pallas kernels, attention_backward(): pl.pallas_call(functools.partial(backward_kernel, len(parts), piece_len,...  67.2 us
    all_to_all x4, blocking collectives, received_sum(): lax.all_to_all(sends.reshape(count, -1, sends.shape[1]), 'tensor', 0, 0,...  58.8 us
    all_to_all x4, blocking collectives, gathered(): lax.all_to_all(copies, axis, 0, 0, tiled=True)  52 us
    ppermute x61, starting transfers between devices, swap(): return lax.ppermute(x, axis, [(i, i ^ k) for i in range(n)])  43.8 us
    pallas_call x2, Pallas kernels, ffn_theirs(): pl.pallas_call(ffn_theirs_kernel, grid=(inner // hidden_block,), in_specs...  42.4 us
    pallas_call x2, Pallas kernels, forward_own(): pl.pallas_call(functools.partial(forward_own_kernel, len(parts), piece_le...  38.9 us
    pallas_call x4, Pallas kernels, attention_grads(): pl.pallas_call(functools.partial(attention_grads_kernel, steps, mine), gr...  36.1 us
  transfers between devices with their start and end apart: 75, of which 30 were waited for; matrix products, arithmetic and copies ran while one was open for 7% of the time, Pallas kernels for 31%

profile of v14, /device:TPU:0, one launch (start us, length us, event | category | flops | bytes accessed | tf_op | source)
XLA Modules:
  0.0 631.5 jit_solution(9785237101051441156)
XLA Ops:
  29.8 18.9 %collective-permute-done.7.refs_7_.refs_2_ = bf16[64,1536]{1,0:T(8,128)(2,1)S(1)} collective-permute-done((bf16[64,1536]{1,0:T(8,128)(2,1)}, bf16[64,1536]{1,0:T(8,128)(2,1)S(1)}, u32[]{:S(2)}, u32[]{:S(2)}) %collective-permute-start.7) | collective-permute-done | bytes 196640 | tf_op jit(solution)/shard_map/ppermute | solution.py:25
  74.9 19.7 %shard_map.256 = (bf16[1024,1536]{1,0:T(8,128)(2,1)}, bf16[1024,384]{1,0:T(8,128)(2,1)}, bf16[1024,384]{1,0:T(8,128)(2,1)}, bf16[1024,384]{1,0:T(8,128)(2,1)}, f...) custom-call(s32[2]{0:T(128)} %pad_add_fusion.refs_4_.refs_0_, ...), custom_call_target="tpu_custom_call" | custom-call | flops 20899999744 | tf_op jit(solution)/shard_map/pallas_call | solution.py:585
  94.6 15.4 %all_to_all.85 = bf16[4,64,1536]{2,1,0:T(8,128)(2,1)S(1)} all-to-all(bf16[4,64,1536]{2,1,0:T(8,128)(2,1)} %bitcast.72), channel_id=1, replica_groups=mesh['fsdp'=2,'context'=4,'tensor'=4] {'tensor'}, dimensions={0} | all-to-all | bytes 1572864 | tf_op jit(solution)/shard_map/all_to_all | solution.py:84
  111.0 13.9 %all_to_all.86 = bf16[4,64,1536]{2,1,0:T(8,128)(2,1)} all-to-all(bf16[4,64,1536]{2,1,0:T(8,128)(2,1)S(1)} %broadcast_in_dim.29), channel_id=1, replica_groups=mesh['fsdp'=2,'context'=4,'tensor'=4] {'tensor'}, dimensions={0} | all-to-all | bytes 1572864 | tf_op jit(solution)/shard_map/all_to_all | solution.py:48
  124.9 8.4 %shard_map.257 = (f32[256,1024]{1,0:T(8,128)}, f32[256,1024]{1,0:T(8,128)}, bf16[256,1536]{1,0:T(8,128)(2,1)}) custom-call(bf16[256,1536]{1,0:T(8,128)(2,1)} %bitcast.73, bf16[2,768,1024]{2,1,0:T(8,128)(2,1)} %wg.11, bf16[2,768,1024]{2,1,0:T(8,128)(2,1)} %wu.11, bf16[2,1024,768]{2,1,0:T(8,128)(2,1)} %wd.11, ...), custom_call_target="tpu_custom_call" | custom-call | flops 7699999744 | tf_op jit(solution)/shard_map/pallas_call | solution.py:652
  133.4 13.0 %all_to_all.87 = bf16[4,64,1536]{2,1,0:T(8,128)(2,1)S(1)} all-to-all(bf16[4,64,1536]{2,1,0:T(8,128)(2,1)} %bitcast.74), channel_id=1, replica_groups=mesh['fsdp'=2,'context'=4,'tensor'=4] {'tensor'}, dimensions={0} | all-to-all | bytes 1572864 | tf_op jit(solution)/shard_map/all_to_all | solution.py:84
  149.0 11.1 %all_to_all.88 = bf16[4,64,1536]{2,1,0:T(8,128)(2,1)S(1)} all-to-all(bf16[4,64,1536]{2,1,0:T(8,128)(2,1)S(1)} %broadcast_in_dim.30), channel_id=1, replica_groups=mesh['fsdp'=2,'context'=4,'tensor'=4] {'tensor'}, dimensions={0} | all-to-all | bytes 1572864 | tf_op jit(solution)/shard_map/all_to_all | solution.py:48
  163.6 16.8 %collective-permute-done.24.refs_7_ = bf16[64,1536]{1,0:T(8,128)(2,1)S(1)} collective-permute-done((bf16[64,1536]{1,0:T(8,128)(2,1)S(1)}, bf16[64,1536]{1,0:T(8,128)(2,1)S(1)}, u32[]{:S(2)}, u32[]{:S(2)}) %collective-permute-start.24) | collective-permute-done | bytes 196640 | tf_op jit(solution)/shard_map/ppermute | solution.py:25
  195.7 19.3 %shard_map.262 = (bf16[1024,1536]{1,0:T(8,128)(2,1)}, bf16[1024,384]{1,0:T(8,128)(2,1)}, bf16[1024,384]{1,0:T(8,128)(2,1)}, bf16[1024,384]{1,0:T(8,128)(2,1)}, f...) custom-call(s32[2]{0:T(128)} %pad_add_fusion.refs_4_.refs_0_, ...), custom_call_target="tpu_custom_call" | custom-call | flops 20899999744 | tf_op jit(solution)/shard_map/pallas_call | solution.py:585
  215.0 17.9 %all_to_all.89 = bf16[4,64,1536]{2,1,0:T(8,128)(2,1)S(1)} all-to-all(bf16[4,64,1536]{2,1,0:T(8,128)(2,1)} %bitcast.71), channel_id=1, replica_groups=mesh['fsdp'=2,'context'=4,'tensor'=4] {'tensor'}, dimensions={0} | all-to-all | bytes 1572864 | tf_op jit(solution)/shard_map/all_to_all | solution.py:84
  233.4 15.8 %all_to_all.90 = bf16[4,64,1536]{2,1,0:T(8,128)(2,1)} all-to-all(bf16[4,64,1536]{2,1,0:T(8,128)(2,1)S(1)} %broadcast_in_dim.31), channel_id=1, replica_groups=mesh['fsdp'=2,'context'=4,'tensor'=4] {'tensor'}, dimensions={0} | all-to-all | bytes 1572864 | tf_op jit(solution)/shard_map/all_to_all | solution.py:48
  249.2 8.4 %shard_map.263 = (f32[256,1024]{1,0:T(8,128)}, f32[256,1024]{1,0:T(8,128)}, bf16[256,1536]{1,0:T(8,128)(2,1)}) custom-call(bf16[256,1536]{1,0:T(8,128)(2,1)} %bitcast.75, bf16[2,768,1024]{2,1,0:T(8,128)(2,1)} %wg.11, bf16[2,768,1024]{2,1,0:T(8,128)(2,1)} %wu.11, bf16[2,1024,768]{2,1,0:T(8,128)(2,1)} %wd.11, ...), custom_call_target="tpu_custom_call" | custom-call | flops 7699999744 | tf_op jit(solution)/shard_map/pallas_call | solution.py:652
  257.6 9.3 %shard_map.264 = bf16[256,1536]{1,0:T(8,128)(2,1)} custom-call(bf16[256,1536]{1,0:T(8,128)(2,1)} %copy-done.3, f32[256,1024]{1,0:T(8,128)} %get-tuple-element.106.gt_ref, f32[256,1024]{1,0:T(8,128)} %get-tuple-element.107.up_ref, bf16[2,768,1024]{2,1,0:T(8,128)(2,1)} %wg.11, bf16[2,768,1024]{2,1,0:T(8,128)(2,1)} %wu.11, bf16[2,1024,768]{2,1,0:T(8,128)(2,1)} %wd.11, ...), custom_call_target="tpu_custom_call" | custom-call | flops 8800000000 | tf_op jit(solution)/shard_map/pallas_call | solution.py:666
  266.9 12.4 %all_to_all.91 = bf16[4,64,1536]{2,1,0:T(8,128)(2,1)S(1)} all-to-all(bf16[4,64,1536]{2,1,0:T(8,128)(2,1)} %bitcast.76), channel_id=1, replica_groups=mesh['fsdp'=2,'context'=4,'tensor'=4] {'tensor'}, dimensions={0} | all-to-all | bytes 1572864 | tf_op jit(solution)/shard_map/all_to_all | solution.py:84
  282.1 11.1 %all_to_all.92 = bf16[4,64,1536]{2,1,0:T(8,128)(2,1)S(1)} all-to-all(bf16[4,64,1536]{2,1,0:T(8,128)(2,1)S(1)} %broadcast_in_dim.32), channel_id=1, replica_groups=mesh['fsdp'=2,'context'=4,'tensor'=4] {'tensor'}, dimensions={0} | all-to-all | bytes 1572864 | tf_op jit(solution)/shard_map/all_to_all | solution.py:48
  297.9 11.6 %collective-permute-done.33.refs_7_ = bf16[64,1536]{1,0:T(8,128)(2,1)S(1)} collective-permute-done((bf16[64,1536]{1,0:T(8,128)(2,1)S(1)}, bf16[64,1536]{1,0:T(8,128)(2,1)S(1)}, u32[]{:S(2)}, u32[]{:S(2)}) %collective-permute-start.33) | collective-permute-done | bytes 196640 | tf_op jit(solution)/shard_map/ppermute | solution.py:25
  324.8 33.6 %shard_map.266 = (bf16[1024,1536]{1,0:T(8,128)(2,1)}, bf16[1024,384]{1,0:T(8,128)(2,1)}, bf16[1024,384]{1,0:T(8,128)(2,1)}, bf16[1024,384]{1,0:T(8,128)(2,1)}, b...) custom-call(s32[2]{0:T(128)} %pad_add_fusion.refs_4_.refs_0_, ...), custom_call_target="tpu_custom_call" | custom-call | flops 36300001280 | tf_op jit(solution)/shard_map/pallas_call | solution.py:615
  362.8 7.2 %all-to-all-done.9 = bf16[4,64,1536]{2,1,0:T(8,128)(2,1)S(1)} async-done(((bf16[4,64,1536]{2,1,0:T(8,128)(2,1)}), bf16[4,64,1536]{2,1,0:T(8,128)(2,1)S(1)}, u32[]{:S(2)}, u32[]{:S(2)}) %all-to-all-start.9) | async-done | bytes 786464 | tf_op jit(solution)/shard_map/all_to_all | solution.py:84
  376.0 8.5 %shard_map.267 = (bf16[768,384]{1,0:T(8,128)(2,1)}, bf16[768,384]{1,0:T(8,128)(2,1)}, bf16[768,384]{1,0:T(8,128)(2,1)}, bf16[768,384]{1,0:T(8,128)(2,1)}, bf16[7...) custom-call(bf16[1024,1536]{1,0:T(8,128)(2,1)} %get-tuple-element.117.refs_0_, ...), custom_call_target="tpu_custom_call" | custom-call | flops 7699999744 | tf_op jit(solution)/shard_map/pallas_call | solution.py:748
  387.5 9.3 %shard_map.268.refs_0_ = bf16[256,1536]{1,0:T(8,128)(2,1)} custom-call(bf16[256,1536]{1,0:T(8,128)(2,1)} %bitcast.69, f32[256,1024]{1,0:T(8,128)} %get-tuple-element.115.gt_ref, f32[256,1024]{1,0:T(8,128)} %get-tuple-element.116.up_ref, bf16[2,768,1024]{2,1,0:T(8,128)(2,1)} %wg.11, bf16[2,768,1024]{2,1,0:T(8,128)(2,1)} %wu.11, bf16[2,1024,768]{2,1,0:T(8,128)(2,1)} %wd.11, ...), custom_call_target="tpu_custom_call" | custom-call | flops 8800000000 | tf_op jit(solution)/shard_map/pallas_call | solution.py:666
  401.9 9.5 %shard_map.271 = (f32[2,768,384]{2,1,0:T(8,128)}, f32[2,768,384]{2,1,0:T(8,128)}, f32[2,768,384]{2,1,0:T(8,128)}, f32[2,768,384]{2,1,0:T(8,128)}, f32[768,128]{1,0:T(8,128)}, /*index=5*/f32[2,384,768]{2,1,0:T(8,128)}) custom-call(bf16[1024,1536]{1,0:T(8,128)(2,1)} %get-tuple-element.11, ...), custom_call_target="tpu_custom_call", output_to_operand_aliasing={{0}: (14, {}), {1}: (15, {}), {2}: (16, {}), {3}: (17, {}),... | custom-call | flops 7699999744 | tf_op jit(solution)/shard_map/pallas_call | solution.py:748
  426.2 8.1 %collective-permute-done.45.refs_1_ = bf16[64,1536]{1,0:T(8,128)(2,1)S(1)} collective-permute-done((bf16[64,1536]{1,0:T(8,128)(2,1)S(1)}, bf16[64,1536]{1,0:T(8,128)(2,1)S(1)}, u32[]{:S(2)}, u32[]{:S(2)}) %collective-permute-start.45) | collective-permute-done | bytes 196640 | tf_op jit(solution)/shard_map/ppermute | solution.py:25
  434.3 13.2 %collective-permute-done.44.refs_0_ = bf16[64,1536]{1,0:T(8,128)(2,1)S(1)} collective-permute-done((bf16[64,1536]{1,0:T(8,128)(2,1)S(1)}, bf16[64,1536]{1,0:T(8,128)(2,1)S(1)}, u32[]{:S(2)}, u32[]{:S(2)}) %collective-permute-start.44) | collective-permute-done | bytes 196640 | tf_op jit(solution)/shard_map/ppermute | solution.py:25
  455.3 21.0 %shard_map.275 = (bf16[1024,1024]{1,0:T(8,128)(2,1)}, bf16[1024,1024]{1,0:T(8,128)(2,1)}, bf16[1024,1024]{1,0:T(8,128)(2,1)}, bf16[768,1024]{1,0:T(8,128)(2,1)},...) custom-call(bf16[1024,1536]{1,0:T(8,128)(2,1)} %all-gather.9.cloned.1.call-done.b_ref, ...), custom_call_target="tpu_custom_call" | custom-call | flops 26400000000 | tf_op jit(solution)/shard_map/pallas_call | solution.py:683
  477.5 33.6 %shard_map.277 = (bf16[1024,1536]{1,0:T(8,128)(2,1)}, bf16[1024,384]{1,0:T(8,128)(2,1)}, bf16[1024,384]{1,0:T(8,128)(2,1)}, bf16[1024,384]{1,0:T(8,128)(2,1)}, b...) custom-call(s32[2]{0:T(128)} %pad_add_fusion.refs_4_.refs_0_, ...), custom_call_target="tpu_custom_call" | custom-call | flops 36300001280 | tf_op jit(solution)/shard_map/pallas_call | solution.py:615
  516.1 8.6 %shard_map.282 = (bf16[768,384]{1,0:T(8,128)(2,1)}, bf16[768,384]{1,0:T(8,128)(2,1)}, bf16[768,384]{1,0:T(8,128)(2,1)}, bf16[768,384]{1,0:T(8,128)(2,1)}, bf16[7...) custom-call(bf16[1024,1536]{1,0:T(8,128)(2,1)} %get-tuple-element.146.refs_0_, ...), custom_call_target="tpu_custom_call" | custom-call | flops 7699999744 | tf_op jit(solution)/shard_map/pallas_call | solution.py:748
  538.1 12.0 %shard_map.284 = (f32[2,768,1024]{2,1,0:T(8,128)}, f32[2,768,1024]{2,1,0:T(8,128)}, f32[2,1024,768]{2,1,0:T(8,128)}) custom-call(bf16[1024,1536]{1,0:T(8,128)(2,1)} %all-gather.9.cloned.1.call-done.b_ref, bf16[1024,1536]{1,0:T(8,128)(2,1)} %all-gather.5.cloned.1.call-done.refs_1_.g_ref, ...), custom_call_target="tpu_custom_call", output_to_operand_aliasing={{0}: (8, {}), {1}: (9, {}), {2}: (10, {})} | custom-call | flops 9900000256 | tf_op jit(solution)/shard_map/pallas_call | solution.py:708
  559.1 6.6 %all-to-all-done.16 = f32[16,1,6144]{2,1,0:T(1,128)S(1)} async-done(((f32[16,1,6144]{2,1,0:T(1,128)}), f32[16,1,6144]{2,1,0:T(1,128)S(1)}, u32[]{:S(2)}, u32[]{:S(2)}) %all-to-all-start.16) | async-done | bytes 393248 | tf_op jit(solution)/shard_map/all_to_all | solution.py:48
  568.4 21.4 %shard_map.280 = (bf16[1024,1024]{1,0:T(8,128)(2,1)}, bf16[1024,1024]{1,0:T(8,128)(2,1)}, bf16[1024,1024]{1,0:T(8,128)(2,1)}, bf16[768,1024]{1,0:T(8,128)(2,1)},...) custom-call(bf16[1024,1536]{1,0:T(8,128)(2,1)} %all-gather.7.cloned.1.call-done.refs_1_.b_ref, ...), custom_call_target="tpu_custom_call" | custom-call | flops 26400000000 | tf_op jit(solution)/shard_map/pallas_call | solution.py:683
  591.7 9.5 %shard_map.286 = (f32[2,768,384]{2,1,0:T(8,128)}, f32[2,768,384]{2,1,0:T(8,128)}, f32[2,768,384]{2,1,0:T(8,128)}, f32[2,768,384]{2,1,0:T(8,128)}, f32[768,128]{1,0:T(8,128)}, /*index=5*/f32[2,384,768]{2,1,0:T(8,128)}) custom-call(bf16[1024,1536]{1,0:T(8,128)(2,1)} %get-tuple-element.14, ...), custom_call_target="tpu_custom_call", output_to_operand_aliasing={{0}: (14, {}), {1}: (15, {}), {2}: (16, {}), {3}: (17, {}),... | custom-call | flops 7699999744 | tf_op jit(solution)/shard_map/pallas_call | solution.py:748
  602.4 7.4 %all-reduce.4.cloned.1.call-done.refs_0_ = bf16[256,1536]{1,0:T(8,128)(2,1)} async-done(((bf16[256,1536]{1,0:T(8,128)(2,1)}), bf16[256,1536]{1,0:T(8,128)(2,1)}) %all-reduce.4.cloned.1.call-update) | async-done | bytes 786448 | tf_op jit(solution)/shard_map/psum | solution.py:946
  612.6 11.8 %shard_map.287 = (f32[2,768,1024]{2,1,0:T(8,128)}, f32[2,768,1024]{2,1,0:T(8,128)}, f32[2,1024,768]{2,1,0:T(8,128)}) custom-call(bf16[1024,1536]{1,0:T(8,128)(2,1)} %all-gather.7.cloned.1.call-done.refs_1_.b_ref, bf16[1024,1536]{1,0:T(8,128)(2,1)} %all-gather.11.cloned.1.call-done.g_ref, ...), custom_call_target="tpu_custom_call", output_to_operand_aliasing={{0}: (8, {}), {1}: (9, {}), {2}: (10, {})} | custom-call | flops 9900000256 | tf_op jit(solution)/shard_map/pallas_call | solution.py:708
  (407 shorter events, 171.6 us)
Async XLA Ops:
  14.9 133.0 %all-gather.5.cloned.1.call-start = ((), (), s32[]{:S(2)}) async-start(), calls=%async_computation.17 | async-start | bytes 3932160 | tf_op jit(solution)/shard_map/all_gather | solution.py:849
  21.5 48.4 %collective-permute-start.1 = (bf16[256,1536]{1,0:T(8,128)(2,1)}, bf16[256,1536]{1,0:T(8,128)(2,1)}, u32[]{:S(2)}, u32[]{:S(2)}) collective-permute-start(bf16[256,1536]{1,0:T(8,128)(2,1)} %multiply_convert_fusion.refs_1_), channel_id=1, source_target_pairs={{0,4},{4,0},{8,12},{12,8},{1,5},{5,1},{9,13},{13,9},{2,6},{6,2},{1... | collective-permute-start | bytes 2359304 | tf_op jit(solution)/shard_map/ppermute | solution.py:25
  25.8 23.0 %collective-permute-start.7 = (bf16[64,1536]{1,0:T(8,128)(2,1)}, bf16[64,1536]{1,0:T(8,128)(2,1)S(1)}, u32[]{:S(2)}, u32[]{:S(2)}) collective-permute-start(bf16[64,1536]{1,0:T(8,128)(2,1)} %shard_map.254), channel_id=1, source_target_pairs={{0,12},{4,8},{8,4},{12,0},{1,13},{5,9},{9,5},{13,1},{2,14},{6,10},... | collective-permute-start | bytes 589832 | tf_op jit(solution)/shard_map/ppermute | solution.py:25
  28.2 25.1 %collective-permute-start.2 = (bf16[64,1536]{1,0:T(8,128)(2,1)}, bf16[64,1536]{1,0:T(8,128)(2,1)S(1)}, u32[]{:S(2)}, u32[]{:S(2)}) collective-permute-start(bf16[64,1536]{1,0:T(8,128)(2,1)} %shard_map.254), channel_id=1, source_target_pairs={{0,8},{4,12},{8,0},{12,4},{1,9},{5,13},{9,1},{13,5},{2,10},{6,14},... | collective-permute-start | bytes 589832 | tf_op jit(solution)/shard_map/ppermute | solution.py:25
  72.0 209.1 %all-gather.7.cloned.1.call-start = ((), (), s32[]{:S(2)}) async-start(), calls=%async_computation.18 | async-start | bytes 3342336 | tf_op jit(solution)/shard_map/all_gather | solution.py:52
  72.1 52.9 %collective-permute-start.16 = (bf16[2,768,1024]{2,1,0:T(8,128)(2,1)}, bf16[2,768,1024]{2,1,0:T(8,128)(2,1)}, u32[]{:S(2)}, u32[]{:S(2)}) collective-permute-start(bf16[2,768,1024]{2,1,0:T(8,128)(2,1)} %wg.11), channel_id=1, source_target_pairs={{0,16},{16,0},{1,17},{17,1},{2,18},{18,2},{3,19},{19,3},{4,20},{20... | collective-permute-start | bytes 9437192 | tf_op jit(solution)/shard_map/ppermute | solution.py:25
  72.1 52.8 %collective-permute-start.17 = (bf16[2,768,1024]{2,1,0:T(8,128)(2,1)}, bf16[2,768,1024]{2,1,0:T(8,128)(2,1)}, u32[]{:S(2)}, u32[]{:S(2)}) collective-permute-start(bf16[2,768,1024]{2,1,0:T(8,128)(2,1)} %wu.11), channel_id=1, source_target_pairs={{0,16},{16,0},{1,17},{17,1},{2,18},{18,2},{3,19},{19,3},{4,20},{20... | collective-permute-start | bytes 9437192 | tf_op jit(solution)/shard_map/ppermute | solution.py:25
  72.6 52.3 %collective-permute-start.18 = (bf16[2,1024,768]{2,1,0:T(8,128)(2,1)}, bf16[2,1024,768]{2,1,0:T(8,128)(2,1)}, u32[]{:S(2)}, u32[]{:S(2)}) collective-permute-start(bf16[2,1024,768]{2,1,0:T(8,128)(2,1)} %wd.11), channel_id=1, source_target_pairs={{0,16},{16,0},{1,17},{17,1},{2,18},{18,2},{3,19},{19,3},{4,20},{20... | collective-permute-start | bytes 9437192 | tf_op jit(solution)/shard_map/ppermute | solution.py:25
  160.1 34.8 %collective-permute-start.19 = (bf16[256,1536]{1,0:T(8,128)(2,1)S(1)}, bf16[256,1536]{1,0:T(8,128)(2,1)S(1)}, u32[]{:S(2)}, u32[]{:S(2)}) collective-permute-start(bf16[256,1536]{1,0:T(8,128)(2,1)S(1)} %bitcast.67), channel_id=1, source_target_pairs={{0,4},{4,0},{8,12},{12,8},{1,5},{5,1},{9,13},{13,9},{2,6},{6,2},{1... | collective-permute-start | bytes 2359304 | tf_op jit(solution)/shard_map/ppermute | solution.py:25
  160.1 20.3 %collective-permute-start.24 = (bf16[64,1536]{1,0:T(8,128)(2,1)S(1)}, bf16[64,1536]{1,0:T(8,128)(2,1)S(1)}, u32[]{:S(2)}, u32[]{:S(2)}) collective-permute-start(bf16[64,1536]{1,0:T(8,128)(2,1)S(1)} %copy-done.13), channel_id=1, source_target_pairs={{0,12},{4,8},{8,4},{12,0},{1,13},{5,9},{9,5},{13,1},{2,14},{6,10},... | collective-permute-start | bytes 589832 | tf_op jit(solution)/shard_map/ppermute | solution.py:25
  161.2 22.7 %collective-permute-start.20 = (bf16[64,1536]{1,0:T(8,128)(2,1)S(1)}, bf16[64,1536]{1,0:T(8,128)(2,1)S(1)}, u32[]{:S(2)}, u32[]{:S(2)}) collective-permute-start(bf16[64,1536]{1,0:T(8,128)(2,1)S(1)} %copy-done.13), channel_id=1, source_target_pairs={{0,8},{4,12},{8,0},{12,4},{1,9},{5,13},{9,1},{13,5},{2,10},{6,14},... | collective-permute-start | bytes 589832 | tf_op jit(solution)/shard_map/ppermute | solution.py:25
  293.3 30.6 %collective-permute-start.28 = (bf16[256,1536]{1,0:T(8,128)(2,1)S(1)}, bf16[256,1536]{1,0:T(8,128)(2,1)S(1)}, u32[]{:S(2)}, u32[]{:S(2)}) collective-permute-start(bf16[256,1536]{1,0:T(8,128)(2,1)S(1)} %bitcast.57), channel_id=1, source_target_pairs={{0,4},{4,0},{8,12},{12,8},{1,5},{5,1},{9,13},{13,9},{2,6},{6,2},{1... | collective-permute-start | bytes 2359304 | tf_op jit(solution)/shard_map/ppermute | solution.py:25
  362.0 93.2 %all-gather.9.cloned.1.call-start = ((), (), s32[]{:S(2)}) async-start(), calls=%async_computation.19 | async-start | bytes 3342336 | tf_op jit(solution)/shard_map/all_gather | solution.py:52
  397.8 17.0 %all-to-all-start.11 = ((bf16[4,64,1536]{2,1,0:T(8,128)(2,1)}), bf16[4,64,1536]{2,1,0:T(8,128)(2,1)S(1)}, u32[]{:S(2)}, u32[]{:S(2)}) async-start(bf16[4,64,1536]{2,1,0:T(8,128)(2,1)} %bitcast.60), calls=%async_computation.11 | async-start | bytes 1572864 | tf_op jit(solution)/shard_map/all_to_all | solution.py:84
  417.9 30.4 %all-to-all-start.12 = ((bf16[4,64,1536]{2,1,0:T(8,128)(2,1)}), bf16[4,64,1536]{2,1,0:T(8,128)(2,1)S(1)}, u32[]{:S(2)}, u32[]{:S(2)}) async-start(bf16[4,64,1536]{2,1,0:T(8,128)(2,1)} %broadcast_in_dim.34), calls=%async_computation.12 | async-start | bytes 1572864 | tf_op jit(solution)/shard_map/all_to_all | solution.py:48
  423.4 24.1 %collective-permute-start.44 = (bf16[64,1536]{1,0:T(8,128)(2,1)S(1)}, bf16[64,1536]{1,0:T(8,128)(2,1)S(1)}, u32[]{:S(2)}, u32[]{:S(2)}) collective-permute-start(bf16[64,1536]{1,0:T(8,128)(2,1)S(1)} %copy-done.14), channel_id=1, source_target_pairs={{0,8},{4,12},{8,0},{12,4},{1,9},{5,13},{9,1},{13,5},{2,10},{6,14},... | collective-permute-start | bytes 589832 | tf_op jit(solution)/shard_map/ppermute | solution.py:25
  448.3 28.0 %collective-permute-start.43 = (bf16[256,1536]{1,0:T(8,128)(2,1)S(1)}, bf16[256,1536]{1,0:T(8,128)(2,1)}, u32[]{:S(2)}, u32[]{:S(2)}) collective-permute-start(bf16[256,1536]{1,0:T(8,128)(2,1)S(1)} %bitcast.61), channel_id=1, source_target_pairs={{0,4},{4,0},{8,12},{12,8},{1,5},{5,1},{9,13},{13,9},{2,6},{6,2},{1... | collective-permute-start | bytes 2359304 | tf_op jit(solution)/shard_map/ppermute | solution.py:25
  451.5 24.9 %all-to-all-start.13 = ((bf16[4,128,1536]{2,1,0:T(8,128)(2,1)}), bf16[4,128,1536]{2,1,0:T(8,128)(2,1)S(1)}, u32[]{:S(2)}, u32[]{:S(2)}) async-start(bf16[4,128,1536]{2,1,0:T(8,128)(2,1)} %broadcast_in_dim.35), calls=%async_computation.13 | async-start | bytes 3145728 | tf_op jit(solution)/shard_map/all_to_all | solution.py:48
  455.0 113.4 %all-gather.11.cloned.1.call-start = ((), (), s32[]{:S(2)}) async-start(), calls=%async_computation.21 | async-start | bytes 3342336 | tf_op jit(solution)/shard_map/all_gather | solution.py:52
  511.1 19.5 %all-to-all-start.14 = ((bf16[4,64,1536]{2,1,0:T(8,128)(2,1)}), bf16[4,64,1536]{2,1,0:T(8,128)(2,1)S(1)}, u32[]{:S(2)}, u32[]{:S(2)}) async-start(bf16[4,64,1536]{2,1,0:T(8,128)(2,1)} %bitcast.55), calls=%async_computation.14 | async-start | bytes 1572864 | tf_op jit(solution)/shard_map/all_to_all | solution.py:84
  515.5 22.6 %collective-permute-start.52 = (bf16[768,1024]{1,0:T(8,128)(2,1)}, bf16[768,1024]{1,0:T(8,128)(2,1)}, u32[]{:S(2)}, u32[]{:S(2)}) collective-permute-start(bf16[768,1024]{1,0:T(8,128)(2,1)} %get-tuple-element.166), channel_id=1, source_target_pairs={{0,16},{16,0},{1,17},{17,1},{2,18},{18,2},{3,19},{19,3},{4,20},{20... | collective-permute-start | bytes 4718600 | tf_op jit(solution)/shard_map/ppermute | solution.py:25
  515.5 22.6 %collective-permute-start.53 = (bf16[768,1024]{1,0:T(8,128)(2,1)}, bf16[768,1024]{1,0:T(8,128)(2,1)}, u32[]{:S(2)}, u32[]{:S(2)}) collective-permute-start(bf16[768,1024]{1,0:T(8,128)(2,1)} %get-tuple-element.167), channel_id=1, source_target_pairs={{0,16},{16,0},{1,17},{17,1},{2,18},{18,2},{3,19},{19,3},{4,20},{20... | collective-permute-start | bytes 4718600 | tf_op jit(solution)/shard_map/ppermute | solution.py:25
  516.0 22.1 %collective-permute-start.54 = (bf16[1024,768]{1,0:T(8,128)(2,1)}, bf16[1024,768]{1,0:T(8,128)(2,1)}, u32[]{:S(2)}, u32[]{:S(2)}) collective-permute-start(bf16[1024,768]{1,0:T(8,128)(2,1)} %get-tuple-element.168), channel_id=1, source_target_pairs={{0,16},{16,0},{1,17},{17,1},{2,18},{18,2},{3,19},{19,3},{4,20},{20... | collective-permute-start | bytes 4718600 | tf_op jit(solution)/shard_map/ppermute | solution.py:25
  556.1 53.7 %all-reduce.4.cloned.1.call-start = ((), (), s32[]{:S(2)}) async-start(), calls=%async_computation.20 | async-start | bytes 1572864 | tf_op jit(solution)/shard_map/psum | solution.py:946
  556.3 34.5 %collective-permute-start.46 = (bf16[768,384]{1,0:T(8,128)(2,1)S(1)}, bf16[768,384]{1,0:T(8,128)(2,1)}, u32[]{:S(2)}, u32[]{:S(2)}) collective-permute-start(bf16[768,384]{1,0:T(8,128)(2,1)S(1)} %copy-done.23), channel_id=1, source_target_pairs={{0,16},{16,0},{1,17},{17,1},{2,18},{18,2},{3,19},{19,3},{4,20},{20... | collective-permute-start | bytes 1769480 | tf_op jit(solution)/shard_map/ppermute | solution.py:25
  557.8 32.0 %collective-permute-start.47 = (bf16[768,384]{1,0:T(8,128)(2,1)}, bf16[768,384]{1,0:T(8,128)(2,1)}, u32[]{:S(2)}, u32[]{:S(2)}) collective-permute-start(bf16[768,384]{1,0:T(8,128)(2,1)} %get-tuple-element.155), channel_id=1, source_target_pairs={{0,16},{16,0},{1,17},{17,1},{2,18},{18,2},{3,19},{19,3},{4,20},{20... | collective-permute-start | bytes 1769480 | tf_op jit(solution)/shard_map/ppermute | solution.py:25
  557.9 32.4 %collective-permute-start.48 = (bf16[768,384]{1,0:T(8,128)(2,1)}, bf16[768,384]{1,0:T(8,128)(2,1)}, u32[]{:S(2)}, u32[]{:S(2)}) collective-permute-start(bf16[768,384]{1,0:T(8,128)(2,1)} %get-tuple-element.156), channel_id=1, source_target_pairs={{0,16},{16,0},{1,17},{17,1},{2,18},{18,2},{3,19},{19,3},{4,20},{20... | collective-permute-start | bytes 1769480 | tf_op jit(solution)/shard_map/ppermute | solution.py:25
  567.2 23.2 %collective-permute-start.49 = (bf16[768,384]{1,0:T(8,128)(2,1)}, bf16[768,384]{1,0:T(8,128)(2,1)S(1)}, u32[]{:S(2)}, u32[]{:S(2)}) collective-permute-start(bf16[768,384]{1,0:T(8,128)(2,1)} %get-tuple-element.157), channel_id=1, source_target_pairs={{0,16},{16,0},{1,17},{17,1},{2,18},{18,2},{3,19},{19,3},{4,20},{20... | collective-permute-start | bytes 1769480 | tf_op jit(solution)/shard_map/ppermute | solution.py:25
  568.2 22.6 %collective-permute-start.51 = (bf16[384,768]{1,0:T(8,128)(2,1)S(1)}, bf16[384,768]{1,0:T(8,128)(2,1)S(1)}, u32[]{:S(2)}, u32[]{:S(2)}) collective-permute-start(bf16[384,768]{1,0:T(8,128)(2,1)S(1)} %copy-done.65), channel_id=1, source_target_pairs={{0,16},{16,0},{1,17},{17,1},{2,18},{18,2},{3,19},{19,3},{4,20},{20... | collective-permute-start | bytes 1769480 | tf_op jit(solution)/shard_map/ppermute | solution.py:25
  589.8 22.8 %collective-permute-start.58 = (bf16[768,1024]{1,0:T(8,128)(2,1)}, bf16[768,1024]{1,0:T(8,128)(2,1)}, u32[]{:S(2)}, u32[]{:S(2)}) collective-permute-start(bf16[768,1024]{1,0:T(8,128)(2,1)} %get-tuple-element.182), channel_id=1, source_target_pairs={{0,16},{16,0},{1,17},{17,1},{2,18},{18,2},{3,19},{19,3},{4,20},{20... | collective-permute-start | bytes 4718600 | tf_op jit(solution)/shard_map/ppermute | solution.py:25
  590.3 22.3 %collective-permute-start.59 = (bf16[768,1024]{1,0:T(8,128)(2,1)}, bf16[768,1024]{1,0:T(8,128)(2,1)}, u32[]{:S(2)}, u32[]{:S(2)}) collective-permute-start(bf16[768,1024]{1,0:T(8,128)(2,1)} %get-tuple-element.183), channel_id=1, source_target_pairs={{0,16},{16,0},{1,17},{17,1},{2,18},{18,2},{3,19},{19,3},{4,20},{20... | collective-permute-start | bytes 4718600 | tf_op jit(solution)/shard_map/ppermute | solution.py:25
  590.4 22.2 %collective-permute-start.60 = (bf16[1024,768]{1,0:T(8,128)(2,1)}, bf16[1024,768]{1,0:T(8,128)(2,1)}, u32[]{:S(2)}, u32[]{:S(2)}) collective-permute-start(bf16[1024,768]{1,0:T(8,128)(2,1)} %get-tuple-element.184), channel_id=1, source_target_pairs={{0,16},{16,0},{1,17},{17,1},{2,18},{18,2},{3,19},{19,3},{4,20},{20... | collective-permute-start | bytes 4718600 | tf_op jit(solution)/shard_map/ppermute | solution.py:25
  (121 other events, 1192.9 us)
Sparse Core Ops, SparseCore 0:
  72.1 61.0 all-gather.4
  191.2 71.4 all-gather.6
  365.6 82.4 all-gather.8
  476.5 69.8 all-gather.10
  559.7 50.0 all-reduce.3

commit v15 on v14

--- a/solution.py
+++ b/solution.py
@@ -906,7 +906,7 @@
         else:
             g_shard = grad.astype(bf16)
             g = gathered(g_shard, "tensor")
-            tokens = (saved[layer + 1]["theirs"][0],)
+            tokens = (saved[layer + 1]["theirs"][0], output)
         if not shared_rows:
             s.update(b_rows=s["b"], g_rows=g)
         sends = ffn_backward(g, s["gt"], s["up"], layer, w3, t3, *tokens)
@@ -931,6 +931,10 @@
             place, y_parts, layer, w4, t4, w_attn_out, to, w_forget_full[layer], kept, doc_start, piece_len,
         )
         token = y_parts[-1]
+        if layer == last:
+            block_sum = own_block(last_sends).astype(f32) + s["mixed"]
+            with_rows = lax.dynamic_update_slice_in_dim(last_sends, block_sum.astype(bf16), t * block, 0)
+            output = lax.psum(after(with_rows, *y_parts), "tensor")
         if shared_rows and layer == last:
             s.update(b_rows=sequence_rows(after(s["b_shard"], *y_parts)), g_rows=g_last)
         elif shared_rows:
@@ -941,9 +945,6 @@
         back, gain_grads[layer] = norm_back(received_sum(sends), s["hidden"], s["inverse_one"], gain_one)
         grad = grad_mixed + back
 
-    block_sum = own_block(last_sends).astype(f32) + saved[last]["mixed"]
-    with_rows = lax.dynamic_update_slice_in_dim(last_sends, block_sum.astype(bf16), t * block, 0)
-    output = lax.psum(after(with_rows, sends), "tensor")
     for layer in reversed(range(1, layers)):
         ffn_mine_of(layer, sends)
     attention_theirs_of(0, sends)
@@ -958,7 +959,7 @@
     ffn_mine_of(0)
     if not shared_rows:
         results[5:] = [lax.psum(x, "context") for x in results[5:]]
-    output = features(after(output, saved[0]["values"][0])).reshape(1, piece_len, width)
+    output = features(output).reshape(1, piece_len, width)
     return (
         output, grad_input, *results[:5], jnp.stack(small[0]), jnp.stack(small[1]),
         gain_total[:layers], gain_total[layers:], *results[5:],

time: 641 us -> 653 us (1.019)
  waiting for transfers between devices: 126 us -> 136 us
  blocking collectives: 111 us -> 103 us
  starting transfers between devices: 81.1 us -> 89 us
    all_to_all x6 -> x7, waiting for transfers between devices: 6.63 us -> 18.2 us  [gathered(): lax.all_to_all(copies, axis, 0, 0, tiled=True)]
    ppermute x61, waiting for transfers between devices: 95.2 us -> 104 us  [swap(): return lax.ppermute(x, axis, [(i, i ^ k) for i in range(n)])]
    psum x1, waiting for transfers between devices: 7.36 us -> 0.01 us  [local(): output = lax.psum(after(with_rows, *y_parts), 'tensor')]
    all_to_all x4 -> x3, blocking collectives: 52 us -> 45.4 us  [gathered(): lax.all_to_all(copies, axis, 0, 0, tiled=True)]
    all_to_all x6 -> x7, starting transfers between devices: 24.9 us -> 30.8 us  [gathered(): lax.all_to_all(copies, axis, 0, 0, tiled=True)]
    unnamed x159 -> x173, local copies, waits for them, and re-layouts: 11.1 us -> 14.4 us
  transfers between devices with their start and end apart: 75 -> 76, of which waited for: 30 -> 28; matrix products, arithmetic and copies ran while one was open for 7% -> 7% of each run, Pallas kernels for 31% -> 36%
where the time goes in v15:
time: 653 us; the launch traced here: 645 us
  Pallas kernels  244 us (37%)
  waiting for transfers between devices  136 us (21%)
  blocking collectives  103 us (16%)
  starting transfers between devices  89 us (14%)
  local copies, waits for them, and re-layouts  38.1 us (6%)
  other arithmetic  20.5 us (3%)
  between operations  15.3 us (2%)
    ppermute x61, waiting for transfers between devices, swap(): return lax.ppermute(x, axis, [(i, i ^ k) for i in range(n)])  104 us
    pallas_call x2, Pallas kernels, attention_backward(): pl.pallas_call(functools.partial(backward_kernel, len(parts), piece_len,...  67.4 us
    all_to_all x4, blocking collectives, received_sum(): lax.all_to_all(sends.reshape(count, -1, sends.shape[1]), 'tensor', 0, 0,...  57.3 us
    ppermute x61, starting transfers between devices, swap(): return lax.ppermute(x, axis, [(i, i ^ k) for i in range(n)])  45.6 us
    all_to_all x3, blocking collectives, gathered(): lax.all_to_all(copies, axis, 0, 0, tiled=True)  45.4 us
    pallas_call x2, Pallas kernels, ffn_theirs(): pl.pallas_call(ffn_theirs_kernel, grid=(inner // hidden_block,), in_specs...  42.2 us
    pallas_call x2, Pallas kernels, forward_own(): pl.pallas_call(functools.partial(forward_own_kernel, len(parts), piece_le...  39 us
    pallas_call x4, Pallas kernels, attention_grads(): pl.pallas_call(functools.partial(attention_grads_kernel, steps, mine), gr...  36.1 us
  transfers between devices with their start and end apart: 76, of which 28 were waited for; matrix products, arithmetic and copies ran while one was open for 7% of the time, Pallas kernels for 36%

profile of v15, /device:TPU:0, one launch (start us, length us, event | category | flops | bytes accessed | tf_op | source)
XLA Modules:
  0.0 645.3 jit_solution(3483264028538557960)
XLA Ops:
  9.8 5.9 all-to-all-start
  30.2 14.9 %collective-permute-done.2.refs_0_ = bf16[64,1536]{1,0:T(8,128)(2,1)S(1)} collective-permute-done((bf16[64,1536]{1,0:T(8,128)(2,1)}, bf16[64,1536]{1,0:T(8,128)(2,1)S(1)}, u32[]{:S(2)}, u32[]{:S(2)}) %collective-permute-start.2) | collective-permute-done | bytes 196640 | tf_op jit(solution)/shard_map/ppermute | solution.py:25
  72.6 19.6 %shard_map.256 = (bf16[1024,1536]{1,0:T(8,128)(2,1)}, bf16[1024,384]{1,0:T(8,128)(2,1)}, bf16[1024,384]{1,0:T(8,128)(2,1)}, bf16[1024,384]{1,0:T(8,128)(2,1)}, f...) custom-call(s32[2]{0:T(128)} %pad_add_fusion.refs_4_.refs_0_, ...), custom_call_target="tpu_custom_call" | custom-call | flops 20899999744 | tf_op jit(solution)/shard_map/pallas_call | solution.py:585
  92.2 15.3 %all_to_all.85 = bf16[4,64,1536]{2,1,0:T(8,128)(2,1)S(1)} all-to-all(bf16[4,64,1536]{2,1,0:T(8,128)(2,1)} %bitcast.73), channel_id=1, replica_groups=mesh['fsdp'=2,'context'=4,'tensor'=4] {'tensor'}, dimensions={0} | all-to-all | bytes 1572864 | tf_op jit(solution)/shard_map/all_to_all | solution.py:84
  108.5 13.9 %all_to_all.86 = bf16[4,64,1536]{2,1,0:T(8,128)(2,1)} all-to-all(bf16[4,64,1536]{2,1,0:T(8,128)(2,1)S(1)} %broadcast_in_dim.29), channel_id=1, replica_groups=mesh['fsdp'=2,'context'=4,'tensor'=4] {'tensor'}, dimensions={0} | all-to-all | bytes 1572864 | tf_op jit(solution)/shard_map/all_to_all | solution.py:48
  122.4 8.4 %shard_map.257 = (f32[256,1024]{1,0:T(8,128)}, f32[256,1024]{1,0:T(8,128)}, bf16[256,1536]{1,0:T(8,128)(2,1)}) custom-call(bf16[256,1536]{1,0:T(8,128)(2,1)} %bitcast.74, bf16[2,768,1024]{2,1,0:T(8,128)(2,1)} %wg.11, bf16[2,768,1024]{2,1,0:T(8,128)(2,1)} %wu.11, bf16[2,1024,768]{2,1,0:T(8,128)(2,1)} %wd.11, ...), custom_call_target="tpu_custom_call" | custom-call | flops 7699999744 | tf_op jit(solution)/shard_map/pallas_call | solution.py:652
  130.9 12.9 %all_to_all.87 = bf16[4,64,1536]{2,1,0:T(8,128)(2,1)S(1)} all-to-all(bf16[4,64,1536]{2,1,0:T(8,128)(2,1)} %bitcast.75), channel_id=1, replica_groups=mesh['fsdp'=2,'context'=4,'tensor'=4] {'tensor'}, dimensions={0} | all-to-all | bytes 1572864 | tf_op jit(solution)/shard_map/all_to_all | solution.py:84
  146.4 11.1 %all_to_all.88 = bf16[4,64,1536]{2,1,0:T(8,128)(2,1)S(1)} all-to-all(bf16[4,64,1536]{2,1,0:T(8,128)(2,1)S(1)} %broadcast_in_dim.30), channel_id=1, replica_groups=mesh['fsdp'=2,'context'=4,'tensor'=4] {'tensor'}, dimensions={0} | all-to-all | bytes 1572864 | tf_op jit(solution)/shard_map/all_to_all | solution.py:48
  163.3 15.9 %collective-permute-done.20.refs_3_ = bf16[64,1536]{1,0:T(8,128)(2,1)S(1)} collective-permute-done((bf16[64,1536]{1,0:T(8,128)(2,1)S(1)}, bf16[64,1536]{1,0:T(8,128)(2,1)S(1)}, u32[]{:S(2)}, u32[]{:S(2)}) %collective-permute-start.20) | collective-permute-done | bytes 196640 | tf_op jit(solution)/shard_map/ppermute | solution.py:25
  198.4 19.4 %shard_map.262 = (bf16[1024,1536]{1,0:T(8,128)(2,1)}, bf16[1024,384]{1,0:T(8,128)(2,1)}, bf16[1024,384]{1,0:T(8,128)(2,1)}, bf16[1024,384]{1,0:T(8,128)(2,1)}, f...) custom-call(s32[2]{0:T(128)} %pad_add_fusion.refs_4_.refs_0_, ...), custom_call_target="tpu_custom_call" | custom-call | flops 20899999744 | tf_op jit(solution)/shard_map/pallas_call | solution.py:585
  217.8 16.9 %all_to_all.89 = bf16[4,64,1536]{2,1,0:T(8,128)(2,1)S(1)} all-to-all(bf16[4,64,1536]{2,1,0:T(8,128)(2,1)} %bitcast.72), channel_id=1, replica_groups=mesh['fsdp'=2,'context'=4,'tensor'=4] {'tensor'}, dimensions={0} | all-to-all | bytes 1572864 | tf_op jit(solution)/shard_map/all_to_all | solution.py:84
  235.2 20.4 %all_to_all.90 = bf16[4,64,1536]{2,1,0:T(8,128)(2,1)} all-to-all(bf16[4,64,1536]{2,1,0:T(8,128)(2,1)S(1)} %broadcast_in_dim.31), channel_id=1, replica_groups=mesh['fsdp'=2,'context'=4,'tensor'=4] {'tensor'}, dimensions={0} | all-to-all | bytes 1572864 | tf_op jit(solution)/shard_map/all_to_all | solution.py:48
  255.6 8.4 %shard_map.263 = (f32[256,1024]{1,0:T(8,128)}, f32[256,1024]{1,0:T(8,128)}, bf16[256,1536]{1,0:T(8,128)(2,1)}) custom-call(bf16[256,1536]{1,0:T(8,128)(2,1)} %bitcast.76, bf16[2,768,1024]{2,1,0:T(8,128)(2,1)} %wg.11, bf16[2,768,1024]{2,1,0:T(8,128)(2,1)} %wu.11, bf16[2,1024,768]{2,1,0:T(8,128)(2,1)} %wd.11, ...), custom_call_target="tpu_custom_call" | custom-call | flops 7699999744 | tf_op jit(solution)/shard_map/pallas_call | solution.py:652
  264.1 9.3 %shard_map.264 = bf16[256,1536]{1,0:T(8,128)(2,1)} custom-call(bf16[256,1536]{1,0:T(8,128)(2,1)} %copy-done.3, f32[256,1024]{1,0:T(8,128)} %get-tuple-element.106.gt_ref, f32[256,1024]{1,0:T(8,128)} %get-tuple-element.107.up_ref, bf16[2,768,1024]{2,1,0:T(8,128)(2,1)} %wg.11, bf16[2,768,1024]{2,1,0:T(8,128)(2,1)} %wu.11, bf16[2,1024,768]{2,1,0:T(8,128)(2,1)} %wd.11, ...), custom_call_target="tpu_custom_call" | custom-call | flops 8800000000 | tf_op jit(solution)/shard_map/pallas_call | solution.py:666
  273.4 12.1 %all_to_all.91 = bf16[4,64,1536]{2,1,0:T(8,128)(2,1)S(1)} all-to-all(bf16[4,64,1536]{2,1,0:T(8,128)(2,1)} %bitcast.77), channel_id=1, replica_groups=mesh['fsdp'=2,'context'=4,'tensor'=4] {'tensor'}, dimensions={0} | all-to-all | bytes 1572864 | tf_op jit(solution)/shard_map/all_to_all | solution.py:84
  294.7 10.1 %all-to-all-done.8 = bf16[4,64,1536]{2,1,0:T(8,128)(2,1)S(1)} async-done(((bf16[4,64,1536]{2,1,0:T(8,128)(2,1)}), bf16[4,64,1536]{2,1,0:T(8,128)(2,1)S(1)}, u32[]{:S(2)}, u32[]{:S(2)}) %all-to-all-start.8) | async-done | bytes 786464 | tf_op jit(solution)/shard_map/all_to_all | solution.py:48
  311.6 8.6 %collective-permute-done.33.refs_7_ = bf16[64,1536]{1,0:T(8,128)(2,1)S(1)} collective-permute-done((bf16[64,1536]{1,0:T(8,128)(2,1)S(1)}, bf16[64,1536]{1,0:T(8,128)(2,1)S(1)}, u32[]{:S(2)}, u32[]{:S(2)}) %collective-permute-start.33) | collective-permute-done | bytes 196640 | tf_op jit(solution)/shard_map/ppermute | solution.py:25
  330.7 33.9 %shard_map.267 = (bf16[1024,1536]{1,0:T(8,128)(2,1)}, bf16[1024,384]{1,0:T(8,128)(2,1)}, bf16[1024,384]{1,0:T(8,128)(2,1)}, bf16[1024,384]{1,0:T(8,128)(2,1)}, b...) custom-call(s32[2]{0:T(128)} %pad_add_fusion.refs_4_.refs_0_, ...), custom_call_target="tpu_custom_call" | custom-call | flops 36300001280 | tf_op jit(solution)/shard_map/pallas_call | solution.py:615
  369.9 7.5 %all-to-all-done.9 = bf16[4,64,1536]{2,1,0:T(8,128)(2,1)S(1)} async-done(((bf16[4,64,1536]{2,1,0:T(8,128)(2,1)}), bf16[4,64,1536]{2,1,0:T(8,128)(2,1)S(1)}, u32[]{:S(2)}, u32[]{:S(2)}) %all-to-all-start.9) | async-done | bytes 786464 | tf_op jit(solution)/shard_map/all_to_all | solution.py:84
  383.4 8.5 %shard_map.268 = (bf16[768,384]{1,0:T(8,128)(2,1)}, bf16[768,384]{1,0:T(8,128)(2,1)}, bf16[768,384]{1,0:T(8,128)(2,1)}, bf16[768,384]{1,0:T(8,128)(2,1)}, bf16[7...) custom-call(bf16[1024,1536]{1,0:T(8,128)(2,1)} %get-tuple-element.117.refs_0_, ...), custom_call_target="tpu_custom_call" | custom-call | flops 7699999744 | tf_op jit(solution)/shard_map/pallas_call | solution.py:748
  398.3 9.3 %shard_map.269.refs_0_ = bf16[256,1536]{1,0:T(8,128)(2,1)} custom-call(bf16[256,1536]{1,0:T(8,128)(2,1)} %bitcast.70, f32[256,1024]{1,0:T(8,128)} %get-tuple-element.115.gt_ref, f32[256,1024]{1,0:T(8,128)} %get-tuple-element.116.up_ref, bf16[2,768,1024]{2,1,0:T(8,128)(2,1)} %wg.11, bf16[2,768,1024]{2,1,0:T(8,128)(2,1)} %wu.11, bf16[2,1024,768]{2,1,0:T(8,128)(2,1)} %wd.11, ...), custom_call_target="tpu_custom_call" | custom-call | flops 8800000000 | tf_op jit(solution)/shard_map/pallas_call | solution.py:666
  412.9 9.5 %shard_map.272 = (f32[2,768,384]{2,1,0:T(8,128)}, f32[2,768,384]{2,1,0:T(8,128)}, f32[2,768,384]{2,1,0:T(8,128)}, f32[2,768,384]{2,1,0:T(8,128)}, f32[768,128]{1,0:T(8,128)}, /*index=5*/f32[2,384,768]{2,1,0:T(8,128)}) custom-call(bf16[1024,1536]{1,0:T(8,128)(2,1)} %get-tuple-element.11, ...), custom_call_target="tpu_custom_call", output_to_operand_aliasing={{0}: (14, {}), {1}: (15, {}), {2}: (16, {}), {3}: (17, {}),... | custom-call | flops 7699999744 | tf_op jit(solution)/shard_map/pallas_call | solution.py:748
  440.1 8.9 %collective-permute-done.45.refs_1_ = bf16[64,1536]{1,0:T(8,128)(2,1)S(1)} collective-permute-done((bf16[64,1536]{1,0:T(8,128)(2,1)S(1)}, bf16[64,1536]{1,0:T(8,128)(2,1)S(1)}, u32[]{:S(2)}, u32[]{:S(2)}) %collective-permute-start.45) | collective-permute-done | bytes 196640 | tf_op jit(solution)/shard_map/ppermute | solution.py:25
  449.0 20.1 %collective-permute-done.44.refs_0_ = bf16[64,1536]{1,0:T(8,128)(2,1)S(1)} collective-permute-done((bf16[64,1536]{1,0:T(8,128)(2,1)S(1)}, bf16[64,1536]{1,0:T(8,128)(2,1)S(1)}, u32[]{:S(2)}, u32[]{:S(2)}) %collective-permute-start.44) | collective-permute-done | bytes 196640 | tf_op jit(solution)/shard_map/ppermute | solution.py:25
  477.5 21.0 %shard_map.276 = (bf16[1024,1024]{1,0:T(8,128)(2,1)}, bf16[1024,1024]{1,0:T(8,128)(2,1)}, bf16[1024,1024]{1,0:T(8,128)(2,1)}, bf16[768,1024]{1,0:T(8,128)(2,1)},...) custom-call(bf16[1024,1536]{1,0:T(8,128)(2,1)} %all-gather.9.cloned.1.call-done.b_ref, ...), custom_call_target="tpu_custom_call" | custom-call | flops 26400000000 | tf_op jit(solution)/shard_map/pallas_call | solution.py:683
  499.8 33.6 %shard_map.278 = (bf16[1024,1536]{1,0:T(8,128)(2,1)}, bf16[1024,384]{1,0:T(8,128)(2,1)}, bf16[1024,384]{1,0:T(8,128)(2,1)}, bf16[1024,384]{1,0:T(8,128)(2,1)}, b...) custom-call(s32[2]{0:T(128)} %pad_add_fusion.refs_4_.refs_0_, ...), custom_call_target="tpu_custom_call" | custom-call | flops 36300001280 | tf_op jit(solution)/shard_map/pallas_call | solution.py:615
  538.4 8.6 %shard_map.279 = (bf16[768,384]{1,0:T(8,128)(2,1)}, bf16[768,384]{1,0:T(8,128)(2,1)}, bf16[768,384]{1,0:T(8,128)(2,1)}, bf16[768,384]{1,0:T(8,128)(2,1)}, bf16[7...) custom-call(bf16[1024,1536]{1,0:T(8,128)(2,1)} %get-tuple-element.145.refs_0_, ...), custom_call_target="tpu_custom_call" | custom-call | flops 7699999744 | tf_op jit(solution)/shard_map/pallas_call | solution.py:748
  555.9 12.0 %shard_map.281 = (f32[2,768,1024]{2,1,0:T(8,128)}, f32[2,768,1024]{2,1,0:T(8,128)}, f32[2,1024,768]{2,1,0:T(8,128)}) custom-call(bf16[1024,1536]{1,0:T(8,128)(2,1)} %all-gather.9.cloned.1.call-done.b_ref, bf16[1024,1536]{1,0:T(8,128)(2,1)} %all-gather.5.cloned.1.call-done.refs_1_.g_ref, ...), custom_call_target="tpu_custom_call", output_to_operand_aliasing={{0}: (8, {}), {1}: (9, {}), {2}: (10, {})} | custom-call | flops 9900000256 | tf_op jit(solution)/shard_map/pallas_call | solution.py:708
  579.6 8.1 %all-to-all-done.16 = f32[16,1,6144]{2,1,0:T(1,128)S(1)} async-done(((f32[16,1,6144]{2,1,0:T(1,128)}), f32[16,1,6144]{2,1,0:T(1,128)S(1)}, u32[]{:S(2)}, u32[]{:S(2)}) %all-to-all-start.16) | async-done | bytes 393248 | tf_op jit(solution)/shard_map/all_to_all | solution.py:48
  588.1 21.2 %shard_map.284 = (bf16[1024,1024]{1,0:T(8,128)(2,1)}, bf16[1024,1024]{1,0:T(8,128)(2,1)}, bf16[1024,1024]{1,0:T(8,128)(2,1)}, bf16[768,1024]{1,0:T(8,128)(2,1)},...) custom-call(bf16[1024,1536]{1,0:T(8,128)(2,1)} %all-gather.7.cloned.1.call-done.refs_1_.b_ref, ...), custom_call_target="tpu_custom_call" | custom-call | flops 26400000000 | tf_op jit(solution)/shard_map/pallas_call | solution.py:683
  614.0 9.5 %shard_map.285 = (f32[2,768,384]{2,1,0:T(8,128)}, f32[2,768,384]{2,1,0:T(8,128)}, f32[2,768,384]{2,1,0:T(8,128)}, f32[2,768,384]{2,1,0:T(8,128)}, f32[768,128]{1,0:T(8,128)}, /*index=5*/f32[2,384,768]{2,1,0:T(8,128)}) custom-call(bf16[1024,1536]{1,0:T(8,128)(2,1)} %get-tuple-element.14, ...), custom_call_target="tpu_custom_call", output_to_operand_aliasing={{0}: (14, {}), {1}: (15, {}), {2}: (16, {}), {3}: (17, {}),... | custom-call | flops 7699999744 | tf_op jit(solution)/shard_map/pallas_call | solution.py:748
  626.5 11.8 %shard_map.286 = (f32[2,768,1024]{2,1,0:T(8,128)}, f32[2,768,1024]{2,1,0:T(8,128)}, f32[2,1024,768]{2,1,0:T(8,128)}) custom-call(bf16[1024,1536]{1,0:T(8,128)(2,1)} %all-gather.7.cloned.1.call-done.refs_1_.b_ref, bf16[1024,1536]{1,0:T(8,128)(2,1)} %all-gather.11.cloned.1.call-done.g_ref, ...), custom_call_target="tpu_custom_call", output_to_operand_aliasing={{0}: (8, {}), {1}: (9, {}), {2}: (10, {})} | custom-call | flops 9900000256 | tf_op jit(solution)/shard_map/pallas_call | solution.py:708
  (421 shorter events, 183.4 us)
Async XLA Ops:
  15.7 129.6 %all-gather.5.cloned.1.call-start = ((), (), s32[]{:S(2)}) async-start(), calls=%async_computation.17 | async-start | bytes 3932160 | tf_op jit(solution)/shard_map/all_gather | solution.py:849
  20.9 45.6 %collective-permute-start.1 = (bf16[256,1536]{1,0:T(8,128)(2,1)}, bf16[256,1536]{1,0:T(8,128)(2,1)}, u32[]{:S(2)}, u32[]{:S(2)}) collective-permute-start(bf16[256,1536]{1,0:T(8,128)(2,1)} %multiply_convert_fusion.refs_1_), channel_id=1, source_target_pairs={{0,4},{4,0},{8,12},{12,8},{1,5},{5,1},{9,13},{13,9},{2,6},{6,2},{1... | collective-permute-start | bytes 2359304 | tf_op jit(solution)/shard_map/ppermute | solution.py:25
  25.0 20.1 %collective-permute-start.2 = (bf16[64,1536]{1,0:T(8,128)(2,1)}, bf16[64,1536]{1,0:T(8,128)(2,1)S(1)}, u32[]{:S(2)}, u32[]{:S(2)}) collective-permute-start(bf16[64,1536]{1,0:T(8,128)(2,1)} %shard_map.254), channel_id=1, source_target_pairs={{0,8},{4,12},{8,0},{12,4},{1,9},{5,13},{9,1},{13,5},{2,10},{6,14},... | collective-permute-start | bytes 589832 | tf_op jit(solution)/shard_map/ppermute | solution.py:25
  27.4 24.2 %collective-permute-start.7 = (bf16[64,1536]{1,0:T(8,128)(2,1)}, bf16[64,1536]{1,0:T(8,128)(2,1)S(1)}, u32[]{:S(2)}, u32[]{:S(2)}) collective-permute-start(bf16[64,1536]{1,0:T(8,128)(2,1)} %shard_map.254), channel_id=1, source_target_pairs={{0,12},{4,8},{8,4},{12,0},{1,13},{5,9},{9,5},{13,1},{2,14},{6,10},... | collective-permute-start | bytes 589832 | tf_op jit(solution)/shard_map/ppermute | solution.py:25
  68.3 219.5 %all-gather.7.cloned.1.call-start = ((), (), s32[]{:S(2)}) async-start(), calls=%async_computation.18 | async-start | bytes 3342336 | tf_op jit(solution)/shard_map/all_gather | solution.py:52
  68.3 54.1 %collective-permute-start.16 = (bf16[2,768,1024]{2,1,0:T(8,128)(2,1)}, bf16[2,768,1024]{2,1,0:T(8,128)(2,1)}, u32[]{:S(2)}, u32[]{:S(2)}) collective-permute-start(bf16[2,768,1024]{2,1,0:T(8,128)(2,1)} %wg.11), channel_id=1, source_target_pairs={{0,16},{16,0},{1,17},{17,1},{2,18},{18,2},{3,19},{19,3},{4,20},{20... | collective-permute-start | bytes 9437192 | tf_op jit(solution)/shard_map/ppermute | solution.py:25
  68.8 53.6 %collective-permute-start.17 = (bf16[2,768,1024]{2,1,0:T(8,128)(2,1)}, bf16[2,768,1024]{2,1,0:T(8,128)(2,1)}, u32[]{:S(2)}, u32[]{:S(2)}) collective-permute-start(bf16[2,768,1024]{2,1,0:T(8,128)(2,1)} %wu.11), channel_id=1, source_target_pairs={{0,16},{16,0},{1,17},{17,1},{2,18},{18,2},{3,19},{19,3},{4,20},{20... | collective-permute-start | bytes 9437192 | tf_op jit(solution)/shard_map/ppermute | solution.py:25
  69.2 53.2 %collective-permute-start.18 = (bf16[2,1024,768]{2,1,0:T(8,128)(2,1)}, bf16[2,1024,768]{2,1,0:T(8,128)(2,1)}, u32[]{:S(2)}, u32[]{:S(2)}) collective-permute-start(bf16[2,1024,768]{2,1,0:T(8,128)(2,1)} %wd.11), channel_id=1, source_target_pairs={{0,16},{16,0},{1,17},{17,1},{2,18},{18,2},{3,19},{19,3},{4,20},{20... | collective-permute-start | bytes 9437192 | tf_op jit(solution)/shard_map/ppermute | solution.py:25
  157.5 40.1 %collective-permute-start.19 = (bf16[256,1536]{1,0:T(8,128)(2,1)S(1)}, bf16[256,1536]{1,0:T(8,128)(2,1)S(1)}, u32[]{:S(2)}, u32[]{:S(2)}) collective-permute-start(bf16[256,1536]{1,0:T(8,128)(2,1)S(1)} %bitcast.68), channel_id=1, source_target_pairs={{0,4},{4,0},{8,12},{12,8},{1,5},{5,1},{9,13},{13,9},{2,6},{6,2},{1... | collective-permute-start | bytes 2359304 | tf_op jit(solution)/shard_map/ppermute | solution.py:25
  160.8 18.3 %collective-permute-start.20 = (bf16[64,1536]{1,0:T(8,128)(2,1)S(1)}, bf16[64,1536]{1,0:T(8,128)(2,1)S(1)}, u32[]{:S(2)}, u32[]{:S(2)}) collective-permute-start(bf16[64,1536]{1,0:T(8,128)(2,1)S(1)} %copy-done.13), channel_id=1, source_target_pairs={{0,8},{4,12},{8,0},{12,4},{1,9},{5,13},{9,1},{13,5},{2,10},{6,14},... | collective-permute-start | bytes 589832 | tf_op jit(solution)/shard_map/ppermute | solution.py:25
  161.0 22.3 %collective-permute-start.24 = (bf16[64,1536]{1,0:T(8,128)(2,1)S(1)}, bf16[64,1536]{1,0:T(8,128)(2,1)S(1)}, u32[]{:S(2)}, u32[]{:S(2)}) collective-permute-start(bf16[64,1536]{1,0:T(8,128)(2,1)S(1)} %copy-done.13), channel_id=1, source_target_pairs={{0,12},{4,8},{8,4},{12,0},{1,13},{5,9},{9,5},{13,1},{2,14},{6,10},... | collective-permute-start | bytes 589832 | tf_op jit(solution)/shard_map/ppermute | solution.py:25
  293.2 104.2 %all-reduce.4.cloned.1.call-start = ((), (), s32[]{:S(2)}) async-start(), calls=%async_computation.19 | async-start | bytes 1572864 | tf_op jit(solution)/shard_map/psum | solution.py:937
  304.8 25.8 %collective-permute-start.28 = (bf16[256,1536]{1,0:T(8,128)(2,1)S(1)}, bf16[256,1536]{1,0:T(8,128)(2,1)}, u32[]{:S(2)}, u32[]{:S(2)}) collective-permute-start(bf16[256,1536]{1,0:T(8,128)(2,1)S(1)} %bitcast.53), channel_id=1, source_target_pairs={{0,4},{4,0},{8,12},{12,8},{1,5},{5,1},{9,13},{13,9},{2,6},{6,2},{1... | collective-permute-start | bytes 2359304 | tf_op jit(solution)/shard_map/ppermute | solution.py:25
  309.7 15.8 %collective-permute-start.32 = (bf16[64,1536]{1,0:T(8,128)(2,1)S(1)}, bf16[64,1536]{1,0:T(8,128)(2,1)S(1)}, u32[]{:S(2)}, u32[]{:S(2)}) collective-permute-start(bf16[64,1536]{1,0:T(8,128)(2,1)S(1)} %collective-permute-done.29.refs_3_), channel_id=1, source_target_pairs={{0,3},{1,2},{2,1},{3,0},{4,7},{5,6},{6,5},{7,4},{8,11},{9,10},{10,... | collective-permute-start | bytes 589832 | tf_op jit(solution)/shard_map/ppermute | solution.py:25
  368.1 109.4 %all-gather.9.cloned.1.call-start = ((), (), s32[]{:S(2)}) async-start(), calls=%async_computation.20 | async-start | bytes 3342336 | tf_op jit(solution)/shard_map/all_gather | solution.py:52
  379.5 17.9 %all-to-all-start.10 = ((bf16[4,64,1536]{2,1,0:T(8,128)(2,1)}), bf16[4,64,1536]{2,1,0:T(8,128)(2,1)S(1)}, u32[]{:S(2)}, u32[]{:S(2)}) async-start(bf16[4,64,1536]{2,1,0:T(8,128)(2,1)} %broadcast_in_dim.33), calls=%async_computation.10 | async-start | bytes 1572864 | tf_op jit(solution)/shard_map/all_to_all | solution.py:48
  408.8 18.8 %all-to-all-start.11 = ((bf16[4,64,1536]{2,1,0:T(8,128)(2,1)}), bf16[4,64,1536]{2,1,0:T(8,128)(2,1)S(1)}, u32[]{:S(2)}, u32[]{:S(2)}) async-start(bf16[4,64,1536]{2,1,0:T(8,128)(2,1)} %bitcast.60), calls=%async_computation.11 | async-start | bytes 1572864 | tf_op jit(solution)/shard_map/all_to_all | solution.py:84
  430.9 39.0 %all-to-all-start.12 = ((bf16[4,64,1536]{2,1,0:T(8,128)(2,1)}), bf16[4,64,1536]{2,1,0:T(8,128)(2,1)S(1)}, u32[]{:S(2)}, u32[]{:S(2)}) async-start(bf16[4,64,1536]{2,1,0:T(8,128)(2,1)} %broadcast_in_dim.34), calls=%async_computation.12 | async-start | bytes 1572864 | tf_op jit(solution)/shard_map/all_to_all | solution.py:48
  438.7 30.4 %collective-permute-start.44 = (bf16[64,1536]{1,0:T(8,128)(2,1)S(1)}, bf16[64,1536]{1,0:T(8,128)(2,1)S(1)}, u32[]{:S(2)}, u32[]{:S(2)}) collective-permute-start(bf16[64,1536]{1,0:T(8,128)(2,1)S(1)} %copy-done.14), channel_id=1, source_target_pairs={{0,8},{4,12},{8,0},{12,4},{1,9},{5,13},{9,1},{13,5},{2,10},{6,14},... | collective-permute-start | bytes 589832 | tf_op jit(solution)/shard_map/ppermute | solution.py:25
  469.9 28.7 %collective-permute-start.43 = (bf16[256,1536]{1,0:T(8,128)(2,1)S(1)}, bf16[256,1536]{1,0:T(8,128)(2,1)}, u32[]{:S(2)}, u32[]{:S(2)}) collective-permute-start(bf16[256,1536]{1,0:T(8,128)(2,1)S(1)} %bitcast.61), channel_id=1, source_target_pairs={{0,4},{4,0},{8,12},{12,8},{1,5},{5,1},{9,13},{13,9},{2,6},{6,2},{1... | collective-permute-start | bytes 2359304 | tf_op jit(solution)/shard_map/ppermute | solution.py:25
  473.1 25.6 %all-to-all-start.13 = ((bf16[4,128,1536]{2,1,0:T(8,128)(2,1)}), bf16[4,128,1536]{2,1,0:T(8,128)(2,1)S(1)}, u32[]{:S(2)}, u32[]{:S(2)}) async-start(bf16[4,128,1536]{2,1,0:T(8,128)(2,1)} %broadcast_in_dim.35), calls=%async_computation.13 | async-start | bytes 3145728 | tf_op jit(solution)/shard_map/all_to_all | solution.py:48
  477.3 110.8 %all-gather.11.cloned.1.call-start = ((), (), s32[]{:S(2)}) async-start(), calls=%async_computation.21 | async-start | bytes 3342336 | tf_op jit(solution)/shard_map/all_gather | solution.py:52
  537.8 18.1 %collective-permute-start.52 = (bf16[768,1024]{1,0:T(8,128)(2,1)}, bf16[768,1024]{1,0:T(8,128)(2,1)}, u32[]{:S(2)}, u32[]{:S(2)}) collective-permute-start(bf16[768,1024]{1,0:T(8,128)(2,1)} %get-tuple-element.165), channel_id=1, source_target_pairs={{0,16},{16,0},{1,17},{17,1},{2,18},{18,2},{3,19},{19,3},{4,20},{20... | collective-permute-start | bytes 4718600 | tf_op jit(solution)/shard_map/ppermute | solution.py:25
  537.8 18.0 %collective-permute-start.53 = (bf16[768,1024]{1,0:T(8,128)(2,1)}, bf16[768,1024]{1,0:T(8,128)(2,1)}, u32[]{:S(2)}, u32[]{:S(2)}) collective-permute-start(bf16[768,1024]{1,0:T(8,128)(2,1)} %get-tuple-element.166), channel_id=1, source_target_pairs={{0,16},{16,0},{1,17},{17,1},{2,18},{18,2},{3,19},{19,3},{4,20},{20... | collective-permute-start | bytes 4718600 | tf_op jit(solution)/shard_map/ppermute | solution.py:25
  538.3 17.5 %collective-permute-start.54 = (bf16[1024,768]{1,0:T(8,128)(2,1)}, bf16[1024,768]{1,0:T(8,128)(2,1)}, u32[]{:S(2)}, u32[]{:S(2)}) collective-permute-start(bf16[1024,768]{1,0:T(8,128)(2,1)} %get-tuple-element.167), channel_id=1, source_target_pairs={{0,16},{16,0},{1,17},{17,1},{2,18},{18,2},{3,19},{19,3},{4,20},{20... | collective-permute-start | bytes 4718600 | tf_op jit(solution)/shard_map/ppermute | solution.py:25
  551.0 16.9 %all-to-all-start.15 = ((bf16[4,64,1536]{2,1,0:T(8,128)(2,1)}), bf16[4,64,1536]{2,1,0:T(8,128)(2,1)S(1)}, u32[]{:S(2)}, u32[]{:S(2)}) async-start(bf16[4,64,1536]{2,1,0:T(8,128)(2,1)} %broadcast_in_dim.36), calls=%async_computation.15 | async-start | bytes 1572864 | tf_op jit(solution)/shard_map/all_to_all | solution.py:48
  569.6 18.1 %all-to-all-start.16 = ((f32[16,1,6144]{2,1,0:T(1,128)}), f32[16,1,6144]{2,1,0:T(1,128)S(1)}, u32[]{:S(2)}, u32[]{:S(2)}) async-start(f32[16,1,6144]{2,1,0:T(1,128)} %broadcast_in_dim.38), calls=%async_computation.16 | async-start | bytes 786432 | tf_op jit(solution)/shard_map/all_to_all | solution.py:48
  576.1 33.7 %collective-permute-start.46 = (bf16[768,384]{1,0:T(8,128)(2,1)S(1)}, bf16[768,384]{1,0:T(8,128)(2,1)S(1)}, u32[]{:S(2)}, u32[]{:S(2)}) collective-permute-start(bf16[768,384]{1,0:T(8,128)(2,1)S(1)} %copy-done.33), channel_id=1, source_target_pairs={{0,16},{16,0},{1,17},{17,1},{2,18},{18,2},{3,19},{19,3},{4,20},{20... | collective-permute-start | bytes 1769480 | tf_op jit(solution)/shard_map/ppermute | solution.py:25
  576.1 33.8 %collective-permute-start.47 = (bf16[768,384]{1,0:T(8,128)(2,1)}, bf16[768,384]{1,0:T(8,128)(2,1)}, u32[]{:S(2)}, u32[]{:S(2)}) collective-permute-start(bf16[768,384]{1,0:T(8,128)(2,1)} %get-tuple-element.154), channel_id=1, source_target_pairs={{0,16},{16,0},{1,17},{17,1},{2,18},{18,2},{3,19},{19,3},{4,20},{20... | collective-permute-start | bytes 1769480 | tf_op jit(solution)/shard_map/ppermute | solution.py:25
  576.7 34.1 %collective-permute-start.48 = (bf16[768,384]{1,0:T(8,128)(2,1)}, bf16[768,384]{1,0:T(8,128)(2,1)}, u32[]{:S(2)}, u32[]{:S(2)}) collective-permute-start(bf16[768,384]{1,0:T(8,128)(2,1)} %get-tuple-element.155), channel_id=1, source_target_pairs={{0,16},{16,0},{1,17},{17,1},{2,18},{18,2},{3,19},{19,3},{4,20},{20... | collective-permute-start | bytes 1769480 | tf_op jit(solution)/shard_map/ppermute | solution.py:25
  576.7 32.7 %collective-permute-start.50 = (bf16[768,128]{1,0:T(8,128)(2,1)}, bf16[768,128]{1,0:T(8,128)(2,1)S(1)}, u32[]{:S(2)}, u32[]{:S(2)}) collective-permute-start(bf16[768,128]{1,0:T(8,128)(2,1)} %get-tuple-element.157), channel_id=1, source_target_pairs={{0,16},{16,0},{1,17},{17,1},{2,18},{18,2},{3,19},{19,3},{4,20},{20... | collective-permute-start | bytes 589832 | tf_op jit(solution)/shard_map/ppermute | solution.py:25
  588.0 23.2 %collective-permute-start.55 = (f32[4,768]{1,0:T(4,128)S(1)}, f32[4,768]{1,0:T(4,128)S(1)}, u32[]{:S(2)}, u32[]{:S(2)}) collective-permute-start(f32[4,768]{1,0:T(4,128)S(1)} %slice.113), channel_id=1, source_target_pairs={{0,16},{16,0},{1,17},{17,1},{2,18},{18,2},{3,19},{19,3},{4,20},{20... | collective-permute-start | bytes 36872 | tf_op jit(solution)/shard_map/ppermute | solution.py:25
  (129 other events, 1227.2 us)
Sparse Core Ops, SparseCore 0:
  68.4 63.5 all-gather.4
  193.7 72.3 all-gather.6
  330.8 51.8 all-reduce.3
  385.7 84.4 all-gather.8
  498.7 67.3 all-gather.10

commit v16 on v14

--- a/solution.py
+++ b/solution.py
@@ -947,14 +947,14 @@
     for layer in reversed(range(1, layers)):
         ffn_mine_of(layer, sends)
     attention_theirs_of(0, sends)
-    gain_total = after(jnp.stack(gain_grads).reshape(1, -1), *([results[5]] if layers > 1 else []))
+    ffn_theirs_of(0)
+    gain_total = after(jnp.stack(gain_grads).reshape(1, -1), saved[0]["values"][0])
     for axis in (("context", "tensor"),) if shared_rows else ("context", "tensor"):
         gain_total = jnp.sum(gathered(gain_total, axis), axis=0, keepdims=True)
     gain_total = gain_total.reshape(2 * layers, width)
     gain_total = gain_total[:, :half] + other(gain_total[:, half:])
     grad_input = finish(after(grad, saved[0]["theirs"][0]))
-    ffn_theirs_of(0)
-    attention_mine_of(0, gain_total, saved[0]["values"][0])
+    attention_mine_of(0, saved[0]["values"][0])
     ffn_mine_of(0)
     if not shared_rows:
         results[5:] = [lax.psum(x, "context") for x in results[5:]]

time: 641 us -> 658 us (1.027)
  blocking collectives: 111 us -> 129 us
    all_to_all x4 -> x5, blocking collectives: 58.8 us -> 72.8 us  [received_sum(): lax.all_to_all(sends.reshape(count, -1, sends.shape[1]), 'tensor', 0, 0,...]
    all_to_all x6, waiting for transfers between devices: 6.63 us -> 17.9 us  [gathered(): lax.all_to_all(copies, axis, 0, 0, tiled=True)]
    psum x1, waiting for transfers between devices: 7.36 us -> 0.02 us  [local(): output = lax.psum(after(with_rows, sends), 'tensor')]
    all_to_all x3 -> x2, waiting for transfers between devices: 16.5 us -> 12.3 us  [received_sum(): lax.all_to_all(sends.reshape(count, -1, sends.shape[1]), 'tensor', 0, 0,...]
  transfers between devices with their start and end apart: 75 -> 74, of which waited for: 30 -> 33; matrix products, arithmetic and copies ran while one was open for 7% -> 7% of each run, Pallas kernels for 31% -> 36%
where the time goes in v16:
time: 658 us; the launch traced here: 648 us
  Pallas kernels  244 us (37%)
  blocking collectives  129 us (20%)
  waiting for transfers between devices  126 us (19%)
  starting transfers between devices  77.6 us (12%)
  local copies, waits for them, and re-layouts  35.2 us (5%)
  other arithmetic  20.4 us (3%)
  between operations  15.1 us (2%)
    ppermute x61, waiting for transfers between devices, swap(): return lax.ppermute(x, axis, [(i, i ^ k) for i in range(n)])  95.9 us
    all_to_all x5, blocking collectives, received_sum(): lax.all_to_all(sends.reshape(count, -1, sends.shape[1]), 'tensor', 0, 0,...  72.8 us
    pallas_call x2, Pallas kernels, attention_backward(): pl.pallas_call(functools.partial(backward_kernel, len(parts), piece_len,...  67.3 us
    all_to_all x4, blocking collectives, gathered(): lax.all_to_all(copies, axis, 0, 0, tiled=True)  56.7 us
    ppermute x61, starting transfers between devices, swap(): return lax.ppermute(x, axis, [(i, i ^ k) for i in range(n)])  43.6 us
    pallas_call x2, Pallas kernels, ffn_theirs(): pl.pallas_call(ffn_theirs_kernel, grid=(inner // hidden_block,), in_specs...  42.1 us
    pallas_call x2, Pallas kernels, forward_own(): pl.pallas_call(functools.partial(forward_own_kernel, len(parts), piece_le...  39 us
    pallas_call x4, Pallas kernels, attention_grads(): pl.pallas_call(functools.partial(attention_grads_kernel, steps, mine), gr...  36.4 us
  transfers between devices with their start and end apart: 74, of which 33 were waited for; matrix products, arithmetic and copies ran while one was open for 7% of the time, Pallas kernels for 36%

profile of v16, /device:TPU:0, one launch (start us, length us, event | category | flops | bytes accessed | tf_op | source)
XLA Modules:
  0.0 648.3 jit_solution(8572110599526864764)
XLA Ops:
  30.2 15.0 %collective-permute-done.2.refs_0_ = bf16[64,1536]{1,0:T(8,128)(2,1)S(1)} collective-permute-done((bf16[64,1536]{1,0:T(8,128)(2,1)}, bf16[64,1536]{1,0:T(8,128)(2,1)S(1)}, u32[]{:S(2)}, u32[]{:S(2)}) %collective-permute-start.2) | collective-permute-done | bytes 196640 | tf_op jit(solution)/shard_map/ppermute | solution.py:25
  72.6 19.6 %shard_map.256 = (bf16[1024,1536]{1,0:T(8,128)(2,1)}, bf16[1024,384]{1,0:T(8,128)(2,1)}, bf16[1024,384]{1,0:T(8,128)(2,1)}, bf16[1024,384]{1,0:T(8,128)(2,1)}, f...) custom-call(s32[2]{0:T(128)} %pad_add_fusion.refs_4_.refs_0_, ...), custom_call_target="tpu_custom_call" | custom-call | flops 20899999744 | tf_op jit(solution)/shard_map/pallas_call | solution.py:585
  92.2 15.3 %all_to_all.85 = bf16[4,64,1536]{2,1,0:T(8,128)(2,1)S(1)} all-to-all(bf16[4,64,1536]{2,1,0:T(8,128)(2,1)} %bitcast.72), channel_id=1, replica_groups=mesh['fsdp'=2,'context'=4,'tensor'=4] {'tensor'}, dimensions={0} | all-to-all | bytes 1572864 | tf_op jit(solution)/shard_map/all_to_all | solution.py:84
  108.5 13.9 %all_to_all.86 = bf16[4,64,1536]{2,1,0:T(8,128)(2,1)} all-to-all(bf16[4,64,1536]{2,1,0:T(8,128)(2,1)S(1)} %broadcast_in_dim.29), channel_id=1, replica_groups=mesh['fsdp'=2,'context'=4,'tensor'=4] {'tensor'}, dimensions={0} | all-to-all | bytes 1572864 | tf_op jit(solution)/shard_map/all_to_all | solution.py:48
  122.4 8.4 %shard_map.257 = (f32[256,1024]{1,0:T(8,128)}, f32[256,1024]{1,0:T(8,128)}, bf16[256,1536]{1,0:T(8,128)(2,1)}) custom-call(bf16[256,1536]{1,0:T(8,128)(2,1)} %bitcast.73, bf16[2,768,1024]{2,1,0:T(8,128)(2,1)} %wg.11, bf16[2,768,1024]{2,1,0:T(8,128)(2,1)} %wu.11, bf16[2,1024,768]{2,1,0:T(8,128)(2,1)} %wd.11, ...), custom_call_target="tpu_custom_call" | custom-call | flops 7699999744 | tf_op jit(solution)/shard_map/pallas_call | solution.py:652
  130.9 13.0 %all_to_all.87 = bf16[4,64,1536]{2,1,0:T(8,128)(2,1)S(1)} all-to-all(bf16[4,64,1536]{2,1,0:T(8,128)(2,1)} %bitcast.74), channel_id=1, replica_groups=mesh['fsdp'=2,'context'=4,'tensor'=4] {'tensor'}, dimensions={0} | all-to-all | bytes 1572864 | tf_op jit(solution)/shard_map/all_to_all | solution.py:84
  146.4 11.1 %all_to_all.88 = bf16[4,64,1536]{2,1,0:T(8,128)(2,1)S(1)} all-to-all(bf16[4,64,1536]{2,1,0:T(8,128)(2,1)S(1)} %broadcast_in_dim.30), channel_id=1, replica_groups=mesh['fsdp'=2,'context'=4,'tensor'=4] {'tensor'}, dimensions={0} | all-to-all | bytes 1572864 | tf_op jit(solution)/shard_map/all_to_all | solution.py:48
  163.3 15.9 %collective-permute-done.20.refs_3_ = bf16[64,1536]{1,0:T(8,128)(2,1)S(1)} collective-permute-done((bf16[64,1536]{1,0:T(8,128)(2,1)S(1)}, bf16[64,1536]{1,0:T(8,128)(2,1)S(1)}, u32[]{:S(2)}, u32[]{:S(2)}) %collective-permute-start.20) | collective-permute-done | bytes 196640 | tf_op jit(solution)/shard_map/ppermute | solution.py:25
  198.4 19.4 %shard_map.262 = (bf16[1024,1536]{1,0:T(8,128)(2,1)}, bf16[1024,384]{1,0:T(8,128)(2,1)}, bf16[1024,384]{1,0:T(8,128)(2,1)}, bf16[1024,384]{1,0:T(8,128)(2,1)}, f...) custom-call(s32[2]{0:T(128)} %pad_add_fusion.refs_4_.refs_0_, ...), custom_call_target="tpu_custom_call" | custom-call | flops 20899999744 | tf_op jit(solution)/shard_map/pallas_call | solution.py:585
  217.8 17.1 %all_to_all.89 = bf16[4,64,1536]{2,1,0:T(8,128)(2,1)S(1)} all-to-all(bf16[4,64,1536]{2,1,0:T(8,128)(2,1)} %bitcast.71), channel_id=1, replica_groups=mesh['fsdp'=2,'context'=4,'tensor'=4] {'tensor'}, dimensions={0} | all-to-all | bytes 1572864 | tf_op jit(solution)/shard_map/all_to_all | solution.py:84
  235.3 20.3 %all_to_all.90 = bf16[4,64,1536]{2,1,0:T(8,128)(2,1)} all-to-all(bf16[4,64,1536]{2,1,0:T(8,128)(2,1)S(1)} %broadcast_in_dim.31), channel_id=1, replica_groups=mesh['fsdp'=2,'context'=4,'tensor'=4] {'tensor'}, dimensions={0} | all-to-all | bytes 1572864 | tf_op jit(solution)/shard_map/all_to_all | solution.py:48
  255.6 8.5 %shard_map.263 = (f32[256,1024]{1,0:T(8,128)}, f32[256,1024]{1,0:T(8,128)}, bf16[256,1536]{1,0:T(8,128)(2,1)}) custom-call(bf16[256,1536]{1,0:T(8,128)(2,1)} %bitcast.75, bf16[2,768,1024]{2,1,0:T(8,128)(2,1)} %wg.11, bf16[2,768,1024]{2,1,0:T(8,128)(2,1)} %wu.11, bf16[2,1024,768]{2,1,0:T(8,128)(2,1)} %wd.11, ...), custom_call_target="tpu_custom_call" | custom-call | flops 7699999744 | tf_op jit(solution)/shard_map/pallas_call | solution.py:652
  264.1 9.3 %shard_map.264 = bf16[256,1536]{1,0:T(8,128)(2,1)} custom-call(bf16[256,1536]{1,0:T(8,128)(2,1)} %copy-done.3, f32[256,1024]{1,0:T(8,128)} %get-tuple-element.106.gt_ref, f32[256,1024]{1,0:T(8,128)} %get-tuple-element.107.up_ref, bf16[2,768,1024]{2,1,0:T(8,128)(2,1)} %wg.11, bf16[2,768,1024]{2,1,0:T(8,128)(2,1)} %wu.11, bf16[2,1024,768]{2,1,0:T(8,128)(2,1)} %wd.11, ...), custom_call_target="tpu_custom_call" | custom-call | flops 8800000000 | tf_op jit(solution)/shard_map/pallas_call | solution.py:666
  273.4 12.2 %all_to_all.91 = bf16[4,64,1536]{2,1,0:T(8,128)(2,1)S(1)} all-to-all(bf16[4,64,1536]{2,1,0:T(8,128)(2,1)} %bitcast.76), channel_id=1, replica_groups=mesh['fsdp'=2,'context'=4,'tensor'=4] {'tensor'}, dimensions={0} | all-to-all | bytes 1572864 | tf_op jit(solution)/shard_map/all_to_all | solution.py:84
  288.3 11.3 %all_to_all.92 = bf16[4,64,1536]{2,1,0:T(8,128)(2,1)S(1)} all-to-all(bf16[4,64,1536]{2,1,0:T(8,128)(2,1)S(1)} %broadcast_in_dim.32), channel_id=1, replica_groups=mesh['fsdp'=2,'context'=4,'tensor'=4] {'tensor'}, dimensions={0} | all-to-all | bytes 1572864 | tf_op jit(solution)/shard_map/all_to_all | solution.py:48
  304.1 9.1 %collective-permute-done.29.refs_3_ = bf16[64,1536]{1,0:T(8,128)(2,1)S(1)} collective-permute-done((bf16[64,1536]{1,0:T(8,128)(2,1)S(1)}, bf16[64,1536]{1,0:T(8,128)(2,1)S(1)}, u32[]{:S(2)}, u32[]{:S(2)}) %collective-permute-start.29) | collective-permute-done | bytes 196640 | tf_op jit(solution)/shard_map/ppermute | solution.py:25
  329.2 33.6 %shard_map.266 = (bf16[1024,1536]{1,0:T(8,128)(2,1)}, bf16[1024,384]{1,0:T(8,128)(2,1)}, bf16[1024,384]{1,0:T(8,128)(2,1)}, bf16[1024,384]{1,0:T(8,128)(2,1)}, b...) custom-call(s32[2]{0:T(128)} %pad_add_fusion.refs_4_.refs_0_, ...), custom_call_target="tpu_custom_call" | custom-call | flops 36300001280 | tf_op jit(solution)/shard_map/pallas_call | solution.py:615
  362.8 15.3 %all_to_all.93 = bf16[4,64,1536]{2,1,0:T(8,128)(2,1)S(1)} all-to-all(bf16[4,64,1536]{2,1,0:T(8,128)(2,1)} %bitcast.70), channel_id=1, replica_groups=mesh['fsdp'=2,'context'=4,'tensor'=4] {'tensor'}, dimensions={0} | all-to-all | bytes 1572864 | tf_op jit(solution)/shard_map/all_to_all | solution.py:84
  383.9 8.5 %shard_map.267 = (bf16[768,384]{1,0:T(8,128)(2,1)}, bf16[768,384]{1,0:T(8,128)(2,1)}, bf16[768,384]{1,0:T(8,128)(2,1)}, bf16[768,384]{1,0:T(8,128)(2,1)}, bf16[7...) custom-call(bf16[1024,1536]{1,0:T(8,128)(2,1)} %get-tuple-element.117.refs_0_, ...), custom_call_target="tpu_custom_call" | custom-call | flops 7699999744 | tf_op jit(solution)/shard_map/pallas_call | solution.py:748
  395.1 9.3 %shard_map.268.refs_0_ = bf16[256,1536]{1,0:T(8,128)(2,1)} custom-call(bf16[256,1536]{1,0:T(8,128)(2,1)} %bitcast.69, f32[256,1024]{1,0:T(8,128)} %get-tuple-element.115.gt_ref, f32[256,1024]{1,0:T(8,128)} %get-tuple-element.116.up_ref, bf16[2,768,1024]{2,1,0:T(8,128)(2,1)} %wg.11, bf16[2,768,1024]{2,1,0:T(8,128)(2,1)} %wu.11, bf16[2,1024,768]{2,1,0:T(8,128)(2,1)} %wd.11, ...), custom_call_target="tpu_custom_call" | custom-call | flops 8800000000 | tf_op jit(solution)/shard_map/pallas_call | solution.py:666
  409.6 9.5 %shard_map.271 = (f32[2,768,384]{2,1,0:T(8,128)}, f32[2,768,384]{2,1,0:T(8,128)}, f32[2,768,384]{2,1,0:T(8,128)}, f32[2,768,384]{2,1,0:T(8,128)}, f32[768,128]{1,0:T(8,128)}, /*index=5*/f32[2,384,768]{2,1,0:T(8,128)}) custom-call(bf16[1024,1536]{1,0:T(8,128)(2,1)} %get-tuple-element.11, ...), custom_call_target="tpu_custom_call", output_to_operand_aliasing={{0}: (14, {}), {1}: (15, {}), {2}: (16, {}), {3}: (17, {}),... | custom-call | flops 7699999744 | tf_op jit(solution)/shard_map/pallas_call | solution.py:748
  437.9 9.8 %collective-permute-done.44.refs_0_ = bf16[64,1536]{1,0:T(8,128)(2,1)S(1)} collective-permute-done((bf16[64,1536]{1,0:T(8,128)(2,1)S(1)}, bf16[64,1536]{1,0:T(8,128)(2,1)S(1)}, u32[]{:S(2)}, u32[]{:S(2)}) %collective-permute-start.44) | collective-permute-done | bytes 196640 | tf_op jit(solution)/shard_map/ppermute | solution.py:25
  455.9 21.0 %shard_map.275 = (bf16[1024,1024]{1,0:T(8,128)(2,1)}, bf16[1024,1024]{1,0:T(8,128)(2,1)}, bf16[1024,1024]{1,0:T(8,128)(2,1)}, bf16[768,1024]{1,0:T(8,128)(2,1)},...) custom-call(bf16[1024,1536]{1,0:T(8,128)(2,1)} %all-gather.9.cloned.1.call-done.b_ref, ...), custom_call_target="tpu_custom_call" | custom-call | flops 26400000000 | tf_op jit(solution)/shard_map/pallas_call | solution.py:683
  484.7 33.7 %shard_map.277 = (bf16[1024,1536]{1,0:T(8,128)(2,1)}, bf16[1024,384]{1,0:T(8,128)(2,1)}, bf16[1024,384]{1,0:T(8,128)(2,1)}, bf16[1024,384]{1,0:T(8,128)(2,1)}, b...) custom-call(s32[2]{0:T(128)} %pad_add_fusion.refs_4_.refs_0_, ...), custom_call_target="tpu_custom_call" | custom-call | flops 36300001280 | tf_op jit(solution)/shard_map/pallas_call | solution.py:615
  522.8 8.6 %shard_map.282 = (bf16[768,384]{1,0:T(8,128)(2,1)}, bf16[768,384]{1,0:T(8,128)(2,1)}, bf16[768,384]{1,0:T(8,128)(2,1)}, bf16[768,384]{1,0:T(8,128)(2,1)}, bf16[7...) custom-call(bf16[1024,1536]{1,0:T(8,128)(2,1)} %get-tuple-element.146.refs_0_, ...), custom_call_target="tpu_custom_call" | custom-call | flops 7699999744 | tf_op jit(solution)/shard_map/pallas_call | solution.py:748
  532.4 10.4 %all-to-all-done.14 = bf16[4,64,1536]{2,1,0:T(8,128)(2,1)S(1)} async-done(((bf16[4,64,1536]{2,1,0:T(8,128)(2,1)}), bf16[4,64,1536]{2,1,0:T(8,128)(2,1)S(1)}, u32[]{:S(2)}, u32[]{:S(2)}) %all-to-all-start.14) | async-done | bytes 786464 | tf_op jit(solution)/shard_map/all_to_all | solution.py:84
  552.5 7.3 %all-to-all-done.15 = bf16[4,64,1536]{2,1,0:T(8,128)(2,1)S(1)} async-done(((bf16[4,64,1536]{2,1,0:T(8,128)(2,1)}), bf16[4,64,1536]{2,1,0:T(8,128)(2,1)S(1)}, u32[]{:S(2)}, u32[]{:S(2)}) %all-to-all-start.15) | async-done | bytes 786464 | tf_op jit(solution)/shard_map/all_to_all | solution.py:48
  561.5 12.0 %shard_map.286 = (f32[2,768,1024]{2,1,0:T(8,128)}, f32[2,768,1024]{2,1,0:T(8,128)}, f32[2,1024,768]{2,1,0:T(8,128)}) custom-call(bf16[1024,1536]{1,0:T(8,128)(2,1)} %all-gather.9.cloned.1.call-done.b_ref, bf16[1024,1536]{1,0:T(8,128)(2,1)} %all-gather.5.cloned.1.call-done.refs_1_.g_ref, ...), custom_call_target="tpu_custom_call", output_to_operand_aliasing={{0}: (8, {}), {1}: (9, {}), {2}: (10, {})} | custom-call | flops 9900000256 | tf_op jit(solution)/shard_map/pallas_call | solution.py:708
  574.0 21.1 %shard_map.280 = (bf16[1024,1024]{1,0:T(8,128)(2,1)}, bf16[1024,1024]{1,0:T(8,128)(2,1)}, bf16[1024,1024]{1,0:T(8,128)(2,1)}, bf16[768,1024]{1,0:T(8,128)(2,1)},...) custom-call(bf16[1024,1536]{1,0:T(8,128)(2,1)} %all-gather.7.cloned.1.call-done.refs_1_.b_ref, ...), custom_call_target="tpu_custom_call" | custom-call | flops 26400000000 | tf_op jit(solution)/shard_map/pallas_call | solution.py:683
  596.0 9.8 %shard_map.284 = (f32[2,768,384]{2,1,0:T(8,128)}, f32[2,768,384]{2,1,0:T(8,128)}, f32[2,768,384]{2,1,0:T(8,128)}, f32[2,768,384]{2,1,0:T(8,128)}, f32[768,128]{1,0:T(8,128)}, /*index=5*/f32[2,384,768]{2,1,0:T(8,128)}) custom-call(bf16[1024,1536]{1,0:T(8,128)(2,1)} %get-tuple-element.14, ...), custom_call_target="tpu_custom_call", output_to_operand_aliasing={{0}: (14, {}), {1}: (15, {}), {2}: (16, {}), {3}: (17, {}),... | custom-call | flops 7699999744 | tf_op jit(solution)/shard_map/pallas_call | solution.py:748
  615.8 10.6 %all-to-all-done.16 = f32[16,1,6144]{2,1,0:T(1,128)S(1)} async-done(((f32[16,1,6144]{2,1,0:T(1,128)}), f32[16,1,6144]{2,1,0:T(1,128)S(1)}, u32[]{:S(2)}, u32[]{:S(2)}) %all-to-all-start.16) | async-done | bytes 393248 | tf_op jit(solution)/shard_map/all_to_all | solution.py:48
  629.7 11.8 %shard_map.287 = (f32[2,768,1024]{2,1,0:T(8,128)}, f32[2,768,1024]{2,1,0:T(8,128)}, f32[2,1024,768]{2,1,0:T(8,128)}) custom-call(bf16[1024,1536]{1,0:T(8,128)(2,1)} %all-gather.7.cloned.1.call-done.refs_1_.b_ref, bf16[1024,1536]{1,0:T(8,128)(2,1)} %all-gather.11.cloned.1.call-done.g_ref, ...), custom_call_target="tpu_custom_call", output_to_operand_aliasing={{0}: (8, {}), {1}: (9, {}), {2}: (10, {})} | custom-call | flops 9900000256 | tf_op jit(solution)/shard_map/pallas_call | solution.py:708
  (408 shorter events, 181.8 us)
Async XLA Ops:
  15.7 129.7 %all-gather.5.cloned.1.call-start = ((), (), s32[]{:S(2)}) async-start(), calls=%async_computation.17 | async-start | bytes 3932160 | tf_op jit(solution)/shard_map/all_gather | solution.py:849
  20.9 45.6 %collective-permute-start.1 = (bf16[256,1536]{1,0:T(8,128)(2,1)}, bf16[256,1536]{1,0:T(8,128)(2,1)}, u32[]{:S(2)}, u32[]{:S(2)}) collective-permute-start(bf16[256,1536]{1,0:T(8,128)(2,1)} %multiply_convert_fusion.refs_1_), channel_id=1, source_target_pairs={{0,4},{4,0},{8,12},{12,8},{1,5},{5,1},{9,13},{13,9},{2,6},{6,2},{1... | collective-permute-start | bytes 2359304 | tf_op jit(solution)/shard_map/ppermute | solution.py:25
  25.0 20.1 %collective-permute-start.2 = (bf16[64,1536]{1,0:T(8,128)(2,1)}, bf16[64,1536]{1,0:T(8,128)(2,1)S(1)}, u32[]{:S(2)}, u32[]{:S(2)}) collective-permute-start(bf16[64,1536]{1,0:T(8,128)(2,1)} %shard_map.254), channel_id=1, source_target_pairs={{0,8},{4,12},{8,0},{12,4},{1,9},{5,13},{9,1},{13,5},{2,10},{6,14},... | collective-permute-start | bytes 589832 | tf_op jit(solution)/shard_map/ppermute | solution.py:25
  27.4 24.2 %collective-permute-start.7 = (bf16[64,1536]{1,0:T(8,128)(2,1)}, bf16[64,1536]{1,0:T(8,128)(2,1)S(1)}, u32[]{:S(2)}, u32[]{:S(2)}) collective-permute-start(bf16[64,1536]{1,0:T(8,128)(2,1)} %shard_map.254), channel_id=1, source_target_pairs={{0,12},{4,8},{8,4},{12,0},{1,13},{5,9},{9,5},{13,1},{2,14},{6,10},... | collective-permute-start | bytes 589832 | tf_op jit(solution)/shard_map/ppermute | solution.py:25
  68.3 219.0 %all-gather.7.cloned.1.call-start = ((), (), s32[]{:S(2)}) async-start(), calls=%async_computation.18 | async-start | bytes 3342336 | tf_op jit(solution)/shard_map/all_gather | solution.py:52
  68.3 54.1 %collective-permute-start.16 = (bf16[2,768,1024]{2,1,0:T(8,128)(2,1)}, bf16[2,768,1024]{2,1,0:T(8,128)(2,1)}, u32[]{:S(2)}, u32[]{:S(2)}) collective-permute-start(bf16[2,768,1024]{2,1,0:T(8,128)(2,1)} %wg.11), channel_id=1, source_target_pairs={{0,16},{16,0},{1,17},{17,1},{2,18},{18,2},{3,19},{19,3},{4,20},{20... | collective-permute-start | bytes 9437192 | tf_op jit(solution)/shard_map/ppermute | solution.py:25
  68.8 53.6 %collective-permute-start.17 = (bf16[2,768,1024]{2,1,0:T(8,128)(2,1)}, bf16[2,768,1024]{2,1,0:T(8,128)(2,1)}, u32[]{:S(2)}, u32[]{:S(2)}) collective-permute-start(bf16[2,768,1024]{2,1,0:T(8,128)(2,1)} %wu.11), channel_id=1, source_target_pairs={{0,16},{16,0},{1,17},{17,1},{2,18},{18,2},{3,19},{19,3},{4,20},{20... | collective-permute-start | bytes 9437192 | tf_op jit(solution)/shard_map/ppermute | solution.py:25
  69.2 53.2 %collective-permute-start.18 = (bf16[2,1024,768]{2,1,0:T(8,128)(2,1)}, bf16[2,1024,768]{2,1,0:T(8,128)(2,1)}, u32[]{:S(2)}, u32[]{:S(2)}) collective-permute-start(bf16[2,1024,768]{2,1,0:T(8,128)(2,1)} %wd.11), channel_id=1, source_target_pairs={{0,16},{16,0},{1,17},{17,1},{2,18},{18,2},{3,19},{19,3},{4,20},{20... | collective-permute-start | bytes 9437192 | tf_op jit(solution)/shard_map/ppermute | solution.py:25
  157.5 40.0 %collective-permute-start.19 = (bf16[256,1536]{1,0:T(8,128)(2,1)S(1)}, bf16[256,1536]{1,0:T(8,128)(2,1)S(1)}, u32[]{:S(2)}, u32[]{:S(2)}) collective-permute-start(bf16[256,1536]{1,0:T(8,128)(2,1)S(1)} %bitcast.67), channel_id=1, source_target_pairs={{0,4},{4,0},{8,12},{12,8},{1,5},{5,1},{9,13},{13,9},{2,6},{6,2},{1... | collective-permute-start | bytes 2359304 | tf_op jit(solution)/shard_map/ppermute | solution.py:25
  160.8 18.3 %collective-permute-start.20 = (bf16[64,1536]{1,0:T(8,128)(2,1)S(1)}, bf16[64,1536]{1,0:T(8,128)(2,1)S(1)}, u32[]{:S(2)}, u32[]{:S(2)}) collective-permute-start(bf16[64,1536]{1,0:T(8,128)(2,1)S(1)} %copy-done.13), channel_id=1, source_target_pairs={{0,8},{4,12},{8,0},{12,4},{1,9},{5,13},{9,1},{13,5},{2,10},{6,14},... | collective-permute-start | bytes 589832 | tf_op jit(solution)/shard_map/ppermute | solution.py:25
  161.0 22.3 %collective-permute-start.24 = (bf16[64,1536]{1,0:T(8,128)(2,1)S(1)}, bf16[64,1536]{1,0:T(8,128)(2,1)S(1)}, u32[]{:S(2)}, u32[]{:S(2)}) collective-permute-start(bf16[64,1536]{1,0:T(8,128)(2,1)S(1)} %copy-done.13), channel_id=1, source_target_pairs={{0,12},{4,8},{8,4},{12,0},{1,13},{5,9},{9,5},{13,1},{2,14},{6,10},... | collective-permute-start | bytes 589832 | tf_op jit(solution)/shard_map/ppermute | solution.py:25
  193.6 262.3 %all-gather.9.cloned.1.call-start = ((), (), s32[]{:S(2)}) async-start(), calls=%async_computation.19 | async-start | bytes 3342336 | tf_op jit(solution)/shard_map/all_gather | solution.py:52
  299.7 29.4 %collective-permute-start.28 = (bf16[256,1536]{1,0:T(8,128)(2,1)S(1)}, bf16[256,1536]{1,0:T(8,128)(2,1)}, u32[]{:S(2)}, u32[]{:S(2)}) collective-permute-start(bf16[256,1536]{1,0:T(8,128)(2,1)S(1)} %bitcast.57), channel_id=1, source_target_pairs={{0,4},{4,0},{8,12},{12,8},{1,5},{5,1},{9,13},{13,9},{2,6},{6,2},{1... | collective-permute-start | bytes 2359304 | tf_op jit(solution)/shard_map/ppermute | solution.py:25
  424.6 23.9 %all-to-all-start.12 = ((bf16[4,64,1536]{2,1,0:T(8,128)(2,1)}), bf16[4,64,1536]{2,1,0:T(8,128)(2,1)S(1)}, u32[]{:S(2)}, u32[]{:S(2)}) async-start(bf16[4,64,1536]{2,1,0:T(8,128)(2,1)} %broadcast_in_dim.34), calls=%async_computation.12 | async-start | bytes 1572864 | tf_op jit(solution)/shard_map/all_to_all | solution.py:48
  429.5 18.2 %collective-permute-start.44 = (bf16[64,1536]{1,0:T(8,128)(2,1)S(1)}, bf16[64,1536]{1,0:T(8,128)(2,1)S(1)}, u32[]{:S(2)}, u32[]{:S(2)}) collective-permute-start(bf16[64,1536]{1,0:T(8,128)(2,1)S(1)} %copy-done.14), channel_id=1, source_target_pairs={{0,8},{4,12},{8,0},{12,4},{1,9},{5,13},{9,1},{13,5},{2,10},{6,14},... | collective-permute-start | bytes 589832 | tf_op jit(solution)/shard_map/ppermute | solution.py:25
  448.5 35.1 %collective-permute-start.43 = (bf16[256,1536]{1,0:T(8,128)(2,1)S(1)}, bf16[256,1536]{1,0:T(8,128)(2,1)}, u32[]{:S(2)}, u32[]{:S(2)}) collective-permute-start(bf16[256,1536]{1,0:T(8,128)(2,1)S(1)} %bitcast.61), channel_id=1, source_target_pairs={{0,4},{4,0},{8,12},{12,8},{1,5},{5,1},{9,13},{13,9},{2,6},{6,2},{1... | collective-permute-start | bytes 2359304 | tf_op jit(solution)/shard_map/ppermute | solution.py:25
  451.6 31.9 %all-to-all-start.13 = ((bf16[4,128,1536]{2,1,0:T(8,128)(2,1)}), bf16[4,128,1536]{2,1,0:T(8,128)(2,1)S(1)}, u32[]{:S(2)}, u32[]{:S(2)}) async-start(bf16[4,128,1536]{2,1,0:T(8,128)(2,1)} %broadcast_in_dim.35), calls=%async_computation.13 | async-start | bytes 3145728 | tf_op jit(solution)/shard_map/all_to_all | solution.py:48
  455.4 118.6 %all-gather.11.cloned.1.call-start = ((), (), s32[]{:S(2)}) async-start(), calls=%async_computation.21 | async-start | bytes 3342336 | tf_op jit(solution)/shard_map/all_gather | solution.py:52
  518.4 24.4 %all-to-all-start.14 = ((bf16[4,64,1536]{2,1,0:T(8,128)(2,1)}), bf16[4,64,1536]{2,1,0:T(8,128)(2,1)S(1)}, u32[]{:S(2)}, u32[]{:S(2)}) async-start(bf16[4,64,1536]{2,1,0:T(8,128)(2,1)} %bitcast.55), calls=%async_computation.14 | async-start | bytes 1572864 | tf_op jit(solution)/shard_map/all_to_all | solution.py:84
  531.4 63.8 %collective-permute-start.46 = (bf16[768,384]{1,0:T(8,128)(2,1)}, bf16[768,384]{1,0:T(8,128)(2,1)S(1)}, u32[]{:S(2)}, u32[]{:S(2)}) collective-permute-start(bf16[768,384]{1,0:T(8,128)(2,1)} %get-tuple-element.154.refs_1_), channel_id=1, source_target_pairs={{0,16},{16,0},{1,17},{17,1},{2,18},{18,2},{3,19},{19,3},{4,20},{20... | collective-permute-start | bytes 1769480 | tf_op jit(solution)/shard_map/ppermute | solution.py:25
  531.4 29.5 %collective-permute-start.58 = (bf16[768,1024]{1,0:T(8,128)(2,1)}, bf16[768,1024]{1,0:T(8,128)(2,1)}, u32[]{:S(2)}, u32[]{:S(2)}) collective-permute-start(bf16[768,1024]{1,0:T(8,128)(2,1)} %get-tuple-element.178), channel_id=1, source_target_pairs={{0,16},{16,0},{1,17},{17,1},{2,18},{18,2},{3,19},{19,3},{4,20},{20... | collective-permute-start | bytes 4718600 | tf_op jit(solution)/shard_map/ppermute | solution.py:25
  531.9 29.0 %collective-permute-start.59 = (bf16[768,1024]{1,0:T(8,128)(2,1)}, bf16[768,1024]{1,0:T(8,128)(2,1)}, u32[]{:S(2)}, u32[]{:S(2)}) collective-permute-start(bf16[768,1024]{1,0:T(8,128)(2,1)} %get-tuple-element.179), channel_id=1, source_target_pairs={{0,16},{16,0},{1,17},{17,1},{2,18},{18,2},{3,19},{19,3},{4,20},{20... | collective-permute-start | bytes 4718600 | tf_op jit(solution)/shard_map/ppermute | solution.py:25
  531.9 29.5 %collective-permute-start.60 = (bf16[1024,768]{1,0:T(8,128)(2,1)}, bf16[1024,768]{1,0:T(8,128)(2,1)}, u32[]{:S(2)}, u32[]{:S(2)}) collective-permute-start(bf16[1024,768]{1,0:T(8,128)(2,1)} %get-tuple-element.180), channel_id=1, source_target_pairs={{0,16},{16,0},{1,17},{17,1},{2,18},{18,2},{3,19},{19,3},{4,20},{20... | collective-permute-start | bytes 4718600 | tf_op jit(solution)/shard_map/ppermute | solution.py:25
  549.6 63.7 %all-reduce.4.cloned.1.call-start = ((), (), s32[]{:S(2)}) async-start(), calls=%async_computation.20 | async-start | bytes 1572864 | tf_op jit(solution)/shard_map/psum | solution.py:946
  551.0 44.3 %collective-permute-start.47 = (bf16[768,384]{1,0:T(8,128)(2,1)}, bf16[768,384]{1,0:T(8,128)(2,1)}, u32[]{:S(2)}, u32[]{:S(2)}) collective-permute-start(bf16[768,384]{1,0:T(8,128)(2,1)} %get-tuple-element.155), channel_id=1, source_target_pairs={{0,16},{16,0},{1,17},{17,1},{2,18},{18,2},{3,19},{19,3},{4,20},{20... | collective-permute-start | bytes 1769480 | tf_op jit(solution)/shard_map/ppermute | solution.py:25
  560.9 34.9 %collective-permute-start.48 = (bf16[768,384]{1,0:T(8,128)(2,1)}, bf16[768,384]{1,0:T(8,128)(2,1)}, u32[]{:S(2)}, u32[]{:S(2)}) collective-permute-start(bf16[768,384]{1,0:T(8,128)(2,1)} %get-tuple-element.156), channel_id=1, source_target_pairs={{0,16},{16,0},{1,17},{17,1},{2,18},{18,2},{3,19},{19,3},{4,20},{20... | collective-permute-start | bytes 1769480 | tf_op jit(solution)/shard_map/ppermute | solution.py:25
  560.9 34.9 %collective-permute-start.49 = (bf16[768,384]{1,0:T(8,128)(2,1)}, bf16[768,384]{1,0:T(8,128)(2,1)}, u32[]{:S(2)}, u32[]{:S(2)}) collective-permute-start(bf16[768,384]{1,0:T(8,128)(2,1)} %get-tuple-element.157), channel_id=1, source_target_pairs={{0,16},{16,0},{1,17},{17,1},{2,18},{18,2},{3,19},{19,3},{4,20},{20... | collective-permute-start | bytes 1769480 | tf_op jit(solution)/shard_map/ppermute | solution.py:25
  573.5 22.4 %collective-permute-start.51 = (bf16[384,768]{1,0:T(8,128)(2,1)}, bf16[384,768]{1,0:T(8,128)(2,1)}, u32[]{:S(2)}, u32[]{:S(2)}) collective-permute-start(bf16[384,768]{1,0:T(8,128)(2,1)} %get-tuple-element.159), channel_id=1, source_target_pairs={{0,16},{16,0},{1,17},{17,1},{2,18},{18,2},{3,19},{19,3},{4,20},{20... | collective-permute-start | bytes 1769480 | tf_op jit(solution)/shard_map/ppermute | solution.py:25
  595.2 33.3 %collective-permute-start.55 = (bf16[768,1024]{1,0:T(8,128)(2,1)}, bf16[768,1024]{1,0:T(8,128)(2,1)S(1)}, u32[]{:S(2)}, u32[]{:S(2)}) collective-permute-start(bf16[768,1024]{1,0:T(8,128)(2,1)} %get-tuple-element.173), channel_id=1, source_target_pairs={{0,16},{16,0},{1,17},{17,1},{2,18},{18,2},{3,19},{19,3},{4,20},{20... | collective-permute-start | bytes 4718600 | tf_op jit(solution)/shard_map/ppermute | solution.py:25
  595.3 33.2 %collective-permute-start.56 = (bf16[768,1024]{1,0:T(8,128)(2,1)}, bf16[768,1024]{1,0:T(8,128)(2,1)}, u32[]{:S(2)}, u32[]{:S(2)}) collective-permute-start(bf16[768,1024]{1,0:T(8,128)(2,1)} %get-tuple-element.174), channel_id=1, source_target_pairs={{0,16},{16,0},{1,17},{17,1},{2,18},{18,2},{3,19},{19,3},{4,20},{20... | collective-permute-start | bytes 4718600 | tf_op jit(solution)/shard_map/ppermute | solution.py:25
  595.8 32.8 %collective-permute-start.57 = (bf16[1024,768]{1,0:T(8,128)(2,1)}, bf16[1024,768]{1,0:T(8,128)(2,1)}, u32[]{:S(2)}, u32[]{:S(2)}) collective-permute-start(bf16[1024,768]{1,0:T(8,128)(2,1)} %get-tuple-element.175), channel_id=1, source_target_pairs={{0,16},{16,0},{1,17},{17,1},{2,18},{18,2},{3,19},{19,3},{4,20},{20... | collective-permute-start | bytes 4718600 | tf_op jit(solution)/shard_map/ppermute | solution.py:25
  608.7 17.7 %all-to-all-start.16 = ((f32[16,1,6144]{2,1,0:T(1,128)}), f32[16,1,6144]{2,1,0:T(1,128)S(1)}, u32[]{:S(2)}, u32[]{:S(2)}) async-start(f32[16,1,6144]{2,1,0:T(1,128)} %broadcast_in_dim.38), calls=%async_computation.16 | async-start | bytes 786432 | tf_op jit(solution)/shard_map/all_to_all | solution.py:48
  (121 other events, 1233.0 us)
Sparse Core Ops, SparseCore 0:
  68.4 63.5 all-gather.4
  193.7 72.5 all-gather.6
  329.3 75.3 all-gather.8
  477.1 77.0 all-gather.10
  557.1 47.1 all-reduce.3
